TPU v7x, 32 devices: a whole 2x2x4 slice. The times are simulated.
32 devices in a mesh: groups: 2 (over y), fsdp: 4 (over x, core), tensor: 4 (over z).
Axes of the slice: x: 2, y: 2, z: 4, core: 2. Of those that a mesh axis runs over, the one named last changes fastest.
Arguments:
- tokens: bfloat16 [1024, 8192], P(('groups', 'fsdp')), parts along dimension 0, may hold values from -64 to 64
- gate_weight: bfloat16 [8192, 14336], P('fsdp', 'tensor'), may hold values from -0.0625 to 0.0625
- up_weight: bfloat16 [8192, 14336], P('fsdp', 'tensor'), may hold values from -0.0625 to 0.0625
- down_weight: bfloat16 [14336, 8192], P('tensor', 'fsdp'), may hold values from -0.046875 to 0.046875
- right_factor: bfloat16 [64, 128, 128], P('fsdp', 'tensor'), may hold values from -0.5 to 0.5
- left_factor: bfloat16 [128, 64, 64], P('fsdp', 'tensor'), may hold values from -0.75 to 0.75
Outputs:
- grad_right: float32 [128, 128, 128], P(('groups', 'fsdp'), 'tensor'), parts along dimension 0
- grad_left: float32 [256, 64, 64], P(('groups', 'fsdp'), 'tensor'), parts along dimension 0
There are 2 independent parts, one for each index of `groups`. A program takes and returns all parts, laid end to end along the dimension named above; an argument that names none is the same for every part. Nothing has to cross between parts.
All inputs are finite; a program needn't handle non-finite values.
Results may differ from a plain program's by a relative error of at most 0.0055.
Values may be sent and summed in bfloat16 or wider, within the bound.
No kernel may reach another device: no remote copies, remote signals or barrier semaphores. Data moves between devices by JAX's collectives and lax.ppermute only.
A program may use at most 128 MiB of HBM per device.

v0:
```python
import math

import jax
import jax.numpy as jnp
from jax import lax
from jax.sharding import PartitionSpec as P


def body(tokens, gate_weight, up_weight, down_weight, right_factor, left_factor):
    fsdp_count = lax.axis_size("fsdp")
    tensor_count = lax.axis_size("tensor")
    tok_local = tokens.shape[0]
    group_rows = tok_local * fsdp_count
    share_rows = group_rows // tensor_count
    hid_local = gate_weight.shape[1]
    spread = lax.all_to_all(tokens, "fsdp", split_axis=1, concat_axis=0, tiled=True)
    student_in = lax.dynamic_slice_in_dim(
        spread, lax.axis_index("tensor") * share_rows, share_rows, 0
    )
    gate_part = jnp.dot(spread, gate_weight, preferred_element_type=jnp.float32)
    up_part = jnp.dot(spread, up_weight, preferred_element_type=jnp.float32)
    partial_value = jnp.concatenate([gate_part, up_part], axis=1)
    summed = lax.psum(partial_value.astype(jnp.bfloat16), "fsdp").astype(jnp.float32)
    hidden = (jax.nn.silu(summed[:, :hid_local]) * summed[:, hid_local:]).astype(jnp.bfloat16)
    target = lax.psum_scatter(
        jnp.dot(hidden, down_weight, preferred_element_type=jnp.float32).astype(jnp.bfloat16),
        "tensor",
        scatter_dimension=0,
        tiled=True,
    ).astype(jnp.float32)
    right_full, left_full = (
        lax.all_gather(right_factor, "tensor", axis=1, tiled=True),
        lax.all_gather(left_factor, "tensor", axis=1, tiled=True),
    )
    blocks_local = right_full.shape[0]
    block_size = right_full.shape[2]
    block_input = student_in.reshape(share_rows, blocks_local, block_size)
    mixed = jnp.einsum(
        "nij,ikj->nik", block_input, right_full, preferred_element_type=jnp.float32
    ).astype(jnp.bfloat16)
    routed = lax.all_to_all(mixed, "fsdp", split_axis=2, concat_axis=1, tiled=True)
    student = jnp.einsum("nij,jki->njk", routed, left_full, preferred_element_type=jnp.float32)
    inv_root = 1.0 / math.sqrt(group_rows)
    out_grad = (student - target.reshape(student.shape)) * inv_root
    grad_left = jnp.einsum("njk,nij->jki", out_grad, routed.astype(jnp.float32))
    mixed_grad = jnp.einsum("njk,jki->nij", out_grad, left_full.astype(jnp.float32)).astype(
        jnp.bfloat16
    )
    returned = lax.all_to_all(mixed_grad, "fsdp", split_axis=1, concat_axis=2, tiled=True)
    grad_right = jnp.einsum(
        "nik,nij->ikj", returned.astype(jnp.float32), block_input.astype(jnp.float32)
    )
    grad_right, grad_left = (
        lax.psum_scatter(grad_right, "tensor", scatter_dimension=1, tiled=True),
        lax.psum_scatter(grad_left, "tensor", scatter_dimension=1, tiled=True),
    )
    return (grad_right, grad_left)


def solution(mesh):
    return jax.shard_map(
        body,
        mesh=mesh,
        in_specs=(
            P(("groups", "fsdp"), None),
            P("fsdp", "tensor"),
            P("fsdp", "tensor"),
            P("tensor", "fsdp"),
            P("fsdp", "tensor", None),
            P("fsdp", "tensor", None),
        ),
        out_specs=(P(("groups", "fsdp"), "tensor", None), P(("groups", "fsdp"), "tensor", None)),
        check_vma=False,
    )
```

profile of v0, /device:TPU:0, one launch (start us, length us, event | category | flops | bytes accessed | tf_op | source)
XLA Modules:
  0.0 363.5 jit_solution(13968210217118573609)
XLA Ops:
  7.2 0.0 all-reduce.2.cloned.1.call-start
  7.2 4.1 %copy.27 = bf16[128,8192]{0,1:T(8,128)(2,1)} copy(bf16[128,8192]{1,0:T(8,128)(2,1)} %param.6) | data formatting | bytes 4194304 | tf_op args[0]
  11.3 29.9 %all_to_all.55 = bf16[128,4,2048]{0,2,1:T(8,128)(2,1)S(1)} all-to-all(bf16[128,4,2048]{0,2,1:T(8,128)(2,1)} %bitcast.39), channel_id=1, replica_groups=mesh['groups'=2,'fsdp'=4,'tensor'=4] {'fsdp'}, dimensions={1} | all-to-all | bytes 4194304 | tf_op jit(solution)/shard_map/all_to_all | solution.py:16
  41.2 2.6 copy.28
  43.8 0.0 copy-start
  43.8 13.7 %convolution_convert_fusion = bf16[512,3584]{1,0:T(8,128)(2,1)S(1)} fusion(bf16[512,2048]{1,0:T(8,128)(2,1)} %bitcast.45, bf16[2048,3584]{1,0:T(8,128)(2,1)} %param.8), kind=kOutput, calls=%fused_computation.3 | convolution fusion | flops 7518027776 | bytes 20447232 | tf_op jit(solution)/shard_map/dot_general | solution.py:21
  57.5 0.0 copy-done
  57.5 12.4 %convolution_convert_fusion.1 = bf16[512,3584]{1,0:T(8,128)(2,1)} fusion(bf16[512,2048]{1,0:T(8,128)(2,1)S(1)} %bitcast.47, bf16[2048,3584]{1,0:T(8,128)(2,1)} %param.7), kind=kOutput, calls=%fused_computation.4 | convolution fusion | flops 7518027776 | bytes 20447232 | tf_op jit(solution)/shard_map/dot_general | solution.py:20
  69.9 6.0 %pad_maximum_fusion = bf16[512,7168]{1,0:T(8,128)(2,1)} fusion(bf16[512,3584]{1,0:T(8,128)(2,1)S(1)} %convolution_convert_fusion, bf16[512,3584]{1,0:T(8,128)(2,1)} %convolution_convert_fusion.1), kind=kLoop, calls=%fused_computation.2 | loop fusion | flops 14680064 | bytes 14680064 | tf_op jit(solution)/shard_map/concatenate | solution.py:22
  75.9 0.0 all-reduce.2.cloned.1.call-update
  75.9 0.0 reduce-scatter.4.cloned.1.call-start
  76.0 137.9 %all-reduce.2.cloned.1.call-done = bf16[512,7168]{1,0:T(8,128)(2,1)} async-done(((bf16[512,7168]{1,0:T(8,128)(2,1)}), bf16[512,7168]{1,0:T(8,128)(2,1)}) %all-reduce.2.cloned.1.call-update) | async-done | bytes 7340048 | tf_op jit(solution)/shard_map/psum | solution.py:23
  213.9 10.2 %convert_element_type.29 = f32[512,7168]{1,0:T(8,128)} convert(bf16[512,7168]{1,0:T(8,128)(2,1)} %all-reduce.2.cloned.1.call-done) | non-fusion elementwise | flops 3670016 | bytes 22020096 | tf_op jit(solution)/shard_map/convert_element_type | solution.py:23
  224.1 0.0 copy-start.1
  224.1 16.5 %fusion.3 = bf16[512,2048]{1,0:T(8,128)(2,1)} fusion(bf16[3584,2048]{1,0:T(8,128)(2,1)} %param.9, f32[512,7168]{1,0:T(8,128)} %convert_element_type.29), kind=kOutput, calls=%fused_computation.6 | convolution fusion | flops 7528251392 | bytes 31457280 | tf_op jit(solution)/shard_map/dot_general | solution.py:26
  240.6 0.0 copy-start.2
  240.6 0.0 reduce-scatter.4.cloned.1.call-update
  240.6 0.0 copy-done.1
  240.6 22.3 %all_gather.6 = bf16[16,128,128]{2,1,0:T(8,128)(2,1)S(1)} all-gather(bf16[16,32,128]{2,1,0:T(8,128)(2,1)S(1)} %copy-done.1), channel_id=1, replica_groups=mesh['groups'=2,'fsdp'=4,'tensor'=4] {'tensor'}, dimensions={1}, use_global_device_ids=true | all-gather | bytes 655360 | tf_op jit(solution)/shard_map/all_gather | solution.py:32
  262.9 1.1 constant_dynamic-slice_fusion
  264.0 0.3 copy.29
  264.2 0.5 fusion.9
  264.8 1.2 copy.31
  266.0 3.5 all-to-all-start.1
  269.4 0.0 reduce-scatter.8.cloned.1.call-start
  269.5 0.0 copy-done.2
  269.5 22.2 %all_gather.7 = bf16[32,64,64]{2,1,0:T(8,128)(2,1)S(1)} all-gather(bf16[32,16,64]{2,1,0:T(8,128)(2,1)S(1)} %copy-done.2), channel_id=1, replica_groups=mesh['groups'=2,'fsdp'=4,'tensor'=4] {'tensor'}, dimensions={1}, use_global_device_ids=true | all-gather | bytes 327680 | tf_op jit(solution)/shard_map/all_gather | solution.py:33
  291.7 0.0 all-to-all-done.1
  291.7 0.1 copy.33
  291.7 6.0 %reduce-scatter.4.cloned.1.call-done = bf16[128,2048]{1,0:T(8,128)(2,1)} async-done(((bf16[512,2048]{1,0:T(8,128)(2,1)}), bf16[128,2048]{1,0:T(8,128)(2,1)}) %reduce-scatter.4.cloned.1.call-update) | async-done | bytes 524304 | tf_op jit(solution)/shard_map/reduce_scatter | solution.py:25
  297.7 1.2 copy.34
  299.0 0.3 fusion.7
  299.3 1.4 fusion.12
  300.7 0.0 reduce-scatter.8.cloned.1.call-update
  300.7 0.0 reduce-scatter.6.cloned.1.call-start
  300.8 0.3 fusion.8
  301.1 0.3 copy.35
  301.5 11.3 %all_to_all.56 = bf16[128,64,32]{0,2,1:T(8,128)(2,1)S(1)} all-to-all(bf16[128,64,32]{0,2,1:T(8,128)(2,1)S(1)} %copy.35), channel_id=1, replica_groups=mesh['groups'=2,'fsdp'=4,'tensor'=4] {'fsdp'}, dimensions={1} | all-to-all | bytes 1048576 | tf_op jit(solution)/shard_map/all_to_all | solution.py:49
  312.8 1.5 fusion.11
  314.3 0.0 reduce-scatter.6.cloned.1.call-update
  314.3 14.2 %reduce-scatter.8.cloned.1.call-done = f32[32,16,64]{2,1,0:T(8,128)} async-done(((f32[32,64,64]{2,1,0:T(8,128)}), f32[32,16,64]{2,1,0:T(8,128)}) %reduce-scatter.8.cloned.1.call-update) | async-done | bytes 131088 | tf_op jit(solution)/shard_map/reduce_scatter | solution.py:55
  328.5 28.5 %reduce-scatter.6.cloned.1.call-done = f32[16,32,128]{2,1,0:T(8,128)} async-done(((f32[16,128,128]{2,1,0:T(8,128)}), f32[16,32,128]{2,1,0:T(8,128)}) %reduce-scatter.6.cloned.1.call-update) | async-done | bytes 262160 | tf_op jit(solution)/shard_map/reduce_scatter | solution.py:54
  (1 shorter events, 0.0 us)
Async XLA Ops:
  7.2 206.7 %all-reduce.2.cloned.1.call-start = ((), (), s32[]{:S(2)}) async-start(), calls=%async_computation.6 | async-start | bytes 14680064 | tf_op jit(solution)/shard_map/psum | solution.py:23
  43.8 13.7 %copy-start = (bf16[4,128,2048]{2,1,0:T(8,128)(2,1)S(1)}, bf16[4,128,2048]{2,1,0:T(8,128)(2,1)}, u32[]{:S(2)}) copy-start(bf16[4,128,2048]{2,1,0:T(8,128)(2,1)} %copy.28) | copy-start | bytes 6291460
  75.9 221.8 %reduce-scatter.4.cloned.1.call-start = ((), (), s32[]{:S(2)}) async-start(), calls=%async_computation.7 | async-start | bytes 2621440 | tf_op jit(solution)/shard_map/reduce_scatter | solution.py:25
  224.1 16.6 %copy-start.1 = (bf16[16,32,128]{2,1,0:T(8,128)(2,1)S(1)}, bf16[16,32,128]{2,1,0:T(8,128)(2,1)}, u32[]{:S(2)}) copy-start(bf16[16,32,128]{2,1,0:T(8,128)(2,1)} %param.10) | copy-start | bytes 393220
  240.6 28.9 %copy-start.2 = (bf16[32,16,64]{2,1,0:T(8,128)(2,1)S(1)}, bf16[32,16,64]{2,1,0:T(8,128)(2,1)}, u32[]{:S(2)}) copy-start(bf16[32,16,64]{2,1,0:T(8,128)(2,1)} %param.11) | copy-start | bytes 196612
  266.0 25.7 %all-to-all-start.1 = ((bf16[128,16,128]{0,1,2:T(8,128)(2,1)}), bf16[128,16,128]{0,1,2:T(8,128)(2,1)S(1)}, u32[]{:S(2)}, u32[]{:S(2)}) async-start(bf16[128,16,128]{0,1,2:T(8,128)(2,1)} %copy.31), calls=%async_computation.1 | async-start | bytes 1048576 | tf_op jit(solution)/shard_map/all_to_all | solution.py:41
  269.4 59.0 %reduce-scatter.8.cloned.1.call-start = ((), (), s32[]{:S(2)}) async-start(), calls=%async_computation.9 | async-start | bytes 1310720 | tf_op jit(solution)/shard_map/reduce_scatter | solution.py:55
  300.7 56.3 %reduce-scatter.6.cloned.1.call-start = ((), (), s32[]{:S(2)}) async-start(), calls=%async_computation.8 | async-start | bytes 1310720 | tf_op jit(solution)/shard_map/reduce_scatter | solution.py:54
Sparse Core Ops, SparseCore 0:
  76.1 137.7 all-reduce.1
  240.7 56.9 reduce-scatter.3
  300.9 27.5 reduce-scatter.7
  331.2 25.7 reduce-scatter.5
where the time goes:
time: 364 us
  waiting for transfers between devices  187 us (51%)
  blocking collectives  85.6 us (24%)
  matrix products  46.6 us (13%)
  other arithmetic  16.2 us (4%)
  between operations  13.9 us (4%)
  local copies, waits for them, and re-layouts  11 us (3%)
  starting transfers between devices  3.64 us (1%)
    psum x1, waiting for transfers between devices, body(): lax.psum(partial_value.astype(jnp.bfloat16), 'fsdp').astype(jnp.float32)  138 us
    all_to_all x1, blocking collectives, body(): lax.all_to_all(tokens, 'fsdp', split_axis=1, concat_axis=0, tiled=True)  29.9 us
    reduce_scatter x1, waiting for transfers between devices, body(): lax.psum_scatter(grad_right, 'tensor', scatter_dimension=1, tiled=True)  28.5 us
    all_gather x1, blocking collectives, body(): lax.all_gather(right_factor, 'tensor', axis=1, tiled=True)  22.3 us
    all_gather x1, blocking collectives, body(): lax.all_gather(left_factor, 'tensor', axis=1, tiled=True)  22.2 us
    dot_general x1, matrix products, body(): jnp.dot(hidden, down_weight, preferred_element_type=jnp.float32)  16.5 us
    reduce_scatter x1, waiting for transfers between devices, body(): lax.psum_scatter(grad_left, 'tensor', scatter_dimension=1, tiled=True)  14.2 us
    dot_general x1, matrix products, body(): up_part = jnp.dot(spread, up_weight, preferred_element_type=jnp.float32)  13.7 us
  transfers between devices with their start and end apart: 5, of which 4 were waited for; matrix products, arithmetic and copies ran while one was open for 1% of the time, Pallas kernels for 0%

commit v1 on v0

v1 whole, which is shorter than its diff:
```python
import functools
import math

import jax
import jax.numpy as jnp
from jax import lax
from jax.experimental import pallas as pl
from jax.experimental.pallas import tpu as pltpu
from jax.sharding import PartitionSpec as P

BLK = 256
F32 = jnp.float32
BF16 = jnp.bfloat16


def gate_up_kernel(idx_ref, top_ref, bottom_ref, gate_ref, up_ref, mine_ref, other_ref):
    rows = top_ref.shape[0]
    lhs = jnp.concatenate([top_ref[...], bottom_ref[...]], axis=0)
    for slot, weight_ref in enumerate((gate_ref, up_ref)):
        product = jnp.dot(lhs, weight_ref[...], preferred_element_type=F32).astype(BF16)
        mine_ref[slot] = product[:rows]
        other_ref[slot] = product[rows:]


def gate_up(top, top_block, bottom, gate, up, column, first, width):
    rows, feat = bottom.shape
    if width % BLK or gate.shape[1] % BLK or rows % 16 or feat % 128:
        lhs = jnp.concatenate(
            [lax.dynamic_slice_in_dim(top, top_block * feat, feat, 1), bottom], axis=0
        )
        both = [
            jnp.dot(
                lhs,
                lax.dynamic_slice_in_dim(w, column + first, width, 1),
                preferred_element_type=F32,
            ).astype(BF16)
            for w in (gate, up)
        ]
        both = jnp.stack(both)
        return both[:, :rows], both[:, rows:]
    scalars = jnp.stack([top_block, column // BLK + first // BLK]).astype(jnp.int32)
    weight_spec = pl.BlockSpec((feat, BLK), lambda n, s: (0, s[1] + n))
    out_spec = pl.BlockSpec((2, rows, BLK), lambda n, s: (0, 0, n))
    shape = jax.ShapeDtypeStruct((2, rows, width), BF16)
    return pl.pallas_call(
        gate_up_kernel,
        grid_spec=pltpu.PrefetchScalarGridSpec(
            num_scalar_prefetch=1,
            grid=(width // BLK,),
            in_specs=[
                pl.BlockSpec((rows, feat), lambda n, s: (0, s[0])),
                pl.BlockSpec((rows, feat), lambda n, s: (0, 0)),
                weight_spec,
                weight_spec,
            ],
            out_specs=[out_spec, out_spec],
        ),
        out_shape=[shape, shape],
        compiler_params=pltpu.CompilerParams(vmem_limit_bytes=24 * 2**20),
        cost_estimate=pl.CostEstimate(
            flops=2 * 2 * rows * feat * 2 * width,
            bytes_accessed=2 * feat * 2 * width + 2 * 2 * rows * (feat + 2 * width),
            transcendentals=0,
        ),
        name="gate_up",
    )(scalars, top, bottom, gate, up)


def down_kernel(idx_ref, mine_ref, other_ref, weight_ref, total_ref, out_ref):
    lhs = jnp.concatenate([mine_ref[...], other_ref[...]], axis=0)
    product = jnp.dot(lhs, weight_ref[...], preferred_element_type=F32)

    @pl.when(pl.program_id(0) == 0)
    def _():
        out_ref[...] = total_ref[...] + product

    @pl.when(pl.program_id(0) > 0)
    def _():
        out_ref[...] += product


def down_add(total, mine, other, weight, row):
    rows, width = mine.shape
    outs = weight.shape[1]
    if width % BLK or weight.shape[0] % BLK or rows % 16 or outs % 128:
        lhs = jnp.concatenate([mine, other], axis=0)
        part = lax.dynamic_slice_in_dim(weight, row, width, 0)
        return total + jnp.dot(lhs, part, preferred_element_type=F32)
    scalars = jnp.reshape(row // BLK, (1,)).astype(jnp.int32)
    hidden_spec = pl.BlockSpec((rows, BLK), lambda k, s: (0, k))
    whole = pl.BlockSpec((2 * rows, outs), lambda k, s: (0, 0))
    return pl.pallas_call(
        down_kernel,
        grid_spec=pltpu.PrefetchScalarGridSpec(
            num_scalar_prefetch=1,
            grid=(width // BLK,),
            in_specs=[
                hidden_spec,
                hidden_spec,
                pl.BlockSpec((BLK, outs), lambda k, s: (s[0] + k, 0)),
                whole,
            ],
            out_specs=whole,
        ),
        out_shape=jax.ShapeDtypeStruct((2 * rows, outs), F32),
        compiler_params=pltpu.CompilerParams(vmem_limit_bytes=24 * 2**20),
        cost_estimate=pl.CostEstimate(
            flops=2 * 2 * rows * width * outs,
            bytes_accessed=2 * width * outs + 2 * 2 * rows * width + 16 * rows * outs,
            transcendentals=0,
        ),
        name="down_add",
    )(scalars, mine, other, weight, total)


def body(tokens, gate_weight, up_weight, down_weight, right_factor, left_factor):
    fsdp_count = lax.axis_size("fsdp")
    tensor_count = lax.axis_size("tensor")
    chips = fsdp_count // 2
    rows, model = tokens.shape
    feat, hid = gate_weight.shape
    part = hid // chips
    me = lax.axis_index("fsdp")
    chip, core = me // 2, me % 2
    z = lax.axis_index("tensor")

    def swap(value):
        return lax.ppermute(value, "fsdp", [(i, i ^ 1) for i in range(fsdp_count)])

    def shift(value, hops):
        perm = [(i, (i + 2 * hops) % fsdp_count) for i in range(fsdp_count)]
        return lax.ppermute(value, "fsdp", perm)

    def gather_z(value):
        if tensor_count > 4:
            return lax.all_gather(value, "tensor", axis=0, tiled=True)
        size = value.shape[0]
        whole = jnp.zeros((size * tensor_count,) + value.shape[1:], value.dtype)
        whole = lax.dynamic_update_slice_in_dim(whole, value, z * size, 0)
        for step in range(1, tensor_count):
            perm = [(i, (i + step) % tensor_count) for i in range(tensor_count)]
            got = lax.ppermute(value, "tensor", perm)
            source = lax.rem(z - step + tensor_count, tensor_count)
            whole = lax.dynamic_update_slice_in_dim(whole, got, source * size, 0)
        return whole

    def scatter_z(value):
        if tensor_count > 4:
            return lax.psum_scatter(value, "tensor", scatter_dimension=0, tiled=False)
        total = lax.dynamic_index_in_dim(value, z, 0, keepdims=False)
        for step in range(1, tensor_count):
            target_z = lax.rem(z + step, tensor_count)
            piece = lax.dynamic_index_in_dim(value, target_z, 0, keepdims=False)
            perm = [(i, (i + step) % tensor_count) for i in range(tensor_count)]
            total += lax.ppermute(piece.astype(BF16), "tensor", perm).astype(F32)
        return total

    def columns(value, start, width):
        return lax.dynamic_slice_in_dim(value, start, width, 1)

    pairs = {0: (tokens, me, swap(columns(tokens, (me ^ 1) * feat, feat)))}
    row_share = rows // tensor_count
    own_share = lax.dynamic_slice_in_dim(tokens, z * row_share, row_share, 0)
    gathered = {}
    for dt in range(1, chips):
        for g in range(chips):
            features = (chip - dt + g + chips) % chips * (2 * feat)
            piece = shift(columns(own_share, features, 2 * feat), -dt)
            gathered[dt, g] = gather_z(piece)
        got = gathered[dt, 0]
        pairs[dt] = (
            columns(got, core * feat, feat),
            jnp.int32(0),
            swap(columns(got, (1 - core) * feat, feat)),
        )

    if part % BLK == 0 and part // BLK > 1:
        head = (part // BLK + 1) // 2 * BLK
        chunks = [(0, head), (head, part - head)]
    else:
        chunks = [(0, part)]

    def partial(dt, dp, chunk):
        column = (chip + dp) % chips * part
        top, block, bottom = pairs[dt]
        mine, other = gate_up(top, block, bottom, gate_weight, up_weight, column, *chunk)
        return mine, swap(other)

    kept, got = {}, {}
    for dt in range(chips):
        for dp in list(range(1, chips)) + [0]:
            for n, chunk in enumerate(chunks):
                mine, from_core = partial(dt, dp, chunk)
                if dp:
                    both = (mine.astype(F32) + from_core.astype(F32)).astype(BF16)
                    got[dt, dp, n] = shift(both, dp)
                else:
                    kept[dt, n] = (mine, from_core)

    hidden = {}
    for e in list(range(1, chips)) + [0]:
        for n in range(len(chunks)):
            terms = list(kept[e, n])
            terms += [got[(e + dp) % chips, dp, n] for dp in range(1, chips)]
            total = sum(term.astype(F32) for term in terms)
            value = (jax.nn.silu(total[0]) * total[1]).astype(BF16)
            hidden[e, 0, n] = value
            for d in range(1, chips):
                hidden[e, d, n] = shift(value, d)

    totals = {u: jnp.zeros((2 * rows, down_weight.shape[1]), F32) for u in range(chips)}
    for e in list(range(1, chips)) + [0]:
        for n, (first, width) in enumerate(chunks):
            for d in range(chips):
                u = (e - d + chips) % chips
                mine = hidden[e, d, n]
                row = (chip - d + chips) % chips * part + first
                totals[u] = down_add(totals[u], mine, swap(mine), down_weight, row)

    token_rows = []
    for dt in range(chips):
        if dt == 0:
            full = tokens
        else:
            full = jnp.zeros((rows, model), BF16)
            for g in range(chips):
                features = (chip + g) % chips * (2 * feat)
                full = lax.dynamic_update_slice_in_dim(full, gathered[dt, g], features, 1)
        token_rows += [full, swap(full)]
    inputs = jnp.concatenate(token_rows, axis=0)
    count = inputs.shape[0]

    blocks, share, size = right_factor.shape
    ratio = tensor_count // fsdp_count
    turn = []
    for a in range(fsdp_count):
        for b in range(tensor_count):
            turn.append((a * tensor_count + b, (b // ratio) * tensor_count + a * ratio + b % ratio))
    back = [(b, a) for a, b in turn]
    right_rows = gather_z(lax.ppermute(right_factor, ("fsdp", "tensor"), turn)[None])
    right_rows = right_rows.reshape(fsdp_count, ratio, blocks, share, size)
    right_rows = right_rows.transpose(0, 2, 1, 3, 4).reshape(
        fsdp_count * blocks, ratio * share, size
    )
    left_rows = jnp.moveaxis(gather_z(jnp.moveaxis(left_factor, 1, 0)), 0, 1)

    block_input = inputs.reshape(count, fsdp_count * blocks, size)
    mixed = jnp.einsum(
        "nim,ijm->nij", block_input, right_rows, preferred_element_type=F32
    ).astype(BF16)
    student = jnp.einsum("nij,jki->njk", mixed, left_rows, preferred_element_type=F32)
    target = jnp.concatenate([totals[u] for u in range(chips)], axis=0)
    scale = 1.0 / math.sqrt(count)
    out_grad = (student * (1.0 / tensor_count) - target.reshape(student.shape)) * scale
    out_grad = out_grad.astype(BF16)
    grad_left = jnp.einsum("njk,nij->kji", out_grad, mixed, preferred_element_type=F32)
    mixed_grad = jnp.einsum(
        "njk,jki->nij", out_grad, left_rows, preferred_element_type=F32
    ).astype(BF16)
    grad_right = jnp.einsum(
        "nij,nim->ijm", mixed_grad, block_input, preferred_element_type=F32
    )
    grad_left = scatter_z(
        grad_left.reshape((tensor_count, -1) + grad_left.shape[1:])
    )
    grad_left = jnp.moveaxis(grad_left, 0, 1)
    grad_right = grad_right.reshape(fsdp_count, blocks, ratio, share, size)
    grad_right = grad_right.transpose(0, 2, 1, 3, 4).reshape(
        tensor_count, blocks, share, size
    )
    grad_right = lax.ppermute(scatter_z(grad_right), ("fsdp", "tensor"), back)
    return grad_right, grad_left


def solution(mesh):
    return jax.shard_map(
        body,
        mesh=mesh,
        in_specs=(
            P(("groups", "fsdp"), None),
            P("fsdp", "tensor"),
            P("fsdp", "tensor"),
            P("tensor", "fsdp"),
            P("fsdp", "tensor", None),
            P("fsdp", "tensor", None),
        ),
        out_specs=(P(("groups", "fsdp"), "tensor", None), P(("groups", "fsdp"), "tensor", None)),
        check_vma=False,
    )
```

time: 364 us -> 299 us (0.82)
  the two profiles are of different devices: /device:TPU:0 before, /device:TPU:17 now
where the time goes in v1:
time: 299 us; the launch traced here: 298 us
  waiting for transfers between devices  78.8 us (26%)
  local copies, waits for them, and re-layouts  73.5 us (25%)
  Pallas kernels  65.4 us (22%)
  starting transfers between devices  57.5 us (19%)
  other arithmetic  13.1 us (4%)
  matrix products  8.47 us (3%)
    pallas_call x8, Pallas kernels, gate_up(): pl.pallas_call(gate_up_kernel, grid_spec=pltpu.PrefetchScalarGridSpec(num...  45 us
    unnamed x71, local copies, waits for them, and re-layouts  36 us
    ppermute x12, waiting for transfers between devices, gather_z(): got = lax.ppermute(value, 'tensor', perm)  29.3 us
    ppermute x10, waiting for transfers between devices, shift(): return lax.ppermute(value, 'fsdp', perm)  24.2 us
    pallas_call x8, Pallas kernels, down_add(): pl.pallas_call(down_kernel, grid_spec=pltpu.PrefetchScalarGridSpec(num_sc...  20.4 us
    ppermute x20, starting transfers between devices, swap(): return lax.ppermute(value, 'fsdp', [(i, i ^ 1) for i in range(fsdp_count)])  16.4 us
    dynamic_update_slice x14, local copies, waits for them, and re-layouts, gather_z(): whole = lax.dynamic_update_slice_in_dim(whole, got, source * size, 0)  13.6 us
    ppermute x1, waiting for transfers between devices, body(): grad_right = lax.ppermute(scatter_z(grad_right), ('fsdp', 'tensor'), back)  13.1 us
  transfers between devices with their start and end apart: 50, of which 12 were waited for; matrix products, arithmetic and copies ran while one was open for 17% of the time, Pallas kernels for 22%

profile of v1, /device:TPU:17, one launch (start us, length us, event | category | flops | bytes accessed | tf_op | source)
XLA Modules:
  0.0 298.2 jit_solution(8361658934211173234)
XLA Ops:
  3.3 2.0 fusion.32
  6.5 1.9 constant_dynamic-slice_fusion.2
  8.4 1.7 collective-permute-start.17
  10.1 2.4 copy.18
  16.0 4.7 %collective-permute-start.3 = (bf16[16,32,128]{2,1,0:T(8,128)(2,1)}, bf16[16,32,128]{2,1,0:T(8,128)(2,1)S(1)}, u32[]{:S(2)}, u32[]{:S(2)}) collective-permute-start(bf16[16,32,128]{2,1,0:T(8,128)(2,1)} %param.10), channel_id=1, source_target_pairs={{0,0},{1,4},{2,8},{3,12},{4,1},{5,5},{6,9},{7,13},{8,2},{9,6},{10,... | collective-permute-start | bytes 393224 | tf_op jit(solution)/shard_map/ppermute | solution.py:240
  23.8 3.5 %collective-permute-done.3 = bf16[16,32,128]{2,1,0:T(8,128)(2,1)S(1)} collective-permute-done((bf16[16,32,128]{2,1,0:T(8,128)(2,1)}, bf16[16,32,128]{2,1,0:T(8,128)(2,1)S(1)}, u32[]{:S(2)}, u32[]{:S(2)}) %collective-permute-start.3) | collective-permute-done | bytes 131104 | tf_op jit(solution)/shard_map/ppermute | solution.py:240
  29.3 1.7 constant_dynamic-update-slice_fusion.9
  31.0 1.8 collective-permute-start.9
  33.9 1.7 constant_dynamic-update-slice_fusion.4
  36.2 11.1 %collective-permute-done.5 = bf16[1,16,32,128]{3,2,1,0:T(8,128)(2,1)S(1)} collective-permute-done((bf16[1,16,32,128]{3,2,1,0:T(8,128)(2,1)S(1)}, bf16[1,16,32,128]{3,2,1,0:T(8,128)(2,1)S(1)}, u32[]{:S(2)}, u32[]{:S(2)}) %collective-permute-start.5) | collective-permute-done | bytes 131104 | tf_op jit(solution)/shard_map/ppermute | solution.py:142
  47.3 1.7 collective-permute-done.9
  49.7 3.3 %collective-permute-done.10 = bf16[32,4096]{1,0:T(8,128)(2,1)S(1)} collective-permute-done((bf16[32,4096]{1,0:T(8,128)(2,1)}, bf16[32,4096]{1,0:T(8,128)(2,1)S(1)}, u32[]{:S(2)}, u32[]{:S(2)}) %collective-permute-start.10) | collective-permute-done | bytes 262176 | tf_op jit(solution)/shard_map/ppermute | solution.py:142
  53.1 2.9 collective-permute-start.14
  56.7 13.2 %collective-permute-done.11 = bf16[32,4096]{1,0:T(8,128)(2,1)S(1)} collective-permute-done((bf16[32,4096]{1,0:T(8,128)(2,1)}, bf16[32,4096]{1,0:T(8,128)(2,1)S(1)}, u32[]{:S(2)}, u32[]{:S(2)}) %collective-permute-start.11) | collective-permute-done | bytes 262176 | tf_op jit(solution)/shard_map/ppermute | solution.py:142
  69.9 2.0 collective-permute-start.15
  72.7 2.1 constant_dynamic-slice_fusion
  74.7 2.3 copy.16
  77.7 5.2 %copy-done = bf16[2048,3584]{1,0:T(8,128)(2,1)S(1)} copy-done((bf16[2048,3584]{1,0:T(8,128)(2,1)S(1)}, bf16[2048,3584]{1,0:T(8,128)(2,1)}, u32[]{:S(2)}) %copy-start) | copy-done | bytes 14680088
  82.9 6.2 %gate_up.15 = (bf16[2,128,1024]{2,1,0:T(8,128)(2,1)S(1)}, bf16[2,128,1024]{2,1,0:T(8,128)(2,1)}) custom-call(s32[2]{0:T(128)S(1)} %get-tuple-element.53.idx_ref, bf16[128,8192]{1,0:T(8,128)(2,1)S(1)} %copy-done.6, bf16[128,2048]{1,0:T(8,128)(2,1)S(1)} %collective-permute-done.17.bottom_ref, bf16[2048,3584]{1,0:T(8,128)(2,1)S(1)} %copy-done, ...), custom_call_target="tpu_custom_call" | custom-call | flops 2147483648 | bytes 10485760 | tf_op jit(solution)/shard_map/gate_up/pallas_call | solution.py:45
  90.7 5.3 %gate_up.13 = (bf16[2,128,768]{2,1,0:T(8,128)(2,1)S(1)}, bf16[2,128,768]{2,1,0:T(8,128)(2,1)}) custom-call(s32[2]{0:T(128)S(1)} %copy-done.9, bf16[128,8192]{1,0:T(8,128)(2,1)S(1)} %copy-done.6, bf16[128,2048]{1,0:T(8,128)(2,1)S(1)} %collective-permute-done.17.bottom_ref, bf16[2048,3584]{1,0:T(8,128)(2,1)S(1)} %copy-done, bf16[2048,3584]{1,0:T(8,128)(2,1)} %up_ref.15), custom_call_target="tpu_custom_call" | custom-call | flops 1610612736 | bytes 8126464 | tf_op jit(solution)/shard_map/gate_up/pallas_call | solution.py:45
  96.4 1.7 constant_dynamic-update-slice_fusion.2
  98.1 1.7 constant_dynamic-update-slice_fusion.1
  99.8 2.3 copy.17
  102.1 1.6 broadcast_in_dim.15
  105.8 5.2 %copy-done.1 = bf16[2048,3584]{1,0:T(8,128)(2,1)S(1)} copy-done((bf16[2048,3584]{1,0:T(8,128)(2,1)S(1)}, bf16[2048,3584]{1,0:T(8,128)(2,1)}, u32[]{:S(2)}) %copy-start.1) | copy-done | bytes 14680088
  111.0 4.6 %gate_up.8 = (bf16[2,128,768]{2,1,0:T(8,128)(2,1)S(1)}, bf16[2,128,768]{2,1,0:T(8,128)(2,1)S(1)}) custom-call(s32[2]{0:T(128)S(1)} %get-tuple-element.50.idx_ref, bf16[128,8192]{1,0:T(8,128)(2,1)S(1)} %copy-done.6, bf16[128,2048]{1,0:T(8,128)(2,1)S(1)} %collective-permute-done.17.bottom_ref, bf16[2048,3584]{1,0:T(8,128)(2,1)S(1)} %copy-done.1, ...), custom_call_target="tpu_custom_call" | custom-call | flops 1610612736 | bytes 8126464 | tf_op jit(solution)/shard_map/gate_up/pallas_call | solution.py:45
  115.7 6.6 %gate_up.10 = (bf16[2,128,1024]{2,1,0:T(8,128)(2,1)S(1)}, bf16[2,128,1024]{2,1,0:T(8,128)(2,1)S(1)}) custom-call(s32[2]{0:T(128)S(1)} %get-tuple-element.52.idx_ref, bf16[128,8192]{1,0:T(8,128)(2,1)S(1)} %copy-done.6, bf16[128,2048]{1,0:T(8,128)(2,1)S(1)} %collective-permute-done.17.bottom_ref, bf16[2048,3584]{1,0:T(8,128)(2,1)S(1)} %copy-done.1, ...), custom_call_target="tpu_custom_call" | custom-call | flops 2147483648 | bytes 10485760 | tf_op jit(solution)/shard_map/gate_up/pallas_call | solution.py:45
  123.5 3.1 %collective-permute-start.29 = (bf16[2,128,768]{2,1,0:T(8,128)(2,1)S(1)}, bf16[2,128,768]{2,1,0:T(8,128)(2,1)S(1)}, u32[]{:S(2)}, u32[]{:S(2)}) collective-permute-start(bf16[2,128,768]{2,1,0:T(8,128)(2,1)S(1)} %add_convert_fusion.2), channel_id=1, source_target_pairs={{0,8},{4,12},{8,0},{12,4},{1,9},{5,13},{9,1},{13,5},{2,10},{6,14},... | collective-permute-start | bytes 1179656 | tf_op jit(solution)/shard_map/ppermute | solution.py:132
  126.6 6.8 %gate_up.14 = (bf16[2,128,1024]{2,1,0:T(8,128)(2,1)S(1)}, bf16[2,128,1024]{2,1,0:T(8,128)(2,1)S(1)}) custom-call(s32[2]{0:T(128)S(1)} %get-tuple-element.46.idx_ref, bf16[128,2048]{1,0:T(8,128)(2,1)S(1)} %get-tuple-element.45.top_ref, bf16[128,2048]{1,0:T(8,128)(2,1)} %collective-permute-done.19.bottom_ref, bf16[2048,3584]{1,0:T(8,128)(2,1)S(1)} %bitcast.106, ...), custom_call_target="tpu_custom_call" | custom-call | flops 2147483648 | bytes 10485760 | tf_op jit(solution)/shard_map/gate_up/pallas_call | solution.py:45
  133.8 5.2 %copy-done.4 = bf16[2048,3584]{1,0:T(8,128)(2,1)S(1)} copy-done((bf16[2048,3584]{1,0:T(8,128)(2,1)S(1)}, bf16[2048,3584]{1,0:T(8,128)(2,1)}, u32[]{:S(2)}) %copy-start.4) | copy-done | bytes 14680088
  139.0 4.1 %gate_up.12 = (bf16[2,128,768]{2,1,0:T(8,128)(2,1)S(1)}, bf16[2,128,768]{2,1,0:T(8,128)(2,1)S(1)}) custom-call(s32[2]{0:T(128)S(1)} %get-tuple-element.47.idx_ref, bf16[128,2048]{1,0:T(8,128)(2,1)S(1)} %get-tuple-element.45.top_ref, bf16[128,2048]{1,0:T(8,128)(2,1)} %collective-permute-done.19.bottom_ref, bf16[2048,3584]{1,0:T(8,128)(2,1)S(1)} %bitcast.108, ...), custom_call_target="tpu_custom_call" | custom-call | flops 1610612736 | bytes 8126464 | tf_op jit(solution)/shard_map/gate_up/pallas_call | solution.py:45
  144.8 5.2 %copy-done.2 = bf16[2048,3584]{1,0:T(8,128)(2,1)S(1)} copy-done((bf16[2048,3584]{1,0:T(8,128)(2,1)S(1)}, bf16[2048,3584]{1,0:T(8,128)(2,1)}, u32[]{:S(2)}) %copy-start.2) | copy-done | bytes 14680088
  150.0 5.2 %copy-done.5 = bf16[2048,3584]{1,0:T(8,128)(2,1)S(1)} copy-done((bf16[2048,3584]{1,0:T(8,128)(2,1)S(1)}, bf16[2048,3584]{1,0:T(8,128)(2,1)}, u32[]{:S(2)}) %copy-start.5) | copy-done | bytes 14680088
  155.1 4.1 %gate_up.9 = (bf16[2,128,768]{2,1,0:T(8,128)(2,1)S(1)}, bf16[2,128,768]{2,1,0:T(8,128)(2,1)S(1)}) custom-call(s32[2]{0:T(128)S(1)} %copy-done.11, bf16[128,2048]{1,0:T(8,128)(2,1)S(1)} %get-tuple-element.45.top_ref, bf16[128,2048]{1,0:T(8,128)(2,1)} %collective-permute-done.19.bottom_ref, bf16[2048,3584]{1,0:T(8,128)(2,1)S(1)} %copy-done.2, ...), custom_call_target="tpu_custom_call" | custom-call | flops 1610612736 | bytes 8126464 | tf_op jit(solution)/shard_map/gate_up/pallas_call | solution.py:45
  159.3 5.2 %copy-done.3 = bf16[2048,3584]{1,0:T(8,128)(2,1)S(1)} copy-done((bf16[2048,3584]{1,0:T(8,128)(2,1)S(1)}, bf16[2048,3584]{1,0:T(8,128)(2,1)}, u32[]{:S(2)}) %copy-start.3) | copy-done | bytes 14680088
  164.5 7.2 %gate_up.11 = (bf16[2,128,1024]{2,1,0:T(8,128)(2,1)S(1)}, bf16[2,128,1024]{2,1,0:T(8,128)(2,1)S(1)}) custom-call(s32[2]{0:T(128)S(1)} %copy-done.10, bf16[128,2048]{1,0:T(8,128)(2,1)S(1)} %get-tuple-element.45.top_ref, bf16[128,2048]{1,0:T(8,128)(2,1)} %collective-permute-done.19.bottom_ref, bf16[2048,3584]{1,0:T(8,128)(2,1)S(1)} %copy-done.3, ...), custom_call_target="tpu_custom_call" | custom-call | flops 2147483648 | bytes 10485760 | tf_op jit(solution)/shard_map/gate_up/pallas_call | solution.py:45
  172.5 1.7 collective-permute-done.20
  175.1 1.7 collective-permute-start.21
  177.6 8.3 %collective-permute-done.21 = bf16[2,128,768]{2,1,0:T(8,128)(2,1)S(1)} collective-permute-done((bf16[2,128,768]{2,1,0:T(8,128)(2,1)S(1)}, bf16[2,128,768]{2,1,0:T(8,128)(2,1)S(1)}, u32[]{:S(2)}, u32[]{:S(2)}) %collective-permute-start.21) | collective-permute-done | bytes 393248 | tf_op jit(solution)/shard_map/ppermute | solution.py:132
  185.9 1.6 collective-permute-start.16
  187.6 1.8 collective-permute-start.30
  189.8 11.5 %collective-permute-done.30.mine_ref = bf16[128,768]{1,0:T(8,128)(2,1)S(1)} collective-permute-done((bf16[128,768]{1,0:T(8,128)(2,1)S(1)}, bf16[128,768]{1,0:T(8,128)(2,1)S(1)}, u32[]{:S(2)}, u32[]{:S(2)}) %collective-permute-start.30) | collective-permute-done | bytes 196640 | tf_op jit(solution)/shard_map/ppermute | solution.py:132
  202.6 1.5 collective-permute-start.42
  204.4 3.8 %collective-permute-done.35.mine_ref = bf16[128,1024]{1,0:T(8,128)(2,1)S(1)} collective-permute-done((bf16[128,1024]{1,0:T(8,128)(2,1)S(1)}, bf16[128,1024]{1,0:T(8,128)(2,1)S(1)}, u32[]{:S(2)}, u32[]{:S(2)}) %collective-permute-start.35) | collective-permute-done | bytes 262176 | tf_op jit(solution)/shard_map/ppermute | solution.py:132
  209.3 2.5 collective-permute-start.36
  212.7 3.9 %collective-permute-start.26 = (bf16[128,1024]{1,0:T(8,128)(2,1)S(1)}, bf16[128,1024]{1,0:T(8,128)(2,1)S(1)}, u32[]{:S(2)}, u32[]{:S(2)}) collective-permute-start(bf16[128,1024]{1,0:T(8,128)(2,1)S(1)} %fusion.13.mine_ref), channel_id=1, source_target_pairs={{0,4},{4,0},{8,12},{12,8},{1,5},{5,1},{9,13},{13,9},{2,6},{6,2},{1... | collective-permute-start | bytes 786440 | tf_op jit(solution)/shard_map/ppermute | solution.py:128
  216.8 3.0 down_add.12.total_ref
  219.8 2.2 down_add.13.total_ref
  222.6 2.9 down_add.8.total_ref
  225.6 2.2 down_add.9.total_ref
  227.9 2.9 down_add.10.total_ref
  230.9 2.2 down_add.11
  233.1 2.8 down_add.14.total_ref
  235.9 2.1 down_add.15
  238.1 2.5 pad_maximum_fusion.1
  240.6 5.5 %copy.21 = f32[512,2048]{0,1:T(8,128)} copy(f32[512,2048]{1,0:T(8,128)} %pad_maximum_fusion.1) | data formatting | bytes 8388608 | tf_op jit(solution)/shard_map/concatenate | solution.py:252
  246.1 4.0 %pad_maximum_fusion = bf16[512,8192]{0,1:T(8,128)(2,1)S(1)} fusion(bf16[128,8192]{0,1:T(8,128)(2,1)} %collective-permute-done.16, bf16[128,8192]{0,1:T(8,128)(2,1)} %constant_dynamic-update-slice_fusion, bf16[128,8192]{0,1:T(8,128)(2,1)} %collective-permute-done.7, bf16[128,8192]{0,1:T(8,128)(2,1)S(1)} %copy-done.13), kind=kLoop, calls=%fused_computation | loop fusion | flops 33554432 | bytes 16777216 | tf_op jit(solution)/shard_map/concatenate | solution.py:230
  251.4 2.8 fusion.5
  256.1 2.3 fusion.2
  264.3 2.2 collective-permute-start.48
  266.4 2.3 collective-permute-start.49
  268.7 7.0 %collective-permute-done.45 = bf16[16,32,128]{2,1,0:T(8,128)(2,1)S(1)} collective-permute-done((bf16[16,32,128]{2,1,0:T(8,128)(2,1)}, bf16[16,32,128]{2,1,0:T(8,128)(2,1)S(1)}, u32[]{:S(2)}, u32[]{:S(2)}) %collective-permute-start.45) | collective-permute-done | bytes 131104 | tf_op jit(solution)/shard_map/ppermute | solution.py:155
  275.8 7.7 %collective-permute-start.46 = (f32[16,32,128]{2,1,0:T(8,128)S(1)}, f32[16,32,128]{2,1,0:T(8,128)S(1)}, u32[]{:S(2)}, u32[]{:S(2)}) collective-permute-start(f32[16,32,128]{2,1,0:T(8,128)S(1)} %fusion.25), channel_id=1, source_target_pairs={{0,0},{4,1},{8,2},{12,3},{1,4},{5,5},{9,6},{13,7},{2,8},{6,9},{10,... | collective-permute-start | bytes 786440 | tf_op jit(solution)/shard_map/ppermute | solution.py:271
  284.4 13.1 %collective-permute-done.46 = f32[16,32,128]{2,1,0:T(8,128)S(1)} collective-permute-done((f32[16,32,128]{2,1,0:T(8,128)S(1)}, f32[16,32,128]{2,1,0:T(8,128)S(1)}, u32[]{:S(2)}, u32[]{:S(2)}) %collective-permute-start.46) | collective-permute-done | bytes 262176 | tf_op jit(solution)/shard_map/ppermute | solution.py:271
  (185 shorter events, 42.7 us)
Async XLA Ops:
  0.6 9.4 %copy-start.6 = (bf16[128,8192]{1,0:T(8,128)(2,1)S(1)}, bf16[128,8192]{1,0:T(8,128)(2,1)}, u32[]{:S(2)}) copy-start(bf16[128,8192]{1,0:T(8,128)(2,1)} %top_ref.7) | copy-start | bytes 6291460
  0.6 14.3 %collective-permute-start = (bf16[16,32,64]{2,0,1:T(8,128)(2,1)}, bf16[16,32,64]{2,0,1:T(8,128)(2,1)}, u32[]{:S(2)}, u32[]{:S(2)}) collective-permute-start(bf16[16,32,64]{2,0,1:T(8,128)(2,1)} %bitcast.119), channel_id=1, source_target_pairs={{0,1},{1,2},{2,3},{3,0},{4,5},{5,6},{6,7},{7,4},{8,9},{9,10},{10,1... | collective-permute-start | bytes 196616 | tf_op jit(solution)/shard_map/ppermute | solution.py:142
  2.0 14.0 %collective-permute-start.1 = (bf16[16,32,64]{2,0,1:T(8,128)(2,1)}, bf16[16,32,64]{2,0,1:T(8,128)(2,1)}, u32[]{:S(2)}, u32[]{:S(2)}) collective-permute-start(bf16[16,32,64]{2,0,1:T(8,128)(2,1)} %bitcast.120), channel_id=1, source_target_pairs={{0,2},{1,3},{2,0},{3,1},{4,6},{5,7},{6,4},{7,5},{8,10},{9,11},{10,... | collective-permute-start | bytes 196616 | tf_op jit(solution)/shard_map/ppermute | solution.py:142
  2.0 19.5 %collective-permute-start.2 = (bf16[16,32,64]{2,0,1:T(8,128)(2,1)}, bf16[16,32,64]{2,0,1:T(8,128)(2,1)}, u32[]{:S(2)}, u32[]{:S(2)}) collective-permute-start(bf16[16,32,64]{2,0,1:T(8,128)(2,1)} %bitcast.121), channel_id=1, source_target_pairs={{0,3},{1,0},{2,1},{3,2},{4,7},{5,4},{6,5},{7,6},{8,11},{9,8},{10,9... | collective-permute-start | bytes 196616 | tf_op jit(solution)/shard_map/ppermute | solution.py:142
  5.3 22.9 %collective-permute-start.8 = (bf16[32,4096]{1,0:T(8,128)(2,1)}, bf16[32,4096]{1,0:T(8,128)(2,1)}, u32[]{:S(2)}, u32[]{:S(2)}) collective-permute-start(bf16[32,4096]{1,0:T(8,128)(2,1)} %get-tuple-element.37), channel_id=1, source_target_pairs={{0,8},{4,12},{8,0},{12,4},{1,9},{5,13},{9,1},{13,5},{2,10},{6,14},... | collective-permute-start | bytes 786440 | tf_op jit(solution)/shard_map/ppermute | solution.py:132
  8.4 68.6 %collective-permute-start.17 = (bf16[128,2048]{1,0:T(8,128)(2,1)}, bf16[128,2048]{1,0:T(8,128)(2,1)S(1)}, u32[]{:S(2)}, u32[]{:S(2)}) collective-permute-start(bf16[128,2048]{1,0:T(8,128)(2,1)} %constant_dynamic-slice_fusion.2), channel_id=1, source_target_pairs={{0,4},{4,0},{8,12},{12,8},{1,5},{5,1},{9,13},{13,9},{2,6},{6,2},{1... | collective-permute-start | bytes 1572872 | tf_op jit(solution)/shard_map/ppermute | solution.py:128
  14.9 16.1 %collective-permute-start.12 = (bf16[32,4096]{1,0:T(8,128)(2,1)S(1)}, bf16[32,4096]{1,0:T(8,128)(2,1)}, u32[]{:S(2)}, u32[]{:S(2)}) collective-permute-start(bf16[32,4096]{1,0:T(8,128)(2,1)S(1)} %get-tuple-element.36), channel_id=1, source_target_pairs={{0,8},{4,12},{8,0},{12,4},{1,9},{5,13},{9,1},{13,5},{2,10},{6,14},... | collective-permute-start | bytes 786440 | tf_op jit(solution)/shard_map/ppermute | solution.py:132
  16.0 11.3 %collective-permute-start.3 = (bf16[16,32,128]{2,1,0:T(8,128)(2,1)}, bf16[16,32,128]{2,1,0:T(8,128)(2,1)S(1)}, u32[]{:S(2)}, u32[]{:S(2)}) collective-permute-start(bf16[16,32,128]{2,1,0:T(8,128)(2,1)} %param.10), channel_id=1, source_target_pairs={{0,0},{1,4},{2,8},{3,12},{4,1},{5,5},{6,9},{7,13},{8,2},{9,6},{10,... | collective-permute-start | bytes 393224 | tf_op jit(solution)/shard_map/ppermute | solution.py:240
  21.6 224.5 %collective-permute-start.7 = (bf16[128,8192]{0,1:T(8,128)(2,1)}, bf16[128,8192]{0,1:T(8,128)(2,1)}, u32[]{:S(2)}, u32[]{:S(2)}) collective-permute-start(bf16[128,8192]{0,1:T(8,128)(2,1)} %copy.18), channel_id=1, source_target_pairs={{0,4},{4,0},{8,12},{12,8},{1,5},{5,1},{9,13},{13,9},{2,6},{6,2},{1... | collective-permute-start | bytes 6291464 | tf_op jit(solution)/shard_map/ppermute | solution.py:128
  23.8 12.4 %copy-start.14 = (bf16[64,32,64]{2,0,1:T(8,128)(2,1)}, bf16[64,32,64]{2,0,1:T(8,128)(2,1)S(1)}, u32[]{:S(2)}) copy-start(bf16[64,32,64]{2,0,1:T(8,128)(2,1)S(1)} %constant_dynamic-update-slice_fusion.14) | copy-start | bytes 786436
  27.3 8.9 %copy-start.20 = (bf16[16,32,128]{2,1,0:T(8,128)(2,1)}, bf16[16,32,128]{2,1,0:T(8,128)(2,1)S(1)}, u32[]{:S(2)}) copy-start(bf16[16,32,128]{2,1,0:T(8,128)(2,1)S(1)} %collective-permute-done.3) | copy-start | bytes 393220
  27.3 8.4 %collective-permute-start.4 = (bf16[1,16,32,128]{3,2,1,0:T(8,128)(2,1)S(1)}, bf16[1,16,32,128]{3,2,1,0:T(8,128)(2,1)S(1)}, u32[]{:S(2)}, u32[]{:S(2)}) collective-permute-start(bf16[1,16,32,128]{3,2,1,0:T(8,128)(2,1)S(1)} %bitcast.122), channel_id=1, source_target_pairs={{0,1},{1,2},{2,3},{3,0},{4,5},{5,6},{6,7},{7,4},{8,9},{9,10},{10,1... | collective-permute-start | bytes 393224 | tf_op jit(solution)/shard_map/ppermute | solution.py:142
  28.2 19.1 %collective-permute-start.5 = (bf16[1,16,32,128]{3,2,1,0:T(8,128)(2,1)S(1)}, bf16[1,16,32,128]{3,2,1,0:T(8,128)(2,1)S(1)}, u32[]{:S(2)}, u32[]{:S(2)}) collective-permute-start(bf16[1,16,32,128]{3,2,1,0:T(8,128)(2,1)S(1)} %bitcast.123), channel_id=1, source_target_pairs={{0,2},{1,3},{2,0},{3,1},{4,6},{5,7},{6,4},{7,5},{8,10},{9,11},{10,... | collective-permute-start | bytes 393224 | tf_op jit(solution)/shard_map/ppermute | solution.py:142
  31.0 18.0 %collective-permute-start.9 = (bf16[32,4096]{1,0:T(8,128)(2,1)}, bf16[32,4096]{1,0:T(8,128)(2,1)S(1)}, u32[]{:S(2)}, u32[]{:S(2)}) collective-permute-start(bf16[32,4096]{1,0:T(8,128)(2,1)} %collective-permute-done.8), channel_id=1, source_target_pairs={{0,1},{1,2},{2,3},{3,0},{4,5},{5,6},{6,7},{7,4},{8,9},{9,10},{10,1... | collective-permute-start | bytes 786440 | tf_op jit(solution)/shard_map/ppermute | solution.py:142
  35.6 17.4 %collective-permute-start.10 = (bf16[32,4096]{1,0:T(8,128)(2,1)}, bf16[32,4096]{1,0:T(8,128)(2,1)S(1)}, u32[]{:S(2)}, u32[]{:S(2)}) collective-permute-start(bf16[32,4096]{1,0:T(8,128)(2,1)} %collective-permute-done.8), channel_id=1, source_target_pairs={{0,2},{1,3},{2,0},{3,1},{4,6},{5,7},{6,4},{7,5},{8,10},{9,11},{10,... | collective-permute-start | bytes 786440 | tf_op jit(solution)/shard_map/ppermute | solution.py:142
  47.3 22.6 %collective-permute-start.11 = (bf16[32,4096]{1,0:T(8,128)(2,1)}, bf16[32,4096]{1,0:T(8,128)(2,1)S(1)}, u32[]{:S(2)}, u32[]{:S(2)}) collective-permute-start(bf16[32,4096]{1,0:T(8,128)(2,1)} %collective-permute-done.8), channel_id=1, source_target_pairs={{0,3},{1,0},{2,1},{3,2},{4,7},{5,4},{6,5},{7,6},{8,11},{9,8},{10,9... | collective-permute-start | bytes 786440 | tf_op jit(solution)/shard_map/ppermute | solution.py:142
  47.3 24.6 %copy-start.18 = (bf16[4,16,32,128]{3,2,1,0:T(8,128)(2,1)}, bf16[4,16,32,128]{3,2,1,0:T(8,128)(2,1)S(1)}, u32[]{:S(2)}) copy-start(bf16[4,16,32,128]{3,2,1,0:T(8,128)(2,1)S(1)} %constant_dynamic-update-slice_fusion.11) | copy-start | bytes 1572868
  49.0 40.9 %collective-permute-start.13 = (bf16[32,4096]{1,0:T(8,128)(2,1)}, bf16[32,4096]{1,0:T(8,128)(2,1)S(1)}, u32[]{:S(2)}, u32[]{:S(2)}) collective-permute-start(bf16[32,4096]{1,0:T(8,128)(2,1)} %collective-permute-done.12), channel_id=1, source_target_pairs={{0,1},{1,2},{2,3},{3,0},{4,5},{5,6},{6,7},{7,4},{8,9},{9,10},{10,1... | collective-permute-start | bytes 786440 | tf_op jit(solution)/shard_map/ppermute | solution.py:142
  53.1 42.9 %collective-permute-start.14 = (bf16[32,4096]{1,0:T(8,128)(2,1)}, bf16[32,4096]{1,0:T(8,128)(2,1)}, u32[]{:S(2)}, u32[]{:S(2)}) collective-permute-start(bf16[32,4096]{1,0:T(8,128)(2,1)} %collective-permute-done.12), channel_id=1, source_target_pairs={{0,2},{1,3},{2,0},{3,1},{4,6},{5,7},{6,4},{7,5},{8,10},{9,11},{10,... | collective-permute-start | bytes 786440 | tf_op jit(solution)/shard_map/ppermute | solution.py:142
  69.9 28.2 %collective-permute-start.15 = (bf16[32,4096]{1,0:T(8,128)(2,1)}, bf16[32,4096]{1,0:T(8,128)(2,1)}, u32[]{:S(2)}, u32[]{:S(2)}) collective-permute-start(bf16[32,4096]{1,0:T(8,128)(2,1)} %collective-permute-done.12), channel_id=1, source_target_pairs={{0,3},{1,0},{2,1},{3,2},{4,7},{5,4},{6,5},{7,6},{8,11},{9,8},{10,9... | collective-permute-start | bytes 786440 | tf_op jit(solution)/shard_map/ppermute | solution.py:142
  77.0 49.6 %collective-permute-start.19 = (bf16[128,2048]{1,0:T(8,128)(2,1)}, bf16[128,2048]{1,0:T(8,128)(2,1)}, u32[]{:S(2)}, u32[]{:S(2)}) collective-permute-start(bf16[128,2048]{1,0:T(8,128)(2,1)} %get-tuple-element.44), channel_id=1, source_target_pairs={{0,4},{4,0},{8,12},{12,8},{1,5},{5,1},{9,13},{13,9},{2,6},{6,2},{1... | collective-permute-start | bytes 1572872 | tf_op jit(solution)/shard_map/ppermute | solution.py:128
  82.9 7.8 %copy-start.9 = (s32[2]{0:T(128)S(1)}, s32[2]{0:T(128)}, u32[]{:S(2)}) copy-start(s32[2]{0:T(128)} %get-tuple-element.51.idx_ref) | copy-start | bytes 28
  89.9 53.5 %collective-permute-start.33 = (bf16[2,128,1024]{2,1,0:T(8,128)(2,1)}, bf16[2,128,1024]{2,1,0:T(8,128)(2,1)}, u32[]{:S(2)}, u32[]{:S(2)}) collective-permute-start(bf16[2,128,1024]{2,1,0:T(8,128)(2,1)} %get-tuple-element.33), channel_id=1, source_target_pairs={{0,4},{4,0},{8,12},{12,8},{1,5},{5,1},{9,13},{13,9},{2,6},{6,2},{1... | collective-permute-start | bytes 1572872 | tf_op jit(solution)/shard_map/ppermute | solution.py:128
  95.9 26.4 %collective-permute-start.28 = (bf16[2,128,768]{2,1,0:T(8,128)(2,1)}, bf16[2,128,768]{2,1,0:T(8,128)(2,1)}, u32[]{:S(2)}, u32[]{:S(2)}) collective-permute-start(bf16[2,128,768]{2,1,0:T(8,128)(2,1)} %get-tuple-element.29), channel_id=1, source_target_pairs={{0,4},{4,0},{8,12},{12,8},{1,5},{5,1},{9,13},{13,9},{2,6},{6,2},{1... | collective-permute-start | bytes 1179656 | tf_op jit(solution)/shard_map/ppermute | solution.py:128
  115.7 10.9 %slice-start = ((s8[14680064]{0:T(1024)(128)(4,1)}), s8[4194304]{0:T(1024)(128)(4,1)S(1)}, s32[]{:S(2)}) async-start(s8[14680064]{0:T(1024)(128)(4,1)} %bitcast.105), calls=%async_computation | async-start | bytes 8388608
  115.7 10.9 %slice-start.1 = ((s8[14680064]{0:T(1024)(128)(4,1)}), s8[4194304]{0:T(1024)(128)(4,1)S(1)}, s32[]{:S(2)}) async-start(s8[14680064]{0:T(1024)(128)(4,1)} %bitcast.105), calls=%async_computation.1 | async-start | bytes 8388608
  115.7 10.9 %slice-start.2 = ((s8[14680064]{0:T(1024)(128)(4,1)}), s8[4194304]{0:T(1024)(128)(4,1)S(1)}, s32[]{:S(2)}) async-start(s8[14680064]{0:T(1024)(128)(4,1)} %bitcast.105), calls=%async_computation.2 | async-start | bytes 8388608
  115.7 10.9 %slice-start.3 = ((s8[14680064]{0:T(1024)(128)(4,1)}), s8[2097152]{0:T(1024)(128)(4,1)S(1)}, s32[]{:S(2)}) async-start(s8[14680064]{0:T(1024)(128)(4,1)} %bitcast.105), calls=%async_computation.3 | async-start | bytes 4194304
  123.5 48.2 %collective-permute-start.29 = (bf16[2,128,768]{2,1,0:T(8,128)(2,1)S(1)}, bf16[2,128,768]{2,1,0:T(8,128)(2,1)S(1)}, u32[]{:S(2)}, u32[]{:S(2)}) collective-permute-start(bf16[2,128,768]{2,1,0:T(8,128)(2,1)S(1)} %add_convert_fusion.2), channel_id=1, source_target_pairs={{0,8},{4,12},{8,0},{12,4},{1,9},{5,13},{9,1},{13,5},{2,10},{6,14},... | collective-permute-start | bytes 1179656 | tf_op jit(solution)/shard_map/ppermute | solution.py:132
  133.5 41.7 %collective-permute-start.32 = (bf16[2,128,1024]{2,1,0:T(8,128)(2,1)S(1)}, bf16[2,128,1024]{2,1,0:T(8,128)(2,1)S(1)}, u32[]{:S(2)}, u32[]{:S(2)}) collective-permute-start(bf16[2,128,1024]{2,1,0:T(8,128)(2,1)S(1)} %get-tuple-element.31), channel_id=1, source_target_pairs={{0,4},{4,0},{8,12},{12,8},{1,5},{5,1},{9,13},{13,9},{2,6},{6,2},{1... | collective-permute-start | bytes 1572872 | tf_op jit(solution)/shard_map/ppermute | solution.py:128
  143.1 28.9 %collective-permute-start.27 = (bf16[2,128,768]{2,1,0:T(8,128)(2,1)S(1)}, bf16[2,128,768]{2,1,0:T(8,128)(2,1)S(1)}, u32[]{:S(2)}, u32[]{:S(2)}) collective-permute-start(bf16[2,128,768]{2,1,0:T(8,128)(2,1)S(1)} %get-tuple-element.27), channel_id=1, source_target_pairs={{0,4},{4,0},{8,12},{12,8},{1,5},{5,1},{9,13},{13,9},{2,6},{6,2},{1... | collective-permute-start | bytes 1179656 | tf_op jit(solution)/shard_map/ppermute | solution.py:128
  144.7 32.1 %collective-permute-start.34 = (bf16[2,128,1024]{2,1,0:T(8,128)(2,1)S(1)}, bf16[2,128,1024]{2,1,0:T(8,128)(2,1)S(1)}, u32[]{:S(2)}, u32[]{:S(2)}) collective-permute-start(bf16[2,128,1024]{2,1,0:T(8,128)(2,1)S(1)} %add_convert_fusion), channel_id=1, source_target_pairs={{0,8},{4,12},{8,0},{12,4},{1,9},{5,13},{9,1},{13,5},{2,10},{6,14},... | collective-permute-start | bytes 1572872 | tf_op jit(solution)/shard_map/ppermute | solution.py:132
  164.5 52.3 %slice-start.8 = ((s8[14680064]{0:T(1024)(128)(4,1)}), s8[4194304]{0:T(1024)(128)(4,1)S(1)}, s32[]{:S(2)}) async-start(s8[14680064]{0:T(1024)(128)(4,1)} %bitcast.109), calls=%async_computation.8 | async-start | bytes 8388608
  164.5 52.4 %slice-start.9 = ((s8[14680064]{0:T(1024)(128)(4,1)}), s8[4194304]{0:T(1024)(128)(4,1)S(1)}, s32[]{:S(2)}) async-start(s8[14680064]{0:T(1024)(128)(4,1)} %bitcast.109), calls=%async_computation.9 | async-start | bytes 8388608
  164.5 52.4 %slice-start.10 = ((s8[14680064]{0:T(1024)(128)(4,1)}), s8[4194304]{0:T(1024)(128)(4,1)S(1)}, s32[]{:S(2)}) async-start(s8[14680064]{0:T(1024)(128)(4,1)} %bitcast.109), calls=%async_computation.10 | async-start | bytes 8388608
  171.7 3.0 collective-permute-start.24
  172.1 2.1 collective-permute-start.20
  174.2 15.3 %collective-permute-start.23 = (bf16[2,128,1024]{2,1,0:T(8,128)(2,1)S(1)}, bf16[2,128,1024]{2,1,0:T(8,128)(2,1)S(1)}, u32[]{:S(2)}, u32[]{:S(2)}) collective-permute-start(bf16[2,128,1024]{2,1,0:T(8,128)(2,1)S(1)} %get-tuple-element.23), channel_id=1, source_target_pairs={{0,4},{4,0},{8,12},{12,8},{1,5},{5,1},{9,13},{13,9},{2,6},{6,2},{1... | collective-permute-start | bytes 1572872 | tf_op jit(solution)/shard_map/ppermute | solution.py:128
  174.6 2.7 collective-permute-start.18
  175.1 10.8 %collective-permute-start.21 = (bf16[2,128,768]{2,1,0:T(8,128)(2,1)S(1)}, bf16[2,128,768]{2,1,0:T(8,128)(2,1)S(1)}, u32[]{:S(2)}, u32[]{:S(2)}) collective-permute-start(bf16[2,128,768]{2,1,0:T(8,128)(2,1)S(1)} %add_convert_fusion.3), channel_id=1, source_target_pairs={{0,8},{4,12},{8,0},{12,4},{1,9},{5,13},{9,1},{13,5},{2,10},{6,14},... | collective-permute-start | bytes 1179656 | tf_op jit(solution)/shard_map/ppermute | solution.py:132
  176.8 25.8 %collective-permute-start.25 = (bf16[2,128,1024]{2,1,0:T(8,128)(2,1)S(1)}, bf16[2,128,1024]{2,1,0:T(8,128)(2,1)S(1)}, u32[]{:S(2)}, u32[]{:S(2)}) collective-permute-start(bf16[2,128,1024]{2,1,0:T(8,128)(2,1)S(1)} %add_convert_fusion.1), channel_id=1, source_target_pairs={{0,8},{4,12},{8,0},{12,4},{1,9},{5,13},{9,1},{13,5},{2,10},{6,14},... | collective-permute-start | bytes 1572872 | tf_op jit(solution)/shard_map/ppermute | solution.py:132
  176.9 39.9 %slice-start.11 = ((s8[14680064]{0:T(1024)(128)(4,1)}), s8[2097152]{0:T(1024)(128)(4,1)S(1)}, s32[]{:S(2)}) async-start(s8[14680064]{0:T(1024)(128)(4,1)} %bitcast.109), calls=%async_computation.11 | async-start | bytes 4194304
  177.3 10.2 %collective-permute-start.6 = (bf16[1,16,32,128]{3,2,1,0:T(8,128)(2,1)S(1)}, bf16[1,16,32,128]{3,2,1,0:T(8,128)(2,1)S(1)}, u32[]{:S(2)}, u32[]{:S(2)}) collective-permute-start(bf16[1,16,32,128]{3,2,1,0:T(8,128)(2,1)S(1)} %bitcast.124), channel_id=1, source_target_pairs={{0,3},{1,0},{2,1},{3,2},{4,7},{5,4},{6,5},{7,6},{8,11},{9,8},{10,9... | collective-permute-start | bytes 393224 | tf_op jit(solution)/shard_map/ppermute | solution.py:142
  185.9 60.2 %collective-permute-start.16 = (bf16[128,8192]{0,1:T(8,128)(2,1)}, bf16[128,8192]{0,1:T(8,128)(2,1)}, u32[]{:S(2)}, u32[]{:S(2)}) collective-permute-start(bf16[128,8192]{0,1:T(8,128)(2,1)} %constant_dynamic-update-slice_fusion), channel_id=1, source_target_pairs={{0,4},{4,0},{8,12},{12,8},{1,5},{5,1},{9,13},{13,9},{2,6},{6,2},{1... | collective-permute-start | bytes 6291464 | tf_op jit(solution)/shard_map/ppermute | solution.py:128
  187.6 13.8 %collective-permute-start.30 = (bf16[128,768]{1,0:T(8,128)(2,1)S(1)}, bf16[128,768]{1,0:T(8,128)(2,1)S(1)}, u32[]{:S(2)}, u32[]{:S(2)}) collective-permute-start(bf16[128,768]{1,0:T(8,128)(2,1)S(1)} %fusion.18.mine_ref), channel_id=1, source_target_pairs={{0,8},{4,12},{8,0},{12,4},{1,9},{5,13},{9,1},{13,5},{2,10},{6,14},... | collective-permute-start | bytes 589832 | tf_op jit(solution)/shard_map/ppermute | solution.py:132
  189.5 22.6 %copy-start.19 = (bf16[4,16,32,128]{3,2,1,0:T(8,128)(2,1)S(1)}, bf16[4,16,32,128]{3,2,1,0:T(8,128)(2,1)}, u32[]{:S(2)}) copy-start(bf16[4,16,32,128]{3,2,1,0:T(8,128)(2,1)} %copy-done.18) | copy-start | bytes 1572868
  189.5 14.9 %collective-permute-start.41 = (bf16[128,768]{1,0:T(8,128)(2,1)S(1)}, bf16[128,768]{1,0:T(8,128)(2,1)S(1)}, u32[]{:S(2)}, u32[]{:S(2)}) collective-permute-start(bf16[128,768]{1,0:T(8,128)(2,1)S(1)} %fusion.18.mine_ref), channel_id=1, source_target_pairs={{0,4},{4,0},{8,12},{12,8},{1,5},{5,1},{9,13},{13,9},{2,6},{6,2},{1... | collective-permute-start | bytes 589832 | tf_op jit(solution)/shard_map/ppermute | solution.py:128
  201.3 6.8 %collective-permute-start.35 = (bf16[128,1024]{1,0:T(8,128)(2,1)S(1)}, bf16[128,1024]{1,0:T(8,128)(2,1)S(1)}, u32[]{:S(2)}, u32[]{:S(2)}) collective-permute-start(bf16[128,1024]{1,0:T(8,128)(2,1)S(1)} %fusion.11.mine_ref), channel_id=1, source_target_pairs={{0,8},{4,12},{8,0},{12,4},{1,9},{5,13},{9,1},{13,5},{2,10},{6,14},... | collective-permute-start | bytes 786440 | tf_op jit(solution)/shard_map/ppermute | solution.py:132
  202.6 6.8 %collective-permute-start.42 = (bf16[128,1024]{1,0:T(8,128)(2,1)S(1)}, bf16[128,1024]{1,0:T(8,128)(2,1)S(1)}, u32[]{:S(2)}, u32[]{:S(2)}) collective-permute-start(bf16[128,1024]{1,0:T(8,128)(2,1)S(1)} %fusion.11.mine_ref), channel_id=1, source_target_pairs={{0,4},{4,0},{8,12},{12,8},{1,5},{5,1},{9,13},{13,9},{2,6},{6,2},{1... | collective-permute-start | bytes 786440 | tf_op jit(solution)/shard_map/ppermute | solution.py:128
  204.3 7.5 %collective-permute-start.31 = (bf16[128,768]{1,0:T(8,128)(2,1)S(1)}, bf16[128,768]{1,0:T(8,128)(2,1)S(1)}, u32[]{:S(2)}, u32[]{:S(2)}) collective-permute-start(bf16[128,768]{1,0:T(8,128)(2,1)S(1)} %collective-permute-done.30.mine_ref), channel_id=1, source_target_pairs={{0,4},{4,0},{8,12},{12,8},{1,5},{5,1},{9,13},{13,9},{2,6},{6,2},{1... | collective-permute-start | bytes 589832 | tf_op jit(solution)/shard_map/ppermute | solution.py:128
  208.2 4.5 %collective-permute-start.37 = (bf16[128,768]{1,0:T(8,128)(2,1)S(1)}, bf16[128,768]{1,0:T(8,128)(2,1)S(1)}, u32[]{:S(2)}, u32[]{:S(2)}) collective-permute-start(bf16[128,768]{1,0:T(8,128)(2,1)S(1)} %fusion.20.mine_ref), channel_id=1, source_target_pairs={{0,8},{4,12},{8,0},{12,4},{1,9},{5,13},{9,1},{13,5},{2,10},{6,14},... | collective-permute-start | bytes 589832 | tf_op jit(solution)/shard_map/ppermute | solution.py:132
  209.3 12.7 %collective-permute-start.36 = (bf16[128,1024]{1,0:T(8,128)(2,1)S(1)}, bf16[128,1024]{1,0:T(8,128)(2,1)S(1)}, u32[]{:S(2)}, u32[]{:S(2)}) collective-permute-start(bf16[128,1024]{1,0:T(8,128)(2,1)S(1)} %collective-permute-done.35.mine_ref), channel_id=1, source_target_pairs={{0,4},{4,0},{8,12},{12,8},{1,5},{5,1},{9,13},{13,9},{2,6},{6,2},{1... | collective-permute-start | bytes 786440 | tf_op jit(solution)/shard_map/ppermute | solution.py:128
  211.8 10.3 %collective-permute-start.39 = (bf16[128,1024]{1,0:T(8,128)(2,1)S(1)}, bf16[128,1024]{1,0:T(8,128)(2,1)S(1)}, u32[]{:S(2)}, u32[]{:S(2)}) collective-permute-start(bf16[128,1024]{1,0:T(8,128)(2,1)S(1)} %fusion.13.mine_ref), channel_id=1, source_target_pairs={{0,8},{4,12},{8,0},{12,4},{1,9},{5,13},{9,1},{13,5},{2,10},{6,14},... | collective-permute-start | bytes 786440 | tf_op jit(solution)/shard_map/ppermute | solution.py:132
  212.7 15.1 %collective-permute-start.26 = (bf16[128,1024]{1,0:T(8,128)(2,1)S(1)}, bf16[128,1024]{1,0:T(8,128)(2,1)S(1)}, u32[]{:S(2)}, u32[]{:S(2)}) collective-permute-start(bf16[128,1024]{1,0:T(8,128)(2,1)S(1)} %fusion.13.mine_ref), channel_id=1, source_target_pairs={{0,4},{4,0},{8,12},{12,8},{1,5},{5,1},{9,13},{13,9},{2,6},{6,2},{1... | collective-permute-start | bytes 786440 | tf_op jit(solution)/shard_map/ppermute | solution.py:128
  222.0 8.9 %collective-permute-start.22 = (bf16[128,768]{1,0:T(8,128)(2,1)S(1)}, bf16[128,768]{1,0:T(8,128)(2,1)S(1)}, u32[]{:S(2)}, u32[]{:S(2)}) collective-permute-start(bf16[128,768]{1,0:T(8,128)(2,1)S(1)} %fusion.20.mine_ref), channel_id=1, source_target_pairs={{0,4},{4,0},{8,12},{12,8},{1,5},{5,1},{9,13},{13,9},{2,6},{6,2},{1... | collective-permute-start | bytes 589832 | tf_op jit(solution)/shard_map/ppermute | solution.py:128
  222.1 11.0 %collective-permute-start.40 = (bf16[128,1024]{1,0:T(8,128)(2,1)S(1)}, bf16[128,1024]{1,0:T(8,128)(2,1)S(1)}, u32[]{:S(2)}, u32[]{:S(2)}) collective-permute-start(bf16[128,1024]{1,0:T(8,128)(2,1)S(1)} %collective-permute-done.39.mine_ref), channel_id=1, source_target_pairs={{0,4},{4,0},{8,12},{12,8},{1,5},{5,1},{9,13},{13,9},{2,6},{6,2},{1... | collective-permute-start | bytes 786440 | tf_op jit(solution)/shard_map/ppermute | solution.py:128
  227.8 8.1 %collective-permute-start.38 = (bf16[128,768]{1,0:T(8,128)(2,1)S(1)}, bf16[128,768]{1,0:T(8,128)(2,1)S(1)}, u32[]{:S(2)}, u32[]{:S(2)}) collective-permute-start(bf16[128,768]{1,0:T(8,128)(2,1)S(1)} %collective-permute-done.37.mine_ref), channel_id=1, source_target_pairs={{0,4},{4,0},{8,12},{12,8},{1,5},{5,1},{9,13},{13,9},{2,6},{6,2},{1... | collective-permute-start | bytes 589832 | tf_op jit(solution)/shard_map/ppermute | solution.py:128
  259.2 7.2 %collective-permute-start.43 = (bf16[16,32,128]{2,1,0:T(8,128)(2,1)}, bf16[16,32,128]{2,1,0:T(8,128)(2,1)S(1)}, u32[]{:S(2)}, u32[]{:S(2)}) collective-permute-start(bf16[16,32,128]{2,1,0:T(8,128)(2,1)} %get-tuple-element.41), channel_id=1, source_target_pairs={{0,1},{1,2},{2,3},{3,0},{4,5},{5,6},{6,7},{7,4},{8,9},{9,10},{10,1... | collective-permute-start | bytes 393224 | tf_op jit(solution)/shard_map/ppermute | solution.py:155
  259.2 9.5 %collective-permute-start.44 = (bf16[16,32,128]{2,1,0:T(8,128)(2,1)}, bf16[16,32,128]{2,1,0:T(8,128)(2,1)S(1)}, u32[]{:S(2)}, u32[]{:S(2)}) collective-permute-start(bf16[16,32,128]{2,1,0:T(8,128)(2,1)} %get-tuple-element.43), channel_id=1, source_target_pairs={{0,2},{1,3},{2,0},{3,1},{4,6},{5,7},{6,4},{7,5},{8,10},{9,11},{10,... | collective-permute-start | bytes 393224 | tf_op jit(solution)/shard_map/ppermute | solution.py:155
  260.1 15.6 %collective-permute-start.45 = (bf16[16,32,128]{2,1,0:T(8,128)(2,1)}, bf16[16,32,128]{2,1,0:T(8,128)(2,1)S(1)}, u32[]{:S(2)}, u32[]{:S(2)}) collective-permute-start(bf16[16,32,128]{2,1,0:T(8,128)(2,1)} %get-tuple-element.42), channel_id=1, source_target_pairs={{0,3},{1,0},{2,1},{3,2},{4,7},{5,4},{6,5},{7,6},{8,11},{9,8},{10,9... | collective-permute-start | bytes 393224 | tf_op jit(solution)/shard_map/ppermute | solution.py:155
  263.0 20.4 %collective-permute-start.47 = (bf16[16,32,64]{2,1,0:T(8,128)(2,1)S(1)}, bf16[16,32,64]{2,1,0:T(8,128)(2,1)S(1)}, u32[]{:S(2)}, u32[]{:S(2)}) collective-permute-start(bf16[16,32,64]{2,1,0:T(8,128)(2,1)S(1)} %get-tuple-element.38), channel_id=1, source_target_pairs={{0,1},{1,2},{2,3},{3,0},{4,5},{5,6},{6,7},{7,4},{8,9},{9,10},{10,1... | collective-permute-start | bytes 196616 | tf_op jit(solution)/shard_map/ppermute | solution.py:155
  264.3 19.2 %collective-permute-start.48 = (bf16[16,32,64]{2,1,0:T(8,128)(2,1)S(1)}, bf16[16,32,64]{2,1,0:T(8,128)(2,1)S(1)}, u32[]{:S(2)}, u32[]{:S(2)}) collective-permute-start(bf16[16,32,64]{2,1,0:T(8,128)(2,1)S(1)} %get-tuple-element.40), channel_id=1, source_target_pairs={{0,2},{1,3},{2,0},{3,1},{4,6},{5,7},{6,4},{7,5},{8,10},{9,11},{10,... | collective-permute-start | bytes 196616 | tf_op jit(solution)/shard_map/ppermute | solution.py:155
  266.4 17.0 %collective-permute-start.49 = (bf16[16,32,64]{2,1,0:T(8,128)(2,1)S(1)}, bf16[16,32,64]{2,1,0:T(8,128)(2,1)S(1)}, u32[]{:S(2)}, u32[]{:S(2)}) collective-permute-start(bf16[16,32,64]{2,1,0:T(8,128)(2,1)S(1)} %get-tuple-element.39), channel_id=1, source_target_pairs={{0,3},{1,0},{2,1},{3,2},{4,7},{5,4},{6,5},{7,6},{8,11},{9,8},{10,9... | collective-permute-start | bytes 196616 | tf_op jit(solution)/shard_map/ppermute | solution.py:155
  275.8 21.8 %collective-permute-start.46 = (f32[16,32,128]{2,1,0:T(8,128)S(1)}, f32[16,32,128]{2,1,0:T(8,128)S(1)}, u32[]{:S(2)}, u32[]{:S(2)}) collective-permute-start(f32[16,32,128]{2,1,0:T(8,128)S(1)} %fusion.25), channel_id=1, source_target_pairs={{0,0},{4,1},{8,2},{12,3},{1,4},{5,5},{9,6},{13,7},{2,8},{6,9},{10,... | collective-permute-start | bytes 786440 | tf_op jit(solution)/shard_map/ppermute | solution.py:271
  (20 other events, 91.2 us)

commit v2 on v1

--- a/solution.py
+++ b/solution.py
@@ -38,7 +38,7 @@
         ]
         both = jnp.stack(both)
         return both[:, :rows], both[:, rows:]
-    scalars = jnp.stack([top_block, column // BLK + first // BLK]).astype(jnp.int32)
+    scalars = jnp.stack([top_block, lax.div(column, BLK) + first // BLK]).astype(jnp.int32)
     weight_spec = pl.BlockSpec((feat, BLK), lambda n, s: (0, s[1] + n))
     out_spec = pl.BlockSpec((2, rows, BLK), lambda n, s: (0, 0, n))
     shape = jax.ShapeDtypeStruct((2, rows, width), BF16)
@@ -56,7 +56,7 @@
             out_specs=[out_spec, out_spec],
         ),
         out_shape=[shape, shape],
-        compiler_params=pltpu.CompilerParams(vmem_limit_bytes=24 * 2**20),
+        compiler_params=pltpu.CompilerParams(vmem_limit_bytes=50 * 2**20),
         cost_estimate=pl.CostEstimate(
             flops=2 * 2 * rows * feat * 2 * width,
             bytes_accessed=2 * feat * 2 * width + 2 * 2 * rows * (feat + 2 * width),
@@ -66,13 +66,14 @@
     )(scalars, top, bottom, gate, up)
 
 
-def down_kernel(idx_ref, mine_ref, other_ref, weight_ref, total_ref, out_ref):
+def down_kernel(idx_ref, mine_ref, other_ref, weight_ref, *refs):
+    out_ref = refs[-1]
     lhs = jnp.concatenate([mine_ref[...], other_ref[...]], axis=0)
     product = jnp.dot(lhs, weight_ref[...], preferred_element_type=F32)
 
     @pl.when(pl.program_id(0) == 0)
     def _():
-        out_ref[...] = total_ref[...] + product
+        out_ref[...] = refs[0][...] + product if len(refs) > 1 else product
 
     @pl.when(pl.program_id(0) > 0)
     def _():
@@ -85,10 +86,12 @@
     if width % BLK or weight.shape[0] % BLK or rows % 16 or outs % 128:
         lhs = jnp.concatenate([mine, other], axis=0)
         part = lax.dynamic_slice_in_dim(weight, row, width, 0)
-        return total + jnp.dot(lhs, part, preferred_element_type=F32)
-    scalars = jnp.reshape(row // BLK, (1,)).astype(jnp.int32)
+        product = jnp.dot(lhs, part, preferred_element_type=F32)
+        return product if total is None else total + product
+    scalars = jnp.reshape(lax.div(row, BLK), (1,)).astype(jnp.int32)
     hidden_spec = pl.BlockSpec((rows, BLK), lambda k, s: (0, k))
     whole = pl.BlockSpec((2 * rows, outs), lambda k, s: (0, 0))
+    totals = [] if total is None else [total]
     return pl.pallas_call(
         down_kernel,
         grid_spec=pltpu.PrefetchScalarGridSpec(
@@ -98,19 +101,19 @@
                 hidden_spec,
                 hidden_spec,
                 pl.BlockSpec((BLK, outs), lambda k, s: (s[0] + k, 0)),
-                whole,
-            ],
+            ]
+            + [whole] * len(totals),
             out_specs=whole,
         ),
         out_shape=jax.ShapeDtypeStruct((2 * rows, outs), F32),
-        compiler_params=pltpu.CompilerParams(vmem_limit_bytes=24 * 2**20),
+        compiler_params=pltpu.CompilerParams(vmem_limit_bytes=50 * 2**20),
         cost_estimate=pl.CostEstimate(
             flops=2 * 2 * rows * width * outs,
             bytes_accessed=2 * width * outs + 2 * 2 * rows * width + 16 * rows * outs,
             transcendentals=0,
         ),
         name="down_add",
-    )(scalars, mine, other, weight, total)
+    )(scalars, mine, other, weight, *totals)
 
 
 def body(tokens, gate_weight, up_weight, down_weight, right_factor, left_factor):
@@ -121,7 +124,7 @@
     feat, hid = gate_weight.shape
     part = hid // chips
     me = lax.axis_index("fsdp")
-    chip, core = me // 2, me % 2
+    chip, core = lax.div(me, 2), lax.rem(me, 2)
     z = lax.axis_index("tensor")
 
     def swap(value):
@@ -158,20 +161,15 @@
     def columns(value, start, width):
         return lax.dynamic_slice_in_dim(value, start, width, 1)
 
-    pairs = {0: (tokens, me, swap(columns(tokens, (me ^ 1) * feat, feat)))}
-    row_share = rows // tensor_count
-    own_share = lax.dynamic_slice_in_dim(tokens, z * row_share, row_share, 0)
-    gathered = {}
-    for dt in range(1, chips):
-        for g in range(chips):
-            features = (chip - dt + g + chips) % chips * (2 * feat)
-            piece = shift(columns(own_share, features, 2 * feat), -dt)
-            gathered[dt, g] = gather_z(piece)
-        got = gathered[dt, 0]
-        pairs[dt] = (
-            columns(got, core * feat, feat),
-            jnp.int32(0),
-            swap(columns(got, (1 - core) * feat, feat)),
+    def after(value, *others):
+        return lax.optimization_barrier((value,) + others)[0]
+
+    def pair_z(value):
+        perm = [(i, i ^ 1) for i in range(tensor_count)]
+        got = lax.ppermute(value, "tensor", perm)
+        odd = lax.rem(z, 2) == 1
+        return jnp.concatenate(
+            [jnp.where(odd, got, value), jnp.where(odd, value, got)], axis=0
         )
 
     if part % BLK == 0 and part // BLK > 1:
@@ -180,51 +178,80 @@
     else:
         chunks = [(0, part)]
 
-    def partial(dt, dp, chunk):
-        column = (chip + dp) % chips * part
-        top, block, bottom = pairs[dt]
-        mine, other = gate_up(top, block, bottom, gate_weight, up_weight, column, *chunk)
+    half = rows // 2
+    own_half = lax.dynamic_slice_in_dim(tokens, lax.rem(z, 2) * half, half, 0)
+
+    def send_tokens(value, dt, g):
+        features = lax.rem(chip - dt + g + chips, chips) * (2 * feat)
+        return shift(columns(value, features, 2 * feat), -dt)
+
+    def partial(pair, dp, first, width):
+        column = lax.rem(chip + dp, chips) * part
+        top, block, bottom = pair
+        mine, other = gate_up(top, block, bottom, gate_weight, up_weight, column, first, width)
         return mine, swap(other)
 
-    kept, got = {}, {}
-    for dt in range(chips):
-        for dp in list(range(1, chips)) + [0]:
-            for n, chunk in enumerate(chunks):
-                mine, from_core = partial(dt, dp, chunk)
-                if dp:
-                    both = (mine.astype(F32) + from_core.astype(F32)).astype(BF16)
-                    got[dt, dp, n] = shift(both, dp)
-                else:
-                    kept[dt, n] = (mine, from_core)
-
-    hidden = {}
+    def send_partials(pair, got, dt):
+        sums = []
+        for dp in range(1, chips):
+            pieces = [partial(pair, dp, *chunk) for chunk in chunks]
+            for n, (mine, from_core) in enumerate(pieces):
+                both = (mine.astype(F32) + from_core.astype(F32)).astype(BF16)
+                got[dt, dp, n] = shift(both, dp)
+                sums.append(both)
+        return sums
+
+    got, kept, gathered = {}, {}, {}
+    local = swap(columns(tokens, (me ^ 1) * feat, feat))
+    arrived = {dt: send_tokens(own_half, dt, 0) for dt in range(1, chips)}
+    sums = send_partials((tokens, me, local), got, 0)
+    if sums:
+        local = after(local, *sums)
+    kept[0] = partial((tokens, me, local), 0, 0, part)
+    late_tokens = after(tokens, kept[0][0])
+    neighbour_tokens = swap(late_tokens)
+    late_half = after(own_half, *sums) if sums else own_half
+
+    for dt in range(1, chips):
+        gathered[dt, 0] = pair_z(after(arrived[dt], *sums))
+        whole = gathered[dt, 0]
+        top = columns(whole, core * feat, feat)
+        bottom = swap(columns(whole, (1 - core) * feat, feat))
+        pair = (top, jnp.int32(0), bottom)
+        sums = send_partials(pair, got, dt)
+        pair = (top, jnp.int32(0), after(bottom, *sums))
+        kept[dt] = partial(pair, 0, 0, part)
+        for g in range(1, chips):
+            gathered[dt, g] = pair_z(after(send_tokens(late_half, dt, g), kept[dt][0]))
+
+    def activate(e, first, width, n):
+        terms = [lax.slice_in_dim(term, first, first + width, axis=2) for term in kept[e]]
+        terms += [got[(e + dp) % chips, dp, n] for dp in range(1, chips)]
+        total = sum(term.astype(F32) for term in terms)
+        return (jax.nn.silu(total[0]) * total[1]).astype(BF16)
+
+    totals = {u: None for u in range(chips)}
     for e in list(range(1, chips)) + [0]:
-        for n in range(len(chunks)):
-            terms = list(kept[e, n])
-            terms += [got[(e + dp) % chips, dp, n] for dp in range(1, chips)]
-            total = sum(term.astype(F32) for term in terms)
-            value = (jax.nn.silu(total[0]) * total[1]).astype(BF16)
-            hidden[e, 0, n] = value
-            for d in range(1, chips):
-                hidden[e, d, n] = shift(value, d)
-
-    totals = {u: jnp.zeros((2 * rows, down_weight.shape[1]), F32) for u in range(chips)}
-    for e in list(range(1, chips)) + [0]:
-        for n, (first, width) in enumerate(chunks):
-            for d in range(chips):
+        values = [activate(e, *chunk, n) for n, chunk in enumerate(chunks)]
+        spans = list(chunks)
+        if e:
+            values, spans = [jnp.concatenate(values, axis=1)], [(0, part)]
+        sent = [[value] + [shift(value, d) for d in range(1, chips)] for value in values]
+        for (first, width), copies in zip(spans, sent):
+            for d, mine in enumerate(copies):
                 u = (e - d + chips) % chips
-                mine = hidden[e, d, n]
-                row = (chip - d + chips) % chips * part + first
+                row = lax.rem(chip - d + chips, chips) * part + first
                 totals[u] = down_add(totals[u], mine, swap(mine), down_weight, row)
 
     token_rows = []
     for dt in range(chips):
         if dt == 0:
-            full = tokens
+            token_rows += [tokens, neighbour_tokens]
+            continue
         else:
             full = jnp.zeros((rows, model), BF16)
             for g in range(chips):
-                features = (chip + g) % chips * (2 * feat)
+                features = lax.rem(chip + g, chips) * (2 * feat)
                 full = lax.dynamic_update_slice_in_dim(full, gathered[dt, g], features, 1)
         token_rows += [full, swap(full)]
     inputs = jnp.concatenate(token_rows, axis=0)

time: 299 us -> 280 us (0.936)
  the two profiles are of different devices: /device:TPU:17 before, /device:TPU:2 now
where the time goes in v2:
time: 280 us; the launch traced here: 278 us
  Pallas kernels  80.8 us (29%)
  waiting for transfers between devices  78.1 us (28%)
  local copies, waits for them, and re-layouts  43.3 us (15%)
  starting transfers between devices  40.3 us (14%)
  other arithmetic  24 us (9%)
  matrix products  10.7 us (4%)
    pallas_call x6, Pallas kernels, gate_up(): pl.pallas_call(gate_up_kernel, grid_spec=pltpu.PrefetchScalarGridSpec(num...  45.7 us
    ppermute x9, waiting for transfers between devices, shift(): return lax.ppermute(value, 'fsdp', perm)  39.5 us
    pallas_call x6, Pallas kernels, down_add(): pl.pallas_call(down_kernel, grid_spec=pltpu.PrefetchScalarGridSpec(num_sc...  35.1 us
    ppermute x2, waiting for transfers between devices, pair_z(): got = lax.ppermute(value, 'tensor', perm)  15 us
    ppermute x1, waiting for transfers between devices, body(): grad_right = lax.ppermute(scatter_z(grad_right), ('fsdp', 'tensor'), back)  13.9 us
    ppermute x9, starting transfers between devices, shift(): return lax.ppermute(value, 'fsdp', perm)  13 us
    unnamed x37, local copies, waits for them, and re-layouts  10.4 us
    ppermute x6, starting transfers between devices, scatter_z(): total += lax.ppermute(piece.astype(BF16), 'tensor', perm).astype(F32)  8.82 us
  transfers between devices with their start and end apart: 41, of which 12 were waited for; matrix products, arithmetic and copies ran while one was open for 20% of the time, Pallas kernels for 29%

profile of v2, /device:TPU:2, one launch (start us, length us, event | category | flops | bytes accessed | tf_op | source)
XLA Modules:
  0.0 278.3 jit_solution(11142311428190681894)
XLA Ops:
  2.0 1.6 collective-permute-start
  3.6 2.6 collective-permute-start.1
  6.2 2.1 dynamic_slice.45
  8.9 5.8 %gate_up.7 = (bf16[2,128,768]{2,1,0:T(8,128)(2,1)S(1)}, bf16[2,128,768]{2,1,0:T(8,128)(2,1)}) custom-call(s32[2]{0:T(128)S(1)} %get-tuple-element.57.idx_ref, bf16[128,8192]{1,0:T(8,128)(2,1)S(1)} %copy-done, bf16[128,2048]{1,0:T(8,128)(2,1)S(1)} %collective-permute-done.7.bottom_ref, bf16[2048,3584]{1,0:T(8,128)(2,1)} %gate_ref.11, bf16[2048,3584]{1,0:T(8,128)(2,1)} %up_ref.11), custom_call_target="tpu_custom_call" | custom-call | flops 1610612736 | bytes 8126464 | tf_op jit(solution)/shard_map/gate_up/pallas_call | solution.py:45
  14.7 6.8 %gate_up.6 = (bf16[2,128,1024]{2,1,0:T(8,128)(2,1)S(1)}, bf16[2,128,1024]{2,1,0:T(8,128)(2,1)}) custom-call(s32[2]{0:T(128)S(1)} %get-tuple-element.56.idx_ref, bf16[128,8192]{1,0:T(8,128)(2,1)S(1)} %copy-done, bf16[128,2048]{1,0:T(8,128)(2,1)S(1)} %collective-permute-done.7.bottom_ref, bf16[2048,3584]{1,0:T(8,128)(2,1)} %gate_ref.11, bf16[2048,3584]{1,0:T(8,128)(2,1)} %up_ref.11), custom_call_target="tpu_custom_call" | custom-call | flops 2147483648 | bytes 10485760 | tf_op jit(solution)/shard_map/gate_up/pallas_call | solution.py:45
  24.0 1.6 constant_dynamic-update-slice_fusion.9
  25.6 2.4 copy.18
  28.1 1.3 collective-permute-start.2
  29.4 1.8 add_convert_fusion.3
  31.2 3.1 %collective-permute-start.3 = (bf16[16,32,128]{2,1,0:T(8,128)(2,1)}, bf16[16,32,128]{2,1,0:T(8,128)(2,1)}, u32[]{:S(2)}, u32[]{:S(2)}) collective-permute-start(bf16[16,32,128]{2,1,0:T(8,128)(2,1)} %param.10), channel_id=1, source_target_pairs={{0,0},{1,4},{2,8},{3,12},{4,1},{5,5},{6,9},{7,13},{8,2},{9,6},{10,... | collective-permute-start | bytes 393224 | tf_op jit(solution)/shard_map/ppermute | solution.py:267
  34.4 2.0 add_convert_fusion.1
  36.6 1.6 constant_dynamic-update-slice_fusion.8
  38.2 1.6 constant_dynamic-update-slice_fusion.7
  40.5 2.7 collective-permute-done.3
  43.3 13.0 %collective-permute-done.12 = bf16[64,4096]{1,0:T(8,128)(2,1)S(1)} collective-permute-done((bf16[64,4096]{1,0:T(8,128)(2,1)}, bf16[64,4096]{1,0:T(8,128)(2,1)S(1)}, u32[]{:S(2)}, u32[]{:S(2)}) %collective-permute-start.12) | collective-permute-done | bytes 524320 | tf_op jit(solution)/shard_map/ppermute | solution.py:169
  58.6 10.8 %gate_up.8 = (bf16[2,128,1792]{2,1,0:T(8,128)(2,1)S(1)}, bf16[2,128,1792]{2,1,0:T(8,128)(2,1)}) custom-call(s32[2]{0:T(128)S(1)} %get-tuple-element.55.idx_ref, bf16[128,8192]{1,0:T(8,128)(2,1)} %top_ref.5, bf16[128,2048]{1,0:T(8,128)(2,1)S(1)} %collective-permute-done.7.bottom_ref, bf16[2048,3584]{1,0:T(8,128)(2,1)} %gate_ref.11, bf16[2048,3584]{1,0:T(8,128)(2,1)} %up_ref.11), custom_call_target="tpu_custom_call" | custom-call | flops 3758096384 | bytes 17563648 | tf_op jit(solution)/shard_map/gate_up/pallas_call | solution.py:45
  70.8 2.5 copy.15
  73.2 1.9 constant_dynamic-slice_fusion
  75.1 5.3 %gate_up.10 = (bf16[2,128,768]{2,1,0:T(8,128)(2,1)S(1)}, bf16[2,128,768]{2,1,0:T(8,128)(2,1)S(1)}) custom-call(s32[2]{0:T(128)S(1)} %get-tuple-element.52.idx_ref, bf16[128,2048]{1,0:T(8,128)(2,1)S(1)} %get-tuple-element.49.top_ref, bf16[128,2048]{1,0:T(8,128)(2,1)} %collective-permute-done.14.bottom_ref, bf16[2048,3584]{1,0:T(8,128)(2,1)} %gate_ref.11, ...), custom_call_target="tpu_custom_call" | custom-call | flops 1610612736 | bytes 8126464 | tf_op jit(solution)/shard_map/gate_up/pallas_call | solution.py:45
  80.6 6.2 %gate_up.9 = (bf16[2,128,1024]{2,1,0:T(8,128)(2,1)S(1)}, bf16[2,128,1024]{2,1,0:T(8,128)(2,1)S(1)}) custom-call(s32[2]{0:T(128)S(1)} %get-tuple-element.53.idx_ref, bf16[128,2048]{1,0:T(8,128)(2,1)S(1)} %get-tuple-element.49.top_ref, bf16[128,2048]{1,0:T(8,128)(2,1)} %collective-permute-done.14.bottom_ref, bf16[2048,3584]{1,0:T(8,128)(2,1)} %gate_ref.11, ...), custom_call_target="tpu_custom_call" | custom-call | flops 2147483648 | bytes 10485760 | tf_op jit(solution)/shard_map/gate_up/pallas_call | solution.py:45
  88.5 2.2 copy.16
  90.7 3.0 %collective-permute-start.13 = (bf16[64,4096]{1,0:T(8,128)(2,1)}, bf16[64,4096]{1,0:T(8,128)(2,1)S(1)}, u32[]{:S(2)}, u32[]{:S(2)}) collective-permute-start(bf16[64,4096]{1,0:T(8,128)(2,1)} %constant_dynamic-slice_fusion), channel_id=1, source_target_pairs={{0,8},{4,12},{8,0},{12,4},{1,9},{5,13},{9,1},{13,5},{2,10},{6,14},... | collective-permute-start | bytes 1572872 | tf_op jit(solution)/shard_map/ppermute | solution.py:135
  93.9 2.0 add_convert_fusion
  95.9 10.7 %gate_up.11 = (bf16[2,128,1792]{2,1,0:T(8,128)(2,1)S(1)}, bf16[2,128,1792]{2,1,0:T(8,128)(2,1)}) custom-call(s32[2]{0:T(128)S(1)} %get-tuple-element.54.idx_ref, bf16[128,2048]{1,0:T(8,128)(2,1)S(1)} %get-tuple-element.49.top_ref, bf16[128,2048]{1,0:T(8,128)(2,1)} %collective-permute-done.14.bottom_ref, bf16[2048,3584]{1,0:T(8,128)(2,1)} %gate_ref.11, ...), custom_call_target="tpu_custom_call" | custom-call | flops 3758096384 | bytes 17563648 | tf_op jit(solution)/shard_map/gate_up/pallas_call | solution.py:45
  106.7 1.6 broadcast_in_dim.15
  109.4 2.0 collective-permute-start.26
  111.5 3.6 %collective-permute-done.20 = bf16[2,128,768]{2,1,0:T(8,128)(2,1)S(1)} collective-permute-done((bf16[2,128,768]{2,1,0:T(8,128)(2,1)S(1)}, bf16[2,128,768]{2,1,0:T(8,128)(2,1)S(1)}, u32[]{:S(2)}, u32[]{:S(2)}) %collective-permute-start.20) | collective-permute-done | bytes 393248 | tf_op jit(solution)/shard_map/ppermute | solution.py:135
  115.1 2.1 collective-permute-start.22
  118.4 2.0 collective-permute-done.17
  121.5 1.6 copy.17
  124.3 10.0 %collective-permute-done.22 = bf16[2,128,1024]{2,1,0:T(8,128)(2,1)} collective-permute-done((bf16[2,128,1024]{2,1,0:T(8,128)(2,1)}, bf16[2,128,1024]{2,1,0:T(8,128)(2,1)}, u32[]{:S(2)}, u32[]{:S(2)}) %collective-permute-start.22) | collective-permute-done | bytes 524320 | tf_op jit(solution)/shard_map/ppermute | solution.py:135
  134.3 1.7 collective-permute-start.25
  136.0 1.4 convert_add_fusion.1
  137.6 10.1 %collective-permute-done.25 = bf16[2,128,1024]{2,1,0:T(8,128)(2,1)S(1)} collective-permute-done((bf16[2,128,1024]{2,1,0:T(8,128)(2,1)S(1)}, bf16[2,128,1024]{2,1,0:T(8,128)(2,1)S(1)}, u32[]{:S(2)}, u32[]{:S(2)}) %collective-permute-start.25) | collective-permute-done | bytes 524320 | tf_op jit(solution)/shard_map/ppermute | solution.py:135
  151.1 1.5 collective-permute-start.29
  153.3 1.4 collective-permute-start.27
  154.7 4.2 %collective-permute-done.29.mine_ref = bf16[128,768]{1,0:T(8,128)(2,1)S(1)} collective-permute-done((bf16[128,768]{1,0:T(8,128)(2,1)S(1)}, bf16[128,768]{1,0:T(8,128)(2,1)S(1)}, u32[]{:S(2)}, u32[]{:S(2)}) %collective-permute-start.29) | collective-permute-done | bytes 196640 | tf_op jit(solution)/shard_map/ppermute | solution.py:135
  161.8 2.7 collective-permute-done.31.mine_ref
  164.5 8.9 %collective-permute-done.27.mine_ref = bf16[128,1792]{1,0:T(8,128)(2,1)S(1)} collective-permute-done((bf16[128,1792]{1,0:T(8,128)(2,1)S(1)}, bf16[128,1792]{1,0:T(8,128)(2,1)S(1)}, u32[]{:S(2)}, u32[]{:S(2)}) %collective-permute-start.27) | collective-permute-done | bytes 458784 | tf_op jit(solution)/shard_map/ppermute | solution.py:135
  174.0 7.6 %down_add.9.refs_0_ = f32[256,2048]{1,0:T(8,128)S(1)} custom-call(s32[1]{0:T(128)} %bitcast.14.idx_ref, bf16[128,1792]{1,0:T(8,128)(2,1)S(1)} %pad_maximum_fusion.4.mine_ref, bf16[128,1792]{1,0:T(8,128)(2,1)S(1)} %collective-permute-done.33.other_ref, bf16[3584,2048]{1,0:T(8,128)(2,1)} %weight_ref.11), custom_call_target="tpu_custom_call" | custom-call | flops 1879048192 | bytes 12451840 | tf_op jit(solution)/shard_map/down_add/pallas_call | solution.py:95
  181.6 1.3 copy-done.2
  183.0 5.4 %down_add.10.refs_0_ = f32[256,2048]{1,0:T(8,128)S(1)} custom-call(s32[1]{0:T(128)} %bitcast.6.idx_ref, bf16[128,1024]{1,0:T(8,128)(2,1)S(1)} %collective-permute-done.31.mine_ref, bf16[128,1024]{1,0:T(8,128)(2,1)S(1)} %collective-permute-done.32.other_ref, bf16[3584,2048]{1,0:T(8,128)(2,1)} %weight_ref.11, f32[256,2048]{1,0:T(8,128)} %copy-done.2), custom_call_target="tpu_custom_call" | custom-call | flops 1073741824 | bytes 8912896 | tf_op jit(solution)/shard_map/down_add/pallas_call | solution.py:95
  188.4 1.3 copy-done.4
  190.2 4.5 %down_add.11 = f32[256,2048]{1,0:T(8,128)S(1)} custom-call(s32[1]{0:T(128)} %bitcast.21.idx_ref, bf16[128,768]{1,0:T(8,128)(2,1)S(1)} %collective-permute-done.29.mine_ref, bf16[128,768]{1,0:T(8,128)(2,1)S(1)} %collective-permute-done.30.other_ref, bf16[3584,2048]{1,0:T(8,128)(2,1)} %weight_ref.11, f32[256,2048]{1,0:T(8,128)} %copy-done.4), custom_call_target="tpu_custom_call" | custom-call | flops 805306368 | bytes 7733248 | tf_op jit(solution)/shard_map/down_add/pallas_call | solution.py:95
  194.7 7.6 %down_add.6.refs_0_ = f32[256,2048]{1,0:T(8,128)S(1)} custom-call(s32[1]{0:T(128)} %bitcast.6.idx_ref, bf16[128,1792]{1,0:T(8,128)(2,1)S(1)} %collective-permute-done.27.mine_ref, bf16[128,1792]{1,0:T(8,128)(2,1)S(1)} %collective-permute-done.28.other_ref, bf16[3584,2048]{1,0:T(8,128)(2,1)} %weight_ref.11), custom_call_target="tpu_custom_call" | custom-call | flops 1879048192 | bytes 12451840 | tf_op jit(solution)/shard_map/down_add/pallas_call | solution.py:95
  202.4 1.3 copy-done.3
  203.7 5.4 %down_add.7.refs_0_ = f32[256,2048]{1,0:T(8,128)S(1)} custom-call(s32[1]{0:T(128)} %bitcast.14.idx_ref, bf16[128,1024]{1,0:T(8,128)(2,1)S(1)} %fusion.15.mine_ref, bf16[128,1024]{1,0:T(8,128)(2,1)S(1)} %collective-permute-done.23.other_ref, bf16[3584,2048]{1,0:T(8,128)(2,1)} %weight_ref.11, f32[256,2048]{1,0:T(8,128)} %copy-done.3), custom_call_target="tpu_custom_call" | custom-call | flops 1073741824 | bytes 8912896 | tf_op jit(solution)/shard_map/down_add/pallas_call | solution.py:95
  209.1 1.3 copy-done.5
  210.4 4.5 %down_add.8 = f32[256,2048]{1,0:T(8,128)S(1)} custom-call(s32[1]{0:T(128)} %bitcast.11.idx_ref, bf16[128,768]{1,0:T(8,128)(2,1)S(1)} %fusion.22.mine_ref, bf16[128,768]{1,0:T(8,128)(2,1)S(1)} %collective-permute-done.21.other_ref, bf16[3584,2048]{1,0:T(8,128)(2,1)} %weight_ref.11, f32[256,2048]{1,0:T(8,128)} %copy-done.5), custom_call_target="tpu_custom_call" | custom-call | flops 805306368 | bytes 7733248 | tf_op jit(solution)/shard_map/down_add/pallas_call | solution.py:95
  215.0 2.5 pad_maximum_fusion.1
  217.5 5.5 %copy.21 = f32[512,2048]{0,1:T(8,128)} copy(f32[512,2048]{1,0:T(8,128)} %pad_maximum_fusion.1) | data formatting | bytes 8388608 | tf_op jit(solution)/shard_map/concatenate | solution.py:279
  223.0 4.0 %pad_maximum_fusion = bf16[512,8192]{0,1:T(8,128)(2,1)S(1)} fusion(bf16[128,8192]{0,1:T(8,128)(2,1)} %collective-permute-done.18, bf16[128,8192]{0,1:T(8,128)(2,1)} %constant_dynamic-update-slice_fusion, bf16[128,8192]{0,1:T(8,128)(2,1)} %collective-permute-done.10, bf16[128,8192]{0,1:T(8,128)(2,1)S(1)} %copy-done.9), kind=kLoop, calls=%fused_computation | loop fusion | flops 33554432 | bytes 16777216 | tf_op jit(solution)/shard_map/concatenate | solution.py:257
  227.0 1.3 convert_bitcast_fusion
  228.3 4.0 %fusion.5 = f32[32,64,512]{2,1,0:T(8,128)S(1)} fusion(bf16[512,64,32]{0,2,1:T(8,128)(2,1)S(1)} %convert_bitcast_fusion, bf16[64,32,64]{2,0,1:T(8,128)(2,1)} %constant_dynamic-update-slice_fusion.6), kind=kOutput, calls=%fused_computation.10 | convolution fusion | flops 134217728 | bytes 6553600 | tf_op jit(solution)/shard_map/nij,jki->njk/dot_general | solution.py:278
  233.4 1.8 fusion.16
  235.2 2.3 fusion.2
  238.3 2.0 collective-permute-start.34
  240.3 2.4 collective-permute-start.36
  242.7 1.3 fusion.7
  245.1 2.6 collective-permute-start.39
  247.7 1.8 collective-permute-start.40
  249.5 6.8 %collective-permute-done.35 = bf16[16,32,128]{2,1,0:T(8,128)(2,1)S(1)} collective-permute-done((bf16[16,32,128]{2,1,0:T(8,128)(2,1)}, bf16[16,32,128]{2,1,0:T(8,128)(2,1)S(1)}, u32[]{:S(2)}, u32[]{:S(2)}) %collective-permute-start.35) | collective-permute-done | bytes 131104 | tf_op jit(solution)/shard_map/ppermute | solution.py:158
  256.4 6.2 %collective-permute-start.37 = (f32[16,32,128]{2,1,0:T(8,128)S(1)}, f32[16,32,128]{2,1,0:T(8,128)S(1)}, u32[]{:S(2)}, u32[]{:S(2)}) collective-permute-start(f32[16,32,128]{2,1,0:T(8,128)S(1)} %fusion.27), channel_id=1, source_target_pairs={{0,0},{4,1},{8,2},{12,3},{1,4},{5,5},{9,6},{13,7},{2,8},{6,9},{10,... | collective-permute-start | bytes 786440 | tf_op jit(solution)/shard_map/ppermute | solution.py:298
  263.7 13.9 %collective-permute-done.37 = f32[16,32,128]{2,1,0:T(8,128)S(1)} collective-permute-done((f32[16,32,128]{2,1,0:T(8,128)S(1)}, f32[16,32,128]{2,1,0:T(8,128)S(1)}, u32[]{:S(2)}, u32[]{:S(2)}) %collective-permute-start.37) | collective-permute-done | bytes 262176 | tf_op jit(solution)/shard_map/ppermute | solution.py:298
  (122 shorter events, 28.8 us)
Async XLA Ops:
  0.6 8.3 %copy-start = (bf16[128,8192]{1,0:T(8,128)(2,1)S(1)}, bf16[128,8192]{1,0:T(8,128)(2,1)}, u32[]{:S(2)}) copy-start(bf16[128,8192]{1,0:T(8,128)(2,1)} %top_ref.5) | copy-start | bytes 6291460
  1.9 7.0 %collective-permute-start.7 = (bf16[128,2048]{1,0:T(8,128)(2,1)S(1)}, bf16[128,2048]{1,0:T(8,128)(2,1)S(1)}, u32[]{:S(2)}, u32[]{:S(2)}) collective-permute-start(bf16[128,2048]{1,0:T(8,128)(2,1)S(1)} %constant_dynamic-slice_fusion.2), channel_id=1, source_target_pairs={{0,4},{4,0},{8,12},{12,8},{1,5},{5,1},{9,13},{13,9},{2,6},{6,2},{1... | collective-permute-start | bytes 1572872 | tf_op jit(solution)/shard_map/ppermute | solution.py:131
  2.0 34.6 %collective-permute-start = (bf16[16,32,64]{2,0,1:T(8,128)(2,1)}, bf16[16,32,64]{2,0,1:T(8,128)(2,1)}, u32[]{:S(2)}, u32[]{:S(2)}) collective-permute-start(bf16[16,32,64]{2,0,1:T(8,128)(2,1)} %bitcast.112), channel_id=1, source_target_pairs={{0,1},{1,2},{2,3},{3,0},{4,5},{5,6},{6,7},{7,4},{8,9},{9,10},{10,1... | collective-permute-start | bytes 196616 | tf_op jit(solution)/shard_map/ppermute | solution.py:145
  3.6 34.6 %collective-permute-start.1 = (bf16[16,32,64]{2,0,1:T(8,128)(2,1)}, bf16[16,32,64]{2,0,1:T(8,128)(2,1)}, u32[]{:S(2)}, u32[]{:S(2)}) collective-permute-start(bf16[16,32,64]{2,0,1:T(8,128)(2,1)} %bitcast.113), channel_id=1, source_target_pairs={{0,2},{1,3},{2,0},{3,1},{4,6},{5,7},{6,4},{7,5},{8,10},{9,11},{10,... | collective-permute-start | bytes 196616 | tf_op jit(solution)/shard_map/ppermute | solution.py:145
  8.3 28.1 %collective-permute-start.11 = (bf16[64,4096]{1,0:T(8,128)(2,1)}, bf16[64,4096]{1,0:T(8,128)(2,1)}, u32[]{:S(2)}, u32[]{:S(2)}) collective-permute-start(bf16[64,4096]{1,0:T(8,128)(2,1)} %dynamic_slice.45), channel_id=1, source_target_pairs={{0,8},{4,12},{8,0},{12,4},{1,9},{5,13},{9,1},{13,5},{2,10},{6,14},... | collective-permute-start | bytes 1572872 | tf_op jit(solution)/shard_map/ppermute | solution.py:135
  14.7 13.4 %collective-permute-start.9 = (bf16[2,128,768]{2,1,0:T(8,128)(2,1)}, bf16[2,128,768]{2,1,0:T(8,128)(2,1)}, u32[]{:S(2)}, u32[]{:S(2)}) collective-permute-start(bf16[2,128,768]{2,1,0:T(8,128)(2,1)} %get-tuple-element.23), channel_id=1, source_target_pairs={{0,4},{4,0},{8,12},{12,8},{1,5},{5,1},{9,13},{13,9},{2,6},{6,2},{1... | collective-permute-start | bytes 1179656 | tf_op jit(solution)/shard_map/ppermute | solution.py:131
  21.5 9.7 %collective-permute-start.8 = (bf16[2,128,1024]{2,1,0:T(8,128)(2,1)}, bf16[2,128,1024]{2,1,0:T(8,128)(2,1)}, u32[]{:S(2)}, u32[]{:S(2)}) collective-permute-start(bf16[2,128,1024]{2,1,0:T(8,128)(2,1)} %get-tuple-element.21), channel_id=1, source_target_pairs={{0,4},{4,0},{8,12},{12,8},{1,5},{5,1},{9,13},{13,9},{2,6},{6,2},{1... | collective-permute-start | bytes 1572872 | tf_op jit(solution)/shard_map/ppermute | solution.py:131
  28.1 11.7 %collective-permute-start.2 = (bf16[16,32,64]{2,0,1:T(8,128)(2,1)}, bf16[16,32,64]{2,0,1:T(8,128)(2,1)S(1)}, u32[]{:S(2)}, u32[]{:S(2)}) collective-permute-start(bf16[16,32,64]{2,0,1:T(8,128)(2,1)} %bitcast.114), channel_id=1, source_target_pairs={{0,3},{1,0},{2,1},{3,2},{4,7},{5,4},{6,5},{7,6},{8,11},{9,8},{10,9... | collective-permute-start | bytes 196616 | tf_op jit(solution)/shard_map/ppermute | solution.py:145
  31.2 11.9 %collective-permute-start.3 = (bf16[16,32,128]{2,1,0:T(8,128)(2,1)}, bf16[16,32,128]{2,1,0:T(8,128)(2,1)}, u32[]{:S(2)}, u32[]{:S(2)}) collective-permute-start(bf16[16,32,128]{2,1,0:T(8,128)(2,1)} %param.10), channel_id=1, source_target_pairs={{0,0},{1,4},{2,8},{3,12},{4,1},{5,5},{6,9},{7,13},{8,2},{9,6},{10,... | collective-permute-start | bytes 393224 | tf_op jit(solution)/shard_map/ppermute | solution.py:267
  36.4 19.9 %collective-permute-start.12 = (bf16[64,4096]{1,0:T(8,128)(2,1)}, bf16[64,4096]{1,0:T(8,128)(2,1)S(1)}, u32[]{:S(2)}, u32[]{:S(2)}) collective-permute-start(bf16[64,4096]{1,0:T(8,128)(2,1)} %collective-permute-done.11), channel_id=1, source_target_pairs={{0,1},{1,0},{2,3},{3,2},{4,5},{5,4},{6,7},{7,6},{8,9},{9,8},{10,11... | collective-permute-start | bytes 1572872 | tf_op jit(solution)/shard_map/ppermute | solution.py:169
  43.1 107.9 %collective-permute-start.4 = (bf16[1,16,32,128]{3,2,1,0:T(8,128)(2,1)}, bf16[1,16,32,128]{3,2,1,0:T(8,128)(2,1)}, u32[]{:S(2)}, u32[]{:S(2)}) collective-permute-start(bf16[1,16,32,128]{3,2,1,0:T(8,128)(2,1)} %bitcast.2), channel_id=1, source_target_pairs={{0,1},{1,2},{2,3},{3,0},{4,5},{5,6},{6,7},{7,4},{8,9},{9,10},{10,1... | collective-permute-start | bytes 393224 | tf_op jit(solution)/shard_map/ppermute | solution.py:145
  43.3 109.3 %collective-permute-start.5 = (bf16[1,16,32,128]{3,2,1,0:T(8,128)(2,1)}, bf16[1,16,32,128]{3,2,1,0:T(8,128)(2,1)}, u32[]{:S(2)}, u32[]{:S(2)}) collective-permute-start(bf16[1,16,32,128]{3,2,1,0:T(8,128)(2,1)} %bitcast.2), channel_id=1, source_target_pairs={{0,2},{1,3},{2,0},{3,1},{4,6},{5,7},{6,4},{7,5},{8,10},{9,11},{10,... | collective-permute-start | bytes 393224 | tf_op jit(solution)/shard_map/ppermute | solution.py:145
  57.4 1.1 copy-start.10
  57.5 1.1 copy-start.12
  58.5 16.6 %collective-permute-start.14 = (bf16[128,2048]{1,0:T(8,128)(2,1)}, bf16[128,2048]{1,0:T(8,128)(2,1)}, u32[]{:S(2)}, u32[]{:S(2)}) collective-permute-start(bf16[128,2048]{1,0:T(8,128)(2,1)} %get-tuple-element.48), channel_id=1, source_target_pairs={{0,4},{4,0},{8,12},{12,8},{1,5},{5,1},{9,13},{13,9},{2,6},{6,2},{1... | collective-permute-start | bytes 1572872 | tf_op jit(solution)/shard_map/ppermute | solution.py:131
  58.6 12.2 %copy-start.1 = (bf16[128,8192]{1,0:T(8,128)(2,1)S(1)}, bf16[128,8192]{1,0:T(8,128)(2,1)}, u32[]{:S(2)}) copy-start(bf16[128,8192]{1,0:T(8,128)(2,1)} %top_ref.5) | copy-start | bytes 6291460
  69.4 0.9 copy-start.6
  70.3 39.1 %collective-permute-start.19 = (bf16[2,128,1792]{2,1,0:T(8,128)(2,1)}, bf16[2,128,1792]{2,1,0:T(8,128)(2,1)}, u32[]{:S(2)}, u32[]{:S(2)}) collective-permute-start(bf16[2,128,1792]{2,1,0:T(8,128)(2,1)} %get-tuple-element.36), channel_id=1, source_target_pairs={{0,4},{4,0},{8,12},{12,8},{1,5},{5,1},{9,13},{13,9},{2,6},{6,2},{1... | collective-permute-start | bytes 2752520 | tf_op jit(solution)/shard_map/ppermute | solution.py:131
  80.4 10.3 %collective-permute-start.16 = (bf16[2,128,768]{2,1,0:T(8,128)(2,1)S(1)}, bf16[2,128,768]{2,1,0:T(8,128)(2,1)S(1)}, u32[]{:S(2)}, u32[]{:S(2)}) collective-permute-start(bf16[2,128,768]{2,1,0:T(8,128)(2,1)S(1)} %get-tuple-element.32), channel_id=1, source_target_pairs={{0,4},{4,0},{8,12},{12,8},{1,5},{5,1},{9,13},{13,9},{2,6},{6,2},{1... | collective-permute-start | bytes 1179656 | tf_op jit(solution)/shard_map/ppermute | solution.py:131
  80.6 6.8 %copy-start.11 = (bf16[64,4096]{1,0:T(8,128)(2,1)S(1)}, bf16[64,4096]{1,0:T(8,128)(2,1)}, u32[]{:S(2)}) copy-start(bf16[64,4096]{1,0:T(8,128)(2,1)} %copy-done.10) | copy-start | bytes 1572868
  80.6 6.8 %copy-start.13 = (bf16[64,4096]{1,0:T(8,128)(2,1)S(1)}, bf16[64,4096]{1,0:T(8,128)(2,1)}, u32[]{:S(2)}) copy-start(bf16[64,4096]{1,0:T(8,128)(2,1)} %copy-done.12) | copy-start | bytes 1572868
  86.9 6.9 %collective-permute-start.15 = (bf16[2,128,1024]{2,1,0:T(8,128)(2,1)S(1)}, bf16[2,128,1024]{2,1,0:T(8,128)(2,1)}, u32[]{:S(2)}, u32[]{:S(2)}) collective-permute-start(bf16[2,128,1024]{2,1,0:T(8,128)(2,1)S(1)} %get-tuple-element.30), channel_id=1, source_target_pairs={{0,4},{4,0},{8,12},{12,8},{1,5},{5,1},{9,13},{13,9},{2,6},{6,2},{1... | collective-permute-start | bytes 1572872 | tf_op jit(solution)/shard_map/ppermute | solution.py:131
  90.7 15.9 %collective-permute-start.13 = (bf16[64,4096]{1,0:T(8,128)(2,1)}, bf16[64,4096]{1,0:T(8,128)(2,1)S(1)}, u32[]{:S(2)}, u32[]{:S(2)}) collective-permute-start(bf16[64,4096]{1,0:T(8,128)(2,1)} %constant_dynamic-slice_fusion), channel_id=1, source_target_pairs={{0,8},{4,12},{8,0},{12,4},{1,9},{5,13},{9,1},{13,5},{2,10},{6,14},... | collective-permute-start | bytes 1572872 | tf_op jit(solution)/shard_map/ppermute | solution.py:135
  93.8 21.2 %collective-permute-start.20 = (bf16[2,128,768]{2,1,0:T(8,128)(2,1)S(1)}, bf16[2,128,768]{2,1,0:T(8,128)(2,1)S(1)}, u32[]{:S(2)}, u32[]{:S(2)}) collective-permute-start(bf16[2,128,768]{2,1,0:T(8,128)(2,1)S(1)} %add_convert_fusion.2), channel_id=1, source_target_pairs={{0,8},{4,12},{8,0},{12,4},{1,9},{5,13},{9,1},{13,5},{2,10},{6,14},... | collective-permute-start | bytes 1179656 | tf_op jit(solution)/shard_map/ppermute | solution.py:135
  106.6 1.7 copy-start.14
  106.6 2.8 copy-start.16
  106.7 10.5 %copy-start.7 = (bf16[2,128,1792]{2,1,0:T(8,128)(2,1)S(1)}, bf16[2,128,1792]{2,1,0:T(8,128)(2,1)}, u32[]{:S(2)}) copy-start(bf16[2,128,1792]{2,1,0:T(8,128)(2,1)} %copy-done.6) | copy-start | bytes 2752516
  106.7 13.7 %collective-permute-start.17 = (bf16[64,4096]{1,0:T(8,128)(2,1)S(1)}, bf16[64,4096]{1,0:T(8,128)(2,1)S(1)}, u32[]{:S(2)}, u32[]{:S(2)}) collective-permute-start(bf16[64,4096]{1,0:T(8,128)(2,1)S(1)} %collective-permute-done.13), channel_id=1, source_target_pairs={{0,1},{1,0},{2,3},{3,2},{4,5},{5,4},{6,7},{7,6},{8,9},{9,8},{10,11... | collective-permute-start | bytes 1572872 | tf_op jit(solution)/shard_map/ppermute | solution.py:169
  109.4 39.5 %collective-permute-start.26 = (bf16[2,128,768]{2,1,0:T(8,128)(2,1)S(1)}, bf16[2,128,768]{2,1,0:T(8,128)(2,1)}, u32[]{:S(2)}, u32[]{:S(2)}) collective-permute-start(bf16[2,128,768]{2,1,0:T(8,128)(2,1)S(1)} %copy-done.16), channel_id=1, source_target_pairs={{0,8},{4,12},{8,0},{12,4},{1,9},{5,13},{9,1},{13,5},{2,10},{6,14},... | collective-permute-start | bytes 1179656 | tf_op jit(solution)/shard_map/ppermute | solution.py:135
  115.1 19.2 %collective-permute-start.22 = (bf16[2,128,1024]{2,1,0:T(8,128)(2,1)}, bf16[2,128,1024]{2,1,0:T(8,128)(2,1)}, u32[]{:S(2)}, u32[]{:S(2)}) collective-permute-start(bf16[2,128,1024]{2,1,0:T(8,128)(2,1)} %add_convert_fusion), channel_id=1, source_target_pairs={{0,8},{4,12},{8,0},{12,4},{1,9},{5,13},{9,1},{13,5},{2,10},{6,14},... | collective-permute-start | bytes 1572872 | tf_op jit(solution)/shard_map/ppermute | solution.py:135
  120.4 27.3 %collective-permute-start.24 = (bf16[2,128,1792]{2,1,0:T(8,128)(2,1)}, bf16[2,128,1792]{2,1,0:T(8,128)(2,1)}, u32[]{:S(2)}, u32[]{:S(2)}) collective-permute-start(bf16[2,128,1792]{2,1,0:T(8,128)(2,1)} %get-tuple-element.37), channel_id=1, source_target_pairs={{0,4},{4,0},{8,12},{12,8},{1,5},{5,1},{9,13},{13,9},{2,6},{6,2},{1... | collective-permute-start | bytes 2752520 | tf_op jit(solution)/shard_map/ppermute | solution.py:131
  123.1 11.1 %copy-start.15 = (bf16[2,128,1024]{2,1,0:T(8,128)(2,1)S(1)}, bf16[2,128,1024]{2,1,0:T(8,128)(2,1)}, u32[]{:S(2)}) copy-start(bf16[2,128,1024]{2,1,0:T(8,128)(2,1)} %add_convert_fusion.1) | copy-start | bytes 1572868
  134.3 13.4 %collective-permute-start.25 = (bf16[2,128,1024]{2,1,0:T(8,128)(2,1)S(1)}, bf16[2,128,1024]{2,1,0:T(8,128)(2,1)S(1)}, u32[]{:S(2)}, u32[]{:S(2)}) collective-permute-start(bf16[2,128,1024]{2,1,0:T(8,128)(2,1)S(1)} %copy-done.15), channel_id=1, source_target_pairs={{0,8},{4,12},{8,0},{12,4},{1,9},{5,13},{9,1},{13,5},{2,10},{6,14},... | collective-permute-start | bytes 1572872 | tf_op jit(solution)/shard_map/ppermute | solution.py:135
  147.7 5.6 %collective-permute-start.6 = (bf16[1,16,32,128]{3,2,1,0:T(8,128)(2,1)}, bf16[1,16,32,128]{3,2,1,0:T(8,128)(2,1)S(1)}, u32[]{:S(2)}, u32[]{:S(2)}) collective-permute-start(bf16[1,16,32,128]{3,2,1,0:T(8,128)(2,1)} %bitcast.2), channel_id=1, source_target_pairs={{0,3},{1,0},{2,1},{3,2},{4,7},{5,4},{6,5},{7,6},{8,11},{9,8},{10,9... | collective-permute-start | bytes 393224 | tf_op jit(solution)/shard_map/ppermute | solution.py:145
  147.7 75.3 %collective-permute-start.10 = (bf16[128,8192]{0,1:T(8,128)(2,1)}, bf16[128,8192]{0,1:T(8,128)(2,1)}, u32[]{:S(2)}, u32[]{:S(2)}) collective-permute-start(bf16[128,8192]{0,1:T(8,128)(2,1)} %copy.15), channel_id=1, source_target_pairs={{0,4},{4,0},{8,12},{12,8},{1,5},{5,1},{9,13},{13,9},{2,6},{6,2},{1... | collective-permute-start | bytes 6291464 | tf_op jit(solution)/shard_map/ppermute | solution.py:131
  149.0 74.0 %collective-permute-start.18 = (bf16[128,8192]{0,1:T(8,128)(2,1)}, bf16[128,8192]{0,1:T(8,128)(2,1)}, u32[]{:S(2)}, u32[]{:S(2)}) collective-permute-start(bf16[128,8192]{0,1:T(8,128)(2,1)} %constant_dynamic-update-slice_fusion), channel_id=1, source_target_pairs={{0,4},{4,0},{8,12},{12,8},{1,5},{5,1},{9,13},{13,9},{2,6},{6,2},{1... | collective-permute-start | bytes 6291464 | tf_op jit(solution)/shard_map/ppermute | solution.py:131
  151.1 7.8 %collective-permute-start.29 = (bf16[128,768]{1,0:T(8,128)(2,1)S(1)}, bf16[128,768]{1,0:T(8,128)(2,1)S(1)}, u32[]{:S(2)}, u32[]{:S(2)}) collective-permute-start(bf16[128,768]{1,0:T(8,128)(2,1)S(1)} %fusion.22.mine_ref), channel_id=1, source_target_pairs={{0,8},{4,12},{8,0},{12,4},{1,9},{5,13},{9,1},{13,5},{2,10},{6,14},... | collective-permute-start | bytes 589832 | tf_op jit(solution)/shard_map/ppermute | solution.py:135
  152.6 11.9 %collective-permute-start.31 = (bf16[128,1024]{1,0:T(8,128)(2,1)S(1)}, bf16[128,1024]{1,0:T(8,128)(2,1)S(1)}, u32[]{:S(2)}, u32[]{:S(2)}) collective-permute-start(bf16[128,1024]{1,0:T(8,128)(2,1)S(1)} %fusion.15.mine_ref), channel_id=1, source_target_pairs={{0,8},{4,12},{8,0},{12,4},{1,9},{5,13},{9,1},{13,5},{2,10},{6,14},... | collective-permute-start | bytes 786440 | tf_op jit(solution)/shard_map/ppermute | solution.py:135
  153.3 20.1 %collective-permute-start.27 = (bf16[128,1792]{1,0:T(8,128)(2,1)S(1)}, bf16[128,1792]{1,0:T(8,128)(2,1)S(1)}, u32[]{:S(2)}, u32[]{:S(2)}) collective-permute-start(bf16[128,1792]{1,0:T(8,128)(2,1)S(1)} %pad_maximum_fusion.4.mine_ref), channel_id=1, source_target_pairs={{0,8},{4,12},{8,0},{12,4},{1,9},{5,13},{9,1},{13,5},{2,10},{6,14},... | collective-permute-start | bytes 1376264 | tf_op jit(solution)/shard_map/ppermute | solution.py:135
  158.9 14.5 %collective-permute-start.33 = (bf16[128,1792]{1,0:T(8,128)(2,1)S(1)}, bf16[128,1792]{1,0:T(8,128)(2,1)S(1)}, u32[]{:S(2)}, u32[]{:S(2)}) collective-permute-start(bf16[128,1792]{1,0:T(8,128)(2,1)S(1)} %pad_maximum_fusion.4.mine_ref), channel_id=1, source_target_pairs={{0,4},{4,0},{8,12},{12,8},{1,5},{5,1},{9,13},{13,9},{2,6},{6,2},{1... | collective-permute-start | bytes 1376264 | tf_op jit(solution)/shard_map/ppermute | solution.py:131
  164.5 18.5 %collective-permute-start.32 = (bf16[128,1024]{1,0:T(8,128)(2,1)S(1)}, bf16[128,1024]{1,0:T(8,128)(2,1)S(1)}, u32[]{:S(2)}, u32[]{:S(2)}) collective-permute-start(bf16[128,1024]{1,0:T(8,128)(2,1)S(1)} %collective-permute-done.31.mine_ref), channel_id=1, source_target_pairs={{0,4},{4,0},{8,12},{12,8},{1,5},{5,1},{9,13},{13,9},{2,6},{6,2},{1... | collective-permute-start | bytes 786440 | tf_op jit(solution)/shard_map/ppermute | solution.py:131
  173.4 21.3 %collective-permute-start.28 = (bf16[128,1792]{1,0:T(8,128)(2,1)S(1)}, bf16[128,1792]{1,0:T(8,128)(2,1)S(1)}, u32[]{:S(2)}, u32[]{:S(2)}) collective-permute-start(bf16[128,1792]{1,0:T(8,128)(2,1)S(1)} %collective-permute-done.27.mine_ref), channel_id=1, source_target_pairs={{0,4},{4,0},{8,12},{12,8},{1,5},{5,1},{9,13},{13,9},{2,6},{6,2},{1... | collective-permute-start | bytes 1376264 | tf_op jit(solution)/shard_map/ppermute | solution.py:131
  173.4 16.3 %collective-permute-start.30 = (bf16[128,768]{1,0:T(8,128)(2,1)S(1)}, bf16[128,768]{1,0:T(8,128)(2,1)S(1)}, u32[]{:S(2)}, u32[]{:S(2)}) collective-permute-start(bf16[128,768]{1,0:T(8,128)(2,1)S(1)} %collective-permute-done.29.mine_ref), channel_id=1, source_target_pairs={{0,4},{4,0},{8,12},{12,8},{1,5},{5,1},{9,13},{13,9},{2,6},{6,2},{1... | collective-permute-start | bytes 589832 | tf_op jit(solution)/shard_map/ppermute | solution.py:131
  181.6 1.3 copy-start.2
  183.0 20.8 %collective-permute-start.23 = (bf16[128,1024]{1,0:T(8,128)(2,1)S(1)}, bf16[128,1024]{1,0:T(8,128)(2,1)S(1)}, u32[]{:S(2)}, u32[]{:S(2)}) collective-permute-start(bf16[128,1024]{1,0:T(8,128)(2,1)S(1)} %fusion.15.mine_ref), channel_id=1, source_target_pairs={{0,4},{4,0},{8,12},{12,8},{1,5},{5,1},{9,13},{13,9},{2,6},{6,2},{1... | collective-permute-start | bytes 786440 | tf_op jit(solution)/shard_map/ppermute | solution.py:131
  188.4 1.3 copy-start.4
  189.7 20.7 %collective-permute-start.21 = (bf16[128,768]{1,0:T(8,128)(2,1)S(1)}, bf16[128,768]{1,0:T(8,128)(2,1)S(1)}, u32[]{:S(2)}, u32[]{:S(2)}) collective-permute-start(bf16[128,768]{1,0:T(8,128)(2,1)S(1)} %fusion.22.mine_ref), channel_id=1, source_target_pairs={{0,4},{4,0},{8,12},{12,8},{1,5},{5,1},{9,13},{13,9},{2,6},{6,2},{1... | collective-permute-start | bytes 589832 | tf_op jit(solution)/shard_map/ppermute | solution.py:131
  202.4 1.3 copy-start.3
  209.1 1.3 copy-start.5
  217.5 5.5 %copy-start.9 = (bf16[128,8192]{0,1:T(8,128)(2,1)S(1)}, bf16[128,8192]{0,1:T(8,128)(2,1)}, u32[]{:S(2)}) copy-start(bf16[128,8192]{0,1:T(8,128)(2,1)} %copy.18) | copy-start | bytes 6291460
  228.3 4.0 %copy-start.8 = (f32[512,2048]{0,1:T(8,128)S(1)}, f32[512,2048]{0,1:T(8,128)}, u32[]{:S(2)}) copy-start(f32[512,2048]{0,1:T(8,128)} %copy.21) | copy-start | bytes 12582916
  238.3 9.4 %collective-permute-start.34 = (bf16[16,32,128]{2,1,0:T(8,128)(2,1)}, bf16[16,32,128]{2,1,0:T(8,128)(2,1)S(1)}, u32[]{:S(2)}, u32[]{:S(2)}) collective-permute-start(bf16[16,32,128]{2,1,0:T(8,128)(2,1)} %get-tuple-element.43), channel_id=1, source_target_pairs={{0,1},{1,2},{2,3},{3,0},{4,5},{5,6},{6,7},{7,4},{8,9},{9,10},{10,1... | collective-permute-start | bytes 393224 | tf_op jit(solution)/shard_map/ppermute | solution.py:158
  240.3 16.0 %collective-permute-start.35 = (bf16[16,32,128]{2,1,0:T(8,128)(2,1)}, bf16[16,32,128]{2,1,0:T(8,128)(2,1)S(1)}, u32[]{:S(2)}, u32[]{:S(2)}) collective-permute-start(bf16[16,32,128]{2,1,0:T(8,128)(2,1)} %get-tuple-element.45), channel_id=1, source_target_pairs={{0,2},{1,3},{2,0},{3,1},{4,6},{5,7},{6,4},{7,5},{8,10},{9,11},{10,... | collective-permute-start | bytes 393224 | tf_op jit(solution)/shard_map/ppermute | solution.py:158
  240.3 16.0 %collective-permute-start.36 = (bf16[16,32,128]{2,1,0:T(8,128)(2,1)}, bf16[16,32,128]{2,1,0:T(8,128)(2,1)S(1)}, u32[]{:S(2)}, u32[]{:S(2)}) collective-permute-start(bf16[16,32,128]{2,1,0:T(8,128)(2,1)} %get-tuple-element.44), channel_id=1, source_target_pairs={{0,3},{1,0},{2,1},{3,2},{4,7},{5,4},{6,5},{7,6},{8,11},{9,8},{10,9... | collective-permute-start | bytes 393224 | tf_op jit(solution)/shard_map/ppermute | solution.py:158
  245.1 17.5 %collective-permute-start.38 = (bf16[16,32,64]{2,1,0:T(8,128)(2,1)S(1)}, bf16[16,32,64]{2,1,0:T(8,128)(2,1)S(1)}, u32[]{:S(2)}, u32[]{:S(2)}) collective-permute-start(bf16[16,32,64]{2,1,0:T(8,128)(2,1)S(1)} %get-tuple-element.40), channel_id=1, source_target_pairs={{0,1},{1,2},{2,3},{3,0},{4,5},{5,6},{6,7},{7,4},{8,9},{9,10},{10,1... | collective-permute-start | bytes 196616 | tf_op jit(solution)/shard_map/ppermute | solution.py:158
  245.1 17.6 %collective-permute-start.39 = (bf16[16,32,64]{2,1,0:T(8,128)(2,1)S(1)}, bf16[16,32,64]{2,1,0:T(8,128)(2,1)S(1)}, u32[]{:S(2)}, u32[]{:S(2)}) collective-permute-start(bf16[16,32,64]{2,1,0:T(8,128)(2,1)S(1)} %get-tuple-element.42), channel_id=1, source_target_pairs={{0,2},{1,3},{2,0},{3,1},{4,6},{5,7},{6,4},{7,5},{8,10},{9,11},{10,... | collective-permute-start | bytes 196616 | tf_op jit(solution)/shard_map/ppermute | solution.py:158
  247.7 15.1 %collective-permute-start.40 = (bf16[16,32,64]{2,1,0:T(8,128)(2,1)S(1)}, bf16[16,32,64]{2,1,0:T(8,128)(2,1)S(1)}, u32[]{:S(2)}, u32[]{:S(2)}) collective-permute-start(bf16[16,32,64]{2,1,0:T(8,128)(2,1)S(1)} %get-tuple-element.41), channel_id=1, source_target_pairs={{0,3},{1,0},{2,1},{3,2},{4,7},{5,4},{6,5},{7,6},{8,11},{9,8},{10,9... | collective-permute-start | bytes 196616 | tf_op jit(solution)/shard_map/ppermute | solution.py:158
  256.4 21.2 %collective-permute-start.37 = (f32[16,32,128]{2,1,0:T(8,128)S(1)}, f32[16,32,128]{2,1,0:T(8,128)S(1)}, u32[]{:S(2)}, u32[]{:S(2)}) collective-permute-start(f32[16,32,128]{2,1,0:T(8,128)S(1)} %fusion.27), channel_id=1, source_target_pairs={{0,0},{4,1},{8,2},{12,3},{1,4},{5,5},{9,6},{13,7},{2,8},{6,9},{10,... | collective-permute-start | bytes 786440 | tf_op jit(solution)/shard_map/ppermute | solution.py:298

commit v3 on v2

--- a/solution.py
+++ b/solution.py
@@ -9,6 +9,8 @@
 from jax.sharding import PartitionSpec as P
 
 BLK = 256
+LANES = 128
+SMALL = pl.CostEstimate(flops=1, bytes_accessed=1, transcendentals=0)
 F32 = jnp.float32
 BF16 = jnp.bfloat16
 
@@ -116,7 +118,7 @@
     )(scalars, mine, other, weight, *totals)
 
 
-def body(tokens, gate_weight, up_weight, down_weight, right_factor, left_factor):
+def general_body(tokens, gate_weight, up_weight, down_weight, right_factor, left_factor):
     fsdp_count = lax.axis_size("fsdp")
     tensor_count = lax.axis_size("tensor")
     chips = fsdp_count // 2
@@ -299,6 +301,480 @@
     return grad_right, grad_left
 
 
+def pack_kernel(idx_ref, tokens_ref, first_ref, rest_ref, sems):
+    half, width = first_ref.shape
+    row = pl.multiple_of(idx_ref[0] * half, half)
+    copies = []
+    for n, out_ref in enumerate((first_ref, rest_ref)):
+        column = pl.multiple_of(idx_ref[n + 1] * width, width)
+        source = tokens_ref.at[pl.ds(row, half), pl.ds(column, width)]
+        copies.append(pltpu.make_async_copy(source, out_ref, sems.at[n]))
+    for copy in copies:
+        copy.start()
+    for copy in copies:
+        copy.wait()
+
+
+def pack_tokens(tokens, half, chip):
+    rows, model = tokens.shape
+    shape = jax.ShapeDtypeStruct((rows // 2, model // 2), BF16)
+    return pl.pallas_call(
+        pack_kernel,
+        in_specs=[pl.BlockSpec(memory_space=pltpu.SMEM), pl.BlockSpec(memory_space=pl.ANY)],
+        out_specs=[pl.BlockSpec(memory_space=pl.ANY)] * 2,
+        out_shape=[shape, shape],
+        scratch_shapes=[pltpu.SemaphoreType.DMA((2,))],
+        cost_estimate=SMALL,
+        name="pack_tokens",
+    )(jnp.stack([half, 1 - chip, chip]).astype(jnp.int32), tokens)
+
+
+def products_kernel(sets, idx_ref, *refs):
+    pieces, (gate_ref, up_ref, mine_ref, other_ref) = refs[: 4 * sets], refs[4 * sets :]
+    lhs = jnp.concatenate([piece[...] for piece in pieces], axis=0)
+    rows = mine_ref.shape[2]
+    for slot, weight_ref in enumerate((gate_ref, up_ref)):
+        product = jnp.dot(lhs, weight_ref[...], preferred_element_type=F32).astype(BF16)
+        for u in range(sets):
+            mine_ref[u, slot] = product[2 * u * rows : (2 * u + 1) * rows]
+            other_ref[u, slot] = product[(2 * u + 1) * rows : (2 * u + 2) * rows]
+
+
+def products(pieces, scalars, gate, up, first, width):
+    feat = gate.shape[0]
+    sets = len(pieces) // 4
+    half = pieces[0][0].shape[0]
+    half = half // 2 if pieces[0][1] is not None else half
+    start = first // BLK
+
+    def piece_spec(row, column):
+        if row is None:
+            return pl.BlockSpec((half, feat), lambda n, s: (0, s[column]))
+        return pl.BlockSpec((half, feat), lambda n, s: (s[row], s[column]))
+
+    weight_spec = pl.BlockSpec((feat, BLK), lambda n, s: (0, s[4] + start + n))
+    out_spec = pl.BlockSpec((sets, 2, 2 * half, BLK), lambda n, s: (0, 0, 0, n))
+    shape = jax.ShapeDtypeStruct((sets, 2, 2 * half, width), BF16)
+    return pl.pallas_call(
+        functools.partial(products_kernel, sets),
+        grid_spec=pltpu.PrefetchScalarGridSpec(
+            num_scalar_prefetch=1,
+            grid=(width // BLK,),
+            in_specs=[piece_spec(row, column) for _, row, column in pieces]
+            + [weight_spec, weight_spec],
+            out_specs=[out_spec, out_spec],
+        ),
+        out_shape=[shape, shape],
+        compiler_params=pltpu.CompilerParams(vmem_limit_bytes=50 * 2**20),
+        cost_estimate=SMALL,
+        name="gate_up_products",
+    )(scalars, *[piece for piece, _, _ in pieces], gate, up)
+
+
+def target_kernel(idx_ref, *refs):
+    pieces, weight_ref, out_ref = refs[:4], refs[4], refs[-1]
+    lhs = jnp.concatenate([piece[...] for piece in pieces], axis=0)
+    product = jnp.dot(lhs, weight_ref[...], preferred_element_type=F32)
+
+    @pl.when(pl.program_id(0) == 0)
+    def _():
+        out_ref[...] = refs[5][...] + product if len(refs) > 6 else product
+
+    @pl.when(pl.program_id(0) > 0)
+    def _():
+        out_ref[...] += product
+
+
+def target_add(total, pieces, weight, row, width):
+    rows, outs = pieces[0][0].shape[0], weight.shape[1]
+    scalars = jnp.reshape(lax.div(row, BLK), (1,)).astype(jnp.int32)
+
+    def piece_spec(first):
+        return pl.BlockSpec((rows, BLK), lambda k, s: (0, first // BLK + k))
+
+    whole = pl.BlockSpec((4 * rows, outs), lambda k, s: (0, 0))
+    totals = [] if total is None else [total]
+    return pl.pallas_call(
+        target_kernel,
+        grid_spec=pltpu.PrefetchScalarGridSpec(
+            num_scalar_prefetch=1,
+            grid=(width // BLK,),
+            in_specs=[piece_spec(first) for _, first in pieces]
+            + [pl.BlockSpec((BLK, outs), lambda k, s: (s[0] + k, 0))]
+            + [whole] * len(totals),
+            out_specs=whole,
+        ),
+        out_shape=jax.ShapeDtypeStruct((4 * rows, outs), F32),
+        compiler_params=pltpu.CompilerParams(vmem_limit_bytes=50 * 2**20),
+        cost_estimate=SMALL,
+        name="target_add",
+    )(scalars, *[piece for piece, _ in pieces], weight, *totals)
+
+
+TN = (((0,), (0,)), ((), ()))
+NT = (((1,), (1,)), ((), ()))
+WIDE = 8
+
+
+def natural(step, chip, per_chip):
+    return lax.rem(chip + step // per_chip, 2) * per_chip + lax.rem(step, per_chip)
+
+
+def student_kernel(steps, late, tensor_count, idx_ref, *refs):
+    count = 12 if late else 4
+    tokens, (right_ref, left_ref, mixed_ref, student_ref, scratch) = refs[:-5], refs[-5:]
+    step = pl.program_id(0)
+    chunk = natural(step, idx_ref[2], steps // 2)
+    pairs = right_ref.shape[2]
+    size = right_ref.shape[3]
+
+    def mix(pieces):
+        for t in range(WIDE):
+            rows = [piece[:, t * size : (t + 1) * size] for piece in pieces]
+            part = lax.dot_general(
+                right_ref[0, t], jnp.concatenate(rows, axis=0), NT, preferred_element_type=F32
+            )
+            start = pl.multiple_of((chunk * WIDE + t) * pairs, pairs)
+            for h in range(scratch.shape[0]):
+                scratch[h, pl.ds(start, pairs), :] = part[:, h * LANES : (h + 1) * LANES]
+
+    if late:
+        pl.when(step < steps // 2)(lambda: mix(tokens[:4]))
+        pl.when(step >= steps // 2)(lambda: mix(tokens[4:]))
+    else:
+        mix(tokens)
+
+    @pl.when(step == steps - 1)
+    def _():
+        blocks = steps * WIDE
+        for j in range(pairs):
+            for h in range(scratch.shape[0]):
+                rows = scratch[h, pl.ds(j, blocks, stride=pairs), :]
+                mixed_ref[j * blocks : (j + 1) * blocks, h * LANES : (h + 1) * LANES] = (
+                    rows.astype(BF16)
+                )
+        for g in range(left_ref.shape[0]):
+            span = slice(g * BLK, (g + 1) * BLK)
+            student_ref[:, span] = lax.dot_general(
+                mixed_ref[span, :], left_ref[g], TN, preferred_element_type=F32
+            ) * (1.0 / tensor_count)
+
+
+def token_specs(half, width, steps, begin, own):
+    def chunk(n, s):
+        step = jnp.maximum(n - begin, 0)
+        return natural(step, s[2], steps // 2)
+
+    if own:
+        return [
+            pl.BlockSpec((half, width), lambda n, s, p=p: (s[p % 2], chunk(n, s)))
+            for p in range(4)
+        ]
+    near = pl.BlockSpec(
+        (half, width), lambda n, s: (0, jnp.clip(n - begin, 0, steps // 2 - 1))
+    )
+    far = pl.BlockSpec(
+        (half, width),
+        lambda n, s: (0, jnp.clip(n - begin - steps // 2, 0, steps // 2 - 1)),
+    )
+    return [near] * 4 + [far] * 4
+
+
+def student_part(tokens, late, scalars, right_rows, left_diag, tensor_count):
+    per_owner, pairs, size = right_rows.shape[1:]
+    blocks = right_rows.shape[0] * per_owner
+    steps = blocks // WIDE
+    half = tokens[0].shape[0] if late else tokens[0].shape[0] // 2
+    halves = per_owner // WIDE
+
+    def right_block(n, s):
+        chunk = natural(n, s[2], steps // 2)
+        return (s[3] ^ (chunk // halves), lax.rem(chunk, halves), 0, 0)
+
+    outs = left_diag.shape[0] * BLK
+    return pl.pallas_call(
+        functools.partial(student_kernel, steps, late, tensor_count),
+        grid_spec=pltpu.PrefetchScalarGridSpec(
+            num_scalar_prefetch=1,
+            grid=(steps,),
+            in_specs=token_specs(half, WIDE * size, steps, 0, not late)
+            + [
+                pl.BlockSpec((1, WIDE, pairs, size), right_block),
+                pl.BlockSpec(left_diag.shape, lambda n, s: (0, 0, 0)),
+            ],
+            out_specs=[
+                pl.BlockSpec((pairs * blocks, 4 * half), lambda n, s: (0, 0)),
+                pl.BlockSpec((4 * half, outs), lambda n, s: (0, 0)),
+            ],
+            scratch_shapes=[pltpu.VMEM((4 * half // LANES, pairs * blocks, LANES), F32)],
+        ),
+        out_shape=[
+            jax.ShapeDtypeStruct((pairs * blocks, 4 * half), BF16),
+            jax.ShapeDtypeStruct((4 * half, outs), F32),
+        ],
+        compiler_params=pltpu.CompilerParams(vmem_limit_bytes=50 * 2**20),
+        cost_estimate=SMALL,
+        name="student_part",
+    )(scalars, *tokens, right_rows, left_diag)
+
+
+def grads_kernel(groups, steps, scale, idx_ref, *refs):
+    total_ref, student0, student1, mixed0, mixed1, left_ref = refs[:6]
+    own, near, far = refs[6:10], refs[10:14], refs[14:18]
+    out_ref, scratch = refs[18:]
+    step = pl.program_id(0)
+    z = idx_ref[3]
+    parts, size = out_ref.shape[0], out_ref.shape[2]
+    pairs = scratch.shape[1] // (steps * WIDE)
+    blocks = steps * WIDE
+    per_part = blocks // parts
+
+    def place(owner):
+        far_bits = z ^ owner
+        return lax.rem(far_bits, 2) * 2 + far_bits // 2
+
+    @pl.when(step < groups)
+    def _():
+        student = jnp.concatenate([student0[...], student1[...]], axis=0)
+        out_grad = ((student - total_ref[...]) * scale).astype(BF16)
+        mixed = jnp.concatenate([mixed0[...], mixed1[...]], axis=1)
+        left = jnp.dot(mixed, out_grad, preferred_element_type=F32).T
+        row = pl.multiple_of(step * BLK, BLK)
+        back = lax.dot_general(left_ref[0], out_grad, NT, preferred_element_type=F32)
+        for h in range(scratch.shape[0]):
+            scratch[h, pl.ds(row, BLK), :] = back[:, h * LANES : (h + 1) * LANES]
+        low = lax.broadcasted_iota(jnp.int32, (blocks, size), 1) < blocks
+        share = blocks // parts
+        for pair in range(BLK // size):
+            lanes = slice(pair * size, (pair + 1) * size)
+            top = left[pair * size : pair * size + blocks, lanes]
+            bottom = left[pair * size + blocks : (pair + 1) * size, lanes]
+            both = jnp.where(low, top, bottom).astype(BF16)
+            begin = per_part * pairs + (step * (BLK // size) + pair) * share
+            begin = pl.multiple_of(begin, share)
+            for owner in range(parts):
+                out_ref[place(owner), pl.ds(begin, share), :] = both[
+                    owner * share : (owner + 1) * share
+                ]
+
+    def right(later):
+        chunk = natural(step - groups, idx_ref[2], steps // 2)
+        for t in range(WIDE):
+            block = chunk * WIDE + t
+            rows = [piece[:, t * size : (t + 1) * size] for piece in own + later]
+            lhs = [
+                scratch[h, pl.ds(block, pairs, stride=blocks), :]
+                for h in range(scratch.shape[0])
+            ]
+            lhs = jnp.concatenate(lhs, axis=1).astype(BF16)
+            value = jnp.dot(
+                lhs, jnp.concatenate(rows, axis=0), preferred_element_type=F32
+            )
+            begin = pl.multiple_of(lax.rem(block, per_part) * pairs, pairs)
+            out_ref[place(block // per_part), pl.ds(begin, pairs), :] = value.astype(BF16)
+
+    pl.when((step >= groups) & (step < groups + steps // 2))(lambda: right(near))
+    pl.when(step >= groups + steps // 2)(lambda: right(far))
+
+
+def factor_grads(total, students, mixed, left_diag, own, late, scalars, parts, size, scale):
+    groups, count = left_diag.shape[0], total.shape[0]
+    rows = mixed[0].shape[0]
+    half = late[0].shape[0]
+    steps = own[0].shape[1] // (WIDE * size)
+    pairs = rows // (steps * WIDE)
+
+    def group(n):
+        return jnp.minimum(n, groups - 1)
+
+    out_rows = (rows + pairs * (steps * WIDE) * (steps * WIDE) // size) // parts
+    return pl.pallas_call(
+        functools.partial(grads_kernel, groups, steps, scale),
+        grid_spec=pltpu.PrefetchScalarGridSpec(
+            num_scalar_prefetch=1,
+            grid=(groups + steps,),
+            in_specs=[pl.BlockSpec((count, BLK), lambda n, s: (0, group(n)))]
+            + [pl.BlockSpec((count // 2, BLK), lambda n, s: (0, group(n)))] * 2
+            + [pl.BlockSpec((BLK, count // 2), lambda n, s: (group(n), 0))] * 2
+            + [pl.BlockSpec((1, BLK, BLK), lambda n, s: (group(n), 0, 0))]
+            + token_specs(half, WIDE * size, steps, groups, True)
+            + token_specs(half, WIDE * size, steps, groups, False),
+            out_specs=pl.BlockSpec((parts, out_rows, size), lambda n, s: (0, 0, 0)),
+            scratch_shapes=[pltpu.VMEM((count // LANES, rows, LANES), F32)],
+        ),
+        out_shape=jax.ShapeDtypeStruct((parts, out_rows, size), BF16),
+        compiler_params=pltpu.CompilerParams(vmem_limit_bytes=50 * 2**20),
+        cost_estimate=SMALL,
+        name="factor_grads",
+    )(scalars, total, *students, *mixed, left_diag, *own, *late)
+
+
+def tiled_body(tokens, gate_weight, up_weight, down_weight, right_factor, left_factor):
+    fsdp_count = lax.axis_size("fsdp")
+    tensor_count = lax.axis_size("tensor")
+    rows, model = tokens.shape
+    part = gate_weight.shape[1] // 2
+    me, z = lax.axis_index("fsdp"), lax.axis_index("tensor")
+    chip, core, odd = lax.div(me, 2), lax.rem(me, 2), lax.rem(z, 2)
+    both_axes = ("fsdp", "tensor")
+
+    def swap(value):
+        return lax.ppermute(value, "fsdp", [(i, i ^ 1) for i in range(fsdp_count)])
+
+    def across(value):
+        return lax.ppermute(value, "fsdp", [(i, i ^ 2) for i in range(fsdp_count)])
+
+    def along(value, bit):
+        return lax.ppermute(value, "tensor", [(i, i ^ bit) for i in range(tensor_count)])
+
+    def turn(value, bit):
+        perm = []
+        for f in range(fsdp_count):
+            for t in range(tensor_count):
+                perm.append((f * tensor_count + t, (t ^ bit) * tensor_count + f))
+        return lax.ppermute(value, both_axes, perm)
+
+    def after(value, *others):
+        return lax.optimization_barrier((value,) + others)[0]
+
+    def gather(value):
+        value = value[None]
+        for bit in (1, 2):
+            value = jnp.concatenate([value, along(value, bit)], axis=0)
+        return value
+
+    def add(*terms):
+        return sum(term.astype(F32) for term in terms)
+
+    head = (part // BLK + 1) // 2 * BLK
+    chunks = [(0, head), (head, part - head)]
+
+    near_tokens = swap(tokens)
+    first, rest = pack_tokens(tokens, odd, chip)
+    arrived = across(first)
+    base = jnp.stack([odd, 1 - odd])
+    mine_block = lax.div(part, BLK) * chip
+    other_block = lax.div(part, BLK) * (1 - chip)
+
+    def scalars(block):
+        return jnp.concatenate([base, jnp.stack([me, core, block])]).astype(jnp.int32)
+
+    own_pieces = [(t, row, 2) for t in (tokens, near_tokens) for row in (0, 1)]
+    got = {}
+
+    def send(e, pieces, order):
+        values = [
+            products(pieces, order, gate_weight, up_weight, *chunk) for chunk in chunks
+        ]
+        swapped = [swap(other[0]) for _, other in values]
+        sums = [add(mine[0], s).astype(BF16) for (mine, _), s in zip(values, swapped)]
+        got[e] = [across(value) for value in sums]
+        return values, sums
+
+    values, sums = send(0, own_pieces, scalars(other_block))
+    last = values[-1][0]
+
+    right_rows = gather(turn(after(right_factor, first), 0))
+    left_rows = gather(after(left_factor, last))
+    for axis, bit in ((0, 2), (1, 1)):
+        split = left_rows.reshape((2, 2) + left_rows.shape[1:])
+        split = jnp.where(lax.rem(lax.div(z, bit), 2) == 1, jnp.flip(split, axis), split)
+        left_rows = split.reshape(left_rows.shape)
+    left_rows = left_rows.transpose(1, 3, 0, 2)
+    pairs, blocks = left_rows.shape[:2]
+    left_rows = left_rows.reshape(-1, BLK // blocks, blocks, 1, blocks)
+    eye = jnp.eye(BLK // blocks, dtype=jnp.bool_)[None, :, None, :, None]
+    left_diag = jnp.where(eye, left_rows, jnp.zeros((), BF16)).reshape(-1, BLK, BLK)
+
+    arrived = after(arrived, last)
+    partner = along(arrived, 1)
+    near_arrived = swap(arrived)
+    late_first = across(after(rest, *sums))
+    order = jnp.concatenate([base, jnp.stack([chip, z])]).astype(jnp.int32)
+    own = [tokens, tokens, near_tokens, near_tokens]
+    mixed0, student0 = student_part(
+        [after(tokens, *sums)] + own[1:], False, order, right_rows, left_diag, tensor_count
+    )
+    partner = after(partner, mixed0)
+    late = [arrived, partner, near_arrived, swap(partner)]
+    late_pieces = [(t, None, 3) for t in late]
+    values, sums = send(1, late_pieces, scalars(other_block))
+
+    kept, other = products(
+        own_pieces + late_pieces,
+        after(scalars(mine_block), *sums),
+        gate_weight,
+        up_weight,
+        0,
+        part,
+    )
+    kept_other = swap(other)
+    late_first = after(late_first, kept)
+    late_partner = along(late_first, 1)
+    late_rest = [late_first, late_partner, swap(late_first), swap(late_partner)]
+
+    def activate(u, span, term):
+        begin, width = span
+        terms = [value[u, :, :, begin : begin + width] for value in (kept, kept_other)]
+        total = add(*terms, term)
+        return (jax.nn.silu(total[0]) * total[1]).astype(BF16)
+
+    hidden_late = jnp.concatenate(
+        [activate(1, span, term) for span, term in zip(chunks, got[0])], axis=1
+    )
+    got_late = across(hidden_late)
+    near_hidden_late = swap(hidden_late)
+    mixed1, student1 = student_part(
+        late + late_rest, True, order, right_rows, left_diag, tensor_count
+    )
+    near_got_late = swap(got_late)
+    total = None
+    hidden = [activate(0, span, term) for span, term in zip(chunks, got[1])]
+    got_hidden = [across(value) for value in hidden]
+    for span, value in zip(chunks, hidden):
+        begin, width = span
+        pieces = [(value, 0), (swap(value), 0), (hidden_late, begin), (near_hidden_late, begin)]
+        total = target_add(total, pieces, down_weight, chip * part + begin, width)
+    for span, value in zip(chunks, got_hidden):
+        begin, width = span
+        pieces = [(got_late, begin), (near_got_late, begin), (value, 0), (swap(value), 0)]
+        total = target_add(total, pieces, down_weight, (1 - chip) * part + begin, width)
+
+    grads = factor_grads(
+        total,
+        (student0, student1),
+        (mixed0, mixed1),
+        left_diag,
+        own,
+        late + late_rest,
+        order,
+        tensor_count,
+        right_factor.shape[2],
+        1.0 / math.sqrt(rows * fsdp_count),
+    )
+    summed = add(grads[:2], along(grads[2:], 1)).astype(BF16)
+    right_shape = right_factor.shape
+    cut = right_shape[0] * right_shape[1]
+    grad_right = add(turn(summed[0, :cut], 0), turn(summed[1, :cut], 2))
+    grad_left = add(summed[0, cut:], along(summed[1, cut:], 2))
+    grad_left = grad_left.reshape(pairs // 2, -1, 2, blocks).transpose(0, 2, 1, 3)
+    return grad_right.reshape(right_shape), grad_left.reshape(left_factor.shape)
+
+
+def body(*args):
+    tokens, gate_weight, _, _, right_factor, left_factor = args
+    counts = (lax.axis_size("fsdp"), lax.axis_size("tensor"))
+    feat, hid = gate_weight.shape
+    per_owner, share, size = right_factor.shape
+    blocks = left_factor.shape[2]
+    fits = hid % (2 * BLK) == 0
+    fits = fits and counts == (4, 4) and tokens.shape[0] == 128
+    fits = fits and hid >= 4 * BLK and feat % BLK == 0
+    fits = fits and size == 128 and 2 * blocks == size and per_owner % WIDE == 0
+    fits = fits and left_factor.shape[0] == share and share % 16 == 0
+    return (tiled_body if fits else general_body)(*args)
+
+
 def solution(mesh):
     return jax.shard_map(
         body,

time: 280 us -> 311 us (1.11)
  the two profiles are of different devices: /device:TPU:2 before, /device:TPU:0 now
where the time goes in v3:
time: 311 us; the launch traced here: 310 us
  Pallas kernels  143 us (46%)
  waiting for transfers between devices  98.7 us (32%)
  starting transfers between devices  41.3 us (13%)
  other arithmetic  16.1 us (5%)
  local copies, waits for them, and re-layouts  10 us (3%)
    ppermute x9, waiting for transfers between devices, across(): return lax.ppermute(value, 'fsdp', [(i, i ^ 2) for i in range(fsdp_count)])  66.7 us
    pallas_call x5, Pallas kernels, products(): pl.pallas_call(functools.partial(products_kernel, sets), grid_spec=pltpu....  38.4 us
    pallas_call x4, Pallas kernels, target_add(): pl.pallas_call(target_kernel, grid_spec=pltpu.PrefetchScalarGridSpec(num_...  34 us
    pallas_call x1, Pallas kernels, pack_tokens(): pl.pallas_call(pack_kernel, in_specs=[pl.BlockSpec(memory_space=pltpu.SME...  33.5 us
    pallas_call x2, Pallas kernels, student_part(): pl.pallas_call(functools.partial(student_kernel, steps, late, tensor_coun...  19.7 us
    ppermute x8, waiting for transfers between devices, along(): lax.ppermute(value, 'tensor', [(i, i ^ bit) for i in range(tensor_count)])  19.5 us
    ppermute x8, starting transfers between devices, along(): lax.ppermute(value, 'tensor', [(i, i ^ bit) for i in range(tensor_count)])  18.5 us
    pallas_call x1, Pallas kernels, factor_grads(): pl.pallas_call(functools.partial(grads_kernel, groups, steps, scale), gri...  17.1 us
  transfers between devices with their start and end apart: 36, of which 14 were waited for; matrix products, arithmetic and copies ran while one was open for 7% of the time, Pallas kernels for 32%

profile of v3, /device:TPU:0, one launch (start us, length us, event | category | flops | bytes accessed | tf_op | source)
XLA Modules:
  0.0 309.9 jit_solution(15433279097097411599)
XLA Ops:
  0.6 0.5 collective-permute-start.1
  1.2 0.6 pad_add_fusion.1.idx_ref
  1.7 33.5 %pack_tokens.1 = (bf16[64,4096]{1,0:T(8,128)(2,1)}, bf16[64,4096]{1,0:T(8,128)(2,1)}) custom-call(s32[3]{0:T(128)} %pad_add_fusion.1.idx_ref, bf16[128,8192]{1,0:T(8,128)(2,1)} %refs_7_.1), custom_call_target="tpu_custom_call" | custom-call | flops 1 | bytes 1 | tf_op jit(solution)/shard_map/pack_tokens/pallas_call | solution.py:321
  35.3 1.6 collective-permute-start.5
  36.9 7.5 %collective-permute-start.6 = (bf16[1,16,32,128]{3,2,1,0:T(8,128)(2,1)S(1)}, bf16[1,16,32,128]{3,2,1,0:T(8,128)(2,1)S(1)}, u32[]{:S(2)}, u32[]{:S(2)}) collective-permute-start(bf16[1,16,32,128]{3,2,1,0:T(8,128)(2,1)S(1)} %bitcast.106), channel_id=1, source_target_pairs={{0,1},{1,0},{2,3},{3,2},{4,5},{5,4},{6,7},{7,6},{8,9},{9,8},{10,11... | collective-permute-start | bytes 393224 | tf_op jit(solution)/shard_map/ppermute | solution.py:628
  44.4 6.2 %collective-permute-start = (bf16[64,4096]{1,0:T(8,128)(2,1)}, bf16[64,4096]{1,0:T(8,128)(2,1)S(1)}, u32[]{:S(2)}, u32[]{:S(2)}) collective-permute-start(bf16[64,4096]{1,0:T(8,128)(2,1)} %get-tuple-element.26), channel_id=1, source_target_pairs={{0,8},{4,12},{8,0},{12,4},{1,9},{5,13},{9,1},{13,5},{2,10},{6,14},... | collective-permute-start | bytes 1572872 | tf_op jit(solution)/shard_map/ppermute | solution.py:625
  50.7 0.7 pad_maximum_fusion.3
  51.5 3.8 %collective-permute-start.7 = (bf16[2,16,32,128]{3,2,1,0:T(8,128)(2,1)}, bf16[2,16,32,128]{3,2,1,0:T(8,128)(2,1)}, u32[]{:S(2)}, u32[]{:S(2)}) collective-permute-start(bf16[2,16,32,128]{3,2,1,0:T(8,128)(2,1)} %pad_maximum_fusion.3), channel_id=1, source_target_pairs={{0,2},{1,3},{2,0},{3,1},{4,6},{5,7},{6,4},{7,5},{8,10},{9,11},{10,... | collective-permute-start | bytes 786440 | tf_op jit(solution)/shard_map/ppermute | solution.py:628
  55.2 6.0 %gate_up_products.5 = (bf16[1,2,128,768]{3,2,1,0:T(8,128)(2,1)S(1)}, bf16[1,2,128,768]{3,2,1,0:T(8,128)(2,1)}) custom-call(s32[5]{0:T(128)S(1)} %concatenate.33.idx_ref, bf16[128,8192]{1,0:T(8,128)(2,1)S(1)} %copy-done, bf16[128,8192]{1,0:T(8,128)(2,1)S(1)} %copy-done, bf16[128,8192]{1,0:T(8,128)(2,1)} %collective-permute-done.1.refs_2_.refs_3_.refs_8_.refs_9_, ...), custom_call_target="tpu_custom_call" | custom-call | flops 1 | bytes 1 | tf_op jit(solution)/shard_map/gate_up_products/pallas_call | solution.py:358
  61.2 2.0 collective-permute-start.8
  63.2 7.8 %collective-permute-done.8 = bf16[1,32,16,64]{3,2,1,0:T(8,128)(2,1)S(1)} collective-permute-done((bf16[1,32,16,64]{3,2,1,0:T(8,128)(2,1)S(1)}, bf16[1,32,16,64]{3,2,1,0:T(8,128)(2,1)S(1)}, u32[]{:S(2)}, u32[]{:S(2)}) %collective-permute-start.8) | collective-permute-done | bytes 65568 | tf_op jit(solution)/shard_map/ppermute | solution.py:628
  71.0 0.8 pad_maximum_fusion.4
  71.8 1.5 collective-permute-start.9
  73.5 0.9 broadcast_in_dim.37
  74.4 1.9 pad_maximum_fusion.refs_4_.refs_8_
  76.3 2.5 collective-permute-start.2
  78.9 6.9 %gate_up_products.6 = (bf16[1,2,128,1024]{3,2,1,0:T(8,128)(2,1)S(1)}, bf16[1,2,128,1024]{3,2,1,0:T(8,128)(2,1)}) custom-call(s32[5]{0:T(128)S(1)} %concatenate.33.idx_ref, bf16[128,8192]{1,0:T(8,128)(2,1)S(1)} %copy-done, bf16[128,8192]{1,0:T(8,128)(2,1)S(1)} %copy-done, bf16[128,8192]{1,0:T(8,128)(2,1)} %collective-permute-done.1.refs_2_.refs_3_.refs_8_.refs_9_, ...), custom_call_target="tpu_custom_call" | custom-call | flops 1 | bytes 1 | tf_op jit(solution)/shard_map/gate_up_products/pallas_call | solution.py:358
  85.8 0.5 collective-permute-start.3
  86.4 0.7 collective-permute-done.9
  87.1 1.1 pad_maximum_fusion.1
  88.5 1.0 copy.12
  89.6 1.8 broadcast_in_dim.41
  91.4 2.2 broadcast_in_dim.42
  93.6 1.4 broadcast_select_fusion.refs_5_.refs_9_
  95.0 2.2 fusion.3
  97.2 2.0 fusion.1
  99.2 9.6 %student_part.2 = (bf16[2048,256]{1,0:T(8,128)(2,1)S(1)}, f32[256,2048]{1,0:T(8,128)}) custom-call(s32[4]{0:T(128)S(1)} %pad_add_fusion.idx_ref, bf16[128,8192]{1,0:T(8,128)(2,1)} %refs_7_.1, bf16[128,8192]{1,0:T(8,128)(2,1)} %refs_7_.1, bf16[128,8192]{1,0:T(8,128)(2,1)} %collective-permute-done.1.refs_2_.refs_3_.refs_8_.refs_9_, ...), custom_call_target="tpu_custom_call" | custom-call | flops 1 | bytes 1 | tf_op jit(solution)/shard_map/student_part/pallas_call | solution.py:495
  108.9 1.9 collective-permute-done.11.refs_3_.refs_7_.refs_13_
  110.7 5.9 %gate_up_products.8 = (bf16[1,2,128,768]{3,2,1,0:T(8,128)(2,1)S(1)}, bf16[1,2,128,768]{3,2,1,0:T(8,128)(2,1)}) custom-call(s32[5]{0:T(128)S(1)} %concatenate.33.idx_ref, bf16[64,4096]{1,0:T(8,128)(2,1)S(1)} %collective-permute-done.refs_0_.refs_4_.refs_10_, bf16[64,4096]{1,0:T(8,128)(2,1)S(1)} %collective-permute-done.2.refs_1_.refs_5_.refs_11_, ...), custom_call_target="tpu_custom_call" | custom-call | flops 1 | bytes 1 | tf_op jit(solution)/shard_map/gate_up_products/pallas_call | solution.py:358
  116.8 6.2 %gate_up_products.7 = (bf16[1,2,128,1024]{3,2,1,0:T(8,128)(2,1)S(1)}, bf16[1,2,128,1024]{3,2,1,0:T(8,128)(2,1)S(1)}) custom-call(s32[5]{0:T(128)S(1)} %concatenate.33.idx_ref, bf16[64,4096]{1,0:T(8,128)(2,1)S(1)} %collective-permute-done.refs_0_.refs_4_.refs_10_, bf16[64,4096]{1,0:T(8,128)(2,1)S(1)} %collective-permute-done.2.refs_1_.refs_5_.refs_11_, ...), custom_call_target="tpu_custom_call" | custom-call | flops 1 | bytes 1 | tf_op jit(solution)/shard_map/gate_up_products/pallas_call | solution.py:358
  123.0 0.4 collective-permute-start.12
  123.6 1.1 fusion.2
  125.2 13.3 %gate_up_products.9 = (bf16[2,2,128,1792]{3,2,1,0:T(8,128)(2,1)S(1)}, bf16[2,2,128,1792]{3,2,1,0:T(8,128)(2,1)}) custom-call(s32[5]{0:T(128)S(1)} %concatenate.32.idx_ref, bf16[128,8192]{1,0:T(8,128)(2,1)} %refs_7_.1, bf16[128,8192]{1,0:T(8,128)(2,1)} %refs_7_.1, bf16[128,8192]{1,0:T(8,128)(2,1)} %collective-permute-done.1.refs_2_.refs_3_.refs_8_.refs_9_, ...), custom_call_target="tpu_custom_call" | custom-call | flops 1 | bytes 1 | tf_op jit(solution)/shard_map/gate_up_products/pallas_call | solution.py:358
  139.0 2.0 collective-permute-start.15
  141.1 2.0 collective-permute-start.16
  143.0 10.7 %collective-permute-done.28.refs_4_.refs_14_ = bf16[64,4096]{1,0:T(8,128)(2,1)S(1)} collective-permute-done((bf16[64,4096]{1,0:T(8,128)(2,1)S(1)}, bf16[64,4096]{1,0:T(8,128)(2,1)S(1)}, u32[]{:S(2)}, u32[]{:S(2)}) %collective-permute-start.28) | collective-permute-done | bytes 524320 | tf_op jit(solution)/shard_map/ppermute | solution.py:625
  153.7 11.2 %collective-permute-done.15 = bf16[2,128,1024]{2,1,0:T(8,128)(2,1)S(1)} collective-permute-done((bf16[2,128,1024]{2,1,0:T(8,128)(2,1)S(1)}, bf16[2,128,1024]{2,1,0:T(8,128)(2,1)S(1)}, u32[]{:S(2)}, u32[]{:S(2)}) %collective-permute-start.15) | collective-permute-done | bytes 524320 | tf_op jit(solution)/shard_map/ppermute | solution.py:625
  165.0 11.2 %collective-permute-done.22 = bf16[2,128,1024]{2,1,0:T(8,128)(2,1)S(1)} collective-permute-done((bf16[2,128,1024]{2,1,0:T(8,128)(2,1)S(1)}, bf16[2,128,1024]{2,1,0:T(8,128)(2,1)S(1)}, u32[]{:S(2)}, u32[]{:S(2)}) %collective-permute-start.22) | collective-permute-done | bytes 524320 | tf_op jit(solution)/shard_map/ppermute | solution.py:625
  176.7 7.9 %collective-permute-done.16 = bf16[2,128,768]{2,1,0:T(8,128)(2,1)S(1)} collective-permute-done((bf16[2,128,768]{2,1,0:T(8,128)(2,1)S(1)}, bf16[2,128,768]{2,1,0:T(8,128)(2,1)S(1)}, u32[]{:S(2)}, u32[]{:S(2)}) %collective-permute-start.16) | collective-permute-done | bytes 393248 | tf_op jit(solution)/shard_map/ppermute | solution.py:625
  184.6 7.6 %collective-permute-done.19 = bf16[2,128,768]{2,1,0:T(8,128)(2,1)S(1)} collective-permute-done((bf16[2,128,768]{2,1,0:T(8,128)(2,1)S(1)}, bf16[2,128,768]{2,1,0:T(8,128)(2,1)S(1)}, u32[]{:S(2)}, u32[]{:S(2)}) %collective-permute-start.19) | collective-permute-done | bytes 393248 | tf_op jit(solution)/shard_map/ppermute | solution.py:625
  193.0 0.5 collective-permute-start.26
  193.8 1.8 collective-permute-start.23
  195.6 10.7 %collective-permute-done.17.refs_0_ = bf16[128,1792]{1,0:T(8,128)(2,1)} collective-permute-done((bf16[128,1792]{1,0:T(8,128)(2,1)S(1)}, bf16[128,1792]{1,0:T(8,128)(2,1)}, u32[]{:S(2)}, u32[]{:S(2)}) %collective-permute-start.17) | collective-permute-done | bytes 458784 | tf_op jit(solution)/shard_map/ppermute | solution.py:625
  206.3 0.8 fusion.9.refs_0_
  207.4 2.8 collective-permute-done.23.refs_2_
  210.2 4.6 %collective-permute-done.20.refs_2_ = bf16[128,768]{1,0:T(8,128)(2,1)} collective-permute-done((bf16[128,768]{1,0:T(8,128)(2,1)}, bf16[128,768]{1,0:T(8,128)(2,1)}, u32[]{:S(2)}, u32[]{:S(2)}) %collective-permute-start.20) | collective-permute-done | bytes 196640 | tf_op jit(solution)/shard_map/ppermute | solution.py:625
  214.8 0.7 copy-done.8
  215.5 0.5 collective-permute-start.21
  216.0 1.0 copy-done.4
  217.1 10.2 %student_part.3 = (bf16[2048,256]{1,0:T(8,128)(2,1)}, f32[256,2048]{1,0:T(8,128)}) custom-call(s32[4]{0:T(128)S(1)} %pad_add_fusion.idx_ref, bf16[64,4096]{1,0:T(8,128)(2,1)S(1)} %collective-permute-done.refs_0_.refs_4_.refs_10_, bf16[64,4096]{1,0:T(8,128)(2,1)S(1)} %collective-permute-done.2.refs_1_.refs_5_.refs_11_, ...), custom_call_target="tpu_custom_call" | custom-call | flops 1 | bytes 1 | tf_op jit(solution)/shard_map/student_part/pallas_call | solution.py:495
  227.2 7.9 %target_add.4.refs_5_ = f32[512,2048]{1,0:T(8,128)} custom-call(s32[1]{0:T(128)} %bitcast.38.idx_ref, bf16[128,1024]{1,0:T(8,128)(2,1)S(1)} %fusion.5.refs_0_, bf16[128,1024]{1,0:T(8,128)(2,1)S(1)} %copy-done.9, bf16[128,1792]{1,0:T(8,128)(2,1)S(1)} %pad_maximum_fusion.2.refs_2_, bf16[128,1792]{1,0:T(8,128)(2,1)} %collective-permute-done.26.refs_3_, ...), custom_call_target="tpu_custom_call" | custom-call | flops 1 | bytes 1 | tf_op jit(solution)/shard_map/target_add/pallas_call | solution.py:397
  235.2 8.2 %target_add.5.refs_5_ = f32[512,2048]{1,0:T(8,128)} custom-call(s32[1]{0:T(128)} %bitcast.37.idx_ref, bf16[128,768]{1,0:T(8,128)(2,1)} %fusion.9.refs_0_, bf16[128,768]{1,0:T(8,128)(2,1)} %collective-permute-done.25.refs_1_, bf16[128,1792]{1,0:T(8,128)(2,1)S(1)} %pad_maximum_fusion.2.refs_2_, bf16[128,1792]{1,0:T(8,128)(2,1)} %collective-permute-done.26.refs_3_, ...), custom_call_target="tpu_custom_call" | custom-call | flops 1 | bytes 1 | tf_op jit(solution)/shard_map/target_add/pallas_call | solution.py:397
  243.4 9.5 %target_add.6.refs_5_ = f32[512,2048]{1,0:T(8,128)} custom-call(s32[1]{0:T(128)} %bitcast.33.idx_ref, bf16[128,1792]{1,0:T(8,128)(2,1)} %collective-permute-done.17.refs_0_, bf16[128,1792]{1,0:T(8,128)(2,1)} %collective-permute-done.18.refs_1_, bf16[128,1024]{1,0:T(8,128)(2,1)} %collective-permute-done.23.refs_2_, ...), custom_call_target="tpu_custom_call" | custom-call | flops 1 | bytes 1 | tf_op jit(solution)/shard_map/target_add/pallas_call | solution.py:397
  252.9 8.3 %target_add.7.refs_0_ = f32[512,2048]{1,0:T(8,128)} custom-call(s32[1]{0:T(128)} %bitcast.4.idx_ref, bf16[128,1792]{1,0:T(8,128)(2,1)} %collective-permute-done.17.refs_0_, bf16[128,1792]{1,0:T(8,128)(2,1)} %collective-permute-done.18.refs_1_, bf16[128,768]{1,0:T(8,128)(2,1)} %collective-permute-done.20.refs_2_, ...), custom_call_target="tpu_custom_call" | custom-call | flops 1 | bytes 1 | tf_op jit(solution)/shard_map/target_add/pallas_call | solution.py:397
  261.3 17.1 %factor_grads.1 = bf16[4,768,128]{2,1,0:T(8,128)(2,1)} custom-call(s32[4]{0:T(128)S(1)} %pad_add_fusion.idx_ref, f32[512,2048]{1,0:T(8,128)} %target_add.7.refs_0_, f32[256,2048]{1,0:T(8,128)} %get-tuple-element.44.refs_1_, f32[256,2048]{1,0:T(8,128)} %get-tuple-element.48.refs_2_, bf16[2048,256]{1,0:T(8,128)(2,1)} %copy-done.5, ...), custom_call_target="tpu_custom_call" | custom-call | flops 1 | bytes 1 | tf_op jit(solution)/shard_map/factor_grads/pallas_call | solution.py:591
  278.3 1.0 slice.101
  279.4 11.0 %collective-permute-done.32 = bf16[2,768,128]{2,1,0:T(8,128)(2,1)S(1)} collective-permute-done((bf16[2,768,128]{2,1,0:T(8,128)(2,1)S(1)}, bf16[2,768,128]{2,1,0:T(8,128)(2,1)S(1)}, u32[]{:S(2)}, u32[]{:S(2)}) %collective-permute-start.32) | collective-permute-done | bytes 393248 | tf_op jit(solution)/shard_map/ppermute | solution.py:628
  290.5 1.1 add_convert_fusion
  291.6 1.1 collective-permute-start.35
  292.7 0.7 collective-permute-start.33
  293.4 4.6 %collective-permute-start.34 = (bf16[512,128]{1,0:T(8,128)(2,1)S(1)}, bf16[512,128]{1,0:T(8,128)(2,1)S(1)}, u32[]{:S(2)}, u32[]{:S(2)}) collective-permute-start(bf16[512,128]{1,0:T(8,128)(2,1)S(1)} %get-tuple-element.55), channel_id=1, source_target_pairs={{0,8},{1,12},{2,0},{3,4},{4,9},{5,13},{6,1},{7,5},{8,10},{9,14},{1... | collective-permute-start | bytes 393224 | tf_op jit(solution)/shard_map/ppermute | solution.py:635
  298.2 0.7 copy.13
  299.0 10.2 %collective-permute-done.34 = bf16[512,128]{1,0:T(8,128)(2,1)S(1)} collective-permute-done((bf16[512,128]{1,0:T(8,128)(2,1)S(1)}, bf16[512,128]{1,0:T(8,128)(2,1)S(1)}, u32[]{:S(2)}, u32[]{:S(2)}) %collective-permute-start.34) | collective-permute-done | bytes 131104 | tf_op jit(solution)/shard_map/ppermute | solution.py:635
  309.2 0.7 convert_add_fusion.4
  (98 shorter events, 4.3 us)
Async XLA Ops:
  0.6 54.6 %copy-start = (bf16[128,8192]{1,0:T(8,128)(2,1)S(1)}, bf16[128,8192]{1,0:T(8,128)(2,1)}, u32[]{:S(2)}) copy-start(bf16[128,8192]{1,0:T(8,128)(2,1)} %refs_7_.1) | copy-start | bytes 6291460
  0.6 54.6 %collective-permute-start.1 = (bf16[128,8192]{1,0:T(8,128)(2,1)}, bf16[128,8192]{1,0:T(8,128)(2,1)}, u32[]{:S(2)}, u32[]{:S(2)}) collective-permute-start(bf16[128,8192]{1,0:T(8,128)(2,1)} %refs_7_.1), channel_id=1, source_target_pairs={{0,4},{4,0},{8,12},{12,8},{1,5},{5,1},{9,13},{13,9},{2,6},{6,2},{1... | collective-permute-start | bytes 6291464 | tf_op jit(solution)/shard_map/ppermute | solution.py:622
  35.3 1.6 collective-permute-start.5
  36.9 13.8 %copy-start.14 = (bf16[16,32,128]{2,1,0:T(8,128)(2,1)}, bf16[16,32,128]{2,1,0:T(8,128)(2,1)S(1)}, u32[]{:S(2)}) copy-start(bf16[16,32,128]{2,1,0:T(8,128)(2,1)S(1)} %collective-permute-done.5) | copy-start | bytes 393220
  36.9 13.8 %collective-permute-start.6 = (bf16[1,16,32,128]{3,2,1,0:T(8,128)(2,1)S(1)}, bf16[1,16,32,128]{3,2,1,0:T(8,128)(2,1)S(1)}, u32[]{:S(2)}, u32[]{:S(2)}) collective-permute-start(bf16[1,16,32,128]{3,2,1,0:T(8,128)(2,1)S(1)} %bitcast.106), channel_id=1, source_target_pairs={{0,1},{1,0},{2,3},{3,2},{4,5},{5,4},{6,7},{7,6},{8,9},{9,8},{10,11... | collective-permute-start | bytes 393224 | tf_op jit(solution)/shard_map/ppermute | solution.py:628
  44.4 31.9 %collective-permute-start = (bf16[64,4096]{1,0:T(8,128)(2,1)}, bf16[64,4096]{1,0:T(8,128)(2,1)S(1)}, u32[]{:S(2)}, u32[]{:S(2)}) collective-permute-start(bf16[64,4096]{1,0:T(8,128)(2,1)} %get-tuple-element.26), channel_id=1, source_target_pairs={{0,8},{4,12},{8,0},{12,4},{1,9},{5,13},{9,1},{13,5},{2,10},{6,14},... | collective-permute-start | bytes 1572872 | tf_op jit(solution)/shard_map/ppermute | solution.py:625
  50.7 4.5 %copy-start.15 = (bf16[1,16,32,128]{3,2,1,0:T(8,128)(2,1)}, bf16[1,16,32,128]{3,2,1,0:T(8,128)(2,1)S(1)}, u32[]{:S(2)}) copy-start(bf16[1,16,32,128]{3,2,1,0:T(8,128)(2,1)S(1)} %collective-permute-done.6) | copy-start | bytes 393220
  51.5 9.8 %copy-start.12 = (bf16[32,16,64]{2,1,0:T(8,128)(2,1)S(1)}, bf16[32,16,64]{2,1,0:T(8,128)(2,1)}, u32[]{:S(2)}) copy-start(bf16[32,16,64]{2,1,0:T(8,128)(2,1)} %param.11) | copy-start | bytes 196612
  51.5 22.9 %collective-permute-start.7 = (bf16[2,16,32,128]{3,2,1,0:T(8,128)(2,1)}, bf16[2,16,32,128]{3,2,1,0:T(8,128)(2,1)}, u32[]{:S(2)}, u32[]{:S(2)}) collective-permute-start(bf16[2,16,32,128]{3,2,1,0:T(8,128)(2,1)} %pad_maximum_fusion.3), channel_id=1, source_target_pairs={{0,2},{1,3},{2,0},{3,1},{4,6},{5,7},{6,4},{7,5},{8,10},{9,11},{10,... | collective-permute-start | bytes 786440 | tf_op jit(solution)/shard_map/ppermute | solution.py:628
  61.2 9.8 %collective-permute-start.8 = (bf16[1,32,16,64]{3,2,1,0:T(8,128)(2,1)S(1)}, bf16[1,32,16,64]{3,2,1,0:T(8,128)(2,1)S(1)}, u32[]{:S(2)}, u32[]{:S(2)}) collective-permute-start(bf16[1,32,16,64]{3,2,1,0:T(8,128)(2,1)S(1)} %bitcast.103), channel_id=1, source_target_pairs={{0,1},{1,0},{2,3},{3,2},{4,5},{5,4},{6,7},{7,6},{8,9},{9,8},{10,11... | collective-permute-start | bytes 196616 | tf_op jit(solution)/shard_map/ppermute | solution.py:628
  71.0 2.3 copy-start.16
  71.8 15.3 %collective-permute-start.9 = (bf16[2,32,16,64]{3,2,1,0:T(8,128)(2,1)}, bf16[2,32,16,64]{3,2,1,0:T(8,128)(2,1)}, u32[]{:S(2)}, u32[]{:S(2)}) collective-permute-start(bf16[2,32,16,64]{3,2,1,0:T(8,128)(2,1)} %pad_maximum_fusion.4), channel_id=1, source_target_pairs={{0,2},{1,3},{2,0},{3,1},{4,6},{5,7},{6,4},{7,5},{8,10},{9,11},{10,... | collective-permute-start | bytes 393224 | tf_op jit(solution)/shard_map/ppermute | solution.py:628
  76.3 10.8 %copy-start.13 = (bf16[32,16,64]{2,1,0:T(8,128)(2,1)S(1)}, bf16[32,16,64]{2,1,0:T(8,128)(2,1)}, u32[]{:S(2)}) copy-start(bf16[32,16,64]{2,1,0:T(8,128)(2,1)} %param.11) | copy-start | bytes 196612
  76.3 10.8 %copy-start.17 = (bf16[1,32,16,64]{3,2,1,0:T(8,128)(2,1)S(1)}, bf16[1,32,16,64]{3,2,1,0:T(8,128)(2,1)}, u32[]{:S(2)}) copy-start(bf16[1,32,16,64]{3,2,1,0:T(8,128)(2,1)} %copy-done.16) | copy-start | bytes 196612
  76.3 32.5 %collective-permute-start.2 = (bf16[64,4096]{1,0:T(8,128)(2,1)S(1)}, bf16[64,4096]{1,0:T(8,128)(2,1)S(1)}, u32[]{:S(2)}, u32[]{:S(2)}) collective-permute-start(bf16[64,4096]{1,0:T(8,128)(2,1)S(1)} %collective-permute-done.refs_0_.refs_4_.refs_10_), channel_id=1, source_target_pairs={{0,1},{1,0},{2,3},{3,2},{4,5},{5,4},{6,7},{7,6},{8,9},{9,8},{10,11... | collective-permute-start | bytes 1572872 | tf_op jit(solution)/shard_map/ppermute | solution.py:628
  78.9 30.0 %collective-permute-start.10 = (bf16[64,4096]{1,0:T(8,128)(2,1)S(1)}, bf16[64,4096]{1,0:T(8,128)(2,1)}, u32[]{:S(2)}, u32[]{:S(2)}) collective-permute-start(bf16[64,4096]{1,0:T(8,128)(2,1)S(1)} %collective-permute-done.refs_0_.refs_4_.refs_10_), channel_id=1, source_target_pairs={{0,4},{4,0},{8,12},{12,8},{1,5},{5,1},{9,13},{13,9},{2,6},{6,2},{1... | collective-permute-start | bytes 1572872 | tf_op jit(solution)/shard_map/ppermute | solution.py:622
  85.8 2.7 copy-start.6
  85.8 11.4 %collective-permute-start.3 = (bf16[2,128,1024]{2,1,0:T(8,128)(2,1)}, bf16[2,128,1024]{2,1,0:T(8,128)(2,1)}, u32[]{:S(2)}, u32[]{:S(2)}) collective-permute-start(bf16[2,128,1024]{2,1,0:T(8,128)(2,1)} %bitcast.11), channel_id=1, source_target_pairs={{0,4},{4,0},{8,12},{12,8},{1,5},{5,1},{9,13},{13,9},{2,6},{6,2},{1... | collective-permute-start | bytes 1572872 | tf_op jit(solution)/shard_map/ppermute | solution.py:622
  86.3 8.7 %collective-permute-start.4 = (bf16[2,128,768]{2,1,0:T(8,128)(2,1)}, bf16[2,128,768]{2,1,0:T(8,128)(2,1)}, u32[]{:S(2)}, u32[]{:S(2)}) collective-permute-start(bf16[2,128,768]{2,1,0:T(8,128)(2,1)} %bitcast.13), channel_id=1, source_target_pairs={{0,4},{4,0},{8,12},{12,8},{1,5},{5,1},{9,13},{13,9},{2,6},{6,2},{1... | collective-permute-start | bytes 1179656 | tf_op jit(solution)/shard_map/ppermute | solution.py:622
  93.6 3.6 %copy-start.7 = (bf16[1,2,128,1024]{3,2,1,0:T(8,128)(2,1)S(1)}, bf16[1,2,128,1024]{3,2,1,0:T(8,128)(2,1)}, u32[]{:S(2)}) copy-start(bf16[1,2,128,1024]{3,2,1,0:T(8,128)(2,1)} %copy-done.6) | copy-start | bytes 1572868
  93.6 5.6 %copy-start.2 = (bf16[4,16,32,128]{3,2,1,0:T(8,128)(2,1)S(1)}, bf16[4,16,32,128]{3,2,1,0:T(8,128)(2,1)}, u32[]{:S(2)}) copy-start(bf16[4,16,32,128]{3,2,1,0:T(8,128)(2,1)} %pad_maximum_fusion.refs_4_.refs_8_) | copy-start | bytes 1572868
  95.0 13.8 %copy-start.1 = (bf16[8,256,256]{2,1,0:T(8,128)(2,1)}, bf16[8,256,256]{2,1,0:T(8,128)(2,1)S(1)}, u32[]{:S(2)}) copy-start(bf16[8,256,256]{2,1,0:T(8,128)(2,1)S(1)} %broadcast_select_fusion.refs_5_.refs_9_) | copy-start | bytes 3145732
  108.8 7.9 %copy-start.5 = (bf16[2048,256]{1,0:T(8,128)(2,1)}, bf16[2048,256]{1,0:T(8,128)(2,1)S(1)}, u32[]{:S(2)}) copy-start(bf16[2048,256]{1,0:T(8,128)(2,1)S(1)} %get-tuple-element.35.refs_3_) | copy-start | bytes 3145732
  108.8 2.0 collective-permute-start.11
  116.6 6.9 %collective-permute-start.13 = (bf16[2,128,768]{2,1,0:T(8,128)(2,1)}, bf16[2,128,768]{2,1,0:T(8,128)(2,1)}, u32[]{:S(2)}, u32[]{:S(2)}) collective-permute-start(bf16[2,128,768]{2,1,0:T(8,128)(2,1)} %bitcast.23), channel_id=1, source_target_pairs={{0,4},{4,0},{8,12},{12,8},{1,5},{5,1},{9,13},{13,9},{2,6},{6,2},{1... | collective-permute-start | bytes 1179656 | tf_op jit(solution)/shard_map/ppermute | solution.py:622
  123.0 2.0 collective-permute-start.12
  125.2 13.8 %copy-start.19 = (bf16[64,4096]{1,0:T(8,128)(2,1)S(1)}, bf16[64,4096]{1,0:T(8,128)(2,1)}, u32[]{:S(2)}) copy-start(bf16[64,4096]{1,0:T(8,128)(2,1)} %get-tuple-element.46) | copy-start | bytes 1572868
  125.2 13.7 %copy-start.11 = (bf16[2,128,1024]{2,1,0:T(8,128)(2,1)S(1)}, bf16[2,128,1024]{2,1,0:T(8,128)(2,1)}, u32[]{:S(2)}) copy-start(bf16[2,128,1024]{2,1,0:T(8,128)(2,1)} %fusion.1) | copy-start | bytes 1572868
  125.2 15.8 %copy-start.18 = (bf16[2,128,768]{2,1,0:T(8,128)(2,1)S(1)}, bf16[2,128,768]{2,1,0:T(8,128)(2,1)}, u32[]{:S(2)}) copy-start(bf16[2,128,768]{2,1,0:T(8,128)(2,1)} %fusion.3) | copy-start | bytes 1179652
  138.6 37.6 %collective-permute-start.14 = (bf16[2,2,128,1792]{3,2,1,0:T(8,128)(2,1)}, bf16[2,2,128,1792]{3,2,1,0:T(8,128)(2,1)S(1)}, u32[]{:S(2)}, u32[]{:S(2)}) collective-permute-start(bf16[2,2,128,1792]{3,2,1,0:T(8,128)(2,1)} %get-tuple-element.43), channel_id=1, source_target_pairs={{0,4},{4,0},{8,12},{12,8},{1,5},{5,1},{9,13},{13,9},{2,6},{6,2},{1... | collective-permute-start | bytes 5505032 | tf_op jit(solution)/shard_map/ppermute | solution.py:622
  139.0 14.8 %collective-permute-start.28 = (bf16[64,4096]{1,0:T(8,128)(2,1)S(1)}, bf16[64,4096]{1,0:T(8,128)(2,1)S(1)}, u32[]{:S(2)}, u32[]{:S(2)}) collective-permute-start(bf16[64,4096]{1,0:T(8,128)(2,1)S(1)} %copy-done.19), channel_id=1, source_target_pairs={{0,8},{4,12},{8,0},{12,4},{1,9},{5,13},{9,1},{13,5},{2,10},{6,14},... | collective-permute-start | bytes 1572872 | tf_op jit(solution)/shard_map/ppermute | solution.py:625
  139.0 26.0 %collective-permute-start.15 = (bf16[2,128,1024]{2,1,0:T(8,128)(2,1)S(1)}, bf16[2,128,1024]{2,1,0:T(8,128)(2,1)S(1)}, u32[]{:S(2)}, u32[]{:S(2)}) collective-permute-start(bf16[2,128,1024]{2,1,0:T(8,128)(2,1)S(1)} %copy-done.11), channel_id=1, source_target_pairs={{0,8},{4,12},{8,0},{12,4},{1,9},{5,13},{9,1},{13,5},{2,10},{6,14},... | collective-permute-start | bytes 1572872 | tf_op jit(solution)/shard_map/ppermute | solution.py:625
  141.0 35.2 %collective-permute-start.22 = (bf16[2,128,1024]{2,1,0:T(8,128)(2,1)S(1)}, bf16[2,128,1024]{2,1,0:T(8,128)(2,1)S(1)}, u32[]{:S(2)}, u32[]{:S(2)}) collective-permute-start(bf16[2,128,1024]{2,1,0:T(8,128)(2,1)S(1)} %fusion), channel_id=1, source_target_pairs={{0,8},{4,12},{8,0},{12,4},{1,9},{5,13},{9,1},{13,5},{2,10},{6,14},... | collective-permute-start | bytes 1572872 | tf_op jit(solution)/shard_map/ppermute | solution.py:625
  141.1 43.6 %collective-permute-start.16 = (bf16[2,128,768]{2,1,0:T(8,128)(2,1)S(1)}, bf16[2,128,768]{2,1,0:T(8,128)(2,1)S(1)}, u32[]{:S(2)}, u32[]{:S(2)}) collective-permute-start(bf16[2,128,768]{2,1,0:T(8,128)(2,1)S(1)} %copy-done.18), channel_id=1, source_target_pairs={{0,8},{4,12},{8,0},{12,4},{1,9},{5,13},{9,1},{13,5},{2,10},{6,14},... | collective-permute-start | bytes 1179656 | tf_op jit(solution)/shard_map/ppermute | solution.py:625
  153.7 38.5 %collective-permute-start.19 = (bf16[2,128,768]{2,1,0:T(8,128)(2,1)S(1)}, bf16[2,128,768]{2,1,0:T(8,128)(2,1)S(1)}, u32[]{:S(2)}, u32[]{:S(2)}) collective-permute-start(bf16[2,128,768]{2,1,0:T(8,128)(2,1)S(1)} %fusion.2), channel_id=1, source_target_pairs={{0,8},{4,12},{8,0},{12,4},{1,9},{5,13},{9,1},{13,5},{2,10},{6,14},... | collective-permute-start | bytes 1179656 | tf_op jit(solution)/shard_map/ppermute | solution.py:625
  165.0 28.1 %collective-permute-start.29 = (bf16[64,4096]{1,0:T(8,128)(2,1)S(1)}, bf16[64,4096]{1,0:T(8,128)(2,1)S(1)}, u32[]{:S(2)}, u32[]{:S(2)}) collective-permute-start(bf16[64,4096]{1,0:T(8,128)(2,1)S(1)} %collective-permute-done.28.refs_4_.refs_14_), channel_id=1, source_target_pairs={{0,1},{1,0},{2,3},{3,2},{4,5},{5,4},{6,7},{7,6},{8,9},{9,8},{10,11... | collective-permute-start | bytes 1572872 | tf_op jit(solution)/shard_map/ppermute | solution.py:628
  176.2 17.6 %collective-permute-start.30 = (bf16[64,4096]{1,0:T(8,128)(2,1)S(1)}, bf16[64,4096]{1,0:T(8,128)(2,1)S(1)}, u32[]{:S(2)}, u32[]{:S(2)}) collective-permute-start(bf16[64,4096]{1,0:T(8,128)(2,1)S(1)} %collective-permute-done.28.refs_4_.refs_14_), channel_id=1, source_target_pairs={{0,4},{4,0},{8,12},{12,8},{1,5},{5,1},{9,13},{13,9},{2,6},{6,2},{1... | collective-permute-start | bytes 1572872 | tf_op jit(solution)/shard_map/ppermute | solution.py:622
  192.7 13.6 %collective-permute-start.17 = (bf16[128,1792]{1,0:T(8,128)(2,1)S(1)}, bf16[128,1792]{1,0:T(8,128)(2,1)}, u32[]{:S(2)}, u32[]{:S(2)}) collective-permute-start(bf16[128,1792]{1,0:T(8,128)(2,1)S(1)} %pad_maximum_fusion.2.refs_2_), channel_id=1, source_target_pairs={{0,8},{4,12},{8,0},{12,4},{1,9},{5,13},{9,1},{13,5},{2,10},{6,14},... | collective-permute-start | bytes 1376264 | tf_op jit(solution)/shard_map/ppermute | solution.py:625
  193.0 14.1 %collective-permute-start.31 = (bf16[64,4096]{1,0:T(8,128)(2,1)S(1)}, bf16[64,4096]{1,0:T(8,128)(2,1)S(1)}, u32[]{:S(2)}, u32[]{:S(2)}) collective-permute-start(bf16[64,4096]{1,0:T(8,128)(2,1)S(1)} %collective-permute-done.29.refs_5_.refs_15_), channel_id=1, source_target_pairs={{0,4},{4,0},{8,12},{12,8},{1,5},{5,1},{9,13},{13,9},{2,6},{6,2},{1... | collective-permute-start | bytes 1572872 | tf_op jit(solution)/shard_map/ppermute | solution.py:622
  193.0 34.2 %collective-permute-start.26 = (bf16[128,1792]{1,0:T(8,128)(2,1)S(1)}, bf16[128,1792]{1,0:T(8,128)(2,1)}, u32[]{:S(2)}, u32[]{:S(2)}) collective-permute-start(bf16[128,1792]{1,0:T(8,128)(2,1)S(1)} %pad_maximum_fusion.2.refs_2_), channel_id=1, source_target_pairs={{0,4},{4,0},{8,12},{12,8},{1,5},{5,1},{9,13},{13,9},{2,6},{6,2},{1... | collective-permute-start | bytes 1376264 | tf_op jit(solution)/shard_map/ppermute | solution.py:622
  193.7 21.1 %collective-permute-start.27 = (bf16[128,1024]{1,0:T(8,128)(2,1)S(1)}, bf16[128,1024]{1,0:T(8,128)(2,1)S(1)}, u32[]{:S(2)}, u32[]{:S(2)}) collective-permute-start(bf16[128,1024]{1,0:T(8,128)(2,1)S(1)} %fusion.5.refs_0_), channel_id=1, source_target_pairs={{0,4},{4,0},{8,12},{12,8},{1,5},{5,1},{9,13},{13,9},{2,6},{6,2},{1... | collective-permute-start | bytes 786440 | tf_op jit(solution)/shard_map/ppermute | solution.py:622
  193.8 13.3 %copy-start.3 = (bf16[64,4096]{1,0:T(8,128)(2,1)}, bf16[64,4096]{1,0:T(8,128)(2,1)S(1)}, u32[]{:S(2)}) copy-start(bf16[64,4096]{1,0:T(8,128)(2,1)S(1)} %collective-permute-done.30.refs_6_.refs_16_) | copy-start | bytes 1572868
  193.8 16.4 %collective-permute-start.23 = (bf16[128,1024]{1,0:T(8,128)(2,1)S(1)}, bf16[128,1024]{1,0:T(8,128)(2,1)}, u32[]{:S(2)}, u32[]{:S(2)}) collective-permute-start(bf16[128,1024]{1,0:T(8,128)(2,1)S(1)} %fusion.5.refs_0_), channel_id=1, source_target_pairs={{0,8},{4,12},{8,0},{12,4},{1,9},{5,13},{9,1},{13,5},{2,10},{6,14},... | collective-permute-start | bytes 786440 | tf_op jit(solution)/shard_map/ppermute | solution.py:625
  206.3 37.1 %collective-permute-start.18 = (bf16[128,1792]{1,0:T(8,128)(2,1)}, bf16[128,1792]{1,0:T(8,128)(2,1)}, u32[]{:S(2)}, u32[]{:S(2)}) collective-permute-start(bf16[128,1792]{1,0:T(8,128)(2,1)} %collective-permute-done.17.refs_0_), channel_id=1, source_target_pairs={{0,4},{4,0},{8,12},{12,8},{1,5},{5,1},{9,13},{13,9},{2,6},{6,2},{1... | collective-permute-start | bytes 1376264 | tf_op jit(solution)/shard_map/ppermute | solution.py:622
  207.1 7.7 %copy-start.10 = (bf16[64,4096]{1,0:T(8,128)(2,1)}, bf16[64,4096]{1,0:T(8,128)(2,1)S(1)}, u32[]{:S(2)}) copy-start(bf16[64,4096]{1,0:T(8,128)(2,1)S(1)} %collective-permute-done.31.refs_7_.refs_17_) | copy-start | bytes 1572868
  207.1 7.7 %collective-permute-start.20 = (bf16[128,768]{1,0:T(8,128)(2,1)}, bf16[128,768]{1,0:T(8,128)(2,1)}, u32[]{:S(2)}, u32[]{:S(2)}) collective-permute-start(bf16[128,768]{1,0:T(8,128)(2,1)} %fusion.9.refs_0_), channel_id=1, source_target_pairs={{0,8},{4,12},{8,0},{12,4},{1,9},{5,13},{9,1},{13,5},{2,10},{6,14},... | collective-permute-start | bytes 589832 | tf_op jit(solution)/shard_map/ppermute | solution.py:625
  210.2 33.2 %collective-permute-start.24 = (bf16[128,1024]{1,0:T(8,128)(2,1)}, bf16[128,1024]{1,0:T(8,128)(2,1)}, u32[]{:S(2)}, u32[]{:S(2)}) collective-permute-start(bf16[128,1024]{1,0:T(8,128)(2,1)} %collective-permute-done.23.refs_2_), channel_id=1, source_target_pairs={{0,4},{4,0},{8,12},{12,8},{1,5},{5,1},{9,13},{13,9},{2,6},{6,2},{1... | collective-permute-start | bytes 786440 | tf_op jit(solution)/shard_map/ppermute | solution.py:622
  214.8 20.4 %collective-permute-start.25 = (bf16[128,768]{1,0:T(8,128)(2,1)}, bf16[128,768]{1,0:T(8,128)(2,1)}, u32[]{:S(2)}, u32[]{:S(2)}) collective-permute-start(bf16[128,768]{1,0:T(8,128)(2,1)} %fusion.9.refs_0_), channel_id=1, source_target_pairs={{0,4},{4,0},{8,12},{12,8},{1,5},{5,1},{9,13},{13,9},{2,6},{6,2},{1... | collective-permute-start | bytes 589832 | tf_op jit(solution)/shard_map/ppermute | solution.py:622
  214.8 0.7 copy-start.8
  215.5 37.4 %collective-permute-start.21 = (bf16[128,768]{1,0:T(8,128)(2,1)}, bf16[128,768]{1,0:T(8,128)(2,1)}, u32[]{:S(2)}, u32[]{:S(2)}) collective-permute-start(bf16[128,768]{1,0:T(8,128)(2,1)} %collective-permute-done.20.refs_2_), channel_id=1, source_target_pairs={{0,4},{4,0},{8,12},{12,8},{1,5},{5,1},{9,13},{13,9},{2,6},{6,2},{1... | collective-permute-start | bytes 589832 | tf_op jit(solution)/shard_map/ppermute | solution.py:622
  216.0 1.0 copy-start.4
  217.1 10.2 %copy-start.9 = (bf16[128,1024]{1,0:T(8,128)(2,1)S(1)}, bf16[128,1024]{1,0:T(8,128)(2,1)}, u32[]{:S(2)}) copy-start(bf16[128,1024]{1,0:T(8,128)(2,1)} %copy-done.8) | copy-start | bytes 786436
  279.4 11.1 %collective-permute-start.32 = (bf16[2,768,128]{2,1,0:T(8,128)(2,1)S(1)}, bf16[2,768,128]{2,1,0:T(8,128)(2,1)S(1)}, u32[]{:S(2)}, u32[]{:S(2)}) collective-permute-start(bf16[2,768,128]{2,1,0:T(8,128)(2,1)S(1)} %slice.101), channel_id=1, source_target_pairs={{0,1},{1,0},{2,3},{3,2},{4,5},{5,4},{6,7},{7,6},{8,9},{9,8},{10,11... | collective-permute-start | bytes 1179656 | tf_op jit(solution)/shard_map/ppermute | solution.py:628
  291.6 6.4 %collective-permute-start.35 = (bf16[256,128]{1,0:T(8,128)(2,1)S(1)}, bf16[256,128]{1,0:T(8,128)(2,1)S(1)}, u32[]{:S(2)}, u32[]{:S(2)}) collective-permute-start(bf16[256,128]{1,0:T(8,128)(2,1)S(1)} %slice_bitcast_fusion.10), channel_id=1, source_target_pairs={{0,2},{1,3},{2,0},{3,1},{4,6},{5,7},{6,4},{7,5},{8,10},{9,11},{10,... | collective-permute-start | bytes 196616 | tf_op jit(solution)/shard_map/ppermute | solution.py:628
  292.7 6.2 %collective-permute-start.33 = (bf16[512,128]{1,0:T(8,128)(2,1)S(1)}, bf16[512,128]{1,0:T(8,128)(2,1)S(1)}, u32[]{:S(2)}, u32[]{:S(2)}) collective-permute-start(bf16[512,128]{1,0:T(8,128)(2,1)S(1)} %get-tuple-element.54), channel_id=1, source_target_pairs={{0,0},{1,4},{2,8},{3,12},{4,1},{5,5},{6,9},{7,13},{8,2},{9,6},{10,... | collective-permute-start | bytes 393224 | tf_op jit(solution)/shard_map/ppermute | solution.py:635
  293.4 15.7 %collective-permute-start.34 = (bf16[512,128]{1,0:T(8,128)(2,1)S(1)}, bf16[512,128]{1,0:T(8,128)(2,1)S(1)}, u32[]{:S(2)}, u32[]{:S(2)}) collective-permute-start(bf16[512,128]{1,0:T(8,128)(2,1)S(1)} %get-tuple-element.55), channel_id=1, source_target_pairs={{0,8},{1,12},{2,0},{3,4},{4,9},{5,13},{6,1},{7,5},{8,10},{9,14},{1... | collective-permute-start | bytes 393224 | tf_op jit(solution)/shard_map/ppermute | solution.py:635

commit v4 on v3

--- a/solution.py
+++ b/solution.py
@@ -301,32 +301,31 @@
     return grad_right, grad_left
 
 
-def pack_kernel(idx_ref, tokens_ref, first_ref, rest_ref, sems):
-    half, width = first_ref.shape
-    row = pl.multiple_of(idx_ref[0] * half, half)
-    copies = []
-    for n, out_ref in enumerate((first_ref, rest_ref)):
-        column = pl.multiple_of(idx_ref[n + 1] * width, width)
-        source = tokens_ref.at[pl.ds(row, half), pl.ds(column, width)]
-        copies.append(pltpu.make_async_copy(source, out_ref, sems.at[n]))
-    for copy in copies:
-        copy.start()
-    for copy in copies:
-        copy.wait()
-
-
-def pack_tokens(tokens, half, chip):
+def cut_kernel(idx_ref, first_in, rest_in, first_ref, rest_ref):
+    first_ref[...] = first_in[...]
+    rest_ref[...] = rest_in[...]
+
+
+def cut_tokens(tokens, half, chip):
     rows, model = tokens.shape
-    shape = jax.ShapeDtypeStruct((rows // 2, model // 2), BF16)
+    block = (rows // 2, model // 2)
+    shape = jax.ShapeDtypeStruct(block, BF16)
+    whole = pl.BlockSpec(block, lambda n, s: (0, 0))
     return pl.pallas_call(
-        pack_kernel,
-        in_specs=[pl.BlockSpec(memory_space=pltpu.SMEM), pl.BlockSpec(memory_space=pl.ANY)],
-        out_specs=[pl.BlockSpec(memory_space=pl.ANY)] * 2,
+        cut_kernel,
+        grid_spec=pltpu.PrefetchScalarGridSpec(
+            num_scalar_prefetch=1,
+            grid=(1,),
+            in_specs=[
+                pl.BlockSpec(block, lambda n, s: (s[0], s[1])),
+                pl.BlockSpec(block, lambda n, s: (s[0], s[2])),
+            ],
+            out_specs=[whole, whole],
+        ),
         out_shape=[shape, shape],
-        scratch_shapes=[pltpu.SemaphoreType.DMA((2,))],
         cost_estimate=SMALL,
-        name="pack_tokens",
-    )(jnp.stack([half, 1 - chip, chip]).astype(jnp.int32), tokens)
+        name="cut_tokens",
+    )(jnp.stack([half, 1 - chip, chip]).astype(jnp.int32), tokens, tokens)
 
 
 def products_kernel(sets, idx_ref, *refs):
@@ -371,44 +370,55 @@
     )(scalars, *[piece for piece, _, _ in pieces], gate, up)
 
 
-def target_kernel(idx_ref, *refs):
-    pieces, weight_ref, out_ref = refs[:4], refs[4], refs[-1]
-    lhs = jnp.concatenate([piece[...] for piece in pieces], axis=0)
-    product = jnp.dot(lhs, weight_ref[...], preferred_element_type=F32)
-
-    @pl.when(pl.program_id(0) == 0)
-    def _():
-        out_ref[...] = refs[5][...] + product if len(refs) > 6 else product
-
-    @pl.when(pl.program_id(0) > 0)
-    def _():
-        out_ref[...] += product
-
-
-def target_add(total, pieces, weight, row, width):
-    rows, outs = pieces[0][0].shape[0], weight.shape[1]
-    scalars = jnp.reshape(lax.div(row, BLK), (1,)).astype(jnp.int32)
-
-    def piece_spec(first):
-        return pl.BlockSpec((rows, BLK), lambda k, s: (0, first // BLK + k))
-
-    whole = pl.BlockSpec((4 * rows, outs), lambda k, s: (0, 0))
-    totals = [] if total is None else [total]
+def fill_rows(lhs, sets):
+    row = 0
+    for group in sets:
+        column = 0
+        for piece in group:
+            rows, width = piece.shape
+            lhs[row : row + rows, column : column + width] = piece[...]
+            column += width
+        row += group[0].shape[0]
+
+
+def split_sets(refs, counts):
+    sets, start = [], 0
+    for count in counts:
+        sets.append(refs[start : start + count])
+        start += count
+    return sets, refs[start:]
+
+
+def whole_spec(array):
+    return pl.BlockSpec(array.shape, lambda n, s: (0,) * array.ndim)
+
+
+def target_kernel(counts, idx_ref, *refs):
+    sets, (weight_ref, out_ref, lhs) = split_sets(refs, counts)
+    pl.when(pl.program_id(0) == 0)(lambda: fill_rows(lhs, sets))
+    out_ref[...] = jnp.dot(lhs[...], weight_ref[...], preferred_element_type=F32)
+
+
+def target_part(sets, weight, chip):
+    pieces = [piece for group in sets for piece in group]
+    width = sum(piece.shape[1] for piece in sets[0])
+    rows = sum(group[0].shape[0] for group in sets)
+    outs = weight.shape[1]
     return pl.pallas_call(
-        target_kernel,
+        functools.partial(target_kernel, [len(group) for group in sets]),
         grid_spec=pltpu.PrefetchScalarGridSpec(
             num_scalar_prefetch=1,
-            grid=(width // BLK,),
-            in_specs=[piece_spec(first) for _, first in pieces]
-            + [pl.BlockSpec((BLK, outs), lambda k, s: (s[0] + k, 0))]
-            + [whole] * len(totals),
-            out_specs=whole,
-        ),
-        out_shape=jax.ShapeDtypeStruct((4 * rows, outs), F32),
+            grid=(outs // BLK,),
+            in_specs=[whole_spec(piece) for piece in pieces]
+            + [pl.BlockSpec((width, BLK), lambda n, s: (s[0], n))],
+            out_specs=pl.BlockSpec((rows, BLK), lambda n, s: (0, n)),
+            scratch_shapes=[pltpu.VMEM((rows, width), BF16)],
+        ),
+        out_shape=jax.ShapeDtypeStruct((rows, outs), F32),
         compiler_params=pltpu.CompilerParams(vmem_limit_bytes=50 * 2**20),
         cost_estimate=SMALL,
-        name="target_add",
-    )(scalars, *[piece for piece, _ in pieces], weight, *totals)
+        name="target_part",
+    )(jnp.reshape(chip, (1,)).astype(jnp.int32), *pieces, weight)
 
 
 TN = (((0,), (0,)), ((), ()))
@@ -420,23 +430,56 @@
     return lax.rem(chip + step // per_chip, 2) * per_chip + lax.rem(step, per_chip)
 
 
+def spread_kernel(left_ref, out_ref, scratch):
+    groups, fold = out_ref.shape[0], BLK // left_ref.shape[1]
+    blocks = left_ref.shape[1]
+    scratch[...] = jnp.zeros_like(scratch)
+    zeros = jnp.zeros((blocks, blocks), F32)
+    for g in range(groups):
+        for a in range(fold):
+            value = left_ref[g * fold + a].astype(F32)
+            pair = [value, zeros] if a % 2 == 0 else [zeros, value]
+            wide = jnp.concatenate(pair, axis=1)
+            lanes = slice(a // 2 * LANES, (a // 2 + 1) * LANES)
+            for c in range(blocks // WIDE):
+                row = (c * fold + a) * WIDE
+                scratch[row : row + WIDE, lanes] = wide[c * WIDE : (c + 1) * WIDE]
+        out_ref[g] = scratch[...].astype(BF16)
+
+
+def spread_left(left):
+    pairs, blocks, _ = left.shape
+    return pl.pallas_call(
+        spread_kernel,
+        out_shape=jax.ShapeDtypeStruct((pairs * blocks // BLK, BLK, BLK), BF16),
+        scratch_shapes=[pltpu.VMEM((BLK, BLK), F32)],
+        cost_estimate=SMALL,
+        name="spread_left",
+    )(left)
+
+
 def student_kernel(steps, late, tensor_count, idx_ref, *refs):
-    count = 12 if late else 4
-    tokens, (right_ref, left_ref, mixed_ref, student_ref, scratch) = refs[:-5], refs[-5:]
+    tokens, (right_ref, left_ref, mixed_ref, student_ref, spread) = refs[:-5], refs[-5:]
     step = pl.program_id(0)
     chunk = natural(step, idx_ref[2], steps // 2)
+    groups = left_ref.shape[0]
     pairs = right_ref.shape[2]
-    size = right_ref.shape[3]
+    share = BLK // groups
+
+    @pl.when(step == 0)
+    def _():
+        spread[...] = jnp.zeros_like(spread)
+
+    for t in range(WIDE):
+        spread[t, pl.ds(t, pairs, stride=WIDE), :] = right_ref[0, t].astype(F32)
+    factor = jnp.concatenate([spread[t] for t in range(WIDE)], axis=1).astype(BF16)
 
     def mix(pieces):
-        for t in range(WIDE):
-            rows = [piece[:, t * size : (t + 1) * size] for piece in pieces]
-            part = lax.dot_general(
-                right_ref[0, t], jnp.concatenate(rows, axis=0), NT, preferred_element_type=F32
-            )
-            start = pl.multiple_of((chunk * WIDE + t) * pairs, pairs)
-            for h in range(scratch.shape[0]):
-                scratch[h, pl.ds(start, pairs), :] = part[:, h * LANES : (h + 1) * LANES]
+        rows = jnp.concatenate([piece[...] for piece in pieces], axis=0)
+        part = lax.dot_general(factor, rows, NT, preferred_element_type=F32).astype(BF16)
+        start = pl.multiple_of(chunk * share, share)
+        for g in range(groups):
+            mixed_ref[g, pl.ds(start, share), :] = part[g * share : (g + 1) * share]
 
     if late:
         pl.when(step < steps // 2)(lambda: mix(tokens[:4]))
@@ -446,17 +489,9 @@
 
     @pl.when(step == steps - 1)
     def _():
-        blocks = steps * WIDE
-        for j in range(pairs):
-            for h in range(scratch.shape[0]):
-                rows = scratch[h, pl.ds(j, blocks, stride=pairs), :]
-                mixed_ref[j * blocks : (j + 1) * blocks, h * LANES : (h + 1) * LANES] = (
-                    rows.astype(BF16)
-                )
-        for g in range(left_ref.shape[0]):
-            span = slice(g * BLK, (g + 1) * BLK)
-            student_ref[:, span] = lax.dot_general(
-                mixed_ref[span, :], left_ref[g], TN, preferred_element_type=F32
+        for g in range(groups):
+            student_ref[:, g * BLK : (g + 1) * BLK] = lax.dot_general(
+                mixed_ref[g], left_ref[g], TN, preferred_element_type=F32
             ) * (1.0 / tensor_count)
 
 
@@ -491,7 +526,7 @@
         chunk = natural(n, s[2], steps // 2)
         return (s[3] ^ (chunk // halves), lax.rem(chunk, halves), 0, 0)
 
-    outs = left_diag.shape[0] * BLK
+    groups = left_diag.shape[0]
     return pl.pallas_call(
         functools.partial(student_kernel, steps, late, tensor_count),
         grid_spec=pltpu.PrefetchScalarGridSpec(
@@ -500,113 +535,136 @@
             in_specs=token_specs(half, WIDE * size, steps, 0, not late)
             + [
                 pl.BlockSpec((1, WIDE, pairs, size), right_block),
-                pl.BlockSpec(left_diag.shape, lambda n, s: (0, 0, 0)),
+                whole_spec(left_diag),
             ],
             out_specs=[
-                pl.BlockSpec((pairs * blocks, 4 * half), lambda n, s: (0, 0)),
-                pl.BlockSpec((4 * half, outs), lambda n, s: (0, 0)),
+                pl.BlockSpec((groups, BLK, 4 * half), lambda n, s: (0, 0, 0)),
+                pl.BlockSpec((4 * half, groups * BLK), lambda n, s: (0, 0)),
             ],
-            scratch_shapes=[pltpu.VMEM((4 * half // LANES, pairs * blocks, LANES), F32)],
+            scratch_shapes=[pltpu.VMEM((WIDE, pairs * WIDE, size), F32)],
         ),
         out_shape=[
-            jax.ShapeDtypeStruct((pairs * blocks, 4 * half), BF16),
-            jax.ShapeDtypeStruct((4 * half, outs), F32),
+            jax.ShapeDtypeStruct((groups, BLK, 4 * half), BF16),
+            jax.ShapeDtypeStruct((4 * half, groups * BLK), F32),
         ],
         compiler_params=pltpu.CompilerParams(vmem_limit_bytes=50 * 2**20),
-        cost_estimate=SMALL,
+        cost_estimate=pl.CostEstimate(
+            flops=10**10, bytes_accessed=10**7, transcendentals=0
+        ),
         name="student_part",
     )(scalars, *tokens, right_rows, left_diag)
 
 
-def grads_kernel(groups, steps, scale, idx_ref, *refs):
-    total_ref, student0, student1, mixed0, mixed1, left_ref = refs[:6]
-    own, near, far = refs[6:10], refs[10:14], refs[14:18]
-    out_ref, scratch = refs[18:]
+def grads_kernel(groups, steps, scale, counts, idx_ref, *refs):
+    sets, refs = split_sets(refs, counts)
+    weight_ref, total_ref, student0, student1, mixed0, mixed1, left_ref = refs[:7]
+    own, near, far = refs[7:11], refs[11:15], refs[15:19]
+    out_ref, lhs, back, wide = refs[19:]
     step = pl.program_id(0)
     z = idx_ref[3]
     parts, size = out_ref.shape[0], out_ref.shape[2]
-    pairs = scratch.shape[1] // (steps * WIDE)
     blocks = steps * WIDE
     per_part = blocks // parts
+    share = BLK // steps
+    pairs = groups * share // WIDE
+    fold = BLK // blocks
 
     def place(owner):
-        far_bits = z ^ owner
-        return lax.rem(far_bits, 2) * 2 + far_bits // 2
+        bits = z ^ owner
+        return lax.rem(bits, 2) * 2 + bits // 2
+
+    pl.when(step == 0)(lambda: fill_rows(lhs, sets))
 
     @pl.when(step < groups)
     def _():
+        target = total_ref[...] + jnp.dot(
+            lhs[...], weight_ref[...], preferred_element_type=F32
+        )
         student = jnp.concatenate([student0[...], student1[...]], axis=0)
-        out_grad = ((student - total_ref[...]) * scale).astype(BF16)
-        mixed = jnp.concatenate([mixed0[...], mixed1[...]], axis=1)
-        left = jnp.dot(mixed, out_grad, preferred_element_type=F32).T
-        row = pl.multiple_of(step * BLK, BLK)
-        back = lax.dot_general(left_ref[0], out_grad, NT, preferred_element_type=F32)
-        for h in range(scratch.shape[0]):
-            scratch[h, pl.ds(row, BLK), :] = back[:, h * LANES : (h + 1) * LANES]
+        out_grad = ((student - target) * scale).astype(BF16)
+        mixed = jnp.concatenate([mixed0[0], mixed1[0]], axis=1)
+        left = jnp.dot(mixed, out_grad, preferred_element_type=F32)
+        value = lax.dot_general(
+            left_ref[0], out_grad, NT, preferred_element_type=F32
+        ).astype(BF16)
+        row = pl.multiple_of(step * share, share)
+        for c in range(steps):
+            back[c, pl.ds(row, share), :] = value[c * share : (c + 1) * share]
         low = lax.broadcasted_iota(jnp.int32, (blocks, size), 1) < blocks
-        share = blocks // parts
-        for pair in range(BLK // size):
+        rows = blocks // parts
+        for pair in range(fold // 2):
             lanes = slice(pair * size, (pair + 1) * size)
-            top = left[pair * size : pair * size + blocks, lanes]
-            bottom = left[pair * size + blocks : (pair + 1) * size, lanes]
-            both = jnp.where(low, top, bottom).astype(BF16)
-            begin = per_part * pairs + (step * (BLK // size) + pair) * share
-            begin = pl.multiple_of(begin, share)
+            picked = []
+            for a in (2 * pair, 2 * pair + 1):
+                for c in range(steps):
+                    begin = (c * fold + a) * WIDE
+                    picked.append(left[begin : begin + WIDE, lanes])
+            turned = jnp.concatenate(picked, axis=0).T
+            both = jnp.where(low, turned[:blocks], turned[blocks:]).astype(BF16)
+            begin = per_part * pairs + (step * (fold // 2) + pair) * rows
+            begin = pl.multiple_of(begin, rows)
             for owner in range(parts):
-                out_ref[place(owner), pl.ds(begin, share), :] = both[
-                    owner * share : (owner + 1) * share
+                out_ref[place(owner), pl.ds(begin, rows), :] = both[
+                    owner * rows : (owner + 1) * rows
                 ]
 
     def right(later):
         chunk = natural(step - groups, idx_ref[2], steps // 2)
+        rows = jnp.concatenate([piece[...] for piece in own + later], axis=0)
+        value = jnp.dot(back[chunk], rows, preferred_element_type=F32)
+        for t in range(WIDE):
+            wide[t] = value[:, t * size : (t + 1) * size]
         for t in range(WIDE):
             block = chunk * WIDE + t
-            rows = [piece[:, t * size : (t + 1) * size] for piece in own + later]
-            lhs = [
-                scratch[h, pl.ds(block, pairs, stride=blocks), :]
-                for h in range(scratch.shape[0])
-            ]
-            lhs = jnp.concatenate(lhs, axis=1).astype(BF16)
-            value = jnp.dot(
-                lhs, jnp.concatenate(rows, axis=0), preferred_element_type=F32
-            )
             begin = pl.multiple_of(lax.rem(block, per_part) * pairs, pairs)
-            out_ref[place(block // per_part), pl.ds(begin, pairs), :] = value.astype(BF16)
+            out_ref[place(block // per_part), pl.ds(begin, pairs), :] = wide[
+                t, pl.ds(t, pairs, stride=WIDE), :
+            ].astype(BF16)
 
     pl.when((step >= groups) & (step < groups + steps // 2))(lambda: right(near))
     pl.when(step >= groups + steps // 2)(lambda: right(far))
 
 
-def factor_grads(total, students, mixed, left_diag, own, late, scalars, parts, size, scale):
+def factor_grads(
+    sets, weight, total, students, mixed, left_diag, own, late, scalars, parts, size, scale
+):
+    pieces = [piece for group in sets for piece in group]
     groups, count = left_diag.shape[0], total.shape[0]
-    rows = mixed[0].shape[0]
+    width = weight.shape[0] // 2
     half = late[0].shape[0]
     steps = own[0].shape[1] // (WIDE * size)
-    pairs = rows // (steps * WIDE)
+    blocks = steps * WIDE
+    pairs = groups * BLK // blocks
 
     def group(n):
         return jnp.minimum(n, groups - 1)
 
-    out_rows = (rows + pairs * (steps * WIDE) * (steps * WIDE) // size) // parts
+    out_rows = (pairs * blocks + pairs * blocks * blocks // size) // parts
     return pl.pallas_call(
-        functools.partial(grads_kernel, groups, steps, scale),
+        functools.partial(grads_kernel, groups, steps, scale, [len(g) for g in sets]),
         grid_spec=pltpu.PrefetchScalarGridSpec(
             num_scalar_prefetch=1,
             grid=(groups + steps,),
-            in_specs=[pl.BlockSpec((count, BLK), lambda n, s: (0, group(n)))]
+            in_specs=[whole_spec(piece) for piece in pieces]
+            + [pl.BlockSpec((width, BLK), lambda n, s: (1 - s[2], group(n)))]
+            + [pl.BlockSpec((count, BLK), lambda n, s: (0, group(n)))]
             + [pl.BlockSpec((count // 2, BLK), lambda n, s: (0, group(n)))] * 2
-            + [pl.BlockSpec((BLK, count // 2), lambda n, s: (group(n), 0))] * 2
+            + [pl.BlockSpec((1, BLK, count // 2), lambda n, s: (group(n), 0, 0))] * 2
             + [pl.BlockSpec((1, BLK, BLK), lambda n, s: (group(n), 0, 0))]
             + token_specs(half, WIDE * size, steps, groups, True)
             + token_specs(half, WIDE * size, steps, groups, False),
             out_specs=pl.BlockSpec((parts, out_rows, size), lambda n, s: (0, 0, 0)),
-            scratch_shapes=[pltpu.VMEM((count // LANES, rows, LANES), F32)],
+            scratch_shapes=[
+                pltpu.VMEM((count, width), BF16),
+                pltpu.VMEM((steps, groups * (BLK // steps), count), BF16),
+                pltpu.VMEM((WIDE, pairs * WIDE, size), F32),
+            ],
         ),
         out_shape=jax.ShapeDtypeStruct((parts, out_rows, size), BF16),
         compiler_params=pltpu.CompilerParams(vmem_limit_bytes=50 * 2**20),
         cost_estimate=SMALL,
         name="factor_grads",
-    )(scalars, total, *students, *mixed, left_diag, *own, *late)
+    )(scalars, *pieces, weight, total, *students, *mixed, left_diag, *own, *late)
 
 
 def tiled_body(tokens, gate_weight, up_weight, down_weight, right_factor, left_factor):
@@ -637,11 +695,8 @@
     def after(value, *others):
         return lax.optimization_barrier((value,) + others)[0]
 
-    def gather(value):
-        value = value[None]
-        for bit in (1, 2):
-            value = jnp.concatenate([value, along(value, bit)], axis=0)
-        return value
+    def double(value, bit):
+        return jnp.concatenate([value, along(value, bit)], axis=0)
 
     def add(*terms):
         return sum(term.astype(F32) for term in terms)
@@ -650,7 +705,7 @@
     chunks = [(0, head), (head, part - head)]
 
     near_tokens = swap(tokens)
-    first, rest = pack_tokens(tokens, odd, chip)
+    first, rest = cut_tokens(tokens, odd, chip)
     arrived = across(first)
     base = jnp.stack([odd, 1 - odd])
     mine_block = lax.div(part, BLK) * chip
@@ -660,58 +715,51 @@
         return jnp.concatenate([base, jnp.stack([me, core, block])]).astype(jnp.int32)
 
     own_pieces = [(t, row, 2) for t in (tokens, near_tokens) for row in (0, 1)]
-    got = {}
-
-    def send(e, pieces, order):
-        values = [
-            products(pieces, order, gate_weight, up_weight, *chunk) for chunk in chunks
-        ]
-        swapped = [swap(other[0]) for _, other in values]
-        sums = [add(mine[0], s).astype(BF16) for (mine, _), s in zip(values, swapped)]
-        got[e] = [across(value) for value in sums]
-        return values, sums
-
-    values, sums = send(0, own_pieces, scalars(other_block))
-    last = values[-1][0]
-
-    right_rows = gather(turn(after(right_factor, first), 0))
-    left_rows = gather(after(left_factor, last))
+    mine, other = products(
+        own_pieces, scalars(other_block), gate_weight, up_weight, 0, part
+    )
+    early = mine
+    sums = add(mine[0], swap(other[0])).astype(BF16)
+    got_early = across(sums)
+
+    right_rows = turn(after(right_factor, first), 0)[None]
+    left_rows = along(after(left_factor, first), 1)[None]
+    left_rows = jnp.concatenate([left_factor[None], left_rows], axis=0)
+    right_rows = double(double(after(right_rows, early), 1), 2)
+    left_rows = double(after(left_rows, early), 2)
     for axis, bit in ((0, 2), (1, 1)):
         split = left_rows.reshape((2, 2) + left_rows.shape[1:])
         split = jnp.where(lax.rem(lax.div(z, bit), 2) == 1, jnp.flip(split, axis), split)
         left_rows = split.reshape(left_rows.shape)
-    left_rows = left_rows.transpose(1, 3, 0, 2)
-    pairs, blocks = left_rows.shape[:2]
-    left_rows = left_rows.reshape(-1, BLK // blocks, blocks, 1, blocks)
-    eye = jnp.eye(BLK // blocks, dtype=jnp.bool_)[None, :, None, :, None]
-    left_diag = jnp.where(eye, left_rows, jnp.zeros((), BF16)).reshape(-1, BLK, BLK)
-
-    arrived = after(arrived, last)
+    pairs, blocks = left_rows.shape[1], left_rows.shape[3]
+    left_rows = left_rows.transpose(1, 3, 0, 2).reshape(pairs, blocks, blocks)
+    left_diag = spread_left(after(left_rows, early))
+
+    arrived = after(arrived, early)
     partner = along(arrived, 1)
     near_arrived = swap(arrived)
-    late_first = across(after(rest, *sums))
+    late_first = across(after(rest, sums))
     order = jnp.concatenate([base, jnp.stack([chip, z])]).astype(jnp.int32)
     own = [tokens, tokens, near_tokens, near_tokens]
     mixed0, student0 = student_part(
-        [after(tokens, *sums)] + own[1:], False, order, right_rows, left_diag, tensor_count
+        [after(tokens, sums)] + own[1:], False, order, right_rows, left_diag, tensor_count
     )
     partner = after(partner, mixed0)
     late = [arrived, partner, near_arrived, swap(partner)]
     late_pieces = [(t, None, 3) for t in late]
-    values, sums = send(1, late_pieces, scalars(other_block))
 
     kept, other = products(
         own_pieces + late_pieces,
-        after(scalars(mine_block), *sums),
+        after(scalars(mine_block), mixed0, sums),
         gate_weight,
         up_weight,
         0,
         part,
     )
-    kept_other = swap(other)
-    late_first = after(late_first, kept)
-    late_partner = along(late_first, 1)
-    late_rest = [late_first, late_partner, swap(late_first), swap(late_partner)]
+    kept_other = swap(after(other, got_early, late_first))
+    late_order = after(scalars(other_block), kept)
+    value0, other0 = products(late_pieces, late_order, gate_weight, up_weight, *chunks[0])
+    near0 = swap(other0[0])
 
     def activate(u, span, term):
         begin, width = span
@@ -719,28 +767,32 @@
         total = add(*terms, term)
         return (jax.nn.silu(total[0]) * total[1]).astype(BF16)
 
-    hidden_late = jnp.concatenate(
-        [activate(1, span, term) for span, term in zip(chunks, got[0])], axis=1
-    )
+    hidden_late = activate(1, (0, part), after(got_early, value0))
     got_late = across(hidden_late)
+    late_order = after(late_order, value0, hidden_late)
+    value1, other1 = products(late_pieces, late_order, gate_weight, up_weight, *chunks[1])
+    got0 = across(add(value0[0], after(near0, value1)).astype(BF16))
+    near1 = swap(after(other1[0], got_late))
+    got1 = across(add(value1[0], near1).astype(BF16))
+
     near_hidden_late = swap(hidden_late)
+    late_first = after(late_first, value1)
+    late_partner = along(late_first, 1)
+    late_rest = [late_first, late_partner, swap(late_first), swap(late_partner)]
     mixed1, student1 = student_part(
         late + late_rest, True, order, right_rows, left_diag, tensor_count
     )
     near_got_late = swap(got_late)
-    total = None
-    hidden = [activate(0, span, term) for span, term in zip(chunks, got[1])]
+    hidden = [activate(0, span, term) for span, term in zip(chunks, (got0, got1))]
     got_hidden = [across(value) for value in hidden]
-    for span, value in zip(chunks, hidden):
-        begin, width = span
-        pieces = [(value, 0), (swap(value), 0), (hidden_late, begin), (near_hidden_late, begin)]
-        total = target_add(total, pieces, down_weight, chip * part + begin, width)
-    for span, value in zip(chunks, got_hidden):
-        begin, width = span
-        pieces = [(got_late, begin), (near_got_late, begin), (value, 0), (swap(value), 0)]
-        total = target_add(total, pieces, down_weight, (1 - chip) * part + begin, width)
+    sets = [hidden, [swap(value) for value in hidden], [hidden_late], [near_hidden_late]]
+    total = target_part(sets, down_weight, chip)
+    near_hidden = [swap(value) for value in got_hidden]
+    sets = [[got_late], [near_got_late], got_hidden, near_hidden]
 
     grads = factor_grads(
+        sets,
+        down_weight,
         total,
         (student0, student1),
         (mixed0, mixed1),

time: 311 us -> 218 us (0.70)
  Pallas kernels: 143 us -> 90.1 us
  waiting for transfers between devices: 98.7 us -> 72.8 us
  starting transfers between devices: 41.3 us -> 33.9 us
  other arithmetic: 16.1 us -> 10.9 us
    pallas_call x6 -> x4, Pallas kernels: 84.6 us -> 36.4 us  [the longest x1 21.5 us: factor_grads(): pl.pallas_call(functools.partial(grads_kernel, groups, steps, scale, [len...]
    ppermute x9 -> x8, waiting for transfers between devices: 66.7 us -> 35.4 us  [across(): return lax.ppermute(value, 'fsdp', [(i, i ^ 2) for i in range(fsdp_count)])]
    ppermute x8, starting transfers between devices: 18.5 us -> 8.21 us  [along(): lax.ppermute(value, 'tensor', [(i, i ^ bit) for i in range(tensor_count)])]
    ppermute x8, waiting for transfers between devices: 19.5 us -> 25.7 us  [along(): lax.ppermute(value, 'tensor', [(i, i ^ bit) for i in range(tensor_count)])]
    broadcast_in_dim x5 -> x0, local copies, waits for them, and re-layouts: 6.06 us -> none  [tiled_body(): jnp.where(eye, left_rows, jnp.zeros((), BF16)).reshape(-1, BLK, BLK)]
    pallas_call x5 -> x4, Pallas kernels: 38.4 us -> 35.3 us  [products(): pl.pallas_call(functools.partial(products_kernel, sets), grid_spec=pltpu....]
    ppermute x9 -> x8, starting transfers between devices: 12.7 us -> 14.1 us  [across(): return lax.ppermute(value, 'fsdp', [(i, i ^ 2) for i in range(fsdp_count)])]
  transfers between devices with their start and end apart: 36 -> 34, of which waited for: 14 -> 12; matrix products, arithmetic and copies ran while one was open for 7% -> 6% of each run, Pallas kernels for 32% -> 32%
where the time goes in v4:
time: 218 us; the launch traced here: 216 us
  Pallas kernels  90.1 us (41%)
  waiting for transfers between devices  72.8 us (33%)
  starting transfers between devices  33.9 us (16%)
  other arithmetic  10.9 us (5%)
  local copies, waits for them, and re-layouts  7.23 us (3%)
    ppermute x8, waiting for transfers between devices, across(): return lax.ppermute(value, 'fsdp', [(i, i ^ 2) for i in range(fsdp_count)])  35.4 us
    pallas_call x4, Pallas kernels, products(): pl.pallas_call(functools.partial(products_kernel, sets), grid_spec=pltpu....  35.3 us
    ppermute x8, waiting for transfers between devices, along(): lax.ppermute(value, 'tensor', [(i, i ^ bit) for i in range(tensor_count)])  25.7 us
    pallas_call x1, Pallas kernels, factor_grads(): pl.pallas_call(functools.partial(grads_kernel, groups, steps, scale, [len...  21.5 us
    pallas_call x2, Pallas kernels, student_part(): pl.pallas_call(functools.partial(student_kernel, steps, late, tensor_coun...  18.3 us
    ppermute x8, starting transfers between devices, across(): return lax.ppermute(value, 'fsdp', [(i, i ^ 2) for i in range(fsdp_count)])  14.1 us
    ppermute x3, waiting for transfers between devices, turn(): return lax.ppermute(value, both_axes, perm)  9.89 us
    pallas_call x1, Pallas kernels, target_part(): pl.pallas_call(functools.partial(target_kernel, [len(group) for group in...  9.74 us
  transfers between devices with their start and end apart: 34, of which 12 were waited for; matrix products, arithmetic and copies ran while one was open for 6% of the time, Pallas kernels for 32%

profile of v4, /device:TPU:0, one launch (start us, length us, event | category | flops | bytes accessed | tf_op | source)
XLA Modules:
  0.0 215.9 jit_solution(17913603729451301242)
XLA Ops:
  0.6 0.5 collective-permute-start
  1.1 0.7 pad_add_fusion.1.idx_ref
  1.8 3.0 %cut_tokens.1 = (bf16[64,4096]{1,0:T(8,128)(2,1)}, bf16[64,4096]{1,0:T(8,128)(2,1)}) custom-call(s32[3]{0:T(128)} %pad_add_fusion.1.idx_ref, bf16[128,8192]{1,0:T(8,128)(2,1)} %refs_14_.1, bf16[128,8192]{1,0:T(8,128)(2,1)} %refs_14_.1), custom_call_target="tpu_custom_call" | custom-call | flops 1 | bytes 1 | tf_op jit(solution)/shard_map/cut_tokens/pallas_call | solution.py:314
  4.8 2.5 %collective-permute-start.7 = (bf16[64,4096]{1,0:T(8,128)(2,1)}, bf16[64,4096]{1,0:T(8,128)(2,1)S(1)}, u32[]{:S(2)}, u32[]{:S(2)}) collective-permute-start(bf16[64,4096]{1,0:T(8,128)(2,1)} %get-tuple-element.36), channel_id=1, source_target_pairs={{0,8},{4,12},{8,0},{12,4},{1,9},{5,13},{9,1},{13,5},{2,10},{6,14},... | collective-permute-start | bytes 1572872 | tf_op jit(solution)/shard_map/ppermute | solution.py:683
  7.4 2.1 collective-permute-start.2
  9.5 1.7 collective-permute-start.5
  11.3 10.7 %gate_up_products.4 = (bf16[1,2,128,1792]{3,2,1,0:T(8,128)(2,1)S(1)}, bf16[1,2,128,1792]{3,2,1,0:T(8,128)(2,1)}) custom-call(s32[5]{0:T(128)S(1)} %concatenate.29.idx_ref, bf16[128,8192]{1,0:T(8,128)(2,1)S(1)} %copy-done, bf16[128,8192]{1,0:T(8,128)(2,1)S(1)} %copy-done, bf16[128,8192]{1,0:T(8,128)(2,1)} %collective-permute-done.refs_2_.refs_3_.refs_15_.refs_16_, ...), custom_call_target="tpu_custom_call" | custom-call | flops 1 | bytes 1 | tf_op jit(solution)/shard_map/gate_up_products/pallas_call | solution.py:357
  22.1 0.4 collective-permute-start.3
  22.5 1.0 pad_maximum_fusion.2
  23.5 2.5 %collective-permute-start.6 = (bf16[2,32,16,64]{3,2,1,0:T(8,128)(2,1)S(1)}, bf16[2,32,16,64]{3,2,1,0:T(8,128)(2,1)S(1)}, u32[]{:S(2)}, u32[]{:S(2)}) collective-permute-start(bf16[2,32,16,64]{3,2,1,0:T(8,128)(2,1)S(1)} %pad_maximum_fusion.2), channel_id=1, source_target_pairs={{0,2},{1,3},{2,0},{3,1},{4,6},{5,7},{6,4},{7,5},{8,10},{9,11},{10,... | collective-permute-start | bytes 393224 | tf_op jit(solution)/shard_map/ppermute | solution.py:686
  26.0 0.9 constant_dynamic-update-slice_fusion.2
  27.0 0.5 collective-permute-start.1
  27.6 1.7 pad_maximum_fusion.1
  29.3 3.4 %collective-permute-start.4 = (bf16[2,16,32,128]{3,2,1,0:T(8,128)(2,1)}, bf16[2,16,32,128]{3,2,1,0:T(8,128)(2,1)}, u32[]{:S(2)}, u32[]{:S(2)}) collective-permute-start(bf16[2,16,32,128]{3,2,1,0:T(8,128)(2,1)} %pad_maximum_fusion.1), channel_id=1, source_target_pairs={{0,2},{1,3},{2,0},{3,1},{4,6},{5,7},{6,4},{7,5},{8,10},{9,11},{10,... | collective-permute-start | bytes 786440 | tf_op jit(solution)/shard_map/ppermute | solution.py:686
  32.7 12.2 %collective-permute-done.6 = bf16[2,32,16,64]{3,2,1,0:T(8,128)(2,1)S(1)} collective-permute-done((bf16[2,32,16,64]{3,2,1,0:T(8,128)(2,1)S(1)}, bf16[2,32,16,64]{3,2,1,0:T(8,128)(2,1)S(1)}, u32[]{:S(2)}, u32[]{:S(2)}) %collective-permute-start.6) | collective-permute-done | bytes 131104 | tf_op jit(solution)/shard_map/ppermute | solution.py:686
  45.0 0.1 reverse_select_fusion.1
  45.2 0.2 reverse_select_fusion
  45.4 1.0 copy.12.left_ref
  46.4 0.1 collective-permute-start.8
  46.5 2.2 %spread_left.1.refs_5_.refs_9_.refs_12_ = bf16[8,256,256]{2,1,0:T(8,128)(2,1)} custom-call(bf16[32,64,64]{2,1,0:T(8,128)(2,1)} %copy.12.left_ref), custom_call_target="tpu_custom_call" | custom-call | flops 1 | bytes 1 | tf_op jit(solution)/shard_map/spread_left/pallas_call | solution.py:452
  48.7 1.9 collective-permute-done.4
  50.7 1.0 constant_dynamic-update-slice_fusion.refs_4_.refs_8_
  51.7 2.5 %fusion = bf16[2,128,1792]{2,1,0:T(8,128)(2,1)} fusion(bf16[2,128,1792]{2,1,0:T(8,128)(2,1)} %collective-permute-done.1, bf16[1,2,128,1792]{3,2,1,0:T(8,128)(2,1)S(1)} %get-tuple-element.33), kind=kLoop, calls=%fused_computation.1 | loop fusion | flops 1835008 | bytes 2752512 | tf_op jit(solution)/shard_map/convert_element_type | solution.py:722
  54.2 3.3 %collective-permute-start.11 = (bf16[2,128,1792]{2,1,0:T(8,128)(2,1)}, bf16[2,128,1792]{2,1,0:T(8,128)(2,1)}, u32[]{:S(2)}, u32[]{:S(2)}) collective-permute-start(bf16[2,128,1792]{2,1,0:T(8,128)(2,1)} %fusion), channel_id=1, source_target_pairs={{0,8},{4,12},{8,0},{12,4},{1,9},{5,13},{9,1},{13,5},{2,10},{6,14},... | collective-permute-start | bytes 2752520 | tf_op jit(solution)/shard_map/ppermute | solution.py:683
  57.5 1.0 copy-done.7
  58.5 8.8 %student_part.2 = (bf16[8,256,256]{2,1,0:T(8,128)(2,1)S(1)}, f32[256,2048]{1,0:T(8,128)}) custom-call(s32[4]{0:T(128)S(1)} %pad_add_fusion.idx_ref, bf16[128,8192]{1,0:T(8,128)(2,1)} %refs_14_.1, bf16[128,8192]{1,0:T(8,128)(2,1)} %refs_14_.1, bf16[128,8192]{1,0:T(8,128)(2,1)} %collective-permute-done.refs_2_.refs_3_.refs_15_.refs_16_, ...), custom_call_target="tpu_custom_call" | custom-call | flops 10000000000 | bytes 10000000 | tf_op jit(solution)/shard_map/student_part/pallas_call | solution.py:530
  67.4 1.0 copy-done.2
  68.5 1.8 collective-permute-done.10.refs_7_.refs_3_.refs_20_
  70.3 13.2 %gate_up_products.5 = (bf16[2,2,128,1792]{3,2,1,0:T(8,128)(2,1)S(1)}, bf16[2,2,128,1792]{3,2,1,0:T(8,128)(2,1)}) custom-call(s32[5]{0:T(128)S(1)} %concatenate.28.idx_ref, bf16[128,8192]{1,0:T(8,128)(2,1)} %refs_14_.1, bf16[128,8192]{1,0:T(8,128)(2,1)} %refs_14_.1, bf16[128,8192]{1,0:T(8,128)(2,1)} %collective-permute-done.refs_2_.refs_3_.refs_15_.refs_16_, ...), custom_call_target="tpu_custom_call" | custom-call | flops 1 | bytes 1 | tf_op jit(solution)/shard_map/gate_up_products/pallas_call | solution.py:357
  83.5 5.9 %collective-permute-done.12.refs_4_.refs_21_ = bf16[64,4096]{1,0:T(8,128)(2,1)S(1)} collective-permute-done((bf16[64,4096]{1,0:T(8,128)(2,1)}, bf16[64,4096]{1,0:T(8,128)(2,1)S(1)}, u32[]{:S(2)}, u32[]{:S(2)}) %collective-permute-start.12) | collective-permute-done | bytes 524320 | tf_op jit(solution)/shard_map/ppermute | solution.py:683
  89.4 6.2 %gate_up_products.6 = (bf16[1,2,128,1024]{3,2,1,0:T(8,128)(2,1)S(1)}, bf16[1,2,128,1024]{3,2,1,0:T(8,128)(2,1)S(1)}) custom-call(s32[5]{0:T(128)S(1)} %concatenate.29.idx_ref, bf16[64,4096]{1,0:T(8,128)(2,1)S(1)} %collective-permute-done.7.refs_4_.refs_0_.refs_17_, bf16[64,4096]{1,0:T(8,128)(2,1)S(1)} %collective-permute-done.8.refs_5_.refs_1_.refs_18_, ...), custom_call_target="tpu_custom_call" | custom-call | flops 1 | bytes 1 | tf_op jit(solution)/shard_map/gate_up_products/pallas_call | solution.py:357
  95.6 0.6 collective-permute-start.16
  96.2 1.5 bitcast_add_fusion
  97.7 0.3 fusion.3.refs_4_
  98.0 1.8 collective-permute-start.14
  99.8 5.2 %gate_up_products.7 = (bf16[1,2,128,768]{3,2,1,0:T(8,128)(2,1)S(1)}, bf16[1,2,128,768]{3,2,1,0:T(8,128)(2,1)S(1)}) custom-call(s32[5]{0:T(128)S(1)} %concatenate.29.idx_ref, bf16[64,4096]{1,0:T(8,128)(2,1)S(1)} %collective-permute-done.7.refs_4_.refs_0_.refs_17_, bf16[64,4096]{1,0:T(8,128)(2,1)S(1)} %collective-permute-done.8.refs_5_.refs_1_.refs_18_, ...), custom_call_target="tpu_custom_call" | custom-call | flops 1 | bytes 1 | tf_op jit(solution)/shard_map/gate_up_products/pallas_call | solution.py:357
  105.1 5.5 %collective-permute-done.14.refs_0_ = bf16[128,1792]{1,0:T(8,128)(2,1)S(1)} collective-permute-done((bf16[128,1792]{1,0:T(8,128)(2,1)S(1)}, bf16[128,1792]{1,0:T(8,128)(2,1)S(1)}, u32[]{:S(2)}, u32[]{:S(2)}) %collective-permute-start.14) | collective-permute-done | bytes 458784 | tf_op jit(solution)/shard_map/ppermute | solution.py:683
  110.5 0.2 fusion.1
  110.7 1.8 collective-permute-start.17
  112.5 0.2 collective-permute-start.26
  112.8 0.3 collective-permute-start.28
  113.1 1.0 collective-permute-start.20
  114.1 11.4 %collective-permute-done.17 = bf16[2,128,1024]{2,1,0:T(8,128)(2,1)S(1)} collective-permute-done((bf16[2,128,1024]{2,1,0:T(8,128)(2,1)S(1)}, bf16[2,128,1024]{2,1,0:T(8,128)(2,1)S(1)}, u32[]{:S(2)}, u32[]{:S(2)}) %collective-permute-start.17) | collective-permute-done | bytes 524320 | tf_op jit(solution)/shard_map/ppermute | solution.py:683
  125.5 0.2 bitcast_add_fusion.1
  125.7 0.2 fusion.6.refs_0_
  125.8 1.8 collective-permute-start.18
  127.7 6.3 %collective-permute-done.20 = bf16[2,128,768]{2,1,0:T(8,128)(2,1)S(1)} collective-permute-done((bf16[2,128,768]{2,1,0:T(8,128)(2,1)S(1)}, bf16[2,128,768]{2,1,0:T(8,128)(2,1)S(1)}, u32[]{:S(2)}, u32[]{:S(2)}) %collective-permute-start.20) | collective-permute-done | bytes 393248 | tf_op jit(solution)/shard_map/ppermute | solution.py:683
  134.2 1.8 collective-permute-start.21
  136.0 0.5 collective-permute-start.24
  136.5 3.0 %collective-permute-done.18.refs_2_ = bf16[128,1024]{1,0:T(8,128)(2,1)S(1)} collective-permute-done((bf16[128,1024]{1,0:T(8,128)(2,1)S(1)}, bf16[128,1024]{1,0:T(8,128)(2,1)S(1)}, u32[]{:S(2)}, u32[]{:S(2)}) %collective-permute-start.18) | collective-permute-done | bytes 262176 | tf_op jit(solution)/shard_map/ppermute | solution.py:683
  139.6 0.5 collective-permute-start.25
  140.1 3.3 %collective-permute-done.21.refs_3_ = bf16[128,768]{1,0:T(8,128)(2,1)S(1)} collective-permute-done((bf16[128,768]{1,0:T(8,128)(2,1)S(1)}, bf16[128,768]{1,0:T(8,128)(2,1)S(1)}, u32[]{:S(2)}, u32[]{:S(2)}) %collective-permute-start.21) | collective-permute-done | bytes 196640 | tf_op jit(solution)/shard_map/ppermute | solution.py:683
  143.4 9.5 %student_part.3 = (bf16[8,256,256]{2,1,0:T(8,128)(2,1)}, f32[256,2048]{1,0:T(8,128)}) custom-call(s32[4]{0:T(128)S(1)} %pad_add_fusion.idx_ref, bf16[64,4096]{1,0:T(8,128)(2,1)S(1)} %collective-permute-done.7.refs_4_.refs_0_.refs_17_, bf16[64,4096]{1,0:T(8,128)(2,1)S(1)} %collective-permute-done.8.refs_5_.refs_1_.refs_18_, ...), custom_call_target="tpu_custom_call" | custom-call | flops 10000000000 | bytes 10000000 | tf_op jit(solution)/shard_map/student_part/pallas_call | solution.py:530
  153.0 9.7 %target_part.1.refs_7_ = f32[512,2048]{1,0:T(8,128)} custom-call(s32[1]{0:T(128)} %bitcast.2.idx_ref, bf16[128,1024]{1,0:T(8,128)(2,1)S(1)} %fusion.6.refs_0_, bf16[128,768]{1,0:T(8,128)(2,1)S(1)} %fusion.8.refs_1_, bf16[128,1024]{1,0:T(8,128)(2,1)S(1)} %collective-permute-done.24.refs_2_, bf16[128,768]{1,0:T(8,128)(2,1)S(1)} %collective-permute-done.25.refs_3_, ...), custom_call_target="tpu_custom_call" | custom-call | flops 1 | bytes 1 | tf_op jit(solution)/shard_map/target_part/pallas_call | solution.py:407
  162.7 21.5 %factor_grads.1 = bf16[4,768,128]{2,1,0:T(8,128)(2,1)} custom-call(s32[4]{0:T(128)S(1)} %pad_add_fusion.idx_ref, bf16[128,1792]{1,0:T(8,128)(2,1)S(1)} %collective-permute-done.14.refs_0_, bf16[128,1792]{1,0:T(8,128)(2,1)S(1)} %collective-permute-done.15.refs_1_, bf16[128,1024]{1,0:T(8,128)(2,1)S(1)} %collective-permute-done.18.refs_2_, ...), custom_call_target="tpu_custom_call" | custom-call | flops 1 | bytes 1 | tf_op jit(solution)/shard_map/factor_grads/pallas_call | solution.py:643
  184.2 1.0 slice.82
  185.3 11.5 %collective-permute-done.30 = bf16[2,768,128]{2,1,0:T(8,128)(2,1)S(1)} collective-permute-done((bf16[2,768,128]{2,1,0:T(8,128)(2,1)S(1)}, bf16[2,768,128]{2,1,0:T(8,128)(2,1)S(1)}, u32[]{:S(2)}, u32[]{:S(2)}) %collective-permute-start.30) | collective-permute-done | bytes 393248 | tf_op jit(solution)/shard_map/ppermute | solution.py:686
  196.8 1.1 add_convert_fusion
  198.0 0.7 collective-permute-start.31
  198.7 5.7 %collective-permute-start.32 = (bf16[512,128]{1,0:T(8,128)(2,1)S(1)}, bf16[512,128]{1,0:T(8,128)(2,1)S(1)}, u32[]{:S(2)}, u32[]{:S(2)}) collective-permute-start(bf16[512,128]{1,0:T(8,128)(2,1)S(1)} %get-tuple-element.65), channel_id=1, source_target_pairs={{0,8},{1,12},{2,0},{3,4},{4,9},{5,13},{6,1},{7,5},{8,10},{9,14},{1... | collective-permute-start | bytes 393224 | tf_op jit(solution)/shard_map/ppermute | solution.py:693
  204.4 0.2 reshape.44
  204.6 0.7 copy.13
  205.3 9.9 %collective-permute-done.32 = bf16[512,128]{1,0:T(8,128)(2,1)S(1)} collective-permute-done((bf16[512,128]{1,0:T(8,128)(2,1)S(1)}, bf16[512,128]{1,0:T(8,128)(2,1)S(1)}, u32[]{:S(2)}, u32[]{:S(2)}) %collective-permute-start.32) | collective-permute-done | bytes 131104 | tf_op jit(solution)/shard_map/ppermute | solution.py:693
  215.2 0.7 convert_add_fusion.3
  (67 shorter events, 1.3 us)
Async XLA Ops:
  0.6 10.7 %collective-permute-start = (bf16[128,8192]{1,0:T(8,128)(2,1)}, bf16[128,8192]{1,0:T(8,128)(2,1)}, u32[]{:S(2)}, u32[]{:S(2)}) collective-permute-start(bf16[128,8192]{1,0:T(8,128)(2,1)} %refs_14_.1), channel_id=1, source_target_pairs={{0,4},{4,0},{8,12},{12,8},{1,5},{5,1},{9,13},{13,9},{2,6},{6,2},{1... | collective-permute-start | bytes 6291464 | tf_op jit(solution)/shard_map/ppermute | solution.py:680
  1.8 9.5 %copy-start = (bf16[128,8192]{1,0:T(8,128)(2,1)S(1)}, bf16[128,8192]{1,0:T(8,128)(2,1)}, u32[]{:S(2)}) copy-start(bf16[128,8192]{1,0:T(8,128)(2,1)} %refs_14_.1) | copy-start | bytes 6291460
  4.8 22.0 %collective-permute-start.7 = (bf16[64,4096]{1,0:T(8,128)(2,1)}, bf16[64,4096]{1,0:T(8,128)(2,1)S(1)}, u32[]{:S(2)}, u32[]{:S(2)}) collective-permute-start(bf16[64,4096]{1,0:T(8,128)(2,1)} %get-tuple-element.36), channel_id=1, source_target_pairs={{0,8},{4,12},{8,0},{12,4},{1,9},{5,13},{9,1},{13,5},{2,10},{6,14},... | collective-permute-start | bytes 1572872 | tf_op jit(solution)/shard_map/ppermute | solution.py:683
  7.4 14.7 %collective-permute-start.2 = (bf16[16,32,128]{2,1,0:T(8,128)(2,1)}, bf16[16,32,128]{2,1,0:T(8,128)(2,1)}, u32[]{:S(2)}, u32[]{:S(2)}) collective-permute-start(bf16[16,32,128]{2,1,0:T(8,128)(2,1)} %param.10), channel_id=1, source_target_pairs={{0,0},{1,4},{2,8},{3,12},{4,1},{5,5},{6,9},{7,13},{8,2},{9,6},{10,... | collective-permute-start | bytes 393224 | tf_op jit(solution)/shard_map/ppermute | solution.py:693
  9.5 12.9 %collective-permute-start.5 = (bf16[32,16,64]{2,1,0:T(8,128)(2,1)}, bf16[32,16,64]{2,1,0:T(8,128)(2,1)}, u32[]{:S(2)}, u32[]{:S(2)}) collective-permute-start(bf16[32,16,64]{2,1,0:T(8,128)(2,1)} %param.11), channel_id=1, source_target_pairs={{0,1},{1,0},{2,3},{3,2},{4,5},{5,4},{6,7},{7,6},{8,9},{9,8},{10,11... | collective-permute-start | bytes 196616 | tf_op jit(solution)/shard_map/ppermute | solution.py:686
  22.1 5.5 %collective-permute-start.3 = (bf16[1,16,32,128]{3,2,1,0:T(8,128)(2,1)}, bf16[1,16,32,128]{3,2,1,0:T(8,128)(2,1)S(1)}, u32[]{:S(2)}, u32[]{:S(2)}) collective-permute-start(bf16[1,16,32,128]{3,2,1,0:T(8,128)(2,1)} %bitcast.11), channel_id=1, source_target_pairs={{0,1},{1,0},{2,3},{3,2},{4,5},{5,4},{6,7},{7,6},{8,9},{9,8},{10,11... | collective-permute-start | bytes 393224 | tf_op jit(solution)/shard_map/ppermute | solution.py:686
  23.5 21.4 %collective-permute-start.6 = (bf16[2,32,16,64]{3,2,1,0:T(8,128)(2,1)S(1)}, bf16[2,32,16,64]{3,2,1,0:T(8,128)(2,1)S(1)}, u32[]{:S(2)}, u32[]{:S(2)}) collective-permute-start(bf16[2,32,16,64]{3,2,1,0:T(8,128)(2,1)S(1)} %pad_maximum_fusion.2), channel_id=1, source_target_pairs={{0,2},{1,3},{2,0},{3,1},{4,6},{5,7},{6,4},{7,5},{8,10},{9,11},{10,... | collective-permute-start | bytes 393224 | tf_op jit(solution)/shard_map/ppermute | solution.py:686
  26.9 41.6 %collective-permute-start.9 = (bf16[64,4096]{1,0:T(8,128)(2,1)S(1)}, bf16[64,4096]{1,0:T(8,128)(2,1)S(1)}, u32[]{:S(2)}, u32[]{:S(2)}) collective-permute-start(bf16[64,4096]{1,0:T(8,128)(2,1)S(1)} %collective-permute-done.7.refs_4_.refs_0_.refs_17_), channel_id=1, source_target_pairs={{0,4},{4,0},{8,12},{12,8},{1,5},{5,1},{9,13},{13,9},{2,6},{6,2},{1... | collective-permute-start | bytes 1572872 | tf_op jit(solution)/shard_map/ppermute | solution.py:680
  27.0 24.7 %collective-permute-start.1 = (bf16[2,128,1792]{2,1,0:T(8,128)(2,1)}, bf16[2,128,1792]{2,1,0:T(8,128)(2,1)}, u32[]{:S(2)}, u32[]{:S(2)}) collective-permute-start(bf16[2,128,1792]{2,1,0:T(8,128)(2,1)} %bitcast.9), channel_id=1, source_target_pairs={{0,4},{4,0},{8,12},{12,8},{1,5},{5,1},{9,13},{13,9},{2,6},{6,2},{1... | collective-permute-start | bytes 2752520 | tf_op jit(solution)/shard_map/ppermute | solution.py:680
  27.6 17.4 %copy-start.9 = (bf16[1,16,32,128]{3,2,1,0:T(8,128)(2,1)}, bf16[1,16,32,128]{3,2,1,0:T(8,128)(2,1)S(1)}, u32[]{:S(2)}) copy-start(bf16[1,16,32,128]{3,2,1,0:T(8,128)(2,1)S(1)} %collective-permute-done.3) | copy-start | bytes 393220
  29.3 21.4 %collective-permute-start.4 = (bf16[2,16,32,128]{3,2,1,0:T(8,128)(2,1)}, bf16[2,16,32,128]{3,2,1,0:T(8,128)(2,1)}, u32[]{:S(2)}, u32[]{:S(2)}) collective-permute-start(bf16[2,16,32,128]{3,2,1,0:T(8,128)(2,1)} %pad_maximum_fusion.1), channel_id=1, source_target_pairs={{0,2},{1,3},{2,0},{3,1},{4,6},{5,7},{6,4},{7,5},{8,10},{9,11},{10,... | collective-permute-start | bytes 786440 | tf_op jit(solution)/shard_map/ppermute | solution.py:686
  45.2 3.5 %copy-start.10 = (bf16[1,16,32,128]{3,2,1,0:T(8,128)(2,1)S(1)}, bf16[1,16,32,128]{3,2,1,0:T(8,128)(2,1)}, u32[]{:S(2)}) copy-start(bf16[1,16,32,128]{3,2,1,0:T(8,128)(2,1)} %copy-done.9) | copy-start | bytes 393220
  46.4 22.0 %collective-permute-start.8 = (bf16[64,4096]{1,0:T(8,128)(2,1)S(1)}, bf16[64,4096]{1,0:T(8,128)(2,1)S(1)}, u32[]{:S(2)}, u32[]{:S(2)}) collective-permute-start(bf16[64,4096]{1,0:T(8,128)(2,1)S(1)} %collective-permute-done.7.refs_4_.refs_0_.refs_17_), channel_id=1, source_target_pairs={{0,1},{1,0},{2,3},{3,2},{4,5},{5,4},{6,7},{7,6},{8,9},{9,8},{10,11... | collective-permute-start | bytes 1572872 | tf_op jit(solution)/shard_map/ppermute | solution.py:686
  48.7 8.8 %copy-start.1 = (bf16[8,256,256]{2,1,0:T(8,128)(2,1)S(1)}, bf16[8,256,256]{2,1,0:T(8,128)(2,1)}, u32[]{:S(2)}) copy-start(bf16[8,256,256]{2,1,0:T(8,128)(2,1)} %spread_left.1.refs_5_.refs_9_.refs_12_) | copy-start | bytes 3145732
  51.7 2.5 %copy-start.6 = (bf16[4,16,32,128]{3,2,1,0:T(8,128)(2,1)}, bf16[4,16,32,128]{3,2,1,0:T(8,128)(2,1)S(1)}, u32[]{:S(2)}) copy-start(bf16[4,16,32,128]{3,2,1,0:T(8,128)(2,1)S(1)} %constant_dynamic-update-slice_fusion.refs_4_.refs_8_) | copy-start | bytes 1572868
  54.2 35.2 %collective-permute-start.11 = (bf16[2,128,1792]{2,1,0:T(8,128)(2,1)}, bf16[2,128,1792]{2,1,0:T(8,128)(2,1)}, u32[]{:S(2)}, u32[]{:S(2)}) collective-permute-start(bf16[2,128,1792]{2,1,0:T(8,128)(2,1)} %fusion), channel_id=1, source_target_pairs={{0,8},{4,12},{8,0},{12,4},{1,9},{5,13},{9,1},{13,5},{2,10},{6,14},... | collective-permute-start | bytes 2752520 | tf_op jit(solution)/shard_map/ppermute | solution.py:683
  57.5 1.0 copy-start.7
  67.3 1.0 copy-start.2
  68.4 1.9 collective-permute-start.10
  68.4 21.0 %collective-permute-start.12 = (bf16[64,4096]{1,0:T(8,128)(2,1)}, bf16[64,4096]{1,0:T(8,128)(2,1)S(1)}, u32[]{:S(2)}, u32[]{:S(2)}) collective-permute-start(bf16[64,4096]{1,0:T(8,128)(2,1)} %get-tuple-element.49), channel_id=1, source_target_pairs={{0,8},{4,12},{8,0},{12,4},{1,9},{5,13},{9,1},{13,5},{2,10},{6,14},... | collective-permute-start | bytes 1572872 | tf_op jit(solution)/shard_map/ppermute | solution.py:683
  89.4 54.0 %copy-start.3 = (bf16[64,4096]{1,0:T(8,128)(2,1)}, bf16[64,4096]{1,0:T(8,128)(2,1)S(1)}, u32[]{:S(2)}) copy-start(bf16[64,4096]{1,0:T(8,128)(2,1)S(1)} %collective-permute-done.12.refs_4_.refs_21_) | copy-start | bytes 1572868
  89.4 6.8 %collective-permute-start.13 = (bf16[2,2,128,1792]{3,2,1,0:T(8,128)(2,1)}, bf16[2,2,128,1792]{3,2,1,0:T(8,128)(2,1)S(1)}, u32[]{:S(2)}, u32[]{:S(2)}) collective-permute-start(bf16[2,2,128,1792]{3,2,1,0:T(8,128)(2,1)} %get-tuple-element.50), channel_id=1, source_target_pairs={{0,4},{4,0},{8,12},{12,8},{1,5},{5,1},{9,13},{13,9},{2,6},{6,2},{1... | collective-permute-start | bytes 5505032 | tf_op jit(solution)/shard_map/ppermute | solution.py:680
  95.6 9.4 %collective-permute-start.16 = (bf16[2,128,1024]{2,1,0:T(8,128)(2,1)S(1)}, bf16[2,128,1024]{2,1,0:T(8,128)(2,1)S(1)}, u32[]{:S(2)}, u32[]{:S(2)}) collective-permute-start(bf16[2,128,1024]{2,1,0:T(8,128)(2,1)S(1)} %bitcast.80), channel_id=1, source_target_pairs={{0,4},{4,0},{8,12},{12,8},{1,5},{5,1},{9,13},{13,9},{2,6},{6,2},{1... | collective-permute-start | bytes 1572872 | tf_op jit(solution)/shard_map/ppermute | solution.py:680
  98.0 12.5 %collective-permute-start.14 = (bf16[128,1792]{1,0:T(8,128)(2,1)S(1)}, bf16[128,1792]{1,0:T(8,128)(2,1)S(1)}, u32[]{:S(2)}, u32[]{:S(2)}) collective-permute-start(bf16[128,1792]{1,0:T(8,128)(2,1)S(1)} %fusion.3.refs_4_), channel_id=1, source_target_pairs={{0,8},{4,12},{8,0},{12,4},{1,9},{5,13},{9,1},{13,5},{2,10},{6,14},... | collective-permute-start | bytes 1376264 | tf_op jit(solution)/shard_map/ppermute | solution.py:683
  110.5 2.5 %collective-permute-start.19 = (bf16[2,128,768]{2,1,0:T(8,128)(2,1)S(1)}, bf16[2,128,768]{2,1,0:T(8,128)(2,1)S(1)}, u32[]{:S(2)}, u32[]{:S(2)}) collective-permute-start(bf16[2,128,768]{2,1,0:T(8,128)(2,1)S(1)} %bitcast.81), channel_id=1, source_target_pairs={{0,4},{4,0},{8,12},{12,8},{1,5},{5,1},{9,13},{13,9},{2,6},{6,2},{1... | collective-permute-start | bytes 1179656 | tf_op jit(solution)/shard_map/ppermute | solution.py:680
  110.7 14.8 %collective-permute-start.17 = (bf16[2,128,1024]{2,1,0:T(8,128)(2,1)S(1)}, bf16[2,128,1024]{2,1,0:T(8,128)(2,1)S(1)}, u32[]{:S(2)}, u32[]{:S(2)}) collective-permute-start(bf16[2,128,1024]{2,1,0:T(8,128)(2,1)S(1)} %fusion.1), channel_id=1, source_target_pairs={{0,8},{4,12},{8,0},{12,4},{1,9},{5,13},{9,1},{13,5},{2,10},{6,14},... | collective-permute-start | bytes 1572872 | tf_op jit(solution)/shard_map/ppermute | solution.py:683
  112.5 23.5 %collective-permute-start.26 = (bf16[128,1792]{1,0:T(8,128)(2,1)S(1)}, bf16[128,1792]{1,0:T(8,128)(2,1)S(1)}, u32[]{:S(2)}, u32[]{:S(2)}) collective-permute-start(bf16[128,1792]{1,0:T(8,128)(2,1)S(1)} %fusion.3.refs_4_), channel_id=1, source_target_pairs={{0,4},{4,0},{8,12},{12,8},{1,5},{5,1},{9,13},{13,9},{2,6},{6,2},{1... | collective-permute-start | bytes 1376264 | tf_op jit(solution)/shard_map/ppermute | solution.py:680
  112.8 23.3 %collective-permute-start.28 = (bf16[64,4096]{1,0:T(8,128)(2,1)S(1)}, bf16[64,4096]{1,0:T(8,128)(2,1)S(1)}, u32[]{:S(2)}, u32[]{:S(2)}) collective-permute-start(bf16[64,4096]{1,0:T(8,128)(2,1)S(1)} %collective-permute-done.12.refs_4_.refs_21_), channel_id=1, source_target_pairs={{0,4},{4,0},{8,12},{12,8},{1,5},{5,1},{9,13},{13,9},{2,6},{6,2},{1... | collective-permute-start | bytes 1572872 | tf_op jit(solution)/shard_map/ppermute | solution.py:680
  113.0 14.6 %collective-permute-start.27 = (bf16[64,4096]{1,0:T(8,128)(2,1)S(1)}, bf16[64,4096]{1,0:T(8,128)(2,1)S(1)}, u32[]{:S(2)}, u32[]{:S(2)}) collective-permute-start(bf16[64,4096]{1,0:T(8,128)(2,1)S(1)} %collective-permute-done.12.refs_4_.refs_21_), channel_id=1, source_target_pairs={{0,1},{1,0},{2,3},{3,2},{4,5},{5,4},{6,7},{7,6},{8,9},{9,8},{10,11... | collective-permute-start | bytes 1572872 | tf_op jit(solution)/shard_map/ppermute | solution.py:686
  113.1 20.8 %collective-permute-start.20 = (bf16[2,128,768]{2,1,0:T(8,128)(2,1)S(1)}, bf16[2,128,768]{2,1,0:T(8,128)(2,1)S(1)}, u32[]{:S(2)}, u32[]{:S(2)}) collective-permute-start(bf16[2,128,768]{2,1,0:T(8,128)(2,1)S(1)} %fusion.4), channel_id=1, source_target_pairs={{0,8},{4,12},{8,0},{12,4},{1,9},{5,13},{9,1},{13,5},{2,10},{6,14},... | collective-permute-start | bytes 1179656 | tf_op jit(solution)/shard_map/ppermute | solution.py:683
  125.8 13.7 %collective-permute-start.18 = (bf16[128,1024]{1,0:T(8,128)(2,1)S(1)}, bf16[128,1024]{1,0:T(8,128)(2,1)S(1)}, u32[]{:S(2)}, u32[]{:S(2)}) collective-permute-start(bf16[128,1024]{1,0:T(8,128)(2,1)S(1)} %fusion.6.refs_0_), channel_id=1, source_target_pairs={{0,8},{4,12},{8,0},{12,4},{1,9},{5,13},{9,1},{13,5},{2,10},{6,14},... | collective-permute-start | bytes 786440 | tf_op jit(solution)/shard_map/ppermute | solution.py:683
  127.7 25.3 %copy-start.5 = (bf16[64,4096]{1,0:T(8,128)(2,1)}, bf16[64,4096]{1,0:T(8,128)(2,1)S(1)}, u32[]{:S(2)}) copy-start(bf16[64,4096]{1,0:T(8,128)(2,1)S(1)} %collective-permute-done.27.refs_5_.refs_22_) | copy-start | bytes 1572868
  127.7 11.9 %collective-permute-start.29 = (bf16[64,4096]{1,0:T(8,128)(2,1)S(1)}, bf16[64,4096]{1,0:T(8,128)(2,1)S(1)}, u32[]{:S(2)}, u32[]{:S(2)}) collective-permute-start(bf16[64,4096]{1,0:T(8,128)(2,1)S(1)} %collective-permute-done.27.refs_5_.refs_22_), channel_id=1, source_target_pairs={{0,4},{4,0},{8,12},{12,8},{1,5},{5,1},{9,13},{13,9},{2,6},{6,2},{1... | collective-permute-start | bytes 1572872 | tf_op jit(solution)/shard_map/ppermute | solution.py:680
  134.2 9.2 %collective-permute-start.21 = (bf16[128,768]{1,0:T(8,128)(2,1)S(1)}, bf16[128,768]{1,0:T(8,128)(2,1)S(1)}, u32[]{:S(2)}, u32[]{:S(2)}) collective-permute-start(bf16[128,768]{1,0:T(8,128)(2,1)S(1)} %fusion.8.refs_1_), channel_id=1, source_target_pairs={{0,8},{4,12},{8,0},{12,4},{1,9},{5,13},{9,1},{13,5},{2,10},{6,14},... | collective-permute-start | bytes 589832 | tf_op jit(solution)/shard_map/ppermute | solution.py:683
  136.0 26.7 %collective-permute-start.15 = (bf16[128,1792]{1,0:T(8,128)(2,1)S(1)}, bf16[128,1792]{1,0:T(8,128)(2,1)S(1)}, u32[]{:S(2)}, u32[]{:S(2)}) collective-permute-start(bf16[128,1792]{1,0:T(8,128)(2,1)S(1)} %collective-permute-done.14.refs_0_), channel_id=1, source_target_pairs={{0,4},{4,0},{8,12},{12,8},{1,5},{5,1},{9,13},{13,9},{2,6},{6,2},{1... | collective-permute-start | bytes 1376264 | tf_op jit(solution)/shard_map/ppermute | solution.py:680
  136.0 16.9 %copy-start.4 = (bf16[64,4096]{1,0:T(8,128)(2,1)}, bf16[64,4096]{1,0:T(8,128)(2,1)S(1)}, u32[]{:S(2)}) copy-start(bf16[64,4096]{1,0:T(8,128)(2,1)S(1)} %collective-permute-done.28.refs_6_.refs_23_) | copy-start | bytes 1572868
  136.0 16.9 %collective-permute-start.24 = (bf16[128,1024]{1,0:T(8,128)(2,1)S(1)}, bf16[128,1024]{1,0:T(8,128)(2,1)S(1)}, u32[]{:S(2)}, u32[]{:S(2)}) collective-permute-start(bf16[128,1024]{1,0:T(8,128)(2,1)S(1)} %fusion.6.refs_0_), channel_id=1, source_target_pairs={{0,4},{4,0},{8,12},{12,8},{1,5},{5,1},{9,13},{13,9},{2,6},{6,2},{1... | collective-permute-start | bytes 786440 | tf_op jit(solution)/shard_map/ppermute | solution.py:680
  139.6 23.2 %collective-permute-start.22 = (bf16[128,1024]{1,0:T(8,128)(2,1)S(1)}, bf16[128,1024]{1,0:T(8,128)(2,1)S(1)}, u32[]{:S(2)}, u32[]{:S(2)}) collective-permute-start(bf16[128,1024]{1,0:T(8,128)(2,1)S(1)} %collective-permute-done.18.refs_2_), channel_id=1, source_target_pairs={{0,4},{4,0},{8,12},{12,8},{1,5},{5,1},{9,13},{13,9},{2,6},{6,2},{1... | collective-permute-start | bytes 786440 | tf_op jit(solution)/shard_map/ppermute | solution.py:680
  139.6 3.8 %copy-start.8 = (bf16[64,4096]{1,0:T(8,128)(2,1)}, bf16[64,4096]{1,0:T(8,128)(2,1)S(1)}, u32[]{:S(2)}) copy-start(bf16[64,4096]{1,0:T(8,128)(2,1)S(1)} %collective-permute-done.29.refs_7_.refs_24_) | copy-start | bytes 1572868
  139.6 13.4 %collective-permute-start.25 = (bf16[128,768]{1,0:T(8,128)(2,1)S(1)}, bf16[128,768]{1,0:T(8,128)(2,1)S(1)}, u32[]{:S(2)}, u32[]{:S(2)}) collective-permute-start(bf16[128,768]{1,0:T(8,128)(2,1)S(1)} %fusion.8.refs_1_), channel_id=1, source_target_pairs={{0,4},{4,0},{8,12},{12,8},{1,5},{5,1},{9,13},{13,9},{2,6},{6,2},{1... | collective-permute-start | bytes 589832 | tf_op jit(solution)/shard_map/ppermute | solution.py:680
  143.4 19.3 %collective-permute-start.23 = (bf16[128,768]{1,0:T(8,128)(2,1)S(1)}, bf16[128,768]{1,0:T(8,128)(2,1)S(1)}, u32[]{:S(2)}, u32[]{:S(2)}) collective-permute-start(bf16[128,768]{1,0:T(8,128)(2,1)S(1)} %collective-permute-done.21.refs_3_), channel_id=1, source_target_pairs={{0,4},{4,0},{8,12},{12,8},{1,5},{5,1},{9,13},{13,9},{2,6},{6,2},{1... | collective-permute-start | bytes 589832 | tf_op jit(solution)/shard_map/ppermute | solution.py:680
  185.2 11.6 %collective-permute-start.30 = (bf16[2,768,128]{2,1,0:T(8,128)(2,1)S(1)}, bf16[2,768,128]{2,1,0:T(8,128)(2,1)S(1)}, u32[]{:S(2)}, u32[]{:S(2)}) collective-permute-start(bf16[2,768,128]{2,1,0:T(8,128)(2,1)S(1)} %slice.82), channel_id=1, source_target_pairs={{0,1},{1,0},{2,3},{3,2},{4,5},{5,4},{6,7},{7,6},{8,9},{9,8},{10,11... | collective-permute-start | bytes 1179656 | tf_op jit(solution)/shard_map/ppermute | solution.py:686
  197.9 6.4 %collective-permute-start.33 = (bf16[256,128]{1,0:T(8,128)(2,1)S(1)}, bf16[256,128]{1,0:T(8,128)(2,1)S(1)}, u32[]{:S(2)}, u32[]{:S(2)}) collective-permute-start(bf16[256,128]{1,0:T(8,128)(2,1)S(1)} %slice_bitcast_fusion.8), channel_id=1, source_target_pairs={{0,2},{1,3},{2,0},{3,1},{4,6},{5,7},{6,4},{7,5},{8,10},{9,11},{10,... | collective-permute-start | bytes 196616 | tf_op jit(solution)/shard_map/ppermute | solution.py:686
  198.0 7.3 %collective-permute-start.31 = (bf16[512,128]{1,0:T(8,128)(2,1)S(1)}, bf16[512,128]{1,0:T(8,128)(2,1)S(1)}, u32[]{:S(2)}, u32[]{:S(2)}) collective-permute-start(bf16[512,128]{1,0:T(8,128)(2,1)S(1)} %get-tuple-element.64), channel_id=1, source_target_pairs={{0,0},{1,4},{2,8},{3,12},{4,1},{5,5},{6,9},{7,13},{8,2},{9,6},{10,... | collective-permute-start | bytes 393224 | tf_op jit(solution)/shard_map/ppermute | solution.py:693
  198.7 16.5 %collective-permute-start.32 = (bf16[512,128]{1,0:T(8,128)(2,1)S(1)}, bf16[512,128]{1,0:T(8,128)(2,1)S(1)}, u32[]{:S(2)}, u32[]{:S(2)}) collective-permute-start(bf16[512,128]{1,0:T(8,128)(2,1)S(1)} %get-tuple-element.65), channel_id=1, source_target_pairs={{0,8},{1,12},{2,0},{3,4},{4,9},{5,13},{6,1},{7,5},{8,10},{9,14},{1... | collective-permute-start | bytes 393224 | tf_op jit(solution)/shard_map/ppermute | solution.py:693

commit v5 on v4

--- a/solution.py
+++ b/solution.py
@@ -393,24 +393,37 @@
     return pl.BlockSpec(array.shape, lambda n, s: (0,) * array.ndim)
 
 
-def target_kernel(counts, idx_ref, *refs):
-    sets, (weight_ref, out_ref, lhs) = split_sets(refs, counts)
+def target_kernel(counts, tiles, idx_ref, *refs):
+    sets, refs = split_sets(refs, counts)
+    weights, terms, (out_ref, lhs) = refs[:tiles], refs[tiles:-2], refs[-2:]
     pl.when(pl.program_id(0) == 0)(lambda: fill_rows(lhs, sets))
-    out_ref[...] = jnp.dot(lhs[...], weight_ref[...], preferred_element_type=F32)
-
-
-def target_part(sets, weight, chip):
-    pieces = [piece for group in sets for piece in group]
-    width = sum(piece.shape[1] for piece in sets[0])
-    rows = sum(group[0].shape[0] for group in sets)
+    weight = jnp.concatenate([ref[...] for ref in weights], axis=0)
+    product = jnp.dot(lhs[...], weight, preferred_element_type=F32)
+    out_ref[...] = sum((ref[...] for ref in terms), product)
+
+
+def target_part(terms, sets, weight, row, width):
+    counts = [1] * len(sets)
+    rows = sum(piece.shape[0] for piece, _ in sets)
     outs = weight.shape[1]
+    tiles = width // BLK
+
+    def piece_spec(piece, first):
+        return pl.BlockSpec((piece.shape[0], width), lambda n, s: (0, first // width))
+
+    pieces = []
+    for piece, first in sets:
+        if first % width:
+            piece, first = lax.slice_in_dim(piece, first, first + width, axis=1), 0
+        pieces.append((piece, first))
     return pl.pallas_call(
-        functools.partial(target_kernel, [len(group) for group in sets]),
+        functools.partial(target_kernel, counts, tiles),
         grid_spec=pltpu.PrefetchScalarGridSpec(
             num_scalar_prefetch=1,
             grid=(outs // BLK,),
-            in_specs=[whole_spec(piece) for piece in pieces]
-            + [pl.BlockSpec((width, BLK), lambda n, s: (s[0], n))],
+            in_specs=[piece_spec(*piece) for piece in pieces]
+            + [pl.BlockSpec((BLK, BLK), lambda n, s, k=k: (s[0] + k, n)) for k in range(tiles)]
+            + [pl.BlockSpec((term.shape[0], BLK), lambda n, s: (0, n)) for term in terms],
             out_specs=pl.BlockSpec((rows, BLK), lambda n, s: (0, n)),
             scratch_shapes=[pltpu.VMEM((rows, width), BF16)],
         ),
@@ -418,7 +431,12 @@
         compiler_params=pltpu.CompilerParams(vmem_limit_bytes=50 * 2**20),
         cost_estimate=SMALL,
         name="target_part",
-    )(jnp.reshape(chip, (1,)).astype(jnp.int32), *pieces, weight)
+    )(
+        jnp.reshape(lax.div(row, BLK), (1,)).astype(jnp.int32),
+        *[piece for piece, _ in pieces],
+        *[weight] * tiles,
+        *terms,
+    )
 
 
 TN = (((0,), (0,)), ((), ()))
@@ -459,7 +477,8 @@
 
 
 def student_kernel(steps, late, tensor_count, idx_ref, *refs):
-    tokens, (right_ref, left_ref, mixed_ref, student_ref, spread) = refs[:-5], refs[-5:]
+    tokens, refs = refs[:-6], refs[-6:]
+    right_ref, left_ref, target_ref, mixed_ref, rest_ref, spread = refs
     step = pl.program_id(0)
     chunk = natural(step, idx_ref[2], steps // 2)
     groups = left_ref.shape[0]
@@ -490,9 +509,11 @@
     @pl.when(step == steps - 1)
     def _():
         for g in range(groups):
-            student_ref[:, g * BLK : (g + 1) * BLK] = lax.dot_general(
+            span = slice(g * BLK, (g + 1) * BLK)
+            student = lax.dot_general(
                 mixed_ref[g], left_ref[g], TN, preferred_element_type=F32
-            ) * (1.0 / tensor_count)
+            )
+            rest_ref[:, span] = student * (1.0 / tensor_count) - target_ref[:, span]
 
 
 def token_specs(half, width, steps, begin, own):
@@ -515,7 +536,7 @@
     return [near] * 4 + [far] * 4
 
 
-def student_part(tokens, late, scalars, right_rows, left_diag, tensor_count):
+def student_part(tokens, late, scalars, right_rows, left_diag, target, tensor_count):
     per_owner, pairs, size = right_rows.shape[1:]
     blocks = right_rows.shape[0] * per_owner
     steps = blocks // WIDE
@@ -536,6 +557,7 @@
             + [
                 pl.BlockSpec((1, WIDE, pairs, size), right_block),
                 whole_spec(left_diag),
+                pl.BlockSpec((4 * half, groups * BLK), lambda n, s: (int(late), 0)),
             ],
             out_specs=[
                 pl.BlockSpec((groups, BLK, 4 * half), lambda n, s: (0, 0, 0)),
@@ -552,14 +574,14 @@
             flops=10**10, bytes_accessed=10**7, transcendentals=0
         ),
         name="student_part",
-    )(scalars, *tokens, right_rows, left_diag)
+    )(scalars, *tokens, right_rows, left_diag, target)
 
 
 def grads_kernel(groups, steps, scale, counts, idx_ref, *refs):
     sets, refs = split_sets(refs, counts)
-    weight_ref, total_ref, student0, student1, mixed0, mixed1, left_ref = refs[:7]
-    own, near, far = refs[7:11], refs[11:15], refs[15:19]
-    out_ref, lhs, back, wide = refs[19:]
+    weight_ref, rest0, rest1, mixed0, mixed1, left_ref = refs[:6]
+    own, near, far = refs[6:10], refs[10:14], refs[14:18]
+    out_ref, lhs, back, wide = refs[18:]
     step = pl.program_id(0)
     z = idx_ref[3]
     parts, size = out_ref.shape[0], out_ref.shape[2]
@@ -577,11 +599,9 @@
 
     @pl.when(step < groups)
     def _():
-        target = total_ref[...] + jnp.dot(
-            lhs[...], weight_ref[...], preferred_element_type=F32
-        )
-        student = jnp.concatenate([student0[...], student1[...]], axis=0)
-        out_grad = ((student - target) * scale).astype(BF16)
+        target = jnp.dot(lhs[...], weight_ref[...], preferred_element_type=F32)
+        rest = jnp.concatenate([rest0[...], rest1[...]], axis=0)
+        out_grad = ((rest - target) * scale).astype(BF16)
         mixed = jnp.concatenate([mixed0[0], mixed1[0]], axis=1)
         left = jnp.dot(mixed, out_grad, preferred_element_type=F32)
         value = lax.dot_general(
@@ -626,10 +646,10 @@
 
 
 def factor_grads(
-    sets, weight, total, students, mixed, left_diag, own, late, scalars, parts, size, scale
+    sets, weight, rest, mixed, left_diag, own, late, scalars, parts, size, scale
 ):
     pieces = [piece for group in sets for piece in group]
-    groups, count = left_diag.shape[0], total.shape[0]
+    groups, count = left_diag.shape[0], 2 * rest[0].shape[0]
     width = weight.shape[0] // 2
     half = late[0].shape[0]
     steps = own[0].shape[1] // (WIDE * size)
@@ -647,7 +667,6 @@
             grid=(groups + steps,),
             in_specs=[whole_spec(piece) for piece in pieces]
             + [pl.BlockSpec((width, BLK), lambda n, s: (1 - s[2], group(n)))]
-            + [pl.BlockSpec((count, BLK), lambda n, s: (0, group(n)))]
             + [pl.BlockSpec((count // 2, BLK), lambda n, s: (0, group(n)))] * 2
             + [pl.BlockSpec((1, BLK, count // 2), lambda n, s: (group(n), 0, 0))] * 2
             + [pl.BlockSpec((1, BLK, BLK), lambda n, s: (group(n), 0, 0))]
@@ -664,7 +683,7 @@
         compiler_params=pltpu.CompilerParams(vmem_limit_bytes=50 * 2**20),
         cost_estimate=SMALL,
         name="factor_grads",
-    )(scalars, *pieces, weight, total, *students, *mixed, left_diag, *own, *late)
+    )(scalars, *pieces, weight, *rest, *mixed, left_diag, *own, *late)
 
 
 def tiled_body(tokens, gate_weight, up_weight, down_weight, right_factor, left_factor):
@@ -719,21 +738,8 @@
         own_pieces, scalars(other_block), gate_weight, up_weight, 0, part
     )
     early = mine
-    sums = add(mine[0], swap(other[0])).astype(BF16)
+    sums = add(mine[0], swap(after(other[0], arrived))).astype(BF16)
     got_early = across(sums)
-
-    right_rows = turn(after(right_factor, first), 0)[None]
-    left_rows = along(after(left_factor, first), 1)[None]
-    left_rows = jnp.concatenate([left_factor[None], left_rows], axis=0)
-    right_rows = double(double(after(right_rows, early), 1), 2)
-    left_rows = double(after(left_rows, early), 2)
-    for axis, bit in ((0, 2), (1, 1)):
-        split = left_rows.reshape((2, 2) + left_rows.shape[1:])
-        split = jnp.where(lax.rem(lax.div(z, bit), 2) == 1, jnp.flip(split, axis), split)
-        left_rows = split.reshape(left_rows.shape)
-    pairs, blocks = left_rows.shape[1], left_rows.shape[3]
-    left_rows = left_rows.transpose(1, 3, 0, 2).reshape(pairs, blocks, blocks)
-    left_diag = spread_left(after(left_rows, early))
 
     arrived = after(arrived, early)
     partner = along(arrived, 1)
@@ -741,25 +747,41 @@
     late_first = across(after(rest, sums))
     order = jnp.concatenate([base, jnp.stack([chip, z])]).astype(jnp.int32)
     own = [tokens, tokens, near_tokens, near_tokens]
-    mixed0, student0 = student_part(
-        [after(tokens, sums)] + own[1:], False, order, right_rows, left_diag, tensor_count
-    )
-    partner = after(partner, mixed0)
     late = [arrived, partner, near_arrived, swap(partner)]
     late_pieces = [(t, None, 3) for t in late]
 
+    pairs, blocks = left_factor.shape[0], left_factor.shape[2]
+    right_rows = turn(after(right_factor, sums), 0)[None]
+    left_own = left_factor.reshape(1, -1, LANES)
+    left_rows = double(after(left_own, sums), 1)
+
+    late_order = after(scalars(other_block), sums, right_rows, left_rows)
+    value0, other0 = products(late_pieces, late_order, gate_weight, up_weight, *chunks[0])
+    near0 = swap(after(other0[0], got_early))
+    late_order = after(late_order, value0)
+    value1, other1 = products(late_pieces, late_order, gate_weight, up_weight, *chunks[1])
+    near1 = swap(other1[0])
+    sums0 = add(value0[0], after(near0, value1)).astype(BF16)
+    got0 = across(sums0)
+    mine_order = after(scalars(mine_block), value1, sums0)
+    right_rows, left_rows = after(right_rows, value1), after(left_rows, value1)
+    more_right, more_left = along(right_rows, 1), along(left_rows, 2)
     kept, other = products(
-        own_pieces + late_pieces,
-        after(scalars(mine_block), mixed0, sums),
-        gate_weight,
-        up_weight,
-        0,
-        part,
-    )
-    kept_other = swap(after(other, got_early, late_first))
-    late_order = after(scalars(other_block), kept)
-    value0, other0 = products(late_pieces, late_order, gate_weight, up_weight, *chunks[0])
-    near0 = swap(other0[0])
+        own_pieces + late_pieces, mine_order, gate_weight, up_weight, 0, part
+    )
+    kept_other = swap(after(other, got0, late_first, near1, more_right, more_left))
+    right_rows = jnp.concatenate([right_rows, after(more_right, kept)], axis=0)
+    left_rows = jnp.concatenate([left_rows, after(more_left, kept)], axis=0)
+    right_rows = double(right_rows, 2)
+    sums1 = add(value1[0], after(near1, kept)).astype(BF16)
+    got1 = across(sums1)
+
+    left_rows = left_rows.reshape((tensor_count,) + left_factor.shape)
+    for axis, bit in ((0, 2), (1, 1)):
+        split = left_rows.reshape((2, 2) + left_rows.shape[1:])
+        split = jnp.where(lax.rem(lax.div(z, bit), 2) == 1, jnp.flip(split, axis), split)
+        left_rows = split.reshape(left_rows.shape)
+    left_rows = left_rows.transpose(1, 3, 0, 2).reshape(pairs, blocks, blocks)
 
     def activate(u, span, term):
         begin, width = span
@@ -767,34 +789,48 @@
         total = add(*terms, term)
         return (jax.nn.silu(total[0]) * total[1]).astype(BF16)
 
-    hidden_late = activate(1, (0, part), after(got_early, value0))
+    hidden_late = activate(1, (0, part), got_early)
     got_late = across(hidden_late)
-    late_order = after(late_order, value0, hidden_late)
-    value1, other1 = products(late_pieces, late_order, gate_weight, up_weight, *chunks[1])
-    got0 = across(add(value0[0], after(near0, value1)).astype(BF16))
-    near1 = swap(after(other1[0], got_late))
-    got1 = across(add(value1[0], near1).astype(BF16))
-
     near_hidden_late = swap(hidden_late)
-    late_first = after(late_first, value1)
-    late_partner = along(late_first, 1)
+    hidden0 = activate(0, chunks[0], after(got0, hidden_late))
+    got_hidden0 = across(hidden0)
+    left_diag = spread_left(after(left_rows, hidden0))
+    late_partner = along(after(late_first, kept), 1)
+
+    def target(term, span, value):
+        sets = [(value, 0), (swap(value), 0)]
+        sets += [(hidden_late, span[0]), (near_hidden_late, span[0])]
+        return target_part(term, sets, down_weight, chip * part + span[0], span[1])
+
+    total = target([], chunks[0], after(hidden0, sums1))
+    hidden1 = activate(0, chunks[1], after(got1, total, got_late))
+    got_hidden1 = across(hidden1)
+    total = target([total], chunks[1], hidden1)
+    got_late, got_hidden0 = after(got_late, total), after(got_hidden0, total)
+    late_partner = after(late_partner, total)
     late_rest = [late_first, late_partner, swap(late_first), swap(late_partner)]
-    mixed1, student1 = student_part(
-        late + late_rest, True, order, right_rows, left_diag, tensor_count
-    )
     near_got_late = swap(got_late)
-    hidden = [activate(0, span, term) for span, term in zip(chunks, (got0, got1))]
-    got_hidden = [across(value) for value in hidden]
-    sets = [hidden, [swap(value) for value in hidden], [hidden_late], [near_hidden_late]]
-    total = target_part(sets, down_weight, chip)
-    near_hidden = [swap(value) for value in got_hidden]
-    sets = [[got_late], [near_got_late], got_hidden, near_hidden]
+    near_got0 = swap(got_hidden0)
+    mixed0, rest0 = student_part(
+        own, False, order, right_rows, left_diag, total, tensor_count
+    )
+    got_hidden1 = after(got_hidden1, mixed0)
+    mixed1, rest1 = student_part(
+        late + [after(late_rest[0], mixed0)] + late_rest[1:],
+        True,
+        order,
+        right_rows,
+        left_diag,
+        total,
+        tensor_count,
+    )
+    got_hidden = [got_hidden0, got_hidden1]
+    sets = [[got_late], [near_got_late], got_hidden, [near_got0, swap(got_hidden1)]]
 
     grads = factor_grads(
         sets,
         down_weight,
-        total,
-        (student0, student1),
+        (rest0, rest1),
         (mixed0, mixed1),
         left_diag,
         own,

time: 218 us -> 206 us (0.945)
  waiting for transfers between devices: 72.8 us -> 42.6 us
  Pallas kernels: 90.1 us -> 98.4 us
  local copies, waits for them, and re-layouts: 7.23 us -> 10.8 us
  starting transfers between devices: 33.9 us -> 37 us
  other arithmetic: 10.9 us -> 13.8 us
    ppermute x8, waiting for transfers between devices: 35.4 us -> 6.34 us  [across(): return lax.ppermute(value, 'fsdp', [(i, i ^ 2) for i in range(fsdp_count)])]
    pallas_call x1 -> x2, Pallas kernels: 9.74 us -> 17.3 us  [target_part(): pl.pallas_call(functools.partial(target_kernel, counts, tiles), grid_spec...]
    ppermute x8, starting transfers between devices: 8.21 us -> 14.2 us  [along(): lax.ppermute(value, 'tensor', [(i, i ^ bit) for i in range(tensor_count)])]
    ppermute x3, starting transfers between devices: 8.47 us -> 4.81 us  [turn(): return lax.ppermute(value, both_axes, perm)]
    add x5, other arithmetic: 2.58 us -> 5.62 us  [add(): return sum((term.astype(F32) for term in terms))]
    unnamed x24 -> x33, local copies, waits for them, and re-layouts: 3.04 us -> 4.73 us
  transfers between devices with their start and end apart: 34 -> 34, of which waited for: 12 -> 10; matrix products, arithmetic and copies ran while one was open for 6% -> 9% of each run, Pallas kernels for 32% -> 38%
where the time goes in v5:
time: 206 us; the launch traced here: 204 us
  Pallas kernels  98.4 us (48%)
  waiting for transfers between devices  42.6 us (21%)
  starting transfers between devices  37 us (18%)
  other arithmetic  13.8 us (7%)
  local copies, waits for them, and re-layouts  10.8 us (5%)
    pallas_call x4, Pallas kernels, products(): pl.pallas_call(functools.partial(products_kernel, sets), grid_spec=pltpu....  34.8 us
    ppermute x8, waiting for transfers between devices, along(): lax.ppermute(value, 'tensor', [(i, i ^ bit) for i in range(tensor_count)])  24 us
    pallas_call x1, Pallas kernels, factor_grads(): pl.pallas_call(functools.partial(grads_kernel, groups, steps, scale, [len...  20.8 us
    pallas_call x2, Pallas kernels, student_part(): pl.pallas_call(functools.partial(student_kernel, steps, late, tensor_coun...  20.3 us
    pallas_call x2, Pallas kernels, target_part(): pl.pallas_call(functools.partial(target_kernel, counts, tiles), grid_spec...  17.3 us
    ppermute x8, starting transfers between devices, across(): return lax.ppermute(value, 'fsdp', [(i, i ^ 2) for i in range(fsdp_count)])  14.5 us
    ppermute x8, starting transfers between devices, along(): lax.ppermute(value, 'tensor', [(i, i ^ bit) for i in range(tensor_count)])  14.2 us
    ppermute x3, waiting for transfers between devices, turn(): return lax.ppermute(value, both_axes, perm)  11.1 us
  transfers between devices with their start and end apart: 34, of which 10 were waited for; matrix products, arithmetic and copies ran while one was open for 9% of the time, Pallas kernels for 38%

profile of v5, /device:TPU:0, one launch (start us, length us, event | category | flops | bytes accessed | tf_op | source)
XLA Modules:
  0.0 203.8 jit_solution(2467482107125541079)
XLA Ops:
  0.6 0.5 collective-permute-start
  1.1 0.6 pad_add_fusion.1.idx_ref
  1.8 3.0 %cut_tokens.1 = (bf16[64,4096]{1,0:T(8,128)(2,1)}, bf16[64,4096]{1,0:T(8,128)(2,1)}) custom-call(s32[3]{0:T(128)} %pad_add_fusion.1.idx_ref, bf16[128,8192]{1,0:T(8,128)(2,1)} %refs_13_.1, bf16[128,8192]{1,0:T(8,128)(2,1)} %refs_13_.1), custom_call_target="tpu_custom_call" | custom-call | flops 1 | bytes 1 | tf_op jit(solution)/shard_map/cut_tokens/pallas_call | solution.py:314
  4.8 2.5 %collective-permute-start.1 = (bf16[64,4096]{1,0:T(8,128)(2,1)}, bf16[64,4096]{1,0:T(8,128)(2,1)S(1)}, u32[]{:S(2)}, u32[]{:S(2)}) collective-permute-start(bf16[64,4096]{1,0:T(8,128)(2,1)} %get-tuple-element.44), channel_id=1, source_target_pairs={{0,8},{4,12},{8,0},{12,4},{1,9},{5,13},{9,1},{13,5},{2,10},{6,14},... | collective-permute-start | bytes 1572872 | tf_op jit(solution)/shard_map/ppermute | solution.py:702
  7.4 10.1 %gate_up_products.4 = (bf16[1,2,128,1792]{3,2,1,0:T(8,128)(2,1)S(1)}, bf16[1,2,128,1792]{3,2,1,0:T(8,128)(2,1)S(1)}) custom-call(s32[5]{0:T(128)S(1)} %concatenate.29.idx_ref, bf16[128,8192]{1,0:T(8,128)(2,1)S(1)} %copy-done, bf16[128,8192]{1,0:T(8,128)(2,1)S(1)} %copy-done, bf16[128,8192]{1,0:T(8,128)(2,1)} %collective-permute-done.refs_2_.refs_3_.refs_14_.refs_15_, ...), custom_call_target="tpu_custom_call" | custom-call | flops 1 | bytes 1 | tf_op jit(solution)/shard_map/gate_up_products/pallas_call | solution.py:357
  17.6 2.5 %collective-permute-done.1.refs_0_.refs_4_.refs_16_ = bf16[64,4096]{1,0:T(8,128)(2,1)S(1)} collective-permute-done((bf16[64,4096]{1,0:T(8,128)(2,1)}, bf16[64,4096]{1,0:T(8,128)(2,1)S(1)}, u32[]{:S(2)}, u32[]{:S(2)}) %collective-permute-start.1) | collective-permute-done | bytes 524320 | tf_op jit(solution)/shard_map/ppermute | solution.py:702
  20.1 1.8 collective-permute-start.5
  21.9 0.6 collective-permute-done.2
  22.6 1.2 fusion
  23.8 1.7 collective-permute-start.8
  25.5 9.0 %collective-permute-done.5.refs_1_.refs_5_.refs_17_ = bf16[64,4096]{1,0:T(8,128)(2,1)S(1)} collective-permute-done((bf16[64,4096]{1,0:T(8,128)(2,1)S(1)}, bf16[64,4096]{1,0:T(8,128)(2,1)S(1)}, u32[]{:S(2)}, u32[]{:S(2)}) %collective-permute-start.5) | collective-permute-done | bytes 524320 | tf_op jit(solution)/shard_map/ppermute | solution.py:705
  34.6 1.8 collective-permute-start.4
  36.4 0.7 collective-permute-start.3
  37.1 0.6 constant_dynamic-update-slice_fusion.1
  37.7 1.5 collective-permute-done.4
  39.2 0.6 constant_dynamic-update-slice_fusion
  39.9 6.2 %gate_up_products.5 = (bf16[1,2,128,1024]{3,2,1,0:T(8,128)(2,1)S(1)}, bf16[1,2,128,1024]{3,2,1,0:T(8,128)(2,1)S(1)}) custom-call(s32[5]{0:T(128)S(1)} %concatenate.29.idx_ref, bf16[64,4096]{1,0:T(8,128)(2,1)S(1)} %collective-permute-done.1.refs_0_.refs_4_.refs_16_, bf16[64,4096]{1,0:T(8,128)(2,1)S(1)} %collective-permute-done.5.refs_1_.refs_5_.refs_17_, ...), custom_call_target="tpu_custom_call" | custom-call | flops 1 | bytes 1 | tf_op jit(solution)/shard_map/gate_up_products/pallas_call | solution.py:357
  46.0 2.5 %collective-permute-done.8 = bf16[2,128,1792]{2,1,0:T(8,128)(2,1)} collective-permute-done((bf16[2,128,1792]{2,1,0:T(8,128)(2,1)}, bf16[2,128,1792]{2,1,0:T(8,128)(2,1)}, u32[]{:S(2)}, u32[]{:S(2)}) %collective-permute-start.8) | collective-permute-done | bytes 917536 | tf_op jit(solution)/shard_map/ppermute | solution.py:702
  48.6 1.1 collective-permute-start.9
  49.6 6.1 %collective-permute-start.11 = (bf16[64,4096]{1,0:T(8,128)(2,1)}, bf16[64,4096]{1,0:T(8,128)(2,1)}, u32[]{:S(2)}, u32[]{:S(2)}) collective-permute-start(bf16[64,4096]{1,0:T(8,128)(2,1)} %get-tuple-element.60), channel_id=1, source_target_pairs={{0,8},{4,12},{8,0},{12,4},{1,9},{5,13},{9,1},{13,5},{2,10},{6,14},... | collective-permute-start | bytes 1572872 | tf_op jit(solution)/shard_map/ppermute | solution.py:702
  55.7 5.2 %gate_up_products.6 = (bf16[1,2,128,768]{3,2,1,0:T(8,128)(2,1)S(1)}, bf16[1,2,128,768]{3,2,1,0:T(8,128)(2,1)S(1)}) custom-call(s32[5]{0:T(128)S(1)} %concatenate.29.idx_ref, bf16[64,4096]{1,0:T(8,128)(2,1)S(1)} %collective-permute-done.1.refs_0_.refs_4_.refs_16_, bf16[64,4096]{1,0:T(8,128)(2,1)S(1)} %collective-permute-done.5.refs_1_.refs_5_.refs_17_, ...), custom_call_target="tpu_custom_call" | custom-call | flops 1 | bytes 1 | tf_op jit(solution)/shard_map/gate_up_products/pallas_call | solution.py:357
  60.9 1.0 fusion.1
  62.1 2.5 %collective-permute-start.14 = (bf16[2,256,128]{2,1,0:T(8,128)(2,1)}, bf16[2,256,128]{2,1,0:T(8,128)(2,1)S(1)}, u32[]{:S(2)}, u32[]{:S(2)}) collective-permute-start(bf16[2,256,128]{2,1,0:T(8,128)(2,1)} %constant_dynamic-update-slice_fusion), channel_id=1, source_target_pairs={{0,2},{1,3},{2,0},{3,1},{4,6},{5,7},{6,4},{7,5},{8,10},{9,11},{10,... | collective-permute-start | bytes 393224 | tf_op jit(solution)/shard_map/ppermute | solution.py:705
  64.5 0.8 collective-permute-start.13
  65.4 13.2 %gate_up_products.7 = (bf16[2,2,128,1792]{3,2,1,0:T(8,128)(2,1)S(1)}, bf16[2,2,128,1792]{3,2,1,0:T(8,128)(2,1)}) custom-call(s32[5]{0:T(128)S(1)} %concatenate.28.idx_ref, bf16[128,8192]{1,0:T(8,128)(2,1)} %refs_13_.1, bf16[128,8192]{1,0:T(8,128)(2,1)} %refs_13_.1, bf16[128,8192]{1,0:T(8,128)(2,1)} %collective-permute-done.refs_2_.refs_3_.refs_14_.refs_15_, ...), custom_call_target="tpu_custom_call" | custom-call | flops 1 | bytes 1 | tf_op jit(solution)/shard_map/gate_up_products/pallas_call | solution.py:357
  78.6 1.3 copy-done.2
  80.2 0.7 constant_dynamic-update-slice_fusion.4
  81.3 1.8 fusion.4
  83.1 1.5 collective-permute-start.17
  84.6 0.9 pad_maximum_fusion.1
  85.9 2.0 bitcast_add_fusion
  88.3 0.6 collective-permute-start.16
  88.9 0.5 copy-done.3
  89.4 1.4 bitcast_add_fusion.1
  91.2 0.9 copy.13
  92.1 0.5 collective-permute-done.18.refs_1_
  92.6 0.7 collective-permute-start.27
  93.4 1.4 collective-permute-start.24
  94.7 8.2 %target_part.2.refs_7_ = f32[512,2048]{1,0:T(8,128)} custom-call(s32[1]{0:T(128)} %bitcast.21.idx_ref, bf16[128,1024]{1,0:T(8,128)(2,1)S(1)} %fusion.6.refs_0_, bf16[128,1024]{1,0:T(8,128)(2,1)S(1)} %collective-permute-done.18.refs_1_, bf16[128,1792]{1,0:T(8,128)(2,1)S(1)} %fusion.3.refs_2_, bf16[128,1792]{1,0:T(8,128)(2,1)S(1)} %collective-permute-done.19.refs_3_, ...), custom_call_target="tpu_custom_call" | custom-call | flops 1 | bytes 1 | tf_op jit(solution)/shard_map/target_part/pallas_call | solution.py:419
  103.0 1.3 collective-permute-done.16.refs_0_
  104.2 1.4 bitcast_add_fusion.2
  105.7 0.8 fusion.8.refs_0_
  106.5 4.2 %collective-permute-done.24 = bf16[2,16,32,128]{3,2,1,0:T(8,128)(2,1)S(1)} collective-permute-done((bf16[2,16,32,128]{3,2,1,0:T(8,128)(2,1)S(1)}, bf16[2,16,32,128]{3,2,1,0:T(8,128)(2,1)S(1)}, u32[]{:S(2)}, u32[]{:S(2)}) %collective-permute-start.24) | collective-permute-done | bytes 262176 | tf_op jit(solution)/shard_map/ppermute | solution.py:705
  110.8 0.8 copy-done.8
  111.6 2.1 %copy.14.left_ref = bf16[32,64,64]{2,1,0:T(8,128)(2,1)} copy(bf16[32,64,64]{1,2,0:T(8,128)(2,1)} %bitcast.81) | data formatting | bytes 524288 | tf_op jit(solution)/shard_map/optimization_barrier | solution.py:715
  113.6 1.0 collective-permute-start.22
  114.7 2.2 %spread_left.1.refs_5_.refs_9_.refs_11_ = bf16[8,256,256]{2,1,0:T(8,128)(2,1)} custom-call(bf16[32,64,64]{2,1,0:T(8,128)(2,1)} %copy.14.left_ref), custom_call_target="tpu_custom_call" | custom-call | flops 1 | bytes 1 | tf_op jit(solution)/shard_map/spread_left/pallas_call | solution.py:470
  116.9 1.0 collective-permute-start.23
  117.9 9.1 %target_part.3.refs_6_.refs_10_ = f32[512,2048]{1,0:T(8,128)} custom-call(s32[1]{0:T(128)} %bitcast.18.idx_ref, bf16[128,768]{1,0:T(8,128)(2,1)} %fusion.8.refs_0_, bf16[128,768]{1,0:T(8,128)(2,1)} %collective-permute-done.20.refs_1_, bf16[128,768]{1,0:T(8,128)(2,1)S(1)} %slice.89.refs_2_, bf16[128,768]{1,0:T(8,128)(2,1)S(1)} %slice.90.refs_3_, ...), custom_call_target="tpu_custom_call" | custom-call | flops 1 | bytes 1 | tf_op jit(solution)/shard_map/target_part/pallas_call | solution.py:419
  127.1 9.6 %student_part.2 = (bf16[8,256,256]{2,1,0:T(8,128)(2,1)S(1)}, f32[256,2048]{1,0:T(8,128)}) custom-call(s32[4]{0:T(128)S(1)} %pad_add_fusion.idx_ref, bf16[128,8192]{1,0:T(8,128)(2,1)} %refs_13_.1, bf16[128,8192]{1,0:T(8,128)(2,1)} %refs_13_.1, bf16[128,8192]{1,0:T(8,128)(2,1)} %collective-permute-done.refs_2_.refs_3_.refs_14_.refs_15_, ...), custom_call_target="tpu_custom_call" | custom-call | flops 10000000000 | bytes 10000000 | tf_op jit(solution)/shard_map/student_part/pallas_call | solution.py:551
  136.7 0.6 collective-permute-start.26
  137.8 0.8 copy-done.10
  138.6 10.7 %student_part.3 = (bf16[8,256,256]{2,1,0:T(8,128)(2,1)}, f32[256,2048]{1,0:T(8,128)}) custom-call(s32[4]{0:T(128)S(1)} %pad_add_fusion.idx_ref, bf16[64,4096]{1,0:T(8,128)(2,1)S(1)} %collective-permute-done.1.refs_0_.refs_4_.refs_16_, bf16[64,4096]{1,0:T(8,128)(2,1)S(1)} %collective-permute-done.5.refs_1_.refs_5_.refs_17_, ...), custom_call_target="tpu_custom_call" | custom-call | flops 10000000000 | bytes 10000000 | tf_op jit(solution)/shard_map/student_part/pallas_call | solution.py:551
  149.3 20.8 %factor_grads.1 = bf16[4,768,128]{2,1,0:T(8,128)(2,1)} custom-call(s32[4]{0:T(128)S(1)} %pad_add_fusion.idx_ref, bf16[128,1792]{1,0:T(8,128)(2,1)S(1)} %copy-done.6, bf16[128,1792]{1,0:T(8,128)(2,1)S(1)} %collective-permute-done.21.refs_1_, bf16[128,1024]{1,0:T(8,128)(2,1)} %collective-permute-done.22.refs_2_, ...), custom_call_target="tpu_custom_call" | custom-call | flops 1 | bytes 1 | tf_op jit(solution)/shard_map/factor_grads/pallas_call | solution.py:663
  170.1 1.0 slice.92
  171.1 3.0 %collective-permute-start.30 = (bf16[2,768,128]{2,1,0:T(8,128)(2,1)S(1)}, bf16[2,768,128]{2,1,0:T(8,128)(2,1)S(1)}, u32[]{:S(2)}, u32[]{:S(2)}) collective-permute-start(bf16[2,768,128]{2,1,0:T(8,128)(2,1)S(1)} %slice.92), channel_id=1, source_target_pairs={{0,1},{1,0},{2,3},{3,2},{4,5},{5,4},{6,7},{7,6},{8,9},{9,8},{10,11... | collective-permute-start | bytes 1179656 | tf_op jit(solution)/shard_map/ppermute | solution.py:705
  174.1 9.4 %collective-permute-done.30 = bf16[2,768,128]{2,1,0:T(8,128)(2,1)S(1)} collective-permute-done((bf16[2,768,128]{2,1,0:T(8,128)(2,1)S(1)}, bf16[2,768,128]{2,1,0:T(8,128)(2,1)S(1)}, u32[]{:S(2)}, u32[]{:S(2)}) %collective-permute-start.30) | collective-permute-done | bytes 393248 | tf_op jit(solution)/shard_map/ppermute | solution.py:705
  183.5 1.1 add_convert_fusion
  184.6 2.3 %collective-permute-start.33 = (bf16[256,128]{1,0:T(8,128)(2,1)S(1)}, bf16[256,128]{1,0:T(8,128)(2,1)S(1)}, u32[]{:S(2)}, u32[]{:S(2)}) collective-permute-start(bf16[256,128]{1,0:T(8,128)(2,1)S(1)} %slice_bitcast_fusion.8), channel_id=1, source_target_pairs={{0,2},{1,3},{2,0},{3,1},{4,6},{5,7},{6,4},{7,5},{8,10},{9,11},{10,... | collective-permute-start | bytes 196616 | tf_op jit(solution)/shard_map/ppermute | solution.py:705
  186.9 0.7 collective-permute-start.31
  187.6 3.5 %collective-permute-start.32 = (bf16[512,128]{1,0:T(8,128)(2,1)S(1)}, bf16[512,128]{1,0:T(8,128)(2,1)S(1)}, u32[]{:S(2)}, u32[]{:S(2)}) collective-permute-start(bf16[512,128]{1,0:T(8,128)(2,1)S(1)} %get-tuple-element.83), channel_id=1, source_target_pairs={{0,8},{1,12},{2,0},{3,4},{4,9},{5,13},{6,1},{7,5},{8,10},{9,14},{1... | collective-permute-start | bytes 393224 | tf_op jit(solution)/shard_map/ppermute | solution.py:712
  191.3 0.7 copy.15
  192.0 11.1 %collective-permute-done.32 = bf16[512,128]{1,0:T(8,128)(2,1)S(1)} collective-permute-done((bf16[512,128]{1,0:T(8,128)(2,1)S(1)}, bf16[512,128]{1,0:T(8,128)(2,1)S(1)}, u32[]{:S(2)}, u32[]{:S(2)}) %collective-permute-start.32) | collective-permute-done | bytes 131104 | tf_op jit(solution)/shard_map/ppermute | solution.py:712
  203.0 0.7 convert_add_fusion.3
  (81 shorter events, 3.1 us)
Async XLA Ops:
  0.6 6.8 %collective-permute-start = (bf16[128,8192]{1,0:T(8,128)(2,1)}, bf16[128,8192]{1,0:T(8,128)(2,1)}, u32[]{:S(2)}, u32[]{:S(2)}) collective-permute-start(bf16[128,8192]{1,0:T(8,128)(2,1)} %refs_13_.1), channel_id=1, source_target_pairs={{0,4},{4,0},{8,12},{12,8},{1,5},{5,1},{9,13},{13,9},{2,6},{6,2},{1... | collective-permute-start | bytes 6291464 | tf_op jit(solution)/shard_map/ppermute | solution.py:699
  1.8 5.6 %copy-start = (bf16[128,8192]{1,0:T(8,128)(2,1)S(1)}, bf16[128,8192]{1,0:T(8,128)(2,1)}, u32[]{:S(2)}) copy-start(bf16[128,8192]{1,0:T(8,128)(2,1)} %refs_13_.1) | copy-start | bytes 6291460
  4.8 15.3 %collective-permute-start.1 = (bf16[64,4096]{1,0:T(8,128)(2,1)}, bf16[64,4096]{1,0:T(8,128)(2,1)S(1)}, u32[]{:S(2)}, u32[]{:S(2)}) collective-permute-start(bf16[64,4096]{1,0:T(8,128)(2,1)} %get-tuple-element.44), channel_id=1, source_target_pairs={{0,8},{4,12},{8,0},{12,4},{1,9},{5,13},{9,1},{13,5},{2,10},{6,14},... | collective-permute-start | bytes 1572872 | tf_op jit(solution)/shard_map/ppermute | solution.py:702
  17.5 17.0 %copy-start.13 = (bf16[32,16,64]{2,1,0:T(8,128)(2,1)S(1)}, bf16[32,16,64]{2,1,0:T(8,128)(2,1)}, u32[]{:S(2)}) copy-start(bf16[32,16,64]{2,1,0:T(8,128)(2,1)} %param.11) | copy-start | bytes 196612
  17.5 18.9 %copy-start.14 = (bf16[16,32,128]{2,1,0:T(8,128)(2,1)S(1)}, bf16[16,32,128]{2,1,0:T(8,128)(2,1)}, u32[]{:S(2)}) copy-start(bf16[16,32,128]{2,1,0:T(8,128)(2,1)} %param.10) | copy-start | bytes 393220
  20.1 2.5 %collective-permute-start.2 = (bf16[2,128,1792]{2,1,0:T(8,128)(2,1)S(1)}, bf16[2,128,1792]{2,1,0:T(8,128)(2,1)S(1)}, u32[]{:S(2)}, u32[]{:S(2)}) collective-permute-start(bf16[2,128,1792]{2,1,0:T(8,128)(2,1)S(1)} %bitcast.78), channel_id=1, source_target_pairs={{0,4},{4,0},{8,12},{12,8},{1,5},{5,1},{9,13},{13,9},{2,6},{6,2},{1... | collective-permute-start | bytes 2752520 | tf_op jit(solution)/shard_map/ppermute | solution.py:699
  20.1 14.4 %collective-permute-start.5 = (bf16[64,4096]{1,0:T(8,128)(2,1)S(1)}, bf16[64,4096]{1,0:T(8,128)(2,1)S(1)}, u32[]{:S(2)}, u32[]{:S(2)}) collective-permute-start(bf16[64,4096]{1,0:T(8,128)(2,1)S(1)} %collective-permute-done.1.refs_0_.refs_4_.refs_16_), channel_id=1, source_target_pairs={{0,1},{1,0},{2,3},{3,2},{4,5},{5,4},{6,7},{7,6},{8,9},{9,8},{10,11... | collective-permute-start | bytes 1572872 | tf_op jit(solution)/shard_map/ppermute | solution.py:705
  23.8 24.8 %collective-permute-start.8 = (bf16[2,128,1792]{2,1,0:T(8,128)(2,1)}, bf16[2,128,1792]{2,1,0:T(8,128)(2,1)}, u32[]{:S(2)}, u32[]{:S(2)}) collective-permute-start(bf16[2,128,1792]{2,1,0:T(8,128)(2,1)} %fusion), channel_id=1, source_target_pairs={{0,8},{4,12},{8,0},{12,4},{1,9},{5,13},{9,1},{13,5},{2,10},{6,14},... | collective-permute-start | bytes 2752520 | tf_op jit(solution)/shard_map/ppermute | solution.py:702
  25.5 14.3 %collective-permute-start.6 = (bf16[64,4096]{1,0:T(8,128)(2,1)S(1)}, bf16[64,4096]{1,0:T(8,128)(2,1)S(1)}, u32[]{:S(2)}, u32[]{:S(2)}) collective-permute-start(bf16[64,4096]{1,0:T(8,128)(2,1)S(1)} %collective-permute-done.1.refs_0_.refs_4_.refs_16_), channel_id=1, source_target_pairs={{0,4},{4,0},{8,12},{12,8},{1,5},{5,1},{9,13},{13,9},{2,6},{6,2},{1... | collective-permute-start | bytes 1572872 | tf_op jit(solution)/shard_map/ppermute | solution.py:699
  34.5 5.3 %collective-permute-start.7 = (bf16[64,4096]{1,0:T(8,128)(2,1)S(1)}, bf16[64,4096]{1,0:T(8,128)(2,1)S(1)}, u32[]{:S(2)}, u32[]{:S(2)}) collective-permute-start(bf16[64,4096]{1,0:T(8,128)(2,1)S(1)} %collective-permute-done.5.refs_1_.refs_5_.refs_17_), channel_id=1, source_target_pairs={{0,4},{4,0},{8,12},{12,8},{1,5},{5,1},{9,13},{13,9},{2,6},{6,2},{1... | collective-permute-start | bytes 1572872 | tf_op jit(solution)/shard_map/ppermute | solution.py:699
  34.6 4.6 %collective-permute-start.4 = (bf16[1,256,128]{2,1,0:T(8,128)(2,1)S(1)}, bf16[1,256,128]{2,1,0:T(8,128)(2,1)S(1)}, u32[]{:S(2)}, u32[]{:S(2)}) collective-permute-start(bf16[1,256,128]{2,1,0:T(8,128)(2,1)S(1)} %reshape.45), channel_id=1, source_target_pairs={{0,1},{1,0},{2,3},{3,2},{4,5},{5,4},{6,7},{7,6},{8,9},{9,8},{10,11... | collective-permute-start | bytes 196616 | tf_op jit(solution)/shard_map/ppermute | solution.py:705
  36.4 3.4 %collective-permute-start.3 = (bf16[16,32,128]{2,1,0:T(8,128)(2,1)S(1)}, bf16[16,32,128]{2,1,0:T(8,128)(2,1)S(1)}, u32[]{:S(2)}, u32[]{:S(2)}) collective-permute-start(bf16[16,32,128]{2,1,0:T(8,128)(2,1)S(1)} %copy-done.14), channel_id=1, source_target_pairs={{0,0},{1,4},{2,8},{3,12},{4,1},{5,5},{6,9},{7,13},{8,2},{9,6},{10,... | collective-permute-start | bytes 393224 | tf_op jit(solution)/shard_map/ppermute | solution.py:712
  48.6 12.3 %collective-permute-start.9 = (bf16[2,128,1024]{2,1,0:T(8,128)(2,1)S(1)}, bf16[2,128,1024]{2,1,0:T(8,128)(2,1)S(1)}, u32[]{:S(2)}, u32[]{:S(2)}) collective-permute-start(bf16[2,128,1024]{2,1,0:T(8,128)(2,1)S(1)} %bitcast.79), channel_id=1, source_target_pairs={{0,4},{4,0},{8,12},{12,8},{1,5},{5,1},{9,13},{13,9},{2,6},{6,2},{1... | collective-permute-start | bytes 1572872 | tf_op jit(solution)/shard_map/ppermute | solution.py:699
  49.6 30.3 %collective-permute-start.11 = (bf16[64,4096]{1,0:T(8,128)(2,1)}, bf16[64,4096]{1,0:T(8,128)(2,1)}, u32[]{:S(2)}, u32[]{:S(2)}) collective-permute-start(bf16[64,4096]{1,0:T(8,128)(2,1)} %get-tuple-element.60), channel_id=1, source_target_pairs={{0,8},{4,12},{8,0},{12,4},{1,9},{5,13},{9,1},{13,5},{2,10},{6,14},... | collective-permute-start | bytes 1572872 | tf_op jit(solution)/shard_map/ppermute | solution.py:702
  61.9 18.1 %collective-permute-start.10 = (bf16[2,128,1024]{2,1,0:T(8,128)(2,1)}, bf16[2,128,1024]{2,1,0:T(8,128)(2,1)}, u32[]{:S(2)}, u32[]{:S(2)}) collective-permute-start(bf16[2,128,1024]{2,1,0:T(8,128)(2,1)} %fusion.1), channel_id=1, source_target_pairs={{0,8},{4,12},{8,0},{12,4},{1,9},{5,13},{9,1},{13,5},{2,10},{6,14},... | collective-permute-start | bytes 1572872 | tf_op jit(solution)/shard_map/ppermute | solution.py:702
  61.9 18.0 %collective-permute-start.12 = (bf16[2,128,768]{2,1,0:T(8,128)(2,1)S(1)}, bf16[2,128,768]{2,1,0:T(8,128)(2,1)}, u32[]{:S(2)}, u32[]{:S(2)}) collective-permute-start(bf16[2,128,768]{2,1,0:T(8,128)(2,1)S(1)} %bitcast.80), channel_id=1, source_target_pairs={{0,4},{4,0},{8,12},{12,8},{1,5},{5,1},{9,13},{13,9},{2,6},{6,2},{1... | collective-permute-start | bytes 1179656 | tf_op jit(solution)/shard_map/ppermute | solution.py:699
  62.1 17.9 %collective-permute-start.14 = (bf16[2,256,128]{2,1,0:T(8,128)(2,1)}, bf16[2,256,128]{2,1,0:T(8,128)(2,1)S(1)}, u32[]{:S(2)}, u32[]{:S(2)}) collective-permute-start(bf16[2,256,128]{2,1,0:T(8,128)(2,1)} %constant_dynamic-update-slice_fusion), channel_id=1, source_target_pairs={{0,2},{1,3},{2,0},{3,1},{4,6},{5,7},{6,4},{7,5},{8,10},{9,11},{10,... | collective-permute-start | bytes 393224 | tf_op jit(solution)/shard_map/ppermute | solution.py:705
  64.5 15.4 %collective-permute-start.13 = (bf16[1,16,32,128]{3,2,1,0:T(8,128)(2,1)S(1)}, bf16[1,16,32,128]{3,2,1,0:T(8,128)(2,1)S(1)}, u32[]{:S(2)}, u32[]{:S(2)}) collective-permute-start(bf16[1,16,32,128]{3,2,1,0:T(8,128)(2,1)S(1)} %bitcast.84), channel_id=1, source_target_pairs={{0,1},{1,0},{2,3},{3,2},{4,5},{5,4},{6,7},{7,6},{8,9},{9,8},{10,11... | collective-permute-start | bytes 393224 | tf_op jit(solution)/shard_map/ppermute | solution.py:705
  78.6 1.3 copy-start.2
  79.9 3.2 %copy-start.11 = (bf16[1,16,32,128]{3,2,1,0:T(8,128)(2,1)}, bf16[1,16,32,128]{3,2,1,0:T(8,128)(2,1)S(1)}, u32[]{:S(2)}) copy-start(bf16[1,16,32,128]{3,2,1,0:T(8,128)(2,1)S(1)} %collective-permute-done.13) | copy-start | bytes 393220
  80.0 5.9 %collective-permute-start.15 = (bf16[2,2,128,1792]{3,2,1,0:T(8,128)(2,1)}, bf16[2,2,128,1792]{3,2,1,0:T(8,128)(2,1)}, u32[]{:S(2)}, u32[]{:S(2)}) collective-permute-start(bf16[2,2,128,1792]{3,2,1,0:T(8,128)(2,1)} %get-tuple-element.64), channel_id=1, source_target_pairs={{0,4},{4,0},{8,12},{12,8},{1,5},{5,1},{9,13},{13,9},{2,6},{6,2},{1... | collective-permute-start | bytes 5505032 | tf_op jit(solution)/shard_map/ppermute | solution.py:699
  80.8 57.0 %collective-permute-start.28 = (bf16[64,4096]{1,0:T(8,128)(2,1)}, bf16[64,4096]{1,0:T(8,128)(2,1)}, u32[]{:S(2)}, u32[]{:S(2)}) collective-permute-start(bf16[64,4096]{1,0:T(8,128)(2,1)} %collective-permute-done.11.refs_4_.refs_20_), channel_id=1, source_target_pairs={{0,4},{4,0},{8,12},{12,8},{1,5},{5,1},{9,13},{13,9},{2,6},{6,2},{1... | collective-permute-start | bytes 1572872 | tf_op jit(solution)/shard_map/ppermute | solution.py:699
  83.1 19.8 %collective-permute-start.17 = (bf16[2,128,768]{2,1,0:T(8,128)(2,1)}, bf16[2,128,768]{2,1,0:T(8,128)(2,1)}, u32[]{:S(2)}, u32[]{:S(2)}) collective-permute-start(bf16[2,128,768]{2,1,0:T(8,128)(2,1)} %fusion.4), channel_id=1, source_target_pairs={{0,8},{4,12},{8,0},{12,4},{1,9},{5,13},{9,1},{13,5},{2,10},{6,14},... | collective-permute-start | bytes 1179656 | tf_op jit(solution)/shard_map/ppermute | solution.py:702
  87.9 1.5 copy-start.3
  88.2 5.2 %collective-permute-start.19 = (bf16[128,1792]{1,0:T(8,128)(2,1)S(1)}, bf16[128,1792]{1,0:T(8,128)(2,1)S(1)}, u32[]{:S(2)}, u32[]{:S(2)}) collective-permute-start(bf16[128,1792]{1,0:T(8,128)(2,1)S(1)} %fusion.3.refs_2_), channel_id=1, source_target_pairs={{0,4},{4,0},{8,12},{12,8},{1,5},{5,1},{9,13},{13,9},{2,6},{6,2},{1... | collective-permute-start | bytes 1376264 | tf_op jit(solution)/shard_map/ppermute | solution.py:699
  88.3 15.9 %collective-permute-start.16 = (bf16[128,1792]{1,0:T(8,128)(2,1)S(1)}, bf16[128,1792]{1,0:T(8,128)(2,1)S(1)}, u32[]{:S(2)}, u32[]{:S(2)}) collective-permute-start(bf16[128,1792]{1,0:T(8,128)(2,1)S(1)} %fusion.3.refs_2_), channel_id=1, source_target_pairs={{0,8},{4,12},{8,0},{12,4},{1,9},{5,13},{9,1},{13,5},{2,10},{6,14},... | collective-permute-start | bytes 1376264 | tf_op jit(solution)/shard_map/ppermute | solution.py:702
  90.8 1.2 copy-start.12
  91.0 1.6 collective-permute-start.18
  92.6 34.4 %collective-permute-start.27 = (bf16[64,4096]{1,0:T(8,128)(2,1)}, bf16[64,4096]{1,0:T(8,128)(2,1)}, u32[]{:S(2)}, u32[]{:S(2)}) collective-permute-start(bf16[64,4096]{1,0:T(8,128)(2,1)} %collective-permute-done.11.refs_4_.refs_20_), channel_id=1, source_target_pairs={{0,1},{1,0},{2,3},{3,2},{4,5},{5,4},{6,7},{7,6},{8,9},{9,8},{10,11... | collective-permute-start | bytes 1572872 | tf_op jit(solution)/shard_map/ppermute | solution.py:705
  93.4 17.3 %collective-permute-start.24 = (bf16[2,16,32,128]{3,2,1,0:T(8,128)(2,1)S(1)}, bf16[2,16,32,128]{3,2,1,0:T(8,128)(2,1)S(1)}, u32[]{:S(2)}, u32[]{:S(2)}) collective-permute-start(bf16[2,16,32,128]{3,2,1,0:T(8,128)(2,1)S(1)} %pad_maximum_fusion), channel_id=1, source_target_pairs={{0,2},{1,3},{2,0},{3,1},{4,6},{5,7},{6,4},{7,5},{8,10},{9,11},{10,... | collective-permute-start | bytes 786440 | tf_op jit(solution)/shard_map/ppermute | solution.py:705
  102.9 3.5 %copy-start.7 = (bf16[4,16,32,128]{3,2,1,0:T(8,128)(2,1)S(1)}, bf16[4,16,32,128]{3,2,1,0:T(8,128)(2,1)}, u32[]{:S(2)}) copy-start(bf16[4,16,32,128]{3,2,1,0:T(8,128)(2,1)} %constant_dynamic-update-slice_fusion.4) | copy-start | bytes 1572868
  104.2 6.5 %copy-start.5 = (bf16[128,1792]{1,0:T(8,128)(2,1)}, bf16[128,1792]{1,0:T(8,128)(2,1)S(1)}, u32[]{:S(2)}) copy-start(bf16[128,1792]{1,0:T(8,128)(2,1)S(1)} %collective-permute-done.16.refs_0_) | copy-start | bytes 1376260
  106.5 11.4 %collective-permute-start.20 = (bf16[128,768]{1,0:T(8,128)(2,1)}, bf16[128,768]{1,0:T(8,128)(2,1)}, u32[]{:S(2)}, u32[]{:S(2)}) collective-permute-start(bf16[128,768]{1,0:T(8,128)(2,1)} %fusion.8.refs_0_), channel_id=1, source_target_pairs={{0,4},{4,0},{8,12},{12,8},{1,5},{5,1},{9,13},{13,9},{2,6},{6,2},{1... | collective-permute-start | bytes 589832 | tf_op jit(solution)/shard_map/ppermute | solution.py:699
  110.8 0.8 copy-start.8
  113.6 23.6 %collective-permute-start.22 = (bf16[128,1024]{1,0:T(8,128)(2,1)S(1)}, bf16[128,1024]{1,0:T(8,128)(2,1)}, u32[]{:S(2)}, u32[]{:S(2)}) collective-permute-start(bf16[128,1024]{1,0:T(8,128)(2,1)S(1)} %fusion.6.refs_0_), channel_id=1, source_target_pairs={{0,8},{4,12},{8,0},{12,4},{1,9},{5,13},{9,1},{13,5},{2,10},{6,14},... | collective-permute-start | bytes 786440 | tf_op jit(solution)/shard_map/ppermute | solution.py:702
  116.9 19.8 %collective-permute-start.23 = (bf16[128,768]{1,0:T(8,128)(2,1)}, bf16[128,768]{1,0:T(8,128)(2,1)S(1)}, u32[]{:S(2)}, u32[]{:S(2)}) collective-permute-start(bf16[128,768]{1,0:T(8,128)(2,1)} %fusion.8.refs_0_), channel_id=1, source_target_pairs={{0,8},{4,12},{8,0},{12,4},{1,9},{5,13},{9,1},{13,5},{2,10},{6,14},... | collective-permute-start | bytes 589832 | tf_op jit(solution)/shard_map/ppermute | solution.py:702
  117.9 9.2 %copy-start.1 = (bf16[8,256,256]{2,1,0:T(8,128)(2,1)S(1)}, bf16[8,256,256]{2,1,0:T(8,128)(2,1)}, u32[]{:S(2)}) copy-start(bf16[8,256,256]{2,1,0:T(8,128)(2,1)} %spread_left.1.refs_5_.refs_9_.refs_11_) | copy-start | bytes 3145732
  117.9 9.2 %copy-start.9 = (bf16[4,16,32,128]{3,2,1,0:T(8,128)(2,1)S(1)}, bf16[4,16,32,128]{3,2,1,0:T(8,128)(2,1)}, u32[]{:S(2)}) copy-start(bf16[4,16,32,128]{3,2,1,0:T(8,128)(2,1)} %copy-done.8) | copy-start | bytes 1572868
  127.0 10.4 %copy-start.6 = (bf16[128,1792]{1,0:T(8,128)(2,1)S(1)}, bf16[128,1792]{1,0:T(8,128)(2,1)}, u32[]{:S(2)}) copy-start(bf16[128,1792]{1,0:T(8,128)(2,1)} %copy-done.5) | copy-start | bytes 1376260
  127.0 10.8 %collective-permute-start.29 = (bf16[64,4096]{1,0:T(8,128)(2,1)}, bf16[64,4096]{1,0:T(8,128)(2,1)S(1)}, u32[]{:S(2)}, u32[]{:S(2)}) collective-permute-start(bf16[64,4096]{1,0:T(8,128)(2,1)} %collective-permute-done.27.refs_5_.refs_21_), channel_id=1, source_target_pairs={{0,4},{4,0},{8,12},{12,8},{1,5},{5,1},{9,13},{13,9},{2,6},{6,2},{1... | collective-permute-start | bytes 1572872 | tf_op jit(solution)/shard_map/ppermute | solution.py:699
  136.7 12.6 %copy-start.4 = (bf16[8,256,256]{2,1,0:T(8,128)(2,1)}, bf16[8,256,256]{2,1,0:T(8,128)(2,1)S(1)}, u32[]{:S(2)}) copy-start(bf16[8,256,256]{2,1,0:T(8,128)(2,1)S(1)} %get-tuple-element.74.refs_9_) | copy-start | bytes 3145732
  136.7 12.6 %collective-permute-start.26 = (bf16[128,768]{1,0:T(8,128)(2,1)S(1)}, bf16[128,768]{1,0:T(8,128)(2,1)S(1)}, u32[]{:S(2)}, u32[]{:S(2)}) collective-permute-start(bf16[128,768]{1,0:T(8,128)(2,1)S(1)} %collective-permute-done.23.refs_3_), channel_id=1, source_target_pairs={{0,4},{4,0},{8,12},{12,8},{1,5},{5,1},{9,13},{13,9},{2,6},{6,2},{1... | collective-permute-start | bytes 589832 | tf_op jit(solution)/shard_map/ppermute | solution.py:699
  137.3 12.0 %collective-permute-start.25 = (bf16[128,1024]{1,0:T(8,128)(2,1)}, bf16[128,1024]{1,0:T(8,128)(2,1)S(1)}, u32[]{:S(2)}, u32[]{:S(2)}) collective-permute-start(bf16[128,1024]{1,0:T(8,128)(2,1)} %collective-permute-done.22.refs_2_), channel_id=1, source_target_pairs={{0,4},{4,0},{8,12},{12,8},{1,5},{5,1},{9,13},{13,9},{2,6},{6,2},{1... | collective-permute-start | bytes 786440 | tf_op jit(solution)/shard_map/ppermute | solution.py:699
  137.3 11.9 %collective-permute-start.21 = (bf16[128,1792]{1,0:T(8,128)(2,1)S(1)}, bf16[128,1792]{1,0:T(8,128)(2,1)S(1)}, u32[]{:S(2)}, u32[]{:S(2)}) collective-permute-start(bf16[128,1792]{1,0:T(8,128)(2,1)S(1)} %copy-done.6), channel_id=1, source_target_pairs={{0,4},{4,0},{8,12},{12,8},{1,5},{5,1},{9,13},{13,9},{2,6},{6,2},{1... | collective-permute-start | bytes 1376264 | tf_op jit(solution)/shard_map/ppermute | solution.py:699
  137.8 0.8 copy-start.10
  171.1 12.3 %collective-permute-start.30 = (bf16[2,768,128]{2,1,0:T(8,128)(2,1)S(1)}, bf16[2,768,128]{2,1,0:T(8,128)(2,1)S(1)}, u32[]{:S(2)}, u32[]{:S(2)}) collective-permute-start(bf16[2,768,128]{2,1,0:T(8,128)(2,1)S(1)} %slice.92), channel_id=1, source_target_pairs={{0,1},{1,0},{2,3},{3,2},{4,5},{5,4},{6,7},{7,6},{8,9},{9,8},{10,11... | collective-permute-start | bytes 1179656 | tf_op jit(solution)/shard_map/ppermute | solution.py:705
  184.6 6.4 %collective-permute-start.33 = (bf16[256,128]{1,0:T(8,128)(2,1)S(1)}, bf16[256,128]{1,0:T(8,128)(2,1)S(1)}, u32[]{:S(2)}, u32[]{:S(2)}) collective-permute-start(bf16[256,128]{1,0:T(8,128)(2,1)S(1)} %slice_bitcast_fusion.8), channel_id=1, source_target_pairs={{0,2},{1,3},{2,0},{3,1},{4,6},{5,7},{6,4},{7,5},{8,10},{9,11},{10,... | collective-permute-start | bytes 196616 | tf_op jit(solution)/shard_map/ppermute | solution.py:705
  186.9 5.1 %collective-permute-start.31 = (bf16[512,128]{1,0:T(8,128)(2,1)S(1)}, bf16[512,128]{1,0:T(8,128)(2,1)S(1)}, u32[]{:S(2)}, u32[]{:S(2)}) collective-permute-start(bf16[512,128]{1,0:T(8,128)(2,1)S(1)} %get-tuple-element.82), channel_id=1, source_target_pairs={{0,0},{1,4},{2,8},{3,12},{4,1},{5,5},{6,9},{7,13},{8,2},{9,6},{10,... | collective-permute-start | bytes 393224 | tf_op jit(solution)/shard_map/ppermute | solution.py:712
  187.6 15.5 %collective-permute-start.32 = (bf16[512,128]{1,0:T(8,128)(2,1)S(1)}, bf16[512,128]{1,0:T(8,128)(2,1)S(1)}, u32[]{:S(2)}, u32[]{:S(2)}) collective-permute-start(bf16[512,128]{1,0:T(8,128)(2,1)S(1)} %get-tuple-element.83), channel_id=1, source_target_pairs={{0,8},{1,12},{2,0},{3,4},{4,9},{5,13},{6,1},{7,5},{8,10},{9,14},{1... | collective-permute-start | bytes 393224 | tf_op jit(solution)/shard_map/ppermute | solution.py:712

commit v6 on v5

--- a/solution.py
+++ b/solution.py
@@ -351,7 +351,9 @@
             return pl.BlockSpec((half, feat), lambda n, s: (0, s[column]))
         return pl.BlockSpec((half, feat), lambda n, s: (s[row], s[column]))
 
-    weight_spec = pl.BlockSpec((feat, BLK), lambda n, s: (0, s[4] + start + n))
+    weight_spec = pl.BlockSpec(
+        (feat, BLK), lambda n, s: (0, s[4] + start + n), pipeline_mode=pl.Buffered(2)
+    )
     out_spec = pl.BlockSpec((sets, 2, 2 * half, BLK), lambda n, s: (0, 0, 0, n))
     shape = jax.ShapeDtypeStruct((sets, 2, 2 * half, width), BF16)
     return pl.pallas_call(
@@ -370,73 +372,19 @@
     )(scalars, *[piece for piece, _, _ in pieces], gate, up)
 
 
-def fill_rows(lhs, sets):
-    row = 0
-    for group in sets:
-        column = 0
-        for piece in group:
-            rows, width = piece.shape
-            lhs[row : row + rows, column : column + width] = piece[...]
-            column += width
-        row += group[0].shape[0]
-
-
-def split_sets(refs, counts):
-    sets, start = [], 0
-    for count in counts:
-        sets.append(refs[start : start + count])
-        start += count
-    return sets, refs[start:]
+def fill_rows(lhs, pieces, chip):
+    own, near, got, near_got = pieces
+    rows, width = own.shape[1:]
+    for u in range(2):
+        for part, (mine, other) in enumerate(((own, near), (got, near_got))):
+            begin = pl.multiple_of(lax.rem(chip + part, 2) * width, LANES)
+            which = u if part == 0 else 1 - u
+            lhs[2 * u * rows : (2 * u + 1) * rows, pl.ds(begin, width)] = mine[which]
+            lhs[(2 * u + 1) * rows : (2 * u + 2) * rows, pl.ds(begin, width)] = other[which]
 
 
 def whole_spec(array):
     return pl.BlockSpec(array.shape, lambda n, s: (0,) * array.ndim)
-
-
-def target_kernel(counts, tiles, idx_ref, *refs):
-    sets, refs = split_sets(refs, counts)
-    weights, terms, (out_ref, lhs) = refs[:tiles], refs[tiles:-2], refs[-2:]
-    pl.when(pl.program_id(0) == 0)(lambda: fill_rows(lhs, sets))
-    weight = jnp.concatenate([ref[...] for ref in weights], axis=0)
-    product = jnp.dot(lhs[...], weight, preferred_element_type=F32)
-    out_ref[...] = sum((ref[...] for ref in terms), product)
-
-
-def target_part(terms, sets, weight, row, width):
-    counts = [1] * len(sets)
-    rows = sum(piece.shape[0] for piece, _ in sets)
-    outs = weight.shape[1]
-    tiles = width // BLK
-
-    def piece_spec(piece, first):
-        return pl.BlockSpec((piece.shape[0], width), lambda n, s: (0, first // width))
-
-    pieces = []
-    for piece, first in sets:
-        if first % width:
-            piece, first = lax.slice_in_dim(piece, first, first + width, axis=1), 0
-        pieces.append((piece, first))
-    return pl.pallas_call(
-        functools.partial(target_kernel, counts, tiles),
-        grid_spec=pltpu.PrefetchScalarGridSpec(
-            num_scalar_prefetch=1,
-            grid=(outs // BLK,),
-            in_specs=[piece_spec(*piece) for piece in pieces]
-            + [pl.BlockSpec((BLK, BLK), lambda n, s, k=k: (s[0] + k, n)) for k in range(tiles)]
-            + [pl.BlockSpec((term.shape[0], BLK), lambda n, s: (0, n)) for term in terms],
-            out_specs=pl.BlockSpec((rows, BLK), lambda n, s: (0, n)),
-            scratch_shapes=[pltpu.VMEM((rows, width), BF16)],
-        ),
-        out_shape=jax.ShapeDtypeStruct((rows, outs), F32),
-        compiler_params=pltpu.CompilerParams(vmem_limit_bytes=50 * 2**20),
-        cost_estimate=SMALL,
-        name="target_part",
-    )(
-        jnp.reshape(lax.div(row, BLK), (1,)).astype(jnp.int32),
-        *[piece for piece, _ in pieces],
-        *[weight] * tiles,
-        *terms,
-    )
 
 
 TN = (((0,), (0,)), ((), ()))
@@ -477,8 +425,7 @@
 
 
 def student_kernel(steps, late, tensor_count, idx_ref, *refs):
-    tokens, refs = refs[:-6], refs[-6:]
-    right_ref, left_ref, target_ref, mixed_ref, rest_ref, spread = refs
+    tokens, (right_ref, left_ref, mixed_ref, student_ref, spread) = refs[:-5], refs[-5:]
     step = pl.program_id(0)
     chunk = natural(step, idx_ref[2], steps // 2)
     groups = left_ref.shape[0]
@@ -513,7 +460,7 @@
             student = lax.dot_general(
                 mixed_ref[g], left_ref[g], TN, preferred_element_type=F32
             )
-            rest_ref[:, span] = student * (1.0 / tensor_count) - target_ref[:, span]
+            student_ref[:, span] = student * (1.0 / tensor_count)
 
 
 def token_specs(half, width, steps, begin, own):
@@ -523,20 +470,27 @@
 
     if own:
         return [
-            pl.BlockSpec((half, width), lambda n, s, p=p: (s[p % 2], chunk(n, s)))
+            pl.BlockSpec(
+                (half, width),
+                lambda n, s, p=p: (s[p % 2], chunk(n, s)),
+                pipeline_mode=pl.Buffered(2),
+            )
             for p in range(4)
         ]
     near = pl.BlockSpec(
-        (half, width), lambda n, s: (0, jnp.clip(n - begin, 0, steps // 2 - 1))
+        (half, width),
+        lambda n, s: (0, jnp.clip(n - begin, 0, steps // 2 - 1)),
+        pipeline_mode=pl.Buffered(2),
     )
     far = pl.BlockSpec(
         (half, width),
         lambda n, s: (0, jnp.clip(n - begin - steps // 2, 0, steps // 2 - 1)),
+        pipeline_mode=pl.Buffered(2),
     )
     return [near] * 4 + [far] * 4
 
 
-def student_part(tokens, late, scalars, right_rows, left_diag, target, tensor_count):
+def student_part(tokens, late, scalars, right_rows, left_diag, tensor_count):
     per_owner, pairs, size = right_rows.shape[1:]
     blocks = right_rows.shape[0] * per_owner
     steps = blocks // WIDE
@@ -557,7 +511,6 @@
             + [
                 pl.BlockSpec((1, WIDE, pairs, size), right_block),
                 whole_spec(left_diag),
-                pl.BlockSpec((4 * half, groups * BLK), lambda n, s: (int(late), 0)),
             ],
             out_specs=[
                 pl.BlockSpec((groups, BLK, 4 * half), lambda n, s: (0, 0, 0)),
@@ -574,12 +527,12 @@
             flops=10**10, bytes_accessed=10**7, transcendentals=0
         ),
         name="student_part",
-    )(scalars, *tokens, right_rows, left_diag, target)
-
-
-def grads_kernel(groups, steps, scale, counts, idx_ref, *refs):
-    sets, refs = split_sets(refs, counts)
-    weight_ref, rest0, rest1, mixed0, mixed1, left_ref = refs[:6]
+    )(scalars, *tokens, right_rows, left_diag)
+
+
+def grads_kernel(groups, steps, scale, idx_ref, *refs):
+    hidden, refs = refs[:4], refs[4:]
+    weight_ref, student0, student1, mixed0, mixed1, left_ref = refs[:6]
     own, near, far = refs[6:10], refs[10:14], refs[14:18]
     out_ref, lhs, back, wide = refs[18:]
     step = pl.program_id(0)
@@ -595,13 +548,13 @@
         bits = z ^ owner
         return lax.rem(bits, 2) * 2 + bits // 2
 
-    pl.when(step == 0)(lambda: fill_rows(lhs, sets))
+    pl.when(step == 0)(lambda: fill_rows(lhs, hidden, idx_ref[2]))
 
     @pl.when(step < groups)
     def _():
         target = jnp.dot(lhs[...], weight_ref[...], preferred_element_type=F32)
-        rest = jnp.concatenate([rest0[...], rest1[...]], axis=0)
-        out_grad = ((rest - target) * scale).astype(BF16)
+        student = jnp.concatenate([student0[...], student1[...]], axis=0)
+        out_grad = ((student - target) * scale).astype(BF16)
         mixed = jnp.concatenate([mixed0[0], mixed1[0]], axis=1)
         left = jnp.dot(mixed, out_grad, preferred_element_type=F32)
         value = lax.dot_general(
@@ -646,30 +599,35 @@
 
 
 def factor_grads(
-    sets, weight, rest, mixed, left_diag, own, late, scalars, parts, size, scale
+    hidden, weight, students, mixed, left_diag, own, late, scalars, parts, size, scale
 ):
-    pieces = [piece for group in sets for piece in group]
-    groups, count = left_diag.shape[0], 2 * rest[0].shape[0]
-    width = weight.shape[0] // 2
+    groups, count = left_diag.shape[0], 2 * students[0].shape[0]
+    width = weight.shape[0]
     half = late[0].shape[0]
     steps = own[0].shape[1] // (WIDE * size)
     blocks = steps * WIDE
     pairs = groups * BLK // blocks
+    deep = pl.Buffered(2)
 
     def group(n):
         return jnp.minimum(n, groups - 1)
 
+    column = pl.BlockSpec((count // 2, BLK), lambda n, s: (0, group(n)), pipeline_mode=deep)
+    slab = pl.BlockSpec((1, BLK, count // 2), lambda n, s: (group(n), 0, 0), pipeline_mode=deep)
     out_rows = (pairs * blocks + pairs * blocks * blocks // size) // parts
     return pl.pallas_call(
-        functools.partial(grads_kernel, groups, steps, scale, [len(g) for g in sets]),
+        functools.partial(grads_kernel, groups, steps, scale),
         grid_spec=pltpu.PrefetchScalarGridSpec(
             num_scalar_prefetch=1,
             grid=(groups + steps,),
-            in_specs=[whole_spec(piece) for piece in pieces]
-            + [pl.BlockSpec((width, BLK), lambda n, s: (1 - s[2], group(n)))]
-            + [pl.BlockSpec((count // 2, BLK), lambda n, s: (0, group(n)))] * 2
-            + [pl.BlockSpec((1, BLK, count // 2), lambda n, s: (group(n), 0, 0))] * 2
-            + [pl.BlockSpec((1, BLK, BLK), lambda n, s: (group(n), 0, 0))]
+            in_specs=[whole_spec(piece) for piece in hidden]
+            + [pl.BlockSpec((width, BLK), lambda n, s: (0, group(n)), pipeline_mode=deep)]
+            + [column, column, slab, slab]
+            + [
+                pl.BlockSpec(
+                    (1, BLK, BLK), lambda n, s: (group(n), 0, 0), pipeline_mode=deep
+                )
+            ]
             + token_specs(half, WIDE * size, steps, groups, True)
             + token_specs(half, WIDE * size, steps, groups, False),
             out_specs=pl.BlockSpec((parts, out_rows, size), lambda n, s: (0, 0, 0)),
@@ -683,7 +641,7 @@
         compiler_params=pltpu.CompilerParams(vmem_limit_bytes=50 * 2**20),
         cost_estimate=SMALL,
         name="factor_grads",
-    )(scalars, *pieces, weight, *rest, *mixed, left_diag, *own, *late)
+    )(scalars, *hidden, weight, *students, *mixed, left_diag, *own, *late)
 
 
 def tiled_body(tokens, gate_weight, up_weight, down_weight, right_factor, left_factor):
@@ -720,9 +678,6 @@
     def add(*terms):
         return sum(term.astype(F32) for term in terms)
 
-    head = (part // BLK + 1) // 2 * BLK
-    chunks = [(0, head), (head, part - head)]
-
     near_tokens = swap(tokens)
     first, rest = cut_tokens(tokens, odd, chip)
     arrived = across(first)
@@ -756,25 +711,18 @@
     left_rows = double(after(left_own, sums), 1)
 
     late_order = after(scalars(other_block), sums, right_rows, left_rows)
-    value0, other0 = products(late_pieces, late_order, gate_weight, up_weight, *chunks[0])
-    near0 = swap(after(other0[0], got_early))
-    late_order = after(late_order, value0)
-    value1, other1 = products(late_pieces, late_order, gate_weight, up_weight, *chunks[1])
-    near1 = swap(other1[0])
-    sums0 = add(value0[0], after(near0, value1)).astype(BF16)
-    got0 = across(sums0)
-    mine_order = after(scalars(mine_block), value1, sums0)
-    right_rows, left_rows = after(right_rows, value1), after(left_rows, value1)
+    mine, other = products(late_pieces, late_order, gate_weight, up_weight, 0, part)
+    near = swap(after(other[0], got_early, late_first))
+    right_rows, left_rows = after(right_rows, mine), after(left_rows, mine)
     more_right, more_left = along(right_rows, 1), along(left_rows, 2)
+    sums = add(mine[0], near).astype(BF16)
+    got = across(sums)
+    mine_order = after(scalars(mine_block), sums)
     kept, other = products(
         own_pieces + late_pieces, mine_order, gate_weight, up_weight, 0, part
     )
-    kept_other = swap(after(other, got0, late_first, near1, more_right, more_left))
     right_rows = jnp.concatenate([right_rows, after(more_right, kept)], axis=0)
     left_rows = jnp.concatenate([left_rows, after(more_left, kept)], axis=0)
-    right_rows = double(right_rows, 2)
-    sums1 = add(value1[0], after(near1, kept)).astype(BF16)
-    got1 = across(sums1)
 
     left_rows = left_rows.reshape((tensor_count,) + left_factor.shape)
     for axis, bit in ((0, 2), (1, 1)):
@@ -783,54 +731,38 @@
         left_rows = split.reshape(left_rows.shape)
     left_rows = left_rows.transpose(1, 3, 0, 2).reshape(pairs, blocks, blocks)
 
-    def activate(u, span, term):
-        begin, width = span
-        terms = [value[u, :, :, begin : begin + width] for value in (kept, kept_other)]
-        total = add(*terms, term)
-        return (jax.nn.silu(total[0]) * total[1]).astype(BF16)
-
-    hidden_late = activate(1, (0, part), got_early)
-    got_late = across(hidden_late)
-    near_hidden_late = swap(hidden_late)
-    hidden0 = activate(0, chunks[0], after(got0, hidden_late))
-    got_hidden0 = across(hidden0)
-    left_diag = spread_left(after(left_rows, hidden0))
+    left_diag = spread_left(left_rows)
+    near_kept = swap(after(other, got, right_rows, left_diag))
+    more_right = along(right_rows, 2)
     late_partner = along(after(late_first, kept), 1)
-
-    def target(term, span, value):
-        sets = [(value, 0), (swap(value), 0)]
-        sets += [(hidden_late, span[0]), (near_hidden_late, span[0])]
-        return target_part(term, sets, down_weight, chip * part + span[0], span[1])
-
-    total = target([], chunks[0], after(hidden0, sums1))
-    hidden1 = activate(0, chunks[1], after(got1, total, got_late))
-    got_hidden1 = across(hidden1)
-    total = target([total], chunks[1], hidden1)
-    got_late, got_hidden0 = after(got_late, total), after(got_hidden0, total)
-    late_partner = after(late_partner, total)
+    hidden = []
+    for u, term in enumerate((got, got_early)):
+        total = add(kept[u], near_kept[u], term)
+        hidden.append((jax.nn.silu(total[0]) * total[1]).astype(BF16))
+    hidden = jnp.stack(hidden)
+    got_hidden = across(hidden)
+    near_hidden = swap(hidden)
+    more_right, late_partner = after(more_right, hidden), after(late_partner, hidden)
+    right_rows = jnp.concatenate([right_rows, more_right], axis=0)
+    mixed0, student0 = student_part(
+        [after(tokens, hidden)] + own[1:], False, order, right_rows, left_diag, tensor_count
+    )
     late_rest = [late_first, late_partner, swap(late_first), swap(late_partner)]
-    near_got_late = swap(got_late)
-    near_got0 = swap(got_hidden0)
-    mixed0, rest0 = student_part(
-        own, False, order, right_rows, left_diag, total, tensor_count
-    )
-    got_hidden1 = after(got_hidden1, mixed0)
-    mixed1, rest1 = student_part(
+    mixed1, student1 = student_part(
         late + [after(late_rest[0], mixed0)] + late_rest[1:],
         True,
         order,
         right_rows,
         left_diag,
-        total,
         tensor_count,
     )
-    got_hidden = [got_hidden0, got_hidden1]
-    sets = [[got_late], [near_got_late], got_hidden, [near_got0, swap(got_hidden1)]]
+    got_hidden = after(got_hidden, mixed1)
+    hidden = [hidden, near_hidden, got_hidden, swap(got_hidden)]
 
     grads = factor_grads(
-        sets,
+        hidden,
         down_weight,
-        (rest0, rest1),
+        (student0, student1),
         (mixed0, mixed1),
         left_diag,
         own,

time: 206 us -> 196 us (0.951)
  Pallas kernels: 98.4 us -> 82.5 us
  waiting for transfers between devices: 42.6 us -> 54.1 us
  other arithmetic: 13.8 us -> 9.25 us
  starting transfers between devices: 37 us -> 34.7 us
  local copies, waits for them, and re-layouts: 10.8 us -> 12.9 us
    pallas_call x3 -> x1, Pallas kernels: 38.1 us -> 25.6 us  [factor_grads(): pl.pallas_call(functools.partial(grads_kernel, groups, steps, scale), gri...]
    ppermute x8, waiting for transfers between devices: 24 us -> 33.6 us  [along(): lax.ppermute(value, 'tensor', [(i, i ^ bit) for i in range(tensor_count)])]
    ppermute x8 -> x5, starting transfers between devices: 14.5 us -> 10 us  [across(): return lax.ppermute(value, 'fsdp', [(i, i ^ 2) for i in range(fsdp_count)])]
    unnamed x33 -> x29, local copies, waits for them, and re-layouts: 4.73 us -> 7.15 us
    ppermute x8, starting transfers between devices: 14.2 us -> 16.6 us  [along(): lax.ppermute(value, 'tensor', [(i, i ^ bit) for i in range(tensor_count)])]
    convert_element_type x5 -> x2, other arithmetic: 4.04 us -> 1.71 us  [the longest x1 1.15 us: tiled_body(): sums = add(mine[0], near).astype(BF16)]
    add x5 -> x3, other arithmetic: 5.62 us -> 3.35 us  [add(): return sum((term.astype(F32) for term in terms))]
    ppermute x15 -> x10, waiting for transfers between devices: 1.18 us -> 3.3 us  [swap(): return lax.ppermute(value, 'fsdp', [(i, i ^ 1) for i in range(fsdp_count)])]
  transfers between devices with their start and end apart: 34 -> 26, of which waited for: 10 -> 11; matrix products, arithmetic and copies ran while one was open for 9% -> 8% of each run, Pallas kernels for 38% -> 29%
where the time goes in v6:
time: 196 us; the launch traced here: 194 us
  Pallas kernels  82.5 us (42%)
  waiting for transfers between devices  54.1 us (28%)
  starting transfers between devices  34.7 us (18%)
  local copies, waits for them, and re-layouts  12.9 us (7%)
  other arithmetic  9.25 us (5%)
    ppermute x8, waiting for transfers between devices, along(): lax.ppermute(value, 'tensor', [(i, i ^ bit) for i in range(tensor_count)])  33.6 us
    pallas_call x3, Pallas kernels, products(): pl.pallas_call(functools.partial(products_kernel, sets), grid_spec=pltpu....  33.3 us
    pallas_call x1, Pallas kernels, factor_grads(): pl.pallas_call(functools.partial(grads_kernel, groups, steps, scale), gri...  25.6 us
    pallas_call x2, Pallas kernels, student_part(): pl.pallas_call(functools.partial(student_kernel, steps, late, tensor_coun...  18.3 us
    ppermute x8, starting transfers between devices, along(): lax.ppermute(value, 'tensor', [(i, i ^ bit) for i in range(tensor_count)])  16.6 us
    ppermute x3, waiting for transfers between devices, turn(): return lax.ppermute(value, both_axes, perm)  11.4 us
    ppermute x5, starting transfers between devices, across(): return lax.ppermute(value, 'fsdp', [(i, i ^ 2) for i in range(fsdp_count)])  10 us
    unnamed x29, local copies, waits for them, and re-layouts  7.15 us
  transfers between devices with their start and end apart: 26, of which 11 were waited for; matrix products, arithmetic and copies ran while one was open for 8% of the time, Pallas kernels for 29%

profile of v6, /device:TPU:0, one launch (start us, length us, event | category | flops | bytes accessed | tf_op | source)
XLA Modules:
  0.0 194.3 jit_solution(15663876564948078802)
XLA Ops:
  0.6 0.5 collective-permute-start
  1.1 0.6 pad_add_fusion.1.idx_ref
  1.7 3.0 %cut_tokens.1 = (bf16[64,4096]{1,0:T(8,128)(2,1)}, bf16[64,4096]{1,0:T(8,128)(2,1)}) custom-call(s32[3]{0:T(128)} %pad_add_fusion.1.idx_ref, bf16[128,8192]{1,0:T(8,128)(2,1)} %refs_11_.1, bf16[128,8192]{1,0:T(8,128)(2,1)} %refs_11_.1), custom_call_target="tpu_custom_call" | custom-call | flops 1 | bytes 1 | tf_op jit(solution)/shard_map/cut_tokens/pallas_call | solution.py:314
  4.8 2.5 %collective-permute-start.1 = (bf16[64,4096]{1,0:T(8,128)(2,1)}, bf16[64,4096]{1,0:T(8,128)(2,1)S(1)}, u32[]{:S(2)}, u32[]{:S(2)}) collective-permute-start(bf16[64,4096]{1,0:T(8,128)(2,1)} %get-tuple-element.35), channel_id=1, source_target_pairs={{0,8},{4,12},{8,0},{12,4},{1,9},{5,13},{9,1},{13,5},{2,10},{6,14},... | collective-permute-start | bytes 1572872 | tf_op jit(solution)/shard_map/ppermute | solution.py:660
  7.3 0.1 concatenate.29.idx_ref
  7.4 10.1 %gate_up_products.3 = (bf16[1,2,128,1792]{3,2,1,0:T(8,128)(2,1)S(1)}, bf16[1,2,128,1792]{3,2,1,0:T(8,128)(2,1)S(1)}) custom-call(s32[5]{0:T(128)S(1)} %concatenate.29.idx_ref, bf16[128,8192]{1,0:T(8,128)(2,1)S(1)} %copy-done, bf16[128,8192]{1,0:T(8,128)(2,1)S(1)} %copy-done, bf16[128,8192]{1,0:T(8,128)(2,1)} %collective-permute-done.refs_2_.refs_3_.refs_12_.refs_13_, ...), custom_call_target="tpu_custom_call" | custom-call | flops 1 | bytes 1 | tf_op jit(solution)/shard_map/gate_up_products/pallas_call | solution.py:359
  17.5 2.6 %collective-permute-done.1.refs_0_.refs_4_.refs_14_ = bf16[64,4096]{1,0:T(8,128)(2,1)S(1)} collective-permute-done((bf16[64,4096]{1,0:T(8,128)(2,1)}, bf16[64,4096]{1,0:T(8,128)(2,1)S(1)}, u32[]{:S(2)}, u32[]{:S(2)}) %collective-permute-start.1) | collective-permute-done | bytes 524320 | tf_op jit(solution)/shard_map/ppermute | solution.py:660
  20.0 1.8 collective-permute-start.5
  21.9 0.6 collective-permute-done.2
  22.5 1.1 fusion.1
  23.7 1.7 collective-permute-start.8
  25.4 9.1 %collective-permute-done.5.refs_1_.refs_5_.refs_15_ = bf16[64,4096]{1,0:T(8,128)(2,1)S(1)} collective-permute-done((bf16[64,4096]{1,0:T(8,128)(2,1)S(1)}, bf16[64,4096]{1,0:T(8,128)(2,1)S(1)}, u32[]{:S(2)}, u32[]{:S(2)}) %collective-permute-start.5) | collective-permute-done | bytes 524320 | tf_op jit(solution)/shard_map/ppermute | solution.py:663
  34.5 1.7 collective-permute-start.9
  36.1 1.7 reshape.34
  37.8 1.6 collective-permute-start.4
  39.4 2.9 %collective-permute-done.4 = bf16[1,256,128]{2,1,0:T(8,128)(2,1)S(1)} collective-permute-done((bf16[1,256,128]{2,1,0:T(8,128)(2,1)}, bf16[1,256,128]{2,1,0:T(8,128)(2,1)S(1)}, u32[]{:S(2)}, u32[]{:S(2)}) %collective-permute-start.4) | collective-permute-done | bytes 65568 | tf_op jit(solution)/shard_map/ppermute | solution.py:663
  42.3 1.6 collective-permute-start.3
  43.8 1.5 constant_dynamic-update-slice_fusion.1
  45.3 0.6 constant_dynamic-update-slice_fusion
  45.9 0.6 copy-done.11
  46.6 10.0 %gate_up_products.4 = (bf16[1,2,128,1792]{3,2,1,0:T(8,128)(2,1)S(1)}, bf16[1,2,128,1792]{3,2,1,0:T(8,128)(2,1)S(1)}) custom-call(s32[5]{0:T(128)S(1)} %concatenate.29.idx_ref, bf16[64,4096]{1,0:T(8,128)(2,1)S(1)} %collective-permute-done.1.refs_0_.refs_4_.refs_14_, bf16[64,4096]{1,0:T(8,128)(2,1)S(1)} %collective-permute-done.5.refs_1_.refs_5_.refs_15_, ...), custom_call_target="tpu_custom_call" | custom-call | flops 1 | bytes 1 | tf_op jit(solution)/shard_map/gate_up_products/pallas_call | solution.py:359
  56.6 3.1 %collective-permute-done.9.refs_4_.refs_18_ = bf16[64,4096]{1,0:T(8,128)(2,1)S(1)} collective-permute-done((bf16[64,4096]{1,0:T(8,128)(2,1)}, bf16[64,4096]{1,0:T(8,128)(2,1)S(1)}, u32[]{:S(2)}, u32[]{:S(2)}) %collective-permute-start.9) | collective-permute-done | bytes 524320 | tf_op jit(solution)/shard_map/ppermute | solution.py:660
  59.8 6.4 %collective-permute-start.13 = (bf16[2,256,128]{2,1,0:T(8,128)(2,1)}, bf16[2,256,128]{2,1,0:T(8,128)(2,1)}, u32[]{:S(2)}, u32[]{:S(2)}) collective-permute-start(bf16[2,256,128]{2,1,0:T(8,128)(2,1)} %constant_dynamic-update-slice_fusion), channel_id=1, source_target_pairs={{0,2},{1,3},{2,0},{3,1},{4,6},{5,7},{6,4},{7,5},{8,10},{9,11},{10,... | collective-permute-start | bytes 393224 | tf_op jit(solution)/shard_map/ppermute | solution.py:663
  66.2 1.2 fusion
  67.4 2.3 %collective-permute-start.11 = (bf16[2,128,1792]{2,1,0:T(8,128)(2,1)}, bf16[2,128,1792]{2,1,0:T(8,128)(2,1)}, u32[]{:S(2)}, u32[]{:S(2)}) collective-permute-start(bf16[2,128,1792]{2,1,0:T(8,128)(2,1)} %fusion), channel_id=1, source_target_pairs={{0,8},{4,12},{8,0},{12,4},{1,9},{5,13},{9,1},{13,5},{2,10},{6,14},... | collective-permute-start | bytes 2752520 | tf_op jit(solution)/shard_map/ppermute | solution.py:660
  69.8 0.5 collective-permute-start.12
  70.3 13.2 %gate_up_products.5 = (bf16[2,2,128,1792]{3,2,1,0:T(8,128)(2,1)S(1)}, bf16[2,2,128,1792]{3,2,1,0:T(8,128)(2,1)}) custom-call(s32[5]{0:T(128)S(1)} %concatenate.28.idx_ref, bf16[128,8192]{1,0:T(8,128)(2,1)} %refs_11_.1, bf16[128,8192]{1,0:T(8,128)(2,1)} %refs_11_.1, bf16[128,8192]{1,0:T(8,128)(2,1)} %collective-permute-done.refs_2_.refs_3_.refs_12_.refs_13_, ...), custom_call_target="tpu_custom_call" | custom-call | flops 1 | bytes 1 | tf_op jit(solution)/shard_map/gate_up_products/pallas_call | solution.py:359
  83.6 1.2 copy-done.2
  84.8 1.0 pad_maximum_fusion.1
  85.8 0.2 reshape_reshape.3
  86.0 0.1 reverse_select_fusion.1
  86.2 0.1 reverse_select_fusion
  86.3 1.0 copy.14.left_ref
  87.4 2.2 %spread_left.1.refs_5_.refs_9_ = bf16[8,256,256]{2,1,0:T(8,128)(2,1)} custom-call(bf16[32,64,64]{2,1,0:T(8,128)(2,1)} %copy.14.left_ref), custom_call_target="tpu_custom_call" | custom-call | flops 1 | bytes 1 | tf_op jit(solution)/shard_map/spread_left/pallas_call | solution.py:418
  89.6 1.0 constant_dynamic-update-slice_fusion.5
  90.6 0.1 collective-permute-done.11
  90.7 0.5 collective-permute-start.19
  91.2 1.8 collective-permute-start.17
  93.0 1.9 collective-permute-start.18
  94.9 0.5 collective-permute-done.14
  95.4 2.6 %bitcast_add_fusion.1 = (f32[2,128,1792]{2,1,0:T(8,128)S(1)}, f32[2,128,1792]{2,1,0:T(8,128)S(1)}) fusion(bf16[2,128,1792]{2,1,0:T(8,128)(2,1)} %collective-permute-done.11, bf16[2,2,128,1792]{3,2,1,0:T(8,128)(2,1)S(1)} %collective-permute-done.14, bf16[2,2,128,1792]{3,2,1,0:T(8,128)(2,1)} %copy-done.2, bf16[2,128,1792]{2,1,0:T(8,128)(2,1)} %copy-done.6), kind=kLoop, calls=%fused_computation.5 | loop fusion | flops 4587520 | bytes 9175040 | tf_op jit(solution)/shard_map/add | solution.py:679
  98.0 0.6 fusion.2
  98.6 0.1 pad_maximum_fusion.refs_0_
  98.7 1.8 collective-permute-start.16
  100.5 11.2 %collective-permute-done.18.refs_5_.refs_19_ = bf16[64,4096]{1,0:T(8,128)(2,1)S(1)} collective-permute-done((bf16[64,4096]{1,0:T(8,128)(2,1)S(1)}, bf16[64,4096]{1,0:T(8,128)(2,1)S(1)}, u32[]{:S(2)}, u32[]{:S(2)}) %collective-permute-start.18) | collective-permute-done | bytes 524320 | tf_op jit(solution)/shard_map/ppermute | solution.py:663
  111.7 8.7 %student_part.2 = (bf16[8,256,256]{2,1,0:T(8,128)(2,1)S(1)}, f32[256,2048]{1,0:T(8,128)}) custom-call(s32[4]{0:T(128)S(1)} %pad_add_fusion.idx_ref, bf16[128,8192]{1,0:T(8,128)(2,1)} %refs_11_.1, bf16[128,8192]{1,0:T(8,128)(2,1)} %refs_11_.1, bf16[128,8192]{1,0:T(8,128)(2,1)} %collective-permute-done.refs_2_.refs_3_.refs_12_.refs_13_, ...), custom_call_target="tpu_custom_call" | custom-call | flops 10000000000 | bytes 10000000 | tf_op jit(solution)/shard_map/student_part/pallas_call | solution.py:505
  120.5 1.0 copy-done.3
  121.5 0.8 copy-done.10
  122.3 9.6 %student_part.3 = (bf16[8,256,256]{2,1,0:T(8,128)(2,1)}, f32[256,2048]{1,0:T(8,128)}) custom-call(s32[4]{0:T(128)S(1)} %pad_add_fusion.idx_ref, bf16[64,4096]{1,0:T(8,128)(2,1)S(1)} %collective-permute-done.1.refs_0_.refs_4_.refs_14_, bf16[64,4096]{1,0:T(8,128)(2,1)S(1)} %collective-permute-done.5.refs_1_.refs_5_.refs_15_, ...), custom_call_target="tpu_custom_call" | custom-call | flops 10000000000 | bytes 10000000 | tf_op jit(solution)/shard_map/student_part/pallas_call | solution.py:505
  131.9 0.6 collective-permute-start.21
  132.5 2.1 %collective-permute-done.21.refs_3_ = bf16[2,128,1792]{2,1,0:T(8,128)(2,1)S(1)} collective-permute-done((bf16[2,128,1792]{2,1,0:T(8,128)(2,1)S(1)}, bf16[2,128,1792]{2,1,0:T(8,128)(2,1)S(1)}, u32[]{:S(2)}, u32[]{:S(2)}) %collective-permute-start.21) | collective-permute-done | bytes 917536 | tf_op jit(solution)/shard_map/ppermute | solution.py:657
  134.6 1.0 copy-done.9
  135.6 25.6 %factor_grads.1 = bf16[4,768,128]{2,1,0:T(8,128)(2,1)} custom-call(s32[4]{0:T(128)S(1)} %pad_add_fusion.idx_ref, bf16[2,128,1792]{2,1,0:T(8,128)(2,1)} %copy-done.5, bf16[2,128,1792]{2,1,0:T(8,128)(2,1)} %copy-done.8, bf16[2,128,1792]{2,1,0:T(8,128)(2,1)} %copy-done.7, bf16[2,128,1792]{2,1,0:T(8,128)(2,1)} %copy-done.9, bf16[3584,2048]{1,0:T(8,128)(2,1)} %refs_4_.5, ...), custom_call_target="tpu_custom_call" | custom-call | flops 1 | bytes 1 | tf_op jit(solution)/shard_map/factor_grads/pallas_call | solution.py:618
  161.2 1.0 slice.63
  162.2 1.0 collective-permute-start.22
  163.2 10.5 %collective-permute-done.22 = bf16[2,768,128]{2,1,0:T(8,128)(2,1)S(1)} collective-permute-done((bf16[2,768,128]{2,1,0:T(8,128)(2,1)S(1)}, bf16[2,768,128]{2,1,0:T(8,128)(2,1)S(1)}, u32[]{:S(2)}, u32[]{:S(2)}) %collective-permute-start.22) | collective-permute-done | bytes 393248 | tf_op jit(solution)/shard_map/ppermute | solution.py:663
  173.7 1.1 add_convert_fusion
  174.8 1.6 collective-permute-start.25
  176.4 0.7 collective-permute-start.23
  177.1 4.2 %collective-permute-start.24 = (bf16[512,128]{1,0:T(8,128)(2,1)S(1)}, bf16[512,128]{1,0:T(8,128)(2,1)S(1)}, u32[]{:S(2)}, u32[]{:S(2)}) collective-permute-start(bf16[512,128]{1,0:T(8,128)(2,1)S(1)} %get-tuple-element.67), channel_id=1, source_target_pairs={{0,8},{1,12},{2,0},{3,4},{4,9},{5,13},{6,1},{7,5},{8,10},{9,14},{1... | collective-permute-start | bytes 393224 | tf_op jit(solution)/shard_map/ppermute | solution.py:670
  181.3 0.2 reshape.38
  181.5 0.7 copy.15
  182.2 11.4 %collective-permute-done.24 = bf16[512,128]{1,0:T(8,128)(2,1)S(1)} collective-permute-done((bf16[512,128]{1,0:T(8,128)(2,1)S(1)}, bf16[512,128]{1,0:T(8,128)(2,1)S(1)}, u32[]{:S(2)}, u32[]{:S(2)}) %collective-permute-start.24) | collective-permute-done | bytes 131104 | tf_op jit(solution)/shard_map/ppermute | solution.py:670
  193.6 0.7 convert_add_fusion.2
  (51 shorter events, 0.5 us)
Async XLA Ops:
  0.6 6.7 %collective-permute-start = (bf16[128,8192]{1,0:T(8,128)(2,1)}, bf16[128,8192]{1,0:T(8,128)(2,1)}, u32[]{:S(2)}, u32[]{:S(2)}) collective-permute-start(bf16[128,8192]{1,0:T(8,128)(2,1)} %refs_11_.1), channel_id=1, source_target_pairs={{0,4},{4,0},{8,12},{12,8},{1,5},{5,1},{9,13},{13,9},{2,6},{6,2},{1... | collective-permute-start | bytes 6291464 | tf_op jit(solution)/shard_map/ppermute | solution.py:657
  1.7 5.6 %copy-start = (bf16[128,8192]{1,0:T(8,128)(2,1)S(1)}, bf16[128,8192]{1,0:T(8,128)(2,1)}, u32[]{:S(2)}) copy-start(bf16[128,8192]{1,0:T(8,128)(2,1)} %refs_11_.1) | copy-start | bytes 6291460
  4.8 15.3 %collective-permute-start.1 = (bf16[64,4096]{1,0:T(8,128)(2,1)}, bf16[64,4096]{1,0:T(8,128)(2,1)S(1)}, u32[]{:S(2)}, u32[]{:S(2)}) collective-permute-start(bf16[64,4096]{1,0:T(8,128)(2,1)} %get-tuple-element.35), channel_id=1, source_target_pairs={{0,8},{4,12},{8,0},{12,4},{1,9},{5,13},{9,1},{13,5},{2,10},{6,14},... | collective-permute-start | bytes 1572872 | tf_op jit(solution)/shard_map/ppermute | solution.py:660
  20.0 2.5 %collective-permute-start.2 = (bf16[2,128,1792]{2,1,0:T(8,128)(2,1)S(1)}, bf16[2,128,1792]{2,1,0:T(8,128)(2,1)S(1)}, u32[]{:S(2)}, u32[]{:S(2)}) collective-permute-start(bf16[2,128,1792]{2,1,0:T(8,128)(2,1)S(1)} %bitcast.41), channel_id=1, source_target_pairs={{0,4},{4,0},{8,12},{12,8},{1,5},{5,1},{9,13},{13,9},{2,6},{6,2},{1... | collective-permute-start | bytes 2752520 | tf_op jit(solution)/shard_map/ppermute | solution.py:657
  20.0 14.4 %collective-permute-start.5 = (bf16[64,4096]{1,0:T(8,128)(2,1)S(1)}, bf16[64,4096]{1,0:T(8,128)(2,1)S(1)}, u32[]{:S(2)}, u32[]{:S(2)}) collective-permute-start(bf16[64,4096]{1,0:T(8,128)(2,1)S(1)} %collective-permute-done.1.refs_0_.refs_4_.refs_14_), channel_id=1, source_target_pairs={{0,1},{1,0},{2,3},{3,2},{4,5},{5,4},{6,7},{7,6},{8,9},{9,8},{10,11... | collective-permute-start | bytes 1572872 | tf_op jit(solution)/shard_map/ppermute | solution.py:663
  23.7 36.0 %collective-permute-start.8 = (bf16[2,128,1792]{2,1,0:T(8,128)(2,1)}, bf16[2,128,1792]{2,1,0:T(8,128)(2,1)S(1)}, u32[]{:S(2)}, u32[]{:S(2)}) collective-permute-start(bf16[2,128,1792]{2,1,0:T(8,128)(2,1)} %fusion.1), channel_id=1, source_target_pairs={{0,8},{4,12},{8,0},{12,4},{1,9},{5,13},{9,1},{13,5},{2,10},{6,14},... | collective-permute-start | bytes 2752520 | tf_op jit(solution)/shard_map/ppermute | solution.py:660
  25.4 20.5 %collective-permute-start.6 = (bf16[64,4096]{1,0:T(8,128)(2,1)S(1)}, bf16[64,4096]{1,0:T(8,128)(2,1)S(1)}, u32[]{:S(2)}, u32[]{:S(2)}) collective-permute-start(bf16[64,4096]{1,0:T(8,128)(2,1)S(1)} %collective-permute-done.1.refs_0_.refs_4_.refs_14_), channel_id=1, source_target_pairs={{0,4},{4,0},{8,12},{12,8},{1,5},{5,1},{9,13},{13,9},{2,6},{6,2},{1... | collective-permute-start | bytes 1572872 | tf_op jit(solution)/shard_map/ppermute | solution.py:657
  34.5 12.1 %collective-permute-start.7 = (bf16[64,4096]{1,0:T(8,128)(2,1)S(1)}, bf16[64,4096]{1,0:T(8,128)(2,1)S(1)}, u32[]{:S(2)}, u32[]{:S(2)}) collective-permute-start(bf16[64,4096]{1,0:T(8,128)(2,1)S(1)} %collective-permute-done.5.refs_1_.refs_5_.refs_15_), channel_id=1, source_target_pairs={{0,4},{4,0},{8,12},{12,8},{1,5},{5,1},{9,13},{13,9},{2,6},{6,2},{1... | collective-permute-start | bytes 1572872 | tf_op jit(solution)/shard_map/ppermute | solution.py:657
  34.5 25.2 %collective-permute-start.9 = (bf16[64,4096]{1,0:T(8,128)(2,1)}, bf16[64,4096]{1,0:T(8,128)(2,1)S(1)}, u32[]{:S(2)}, u32[]{:S(2)}) collective-permute-start(bf16[64,4096]{1,0:T(8,128)(2,1)} %get-tuple-element.44), channel_id=1, source_target_pairs={{0,8},{4,12},{8,0},{12,4},{1,9},{5,13},{9,1},{13,5},{2,10},{6,14},... | collective-permute-start | bytes 1572872 | tf_op jit(solution)/shard_map/ppermute | solution.py:660
  37.8 4.5 %collective-permute-start.4 = (bf16[1,256,128]{2,1,0:T(8,128)(2,1)}, bf16[1,256,128]{2,1,0:T(8,128)(2,1)S(1)}, u32[]{:S(2)}, u32[]{:S(2)}) collective-permute-start(bf16[1,256,128]{2,1,0:T(8,128)(2,1)} %reshape.34), channel_id=1, source_target_pairs={{0,1},{1,0},{2,3},{3,2},{4,5},{5,4},{6,7},{7,6},{8,9},{9,8},{10,11... | collective-permute-start | bytes 196616 | tf_op jit(solution)/shard_map/ppermute | solution.py:663
  42.3 3.7 %collective-permute-start.3 = (bf16[16,32,128]{2,1,0:T(8,128)(2,1)}, bf16[16,32,128]{2,1,0:T(8,128)(2,1)S(1)}, u32[]{:S(2)}, u32[]{:S(2)}) collective-permute-start(bf16[16,32,128]{2,1,0:T(8,128)(2,1)} %param.10), channel_id=1, source_target_pairs={{0,0},{1,4},{2,8},{3,12},{4,1},{5,5},{6,9},{7,13},{8,2},{9,6},{10,... | collective-permute-start | bytes 393224 | tf_op jit(solution)/shard_map/ppermute | solution.py:670
  45.9 0.7 copy-start.11
  59.7 23.9 %copy-start.6 = (bf16[2,128,1792]{2,1,0:T(8,128)(2,1)}, bf16[2,128,1792]{2,1,0:T(8,128)(2,1)S(1)}, u32[]{:S(2)}) copy-start(bf16[2,128,1792]{2,1,0:T(8,128)(2,1)S(1)} %collective-permute-done.8) | copy-start | bytes 2752516
  59.7 6.5 %collective-permute-start.10 = (bf16[2,128,1792]{2,1,0:T(8,128)(2,1)S(1)}, bf16[2,128,1792]{2,1,0:T(8,128)(2,1)S(1)}, u32[]{:S(2)}, u32[]{:S(2)}) collective-permute-start(bf16[2,128,1792]{2,1,0:T(8,128)(2,1)S(1)} %bitcast.40), channel_id=1, source_target_pairs={{0,4},{4,0},{8,12},{12,8},{1,5},{5,1},{9,13},{13,9},{2,6},{6,2},{1... | collective-permute-start | bytes 2752520 | tf_op jit(solution)/shard_map/ppermute | solution.py:657
  59.8 25.0 %collective-permute-start.13 = (bf16[2,256,128]{2,1,0:T(8,128)(2,1)}, bf16[2,256,128]{2,1,0:T(8,128)(2,1)}, u32[]{:S(2)}, u32[]{:S(2)}) collective-permute-start(bf16[2,256,128]{2,1,0:T(8,128)(2,1)} %constant_dynamic-update-slice_fusion), channel_id=1, source_target_pairs={{0,2},{1,3},{2,0},{3,1},{4,6},{5,7},{6,4},{7,5},{8,10},{9,11},{10,... | collective-permute-start | bytes 393224 | tf_op jit(solution)/shard_map/ppermute | solution.py:663
  67.4 23.3 %collective-permute-start.11 = (bf16[2,128,1792]{2,1,0:T(8,128)(2,1)}, bf16[2,128,1792]{2,1,0:T(8,128)(2,1)}, u32[]{:S(2)}, u32[]{:S(2)}) collective-permute-start(bf16[2,128,1792]{2,1,0:T(8,128)(2,1)} %fusion), channel_id=1, source_target_pairs={{0,8},{4,12},{8,0},{12,4},{1,9},{5,13},{9,1},{13,5},{2,10},{6,14},... | collective-permute-start | bytes 2752520 | tf_op jit(solution)/shard_map/ppermute | solution.py:660
  69.8 19.8 %collective-permute-start.12 = (bf16[1,16,32,128]{3,2,1,0:T(8,128)(2,1)}, bf16[1,16,32,128]{3,2,1,0:T(8,128)(2,1)}, u32[]{:S(2)}, u32[]{:S(2)}) collective-permute-start(bf16[1,16,32,128]{3,2,1,0:T(8,128)(2,1)} %bitcast.47), channel_id=1, source_target_pairs={{0,1},{1,0},{2,3},{3,2},{4,5},{5,4},{6,7},{7,6},{8,9},{9,8},{10,11... | collective-permute-start | bytes 393224 | tf_op jit(solution)/shard_map/ppermute | solution.py:663
  83.5 1.2 copy-start.2
  86.2 1.2 copy-start.12
  90.7 4.7 %collective-permute-start.14 = (bf16[2,2,128,1792]{3,2,1,0:T(8,128)(2,1)}, bf16[2,2,128,1792]{3,2,1,0:T(8,128)(2,1)S(1)}, u32[]{:S(2)}, u32[]{:S(2)}) collective-permute-start(bf16[2,2,128,1792]{3,2,1,0:T(8,128)(2,1)} %get-tuple-element.53), channel_id=1, source_target_pairs={{0,4},{4,0},{8,12},{12,8},{1,5},{5,1},{9,13},{13,9},{2,6},{6,2},{1... | collective-permute-start | bytes 5505032 | tf_op jit(solution)/shard_map/ppermute | solution.py:657
  90.7 30.7 %collective-permute-start.19 = (bf16[64,4096]{1,0:T(8,128)(2,1)S(1)}, bf16[64,4096]{1,0:T(8,128)(2,1)S(1)}, u32[]{:S(2)}, u32[]{:S(2)}) collective-permute-start(bf16[64,4096]{1,0:T(8,128)(2,1)S(1)} %collective-permute-done.9.refs_4_.refs_18_), channel_id=1, source_target_pairs={{0,4},{4,0},{8,12},{12,8},{1,5},{5,1},{9,13},{13,9},{2,6},{6,2},{1... | collective-permute-start | bytes 1572872 | tf_op jit(solution)/shard_map/ppermute | solution.py:657
  91.2 20.4 %collective-permute-start.17 = (bf16[2,16,32,128]{3,2,1,0:T(8,128)(2,1)S(1)}, bf16[2,16,32,128]{3,2,1,0:T(8,128)(2,1)S(1)}, u32[]{:S(2)}, u32[]{:S(2)}) collective-permute-start(bf16[2,16,32,128]{3,2,1,0:T(8,128)(2,1)S(1)} %get-tuple-element.69), channel_id=1, source_target_pairs={{0,2},{1,3},{2,0},{3,1},{4,6},{5,7},{6,4},{7,5},{8,10},{9,11},{10,... | collective-permute-start | bytes 786440 | tf_op jit(solution)/shard_map/ppermute | solution.py:663
  93.0 18.7 %collective-permute-start.18 = (bf16[64,4096]{1,0:T(8,128)(2,1)S(1)}, bf16[64,4096]{1,0:T(8,128)(2,1)S(1)}, u32[]{:S(2)}, u32[]{:S(2)}) collective-permute-start(bf16[64,4096]{1,0:T(8,128)(2,1)S(1)} %collective-permute-done.9.refs_4_.refs_18_), channel_id=1, source_target_pairs={{0,1},{1,0},{2,3},{3,2},{4,5},{5,4},{6,7},{7,6},{8,9},{9,8},{10,11... | collective-permute-start | bytes 1572872 | tf_op jit(solution)/shard_map/ppermute | solution.py:663
  98.6 13.2 %copy-start.1 = (bf16[8,256,256]{2,1,0:T(8,128)(2,1)S(1)}, bf16[8,256,256]{2,1,0:T(8,128)(2,1)}, u32[]{:S(2)}) copy-start(bf16[8,256,256]{2,1,0:T(8,128)(2,1)} %spread_left.1.refs_5_.refs_9_) | copy-start | bytes 3145732
  98.7 21.8 %copy-start.5 = (bf16[2,128,1792]{2,1,0:T(8,128)(2,1)}, bf16[2,128,1792]{2,1,0:T(8,128)(2,1)S(1)}, u32[]{:S(2)}) copy-start(bf16[2,128,1792]{2,1,0:T(8,128)(2,1)S(1)} %pad_maximum_fusion.refs_0_) | copy-start | bytes 2752516
  98.7 33.2 %collective-permute-start.16 = (bf16[2,128,1792]{2,1,0:T(8,128)(2,1)S(1)}, bf16[2,128,1792]{2,1,0:T(8,128)(2,1)S(1)}, u32[]{:S(2)}, u32[]{:S(2)}) collective-permute-start(bf16[2,128,1792]{2,1,0:T(8,128)(2,1)S(1)} %pad_maximum_fusion.refs_0_), channel_id=1, source_target_pairs={{0,8},{4,12},{8,0},{12,4},{1,9},{5,13},{9,1},{13,5},{2,10},{6,14},... | collective-permute-start | bytes 2752520 | tf_op jit(solution)/shard_map/ppermute | solution.py:660
  100.5 32.0 %collective-permute-start.15 = (bf16[2,128,1792]{2,1,0:T(8,128)(2,1)S(1)}, bf16[2,128,1792]{2,1,0:T(8,128)(2,1)S(1)}, u32[]{:S(2)}, u32[]{:S(2)}) collective-permute-start(bf16[2,128,1792]{2,1,0:T(8,128)(2,1)S(1)} %pad_maximum_fusion.refs_0_), channel_id=1, source_target_pairs={{0,4},{4,0},{8,12},{12,8},{1,5},{5,1},{9,13},{13,9},{2,6},{6,2},{1... | collective-permute-start | bytes 2752520 | tf_op jit(solution)/shard_map/ppermute | solution.py:657
  111.7 9.8 %collective-permute-start.20 = (bf16[64,4096]{1,0:T(8,128)(2,1)S(1)}, bf16[64,4096]{1,0:T(8,128)(2,1)S(1)}, u32[]{:S(2)}, u32[]{:S(2)}) collective-permute-start(bf16[64,4096]{1,0:T(8,128)(2,1)S(1)} %collective-permute-done.18.refs_5_.refs_19_), channel_id=1, source_target_pairs={{0,4},{4,0},{8,12},{12,8},{1,5},{5,1},{9,13},{13,9},{2,6},{6,2},{1... | collective-permute-start | bytes 1572872 | tf_op jit(solution)/shard_map/ppermute | solution.py:657
  111.7 8.8 %copy-start.4 = (bf16[4,16,32,128]{3,2,1,0:T(8,128)(2,1)}, bf16[4,16,32,128]{3,2,1,0:T(8,128)(2,1)S(1)}, u32[]{:S(2)}) copy-start(bf16[4,16,32,128]{3,2,1,0:T(8,128)(2,1)S(1)} %constant_dynamic-update-slice_fusion.4.refs_4_.refs_8_) | copy-start | bytes 1572868
  120.5 1.0 copy-start.3
  121.5 0.8 copy-start.10
  131.9 2.7 %copy-start.7 = (bf16[2,128,1792]{2,1,0:T(8,128)(2,1)}, bf16[2,128,1792]{2,1,0:T(8,128)(2,1)S(1)}, u32[]{:S(2)}) copy-start(bf16[2,128,1792]{2,1,0:T(8,128)(2,1)S(1)} %collective-permute-done.16.refs_2_) | copy-start | bytes 2752516
  131.9 2.7 %collective-permute-start.21 = (bf16[2,128,1792]{2,1,0:T(8,128)(2,1)S(1)}, bf16[2,128,1792]{2,1,0:T(8,128)(2,1)S(1)}, u32[]{:S(2)}, u32[]{:S(2)}) collective-permute-start(bf16[2,128,1792]{2,1,0:T(8,128)(2,1)S(1)} %collective-permute-done.16.refs_2_), channel_id=1, source_target_pairs={{0,4},{4,0},{8,12},{12,8},{1,5},{5,1},{9,13},{13,9},{2,6},{6,2},{1... | collective-permute-start | bytes 2752520 | tf_op jit(solution)/shard_map/ppermute | solution.py:657
  132.5 2.1 %copy-start.8 = (bf16[2,128,1792]{2,1,0:T(8,128)(2,1)}, bf16[2,128,1792]{2,1,0:T(8,128)(2,1)S(1)}, u32[]{:S(2)}) copy-start(bf16[2,128,1792]{2,1,0:T(8,128)(2,1)S(1)} %collective-permute-done.15.refs_1_) | copy-start | bytes 2752516
  134.6 1.0 copy-start.9
  162.2 11.5 %collective-permute-start.22 = (bf16[2,768,128]{2,1,0:T(8,128)(2,1)S(1)}, bf16[2,768,128]{2,1,0:T(8,128)(2,1)S(1)}, u32[]{:S(2)}, u32[]{:S(2)}) collective-permute-start(bf16[2,768,128]{2,1,0:T(8,128)(2,1)S(1)} %slice.63), channel_id=1, source_target_pairs={{0,1},{1,0},{2,3},{3,2},{4,5},{5,4},{6,7},{7,6},{8,9},{9,8},{10,11... | collective-permute-start | bytes 1179656 | tf_op jit(solution)/shard_map/ppermute | solution.py:663
  174.8 6.4 %collective-permute-start.25 = (bf16[256,128]{1,0:T(8,128)(2,1)S(1)}, bf16[256,128]{1,0:T(8,128)(2,1)S(1)}, u32[]{:S(2)}, u32[]{:S(2)}) collective-permute-start(bf16[256,128]{1,0:T(8,128)(2,1)S(1)} %slice_bitcast_fusion.2), channel_id=1, source_target_pairs={{0,2},{1,3},{2,0},{3,1},{4,6},{5,7},{6,4},{7,5},{8,10},{9,11},{10,... | collective-permute-start | bytes 196616 | tf_op jit(solution)/shard_map/ppermute | solution.py:663
  176.4 5.8 %collective-permute-start.23 = (bf16[512,128]{1,0:T(8,128)(2,1)S(1)}, bf16[512,128]{1,0:T(8,128)(2,1)S(1)}, u32[]{:S(2)}, u32[]{:S(2)}) collective-permute-start(bf16[512,128]{1,0:T(8,128)(2,1)S(1)} %get-tuple-element.66), channel_id=1, source_target_pairs={{0,0},{1,4},{2,8},{3,12},{4,1},{5,5},{6,9},{7,13},{8,2},{9,6},{10,... | collective-permute-start | bytes 393224 | tf_op jit(solution)/shard_map/ppermute | solution.py:670
  177.1 16.5 %collective-permute-start.24 = (bf16[512,128]{1,0:T(8,128)(2,1)S(1)}, bf16[512,128]{1,0:T(8,128)(2,1)S(1)}, u32[]{:S(2)}, u32[]{:S(2)}) collective-permute-start(bf16[512,128]{1,0:T(8,128)(2,1)S(1)} %get-tuple-element.67), channel_id=1, source_target_pairs={{0,8},{1,12},{2,0},{3,4},{4,9},{5,13},{6,1},{7,5},{8,10},{9,14},{1... | collective-permute-start | bytes 393224 | tf_op jit(solution)/shard_map/ppermute | solution.py:670

commit v7 on v6

--- a/solution.py
+++ b/solution.py
@@ -308,21 +308,22 @@
 
 def cut_tokens(tokens, half, chip):
     rows, model = tokens.shape
-    block = (rows // 2, model // 2)
-    shape = jax.ShapeDtypeStruct(block, BF16)
-    whole = pl.BlockSpec(block, lambda n, s: (0, 0))
+    first, rest = (rows, model // 2), (rows // 2, model // 2)
     return pl.pallas_call(
         cut_kernel,
         grid_spec=pltpu.PrefetchScalarGridSpec(
             num_scalar_prefetch=1,
             grid=(1,),
             in_specs=[
-                pl.BlockSpec(block, lambda n, s: (s[0], s[1])),
-                pl.BlockSpec(block, lambda n, s: (s[0], s[2])),
+                pl.BlockSpec(first, lambda n, s: (0, s[1])),
+                pl.BlockSpec(rest, lambda n, s: (s[0], s[2])),
             ],
-            out_specs=[whole, whole],
-        ),
-        out_shape=[shape, shape],
+            out_specs=[
+                pl.BlockSpec(first, lambda n, s: (0, 0)),
+                pl.BlockSpec(rest, lambda n, s: (0, 0)),
+            ],
+        ),
+        out_shape=[jax.ShapeDtypeStruct(first, BF16), jax.ShapeDtypeStruct(rest, BF16)],
         cost_estimate=SMALL,
         name="cut_tokens",
     )(jnp.stack([half, 1 - chip, chip]).astype(jnp.int32), tokens, tokens)
@@ -342,17 +343,14 @@
 def products(pieces, scalars, gate, up, first, width):
     feat = gate.shape[0]
     sets = len(pieces) // 4
-    half = pieces[0][0].shape[0]
-    half = half // 2 if pieces[0][1] is not None else half
+    half = pieces[0][0].shape[0] // 2
     start = first // BLK
 
     def piece_spec(row, column):
-        if row is None:
-            return pl.BlockSpec((half, feat), lambda n, s: (0, s[column]))
         return pl.BlockSpec((half, feat), lambda n, s: (s[row], s[column]))
 
     weight_spec = pl.BlockSpec(
-        (feat, BLK), lambda n, s: (0, s[4] + start + n), pipeline_mode=pl.Buffered(2)
+        (feat, BLK), lambda n, s: (0, s[4] + start + n)
     )
     out_spec = pl.BlockSpec((sets, 2, 2 * half, BLK), lambda n, s: (0, 0, 0, n))
     shape = jax.ShapeDtypeStruct((sets, 2, 2 * half, width), BF16)
@@ -373,14 +371,14 @@
 
 
 def fill_rows(lhs, pieces, chip):
-    own, near, got, near_got = pieces
-    rows, width = own.shape[1:]
+    rows, width = pieces[0].shape
     for u in range(2):
-        for part, (mine, other) in enumerate(((own, near), (got, near_got))):
+        for part in range(2):
             begin = pl.multiple_of(lax.rem(chip + part, 2) * width, LANES)
-            which = u if part == 0 else 1 - u
-            lhs[2 * u * rows : (2 * u + 1) * rows, pl.ds(begin, width)] = mine[which]
-            lhs[(2 * u + 1) * rows : (2 * u + 2) * rows, pl.ds(begin, width)] = other[which]
+            which = 4 * part + (u if part == 0 else 1 - u)
+            for core in range(2):
+                row = (2 * u + core) * rows
+                lhs[row : row + rows, pl.ds(begin, width)] = pieces[which + 2 * core][...]
 
 
 def whole_spec(array):
@@ -396,56 +394,74 @@
     return lax.rem(chip + step // per_chip, 2) * per_chip + lax.rem(step, per_chip)
 
 
-def spread_kernel(left_ref, out_ref, scratch):
-    groups, fold = out_ref.shape[0], BLK // left_ref.shape[1]
-    blocks = left_ref.shape[1]
+def spread_kernel(idx_ref, rows_ref, out_ref, scratch):
+    groups = out_ref.shape[0]
+    parts, _, size = rows_ref.shape
+    blocks = size // 2
+    share = blocks // parts
+    fold = BLK // blocks
+    begin = rows_ref.shape[1] - groups * fold // 2 * share
     scratch[...] = jnp.zeros_like(scratch)
-    zeros = jnp.zeros((blocks, blocks), F32)
+    low = lax.broadcasted_iota(jnp.int32, (blocks, size), 1) < blocks
     for g in range(groups):
-        for a in range(fold):
-            value = left_ref[g * fold + a].astype(F32)
-            pair = [value, zeros] if a % 2 == 0 else [zeros, value]
-            wide = jnp.concatenate(pair, axis=1)
-            lanes = slice(a // 2 * LANES, (a // 2 + 1) * LANES)
-            for c in range(blocks // WIDE):
-                row = (c * fold + a) * WIDE
-                scratch[row : row + WIDE, lanes] = wide[c * WIDE : (c + 1) * WIDE]
+        for pair in range(fold // 2):
+            row = begin + (g * (fold // 2) + pair) * share
+            picked = [
+                rows_ref[idx_ref[3] ^ owner, row : row + share, :] for owner in range(parts)
+            ]
+            turned = jnp.concatenate(picked + picked, axis=0).astype(F32).T
+            for a in range(2):
+                value = turned[a * blocks : (a + 1) * blocks]
+                value = jnp.where(low if a == 0 else ~low, value, 0.0)
+                lanes = slice(pair * size, (pair + 1) * size)
+                for c in range(blocks // WIDE):
+                    row = (c * fold + 2 * pair + a) * WIDE
+                    scratch[row : row + WIDE, lanes] = value[c * WIDE : (c + 1) * WIDE]
         out_ref[g] = scratch[...].astype(BF16)
 
 
-def spread_left(left):
-    pairs, blocks, _ = left.shape
+def spread_left(scalars, rows, groups):
     return pl.pallas_call(
         spread_kernel,
-        out_shape=jax.ShapeDtypeStruct((pairs * blocks // BLK, BLK, BLK), BF16),
-        scratch_shapes=[pltpu.VMEM((BLK, BLK), F32)],
+        grid_spec=pltpu.PrefetchScalarGridSpec(
+            num_scalar_prefetch=1,
+            grid=(1,),
+            in_specs=[whole_spec(rows)],
+            out_specs=pl.BlockSpec((groups, BLK, BLK), lambda n, s: (0, 0, 0)),
+            scratch_shapes=[pltpu.VMEM((BLK, BLK), F32)],
+        ),
+        out_shape=jax.ShapeDtypeStruct((groups, BLK, BLK), BF16),
         cost_estimate=SMALL,
         name="spread_left",
-    )(left)
+    )(scalars, rows)
 
 
 def student_kernel(steps, late, tensor_count, idx_ref, *refs):
-    tokens, (right_ref, left_ref, mixed_ref, student_ref, spread) = refs[:-5], refs[-5:]
+    tokens, refs = refs[:-6], refs[-6:]
+    rights, (left_ref, mixed_ref, student_ref, spread) = refs[:2], refs[2:]
     step = pl.program_id(0)
-    chunk = natural(step, idx_ref[2], steps // 2)
+    pair = natural(step, idx_ref[2], steps // 2)
     groups = left_ref.shape[0]
-    pairs = right_ref.shape[2]
+    size = spread.shape[2]
+    pairs = spread.shape[1] // WIDE
     share = BLK // groups
 
     @pl.when(step == 0)
     def _():
         spread[...] = jnp.zeros_like(spread)
 
-    for t in range(WIDE):
-        spread[t, pl.ds(t, pairs, stride=WIDE), :] = right_ref[0, t].astype(F32)
-    factor = jnp.concatenate([spread[t] for t in range(WIDE)], axis=1).astype(BF16)
-
     def mix(pieces):
-        rows = jnp.concatenate([piece[...] for piece in pieces], axis=0)
-        part = lax.dot_general(factor, rows, NT, preferred_element_type=F32).astype(BF16)
-        start = pl.multiple_of(chunk * share, share)
-        for g in range(groups):
-            mixed_ref[g, pl.ds(start, share), :] = part[g * share : (g + 1) * share]
+        for half, right_ref in enumerate(rights):
+            for t in range(WIDE):
+                value = right_ref[0, t * pairs : (t + 1) * pairs, :].astype(F32)
+                spread[t, pl.ds(t, pairs, stride=WIDE), :] = value
+            factor = jnp.concatenate([spread[t] for t in range(WIDE)], axis=1).astype(BF16)
+            lanes = slice(half * WIDE * size, (half + 1) * WIDE * size)
+            rows = jnp.concatenate([piece[:, lanes] for piece in pieces], axis=0)
+            part = lax.dot_general(factor, rows, NT, preferred_element_type=F32).astype(BF16)
+            start = pl.multiple_of((2 * pair + half) * share, share)
+            for g in range(groups):
+                mixed_ref[g, pl.ds(start, share), :] = part[g * share : (g + 1) * share]
 
     if late:
         pl.when(step < steps // 2)(lambda: mix(tokens[:4]))
@@ -468,50 +484,44 @@
         step = jnp.maximum(n - begin, 0)
         return natural(step, s[2], steps // 2)
 
-    if own:
+    def near(n, s):
+        return jnp.clip(n - begin, 0, steps // 2 - 1)
+
+    def far(n, s):
+        return jnp.clip(n - begin - steps // 2, 0, steps // 2 - 1)
+
+    def specs(place):
         return [
-            pl.BlockSpec(
-                (half, width),
-                lambda n, s, p=p: (s[p % 2], chunk(n, s)),
-                pipeline_mode=pl.Buffered(2),
-            )
+            pl.BlockSpec((half, width), lambda n, s, p=p: (s[p % 2], place(n, s)))
             for p in range(4)
         ]
-    near = pl.BlockSpec(
-        (half, width),
-        lambda n, s: (0, jnp.clip(n - begin, 0, steps // 2 - 1)),
-        pipeline_mode=pl.Buffered(2),
-    )
-    far = pl.BlockSpec(
-        (half, width),
-        lambda n, s: (0, jnp.clip(n - begin - steps // 2, 0, steps // 2 - 1)),
-        pipeline_mode=pl.Buffered(2),
-    )
-    return [near] * 4 + [far] * 4
-
-
-def student_part(tokens, late, scalars, right_rows, left_diag, tensor_count):
-    per_owner, pairs, size = right_rows.shape[1:]
-    blocks = right_rows.shape[0] * per_owner
-    steps = blocks // WIDE
-    half = tokens[0].shape[0] if late else tokens[0].shape[0] // 2
-    halves = per_owner // WIDE
-
-    def right_block(n, s):
-        chunk = natural(n, s[2], steps // 2)
-        return (s[3] ^ (chunk // halves), lax.rem(chunk, halves), 0, 0)
-
+
+    if own:
+        return specs(chunk)
+    whole = pl.BlockSpec((half, width), lambda n, s: (0, far(n, s)))
+    return specs(near) + [whole] * 4
+
+
+def student_part(tokens, late, scalars, factors, left_diag, pairs, tensor_count):
+    parts, _, size = factors.shape
+    half = tokens[0].shape[0] // 2
     groups = left_diag.shape[0]
+    blocks = groups * BLK // pairs
+    steps = blocks // (2 * WIDE)
+
+    def right_spec(half):
+        return pl.BlockSpec(
+            (1, WIDE * pairs, size),
+            lambda n, s: (s[3] ^ natural(n, s[2], steps // 2), half, 0),
+        )
+
     return pl.pallas_call(
         functools.partial(student_kernel, steps, late, tensor_count),
         grid_spec=pltpu.PrefetchScalarGridSpec(
             num_scalar_prefetch=1,
             grid=(steps,),
-            in_specs=token_specs(half, WIDE * size, steps, 0, not late)
-            + [
-                pl.BlockSpec((1, WIDE, pairs, size), right_block),
-                whole_spec(left_diag),
-            ],
+            in_specs=token_specs(half, 2 * WIDE * size, steps, 0, not late)
+            + [right_spec(0), right_spec(1), whole_spec(left_diag)],
             out_specs=[
                 pl.BlockSpec((groups, BLK, 4 * half), lambda n, s: (0, 0, 0)),
                 pl.BlockSpec((4 * half, groups * BLK), lambda n, s: (0, 0)),
@@ -527,20 +537,21 @@
             flops=10**10, bytes_accessed=10**7, transcendentals=0
         ),
         name="student_part",
-    )(scalars, *tokens, right_rows, left_diag)
+    )(scalars, *tokens, factors, factors, left_diag)
 
 
 def grads_kernel(groups, steps, scale, idx_ref, *refs):
-    hidden, refs = refs[:4], refs[4:]
+    hidden, refs = refs[:8], refs[8:]
     weight_ref, student0, student1, mixed0, mixed1, left_ref = refs[:6]
     own, near, far = refs[6:10], refs[10:14], refs[14:18]
     out_ref, lhs, back, wide = refs[18:]
     step = pl.program_id(0)
     z = idx_ref[3]
     parts, size = out_ref.shape[0], out_ref.shape[2]
-    blocks = steps * WIDE
+    chunks = 2 * steps
+    blocks = chunks * WIDE
     per_part = blocks // parts
-    share = BLK // steps
+    share = BLK // chunks
     pairs = groups * share // WIDE
     fold = BLK // blocks
 
@@ -561,7 +572,7 @@
             left_ref[0], out_grad, NT, preferred_element_type=F32
         ).astype(BF16)
         row = pl.multiple_of(step * share, share)
-        for c in range(steps):
+        for c in range(chunks):
             back[c, pl.ds(row, share), :] = value[c * share : (c + 1) * share]
         low = lax.broadcasted_iota(jnp.int32, (blocks, size), 1) < blocks
         rows = blocks // parts
@@ -569,7 +580,7 @@
             lanes = slice(pair * size, (pair + 1) * size)
             picked = []
             for a in (2 * pair, 2 * pair + 1):
-                for c in range(steps):
+                for c in range(chunks):
                     begin = (c * fold + a) * WIDE
                     picked.append(left[begin : begin + WIDE, lanes])
             turned = jnp.concatenate(picked, axis=0).T
@@ -582,17 +593,20 @@
                 ]
 
     def right(later):
-        chunk = natural(step - groups, idx_ref[2], steps // 2)
-        rows = jnp.concatenate([piece[...] for piece in own + later], axis=0)
-        value = jnp.dot(back[chunk], rows, preferred_element_type=F32)
-        for t in range(WIDE):
-            wide[t] = value[:, t * size : (t + 1) * size]
-        for t in range(WIDE):
-            block = chunk * WIDE + t
-            begin = pl.multiple_of(lax.rem(block, per_part) * pairs, pairs)
-            out_ref[place(block // per_part), pl.ds(begin, pairs), :] = wide[
-                t, pl.ds(t, pairs, stride=WIDE), :
-            ].astype(BF16)
+        pair = natural(step - groups, idx_ref[2], steps // 2)
+        for half in range(2):
+            chunk = 2 * pair + half
+            lanes = slice(half * WIDE * size, (half + 1) * WIDE * size)
+            rows = jnp.concatenate([piece[:, lanes] for piece in own + later], axis=0)
+            value = jnp.dot(back[chunk], rows, preferred_element_type=F32)
+            for t in range(WIDE):
+                wide[t] = value[:, t * size : (t + 1) * size]
+            for t in range(WIDE):
+                block = chunk * WIDE + t
+                begin = pl.multiple_of(lax.rem(block, per_part) * pairs, pairs)
+                out_ref[place(block // per_part), pl.ds(begin, pairs), :] = wide[
+                    t, pl.ds(t, pairs, stride=WIDE), :
+                ].astype(BF16)
 
     pl.when((step >= groups) & (step < groups + steps // 2))(lambda: right(near))
     pl.when(step >= groups + steps // 2)(lambda: right(far))
@@ -603,17 +617,16 @@
 ):
     groups, count = left_diag.shape[0], 2 * students[0].shape[0]
     width = weight.shape[0]
-    half = late[0].shape[0]
-    steps = own[0].shape[1] // (WIDE * size)
-    blocks = steps * WIDE
+    half = own[0].shape[0] // 2
+    steps = own[0].shape[1] // (2 * WIDE * size)
+    blocks = 2 * steps * WIDE
     pairs = groups * BLK // blocks
-    deep = pl.Buffered(2)
 
     def group(n):
         return jnp.minimum(n, groups - 1)
 
-    column = pl.BlockSpec((count // 2, BLK), lambda n, s: (0, group(n)), pipeline_mode=deep)
-    slab = pl.BlockSpec((1, BLK, count // 2), lambda n, s: (group(n), 0, 0), pipeline_mode=deep)
+    column = pl.BlockSpec((count // 2, BLK), lambda n, s: (0, group(n)))
+    slab = pl.BlockSpec((1, BLK, count // 2), lambda n, s: (group(n), 0, 0))
     out_rows = (pairs * blocks + pairs * blocks * blocks // size) // parts
     return pl.pallas_call(
         functools.partial(grads_kernel, groups, steps, scale),
@@ -621,19 +634,19 @@
             num_scalar_prefetch=1,
             grid=(groups + steps,),
             in_specs=[whole_spec(piece) for piece in hidden]
-            + [pl.BlockSpec((width, BLK), lambda n, s: (0, group(n)), pipeline_mode=deep)]
+            + [pl.BlockSpec((width, BLK), lambda n, s: (0, group(n)))]
             + [column, column, slab, slab]
             + [
                 pl.BlockSpec(
-                    (1, BLK, BLK), lambda n, s: (group(n), 0, 0), pipeline_mode=deep
+                    (1, BLK, BLK), lambda n, s: (group(n), 0, 0)
                 )
             ]
-            + token_specs(half, WIDE * size, steps, groups, True)
-            + token_specs(half, WIDE * size, steps, groups, False),
+            + token_specs(half, 2 * WIDE * size, steps, groups, True)
+            + token_specs(half, 2 * WIDE * size, steps, groups, False),
             out_specs=pl.BlockSpec((parts, out_rows, size), lambda n, s: (0, 0, 0)),
             scratch_shapes=[
                 pltpu.VMEM((count, width), BF16),
-                pltpu.VMEM((steps, groups * (BLK // steps), count), BF16),
+                pltpu.VMEM((2 * steps, groups * BLK // (2 * steps), count), BF16),
                 pltpu.VMEM((WIDE, pairs * WIDE, size), F32),
             ],
         ),
@@ -672,9 +685,6 @@
     def after(value, *others):
         return lax.optimization_barrier((value,) + others)[0]
 
-    def double(value, bit):
-        return jnp.concatenate([value, along(value, bit)], axis=0)
-
     def add(*terms):
         return sum(term.astype(F32) for term in terms)
 
@@ -690,74 +700,75 @@
 
     own_pieces = [(t, row, 2) for t in (tokens, near_tokens) for row in (0, 1)]
     mine, other = products(
-        own_pieces, scalars(other_block), gate_weight, up_weight, 0, part
-    )
-    early = mine
-    sums = add(mine[0], swap(after(other[0], arrived))).astype(BF16)
+        own_pieces, after(scalars(other_block), first), gate_weight, up_weight, 0, part
+    )
+    sums = add(mine[0], after(swap(other[0]), arrived)).astype(BF16)
     got_early = across(sums)
-
-    arrived = after(arrived, early)
-    partner = along(arrived, 1)
-    near_arrived = swap(arrived)
     late_first = across(after(rest, sums))
+
+    pairs, blocks = left_factor.shape[0], left_factor.shape[2]
+    left_rows = left_factor.reshape(pairs // 2, 2, -1, blocks).transpose(0, 2, 1, 3)
+    factors = turn(after(right_factor, first), 0)
+    factors = jnp.concatenate(
+        [factors.reshape(-1, LANES), left_rows.reshape(-1, LANES)], axis=0
+    )
+    factors = after(factors, sums)[None]
+    more = along(factors, 1)
+
     order = jnp.concatenate([base, jnp.stack([chip, z])]).astype(jnp.int32)
     own = [tokens, tokens, near_tokens, near_tokens]
-    late = [arrived, partner, near_arrived, swap(partner)]
-    late_pieces = [(t, None, 3) for t in late]
-
-    pairs, blocks = left_factor.shape[0], left_factor.shape[2]
-    right_rows = turn(after(right_factor, sums), 0)[None]
-    left_own = left_factor.reshape(1, -1, LANES)
-    left_rows = double(after(left_own, sums), 1)
-
-    late_order = after(scalars(other_block), sums, right_rows, left_rows)
+    near_arrived = swap(arrived)
+    late_pieces = [(t, row, 3) for t in (arrived, near_arrived) for row in (0, 1)]
+    late_order = after(scalars(other_block), sums)
     mine, other = products(late_pieces, late_order, gate_weight, up_weight, 0, part)
-    near = swap(after(other[0], got_early, late_first))
-    right_rows, left_rows = after(right_rows, mine), after(left_rows, mine)
-    more_right, more_left = along(right_rows, 1), along(left_rows, 2)
-    sums = add(mine[0], near).astype(BF16)
-    got = across(sums)
-    mine_order = after(scalars(mine_block), sums)
+    near = swap(other[0])
+    factors = after(jnp.concatenate([factors, more], axis=0), mine)
+    more = along(factors, 2)
+    mine_order = after(scalars(mine_block), mine)
     kept, other = products(
         own_pieces + late_pieces, mine_order, gate_weight, up_weight, 0, part
     )
-    right_rows = jnp.concatenate([right_rows, after(more_right, kept)], axis=0)
-    left_rows = jnp.concatenate([left_rows, after(more_left, kept)], axis=0)
-
-    left_rows = left_rows.reshape((tensor_count,) + left_factor.shape)
-    for axis, bit in ((0, 2), (1, 1)):
-        split = left_rows.reshape((2, 2) + left_rows.shape[1:])
-        split = jnp.where(lax.rem(lax.div(z, bit), 2) == 1, jnp.flip(split, axis), split)
-        left_rows = split.reshape(left_rows.shape)
-    left_rows = left_rows.transpose(1, 3, 0, 2).reshape(pairs, blocks, blocks)
-
-    left_diag = spread_left(left_rows)
-    near_kept = swap(after(other, got, right_rows, left_diag))
-    more_right = along(right_rows, 2)
+    near_kept = swap(after(other, got_early, late_first, more))
+    sums = add(mine[0], after(near, kept)).astype(BF16)
+    got = across(sums)
+
+    factors = jnp.concatenate([factors, after(more, kept)], axis=0)
+    left_diag = spread_left(order, factors, pairs * blocks // BLK)
+
+    def activate(u, term):
+        total = add(kept[u], near_kept[u], term)
+        return (jax.nn.silu(total[0]) * total[1]).astype(BF16)
+
+    hidden1 = activate(1, got_early)
+    got1 = across(hidden1)
+    near1 = swap(hidden1)
     late_partner = along(after(late_first, kept), 1)
-    hidden = []
-    for u, term in enumerate((got, got_early)):
-        total = add(kept[u], near_kept[u], term)
-        hidden.append((jax.nn.silu(total[0]) * total[1]).astype(BF16))
-    hidden = jnp.stack(hidden)
-    got_hidden = across(hidden)
-    near_hidden = swap(hidden)
-    more_right, late_partner = after(more_right, hidden), after(late_partner, hidden)
-    right_rows = jnp.concatenate([right_rows, more_right], axis=0)
     mixed0, student0 = student_part(
-        [after(tokens, hidden)] + own[1:], False, order, right_rows, left_diag, tensor_count
-    )
-    late_rest = [late_first, late_partner, swap(late_first), swap(late_partner)]
+        [after(tokens, hidden1, sums)] + own[1:],
+        False,
+        order,
+        factors,
+        left_diag,
+        pairs,
+        tensor_count,
+    )
+    hidden0 = activate(0, after(got, mixed0))
+    got0 = across(hidden0)
+    near0 = swap(hidden0)
+    late_partner = after(late_partner, mixed0)
+    late = [arrived, arrived, near_arrived, near_arrived]
+    late += [late_first, late_partner, swap(late_first), swap(late_partner)]
     mixed1, student1 = student_part(
-        late + [after(late_rest[0], mixed0)] + late_rest[1:],
+        [after(arrived, hidden0)] + late[1:],
         True,
         order,
-        right_rows,
+        factors,
         left_diag,
+        pairs,
         tensor_count,
     )
-    got_hidden = after(got_hidden, mixed1)
-    hidden = [hidden, near_hidden, got_hidden, swap(got_hidden)]
+    got1, got0 = after(got1, mixed1), after(got0, mixed1)
+    hidden = [hidden0, hidden1, near0, near1, got0, got1, swap(got0), swap(got1)]
 
     grads = factor_grads(
         hidden,
@@ -766,7 +777,7 @@
         (mixed0, mixed1),
         left_diag,
         own,
-        late + late_rest,
+        late,
         order,
         tensor_count,
         right_factor.shape[2],

time: 196 us -> 185 us (0.944)
  local copies, waits for them, and re-layouts: 12.9 us -> 7.24 us
  waiting for transfers between devices: 54.1 us -> 59.6 us
  Pallas kernels: 82.5 us -> 77.3 us
  starting transfers between devices: 34.7 us -> 29.7 us
    ppermute x5 -> x6, waiting for transfers between devices: 5.77 us -> 33.7 us  [across(): return lax.ppermute(value, 'fsdp', [(i, i ^ 2) for i in range(fsdp_count)])]
    ppermute x8 -> x5, waiting for transfers between devices: 33.6 us -> 12.6 us  [along(): lax.ppermute(value, 'tensor', [(i, i ^ bit) for i in range(tensor_count)])]
    ppermute x8 -> x5, starting transfers between devices: 16.6 us -> 5.36 us  [along(): lax.ppermute(value, 'tensor', [(i, i ^ bit) for i in range(tensor_count)])]
    ppermute x5 -> x6, starting transfers between devices: 10 us -> 17.9 us  [across(): return lax.ppermute(value, 'fsdp', [(i, i ^ 2) for i in range(fsdp_count)])]
    pallas_call x2, Pallas kernels: 18.3 us -> 13.3 us  [student_part(): pl.pallas_call(functools.partial(student_kernel, steps, late, tensor_coun...]
    unnamed x29 -> x33, local copies, waits for them, and re-layouts: 7.15 us -> 3.85 us
    reshape x3 -> x2, local copies, waits for them, and re-layouts: 2.74 us -> 0.21 us  [the longest x1 0.11 us: tiled_body(): left_rows.reshape(-1, LANES)]
    pallas_call x1, Pallas kernels: 25.6 us -> 23.6 us  [factor_grads(): pl.pallas_call(functools.partial(grads_kernel, groups, steps, scale), gri...]
  transfers between devices with their start and end apart: 26 -> 25, of which waited for: 11 -> 9; matrix products, arithmetic and copies ran while one was open for 8% -> 6% of each run, Pallas kernels for 29% -> 29%
where the time goes in v7:
time: 185 us; the launch traced here: 184 us
  Pallas kernels  77.3 us (42%)
  waiting for transfers between devices  59.6 us (32%)
  starting transfers between devices  29.7 us (16%)
  other arithmetic  9.67 us (5%)
  local copies, waits for them, and re-layouts  7.24 us (4%)
    pallas_call x3, Pallas kernels, products(): pl.pallas_call(functools.partial(products_kernel, sets), grid_spec=pltpu....  34 us
    ppermute x6, waiting for transfers between devices, across(): return lax.ppermute(value, 'fsdp', [(i, i ^ 2) for i in range(fsdp_count)])  33.7 us
    pallas_call x1, Pallas kernels, factor_grads(): pl.pallas_call(functools.partial(grads_kernel, groups, steps, scale), gri...  23.6 us
    ppermute x6, starting transfers between devices, across(): return lax.ppermute(value, 'fsdp', [(i, i ^ 2) for i in range(fsdp_count)])  17.9 us
    pallas_call x2, Pallas kernels, student_part(): pl.pallas_call(functools.partial(student_kernel, steps, late, tensor_coun...  13.3 us
    ppermute x5, waiting for transfers between devices, along(): lax.ppermute(value, 'tensor', [(i, i ^ bit) for i in range(tensor_count)])  12.6 us
    ppermute x3, waiting for transfers between devices, turn(): return lax.ppermute(value, both_axes, perm)  11.4 us
    ppermute x5, starting transfers between devices, along(): lax.ppermute(value, 'tensor', [(i, i ^ bit) for i in range(tensor_count)])  5.36 us
  transfers between devices with their start and end apart: 25, of which 9 were waited for; matrix products, arithmetic and copies ran while one was open for 6% of the time, Pallas kernels for 29%

profile of v7, /device:TPU:0, one launch (start us, length us, event | category | flops | bytes accessed | tf_op | source)
XLA Modules:
  0.0 184.3 jit_solution(17144056452416694222)
XLA Ops:
  0.6 0.5 collective-permute-start
  1.1 0.6 pad_add_fusion.1.idx_ref
  1.8 3.4 %cut_tokens.1 = (bf16[128,4096]{1,0:T(8,128)(2,1)}, bf16[64,4096]{1,0:T(8,128)(2,1)}) custom-call(s32[3]{0:T(128)} %pad_add_fusion.1.idx_ref, bf16[128,8192]{1,0:T(8,128)(2,1)} %refs_15_.1, bf16[128,8192]{1,0:T(8,128)(2,1)} %refs_15_.1), custom_call_target="tpu_custom_call" | custom-call | flops 1 | bytes 1 | tf_op jit(solution)/shard_map/cut_tokens/pallas_call | solution.py:312
  5.2 2.5 %collective-permute-start.2 = (bf16[128,4096]{1,0:T(8,128)(2,1)}, bf16[128,4096]{1,0:T(8,128)(2,1)S(1)}, u32[]{:S(2)}, u32[]{:S(2)}) collective-permute-start(bf16[128,4096]{1,0:T(8,128)(2,1)} %get-tuple-element.32), channel_id=1, source_target_pairs={{0,8},{4,12},{8,0},{12,4},{1,9},{5,13},{9,1},{13,5},{2,10},{6,14},... | collective-permute-start | bytes 3145736 | tf_op jit(solution)/shard_map/ppermute | solution.py:673
  7.7 0.1 concatenate.25.idx_ref
  7.8 10.1 %gate_up_products.3 = (bf16[1,2,128,1792]{3,2,1,0:T(8,128)(2,1)S(1)}, bf16[1,2,128,1792]{3,2,1,0:T(8,128)(2,1)S(1)}) custom-call(s32[5]{0:T(128)S(1)} %concatenate.25.idx_ref, bf16[128,8192]{1,0:T(8,128)(2,1)S(1)} %copy-done, bf16[128,8192]{1,0:T(8,128)(2,1)S(1)} %copy-done, bf16[128,8192]{1,0:T(8,128)(2,1)} %collective-permute-done.refs_2_.refs_3_.refs_16_.refs_17_, ...), custom_call_target="tpu_custom_call" | custom-call | flops 1 | bytes 1 | tf_op jit(solution)/shard_map/gate_up_products/pallas_call | solution.py:357
  17.9 0.0 copy-start.14
  18.0 0.3 collective-permute-start.1
  18.2 13.5 %collective-permute-done.2.refs_0_.refs_1_.refs_4_.refs_5_.refs_18_.refs_19_ = bf16[128,4096]{1,0:T(8,128)(2,1)S(1)} collective-permute-done((bf16[128,4096]{1,0:T(8,128)(2,1)}, bf16[128,4096]{1,0:T(8,128)(2,1)S(1)}, u32[]{:S(2)}, u32[]{:S(2)}) %collective-permute-start.2) | collective-permute-done | bytes 1048608 | tf_op jit(solution)/shard_map/ppermute | solution.py:673
  31.7 0.7 collective-permute-start.6
  32.4 1.2 fusion.1
  33.6 5.5 %collective-permute-start.4 = (bf16[2,128,1792]{2,1,0:T(8,128)(2,1)}, bf16[2,128,1792]{2,1,0:T(8,128)(2,1)}, u32[]{:S(2)}, u32[]{:S(2)}) collective-permute-start(bf16[2,128,1792]{2,1,0:T(8,128)(2,1)} %fusion.1), channel_id=1, source_target_pairs={{0,8},{4,12},{8,0},{12,4},{1,9},{5,13},{9,1},{13,5},{2,10},{6,14},... | collective-permute-start | bytes 2752520 | tf_op jit(solution)/shard_map/ppermute | solution.py:673
  39.2 0.1 copy.11
  39.3 0.1 reshape.36
  39.4 0.7 collective-permute-start.7
  40.1 6.1 %collective-permute-start.5 = (bf16[64,4096]{1,0:T(8,128)(2,1)}, bf16[64,4096]{1,0:T(8,128)(2,1)}, u32[]{:S(2)}, u32[]{:S(2)}) collective-permute-start(bf16[64,4096]{1,0:T(8,128)(2,1)} %get-tuple-element.43), channel_id=1, source_target_pairs={{0,8},{4,12},{8,0},{12,4},{1,9},{5,13},{9,1},{13,5},{2,10},{6,14},... | collective-permute-start | bytes 1572872 | tf_op jit(solution)/shard_map/ppermute | solution.py:673
  46.2 10.6 %gate_up_products.4 = (bf16[1,2,128,1792]{3,2,1,0:T(8,128)(2,1)S(1)}, bf16[1,2,128,1792]{3,2,1,0:T(8,128)(2,1)}) custom-call(s32[5]{0:T(128)S(1)} %concatenate.25.idx_ref, bf16[128,4096]{1,0:T(8,128)(2,1)S(1)} %collective-permute-done.2.refs_0_.refs_1_.refs_4_.refs_5_.refs_18_.refs_19_, ...), custom_call_target="tpu_custom_call" | custom-call | flops 1 | bytes 1 | tf_op jit(solution)/shard_map/gate_up_products/pallas_call | solution.py:357
  56.9 0.2 collective-permute-start.8
  57.1 0.1 concatenate.24.idx_ref
  57.2 13.2 %gate_up_products.5 = (bf16[2,2,128,1792]{3,2,1,0:T(8,128)(2,1)S(1)}, bf16[2,2,128,1792]{3,2,1,0:T(8,128)(2,1)}) custom-call(s32[5]{0:T(128)S(1)} %concatenate.24.idx_ref, bf16[128,8192]{1,0:T(8,128)(2,1)} %refs_15_.1, bf16[128,8192]{1,0:T(8,128)(2,1)} %refs_15_.1, bf16[128,8192]{1,0:T(8,128)(2,1)} %collective-permute-done.refs_2_.refs_3_.refs_16_.refs_17_, ...), custom_call_target="tpu_custom_call" | custom-call | flops 1 | bytes 1 | tf_op jit(solution)/shard_map/gate_up_products/pallas_call | solution.py:357
  70.4 1.3 copy-done.4
  71.7 1.5 collective-permute-done.5.refs_4_.refs_22_
  73.2 3.0 %collective-permute-done.8 = bf16[2,768,128]{2,1,0:T(8,128)(2,1)} collective-permute-done((bf16[2,768,128]{2,1,0:T(8,128)(2,1)S(1)}, bf16[2,768,128]{2,1,0:T(8,128)(2,1)}, u32[]{:S(2)}, u32[]{:S(2)}) %collective-permute-start.8) | collective-permute-done | bytes 393248 | tf_op jit(solution)/shard_map/ppermute | solution.py:676
  76.3 0.0 collective-permute-start.9
  76.3 0.5 collective-permute-start.10
  76.8 0.6 pad_add_fusion.idx_ref
  77.4 0.1 collective-permute-start.15
  77.5 1.0 constant_dynamic-update-slice_fusion.rows_ref.refs_4_.refs_5_.refs_8_.refs_9_
  78.5 0.1 collective-permute-start.16
  78.6 0.8 copy-done.6
  79.4 3.0 %spread_left.1.refs_6_.refs_10_.refs_13_ = bf16[8,256,256]{2,1,0:T(8,128)(2,1)} custom-call(s32[4]{0:T(128)} %pad_add_fusion.idx_ref, bf16[4,768,128]{2,1,0:T(8,128)(2,1)} %copy-done.6), custom_call_target="tpu_custom_call" | custom-call | flops 1 | bytes 1 | tf_op jit(solution)/shard_map/spread_left/pallas_call | solution.py:424
  82.4 0.1 collective-permute-done.10
  82.5 1.5 fusion
  84.0 1.7 collective-permute-start.11
  85.7 1.8 bitcast_add_fusion
  87.5 0.0 copy-start.13
  87.5 0.3 fusion.5.refs_1_
  87.8 0.5 collective-permute-start.18
  88.3 0.4 copy-done.3
  88.7 0.2 copy-done.7
  88.9 6.5 %student_part.2 = (bf16[8,256,256]{2,1,0:T(8,128)(2,1)S(1)}, f32[256,2048]{1,0:T(8,128)}) custom-call(s32[4]{0:T(128)S(1)} %copy-done.13, bf16[128,8192]{1,0:T(8,128)(2,1)} %refs_15_.1, bf16[128,8192]{1,0:T(8,128)(2,1)} %refs_15_.1, bf16[128,8192]{1,0:T(8,128)(2,1)} %collective-permute-done.refs_2_.refs_3_.refs_16_.refs_17_, ...), custom_call_target="tpu_custom_call" | custom-call | flops 10000000000 | bytes 10000000 | tf_op jit(solution)/shard_map/student_part/pallas_call | solution.py:518
  95.5 0.1 collective-permute-start.17
  95.5 11.7 %collective-permute-done.11 = bf16[2,128,1792]{2,1,0:T(8,128)(2,1)S(1)} collective-permute-done((bf16[2,128,1792]{2,1,0:T(8,128)(2,1)S(1)}, bf16[2,128,1792]{2,1,0:T(8,128)(2,1)S(1)}, u32[]{:S(2)}, u32[]{:S(2)}) %collective-permute-start.11) | collective-permute-done | bytes 917536 | tf_op jit(solution)/shard_map/ppermute | solution.py:673
  107.3 1.5 bitcast_add_fusion.1
  108.8 0.3 fusion.3.refs_0_
  109.1 1.7 collective-permute-start.14
  110.7 0.5 collective-permute-start.13
  111.3 6.8 %student_part.3 = (bf16[8,256,256]{2,1,0:T(8,128)(2,1)S(1)}, f32[256,2048]{1,0:T(8,128)}) custom-call(s32[4]{0:T(128)S(1)} %copy-done.13, bf16[128,4096]{1,0:T(8,128)(2,1)} %copy-done.1, bf16[128,4096]{1,0:T(8,128)(2,1)} %copy-done.1, bf16[128,4096]{1,0:T(8,128)(2,1)} %copy-done.2, bf16[128,4096]{1,0:T(8,128)(2,1)} %copy-done.2, ...), custom_call_target="tpu_custom_call" | custom-call | flops 10000000000 | bytes 10000000 | tf_op jit(solution)/shard_map/student_part/pallas_call | solution.py:518
  118.1 1.0 copy-done.9
  119.1 0.1 collective-permute-start.20
  119.2 6.9 %collective-permute-done.14.refs_4_ = bf16[128,1792]{1,0:T(8,128)(2,1)S(1)} collective-permute-done((bf16[128,1792]{1,0:T(8,128)(2,1)S(1)}, bf16[128,1792]{1,0:T(8,128)(2,1)S(1)}, u32[]{:S(2)}, u32[]{:S(2)}) %collective-permute-start.14) | collective-permute-done | bytes 458784 | tf_op jit(solution)/shard_map/ppermute | solution.py:673
  126.1 1.8 collective-permute-done.19.refs_6_
  127.9 23.6 %factor_grads.1 = bf16[4,768,128]{2,1,0:T(8,128)(2,1)} custom-call(s32[4]{0:T(128)S(1)} %copy-done.13, bf16[128,1792]{1,0:T(8,128)(2,1)S(1)} %fusion.3.refs_0_, bf16[128,1792]{1,0:T(8,128)(2,1)S(1)} %fusion.5.refs_1_, bf16[128,1792]{1,0:T(8,128)(2,1)S(1)} %collective-permute-done.12.refs_2_, bf16[128,1792]{1,0:T(8,128)(2,1)S(1)} %collective-permute-done.13.refs_3_, ...), custom_call_target="tpu_custom_call" | custom-call | flops 1 | bytes 1 | tf_op jit(solution)/shard_map/factor_grads/pallas_call | solution.py:631
  151.5 1.0 slice.63
  152.5 1.7 collective-permute-start.21
  154.1 9.6 %collective-permute-done.21 = bf16[2,768,128]{2,1,0:T(8,128)(2,1)S(1)} collective-permute-done((bf16[2,768,128]{2,1,0:T(8,128)(2,1)S(1)}, bf16[2,768,128]{2,1,0:T(8,128)(2,1)S(1)}, u32[]{:S(2)}, u32[]{:S(2)}) %collective-permute-start.21) | collective-permute-done | bytes 393248 | tf_op jit(solution)/shard_map/ppermute | solution.py:676
  163.7 1.1 add_convert_fusion
  164.8 2.7 %collective-permute-start.24 = (bf16[256,128]{1,0:T(8,128)(2,1)S(1)}, bf16[256,128]{1,0:T(8,128)(2,1)S(1)}, u32[]{:S(2)}, u32[]{:S(2)}) collective-permute-start(bf16[256,128]{1,0:T(8,128)(2,1)S(1)} %slice_bitcast_fusion.6), channel_id=1, source_target_pairs={{0,2},{1,3},{2,0},{3,1},{4,6},{5,7},{6,4},{7,5},{8,10},{9,11},{10,... | collective-permute-start | bytes 196616 | tf_op jit(solution)/shard_map/ppermute | solution.py:676
  167.5 0.7 collective-permute-start.22
  168.2 3.0 %collective-permute-start.23 = (bf16[512,128]{1,0:T(8,128)(2,1)S(1)}, bf16[512,128]{1,0:T(8,128)(2,1)S(1)}, u32[]{:S(2)}, u32[]{:S(2)}) collective-permute-start(bf16[512,128]{1,0:T(8,128)(2,1)S(1)} %get-tuple-element.63), channel_id=1, source_target_pairs={{0,8},{1,12},{2,0},{3,4},{4,9},{5,13},{6,1},{7,5},{8,10},{9,14},{1... | collective-permute-start | bytes 393224 | tf_op jit(solution)/shard_map/ppermute | solution.py:683
  171.3 0.2 reshape.38
  171.5 0.7 copy.9
  172.2 11.4 %collective-permute-done.23 = bf16[512,128]{1,0:T(8,128)(2,1)S(1)} collective-permute-done((bf16[512,128]{1,0:T(8,128)(2,1)S(1)}, bf16[512,128]{1,0:T(8,128)(2,1)S(1)}, u32[]{:S(2)}, u32[]{:S(2)}) %collective-permute-start.23) | collective-permute-done | bytes 131104 | tf_op jit(solution)/shard_map/ppermute | solution.py:683
  183.6 0.7 convert_add_fusion.2
  (50 shorter events, 0.2 us)
Async XLA Ops:
  0.6 7.2 %collective-permute-start = (bf16[128,8192]{1,0:T(8,128)(2,1)}, bf16[128,8192]{1,0:T(8,128)(2,1)}, u32[]{:S(2)}, u32[]{:S(2)}) collective-permute-start(bf16[128,8192]{1,0:T(8,128)(2,1)} %refs_15_.1), channel_id=1, source_target_pairs={{0,4},{4,0},{8,12},{12,8},{1,5},{5,1},{9,13},{13,9},{2,6},{6,2},{1... | collective-permute-start | bytes 6291464 | tf_op jit(solution)/shard_map/ppermute | solution.py:670
  1.8 6.0 %copy-start = (bf16[128,8192]{1,0:T(8,128)(2,1)S(1)}, bf16[128,8192]{1,0:T(8,128)(2,1)}, u32[]{:S(2)}) copy-start(bf16[128,8192]{1,0:T(8,128)(2,1)} %refs_15_.1) | copy-start | bytes 6291460
  5.2 26.5 %collective-permute-start.2 = (bf16[128,4096]{1,0:T(8,128)(2,1)}, bf16[128,4096]{1,0:T(8,128)(2,1)S(1)}, u32[]{:S(2)}, u32[]{:S(2)}) collective-permute-start(bf16[128,4096]{1,0:T(8,128)(2,1)} %get-tuple-element.32), channel_id=1, source_target_pairs={{0,8},{4,12},{8,0},{12,4},{1,9},{5,13},{9,1},{13,5},{2,10},{6,14},... | collective-permute-start | bytes 3145736 | tf_op jit(solution)/shard_map/ppermute | solution.py:673
  7.8 23.9 %copy-start.15 = (bf16[16,32,128]{2,1,0:T(8,128)(2,1)S(1)}, bf16[16,32,128]{2,1,0:T(8,128)(2,1)}, u32[]{:S(2)}) copy-start(bf16[16,32,128]{2,1,0:T(8,128)(2,1)} %param.10) | copy-start | bytes 393220
  17.9 21.2 %copy-start.14 = (bf16[32,16,64]{2,1,0:T(8,128)(2,1)S(1)}, bf16[32,16,64]{2,1,0:T(8,128)(2,1)}, u32[]{:S(2)}) copy-start(bf16[32,16,64]{2,1,0:T(8,128)(2,1)} %param.11) | copy-start | bytes 196612
  18.0 14.5 %collective-permute-start.1 = (bf16[2,128,1792]{2,1,0:T(8,128)(2,1)S(1)}, bf16[2,128,1792]{2,1,0:T(8,128)(2,1)S(1)}, u32[]{:S(2)}, u32[]{:S(2)}) collective-permute-start(bf16[2,128,1792]{2,1,0:T(8,128)(2,1)S(1)} %bitcast.61), channel_id=1, source_target_pairs={{0,4},{4,0},{8,12},{12,8},{1,5},{5,1},{9,13},{13,9},{2,6},{6,2},{1... | collective-permute-start | bytes 2752520 | tf_op jit(solution)/shard_map/ppermute | solution.py:670
  31.7 25.4 %copy-start.1 = (bf16[128,4096]{1,0:T(8,128)(2,1)}, bf16[128,4096]{1,0:T(8,128)(2,1)S(1)}, u32[]{:S(2)}) copy-start(bf16[128,4096]{1,0:T(8,128)(2,1)S(1)} %collective-permute-done.2.refs_0_.refs_1_.refs_4_.refs_5_.refs_18_.refs_19_) | copy-start | bytes 3145732
  31.7 14.5 %collective-permute-start.3 = (bf16[128,4096]{1,0:T(8,128)(2,1)S(1)}, bf16[128,4096]{1,0:T(8,128)(2,1)S(1)}, u32[]{:S(2)}, u32[]{:S(2)}) collective-permute-start(bf16[128,4096]{1,0:T(8,128)(2,1)S(1)} %collective-permute-done.2.refs_0_.refs_1_.refs_4_.refs_5_.refs_18_.refs_19_), channel_id=1, source_target_pairs={{0,4},{4,0},{8,12},{12,8},{1,5},{5,1},{9,13},{13,9},{2,6},{6,2},{1... | collective-permute-start | bytes 3145736 | tf_op jit(solution)/shard_map/ppermute | solution.py:670
  31.7 7.6 %collective-permute-start.6 = (bf16[16,32,128]{2,1,0:T(8,128)(2,1)S(1)}, bf16[16,32,128]{2,1,0:T(8,128)(2,1)S(1)}, u32[]{:S(2)}, u32[]{:S(2)}) collective-permute-start(bf16[16,32,128]{2,1,0:T(8,128)(2,1)S(1)} %copy-done.15), channel_id=1, source_target_pairs={{0,0},{1,4},{2,8},{3,12},{4,1},{5,5},{6,9},{7,13},{8,2},{9,6},{10,... | collective-permute-start | bytes 393224 | tf_op jit(solution)/shard_map/ppermute | solution.py:683
  33.6 42.7 %collective-permute-start.4 = (bf16[2,128,1792]{2,1,0:T(8,128)(2,1)}, bf16[2,128,1792]{2,1,0:T(8,128)(2,1)}, u32[]{:S(2)}, u32[]{:S(2)}) collective-permute-start(bf16[2,128,1792]{2,1,0:T(8,128)(2,1)} %fusion.1), channel_id=1, source_target_pairs={{0,8},{4,12},{8,0},{12,4},{1,9},{5,13},{9,1},{13,5},{2,10},{6,14},... | collective-permute-start | bytes 2752520 | tf_op jit(solution)/shard_map/ppermute | solution.py:673
  39.4 17.4 %collective-permute-start.7 = (bf16[1,768,128]{2,1,0:T(8,128)(2,1)S(1)}, bf16[1,768,128]{2,1,0:T(8,128)(2,1)S(1)}, u32[]{:S(2)}, u32[]{:S(2)}) collective-permute-start(bf16[1,768,128]{2,1,0:T(8,128)(2,1)S(1)} %bitcast.63), channel_id=1, source_target_pairs={{0,1},{1,0},{2,3},{3,2},{4,5},{5,4},{6,7},{7,6},{8,9},{9,8},{10,11... | collective-permute-start | bytes 589832 | tf_op jit(solution)/shard_map/ppermute | solution.py:676
  40.1 33.1 %collective-permute-start.5 = (bf16[64,4096]{1,0:T(8,128)(2,1)}, bf16[64,4096]{1,0:T(8,128)(2,1)}, u32[]{:S(2)}, u32[]{:S(2)}) collective-permute-start(bf16[64,4096]{1,0:T(8,128)(2,1)} %get-tuple-element.43), channel_id=1, source_target_pairs={{0,8},{4,12},{8,0},{12,4},{1,9},{5,13},{9,1},{13,5},{2,10},{6,14},... | collective-permute-start | bytes 1572872 | tf_op jit(solution)/shard_map/ppermute | solution.py:673
  46.2 11.0 %copy-start.2 = (bf16[128,4096]{1,0:T(8,128)(2,1)}, bf16[128,4096]{1,0:T(8,128)(2,1)S(1)}, u32[]{:S(2)}) copy-start(bf16[128,4096]{1,0:T(8,128)(2,1)S(1)} %collective-permute-done.3.refs_2_.refs_3_.refs_6_.refs_7_.refs_20_.refs_21_) | copy-start | bytes 3145732
  56.9 19.4 %collective-permute-start.8 = (bf16[2,768,128]{2,1,0:T(8,128)(2,1)S(1)}, bf16[2,768,128]{2,1,0:T(8,128)(2,1)}, u32[]{:S(2)}, u32[]{:S(2)}) collective-permute-start(bf16[2,768,128]{2,1,0:T(8,128)(2,1)S(1)} %pad_maximum_fusion), channel_id=1, source_target_pairs={{0,2},{1,3},{2,0},{3,1},{4,6},{5,7},{6,4},{7,5},{8,10},{9,11},{10,... | collective-permute-start | bytes 1179656 | tf_op jit(solution)/shard_map/ppermute | solution.py:676
  70.4 1.3 copy-start.4
  76.3 9.4 %collective-permute-start.9 = (bf16[2,2,128,1792]{3,2,1,0:T(8,128)(2,1)}, bf16[2,2,128,1792]{3,2,1,0:T(8,128)(2,1)}, u32[]{:S(2)}, u32[]{:S(2)}) collective-permute-start(bf16[2,2,128,1792]{3,2,1,0:T(8,128)(2,1)} %get-tuple-element.47), channel_id=1, source_target_pairs={{0,4},{4,0},{8,12},{12,8},{1,5},{5,1},{9,13},{13,9},{2,6},{6,2},{1... | collective-permute-start | bytes 5505032 | tf_op jit(solution)/shard_map/ppermute | solution.py:670
  76.3 6.2 %collective-permute-start.10 = (bf16[2,128,1792]{2,1,0:T(8,128)(2,1)}, bf16[2,128,1792]{2,1,0:T(8,128)(2,1)}, u32[]{:S(2)}, u32[]{:S(2)}) collective-permute-start(bf16[2,128,1792]{2,1,0:T(8,128)(2,1)} %bitcast.17), channel_id=1, source_target_pairs={{0,4},{4,0},{8,12},{12,8},{1,5},{5,1},{9,13},{13,9},{2,6},{6,2},{1... | collective-permute-start | bytes 2752520 | tf_op jit(solution)/shard_map/ppermute | solution.py:670
  77.4 18.0 %collective-permute-start.15 = (bf16[64,4096]{1,0:T(8,128)(2,1)}, bf16[64,4096]{1,0:T(8,128)(2,1)S(1)}, u32[]{:S(2)}, u32[]{:S(2)}) collective-permute-start(bf16[64,4096]{1,0:T(8,128)(2,1)} %collective-permute-done.5.refs_4_.refs_22_), channel_id=1, source_target_pairs={{0,1},{1,0},{2,3},{3,2},{4,5},{5,4},{6,7},{7,6},{8,9},{9,8},{10,11... | collective-permute-start | bytes 1572872 | tf_op jit(solution)/shard_map/ppermute | solution.py:676
  78.5 0.9 copy-start.6
  78.5 32.2 %collective-permute-start.16 = (bf16[64,4096]{1,0:T(8,128)(2,1)}, bf16[64,4096]{1,0:T(8,128)(2,1)S(1)}, u32[]{:S(2)}, u32[]{:S(2)}) collective-permute-start(bf16[64,4096]{1,0:T(8,128)(2,1)} %collective-permute-done.5.refs_4_.refs_22_), channel_id=1, source_target_pairs={{0,4},{4,0},{8,12},{12,8},{1,5},{5,1},{9,13},{13,9},{2,6},{6,2},{1... | collective-permute-start | bytes 1572872 | tf_op jit(solution)/shard_map/ppermute | solution.py:670
  82.4 3.3 %copy-start.5 = (bf16[2,2,128,1792]{3,2,1,0:T(8,128)(2,1)S(1)}, bf16[2,2,128,1792]{3,2,1,0:T(8,128)(2,1)}, u32[]{:S(2)}) copy-start(bf16[2,2,128,1792]{3,2,1,0:T(8,128)(2,1)} %copy-done.4) | copy-start | bytes 5505028
  84.0 23.3 %collective-permute-start.11 = (bf16[2,128,1792]{2,1,0:T(8,128)(2,1)S(1)}, bf16[2,128,1792]{2,1,0:T(8,128)(2,1)S(1)}, u32[]{:S(2)}, u32[]{:S(2)}) collective-permute-start(bf16[2,128,1792]{2,1,0:T(8,128)(2,1)S(1)} %fusion), channel_id=1, source_target_pairs={{0,8},{4,12},{8,0},{12,4},{1,9},{5,13},{9,1},{13,5},{2,10},{6,14},... | collective-permute-start | bytes 2752520 | tf_op jit(solution)/shard_map/ppermute | solution.py:673
  87.5 1.2 copy-start.3
  87.5 1.4 copy-start.7
  87.5 1.4 copy-start.13
  87.8 31.3 %collective-permute-start.18 = (bf16[128,1792]{1,0:T(8,128)(2,1)S(1)}, bf16[128,1792]{1,0:T(8,128)(2,1)S(1)}, u32[]{:S(2)}, u32[]{:S(2)}) collective-permute-start(bf16[128,1792]{1,0:T(8,128)(2,1)S(1)} %fusion.5.refs_1_), channel_id=1, source_target_pairs={{0,8},{4,12},{8,0},{12,4},{1,9},{5,13},{9,1},{13,5},{2,10},{6,14},... | collective-permute-start | bytes 1376264 | tf_op jit(solution)/shard_map/ppermute | solution.py:673
  95.4 13.3 %copy-start.8 = (bf16[8,256,256]{2,1,0:T(8,128)(2,1)}, bf16[8,256,256]{2,1,0:T(8,128)(2,1)S(1)}, u32[]{:S(2)}) copy-start(bf16[8,256,256]{2,1,0:T(8,128)(2,1)S(1)} %get-tuple-element.52.refs_11_) | copy-start | bytes 3145732
  95.4 15.8 %copy-start.10 = (bf16[64,4096]{1,0:T(8,128)(2,1)}, bf16[64,4096]{1,0:T(8,128)(2,1)S(1)}, u32[]{:S(2)}) copy-start(bf16[64,4096]{1,0:T(8,128)(2,1)S(1)} %collective-permute-done.15.refs_5_.refs_23_) | copy-start | bytes 1572868
  95.5 15.8 %collective-permute-start.17 = (bf16[64,4096]{1,0:T(8,128)(2,1)S(1)}, bf16[64,4096]{1,0:T(8,128)(2,1)S(1)}, u32[]{:S(2)}, u32[]{:S(2)}) collective-permute-start(bf16[64,4096]{1,0:T(8,128)(2,1)S(1)} %collective-permute-done.15.refs_5_.refs_23_), channel_id=1, source_target_pairs={{0,4},{4,0},{8,12},{12,8},{1,5},{5,1},{9,13},{13,9},{2,6},{6,2},{1... | collective-permute-start | bytes 1572872 | tf_op jit(solution)/shard_map/ppermute | solution.py:670
  109.1 17.0 %collective-permute-start.14 = (bf16[128,1792]{1,0:T(8,128)(2,1)S(1)}, bf16[128,1792]{1,0:T(8,128)(2,1)S(1)}, u32[]{:S(2)}, u32[]{:S(2)}) collective-permute-start(bf16[128,1792]{1,0:T(8,128)(2,1)S(1)} %fusion.3.refs_0_), channel_id=1, source_target_pairs={{0,8},{4,12},{8,0},{12,4},{1,9},{5,13},{9,1},{13,5},{2,10},{6,14},... | collective-permute-start | bytes 1376264 | tf_op jit(solution)/shard_map/ppermute | solution.py:673
  110.7 15.4 %collective-permute-start.12 = (bf16[128,1792]{1,0:T(8,128)(2,1)S(1)}, bf16[128,1792]{1,0:T(8,128)(2,1)S(1)}, u32[]{:S(2)}, u32[]{:S(2)}) collective-permute-start(bf16[128,1792]{1,0:T(8,128)(2,1)S(1)} %fusion.3.refs_0_), channel_id=1, source_target_pairs={{0,4},{4,0},{8,12},{12,8},{1,5},{5,1},{9,13},{13,9},{2,6},{6,2},{1... | collective-permute-start | bytes 1376264 | tf_op jit(solution)/shard_map/ppermute | solution.py:670
  110.7 7.3 %copy-start.11 = (bf16[64,4096]{1,0:T(8,128)(2,1)}, bf16[64,4096]{1,0:T(8,128)(2,1)S(1)}, u32[]{:S(2)}) copy-start(bf16[64,4096]{1,0:T(8,128)(2,1)S(1)} %collective-permute-done.16.refs_6_.refs_24_) | copy-start | bytes 1572868
  110.7 15.3 %collective-permute-start.13 = (bf16[128,1792]{1,0:T(8,128)(2,1)S(1)}, bf16[128,1792]{1,0:T(8,128)(2,1)S(1)}, u32[]{:S(2)}, u32[]{:S(2)}) collective-permute-start(bf16[128,1792]{1,0:T(8,128)(2,1)S(1)} %fusion.5.refs_1_), channel_id=1, source_target_pairs={{0,4},{4,0},{8,12},{12,8},{1,5},{5,1},{9,13},{13,9},{2,6},{6,2},{1... | collective-permute-start | bytes 1376264 | tf_op jit(solution)/shard_map/ppermute | solution.py:670
  111.3 6.8 %copy-start.12 = (bf16[64,4096]{1,0:T(8,128)(2,1)}, bf16[64,4096]{1,0:T(8,128)(2,1)S(1)}, u32[]{:S(2)}) copy-start(bf16[64,4096]{1,0:T(8,128)(2,1)S(1)} %collective-permute-done.17.refs_7_.refs_25_) | copy-start | bytes 1572868
  118.1 1.0 copy-start.9
  119.1 7.0 %collective-permute-start.20 = (bf16[128,1792]{1,0:T(8,128)(2,1)S(1)}, bf16[128,1792]{1,0:T(8,128)(2,1)S(1)}, u32[]{:S(2)}, u32[]{:S(2)}) collective-permute-start(bf16[128,1792]{1,0:T(8,128)(2,1)S(1)} %collective-permute-done.18.refs_5_), channel_id=1, source_target_pairs={{0,4},{4,0},{8,12},{12,8},{1,5},{5,1},{9,13},{13,9},{2,6},{6,2},{1... | collective-permute-start | bytes 1376264 | tf_op jit(solution)/shard_map/ppermute | solution.py:670
  126.1 1.8 collective-permute-start.19
  152.5 11.2 %collective-permute-start.21 = (bf16[2,768,128]{2,1,0:T(8,128)(2,1)S(1)}, bf16[2,768,128]{2,1,0:T(8,128)(2,1)S(1)}, u32[]{:S(2)}, u32[]{:S(2)}) collective-permute-start(bf16[2,768,128]{2,1,0:T(8,128)(2,1)S(1)} %slice.63), channel_id=1, source_target_pairs={{0,1},{1,0},{2,3},{3,2},{4,5},{5,4},{6,7},{7,6},{8,9},{9,8},{10,11... | collective-permute-start | bytes 1179656 | tf_op jit(solution)/shard_map/ppermute | solution.py:676
  164.8 6.4 %collective-permute-start.24 = (bf16[256,128]{1,0:T(8,128)(2,1)S(1)}, bf16[256,128]{1,0:T(8,128)(2,1)S(1)}, u32[]{:S(2)}, u32[]{:S(2)}) collective-permute-start(bf16[256,128]{1,0:T(8,128)(2,1)S(1)} %slice_bitcast_fusion.6), channel_id=1, source_target_pairs={{0,2},{1,3},{2,0},{3,1},{4,6},{5,7},{6,4},{7,5},{8,10},{9,11},{10,... | collective-permute-start | bytes 196616 | tf_op jit(solution)/shard_map/ppermute | solution.py:676
  167.5 4.7 %collective-permute-start.22 = (bf16[512,128]{1,0:T(8,128)(2,1)S(1)}, bf16[512,128]{1,0:T(8,128)(2,1)S(1)}, u32[]{:S(2)}, u32[]{:S(2)}) collective-permute-start(bf16[512,128]{1,0:T(8,128)(2,1)S(1)} %get-tuple-element.62), channel_id=1, source_target_pairs={{0,0},{1,4},{2,8},{3,12},{4,1},{5,5},{6,9},{7,13},{8,2},{9,6},{10,... | collective-permute-start | bytes 393224 | tf_op jit(solution)/shard_map/ppermute | solution.py:683
  168.2 15.4 %collective-permute-start.23 = (bf16[512,128]{1,0:T(8,128)(2,1)S(1)}, bf16[512,128]{1,0:T(8,128)(2,1)S(1)}, u32[]{:S(2)}, u32[]{:S(2)}) collective-permute-start(bf16[512,128]{1,0:T(8,128)(2,1)S(1)} %get-tuple-element.63), channel_id=1, source_target_pairs={{0,8},{1,12},{2,0},{3,4},{4,9},{5,13},{6,1},{7,5},{8,10},{9,14},{1... | collective-permute-start | bytes 393224 | tf_op jit(solution)/shard_map/ppermute | solution.py:683

commit v8 on v7

--- a/solution.py
+++ b/solution.py
@@ -11,6 +11,7 @@
 BLK = 256
 LANES = 128
 SMALL = pl.CostEstimate(flops=1, bytes_accessed=1, transcendentals=0)
+LARGE = pl.CostEstimate(flops=10**10, bytes_accessed=10**7, transcendentals=0)
 F32 = jnp.float32
 BF16 = jnp.bfloat16
 
@@ -301,32 +302,24 @@
     return grad_right, grad_left
 
 
-def cut_kernel(idx_ref, first_in, rest_in, first_ref, rest_ref):
-    first_ref[...] = first_in[...]
-    rest_ref[...] = rest_in[...]
-
-
-def cut_tokens(tokens, half, chip):
-    rows, model = tokens.shape
-    first, rest = (rows, model // 2), (rows // 2, model // 2)
+def cut_kernel(idx_ref, in_ref, out_ref):
+    out_ref[...] = in_ref[...]
+
+
+def cut_tokens(tokens, rows, row, column, cost=SMALL):
+    block = (rows, tokens.shape[1] // 2)
     return pl.pallas_call(
         cut_kernel,
         grid_spec=pltpu.PrefetchScalarGridSpec(
             num_scalar_prefetch=1,
             grid=(1,),
-            in_specs=[
-                pl.BlockSpec(first, lambda n, s: (0, s[1])),
-                pl.BlockSpec(rest, lambda n, s: (s[0], s[2])),
-            ],
-            out_specs=[
-                pl.BlockSpec(first, lambda n, s: (0, 0)),
-                pl.BlockSpec(rest, lambda n, s: (0, 0)),
-            ],
-        ),
-        out_shape=[jax.ShapeDtypeStruct(first, BF16), jax.ShapeDtypeStruct(rest, BF16)],
-        cost_estimate=SMALL,
+            in_specs=[pl.BlockSpec(block, lambda n, s: (s[0], s[1]))],
+            out_specs=pl.BlockSpec(block, lambda n, s: (0, 0)),
+        ),
+        out_shape=jax.ShapeDtypeStruct(block, BF16),
+        cost_estimate=cost,
         name="cut_tokens",
-    )(jnp.stack([half, 1 - chip, chip]).astype(jnp.int32), tokens, tokens)
+    )(jnp.stack([row, column]).astype(jnp.int32), tokens)
 
 
 def products_kernel(sets, idx_ref, *refs):
@@ -365,24 +358,47 @@
         ),
         out_shape=[shape, shape],
         compiler_params=pltpu.CompilerParams(vmem_limit_bytes=50 * 2**20),
-        cost_estimate=SMALL,
+        cost_estimate=LARGE if sets > 1 else SMALL,
         name="gate_up_products",
     )(scalars, *[piece for piece, _, _ in pieces], gate, up)
 
 
-def fill_rows(lhs, pieces, chip):
-    rows, width = pieces[0].shape
-    for u in range(2):
-        for part in range(2):
-            begin = pl.multiple_of(lax.rem(chip + part, 2) * width, LANES)
-            which = 4 * part + (u if part == 0 else 1 - u)
-            for core in range(2):
-                row = (2 * u + core) * rows
-                lhs[row : row + rows, pl.ds(begin, width)] = pieces[which + 2 * core][...]
+def fill_rows(lhs, pieces):
+    rows = pieces[0].shape[0]
+    for place, which in enumerate((1, 3, 0, 2)):
+        lhs[place * rows : (place + 1) * rows, :] = pieces[which][...]
 
 
 def whole_spec(array):
     return pl.BlockSpec(array.shape, lambda n, s: (0,) * array.ndim)
+
+
+def target_kernel(sign, idx_ref, mine_ref, near_ref, weight_ref, *refs):
+    terms, out_ref = refs[:-1], refs[-1]
+    lhs = jnp.concatenate([mine_ref[...], near_ref[...]], axis=0)
+    product = jnp.dot(lhs, weight_ref[...], preferred_element_type=F32)
+    out_ref[...] = sum((ref[...] for ref in terms), sign * product)
+
+
+def target_part(sign, terms, mine, near, weight, chip):
+    rows, width = mine.shape
+    outs = weight.shape[1]
+    block = pl.BlockSpec((2 * rows, BLK), lambda n, s: (0, n))
+    return pl.pallas_call(
+        functools.partial(target_kernel, sign),
+        grid_spec=pltpu.PrefetchScalarGridSpec(
+            num_scalar_prefetch=1,
+            grid=(outs // BLK,),
+            in_specs=[whole_spec(mine), whole_spec(near)]
+            + [pl.BlockSpec((width, BLK), lambda n, s: (s[0], n))]
+            + [block] * len(terms),
+            out_specs=block,
+        ),
+        out_shape=jax.ShapeDtypeStruct((2 * rows, outs), F32),
+        compiler_params=pltpu.CompilerParams(vmem_limit_bytes=50 * 2**20),
+        cost_estimate=SMALL,
+        name="target_part",
+    )(jnp.reshape(chip, (1,)).astype(jnp.int32), mine, near, weight, *terms)
 
 
 TN = (((0,), (0,)), ((), ()))
@@ -437,8 +453,9 @@
 
 
 def student_kernel(steps, late, tensor_count, idx_ref, *refs):
-    tokens, refs = refs[:-6], refs[-6:]
-    rights, (left_ref, mixed_ref, student_ref, spread) = refs[:2], refs[2:]
+    tokens, refs = refs[: 8 if late else 4], refs[8 if late else 4 :]
+    rights, left_ref, targets = refs[:2], refs[2], refs[3:-3]
+    mixed_ref, student_ref, spread = refs[-3:]
     step = pl.program_id(0)
     pair = natural(step, idx_ref[2], steps // 2)
     groups = left_ref.shape[0]
@@ -476,7 +493,8 @@
             student = lax.dot_general(
                 mixed_ref[g], left_ref[g], TN, preferred_element_type=F32
             )
-            student_ref[:, span] = student * (1.0 / tensor_count)
+            student = student * (1.0 / tensor_count)
+            student_ref[:, span] = sum((-ref[:, span] for ref in targets), student)
 
 
 def token_specs(half, width, steps, begin, own):
@@ -502,7 +520,7 @@
     return specs(near) + [whole] * 4
 
 
-def student_part(tokens, late, scalars, factors, left_diag, pairs, tensor_count):
+def student_part(tokens, late, scalars, factors, left_diag, targets, pairs, tensor_count):
     parts, _, size = factors.shape
     half = tokens[0].shape[0] // 2
     groups = left_diag.shape[0]
@@ -521,7 +539,8 @@
             num_scalar_prefetch=1,
             grid=(steps,),
             in_specs=token_specs(half, 2 * WIDE * size, steps, 0, not late)
-            + [right_spec(0), right_spec(1), whole_spec(left_diag)],
+            + [right_spec(0), right_spec(1), whole_spec(left_diag)]
+            + [whole_spec(target) for target in targets],
             out_specs=[
                 pl.BlockSpec((groups, BLK, 4 * half), lambda n, s: (0, 0, 0)),
                 pl.BlockSpec((4 * half, groups * BLK), lambda n, s: (0, 0)),
@@ -533,16 +552,14 @@
             jax.ShapeDtypeStruct((4 * half, groups * BLK), F32),
         ],
         compiler_params=pltpu.CompilerParams(vmem_limit_bytes=50 * 2**20),
-        cost_estimate=pl.CostEstimate(
-            flops=10**10, bytes_accessed=10**7, transcendentals=0
-        ),
+        cost_estimate=LARGE,
         name="student_part",
-    )(scalars, *tokens, factors, factors, left_diag)
+    )(scalars, *tokens, factors, factors, left_diag, *targets)
 
 
 def grads_kernel(groups, steps, scale, idx_ref, *refs):
-    hidden, refs = refs[:8], refs[8:]
-    weight_ref, student0, student1, mixed0, mixed1, left_ref = refs[:6]
+    hidden, refs = refs[:4], refs[4:]
+    weight_ref, rest0, rest1, mixed0, mixed1, left_ref = refs[:6]
     own, near, far = refs[6:10], refs[10:14], refs[14:18]
     out_ref, lhs, back, wide = refs[18:]
     step = pl.program_id(0)
@@ -559,13 +576,13 @@
         bits = z ^ owner
         return lax.rem(bits, 2) * 2 + bits // 2
 
-    pl.when(step == 0)(lambda: fill_rows(lhs, hidden, idx_ref[2]))
+    pl.when(step == 0)(lambda: fill_rows(lhs, hidden))
 
     @pl.when(step < groups)
     def _():
         target = jnp.dot(lhs[...], weight_ref[...], preferred_element_type=F32)
-        student = jnp.concatenate([student0[...], student1[...]], axis=0)
-        out_grad = ((student - target) * scale).astype(BF16)
+        rest = jnp.concatenate([rest0[...], rest1[...]], axis=0)
+        out_grad = ((rest - target) * scale).astype(BF16)
         mixed = jnp.concatenate([mixed0[0], mixed1[0]], axis=1)
         left = jnp.dot(mixed, out_grad, preferred_element_type=F32)
         value = lax.dot_general(
@@ -613,10 +630,10 @@
 
 
 def factor_grads(
-    hidden, weight, students, mixed, left_diag, own, late, scalars, parts, size, scale
+    hidden, weight, rest, mixed, left_diag, own, late, scalars, parts, size, scale
 ):
-    groups, count = left_diag.shape[0], 2 * students[0].shape[0]
-    width = weight.shape[0]
+    groups, count = left_diag.shape[0], 2 * rest[0].shape[0]
+    width = hidden[0].shape[1]
     half = own[0].shape[0] // 2
     steps = own[0].shape[1] // (2 * WIDE * size)
     blocks = 2 * steps * WIDE
@@ -634,7 +651,7 @@
             num_scalar_prefetch=1,
             grid=(groups + steps,),
             in_specs=[whole_spec(piece) for piece in hidden]
-            + [pl.BlockSpec((width, BLK), lambda n, s: (0, group(n)))]
+            + [pl.BlockSpec((width, BLK), lambda n, s: (1 - s[2], group(n)))]
             + [column, column, slab, slab]
             + [
                 pl.BlockSpec(
@@ -654,7 +671,7 @@
         compiler_params=pltpu.CompilerParams(vmem_limit_bytes=50 * 2**20),
         cost_estimate=SMALL,
         name="factor_grads",
-    )(scalars, *hidden, weight, *students, *mixed, left_diag, *own, *late)
+    )(scalars, *hidden, weight, *rest, *mixed, left_diag, *own, *late)
 
 
 def tiled_body(tokens, gate_weight, up_weight, down_weight, right_factor, left_factor):
@@ -689,8 +706,9 @@
         return sum(term.astype(F32) for term in terms)
 
     near_tokens = swap(tokens)
-    first, rest = cut_tokens(tokens, odd, chip)
+    first = cut_tokens(tokens, rows, jnp.int32(0), 1 - chip)
     arrived = across(first)
+    turned = turn(after(right_factor, first), 0)
     base = jnp.stack([odd, 1 - odd])
     mine_block = lax.div(part, BLK) * chip
     other_block = lax.div(part, BLK) * (1 - chip)
@@ -700,20 +718,22 @@
 
     own_pieces = [(t, row, 2) for t in (tokens, near_tokens) for row in (0, 1)]
     mine, other = products(
-        own_pieces, after(scalars(other_block), first), gate_weight, up_weight, 0, part
-    )
-    sums = add(mine[0], after(swap(other[0]), arrived)).astype(BF16)
+        own_pieces, after(scalars(other_block), turned), gate_weight, up_weight, 0, part
+    )
+
+    pairs, blocks = left_factor.shape[0], left_factor.shape[2]
+    left_rows = left_factor.reshape(pairs // 2, 2, -1, blocks).transpose(0, 2, 1, 3)
+    factors = jnp.concatenate(
+        [turned.reshape(-1, LANES), left_rows.reshape(-1, LANES)], axis=0
+    )[None]
+    more = along(after(factors, mine), 1)
+    rest = cut_tokens(after(tokens, mine), rows // 2, odd, chip, LARGE)
+    sums = add(mine[0], swap(other[0])).astype(BF16)
+    arrived = after(arrived, more, rest, sums)
     got_early = across(sums)
     late_first = across(after(rest, sums))
-
-    pairs, blocks = left_factor.shape[0], left_factor.shape[2]
-    left_rows = left_factor.reshape(pairs // 2, 2, -1, blocks).transpose(0, 2, 1, 3)
-    factors = turn(after(right_factor, first), 0)
-    factors = jnp.concatenate(
-        [factors.reshape(-1, LANES), left_rows.reshape(-1, LANES)], axis=0
-    )
-    factors = after(factors, sums)[None]
-    more = along(factors, 1)
+    factors = jnp.concatenate([factors, more], axis=0)
+    more = along(after(factors, arrived), 2)
 
     order = jnp.concatenate([base, jnp.stack([chip, z])]).astype(jnp.int32)
     own = [tokens, tokens, near_tokens, near_tokens]
@@ -722,19 +742,15 @@
     late_order = after(scalars(other_block), sums)
     mine, other = products(late_pieces, late_order, gate_weight, up_weight, 0, part)
     near = swap(other[0])
-    factors = after(jnp.concatenate([factors, more], axis=0), mine)
-    more = along(factors, 2)
     mine_order = after(scalars(mine_block), mine)
     kept, other = products(
         own_pieces + late_pieces, mine_order, gate_weight, up_weight, 0, part
     )
-    near_kept = swap(after(other, got_early, late_first, more))
     sums = add(mine[0], after(near, kept)).astype(BF16)
     got = across(sums)
+    near_kept = swap(after(other, got_early, late_first, more, sums))
 
     factors = jnp.concatenate([factors, after(more, kept)], axis=0)
-    left_diag = spread_left(order, factors, pairs * blocks // BLK)
-
     def activate(u, term):
         total = add(kept[u], near_kept[u], term)
         return (jax.nn.silu(total[0]) * total[1]).astype(BF16)
@@ -742,38 +758,44 @@
     hidden1 = activate(1, got_early)
     got1 = across(hidden1)
     near1 = swap(hidden1)
-    late_partner = along(after(late_first, kept), 1)
-    mixed0, student0 = student_part(
+    left_diag = spread_left(order, after(factors, hidden1), pairs * blocks // BLK)
+    late_partner = along(after(late_first, hidden1), 1)
+    mixed0, rest0 = student_part(
         [after(tokens, hidden1, sums)] + own[1:],
         False,
         order,
         factors,
         left_diag,
+        [],
         pairs,
         tensor_count,
     )
-    hidden0 = activate(0, after(got, mixed0))
+    target1 = target_part(1.0, [], hidden1, after(near1, mixed0), down_weight, chip)
+    hidden0 = activate(0, after(got, target1))
     got0 = across(hidden0)
     near0 = swap(hidden0)
     late_partner = after(late_partner, mixed0)
     late = [arrived, arrived, near_arrived, near_arrived]
     late += [late_first, late_partner, swap(late_first), swap(late_partner)]
-    mixed1, student1 = student_part(
+    mixed1, rest1 = student_part(
         [after(arrived, hidden0)] + late[1:],
         True,
         order,
         factors,
         left_diag,
+        [target1],
         pairs,
         tensor_count,
     )
-    got1, got0 = after(got1, mixed1), after(got0, mixed1)
-    hidden = [hidden0, hidden1, near0, near1, got0, got1, swap(got0), swap(got1)]
+    near0 = after(near0, mixed1)
+    rest0 = target_part(-1.0, [rest0], hidden0, near0, down_weight, chip)
+    got1, got0 = after(got1, mixed1), after(got0, rest0)
+    hidden = [got0, got1, swap(got0), swap(got1)]
 
     grads = factor_grads(
         hidden,
         down_weight,
-        (student0, student1),
+        (rest0, rest1),
         (mixed0, mixed1),
         left_diag,
         own,

time: 185 us -> 173 us (0.935)
  waiting for transfers between devices: 59.6 us -> 36.9 us
  Pallas kernels: 77.3 us -> 90.1 us
  starting transfers between devices: 29.7 us -> 24.2 us
    ppermute x6, waiting for transfers between devices: 33.7 us -> 14.5 us  [across(): return lax.ppermute(value, 'fsdp', [(i, i ^ 2) for i in range(fsdp_count)])]
    pallas_call x0 -> x2, Pallas kernels: none -> 14.7 us  [target_part(): pl.pallas_call(functools.partial(target_kernel, sign), grid_spec=pltpu.Pr...]
    ppermute x3, waiting for transfers between devices: 11.4 us -> 4.69 us  [turn(): return lax.ppermute(value, both_axes, perm)]
    ppermute x6, starting transfers between devices: 17.9 us -> 11.7 us  [across(): return lax.ppermute(value, 'fsdp', [(i, i ^ 2) for i in range(fsdp_count)])]
    pallas_call x1, Pallas kernels: 23.6 us -> 19 us  [factor_grads(): pl.pallas_call(functools.partial(grads_kernel, groups, steps, scale), gri...]
    ppermute x5, waiting for transfers between devices: 12.6 us -> 15.5 us  [along(): lax.ppermute(value, 'tensor', [(i, i ^ bit) for i in range(tensor_count)])]
    unnamed x33 -> x36, local copies, waits for them, and re-layouts: 3.85 us -> 6.52 us
    pallas_call x1 -> x2, Pallas kernels: 3.41 us -> 5.61 us  [cut_tokens(): pl.pallas_call(cut_kernel, grid_spec=pltpu.PrefetchScalarGridSpec(num_sca...]
  transfers between devices with their start and end apart: 25 -> 25, of which waited for: 9 -> 7; matrix products, arithmetic and copies ran while one was open for 6% -> 6% of each run, Pallas kernels for 29% -> 42%
where the time goes in v8:
time: 173 us; the launch traced here: 171 us
  Pallas kernels  90.1 us (52%)
  waiting for transfers between devices  36.9 us (21%)
  starting transfers between devices  24.2 us (14%)
  other arithmetic  9.99 us (6%)
  local copies, waits for them, and re-layouts  8.86 us (5%)
    pallas_call x3, Pallas kernels, products(): pl.pallas_call(functools.partial(products_kernel, sets), grid_spec=pltpu....  34 us
    pallas_call x1, Pallas kernels, factor_grads(): pl.pallas_call(functools.partial(grads_kernel, groups, steps, scale), gri...  19 us
    ppermute x5, waiting for transfers between devices, along(): lax.ppermute(value, 'tensor', [(i, i ^ bit) for i in range(tensor_count)])  15.5 us
    pallas_call x2, Pallas kernels, target_part(): pl.pallas_call(functools.partial(target_kernel, sign), grid_spec=pltpu.Pr...  14.7 us
    ppermute x6, waiting for transfers between devices, across(): return lax.ppermute(value, 'fsdp', [(i, i ^ 2) for i in range(fsdp_count)])  14.5 us
    pallas_call x2, Pallas kernels, student_part(): pl.pallas_call(functools.partial(student_kernel, steps, late, tensor_coun...  13.8 us
    ppermute x6, starting transfers between devices, across(): return lax.ppermute(value, 'fsdp', [(i, i ^ 2) for i in range(fsdp_count)])  11.7 us
    ppermute x5, starting transfers between devices, along(): lax.ppermute(value, 'tensor', [(i, i ^ bit) for i in range(tensor_count)])  6.82 us
  transfers between devices with their start and end apart: 25, of which 7 were waited for; matrix products, arithmetic and copies ran while one was open for 6% of the time, Pallas kernels for 42%

profile of v8, /device:TPU:0, one launch (start us, length us, event | category | flops | bytes accessed | tf_op | source)
XLA Modules:
  0.0 170.8 jit_solution(723717841144794806)
XLA Ops:
  0.6 0.5 collective-permute-start.1
  1.2 0.6 pad_add_fusion.1.idx_ref
  1.7 3.1 %cut_tokens.2 = bf16[128,4096]{1,0:T(8,128)(2,1)} custom-call(s32[2]{0:T(128)} %pad_add_fusion.1.idx_ref, bf16[128,8192]{1,0:T(8,128)(2,1)} %refs_11_.1), custom_call_target="tpu_custom_call" | custom-call | flops 1 | bytes 1 | tf_op jit(solution)/shard_map/cut_tokens/pallas_call | solution.py:311
  4.8 1.6 collective-permute-start
  6.4 5.5 %collective-permute-start.3 = (bf16[128,4096]{1,0:T(8,128)(2,1)}, bf16[128,4096]{1,0:T(8,128)(2,1)S(1)}, u32[]{:S(2)}, u32[]{:S(2)}) collective-permute-start(bf16[128,4096]{1,0:T(8,128)(2,1)} %cut_tokens.2), channel_id=1, source_target_pairs={{0,8},{4,12},{8,0},{12,4},{1,9},{5,13},{9,1},{13,5},{2,10},{6,14},... | collective-permute-start | bytes 3145736 | tf_op jit(solution)/shard_map/ppermute | solution.py:690
  11.9 0.1 copy.11
  12.0 0.1 reshape.38
  12.1 0.1 concatenate.26.idx_ref
  12.2 0.7 pad_add_fusion.2.idx_ref
  12.9 10.8 %gate_up_products.3 = (bf16[1,2,128,1792]{3,2,1,0:T(8,128)(2,1)S(1)}, bf16[1,2,128,1792]{3,2,1,0:T(8,128)(2,1)}) custom-call(s32[5]{0:T(128)S(1)} %concatenate.26.idx_ref, bf16[128,8192]{1,0:T(8,128)(2,1)S(1)} %copy-done, bf16[128,8192]{1,0:T(8,128)(2,1)S(1)} %copy-done, bf16[128,8192]{1,0:T(8,128)(2,1)} %collective-permute-done.1.refs_2_.refs_3_.refs_12_.refs_13_, ...), custom_call_target="tpu_custom_call" | custom-call | flops 1 | bytes 1 | tf_op jit(solution)/shard_map/gate_up_products/pallas_call | solution.py:350
  23.7 1.0 copy-done.11
  24.6 0.8 collective-permute-start.2
  25.5 0.7 collective-permute-start.4
  26.1 2.5 %cut_tokens.3 = bf16[64,4096]{1,0:T(8,128)(2,1)} custom-call(s32[2]{0:T(128)} %pad_add_fusion.2.idx_ref, bf16[128,8192]{1,0:T(8,128)(2,1)} %refs_11_.1), custom_call_target="tpu_custom_call" | custom-call | flops 10000000000 | bytes 10000000 | tf_op jit(solution)/shard_map/cut_tokens/pallas_call | solution.py:311
  28.7 1.2 fusion.1
  29.9 8.1 %collective-permute-done.3.refs_0_.refs_1_.refs_4_.refs_5_.refs_14_.refs_15_ = bf16[128,4096]{1,0:T(8,128)(2,1)S(1)} collective-permute-done((bf16[128,4096]{1,0:T(8,128)(2,1)}, bf16[128,4096]{1,0:T(8,128)(2,1)S(1)}, u32[]{:S(2)}, u32[]{:S(2)}) %collective-permute-start.3) | collective-permute-done | bytes 1048608 | tf_op jit(solution)/shard_map/ppermute | solution.py:690
  38.0 0.3 collective-permute-start.5
  38.3 0.1 concatenate.25.idx_ref
  38.4 2.3 %collective-permute-start.6 = (bf16[2,128,1792]{2,1,0:T(8,128)(2,1)}, bf16[2,128,1792]{2,1,0:T(8,128)(2,1)S(1)}, u32[]{:S(2)}, u32[]{:S(2)}) collective-permute-start(bf16[2,128,1792]{2,1,0:T(8,128)(2,1)} %fusion.1), channel_id=1, source_target_pairs={{0,8},{4,12},{8,0},{12,4},{1,9},{5,13},{9,1},{13,5},{2,10},{6,14},... | collective-permute-start | bytes 2752520 | tf_op jit(solution)/shard_map/ppermute | solution.py:690
  40.8 1.4 collective-permute-start.8
  42.2 10.0 %gate_up_products.4 = (bf16[1,2,128,1792]{3,2,1,0:T(8,128)(2,1)S(1)}, bf16[1,2,128,1792]{3,2,1,0:T(8,128)(2,1)S(1)}) custom-call(s32[5]{0:T(128)S(1)} %concatenate.26.idx_ref, bf16[128,4096]{1,0:T(8,128)(2,1)S(1)} %collective-permute-done.3.refs_0_.refs_1_.refs_4_.refs_5_.refs_14_.refs_15_, ...), custom_call_target="tpu_custom_call" | custom-call | flops 1 | bytes 1 | tf_op jit(solution)/shard_map/gate_up_products/pallas_call | solution.py:350
  52.3 13.3 %gate_up_products.5 = (bf16[2,2,128,1792]{3,2,1,0:T(8,128)(2,1)S(1)}, bf16[2,2,128,1792]{3,2,1,0:T(8,128)(2,1)}) custom-call(s32[5]{0:T(128)S(1)} %concatenate.25.idx_ref, bf16[128,8192]{1,0:T(8,128)(2,1)} %refs_11_.1, bf16[128,8192]{1,0:T(8,128)(2,1)} %refs_11_.1, bf16[128,8192]{1,0:T(8,128)(2,1)} %collective-permute-done.1.refs_2_.refs_3_.refs_12_.refs_13_, ...), custom_call_target="tpu_custom_call" | custom-call | flops 10000000000 | bytes 10000000 | tf_op jit(solution)/shard_map/gate_up_products/pallas_call | solution.py:350
  65.6 1.2 fusion
  66.7 6.3 %collective-permute-done.7.refs_4_.refs_18_ = bf16[64,4096]{1,0:T(8,128)(2,1)S(1)} collective-permute-done((bf16[64,4096]{1,0:T(8,128)(2,1)}, bf16[64,4096]{1,0:T(8,128)(2,1)S(1)}, u32[]{:S(2)}, u32[]{:S(2)}) %collective-permute-start.7) | collective-permute-done | bytes 524320 | tf_op jit(solution)/shard_map/ppermute | solution.py:690
  73.1 0.6 pad_add_fusion.idx_ref
  73.7 0.5 collective-permute-start.16
  74.2 1.0 pad_maximum_fusion.rows_ref.refs_4_.refs_5_.refs_8_.refs_9_
  75.1 1.7 %collective-permute-start.11 = (bf16[2,128,1792]{2,1,0:T(8,128)(2,1)}, bf16[2,128,1792]{2,1,0:T(8,128)(2,1)}, u32[]{:S(2)}, u32[]{:S(2)}) collective-permute-start(bf16[2,128,1792]{2,1,0:T(8,128)(2,1)} %fusion), channel_id=1, source_target_pairs={{0,8},{4,12},{8,0},{12,4},{1,9},{5,13},{9,1},{13,5},{2,10},{6,14},... | collective-permute-start | bytes 2752520 | tf_op jit(solution)/shard_map/ppermute | solution.py:690
  76.9 0.3 bitcast_add_fusion
  77.2 1.0 copy-done.14
  78.1 0.3 fusion.5.mine_ref
  78.4 0.2 collective-permute-start.12
  78.6 1.8 %collective-permute-start.18 = (bf16[128,1792]{1,0:T(8,128)(2,1)S(1)}, bf16[128,1792]{1,0:T(8,128)(2,1)}, u32[]{:S(2)}, u32[]{:S(2)}) collective-permute-start(bf16[128,1792]{1,0:T(8,128)(2,1)S(1)} %fusion.5.mine_ref), channel_id=1, source_target_pairs={{0,8},{4,12},{8,0},{12,4},{1,9},{5,13},{9,1},{13,5},{2,10},{6,14},... | collective-permute-start | bytes 1376264 | tf_op jit(solution)/shard_map/ppermute | solution.py:690
  80.3 0.1 collective-permute-start.15
  80.4 3.0 %spread_left.1.refs_6_.refs_10_.refs_9_ = bf16[8,256,256]{2,1,0:T(8,128)(2,1)} custom-call(s32[4]{0:T(128)} %pad_add_fusion.idx_ref, bf16[4,768,128]{2,1,0:T(8,128)(2,1)} %pad_maximum_fusion.rows_ref.refs_4_.refs_5_.refs_8_.refs_9_), custom_call_target="tpu_custom_call" | custom-call | flops 1 | bytes 1 | tf_op jit(solution)/shard_map/spread_left/pallas_call | solution.py:440
  83.4 1.2 copy-done.4
  84.7 6.5 %student_part.2 = (bf16[8,256,256]{2,1,0:T(8,128)(2,1)S(1)}, f32[256,2048]{1,0:T(8,128)}) custom-call(s32[4]{0:T(128)S(1)} %copy-done.13, bf16[128,8192]{1,0:T(8,128)(2,1)} %refs_11_.1, bf16[128,8192]{1,0:T(8,128)(2,1)} %refs_11_.1, bf16[128,8192]{1,0:T(8,128)(2,1)} %collective-permute-done.1.refs_2_.refs_3_.refs_12_.refs_13_, ...), custom_call_target="tpu_custom_call" | custom-call | flops 10000000000 | bytes 10000000 | tf_op jit(solution)/shard_map/student_part/pallas_call | solution.py:536
  91.2 1.0 copy-done.9
  92.2 7.2 %target_part.2.refs_11_ = f32[256,2048]{1,0:T(8,128)S(1)} custom-call(s32[1]{0:T(128)} %bitcast.2.idx_ref, bf16[128,1792]{1,0:T(8,128)(2,1)S(1)} %fusion.5.mine_ref, bf16[128,1792]{1,0:T(8,128)(2,1)S(1)} %collective-permute-done.12.near_ref, bf16[3584,2048]{1,0:T(8,128)(2,1)} %refs_4_.5), custom_call_target="tpu_custom_call" | custom-call | flops 1 | bytes 1 | tf_op jit(solution)/shard_map/target_part/pallas_call | solution.py:387
  99.6 2.1 %bitcast_add_fusion.1 = f32[2,128,1792]{2,1,0:T(8,128)S(1)} fusion(bf16[2,128,1792]{2,1,0:T(8,128)(2,1)} %collective-permute-done.11, bf16[2,2,128,1792]{3,2,1,0:T(8,128)(2,1)S(1)} %copy-done.15, bf16[2,2,128,1792]{3,2,1,0:T(8,128)(2,1)S(1)} %copy-done.8), kind=kLoop, calls=%fused_computation.5 | loop fusion | flops 2293760 | bytes 4587520 | tf_op jit(solution)/shard_map/add | solution.py:706
  101.7 0.3 fusion.3.mine_ref
  102.0 0.3 collective-permute-start.13
  102.3 0.2 collective-permute-start.14
  102.5 7.2 %student_part.3 = (bf16[8,256,256]{2,1,0:T(8,128)(2,1)S(1)}, f32[256,2048]{1,0:T(8,128)}) custom-call(s32[4]{0:T(128)S(1)} %copy-done.13, bf16[128,4096]{1,0:T(8,128)(2,1)} %copy-done.1, bf16[128,4096]{1,0:T(8,128)(2,1)} %copy-done.1, bf16[128,4096]{1,0:T(8,128)(2,1)} %copy-done.2, bf16[128,4096]{1,0:T(8,128)(2,1)} %copy-done.2, ...), custom_call_target="tpu_custom_call" | custom-call | flops 10000000000 | bytes 10000000 | tf_op jit(solution)/shard_map/student_part/pallas_call | solution.py:536
  109.7 1.0 copy-done.10
  110.7 7.4 %target_part.3.refs_5_ = f32[256,2048]{1,0:T(8,128)S(1)} custom-call(s32[1]{0:T(128)} %bitcast.2.idx_ref, bf16[128,1792]{1,0:T(8,128)(2,1)S(1)} %fusion.3.mine_ref, bf16[128,1792]{1,0:T(8,128)(2,1)S(1)} %collective-permute-done.14.near_ref, bf16[3584,2048]{1,0:T(8,128)(2,1)} %refs_4_.5, f32[256,2048]{1,0:T(8,128)} %get-tuple-element.62.refs_0_), custom_call_target="tpu_custom_call" | custom-call | flops 1 | bytes 1 | tf_op jit(solution)/shard_map/target_part/pallas_call | solution.py:387
  118.1 1.4 copy-done.3
  119.5 0.4 collective-permute-start.19
  119.8 0.2 collective-permute-start.20
  120.0 1.3 collective-permute-done.19.refs_2_
  121.3 0.9 collective-permute-done.20.refs_3_
  122.1 19.0 %factor_grads.1 = bf16[4,768,128]{2,1,0:T(8,128)(2,1)} custom-call(s32[4]{0:T(128)S(1)} %copy-done.13, bf16[128,1792]{1,0:T(8,128)(2,1)S(1)} %collective-permute-done.13.refs_0_, bf16[128,1792]{1,0:T(8,128)(2,1)} %collective-permute-done.18.refs_1_, bf16[128,1792]{1,0:T(8,128)(2,1)S(1)} %collective-permute-done.19.refs_2_, ...), custom_call_target="tpu_custom_call" | custom-call | flops 1 | bytes 1 | tf_op jit(solution)/shard_map/factor_grads/pallas_call | solution.py:648
  141.2 1.0 slice.63
  142.2 2.0 %collective-permute-start.21 = (bf16[2,768,128]{2,1,0:T(8,128)(2,1)S(1)}, bf16[2,768,128]{2,1,0:T(8,128)(2,1)S(1)}, u32[]{:S(2)}, u32[]{:S(2)}) collective-permute-start(bf16[2,768,128]{2,1,0:T(8,128)(2,1)S(1)} %slice.63), channel_id=1, source_target_pairs={{0,1},{1,0},{2,3},{3,2},{4,5},{5,4},{6,7},{7,6},{8,9},{9,8},{10,11... | collective-permute-start | bytes 1179656 | tf_op jit(solution)/shard_map/ppermute | solution.py:693
  144.2 9.6 %collective-permute-done.21 = bf16[2,768,128]{2,1,0:T(8,128)(2,1)S(1)} collective-permute-done((bf16[2,768,128]{2,1,0:T(8,128)(2,1)S(1)}, bf16[2,768,128]{2,1,0:T(8,128)(2,1)S(1)}, u32[]{:S(2)}, u32[]{:S(2)}) %collective-permute-start.21) | collective-permute-done | bytes 393248 | tf_op jit(solution)/shard_map/ppermute | solution.py:693
  153.9 1.1 add_convert_fusion
  155.0 2.7 %collective-permute-start.24 = (bf16[256,128]{1,0:T(8,128)(2,1)S(1)}, bf16[256,128]{1,0:T(8,128)(2,1)S(1)}, u32[]{:S(2)}, u32[]{:S(2)}) collective-permute-start(bf16[256,128]{1,0:T(8,128)(2,1)S(1)} %slice_bitcast_fusion.6), channel_id=1, source_target_pairs={{0,2},{1,3},{2,0},{3,1},{4,6},{5,7},{6,4},{7,5},{8,10},{9,11},{10,... | collective-permute-start | bytes 196616 | tf_op jit(solution)/shard_map/ppermute | solution.py:693
  157.7 0.3 collective-permute-start.23
  158.0 0.7 collective-permute-start.22
  158.6 5.9 %collective-permute-done.24 = bf16[256,128]{1,0:T(8,128)(2,1)S(1)} collective-permute-done((bf16[256,128]{1,0:T(8,128)(2,1)S(1)}, bf16[256,128]{1,0:T(8,128)(2,1)S(1)}, u32[]{:S(2)}, u32[]{:S(2)}) %collective-permute-start.24) | collective-permute-done | bytes 65568 | tf_op jit(solution)/shard_map/ppermute | solution.py:693
  164.5 0.2 reshape.40
  164.7 0.7 copy.9
  165.4 4.7 %collective-permute-done.23 = bf16[512,128]{1,0:T(8,128)(2,1)S(1)} collective-permute-done((bf16[512,128]{1,0:T(8,128)(2,1)S(1)}, bf16[512,128]{1,0:T(8,128)(2,1)S(1)}, u32[]{:S(2)}, u32[]{:S(2)}) %collective-permute-start.23) | collective-permute-done | bytes 131104 | tf_op jit(solution)/shard_map/ppermute | solution.py:700
  170.1 0.7 convert_add_fusion.2
  (57 shorter events, 0.4 us)
Async XLA Ops:
  0.6 11.2 %copy-start.16 = (bf16[32,16,64]{2,1,0:T(8,128)(2,1)S(1)}, bf16[32,16,64]{2,1,0:T(8,128)(2,1)}, u32[]{:S(2)}) copy-start(bf16[32,16,64]{2,1,0:T(8,128)(2,1)} %param.11) | copy-start | bytes 196612
  0.6 12.2 %collective-permute-start.1 = (bf16[128,8192]{1,0:T(8,128)(2,1)}, bf16[128,8192]{1,0:T(8,128)(2,1)}, u32[]{:S(2)}, u32[]{:S(2)}) collective-permute-start(bf16[128,8192]{1,0:T(8,128)(2,1)} %refs_11_.1), channel_id=1, source_target_pairs={{0,4},{4,0},{8,12},{12,8},{1,5},{5,1},{9,13},{13,9},{2,6},{6,2},{1... | collective-permute-start | bytes 6291464 | tf_op jit(solution)/shard_map/ppermute | solution.py:687
  1.7 11.1 %copy-start = (bf16[128,8192]{1,0:T(8,128)(2,1)S(1)}, bf16[128,8192]{1,0:T(8,128)(2,1)}, u32[]{:S(2)}) copy-start(bf16[128,8192]{1,0:T(8,128)(2,1)} %refs_11_.1) | copy-start | bytes 6291460
  4.8 8.0 %collective-permute-start = (bf16[16,32,128]{2,1,0:T(8,128)(2,1)}, bf16[16,32,128]{2,1,0:T(8,128)(2,1)S(1)}, u32[]{:S(2)}, u32[]{:S(2)}) collective-permute-start(bf16[16,32,128]{2,1,0:T(8,128)(2,1)} %param.10), channel_id=1, source_target_pairs={{0,0},{1,4},{2,8},{3,12},{4,1},{5,5},{6,9},{7,13},{8,2},{9,6},{10,... | collective-permute-start | bytes 393224 | tf_op jit(solution)/shard_map/ppermute | solution.py:700
  6.4 31.7 %collective-permute-start.3 = (bf16[128,4096]{1,0:T(8,128)(2,1)}, bf16[128,4096]{1,0:T(8,128)(2,1)S(1)}, u32[]{:S(2)}, u32[]{:S(2)}) collective-permute-start(bf16[128,4096]{1,0:T(8,128)(2,1)} %cut_tokens.2), channel_id=1, source_target_pairs={{0,8},{4,12},{8,0},{12,4},{1,9},{5,13},{9,1},{13,5},{2,10},{6,14},... | collective-permute-start | bytes 3145736 | tf_op jit(solution)/shard_map/ppermute | solution.py:690
  23.7 1.0 copy-start.11
  24.6 4.1 %collective-permute-start.2 = (bf16[2,128,1792]{2,1,0:T(8,128)(2,1)}, bf16[2,128,1792]{2,1,0:T(8,128)(2,1)S(1)}, u32[]{:S(2)}, u32[]{:S(2)}) collective-permute-start(bf16[2,128,1792]{2,1,0:T(8,128)(2,1)} %bitcast.10), channel_id=1, source_target_pairs={{0,4},{4,0},{8,12},{12,8},{1,5},{5,1},{9,13},{13,9},{2,6},{6,2},{1... | collective-permute-start | bytes 2752520 | tf_op jit(solution)/shard_map/ppermute | solution.py:687
  25.5 3.2 %copy-start.12 = (bf16[1,2,128,1792]{3,2,1,0:T(8,128)(2,1)S(1)}, bf16[1,2,128,1792]{3,2,1,0:T(8,128)(2,1)}, u32[]{:S(2)}) copy-start(bf16[1,2,128,1792]{3,2,1,0:T(8,128)(2,1)} %copy-done.11) | copy-start | bytes 2752516
  25.5 12.5 %collective-permute-start.4 = (bf16[1,768,128]{2,1,0:T(8,128)(2,1)S(1)}, bf16[1,768,128]{2,1,0:T(8,128)(2,1)S(1)}, u32[]{:S(2)}, u32[]{:S(2)}) collective-permute-start(bf16[1,768,128]{2,1,0:T(8,128)(2,1)S(1)} %maximum_bitcast_fusion), channel_id=1, source_target_pairs={{0,1},{1,0},{2,3},{3,2},{4,5},{5,4},{6,7},{7,6},{8,9},{9,8},{10,11... | collective-permute-start | bytes 589832 | tf_op jit(solution)/shard_map/ppermute | solution.py:693
  38.0 14.2 %copy-start.1 = (bf16[128,4096]{1,0:T(8,128)(2,1)}, bf16[128,4096]{1,0:T(8,128)(2,1)S(1)}, u32[]{:S(2)}) copy-start(bf16[128,4096]{1,0:T(8,128)(2,1)S(1)} %collective-permute-done.3.refs_0_.refs_1_.refs_4_.refs_5_.refs_14_.refs_15_) | copy-start | bytes 3145732
  38.0 4.2 %collective-permute-start.5 = (bf16[128,4096]{1,0:T(8,128)(2,1)S(1)}, bf16[128,4096]{1,0:T(8,128)(2,1)S(1)}, u32[]{:S(2)}, u32[]{:S(2)}) collective-permute-start(bf16[128,4096]{1,0:T(8,128)(2,1)S(1)} %collective-permute-done.3.refs_0_.refs_1_.refs_4_.refs_5_.refs_14_.refs_15_), channel_id=1, source_target_pairs={{0,4},{4,0},{8,12},{12,8},{1,5},{5,1},{9,13},{13,9},{2,6},{6,2},{1... | collective-permute-start | bytes 3145736 | tf_op jit(solution)/shard_map/ppermute | solution.py:687
  38.4 34.6 %collective-permute-start.6 = (bf16[2,128,1792]{2,1,0:T(8,128)(2,1)}, bf16[2,128,1792]{2,1,0:T(8,128)(2,1)S(1)}, u32[]{:S(2)}, u32[]{:S(2)}) collective-permute-start(bf16[2,128,1792]{2,1,0:T(8,128)(2,1)} %fusion.1), channel_id=1, source_target_pairs={{0,8},{4,12},{8,0},{12,4},{1,9},{5,13},{9,1},{13,5},{2,10},{6,14},... | collective-permute-start | bytes 2752520 | tf_op jit(solution)/shard_map/ppermute | solution.py:690
  40.7 32.3 %collective-permute-start.7 = (bf16[64,4096]{1,0:T(8,128)(2,1)}, bf16[64,4096]{1,0:T(8,128)(2,1)S(1)}, u32[]{:S(2)}, u32[]{:S(2)}) collective-permute-start(bf16[64,4096]{1,0:T(8,128)(2,1)} %cut_tokens.3), channel_id=1, source_target_pairs={{0,8},{4,12},{8,0},{12,4},{1,9},{5,13},{9,1},{13,5},{2,10},{6,14},... | collective-permute-start | bytes 1572872 | tf_op jit(solution)/shard_map/ppermute | solution.py:690
  40.8 25.9 %collective-permute-start.8 = (bf16[2,768,128]{2,1,0:T(8,128)(2,1)S(1)}, bf16[2,768,128]{2,1,0:T(8,128)(2,1)S(1)}, u32[]{:S(2)}, u32[]{:S(2)}) collective-permute-start(bf16[2,768,128]{2,1,0:T(8,128)(2,1)S(1)} %pad_maximum_fusion.1), channel_id=1, source_target_pairs={{0,2},{1,3},{2,0},{3,1},{4,6},{5,7},{6,4},{7,5},{8,10},{9,11},{10,... | collective-permute-start | bytes 1179656 | tf_op jit(solution)/shard_map/ppermute | solution.py:693
  42.2 10.1 %copy-start.2 = (bf16[128,4096]{1,0:T(8,128)(2,1)}, bf16[128,4096]{1,0:T(8,128)(2,1)S(1)}, u32[]{:S(2)}) copy-start(bf16[128,4096]{1,0:T(8,128)(2,1)S(1)} %collective-permute-done.5.refs_2_.refs_3_.refs_6_.refs_7_.refs_16_.refs_17_) | copy-start | bytes 3145732
  52.2 13.4 %collective-permute-start.9 = (bf16[2,128,1792]{2,1,0:T(8,128)(2,1)S(1)}, bf16[2,128,1792]{2,1,0:T(8,128)(2,1)S(1)}, u32[]{:S(2)}, u32[]{:S(2)}) collective-permute-start(bf16[2,128,1792]{2,1,0:T(8,128)(2,1)S(1)} %bitcast.62), channel_id=1, source_target_pairs={{0,4},{4,0},{8,12},{12,8},{1,5},{5,1},{9,13},{13,9},{2,6},{6,2},{1... | collective-permute-start | bytes 2752520 | tf_op jit(solution)/shard_map/ppermute | solution.py:687
  65.5 11.3 %copy-start.7 = (bf16[2,2,128,1792]{3,2,1,0:T(8,128)(2,1)}, bf16[2,2,128,1792]{3,2,1,0:T(8,128)(2,1)S(1)}, u32[]{:S(2)}) copy-start(bf16[2,2,128,1792]{3,2,1,0:T(8,128)(2,1)S(1)} %get-tuple-element.44) | copy-start | bytes 5505028
  65.5 7.5 %copy-start.17 = (bf16[2,2,128,1792]{3,2,1,0:T(8,128)(2,1)S(1)}, bf16[2,2,128,1792]{3,2,1,0:T(8,128)(2,1)}, u32[]{:S(2)}) copy-start(bf16[2,2,128,1792]{3,2,1,0:T(8,128)(2,1)} %get-tuple-element.50) | copy-start | bytes 5505028
  73.1 3.8 %collective-permute-start.10 = (bf16[2,2,128,1792]{3,2,1,0:T(8,128)(2,1)S(1)}, bf16[2,2,128,1792]{3,2,1,0:T(8,128)(2,1)S(1)}, u32[]{:S(2)}, u32[]{:S(2)}) collective-permute-start(bf16[2,2,128,1792]{3,2,1,0:T(8,128)(2,1)S(1)} %copy-done.17), channel_id=1, source_target_pairs={{0,4},{4,0},{8,12},{12,8},{1,5},{5,1},{9,13},{13,9},{2,6},{6,2},{1... | collective-permute-start | bytes 5505032 | tf_op jit(solution)/shard_map/ppermute | solution.py:687
  73.7 28.8 %collective-permute-start.16 = (bf16[64,4096]{1,0:T(8,128)(2,1)S(1)}, bf16[64,4096]{1,0:T(8,128)(2,1)S(1)}, u32[]{:S(2)}, u32[]{:S(2)}) collective-permute-start(bf16[64,4096]{1,0:T(8,128)(2,1)S(1)} %collective-permute-done.7.refs_4_.refs_18_), channel_id=1, source_target_pairs={{0,4},{4,0},{8,12},{12,8},{1,5},{5,1},{9,13},{13,9},{2,6},{6,2},{1... | collective-permute-start | bytes 1572872 | tf_op jit(solution)/shard_map/ppermute | solution.py:687
  75.1 24.4 %collective-permute-start.11 = (bf16[2,128,1792]{2,1,0:T(8,128)(2,1)}, bf16[2,128,1792]{2,1,0:T(8,128)(2,1)}, u32[]{:S(2)}, u32[]{:S(2)}) collective-permute-start(bf16[2,128,1792]{2,1,0:T(8,128)(2,1)} %fusion), channel_id=1, source_target_pairs={{0,8},{4,12},{8,0},{12,4},{1,9},{5,13},{9,1},{13,5},{2,10},{6,14},... | collective-permute-start | bytes 2752520 | tf_op jit(solution)/shard_map/ppermute | solution.py:690
  76.9 1.3 copy-start.14
  78.1 5.3 %copy-start.5 = (bf16[4,768,128]{2,1,0:T(8,128)(2,1)S(1)}, bf16[4,768,128]{2,1,0:T(8,128)(2,1)}, u32[]{:S(2)}) copy-start(bf16[4,768,128]{2,1,0:T(8,128)(2,1)} %pad_maximum_fusion.rows_ref.refs_4_.refs_5_.refs_8_.refs_9_) | copy-start | bytes 2359300
  78.1 5.3 %copy-start.13 = (s32[4]{0:T(128)S(1)}, s32[4]{0:T(128)}, u32[]{:S(2)}) copy-start(s32[4]{0:T(128)} %pad_add_fusion.idx_ref) | copy-start | bytes 52
  78.4 13.8 %collective-permute-start.12 = (bf16[128,1792]{1,0:T(8,128)(2,1)S(1)}, bf16[128,1792]{1,0:T(8,128)(2,1)S(1)}, u32[]{:S(2)}, u32[]{:S(2)}) collective-permute-start(bf16[128,1792]{1,0:T(8,128)(2,1)S(1)} %fusion.5.mine_ref), channel_id=1, source_target_pairs={{0,4},{4,0},{8,12},{12,8},{1,5},{5,1},{9,13},{13,9},{2,6},{6,2},{1... | collective-permute-start | bytes 1376264 | tf_op jit(solution)/shard_map/ppermute | solution.py:687
  78.6 40.9 %collective-permute-start.18 = (bf16[128,1792]{1,0:T(8,128)(2,1)S(1)}, bf16[128,1792]{1,0:T(8,128)(2,1)}, u32[]{:S(2)}, u32[]{:S(2)}) collective-permute-start(bf16[128,1792]{1,0:T(8,128)(2,1)S(1)} %fusion.5.mine_ref), channel_id=1, source_target_pairs={{0,8},{4,12},{8,0},{12,4},{1,9},{5,13},{9,1},{13,5},{2,10},{6,14},... | collective-permute-start | bytes 1376264 | tf_op jit(solution)/shard_map/ppermute | solution.py:690
  80.3 19.1 %collective-permute-start.15 = (bf16[64,4096]{1,0:T(8,128)(2,1)S(1)}, bf16[64,4096]{1,0:T(8,128)(2,1)S(1)}, u32[]{:S(2)}, u32[]{:S(2)}) collective-permute-start(bf16[64,4096]{1,0:T(8,128)(2,1)S(1)} %collective-permute-done.7.refs_4_.refs_18_), channel_id=1, source_target_pairs={{0,1},{1,0},{2,3},{3,2},{4,5},{5,4},{6,7},{7,6},{8,9},{9,8},{10,11... | collective-permute-start | bytes 1572872 | tf_op jit(solution)/shard_map/ppermute | solution.py:693
  83.4 1.2 copy-start.4
  91.2 1.0 copy-start.9
  92.2 7.4 %copy-start.8 = (bf16[2,2,128,1792]{3,2,1,0:T(8,128)(2,1)S(1)}, bf16[2,2,128,1792]{3,2,1,0:T(8,128)(2,1)}, u32[]{:S(2)}) copy-start(bf16[2,2,128,1792]{3,2,1,0:T(8,128)(2,1)} %copy-done.7) | copy-start | bytes 5505028
  92.2 7.4 %copy-start.15 = (bf16[2,2,128,1792]{3,2,1,0:T(8,128)(2,1)S(1)}, bf16[2,2,128,1792]{3,2,1,0:T(8,128)(2,1)}, u32[]{:S(2)}) copy-start(bf16[2,2,128,1792]{3,2,1,0:T(8,128)(2,1)} %copy-done.14) | copy-start | bytes 5505028
  99.5 2.2 %copy-start.6 = (f32[256,2048]{1,0:T(8,128)}, f32[256,2048]{1,0:T(8,128)S(1)}, u32[]{:S(2)}) copy-start(f32[256,2048]{1,0:T(8,128)S(1)} %target_part.2.refs_11_) | copy-start | bytes 6291460
  99.5 3.0 %collective-permute-start.17 = (bf16[64,4096]{1,0:T(8,128)(2,1)S(1)}, bf16[64,4096]{1,0:T(8,128)(2,1)S(1)}, u32[]{:S(2)}, u32[]{:S(2)}) collective-permute-start(bf16[64,4096]{1,0:T(8,128)(2,1)S(1)} %collective-permute-done.15.refs_5_.refs_19_), channel_id=1, source_target_pairs={{0,4},{4,0},{8,12},{12,8},{1,5},{5,1},{9,13},{13,9},{2,6},{6,2},{1... | collective-permute-start | bytes 1572872 | tf_op jit(solution)/shard_map/ppermute | solution.py:687
  102.0 17.5 %collective-permute-start.13 = (bf16[128,1792]{1,0:T(8,128)(2,1)S(1)}, bf16[128,1792]{1,0:T(8,128)(2,1)S(1)}, u32[]{:S(2)}, u32[]{:S(2)}) collective-permute-start(bf16[128,1792]{1,0:T(8,128)(2,1)S(1)} %fusion.3.mine_ref), channel_id=1, source_target_pairs={{0,8},{4,12},{8,0},{12,4},{1,9},{5,13},{9,1},{13,5},{2,10},{6,14},... | collective-permute-start | bytes 1376264 | tf_op jit(solution)/shard_map/ppermute | solution.py:690
  102.3 8.4 %collective-permute-start.14 = (bf16[128,1792]{1,0:T(8,128)(2,1)S(1)}, bf16[128,1792]{1,0:T(8,128)(2,1)S(1)}, u32[]{:S(2)}, u32[]{:S(2)}) collective-permute-start(bf16[128,1792]{1,0:T(8,128)(2,1)S(1)} %fusion.3.mine_ref), channel_id=1, source_target_pairs={{0,4},{4,0},{8,12},{12,8},{1,5},{5,1},{9,13},{13,9},{2,6},{6,2},{1... | collective-permute-start | bytes 1376264 | tf_op jit(solution)/shard_map/ppermute | solution.py:687
  109.7 1.0 copy-start.10
  118.1 1.4 copy-start.3
  119.5 1.8 %collective-permute-start.19 = (bf16[128,1792]{1,0:T(8,128)(2,1)S(1)}, bf16[128,1792]{1,0:T(8,128)(2,1)S(1)}, u32[]{:S(2)}, u32[]{:S(2)}) collective-permute-start(bf16[128,1792]{1,0:T(8,128)(2,1)S(1)} %collective-permute-done.13.refs_0_), channel_id=1, source_target_pairs={{0,4},{4,0},{8,12},{12,8},{1,5},{5,1},{9,13},{13,9},{2,6},{6,2},{1... | collective-permute-start | bytes 1376264 | tf_op jit(solution)/shard_map/ppermute | solution.py:687
  119.8 2.3 %collective-permute-start.20 = (bf16[128,1792]{1,0:T(8,128)(2,1)}, bf16[128,1792]{1,0:T(8,128)(2,1)S(1)}, u32[]{:S(2)}, u32[]{:S(2)}) collective-permute-start(bf16[128,1792]{1,0:T(8,128)(2,1)} %collective-permute-done.18.refs_1_), channel_id=1, source_target_pairs={{0,4},{4,0},{8,12},{12,8},{1,5},{5,1},{9,13},{13,9},{2,6},{6,2},{1... | collective-permute-start | bytes 1376264 | tf_op jit(solution)/shard_map/ppermute | solution.py:687
  142.2 11.7 %collective-permute-start.21 = (bf16[2,768,128]{2,1,0:T(8,128)(2,1)S(1)}, bf16[2,768,128]{2,1,0:T(8,128)(2,1)S(1)}, u32[]{:S(2)}, u32[]{:S(2)}) collective-permute-start(bf16[2,768,128]{2,1,0:T(8,128)(2,1)S(1)} %slice.63), channel_id=1, source_target_pairs={{0,1},{1,0},{2,3},{3,2},{4,5},{5,4},{6,7},{7,6},{8,9},{9,8},{10,11... | collective-permute-start | bytes 1179656 | tf_op jit(solution)/shard_map/ppermute | solution.py:693
  155.0 9.5 %collective-permute-start.24 = (bf16[256,128]{1,0:T(8,128)(2,1)S(1)}, bf16[256,128]{1,0:T(8,128)(2,1)S(1)}, u32[]{:S(2)}, u32[]{:S(2)}) collective-permute-start(bf16[256,128]{1,0:T(8,128)(2,1)S(1)} %slice_bitcast_fusion.6), channel_id=1, source_target_pairs={{0,2},{1,3},{2,0},{3,1},{4,6},{5,7},{6,4},{7,5},{8,10},{9,11},{10,... | collective-permute-start | bytes 196616 | tf_op jit(solution)/shard_map/ppermute | solution.py:693
  157.7 12.4 %collective-permute-start.23 = (bf16[512,128]{1,0:T(8,128)(2,1)S(1)}, bf16[512,128]{1,0:T(8,128)(2,1)S(1)}, u32[]{:S(2)}, u32[]{:S(2)}) collective-permute-start(bf16[512,128]{1,0:T(8,128)(2,1)S(1)} %get-tuple-element.67), channel_id=1, source_target_pairs={{0,8},{1,12},{2,0},{3,4},{4,9},{5,13},{6,1},{7,5},{8,10},{9,14},{1... | collective-permute-start | bytes 393224 | tf_op jit(solution)/shard_map/ppermute | solution.py:700
  158.0 12.1 %collective-permute-start.22 = (bf16[512,128]{1,0:T(8,128)(2,1)S(1)}, bf16[512,128]{1,0:T(8,128)(2,1)S(1)}, u32[]{:S(2)}, u32[]{:S(2)}) collective-permute-start(bf16[512,128]{1,0:T(8,128)(2,1)S(1)} %get-tuple-element.66), channel_id=1, source_target_pairs={{0,0},{1,4},{2,8},{3,12},{4,1},{5,5},{6,9},{7,13},{8,2},{9,6},{10,... | collective-permute-start | bytes 393224 | tf_op jit(solution)/shard_map/ppermute | solution.py:700

commit v9 on v8

--- a/solution.py
+++ b/solution.py
@@ -59,7 +59,7 @@
             out_specs=[out_spec, out_spec],
         ),
         out_shape=[shape, shape],
-        compiler_params=pltpu.CompilerParams(vmem_limit_bytes=50 * 2**20),
+        compiler_params=pltpu.CompilerParams(vmem_limit_bytes=40 * 2**20),
         cost_estimate=pl.CostEstimate(
             flops=2 * 2 * rows * feat * 2 * width,
             bytes_accessed=2 * feat * 2 * width + 2 * 2 * rows * (feat + 2 * width),
@@ -109,7 +109,7 @@
             out_specs=whole,
         ),
         out_shape=jax.ShapeDtypeStruct((2 * rows, outs), F32),
-        compiler_params=pltpu.CompilerParams(vmem_limit_bytes=50 * 2**20),
+        compiler_params=pltpu.CompilerParams(vmem_limit_bytes=40 * 2**20),
         cost_estimate=pl.CostEstimate(
             flops=2 * 2 * rows * width * outs,
             bytes_accessed=2 * width * outs + 2 * 2 * rows * width + 16 * rows * outs,
@@ -357,7 +357,7 @@
             out_specs=[out_spec, out_spec],
         ),
         out_shape=[shape, shape],
-        compiler_params=pltpu.CompilerParams(vmem_limit_bytes=50 * 2**20),
+        compiler_params=pltpu.CompilerParams(vmem_limit_bytes=40 * 2**20),
         cost_estimate=LARGE if sets > 1 else SMALL,
         name="gate_up_products",
     )(scalars, *[piece for piece, _, _ in pieces], gate, up)
@@ -395,7 +395,7 @@
             out_specs=block,
         ),
         out_shape=jax.ShapeDtypeStruct((2 * rows, outs), F32),
-        compiler_params=pltpu.CompilerParams(vmem_limit_bytes=50 * 2**20),
+        compiler_params=pltpu.CompilerParams(vmem_limit_bytes=40 * 2**20),
         cost_estimate=SMALL,
         name="target_part",
     )(jnp.reshape(chip, (1,)).astype(jnp.int32), mine, near, weight, *terms)
@@ -551,7 +551,7 @@
             jax.ShapeDtypeStruct((groups, BLK, 4 * half), BF16),
             jax.ShapeDtypeStruct((4 * half, groups * BLK), F32),
         ],
-        compiler_params=pltpu.CompilerParams(vmem_limit_bytes=50 * 2**20),
+        compiler_params=pltpu.CompilerParams(vmem_limit_bytes=40 * 2**20),
         cost_estimate=LARGE,
         name="student_part",
     )(scalars, *tokens, factors, factors, left_diag, *targets)
@@ -668,7 +668,7 @@
             ],
         ),
         out_shape=jax.ShapeDtypeStruct((parts, out_rows, size), BF16),
-        compiler_params=pltpu.CompilerParams(vmem_limit_bytes=50 * 2**20),
+        compiler_params=pltpu.CompilerParams(vmem_limit_bytes=40 * 2**20),
         cost_estimate=SMALL,
         name="factor_grads",
     )(scalars, *hidden, weight, *rest, *mixed, left_diag, *own, *late)
@@ -708,7 +708,6 @@
     near_tokens = swap(tokens)
     first = cut_tokens(tokens, rows, jnp.int32(0), 1 - chip)
     arrived = across(first)
-    turned = turn(after(right_factor, first), 0)
     base = jnp.stack([odd, 1 - odd])
     mine_block = lax.div(part, BLK) * chip
     other_block = lax.div(part, BLK) * (1 - chip)
@@ -718,16 +717,17 @@
 
     own_pieces = [(t, row, 2) for t in (tokens, near_tokens) for row in (0, 1)]
     mine, other = products(
-        own_pieces, after(scalars(other_block), turned), gate_weight, up_weight, 0, part
+        own_pieces, after(scalars(other_block), first), gate_weight, up_weight, 0, part
     )
 
     pairs, blocks = left_factor.shape[0], left_factor.shape[2]
     left_rows = left_factor.reshape(pairs // 2, 2, -1, blocks).transpose(0, 2, 1, 3)
+    turned = turn(after(right_factor, mine), 0)
+    rest = cut_tokens(after(tokens, mine), rows // 2, odd, chip, LARGE)
     factors = jnp.concatenate(
-        [turned.reshape(-1, LANES), left_rows.reshape(-1, LANES)], axis=0
+        [after(turned, rest).reshape(-1, LANES), left_rows.reshape(-1, LANES)], axis=0
     )[None]
-    more = along(after(factors, mine), 1)
-    rest = cut_tokens(after(tokens, mine), rows // 2, odd, chip, LARGE)
+    more = along(factors, 1)
     sums = add(mine[0], swap(other[0])).astype(BF16)
     arrived = after(arrived, more, rest, sums)
     got_early = across(sums)

time: 173 us -> 167 us (0.965)
  Pallas kernels: 90.1 us -> 85.2 us
  starting transfers between devices: 24.2 us -> 28.5 us
  waiting for transfers between devices: 36.9 us -> 34 us
  local copies, waits for them, and re-layouts: 8.86 us -> 6.19 us
    ppermute x5, starting transfers between devices: 6.82 us -> 13.9 us  [along(): lax.ppermute(value, 'tensor', [(i, i ^ bit) for i in range(tensor_count)])]
    ppermute x6, waiting for transfers between devices: 14.5 us -> 10.2 us  [across(): return lax.ppermute(value, 'fsdp', [(i, i ^ 2) for i in range(fsdp_count)])]
    ppermute x3, waiting for transfers between devices: 4.69 us -> 8.53 us  [turn(): return lax.ppermute(value, both_axes, perm)]
    pallas_call x2, Pallas kernels: 13.8 us -> 10.3 us  [student_part(): pl.pallas_call(functools.partial(student_kernel, steps, late, tensor_coun...]
    ppermute x5, waiting for transfers between devices: 15.5 us -> 13.1 us  [along(): lax.ppermute(value, 'tensor', [(i, i ^ bit) for i in range(tensor_count)])]
    unnamed x36 -> x30, local copies, waits for them, and re-layouts: 6.52 us -> 4.85 us
  transfers between devices with their start and end apart: 25 -> 25, of which waited for: 7 -> 9; matrix products, arithmetic and copies ran while one was open for 6% -> 6% of each run, Pallas kernels for 42% -> 41%
where the time goes in v9:
time: 167 us; the launch traced here: 164 us
  Pallas kernels  85.2 us (51%)
  waiting for transfers between devices  34 us (20%)
  starting transfers between devices  28.5 us (17%)
  other arithmetic  9.43 us (6%)
  local copies, waits for them, and re-layouts  6.19 us (4%)
    pallas_call x3, Pallas kernels, products(): pl.pallas_call(functools.partial(products_kernel, sets), grid_spec=pltpu....  33.5 us
    pallas_call x1, Pallas kernels, factor_grads(): pl.pallas_call(functools.partial(grads_kernel, groups, steps, scale), gri...  18 us
    pallas_call x2, Pallas kernels, target_part(): pl.pallas_call(functools.partial(target_kernel, sign), grid_spec=pltpu.Pr...  14.7 us
    ppermute x5, starting transfers between devices, along(): lax.ppermute(value, 'tensor', [(i, i ^ bit) for i in range(tensor_count)])  13.9 us
    ppermute x5, waiting for transfers between devices, along(): lax.ppermute(value, 'tensor', [(i, i ^ bit) for i in range(tensor_count)])  13.1 us
    ppermute x6, starting transfers between devices, across(): return lax.ppermute(value, 'fsdp', [(i, i ^ 2) for i in range(fsdp_count)])  10.4 us
    pallas_call x2, Pallas kernels, student_part(): pl.pallas_call(functools.partial(student_kernel, steps, late, tensor_coun...  10.3 us
    ppermute x6, waiting for transfers between devices, across(): return lax.ppermute(value, 'fsdp', [(i, i ^ 2) for i in range(fsdp_count)])  10.2 us
  transfers between devices with their start and end apart: 25, of which 9 were waited for; matrix products, arithmetic and copies ran while one was open for 6% of the time, Pallas kernels for 41%

profile of v9, /device:TPU:0, one launch (start us, length us, event | category | flops | bytes accessed | tf_op | source)
XLA Modules:
  0.0 164.2 jit_solution(89384150713048524)
XLA Ops:
  0.6 0.5 collective-permute-start
  1.2 0.6 pad_add_fusion.1.idx_ref
  1.7 3.1 %cut_tokens.2 = bf16[128,4096]{1,0:T(8,128)(2,1)} custom-call(s32[2]{0:T(128)} %pad_add_fusion.1.idx_ref, bf16[128,8192]{1,0:T(8,128)(2,1)} %refs_11_.1), custom_call_target="tpu_custom_call" | custom-call | flops 1 | bytes 1 | tf_op jit(solution)/shard_map/cut_tokens/pallas_call | solution.py:311
  4.8 2.5 %collective-permute-start.2 = (bf16[128,4096]{1,0:T(8,128)(2,1)}, bf16[128,4096]{1,0:T(8,128)(2,1)S(1)}, u32[]{:S(2)}, u32[]{:S(2)}) collective-permute-start(bf16[128,4096]{1,0:T(8,128)(2,1)} %cut_tokens.2), channel_id=1, source_target_pairs={{0,8},{4,12},{8,0},{12,4},{1,9},{5,13},{9,1},{13,5},{2,10},{6,14},... | collective-permute-start | bytes 3145736 | tf_op jit(solution)/shard_map/ppermute | solution.py:690
  7.3 0.1 concatenate.26.idx_ref
  7.4 0.1 copy.11
  7.5 0.1 reshape.38
  7.6 0.6 pad_add_fusion.2.idx_ref
  8.3 10.8 %gate_up_products.3 = (bf16[1,2,128,1792]{3,2,1,0:T(8,128)(2,1)S(1)}, bf16[1,2,128,1792]{3,2,1,0:T(8,128)(2,1)}) custom-call(s32[5]{0:T(128)S(1)} %concatenate.26.idx_ref, bf16[128,8192]{1,0:T(8,128)(2,1)S(1)} %copy-done, bf16[128,8192]{1,0:T(8,128)(2,1)S(1)} %copy-done, bf16[128,8192]{1,0:T(8,128)(2,1)} %collective-permute-done.refs_2_.refs_3_.refs_12_.refs_13_, ...), custom_call_target="tpu_custom_call" | custom-call | flops 1 | bytes 1 | tf_op jit(solution)/shard_map/gate_up_products/pallas_call | solution.py:350
  19.1 1.0 copy-done.8
  20.0 0.2 collective-permute-start.1
  20.2 0.8 collective-permute-start.3
  21.0 2.5 %cut_tokens.3 = bf16[64,4096]{1,0:T(8,128)(2,1)} custom-call(s32[2]{0:T(128)} %pad_add_fusion.2.idx_ref, bf16[128,8192]{1,0:T(8,128)(2,1)} %refs_11_.1), custom_call_target="tpu_custom_call" | custom-call | flops 10000000000 | bytes 10000000 | tf_op jit(solution)/shard_map/cut_tokens/pallas_call | solution.py:311
  23.6 4.7 %collective-permute-start.4 = (bf16[1,768,128]{2,1,0:T(8,128)(2,1)S(1)}, bf16[1,768,128]{2,1,0:T(8,128)(2,1)S(1)}, u32[]{:S(2)}, u32[]{:S(2)}) collective-permute-start(bf16[1,768,128]{2,1,0:T(8,128)(2,1)S(1)} %maximum_bitcast_fusion), channel_id=1, source_target_pairs={{0,1},{1,0},{2,3},{3,2},{4,5},{5,4},{6,7},{7,6},{8,9},{9,8},{10,11... | collective-permute-start | bytes 589832 | tf_op jit(solution)/shard_map/ppermute | solution.py:693
  28.3 1.2 fusion.1
  29.5 4.0 %collective-permute-done.2.refs_0_.refs_1_.refs_4_.refs_5_.refs_14_.refs_15_ = bf16[128,4096]{1,0:T(8,128)(2,1)S(1)} collective-permute-done((bf16[128,4096]{1,0:T(8,128)(2,1)}, bf16[128,4096]{1,0:T(8,128)(2,1)S(1)}, u32[]{:S(2)}, u32[]{:S(2)}) %collective-permute-start.2) | collective-permute-done | bytes 1048608 | tf_op jit(solution)/shard_map/ppermute | solution.py:690
  33.5 1.6 collective-permute-done.4
  35.1 0.1 collective-permute-start.5
  35.2 0.1 concatenate.25.idx_ref
  35.3 4.0 %collective-permute-start.6 = (bf16[2,128,1792]{2,1,0:T(8,128)(2,1)}, bf16[2,128,1792]{2,1,0:T(8,128)(2,1)S(1)}, u32[]{:S(2)}, u32[]{:S(2)}) collective-permute-start(bf16[2,128,1792]{2,1,0:T(8,128)(2,1)} %fusion.1), channel_id=1, source_target_pairs={{0,8},{4,12},{8,0},{12,4},{1,9},{5,13},{9,1},{13,5},{2,10},{6,14},... | collective-permute-start | bytes 2752520 | tf_op jit(solution)/shard_map/ppermute | solution.py:690
  39.4 3.3 %collective-permute-start.8 = (bf16[2,768,128]{2,1,0:T(8,128)(2,1)S(1)}, bf16[2,768,128]{2,1,0:T(8,128)(2,1)S(1)}, u32[]{:S(2)}, u32[]{:S(2)}) collective-permute-start(bf16[2,768,128]{2,1,0:T(8,128)(2,1)S(1)} %pad_maximum_fusion.1), channel_id=1, source_target_pairs={{0,2},{1,3},{2,0},{3,1},{4,6},{5,7},{6,4},{7,5},{8,10},{9,11},{10,... | collective-permute-start | bytes 1179656 | tf_op jit(solution)/shard_map/ppermute | solution.py:693
  42.7 10.1 %gate_up_products.4 = (bf16[1,2,128,1792]{3,2,1,0:T(8,128)(2,1)S(1)}, bf16[1,2,128,1792]{3,2,1,0:T(8,128)(2,1)S(1)}) custom-call(s32[5]{0:T(128)S(1)} %concatenate.26.idx_ref, bf16[128,4096]{1,0:T(8,128)(2,1)S(1)} %collective-permute-done.2.refs_0_.refs_1_.refs_4_.refs_5_.refs_14_.refs_15_, ...), custom_call_target="tpu_custom_call" | custom-call | flops 1 | bytes 1 | tf_op jit(solution)/shard_map/gate_up_products/pallas_call | solution.py:350
  52.9 12.6 %gate_up_products.5 = (bf16[2,2,128,1792]{3,2,1,0:T(8,128)(2,1)S(1)}, bf16[2,2,128,1792]{3,2,1,0:T(8,128)(2,1)S(1)}) custom-call(s32[5]{0:T(128)S(1)} %concatenate.25.idx_ref, bf16[128,8192]{1,0:T(8,128)(2,1)S(1)} %copy-done.1, bf16[128,8192]{1,0:T(8,128)(2,1)S(1)} %copy-done.1, bf16[128,8192]{1,0:T(8,128)(2,1)} %collective-permute-done.refs_2_.refs_3_.refs_12_.refs_13_, ...), custom_call_target="tpu_custom_call" | custom-call | flops 10000000000 | bytes 10000000 | tf_op jit(solution)/shard_map/gate_up_products/pallas_call | solution.py:350
  65.6 1.4 fusion
  67.0 4.9 %collective-permute-done.7.refs_4_.refs_18_ = bf16[64,4096]{1,0:T(8,128)(2,1)} collective-permute-done((bf16[64,4096]{1,0:T(8,128)(2,1)}, bf16[64,4096]{1,0:T(8,128)(2,1)}, u32[]{:S(2)}, u32[]{:S(2)}) %collective-permute-start.7) | collective-permute-done | bytes 524320 | tf_op jit(solution)/shard_map/ppermute | solution.py:690
  71.9 0.6 pad_add_fusion.idx_ref
  72.5 0.5 collective-permute-start.16
  73.0 1.0 pad_maximum_fusion.rows_ref.refs_4_.refs_5_.refs_8_.refs_9_
  74.0 1.8 %collective-permute-start.11 = (bf16[2,128,1792]{2,1,0:T(8,128)(2,1)}, bf16[2,128,1792]{2,1,0:T(8,128)(2,1)}, u32[]{:S(2)}, u32[]{:S(2)}) collective-permute-start(bf16[2,128,1792]{2,1,0:T(8,128)(2,1)} %fusion), channel_id=1, source_target_pairs={{0,8},{4,12},{8,0},{12,4},{1,9},{5,13},{9,1},{13,5},{2,10},{6,14},... | collective-permute-start | bytes 2752520 | tf_op jit(solution)/shard_map/ppermute | solution.py:690
  75.7 0.3 bitcast_add_fusion
  76.0 1.0 copy-done.11
  77.0 1.1 fusion.5.mine_ref
  78.1 0.1 collective-permute-start.12
  78.1 1.8 %collective-permute-start.18 = (bf16[128,1792]{1,0:T(8,128)(2,1)}, bf16[128,1792]{1,0:T(8,128)(2,1)}, u32[]{:S(2)}, u32[]{:S(2)}) collective-permute-start(bf16[128,1792]{1,0:T(8,128)(2,1)} %fusion.5.mine_ref), channel_id=1, source_target_pairs={{0,8},{4,12},{8,0},{12,4},{1,9},{5,13},{9,1},{13,5},{2,10},{6,14},... | collective-permute-start | bytes 1376264 | tf_op jit(solution)/shard_map/ppermute | solution.py:690
  79.9 1.4 collective-permute-start.15
  81.3 3.0 %spread_left.1.refs_6_.refs_10_.refs_9_ = bf16[8,256,256]{2,1,0:T(8,128)(2,1)} custom-call(s32[4]{0:T(128)} %pad_add_fusion.idx_ref, bf16[4,768,128]{2,1,0:T(8,128)(2,1)} %pad_maximum_fusion.rows_ref.refs_4_.refs_5_.refs_8_.refs_9_), custom_call_target="tpu_custom_call" | custom-call | flops 1 | bytes 1 | tf_op jit(solution)/shard_map/spread_left/pallas_call | solution.py:440
  84.3 1.2 copy-done.2
  85.5 1.1 copy-done.4
  86.7 5.1 %student_part.2 = (bf16[8,256,256]{2,1,0:T(8,128)(2,1)S(1)}, f32[256,2048]{1,0:T(8,128)S(1)}) custom-call(s32[4]{0:T(128)S(1)} %copy-done.10, bf16[128,8192]{1,0:T(8,128)(2,1)S(1)} %copy-done.1, bf16[128,8192]{1,0:T(8,128)(2,1)S(1)} %copy-done.1, bf16[128,8192]{1,0:T(8,128)(2,1)} %collective-permute-done.refs_2_.refs_3_.refs_12_.refs_13_, ...), custom_call_target="tpu_custom_call" | custom-call | flops 10000000000 | bytes 10000000 | tf_op jit(solution)/shard_map/student_part/pallas_call | solution.py:536
  91.8 7.6 %target_part.2.refs_11_ = f32[256,2048]{1,0:T(8,128)S(1)} custom-call(s32[1]{0:T(128)} %bitcast.2.idx_ref, bf16[128,1792]{1,0:T(8,128)(2,1)} %fusion.5.mine_ref, bf16[128,1792]{1,0:T(8,128)(2,1)} %collective-permute-done.12.near_ref, bf16[3584,2048]{1,0:T(8,128)(2,1)} %refs_4_.5), custom_call_target="tpu_custom_call" | custom-call | flops 1 | bytes 1 | tf_op jit(solution)/shard_map/target_part/pallas_call | solution.py:387
  99.4 1.5 bitcast_add_fusion.1
  101.0 0.3 fusion.3.mine_ref
  101.3 0.3 collective-permute-start.13
  101.6 0.3 collective-permute-start.14
  101.9 0.3 copy-done.3
  102.2 0.2 copy-done.5
  102.4 5.3 %student_part.3 = (bf16[8,256,256]{2,1,0:T(8,128)(2,1)S(1)}, f32[256,2048]{1,0:T(8,128)S(1)}) custom-call(s32[4]{0:T(128)S(1)} %copy-done.10, bf16[128,4096]{1,0:T(8,128)(2,1)S(1)} %collective-permute-done.2.refs_0_.refs_1_.refs_4_.refs_5_.refs_14_.refs_15_, bf16[128,4096]{1,0:T(8,128)(2,1)S(1)} %collective-permute-done.2.refs_0_.refs_1_.refs_4_.refs_5_.refs_14_.refs_15_, ...), custom_call_target="tpu_custom_call" | custom-call | flops 10000000000 | bytes 10000000 | tf_op jit(solution)/shard_map/student_part/pallas_call | solution.py:536
  107.7 7.2 %target_part.3.refs_5_ = f32[256,2048]{1,0:T(8,128)S(1)} custom-call(s32[1]{0:T(128)} %bitcast.2.idx_ref, bf16[128,1792]{1,0:T(8,128)(2,1)S(1)} %fusion.3.mine_ref, bf16[128,1792]{1,0:T(8,128)(2,1)S(1)} %collective-permute-done.14.near_ref, bf16[3584,2048]{1,0:T(8,128)(2,1)} %refs_4_.5, f32[256,2048]{1,0:T(8,128)S(1)} %get-tuple-element.62.refs_0_), custom_call_target="tpu_custom_call" | custom-call | flops 1 | bytes 1 | tf_op jit(solution)/shard_map/target_part/pallas_call | solution.py:387
  114.9 1.2 collective-permute-done.13.refs_0_
  116.1 0.5 collective-permute-start.20
  116.6 1.9 %collective-permute-done.19.refs_2_ = bf16[128,1792]{1,0:T(8,128)(2,1)S(1)} collective-permute-done((bf16[128,1792]{1,0:T(8,128)(2,1)S(1)}, bf16[128,1792]{1,0:T(8,128)(2,1)S(1)}, u32[]{:S(2)}, u32[]{:S(2)}) %collective-permute-start.19) | collective-permute-done | bytes 458784 | tf_op jit(solution)/shard_map/ppermute | solution.py:687
  118.6 0.2 collective-permute-done.20.refs_3_
  118.8 18.0 %factor_grads.1 = bf16[4,768,128]{2,1,0:T(8,128)(2,1)S(1)} custom-call(s32[4]{0:T(128)S(1)} %copy-done.10, bf16[128,1792]{1,0:T(8,128)(2,1)S(1)} %collective-permute-done.13.refs_0_, bf16[128,1792]{1,0:T(8,128)(2,1)} %collective-permute-done.18.refs_1_, bf16[128,1792]{1,0:T(8,128)(2,1)S(1)} %collective-permute-done.19.refs_2_, ...), custom_call_target="tpu_custom_call" | custom-call | flops 1 | bytes 1 | tf_op jit(solution)/shard_map/factor_grads/pallas_call | solution.py:648
  136.8 1.4 collective-permute-start.21
  138.3 9.8 %collective-permute-done.21 = bf16[2,768,128]{2,1,0:T(8,128)(2,1)S(1)} collective-permute-done((bf16[2,768,128]{2,1,0:T(8,128)(2,1)S(1)}, bf16[2,768,128]{2,1,0:T(8,128)(2,1)S(1)}, u32[]{:S(2)}, u32[]{:S(2)}) %collective-permute-start.21) | collective-permute-done | bytes 393248 | tf_op jit(solution)/shard_map/ppermute | solution.py:693
  148.0 0.1 add_convert_fusion
  148.2 3.1 %collective-permute-start.24 = (bf16[256,128]{1,0:T(8,128)(2,1)S(1)}, bf16[256,128]{1,0:T(8,128)(2,1)S(1)}, u32[]{:S(2)}, u32[]{:S(2)}) collective-permute-start(bf16[256,128]{1,0:T(8,128)(2,1)S(1)} %slice_bitcast_fusion.6), channel_id=1, source_target_pairs={{0,2},{1,3},{2,0},{3,1},{4,6},{5,7},{6,4},{7,5},{8,10},{9,11},{10,... | collective-permute-start | bytes 196616 | tf_op jit(solution)/shard_map/ppermute | solution.py:693
  151.3 0.3 collective-permute-start.23
  151.6 0.7 collective-permute-start.22
  152.3 1.7 %collective-permute-done.24 = bf16[256,128]{1,0:T(8,128)(2,1)S(1)} collective-permute-done((bf16[256,128]{1,0:T(8,128)(2,1)S(1)}, bf16[256,128]{1,0:T(8,128)(2,1)S(1)}, u32[]{:S(2)}, u32[]{:S(2)}) %collective-permute-start.24) | collective-permute-done | bytes 65568 | tf_op jit(solution)/shard_map/ppermute | solution.py:693
  154.0 0.2 reshape.40
  154.2 0.7 copy.9
  155.0 8.5 %collective-permute-done.23 = bf16[512,128]{1,0:T(8,128)(2,1)S(1)} collective-permute-done((bf16[512,128]{1,0:T(8,128)(2,1)S(1)}, bf16[512,128]{1,0:T(8,128)(2,1)S(1)}, u32[]{:S(2)}, u32[]{:S(2)}) %collective-permute-start.23) | collective-permute-done | bytes 131104 | tf_op jit(solution)/shard_map/ppermute | solution.py:700
  163.5 0.7 convert_add_fusion.2
  (51 shorter events, 0.4 us)
Async XLA Ops:
  0.6 6.8 %copy-start.13 = (bf16[32,16,64]{2,1,0:T(8,128)(2,1)S(1)}, bf16[32,16,64]{2,1,0:T(8,128)(2,1)}, u32[]{:S(2)}) copy-start(bf16[32,16,64]{2,1,0:T(8,128)(2,1)} %param.11) | copy-start | bytes 196612
  0.6 7.7 %collective-permute-start = (bf16[128,8192]{1,0:T(8,128)(2,1)}, bf16[128,8192]{1,0:T(8,128)(2,1)}, u32[]{:S(2)}, u32[]{:S(2)}) collective-permute-start(bf16[128,8192]{1,0:T(8,128)(2,1)} %refs_11_.1), channel_id=1, source_target_pairs={{0,4},{4,0},{8,12},{12,8},{1,5},{5,1},{9,13},{13,9},{2,6},{6,2},{1... | collective-permute-start | bytes 6291464 | tf_op jit(solution)/shard_map/ppermute | solution.py:687
  1.2 7.1 %copy-start = (bf16[128,8192]{1,0:T(8,128)(2,1)S(1)}, bf16[128,8192]{1,0:T(8,128)(2,1)}, u32[]{:S(2)}) copy-start(bf16[128,8192]{1,0:T(8,128)(2,1)} %refs_11_.1) | copy-start | bytes 6291460
  4.8 28.7 %collective-permute-start.2 = (bf16[128,4096]{1,0:T(8,128)(2,1)}, bf16[128,4096]{1,0:T(8,128)(2,1)S(1)}, u32[]{:S(2)}, u32[]{:S(2)}) collective-permute-start(bf16[128,4096]{1,0:T(8,128)(2,1)} %cut_tokens.2), channel_id=1, source_target_pairs={{0,8},{4,12},{8,0},{12,4},{1,9},{5,13},{9,1},{13,5},{2,10},{6,14},... | collective-permute-start | bytes 3145736 | tf_op jit(solution)/shard_map/ppermute | solution.py:690
  8.3 11.9 %copy-start.14 = (bf16[16,32,128]{2,1,0:T(8,128)(2,1)S(1)}, bf16[16,32,128]{2,1,0:T(8,128)(2,1)}, u32[]{:S(2)}) copy-start(bf16[16,32,128]{2,1,0:T(8,128)(2,1)} %param.10) | copy-start | bytes 393220
  19.1 1.0 copy-start.8
  20.0 8.3 %collective-permute-start.1 = (bf16[2,128,1792]{2,1,0:T(8,128)(2,1)}, bf16[2,128,1792]{2,1,0:T(8,128)(2,1)S(1)}, u32[]{:S(2)}, u32[]{:S(2)}) collective-permute-start(bf16[2,128,1792]{2,1,0:T(8,128)(2,1)} %bitcast.10), channel_id=1, source_target_pairs={{0,4},{4,0},{8,12},{12,8},{1,5},{5,1},{9,13},{13,9},{2,6},{6,2},{1... | collective-permute-start | bytes 2752520 | tf_op jit(solution)/shard_map/ppermute | solution.py:687
  20.2 8.1 %copy-start.9 = (bf16[1,2,128,1792]{3,2,1,0:T(8,128)(2,1)S(1)}, bf16[1,2,128,1792]{3,2,1,0:T(8,128)(2,1)}, u32[]{:S(2)}) copy-start(bf16[1,2,128,1792]{3,2,1,0:T(8,128)(2,1)} %copy-done.8) | copy-start | bytes 2752516
  20.2 3.3 %collective-permute-start.3 = (bf16[16,32,128]{2,1,0:T(8,128)(2,1)S(1)}, bf16[16,32,128]{2,1,0:T(8,128)(2,1)S(1)}, u32[]{:S(2)}, u32[]{:S(2)}) collective-permute-start(bf16[16,32,128]{2,1,0:T(8,128)(2,1)S(1)} %copy-done.14), channel_id=1, source_target_pairs={{0,0},{1,4},{2,8},{3,12},{4,1},{5,5},{6,9},{7,13},{8,2},{9,6},{10,... | collective-permute-start | bytes 393224 | tf_op jit(solution)/shard_map/ppermute | solution.py:700
  23.6 11.5 %collective-permute-start.4 = (bf16[1,768,128]{2,1,0:T(8,128)(2,1)S(1)}, bf16[1,768,128]{2,1,0:T(8,128)(2,1)S(1)}, u32[]{:S(2)}, u32[]{:S(2)}) collective-permute-start(bf16[1,768,128]{2,1,0:T(8,128)(2,1)S(1)} %maximum_bitcast_fusion), channel_id=1, source_target_pairs={{0,1},{1,0},{2,3},{3,2},{4,5},{5,4},{6,7},{7,6},{8,9},{9,8},{10,11... | collective-permute-start | bytes 589832 | tf_op jit(solution)/shard_map/ppermute | solution.py:693
  35.1 7.6 %collective-permute-start.5 = (bf16[128,4096]{1,0:T(8,128)(2,1)S(1)}, bf16[128,4096]{1,0:T(8,128)(2,1)}, u32[]{:S(2)}, u32[]{:S(2)}) collective-permute-start(bf16[128,4096]{1,0:T(8,128)(2,1)S(1)} %collective-permute-done.2.refs_0_.refs_1_.refs_4_.refs_5_.refs_14_.refs_15_), channel_id=1, source_target_pairs={{0,4},{4,0},{8,12},{12,8},{1,5},{5,1},{9,13},{13,9},{2,6},{6,2},{1... | collective-permute-start | bytes 3145736 | tf_op jit(solution)/shard_map/ppermute | solution.py:687
  35.3 17.6 %copy-start.1 = (bf16[128,8192]{1,0:T(8,128)(2,1)S(1)}, bf16[128,8192]{1,0:T(8,128)(2,1)}, u32[]{:S(2)}) copy-start(bf16[128,8192]{1,0:T(8,128)(2,1)} %refs_11_.1) | copy-start | bytes 6291460
  35.3 36.6 %collective-permute-start.6 = (bf16[2,128,1792]{2,1,0:T(8,128)(2,1)}, bf16[2,128,1792]{2,1,0:T(8,128)(2,1)S(1)}, u32[]{:S(2)}, u32[]{:S(2)}) collective-permute-start(bf16[2,128,1792]{2,1,0:T(8,128)(2,1)} %fusion.1), channel_id=1, source_target_pairs={{0,8},{4,12},{8,0},{12,4},{1,9},{5,13},{9,1},{13,5},{2,10},{6,14},... | collective-permute-start | bytes 2752520 | tf_op jit(solution)/shard_map/ppermute | solution.py:690
  39.3 32.6 %collective-permute-start.7 = (bf16[64,4096]{1,0:T(8,128)(2,1)}, bf16[64,4096]{1,0:T(8,128)(2,1)}, u32[]{:S(2)}, u32[]{:S(2)}) collective-permute-start(bf16[64,4096]{1,0:T(8,128)(2,1)} %cut_tokens.3), channel_id=1, source_target_pairs={{0,8},{4,12},{8,0},{12,4},{1,9},{5,13},{9,1},{13,5},{2,10},{6,14},... | collective-permute-start | bytes 1572872 | tf_op jit(solution)/shard_map/ppermute | solution.py:690
  39.4 27.6 %collective-permute-start.8 = (bf16[2,768,128]{2,1,0:T(8,128)(2,1)S(1)}, bf16[2,768,128]{2,1,0:T(8,128)(2,1)S(1)}, u32[]{:S(2)}, u32[]{:S(2)}) collective-permute-start(bf16[2,768,128]{2,1,0:T(8,128)(2,1)S(1)} %pad_maximum_fusion.1), channel_id=1, source_target_pairs={{0,2},{1,3},{2,0},{3,1},{4,6},{5,7},{6,4},{7,5},{8,10},{9,11},{10,... | collective-permute-start | bytes 1179656 | tf_op jit(solution)/shard_map/ppermute | solution.py:693
  52.8 12.7 %collective-permute-start.9 = (bf16[2,128,1792]{2,1,0:T(8,128)(2,1)S(1)}, bf16[2,128,1792]{2,1,0:T(8,128)(2,1)S(1)}, u32[]{:S(2)}, u32[]{:S(2)}) collective-permute-start(bf16[2,128,1792]{2,1,0:T(8,128)(2,1)S(1)} %bitcast.62), channel_id=1, source_target_pairs={{0,4},{4,0},{8,12},{12,8},{1,5},{5,1},{9,13},{13,9},{2,6},{6,2},{1... | collective-permute-start | bytes 2752520 | tf_op jit(solution)/shard_map/ppermute | solution.py:687
  65.5 10.2 %copy-start.6 = (bf16[2,2,128,1792]{3,2,1,0:T(8,128)(2,1)}, bf16[2,2,128,1792]{3,2,1,0:T(8,128)(2,1)S(1)}, u32[]{:S(2)}) copy-start(bf16[2,2,128,1792]{3,2,1,0:T(8,128)(2,1)S(1)} %get-tuple-element.44) | copy-start | bytes 5505028
  71.9 3.8 %collective-permute-start.10 = (bf16[2,2,128,1792]{3,2,1,0:T(8,128)(2,1)S(1)}, bf16[2,2,128,1792]{3,2,1,0:T(8,128)(2,1)S(1)}, u32[]{:S(2)}, u32[]{:S(2)}) collective-permute-start(bf16[2,2,128,1792]{3,2,1,0:T(8,128)(2,1)S(1)} %get-tuple-element.50), channel_id=1, source_target_pairs={{0,4},{4,0},{8,12},{12,8},{1,5},{5,1},{9,13},{13,9},{2,6},{6,2},{1... | collective-permute-start | bytes 5505032 | tf_op jit(solution)/shard_map/ppermute | solution.py:687
  72.5 29.4 %collective-permute-start.16 = (bf16[64,4096]{1,0:T(8,128)(2,1)}, bf16[64,4096]{1,0:T(8,128)(2,1)}, u32[]{:S(2)}, u32[]{:S(2)}) collective-permute-start(bf16[64,4096]{1,0:T(8,128)(2,1)} %collective-permute-done.7.refs_4_.refs_18_), channel_id=1, source_target_pairs={{0,4},{4,0},{8,12},{12,8},{1,5},{5,1},{9,13},{13,9},{2,6},{6,2},{1... | collective-permute-start | bytes 1572872 | tf_op jit(solution)/shard_map/ppermute | solution.py:687
  74.0 25.3 %collective-permute-start.11 = (bf16[2,128,1792]{2,1,0:T(8,128)(2,1)}, bf16[2,128,1792]{2,1,0:T(8,128)(2,1)}, u32[]{:S(2)}, u32[]{:S(2)}) collective-permute-start(bf16[2,128,1792]{2,1,0:T(8,128)(2,1)} %fusion), channel_id=1, source_target_pairs={{0,8},{4,12},{8,0},{12,4},{1,9},{5,13},{9,1},{13,5},{2,10},{6,14},... | collective-permute-start | bytes 2752520 | tf_op jit(solution)/shard_map/ppermute | solution.py:690
  75.7 1.3 copy-start.11
  77.0 7.3 %copy-start.10 = (s32[4]{0:T(128)S(1)}, s32[4]{0:T(128)}, u32[]{:S(2)}) copy-start(s32[4]{0:T(128)} %pad_add_fusion.idx_ref) | copy-start | bytes 52
  78.1 13.7 %collective-permute-start.12 = (bf16[128,1792]{1,0:T(8,128)(2,1)}, bf16[128,1792]{1,0:T(8,128)(2,1)}, u32[]{:S(2)}, u32[]{:S(2)}) collective-permute-start(bf16[128,1792]{1,0:T(8,128)(2,1)} %fusion.5.mine_ref), channel_id=1, source_target_pairs={{0,4},{4,0},{8,12},{12,8},{1,5},{5,1},{9,13},{13,9},{2,6},{6,2},{1... | collective-permute-start | bytes 1376264 | tf_op jit(solution)/shard_map/ppermute | solution.py:687
  78.1 38.0 %collective-permute-start.18 = (bf16[128,1792]{1,0:T(8,128)(2,1)}, bf16[128,1792]{1,0:T(8,128)(2,1)}, u32[]{:S(2)}, u32[]{:S(2)}) collective-permute-start(bf16[128,1792]{1,0:T(8,128)(2,1)} %fusion.5.mine_ref), channel_id=1, source_target_pairs={{0,8},{4,12},{8,0},{12,4},{1,9},{5,13},{9,1},{13,5},{2,10},{6,14},... | collective-permute-start | bytes 1376264 | tf_op jit(solution)/shard_map/ppermute | solution.py:690
  79.9 19.4 %collective-permute-start.15 = (bf16[64,4096]{1,0:T(8,128)(2,1)}, bf16[64,4096]{1,0:T(8,128)(2,1)}, u32[]{:S(2)}, u32[]{:S(2)}) collective-permute-start(bf16[64,4096]{1,0:T(8,128)(2,1)} %collective-permute-done.7.refs_4_.refs_18_), channel_id=1, source_target_pairs={{0,1},{1,0},{2,3},{3,2},{4,5},{5,4},{6,7},{7,6},{8,9},{9,8},{10,11... | collective-permute-start | bytes 1572872 | tf_op jit(solution)/shard_map/ppermute | solution.py:693
  84.3 1.2 copy-start.2
  85.5 1.1 copy-start.4
  91.7 7.7 %copy-start.7 = (bf16[2,2,128,1792]{3,2,1,0:T(8,128)(2,1)S(1)}, bf16[2,2,128,1792]{3,2,1,0:T(8,128)(2,1)}, u32[]{:S(2)}) copy-start(bf16[2,2,128,1792]{3,2,1,0:T(8,128)(2,1)} %copy-done.6) | copy-start | bytes 5505028
  91.7 7.7 %copy-start.12 = (bf16[2,2,128,1792]{3,2,1,0:T(8,128)(2,1)S(1)}, bf16[2,2,128,1792]{3,2,1,0:T(8,128)(2,1)}, u32[]{:S(2)}) copy-start(bf16[2,2,128,1792]{3,2,1,0:T(8,128)(2,1)} %copy-done.11) | copy-start | bytes 5505028
  99.3 2.5 %collective-permute-start.17 = (bf16[64,4096]{1,0:T(8,128)(2,1)}, bf16[64,4096]{1,0:T(8,128)(2,1)S(1)}, u32[]{:S(2)}, u32[]{:S(2)}) collective-permute-start(bf16[64,4096]{1,0:T(8,128)(2,1)} %collective-permute-done.15.refs_5_.refs_19_), channel_id=1, source_target_pairs={{0,4},{4,0},{8,12},{12,8},{1,5},{5,1},{9,13},{13,9},{2,6},{6,2},{1... | collective-permute-start | bytes 1572872 | tf_op jit(solution)/shard_map/ppermute | solution.py:687
  101.0 1.2 copy-start.3
  101.0 1.4 copy-start.5
  101.3 14.9 %collective-permute-start.13 = (bf16[128,1792]{1,0:T(8,128)(2,1)S(1)}, bf16[128,1792]{1,0:T(8,128)(2,1)S(1)}, u32[]{:S(2)}, u32[]{:S(2)}) collective-permute-start(bf16[128,1792]{1,0:T(8,128)(2,1)S(1)} %fusion.3.mine_ref), channel_id=1, source_target_pairs={{0,8},{4,12},{8,0},{12,4},{1,9},{5,13},{9,1},{13,5},{2,10},{6,14},... | collective-permute-start | bytes 1376264 | tf_op jit(solution)/shard_map/ppermute | solution.py:690
  101.6 6.1 %collective-permute-start.14 = (bf16[128,1792]{1,0:T(8,128)(2,1)S(1)}, bf16[128,1792]{1,0:T(8,128)(2,1)S(1)}, u32[]{:S(2)}, u32[]{:S(2)}) collective-permute-start(bf16[128,1792]{1,0:T(8,128)(2,1)S(1)} %fusion.3.mine_ref), channel_id=1, source_target_pairs={{0,4},{4,0},{8,12},{12,8},{1,5},{5,1},{9,13},{13,9},{2,6},{6,2},{1... | collective-permute-start | bytes 1376264 | tf_op jit(solution)/shard_map/ppermute | solution.py:687
  116.1 2.4 %collective-permute-start.19 = (bf16[128,1792]{1,0:T(8,128)(2,1)S(1)}, bf16[128,1792]{1,0:T(8,128)(2,1)S(1)}, u32[]{:S(2)}, u32[]{:S(2)}) collective-permute-start(bf16[128,1792]{1,0:T(8,128)(2,1)S(1)} %collective-permute-done.13.refs_0_), channel_id=1, source_target_pairs={{0,4},{4,0},{8,12},{12,8},{1,5},{5,1},{9,13},{13,9},{2,6},{6,2},{1... | collective-permute-start | bytes 1376264 | tf_op jit(solution)/shard_map/ppermute | solution.py:687
  116.1 2.7 %collective-permute-start.20 = (bf16[128,1792]{1,0:T(8,128)(2,1)}, bf16[128,1792]{1,0:T(8,128)(2,1)S(1)}, u32[]{:S(2)}, u32[]{:S(2)}) collective-permute-start(bf16[128,1792]{1,0:T(8,128)(2,1)} %collective-permute-done.18.refs_1_), channel_id=1, source_target_pairs={{0,4},{4,0},{8,12},{12,8},{1,5},{5,1},{9,13},{13,9},{2,6},{6,2},{1... | collective-permute-start | bytes 1376264 | tf_op jit(solution)/shard_map/ppermute | solution.py:687
  136.8 11.2 %collective-permute-start.21 = (bf16[2,768,128]{2,1,0:T(8,128)(2,1)S(1)}, bf16[2,768,128]{2,1,0:T(8,128)(2,1)S(1)}, u32[]{:S(2)}, u32[]{:S(2)}) collective-permute-start(bf16[2,768,128]{2,1,0:T(8,128)(2,1)S(1)} %slice.63), channel_id=1, source_target_pairs={{0,1},{1,0},{2,3},{3,2},{4,5},{5,4},{6,7},{7,6},{8,9},{9,8},{10,11... | collective-permute-start | bytes 1179656 | tf_op jit(solution)/shard_map/ppermute | solution.py:693
  148.2 5.9 %collective-permute-start.24 = (bf16[256,128]{1,0:T(8,128)(2,1)S(1)}, bf16[256,128]{1,0:T(8,128)(2,1)S(1)}, u32[]{:S(2)}, u32[]{:S(2)}) collective-permute-start(bf16[256,128]{1,0:T(8,128)(2,1)S(1)} %slice_bitcast_fusion.6), channel_id=1, source_target_pairs={{0,2},{1,3},{2,0},{3,1},{4,6},{5,7},{6,4},{7,5},{8,10},{9,11},{10,... | collective-permute-start | bytes 196616 | tf_op jit(solution)/shard_map/ppermute | solution.py:693
  151.3 12.2 %collective-permute-start.23 = (bf16[512,128]{1,0:T(8,128)(2,1)S(1)}, bf16[512,128]{1,0:T(8,128)(2,1)S(1)}, u32[]{:S(2)}, u32[]{:S(2)}) collective-permute-start(bf16[512,128]{1,0:T(8,128)(2,1)S(1)} %get-tuple-element.67), channel_id=1, source_target_pairs={{0,8},{1,12},{2,0},{3,4},{4,9},{5,13},{6,1},{7,5},{8,10},{9,14},{1... | collective-permute-start | bytes 393224 | tf_op jit(solution)/shard_map/ppermute | solution.py:700
  151.6 11.9 %collective-permute-start.22 = (bf16[512,128]{1,0:T(8,128)(2,1)S(1)}, bf16[512,128]{1,0:T(8,128)(2,1)S(1)}, u32[]{:S(2)}, u32[]{:S(2)}) collective-permute-start(bf16[512,128]{1,0:T(8,128)(2,1)S(1)} %get-tuple-element.66), channel_id=1, source_target_pairs={{0,0},{1,4},{2,8},{3,12},{4,1},{5,5},{6,9},{7,13},{8,2},{9,6},{10,... | collective-permute-start | bytes 393224 | tf_op jit(solution)/shard_map/ppermute | solution.py:700

commit v10 on v9

--- a/solution.py
+++ b/solution.py
@@ -302,24 +302,31 @@
     return grad_right, grad_left
 
 
-def cut_kernel(idx_ref, in_ref, out_ref):
-    out_ref[...] = in_ref[...]
-
-
-def cut_tokens(tokens, rows, row, column, cost=SMALL):
-    block = (rows, tokens.shape[1] // 2)
+def cut_kernel(count, idx_ref, *refs):
+    for in_ref, out_ref in zip(refs[:count], refs[count:]):
+        out_ref[...] = in_ref[...]
+
+
+def cut_tokens(tokens, places, cost=SMALL):
+    block = (tokens.shape[0] // 2, tokens.shape[1] // 2)
+    shape = jax.ShapeDtypeStruct(block, BF16)
+    count = len(places)
+    flat = [index for place in places for index in place]
     return pl.pallas_call(
-        cut_kernel,
+        functools.partial(cut_kernel, count),
         grid_spec=pltpu.PrefetchScalarGridSpec(
             num_scalar_prefetch=1,
             grid=(1,),
-            in_specs=[pl.BlockSpec(block, lambda n, s: (s[0], s[1]))],
-            out_specs=pl.BlockSpec(block, lambda n, s: (0, 0)),
-        ),
-        out_shape=jax.ShapeDtypeStruct(block, BF16),
+            in_specs=[
+                pl.BlockSpec(block, lambda n, s, k=k: (s[2 * k], s[2 * k + 1]))
+                for k in range(count)
+            ],
+            out_specs=[pl.BlockSpec(block, lambda n, s: (0, 0))] * count,
+        ),
+        out_shape=[shape] * count,
         cost_estimate=cost,
         name="cut_tokens",
-    )(jnp.stack([row, column]).astype(jnp.int32), tokens)
+    )(jnp.stack(flat).astype(jnp.int32), *[tokens] * count)
 
 
 def products_kernel(sets, idx_ref, *refs):
@@ -336,10 +343,12 @@
 def products(pieces, scalars, gate, up, first, width):
     feat = gate.shape[0]
     sets = len(pieces) // 4
-    half = pieces[0][0].shape[0] // 2
+    half = pieces[0][0].shape[0] // (1 if pieces[0][1] is None else 2)
     start = first // BLK
 
     def piece_spec(row, column):
+        if row is None:
+            return pl.BlockSpec((half, feat), lambda n, s: (0, s[column]))
         return pl.BlockSpec((half, feat), lambda n, s: (s[row], s[column]))
 
     weight_spec = pl.BlockSpec(
@@ -497,40 +506,30 @@
             student_ref[:, span] = sum((-ref[:, span] for ref in targets), student)
 
 
-def token_specs(half, width, steps, begin, own):
-    def chunk(n, s):
-        step = jnp.maximum(n - begin, 0)
-        return natural(step, s[2], steps // 2)
-
-    def near(n, s):
-        return jnp.clip(n - begin, 0, steps // 2 - 1)
-
-    def far(n, s):
-        return jnp.clip(n - begin - steps // 2, 0, steps // 2 - 1)
-
-    def specs(place):
+def token_specs(half, width, chunk, late):
+    if not late:
         return [
-            pl.BlockSpec((half, width), lambda n, s, p=p: (s[p % 2], place(n, s)))
+            pl.BlockSpec((half, width), lambda n, s, p=p: (s[p % 2], chunk(n, s)))
             for p in range(4)
         ]
-
-    if own:
-        return specs(chunk)
-    whole = pl.BlockSpec((half, width), lambda n, s: (0, far(n, s)))
-    return specs(near) + [whole] * 4
+    inner = pl.BlockSpec((half, width), lambda n, s: (0, lax.rem(chunk(n, s), 2)))
+    return [inner] * 8
 
 
 def student_part(tokens, late, scalars, factors, left_diag, targets, pairs, tensor_count):
     parts, _, size = factors.shape
-    half = tokens[0].shape[0] // 2
+    half = tokens[0].shape[0] // (1 if late else 2)
     groups = left_diag.shape[0]
     blocks = groups * BLK // pairs
     steps = blocks // (2 * WIDE)
 
+    def chunk(n, s):
+        return natural(n, s[2], steps // 2)
+
     def right_spec(half):
         return pl.BlockSpec(
             (1, WIDE * pairs, size),
-            lambda n, s: (s[3] ^ natural(n, s[2], steps // 2), half, 0),
+            lambda n, s: (s[3] ^ chunk(n, s), half, 0),
         )
 
     return pl.pallas_call(
@@ -538,7 +537,7 @@
         grid_spec=pltpu.PrefetchScalarGridSpec(
             num_scalar_prefetch=1,
             grid=(steps,),
-            in_specs=token_specs(half, 2 * WIDE * size, steps, 0, not late)
+            in_specs=token_specs(half, 2 * WIDE * size, chunk, late)
             + [right_spec(0), right_spec(1), whole_spec(left_diag)]
             + [whole_spec(target) for target in targets],
             out_specs=[
@@ -557,121 +556,126 @@
     )(scalars, *tokens, factors, factors, left_diag, *targets)
 
 
-def grads_kernel(groups, steps, scale, idx_ref, *refs):
+def place(z, owner):
+    bits = z ^ owner
+    return lax.rem(bits, 2) * 2 + bits // 2
+
+
+def left_kernel(chunks, scale, idx_ref, *refs):
     hidden, refs = refs[:4], refs[4:]
-    weight_ref, rest0, rest1, mixed0, mixed1, left_ref = refs[:6]
-    own, near, far = refs[6:10], refs[10:14], refs[14:18]
-    out_ref, lhs, back, wide = refs[18:]
+    weight_ref, rest0, rest1, mixed0, mixed1, left_ref, out_ref, back_ref, lhs = refs
     step = pl.program_id(0)
-    z = idx_ref[3]
     parts, size = out_ref.shape[0], out_ref.shape[2]
-    chunks = 2 * steps
     blocks = chunks * WIDE
-    per_part = blocks // parts
     share = BLK // chunks
-    pairs = groups * share // WIDE
     fold = BLK // blocks
-
-    def place(owner):
-        bits = z ^ owner
-        return lax.rem(bits, 2) * 2 + bits // 2
-
     pl.when(step == 0)(lambda: fill_rows(lhs, hidden))
-
-    @pl.when(step < groups)
-    def _():
-        target = jnp.dot(lhs[...], weight_ref[...], preferred_element_type=F32)
-        rest = jnp.concatenate([rest0[...], rest1[...]], axis=0)
-        out_grad = ((rest - target) * scale).astype(BF16)
-        mixed = jnp.concatenate([mixed0[0], mixed1[0]], axis=1)
-        left = jnp.dot(mixed, out_grad, preferred_element_type=F32)
-        value = lax.dot_general(
-            left_ref[0], out_grad, NT, preferred_element_type=F32
-        ).astype(BF16)
-        row = pl.multiple_of(step * share, share)
-        for c in range(chunks):
-            back[c, pl.ds(row, share), :] = value[c * share : (c + 1) * share]
-        low = lax.broadcasted_iota(jnp.int32, (blocks, size), 1) < blocks
-        rows = blocks // parts
-        for pair in range(fold // 2):
-            lanes = slice(pair * size, (pair + 1) * size)
-            picked = []
-            for a in (2 * pair, 2 * pair + 1):
-                for c in range(chunks):
-                    begin = (c * fold + a) * WIDE
-                    picked.append(left[begin : begin + WIDE, lanes])
-            turned = jnp.concatenate(picked, axis=0).T
-            both = jnp.where(low, turned[:blocks], turned[blocks:]).astype(BF16)
-            begin = per_part * pairs + (step * (fold // 2) + pair) * rows
-            begin = pl.multiple_of(begin, rows)
-            for owner in range(parts):
-                out_ref[place(owner), pl.ds(begin, rows), :] = both[
-                    owner * rows : (owner + 1) * rows
-                ]
+    target = jnp.dot(lhs[...], weight_ref[...], preferred_element_type=F32)
+    rest = jnp.concatenate([rest0[...], rest1[...]], axis=0)
+    out_grad = ((rest - target) * scale).astype(BF16)
+    mixed = jnp.concatenate([mixed0[0], mixed1[0]], axis=1)
+    left = jnp.dot(mixed, out_grad, preferred_element_type=F32)
+    value = lax.dot_general(left_ref[0], out_grad, NT, preferred_element_type=F32)
+    value = value.astype(BF16)
+    for c in range(chunks):
+        back_ref[c] = value[c * share : (c + 1) * share]
+    low = lax.broadcasted_iota(jnp.int32, (blocks, size), 1) < blocks
+    rows = blocks // parts
+    for pair in range(fold // 2):
+        lanes = slice(pair * size, (pair + 1) * size)
+        picked = []
+        for a in (2 * pair, 2 * pair + 1):
+            for c in range(chunks):
+                begin = (c * fold + a) * WIDE
+                picked.append(left[begin : begin + WIDE, lanes])
+        turned = jnp.concatenate(picked, axis=0).T
+        both = jnp.where(low, turned[:blocks], turned[blocks:]).astype(BF16)
+        begin = pl.multiple_of((step * (fold // 2) + pair) * rows, rows)
+        for owner in range(parts):
+            out_ref[place(idx_ref[3], owner), pl.ds(begin, rows), :] = both[
+                owner * rows : (owner + 1) * rows
+            ]
+
+
+def left_grads(hidden, weight, rest, mixed, left_diag, scalars, parts, pairs, size, scale):
+    groups, count = left_diag.shape[0], 2 * rest[0].shape[0]
+    width = hidden[0].shape[1]
+    blocks = groups * BLK // pairs
+    chunks = blocks // WIDE
+    share = BLK // chunks
+    column = pl.BlockSpec((count // 2, BLK), lambda n, s: (0, n))
+    slab = pl.BlockSpec((1, BLK, count // 2), lambda n, s: (n, 0, 0))
+    out_rows = pairs * blocks * blocks // size // parts
+    return pl.pallas_call(
+        functools.partial(left_kernel, chunks, scale),
+        grid_spec=pltpu.PrefetchScalarGridSpec(
+            num_scalar_prefetch=1,
+            grid=(groups,),
+            in_specs=[whole_spec(piece) for piece in hidden]
+            + [pl.BlockSpec((width, BLK), lambda n, s: (1 - s[2], n))]
+            + [column, column, slab, slab]
+            + [pl.BlockSpec((1, BLK, BLK), lambda n, s: (n, 0, 0))],
+            out_specs=[
+                pl.BlockSpec((parts, out_rows, size), lambda n, s: (0, 0, 0)),
+                pl.BlockSpec((chunks, share, count), lambda n, s: (0, n, 0)),
+            ],
+            scratch_shapes=[pltpu.VMEM((count, width), BF16)],
+        ),
+        out_shape=[
+            jax.ShapeDtypeStruct((parts, out_rows, size), BF16),
+            jax.ShapeDtypeStruct((chunks, groups * share, count), BF16),
+        ],
+        compiler_params=pltpu.CompilerParams(vmem_limit_bytes=40 * 2**20),
+        cost_estimate=SMALL,
+        name="left_grads",
+    )(scalars, *hidden, weight, *rest, *mixed, left_diag)
+
+
+def right_kernel(pairs, bit, idx_ref, *refs):
+    own, near, far, (back_ref, out_ref, wide) = refs[:4], refs[4:8], refs[8:12], refs[12:]
+    size = out_ref.shape[2]
+    owner = idx_ref[3] ^ (2 * pl.program_id(0) + bit)
 
     def right(later):
-        pair = natural(step - groups, idx_ref[2], steps // 2)
         for half in range(2):
-            chunk = 2 * pair + half
             lanes = slice(half * WIDE * size, (half + 1) * WIDE * size)
             rows = jnp.concatenate([piece[:, lanes] for piece in own + later], axis=0)
-            value = jnp.dot(back[chunk], rows, preferred_element_type=F32)
+            value = jnp.dot(back_ref[half], rows, preferred_element_type=F32)
             for t in range(WIDE):
                 wide[t] = value[:, t * size : (t + 1) * size]
             for t in range(WIDE):
-                block = chunk * WIDE + t
-                begin = pl.multiple_of(lax.rem(block, per_part) * pairs, pairs)
-                out_ref[place(block // per_part), pl.ds(begin, pairs), :] = wide[
+                begin = (half * WIDE + t) * pairs
+                out_ref[0, begin : begin + pairs, :] = wide[
                     t, pl.ds(t, pairs, stride=WIDE), :
                 ].astype(BF16)
 
-    pl.when((step >= groups) & (step < groups + steps // 2))(lambda: right(near))
-    pl.when(step >= groups + steps // 2)(lambda: right(far))
-
-
-def factor_grads(
-    hidden, weight, rest, mixed, left_diag, own, late, scalars, parts, size, scale
-):
-    groups, count = left_diag.shape[0], 2 * rest[0].shape[0]
-    width = hidden[0].shape[1]
-    half = own[0].shape[0] // 2
-    steps = own[0].shape[1] // (2 * WIDE * size)
-    blocks = 2 * steps * WIDE
-    pairs = groups * BLK // blocks
-
-    def group(n):
-        return jnp.minimum(n, groups - 1)
-
-    column = pl.BlockSpec((count // 2, BLK), lambda n, s: (0, group(n)))
-    slab = pl.BlockSpec((1, BLK, count // 2), lambda n, s: (group(n), 0, 0))
-    out_rows = (pairs * blocks + pairs * blocks * blocks // size) // parts
+    pl.when(owner // 2 == idx_ref[2])(lambda: right(near))
+    pl.when(owner // 2 != idx_ref[2])(lambda: right(far))
+
+
+def right_grads(back, own, late, scalars, pairs, bit, size, cost):
+    half = late[0].shape[0]
+    rows, count = back.shape[1:]
+
+    def owner(n, s):
+        return s[3] ^ (2 * n + bit)
+
     return pl.pallas_call(
-        functools.partial(grads_kernel, groups, steps, scale),
+        functools.partial(right_kernel, pairs, bit),
         grid_spec=pltpu.PrefetchScalarGridSpec(
             num_scalar_prefetch=1,
-            grid=(groups + steps,),
-            in_specs=[whole_spec(piece) for piece in hidden]
-            + [pl.BlockSpec((width, BLK), lambda n, s: (1 - s[2], group(n)))]
-            + [column, column, slab, slab]
-            + [
-                pl.BlockSpec(
-                    (1, BLK, BLK), lambda n, s: (group(n), 0, 0)
-                )
-            ]
-            + token_specs(half, 2 * WIDE * size, steps, groups, True)
-            + token_specs(half, 2 * WIDE * size, steps, groups, False),
-            out_specs=pl.BlockSpec((parts, out_rows, size), lambda n, s: (0, 0, 0)),
-            scratch_shapes=[
-                pltpu.VMEM((count, width), BF16),
-                pltpu.VMEM((2 * steps, groups * BLK // (2 * steps), count), BF16),
-                pltpu.VMEM((WIDE, pairs * WIDE, size), F32),
-            ],
-        ),
-        out_shape=jax.ShapeDtypeStruct((parts, out_rows, size), BF16),
+            grid=(2,),
+            in_specs=token_specs(half, 2 * WIDE * size, owner, False)
+            + token_specs(half, 2 * WIDE * size, owner, True)
+            + [pl.BlockSpec((2, rows, count), lambda n, s: (owner(n, s), 0, 0))],
+            out_specs=pl.BlockSpec((1, 2 * WIDE * pairs, size), lambda n, s: (n, 0, 0)),
+            scratch_shapes=[pltpu.VMEM((WIDE, pairs * WIDE, size), F32)],
+        ),
+        out_shape=jax.ShapeDtypeStruct((2, 2 * WIDE * pairs, size), BF16),
         compiler_params=pltpu.CompilerParams(vmem_limit_bytes=40 * 2**20),
-        cost_estimate=SMALL,
-        name="factor_grads",
-    )(scalars, *hidden, weight, *rest, *mixed, left_diag, *own, *late)
+        cost_estimate=cost,
+        name="right_grads",
+    )(scalars, *own, *late, back)
 
 
 def tiled_body(tokens, gate_weight, up_weight, down_weight, right_factor, left_factor):
@@ -706,8 +710,8 @@
         return sum(term.astype(F32) for term in terms)
 
     near_tokens = swap(tokens)
-    first = cut_tokens(tokens, rows, jnp.int32(0), 1 - chip)
-    arrived = across(first)
+    first = cut_tokens(tokens, [(odd, 1 - chip), (1 - odd, 1 - chip)])
+    arrived = [across(value) for value in first]
     base = jnp.stack([odd, 1 - odd])
     mine_block = lax.div(part, BLK) * chip
     other_block = lax.div(part, BLK) * (1 - chip)
@@ -717,28 +721,29 @@
 
     own_pieces = [(t, row, 2) for t in (tokens, near_tokens) for row in (0, 1)]
     mine, other = products(
-        own_pieces, after(scalars(other_block), first), gate_weight, up_weight, 0, part
+        own_pieces, after(scalars(other_block), *first), gate_weight, up_weight, 0, part
     )
 
     pairs, blocks = left_factor.shape[0], left_factor.shape[2]
     left_rows = left_factor.reshape(pairs // 2, 2, -1, blocks).transpose(0, 2, 1, 3)
     turned = turn(after(right_factor, mine), 0)
-    rest = cut_tokens(after(tokens, mine), rows // 2, odd, chip, LARGE)
+    (rest,) = cut_tokens(after(tokens, mine), [(odd, chip)], LARGE)
     factors = jnp.concatenate(
         [after(turned, rest).reshape(-1, LANES), left_rows.reshape(-1, LANES)], axis=0
     )[None]
     more = along(factors, 1)
     sums = add(mine[0], swap(other[0])).astype(BF16)
-    arrived = after(arrived, more, rest, sums)
+    arrived = [after(arrived[0], rest), after(arrived[1], more, rest, sums)]
     got_early = across(sums)
     late_first = across(after(rest, sums))
     factors = jnp.concatenate([factors, more], axis=0)
-    more = along(after(factors, arrived), 2)
+    more = along(after(factors, arrived[1]), 2)
 
     order = jnp.concatenate([base, jnp.stack([chip, z])]).astype(jnp.int32)
     own = [tokens, tokens, near_tokens, near_tokens]
-    near_arrived = swap(arrived)
-    late_pieces = [(t, row, 3) for t in (arrived, near_arrived) for row in (0, 1)]
+    near_arrived = [swap(value) for value in arrived]
+    late = arrived + near_arrived
+    late_pieces = [(t, None, 3) for t in late]
     late_order = after(scalars(other_block), sums)
     mine, other = products(late_pieces, late_order, gate_weight, up_weight, 0, part)
     near = swap(other[0])
@@ -760,8 +765,9 @@
     near1 = swap(hidden1)
     left_diag = spread_left(order, after(factors, hidden1), pairs * blocks // BLK)
     late_partner = along(after(late_first, hidden1), 1)
+    target1 = target_part(1.0, [], hidden1, near1, down_weight, chip)
     mixed0, rest0 = student_part(
-        [after(tokens, hidden1, sums)] + own[1:],
+        [after(tokens, target1)] + own[1:],
         False,
         order,
         factors,
@@ -770,15 +776,13 @@
         pairs,
         tensor_count,
     )
-    target1 = target_part(1.0, [], hidden1, after(near1, mixed0), down_weight, chip)
-    hidden0 = activate(0, after(got, target1))
+    hidden0 = activate(0, after(got, mixed0))
     got0 = across(hidden0)
     near0 = swap(hidden0)
     late_partner = after(late_partner, mixed0)
-    late = [arrived, arrived, near_arrived, near_arrived]
     late += [late_first, late_partner, swap(late_first), swap(late_partner)]
     mixed1, rest1 = student_part(
-        [after(arrived, hidden0)] + late[1:],
+        [after(late[0], hidden0)] + late[1:],
         True,
         order,
         factors,
@@ -792,26 +796,31 @@
     got1, got0 = after(got1, mixed1), after(got0, rest0)
     hidden = [got0, got1, swap(got0), swap(got1)]
 
-    grads = factor_grads(
+    size = right_factor.shape[2]
+    left, back = left_grads(
         hidden,
         down_weight,
         (rest0, rest1),
         (mixed0, mixed1),
         left_diag,
-        own,
-        late,
         order,
         tensor_count,
-        right_factor.shape[2],
+        pairs,
+        size,
         1.0 / math.sqrt(rows * fsdp_count),
     )
-    summed = add(grads[:2], along(grads[2:], 1)).astype(BF16)
-    right_shape = right_factor.shape
-    cut = right_shape[0] * right_shape[1]
-    grad_right = add(turn(summed[0, :cut], 0), turn(summed[1, :cut], 2))
-    grad_left = add(summed[0, cut:], along(summed[1, cut:], 2))
+    got_left = along(left[2:], 1)
+    sent = right_grads(back, own, late, order, pairs, 1, size, SMALL)
+    left = add(left[:2], after(got_left, sent)).astype(BF16)
+    got_left = along(left[1], 2)
+    got_right = along(sent, 1)
+    kept_back = after(back, sent, left)
+    right = right_grads(kept_back, own, late, order, pairs, 0, size, LARGE)
+    right = add(right, got_right).astype(BF16)
+    grad_right = add(turn(right[0], 0), turn(right[1], 2))
+    grad_left = add(left[0], got_left)
     grad_left = grad_left.reshape(pairs // 2, -1, 2, blocks).transpose(0, 2, 1, 3)
-    return grad_right.reshape(right_shape), grad_left.reshape(left_factor.shape)
+    return grad_right.reshape(right_factor.shape), grad_left.reshape(left_factor.shape)
 
 
 def body(*args):

time: 167 us -> 173 us (1.036)
  waiting for transfers between devices: 34 us -> 39.3 us
  starting transfers between devices: 28.5 us -> 31.6 us
  local copies, waits for them, and re-layouts: 6.19 us -> 3.27 us
    ppermute x6 -> x7, waiting for transfers between devices: 10.2 us -> 17.6 us  [across(): return lax.ppermute(value, 'fsdp', [(i, i ^ 2) for i in range(fsdp_count)])]
    ppermute x5 -> x6, waiting for transfers between devices: 13.1 us -> 6.79 us  [along(): lax.ppermute(value, 'tensor', [(i, i ^ bit) for i in range(tensor_count)])]
    ppermute x5 -> x6, starting transfers between devices: 13.9 us -> 9.45 us  [along(): lax.ppermute(value, 'tensor', [(i, i ^ bit) for i in range(tensor_count)])]
    ppermute x3, starting transfers between devices: 1.78 us -> 6.2 us  [turn(): return lax.ppermute(value, both_axes, perm)]
    ppermute x11 -> x12, waiting for transfers between devices: 2.2 us -> 5.62 us  [swap(): return lax.ppermute(value, 'fsdp', [(i, i ^ 1) for i in range(fsdp_count)])]
    unnamed x30 -> x26, local copies, waits for them, and re-layouts: 4.85 us -> 1.94 us
    ppermute x11 -> x12, starting transfers between devices: 2.39 us -> 5.24 us  [swap(): return lax.ppermute(value, 'fsdp', [(i, i ^ 1) for i in range(fsdp_count)])]
    pallas_call x3 -> x5, Pallas kernels: 23.6 us -> 24.6 us  [the longest x1 11.3 us: left_grads(): pl.pallas_call(functools.partial(left_kernel, chunks, scale), grid_spec=p...]
  transfers between devices with their start and end apart: 25 -> 28, of which waited for: 9 -> 9; matrix products, arithmetic and copies ran while one was open for 6% -> 5% of each run, Pallas kernels for 41% -> 44%
where the time goes in v10:
time: 173 us; the launch traced here: 171 us
  Pallas kernels  86.8 us (50%)
  waiting for transfers between devices  39.3 us (23%)
  starting transfers between devices  31.6 us (18%)
  other arithmetic  9.43 us (5%)
  local copies, waits for them, and re-layouts  3.27 us (2%)
    pallas_call x3, Pallas kernels, products(): pl.pallas_call(functools.partial(products_kernel, sets), grid_spec=pltpu....  33.4 us
    ppermute x7, waiting for transfers between devices, across(): return lax.ppermute(value, 'fsdp', [(i, i ^ 2) for i in range(fsdp_count)])  17.6 us
    pallas_call x2, Pallas kernels, target_part(): pl.pallas_call(functools.partial(target_kernel, sign), grid_spec=pltpu.Pr...  14.7 us
    pallas_call x1, Pallas kernels, left_grads(): pl.pallas_call(functools.partial(left_kernel, chunks, scale), grid_spec=p...  11.3 us
    pallas_call x2, Pallas kernels, student_part(): pl.pallas_call(functools.partial(student_kernel, steps, late, tensor_coun...  11.2 us
    ppermute x7, starting transfers between devices, across(): return lax.ppermute(value, 'fsdp', [(i, i ^ 2) for i in range(fsdp_count)])  10.7 us
    ppermute x6, starting transfers between devices, along(): lax.ppermute(value, 'tensor', [(i, i ^ bit) for i in range(tensor_count)])  9.45 us
    ppermute x3, waiting for transfers between devices, turn(): return lax.ppermute(value, both_axes, perm)  9.29 us
  transfers between devices with their start and end apart: 28, of which 9 were waited for; matrix products, arithmetic and copies ran while one was open for 5% of the time, Pallas kernels for 44%

profile of v10, /device:TPU:0, one launch (start us, length us, event | category | flops | bytes accessed | tf_op | source)
XLA Modules:
  0.0 171.4 jit_solution(2644622925538071395)
XLA Ops:
  0.6 0.5 collective-permute-start
  1.1 0.7 pad_add_fusion.1.idx_ref
  1.8 3.0 %cut_tokens.2 = (bf16[64,4096]{1,0:T(8,128)(2,1)}, bf16[64,4096]{1,0:T(8,128)(2,1)}) custom-call(s32[4]{0:T(128)} %pad_add_fusion.1.idx_ref, bf16[128,8192]{1,0:T(8,128)(2,1)} %refs_1_.11, bf16[128,8192]{1,0:T(8,128)(2,1)} %refs_1_.11), custom_call_target="tpu_custom_call" | custom-call | flops 1 | bytes 1 | tf_op jit(solution)/shard_map/cut_tokens/pallas_call | solution.py:315
  4.8 2.5 %collective-permute-start.2 = (bf16[64,4096]{1,0:T(8,128)(2,1)}, bf16[64,4096]{1,0:T(8,128)(2,1)S(1)}, u32[]{:S(2)}, u32[]{:S(2)}) collective-permute-start(bf16[64,4096]{1,0:T(8,128)(2,1)} %get-tuple-element.41), channel_id=1, source_target_pairs={{0,8},{4,12},{8,0},{12,4},{1,9},{5,13},{9,1},{13,5},{2,10},{6,14},... | collective-permute-start | bytes 1572872 | tf_op jit(solution)/shard_map/ppermute | solution.py:694
  7.4 0.1 concatenate.25.idx_ref
  7.5 0.1 copy.11
  7.6 0.1 reshape.38
  7.7 0.7 pad_add_fusion.2.idx_ref
  8.4 10.8 %gate_up_products.3 = (bf16[1,2,128,1792]{3,2,1,0:T(8,128)(2,1)S(1)}, bf16[1,2,128,1792]{3,2,1,0:T(8,128)(2,1)}) custom-call(s32[5]{0:T(128)S(1)} %concatenate.25.idx_ref, bf16[128,8192]{1,0:T(8,128)(2,1)S(1)} %copy-done, bf16[128,8192]{1,0:T(8,128)(2,1)S(1)} %copy-done, bf16[128,8192]{1,0:T(8,128)(2,1)} %collective-permute-done.refs_2_.refs_3_, ...), custom_call_target="tpu_custom_call" | custom-call | flops 1 | bytes 1 | tf_op jit(solution)/shard_map/gate_up_products/pallas_call | solution.py:359
  19.2 0.9 copy-done.6
  20.1 0.7 collective-permute-start.3
  20.8 3.5 %collective-permute-start.5 = (bf16[2,128,1792]{2,1,0:T(8,128)(2,1)}, bf16[2,128,1792]{2,1,0:T(8,128)(2,1)S(1)}, u32[]{:S(2)}, u32[]{:S(2)}) collective-permute-start(bf16[2,128,1792]{2,1,0:T(8,128)(2,1)} %bitcast.13), channel_id=1, source_target_pairs={{0,4},{4,0},{8,12},{12,8},{1,5},{5,1},{9,13},{13,9},{2,6},{6,2},{1... | collective-permute-start | bytes 2752520 | tf_op jit(solution)/shard_map/ppermute | solution.py:691
  24.3 2.6 %cut_tokens.3 = bf16[64,4096]{1,0:T(8,128)(2,1)} custom-call(s32[2]{0:T(128)} %pad_add_fusion.2.idx_ref, bf16[128,8192]{1,0:T(8,128)(2,1)} %refs_1_.11), custom_call_target="tpu_custom_call" | custom-call | flops 10000000000 | bytes 10000000 | tf_op jit(solution)/shard_map/cut_tokens/pallas_call | solution.py:315
  26.8 6.7 %collective-permute-done.1.refs_0_.refs_4_ = bf16[64,4096]{1,0:T(8,128)(2,1)S(1)} collective-permute-done((bf16[64,4096]{1,0:T(8,128)(2,1)}, bf16[64,4096]{1,0:T(8,128)(2,1)S(1)}, u32[]{:S(2)}, u32[]{:S(2)}) %collective-permute-start.1) | collective-permute-done | bytes 524320 | tf_op jit(solution)/shard_map/ppermute | solution.py:694
  33.6 1.6 collective-permute-start.4
  35.2 1.2 fusion.1
  36.4 4.6 %collective-permute-done.4 = bf16[1,768,128]{2,1,0:T(8,128)(2,1)S(1)} collective-permute-done((bf16[1,768,128]{2,1,0:T(8,128)(2,1)S(1)}, bf16[1,768,128]{2,1,0:T(8,128)(2,1)S(1)}, u32[]{:S(2)}, u32[]{:S(2)}) %collective-permute-start.4) | collective-permute-done | bytes 196640 | tf_op jit(solution)/shard_map/ppermute | solution.py:697
  41.0 0.1 concatenate.27.idx_ref
  41.1 2.4 %collective-permute-start.9 = (bf16[2,128,1792]{2,1,0:T(8,128)(2,1)}, bf16[2,128,1792]{2,1,0:T(8,128)(2,1)S(1)}, u32[]{:S(2)}, u32[]{:S(2)}) collective-permute-start(bf16[2,128,1792]{2,1,0:T(8,128)(2,1)} %fusion.1), channel_id=1, source_target_pairs={{0,8},{4,12},{8,0},{12,4},{1,9},{5,13},{9,1},{13,5},{2,10},{6,14},... | collective-permute-start | bytes 2752520 | tf_op jit(solution)/shard_map/ppermute | solution.py:694
  43.5 1.2 collective-permute-start.10
  44.7 1.9 %collective-permute-start.8 = (bf16[64,4096]{1,0:T(8,128)(2,1)}, bf16[64,4096]{1,0:T(8,128)(2,1)}, u32[]{:S(2)}, u32[]{:S(2)}) collective-permute-start(bf16[64,4096]{1,0:T(8,128)(2,1)} %cut_tokens.3), channel_id=1, source_target_pairs={{0,8},{4,12},{8,0},{12,4},{1,9},{5,13},{9,1},{13,5},{2,10},{6,14},... | collective-permute-start | bytes 1572872 | tf_op jit(solution)/shard_map/ppermute | solution.py:694
  46.7 10.1 %gate_up_products.4 = (bf16[1,2,128,1792]{3,2,1,0:T(8,128)(2,1)S(1)}, bf16[1,2,128,1792]{3,2,1,0:T(8,128)(2,1)S(1)}) custom-call(s32[5]{0:T(128)S(1)} %concatenate.25.idx_ref, bf16[64,4096]{1,0:T(8,128)(2,1)S(1)} %collective-permute-done.1.refs_0_.refs_4_, bf16[64,4096]{1,0:T(8,128)(2,1)S(1)} %collective-permute-done.2.refs_1_.refs_5_, ...), custom_call_target="tpu_custom_call" | custom-call | flops 1 | bytes 1 | tf_op jit(solution)/shard_map/gate_up_products/pallas_call | solution.py:359
  56.8 0.1 collective-permute-start.11
  56.9 12.5 %gate_up_products.5 = (bf16[2,2,128,1792]{3,2,1,0:T(8,128)(2,1)S(1)}, bf16[2,2,128,1792]{3,2,1,0:T(8,128)(2,1)S(1)}) custom-call(s32[5]{0:T(128)S(1)} %concatenate.27.idx_ref, bf16[128,8192]{1,0:T(8,128)(2,1)S(1)} %copy-done.1, bf16[128,8192]{1,0:T(8,128)(2,1)S(1)} %copy-done.1, bf16[128,8192]{1,0:T(8,128)(2,1)} %collective-permute-done.refs_2_.refs_3_, ...), custom_call_target="tpu_custom_call" | custom-call | flops 10000000000 | bytes 10000000 | tf_op jit(solution)/shard_map/gate_up_products/pallas_call | solution.py:359
  69.4 1.3 fusion
  70.8 5.4 %collective-permute-done.8.refs_4_.refs_8_ = bf16[64,4096]{1,0:T(8,128)(2,1)} collective-permute-done((bf16[64,4096]{1,0:T(8,128)(2,1)}, bf16[64,4096]{1,0:T(8,128)(2,1)}, u32[]{:S(2)}, u32[]{:S(2)}) %collective-permute-start.8) | collective-permute-done | bytes 524320 | tf_op jit(solution)/shard_map/ppermute | solution.py:694
  76.1 3.8 %collective-permute-done.12 = bf16[2,2,128,1792]{3,2,1,0:T(8,128)(2,1)S(1)} collective-permute-done((bf16[2,2,128,1792]{3,2,1,0:T(8,128)(2,1)S(1)}, bf16[2,2,128,1792]{3,2,1,0:T(8,128)(2,1)S(1)}, u32[]{:S(2)}, u32[]{:S(2)}) %collective-permute-start.12) | collective-permute-done | bytes 1835040 | tf_op jit(solution)/shard_map/ppermute | solution.py:691
  79.9 0.3 bitcast_add_fusion.1
  80.2 1.0 copy-done.9
  81.2 1.1 fusion.5.mine_ref
  82.2 0.1 collective-permute-start.14
  82.4 0.6 pad_add_fusion.idx_ref
  83.0 0.4 collective-permute-start.15
  83.3 1.0 pad_maximum_fusion.rows_ref.refs_4_.refs_5_.refs_8_.refs_9_
  84.3 1.7 %collective-permute-start.17 = (bf16[2,128,1792]{2,1,0:T(8,128)(2,1)}, bf16[2,128,1792]{2,1,0:T(8,128)(2,1)}, u32[]{:S(2)}, u32[]{:S(2)}) collective-permute-start(bf16[2,128,1792]{2,1,0:T(8,128)(2,1)} %fusion), channel_id=1, source_target_pairs={{0,8},{4,12},{8,0},{12,4},{1,9},{5,13},{9,1},{13,5},{2,10},{6,14},... | collective-permute-start | bytes 2752520 | tf_op jit(solution)/shard_map/ppermute | solution.py:694
  86.0 0.3 collective-permute-start.20
  86.3 1.6 collective-permute-start.13
  87.9 3.0 %spread_left.1.refs_6_.refs_10_.refs_9_ = bf16[8,256,256]{2,1,0:T(8,128)(2,1)} custom-call(s32[4]{0:T(128)} %pad_add_fusion.idx_ref, bf16[4,768,128]{2,1,0:T(8,128)(2,1)} %pad_maximum_fusion.rows_ref.refs_4_.refs_5_.refs_8_.refs_9_), custom_call_target="tpu_custom_call" | custom-call | flops 1 | bytes 1 | tf_op jit(solution)/shard_map/spread_left/pallas_call | solution.py:449
  90.9 7.5 %target_part.2.refs_11_ = f32[256,2048]{1,0:T(8,128)S(1)} custom-call(s32[1]{0:T(128)} %bitcast.2.idx_ref, bf16[128,1792]{1,0:T(8,128)(2,1)} %fusion.5.mine_ref, bf16[128,1792]{1,0:T(8,128)(2,1)} %collective-permute-done.14.near_ref, bf16[3584,2048]{1,0:T(8,128)(2,1)} %refs_4_.5), custom_call_target="tpu_custom_call" | custom-call | flops 1 | bytes 1 | tf_op jit(solution)/shard_map/target_part/pallas_call | solution.py:396
  98.5 5.4 %student_part.2 = (bf16[8,256,256]{2,1,0:T(8,128)(2,1)S(1)}, f32[256,2048]{1,0:T(8,128)S(1)}) custom-call(s32[4]{0:T(128)S(1)} %copy-done.8, bf16[128,8192]{1,0:T(8,128)(2,1)S(1)} %copy-done.1, bf16[128,8192]{1,0:T(8,128)(2,1)S(1)} %copy-done.1, bf16[128,8192]{1,0:T(8,128)(2,1)} %collective-permute-done.refs_2_.refs_3_, ...), custom_call_target="tpu_custom_call" | custom-call | flops 10000000000 | bytes 10000000 | tf_op jit(solution)/shard_map/student_part/pallas_call | solution.py:535
  103.9 3.9 %collective-permute-done.17 = bf16[2,128,1792]{2,1,0:T(8,128)(2,1)} collective-permute-done((bf16[2,128,1792]{2,1,0:T(8,128)(2,1)}, bf16[2,128,1792]{2,1,0:T(8,128)(2,1)}, u32[]{:S(2)}, u32[]{:S(2)}) %collective-permute-start.17) | collective-permute-done | bytes 917536 | tf_op jit(solution)/shard_map/ppermute | solution.py:694
  107.8 1.5 bitcast_add_fusion
  109.4 0.3 fusion.3.mine_ref
  109.6 0.6 collective-permute-start.19
  110.2 1.7 %collective-permute-start.18 = (bf16[128,1792]{1,0:T(8,128)(2,1)S(1)}, bf16[128,1792]{1,0:T(8,128)(2,1)S(1)}, u32[]{:S(2)}, u32[]{:S(2)}) collective-permute-start(bf16[128,1792]{1,0:T(8,128)(2,1)S(1)} %fusion.3.mine_ref), channel_id=1, source_target_pairs={{0,8},{4,12},{8,0},{12,4},{1,9},{5,13},{9,1},{13,5},{2,10},{6,14},... | collective-permute-start | bytes 1376264 | tf_op jit(solution)/shard_map/ppermute | solution.py:694
  111.9 5.8 %student_part.3 = (bf16[8,256,256]{2,1,0:T(8,128)(2,1)S(1)}, f32[256,2048]{1,0:T(8,128)S(1)}) custom-call(s32[4]{0:T(128)S(1)} %copy-done.8, bf16[64,4096]{1,0:T(8,128)(2,1)S(1)} %collective-permute-done.1.refs_0_.refs_4_, bf16[64,4096]{1,0:T(8,128)(2,1)S(1)} %collective-permute-done.2.refs_1_.refs_5_, ...), custom_call_target="tpu_custom_call" | custom-call | flops 10000000000 | bytes 10000000 | tf_op jit(solution)/shard_map/student_part/pallas_call | solution.py:535
  117.8 0.1 collective-permute-start.22
  117.8 7.2 %target_part.3.refs_5_ = f32[256,2048]{1,0:T(8,128)S(1)} custom-call(s32[1]{0:T(128)} %bitcast.2.idx_ref, bf16[128,1792]{1,0:T(8,128)(2,1)S(1)} %fusion.3.mine_ref, bf16[128,1792]{1,0:T(8,128)(2,1)S(1)} %collective-permute-done.19.near_ref, bf16[3584,2048]{1,0:T(8,128)(2,1)} %refs_4_.5, f32[256,2048]{1,0:T(8,128)S(1)} %get-tuple-element.70.refs_0_), custom_call_target="tpu_custom_call" | custom-call | flops 1 | bytes 1 | tf_op jit(solution)/shard_map/target_part/pallas_call | solution.py:396
  125.0 1.5 collective-permute-done.18.refs_0_
  126.6 1.8 %collective-permute-done.21.refs_2_ = bf16[128,1792]{1,0:T(8,128)(2,1)S(1)} collective-permute-done((bf16[128,1792]{1,0:T(8,128)(2,1)S(1)}, bf16[128,1792]{1,0:T(8,128)(2,1)S(1)}, u32[]{:S(2)}, u32[]{:S(2)}) %collective-permute-start.21) | collective-permute-done | bytes 458784 | tf_op jit(solution)/shard_map/ppermute | solution.py:691
  128.4 11.3 %left_grads.1 = (bf16[4,256,128]{2,1,0:T(8,128)(2,1)S(1)}, bf16[8,256,512]{2,1,0:T(8,128)(2,1)S(1)}) custom-call(s32[4]{0:T(128)S(1)} %copy-done.8, bf16[128,1792]{1,0:T(8,128)(2,1)S(1)} %collective-permute-done.18.refs_0_, bf16[128,1792]{1,0:T(8,128)(2,1)} %collective-permute-done.20.refs_1_, bf16[128,1792]{1,0:T(8,128)(2,1)S(1)} %collective-permute-done.21.refs_2_, ...), custom_call_target="tpu_custom_call" | custom-call | flops 1 | bytes 1 | tf_op jit(solution)/shard_map/left_grads/pallas_call | solution.py:609
  139.7 1.6 collective-permute-start.23
  141.4 3.8 %right_grads.2 = bf16[2,512,128]{2,1,0:T(8,128)(2,1)S(1)} custom-call(s32[4]{0:T(128)S(1)} %copy-done.8, bf16[128,8192]{1,0:T(8,128)(2,1)S(1)} %copy-done.1, bf16[128,8192]{1,0:T(8,128)(2,1)S(1)} %copy-done.1, bf16[128,8192]{1,0:T(8,128)(2,1)} %collective-permute-done.refs_2_.refs_3_, bf16[128,8192]{1,0:T(8,128)(2,1)} %collective-permute-done.refs_2_.refs_3_, ...), custom_call_target="tpu_custom_call" | custom-call | flops 1 | bytes 1 | tf_op jit(solution)/shard_map/right_grads/pallas_call | solution.py:663
  145.2 0.5 collective-permute-start.24
  145.8 2.9 %collective-permute-start.27 = (bf16[256,128]{1,0:T(8,128)(2,1)S(1)}, bf16[256,128]{1,0:T(8,128)(2,1)S(1)}, u32[]{:S(2)}, u32[]{:S(2)}) collective-permute-start(bf16[256,128]{1,0:T(8,128)(2,1)S(1)} %slice_bitcast_fusion.6), channel_id=1, source_target_pairs={{0,2},{1,3},{2,0},{3,1},{4,6},{5,7},{6,4},{7,5},{8,10},{9,11},{10,... | collective-permute-start | bytes 196616 | tf_op jit(solution)/shard_map/ppermute | solution.py:697
  148.7 3.8 %right_grads.3 = bf16[2,512,128]{2,1,0:T(8,128)(2,1)S(1)} custom-call(s32[4]{0:T(128)S(1)} %copy-done.8, bf16[128,8192]{1,0:T(8,128)(2,1)S(1)} %copy-done.1, bf16[128,8192]{1,0:T(8,128)(2,1)S(1)} %copy-done.1, bf16[128,8192]{1,0:T(8,128)(2,1)} %collective-permute-done.refs_2_.refs_3_, bf16[128,8192]{1,0:T(8,128)(2,1)} %collective-permute-done.refs_2_.refs_3_, ...), custom_call_target="tpu_custom_call" | custom-call | flops 10000000000 | bytes 10000000 | tf_op jit(solution)/shard_map/right_grads/pallas_call | solution.py:663
  152.5 2.2 %collective-permute-done.24 = bf16[2,512,128]{2,1,0:T(8,128)(2,1)S(1)} collective-permute-done((bf16[2,512,128]{2,1,0:T(8,128)(2,1)S(1)}, bf16[2,512,128]{2,1,0:T(8,128)(2,1)S(1)}, u32[]{:S(2)}, u32[]{:S(2)}) %collective-permute-start.24) | collective-permute-done | bytes 262176 | tf_op jit(solution)/shard_map/ppermute | solution.py:697
  154.7 0.1 add_convert_fusion
  154.9 0.7 collective-permute-start.25
  155.5 4.9 %collective-permute-start.26 = (bf16[512,128]{1,0:T(8,128)(2,1)S(1)}, bf16[512,128]{1,0:T(8,128)(2,1)S(1)}, u32[]{:S(2)}, u32[]{:S(2)}) collective-permute-start(bf16[512,128]{1,0:T(8,128)(2,1)S(1)} %get-tuple-element.79), channel_id=1, source_target_pairs={{0,8},{1,12},{2,0},{3,4},{4,9},{5,13},{6,1},{7,5},{8,10},{9,14},{1... | collective-permute-start | bytes 393224 | tf_op jit(solution)/shard_map/ppermute | solution.py:704
  160.4 0.2 reshape.40
  160.6 0.7 copy.9
  161.3 9.3 %collective-permute-done.26 = bf16[512,128]{1,0:T(8,128)(2,1)S(1)} collective-permute-done((bf16[512,128]{1,0:T(8,128)(2,1)S(1)}, bf16[512,128]{1,0:T(8,128)(2,1)S(1)}, u32[]{:S(2)}, u32[]{:S(2)}) %collective-permute-start.26) | collective-permute-done | bytes 131104 | tf_op jit(solution)/shard_map/ppermute | solution.py:704
  170.6 0.7 convert_add_fusion.2
  (56 shorter events, 0.3 us)
Async XLA Ops:
  0.6 7.7 %collective-permute-start = (bf16[128,8192]{1,0:T(8,128)(2,1)}, bf16[128,8192]{1,0:T(8,128)(2,1)}, u32[]{:S(2)}, u32[]{:S(2)}) collective-permute-start(bf16[128,8192]{1,0:T(8,128)(2,1)} %refs_1_.11), channel_id=1, source_target_pairs={{0,4},{4,0},{8,12},{12,8},{1,5},{5,1},{9,13},{13,9},{2,6},{6,2},{1... | collective-permute-start | bytes 6291464 | tf_op jit(solution)/shard_map/ppermute | solution.py:691
  1.8 5.7 %copy-start.11 = (bf16[32,16,64]{2,1,0:T(8,128)(2,1)S(1)}, bf16[32,16,64]{2,1,0:T(8,128)(2,1)}, u32[]{:S(2)}) copy-start(bf16[32,16,64]{2,1,0:T(8,128)(2,1)} %param.11) | copy-start | bytes 196612
  1.8 6.6 %copy-start = (bf16[128,8192]{1,0:T(8,128)(2,1)S(1)}, bf16[128,8192]{1,0:T(8,128)(2,1)}, u32[]{:S(2)}) copy-start(bf16[128,8192]{1,0:T(8,128)(2,1)} %refs_1_.11) | copy-start | bytes 6291460
  4.8 31.6 %collective-permute-start.2 = (bf16[64,4096]{1,0:T(8,128)(2,1)}, bf16[64,4096]{1,0:T(8,128)(2,1)S(1)}, u32[]{:S(2)}, u32[]{:S(2)}) collective-permute-start(bf16[64,4096]{1,0:T(8,128)(2,1)} %get-tuple-element.41), channel_id=1, source_target_pairs={{0,8},{4,12},{8,0},{12,4},{1,9},{5,13},{9,1},{13,5},{2,10},{6,14},... | collective-permute-start | bytes 1572872 | tf_op jit(solution)/shard_map/ppermute | solution.py:694
  7.4 26.2 %collective-permute-start.1 = (bf16[64,4096]{1,0:T(8,128)(2,1)}, bf16[64,4096]{1,0:T(8,128)(2,1)S(1)}, u32[]{:S(2)}, u32[]{:S(2)}) collective-permute-start(bf16[64,4096]{1,0:T(8,128)(2,1)} %get-tuple-element.40), channel_id=1, source_target_pairs={{0,8},{4,12},{8,0},{12,4},{1,9},{5,13},{9,1},{13,5},{2,10},{6,14},... | collective-permute-start | bytes 1572872 | tf_op jit(solution)/shard_map/ppermute | solution.py:694
  8.4 11.7 %copy-start.12 = (bf16[16,32,128]{2,1,0:T(8,128)(2,1)S(1)}, bf16[16,32,128]{2,1,0:T(8,128)(2,1)}, u32[]{:S(2)}) copy-start(bf16[16,32,128]{2,1,0:T(8,128)(2,1)} %param.10) | copy-start | bytes 393220
  19.1 0.9 copy-start.6
  20.1 13.5 %collective-permute-start.3 = (bf16[16,32,128]{2,1,0:T(8,128)(2,1)S(1)}, bf16[16,32,128]{2,1,0:T(8,128)(2,1)S(1)}, u32[]{:S(2)}, u32[]{:S(2)}) collective-permute-start(bf16[16,32,128]{2,1,0:T(8,128)(2,1)S(1)} %copy-done.12), channel_id=1, source_target_pairs={{0,0},{1,4},{2,8},{3,12},{4,1},{5,5},{6,9},{7,13},{8,2},{9,6},{10,... | collective-permute-start | bytes 393224 | tf_op jit(solution)/shard_map/ppermute | solution.py:704
  20.8 14.5 %copy-start.7 = (bf16[1,2,128,1792]{3,2,1,0:T(8,128)(2,1)S(1)}, bf16[1,2,128,1792]{3,2,1,0:T(8,128)(2,1)}, u32[]{:S(2)}) copy-start(bf16[1,2,128,1792]{3,2,1,0:T(8,128)(2,1)} %copy-done.6) | copy-start | bytes 2752516
  20.8 14.5 %collective-permute-start.5 = (bf16[2,128,1792]{2,1,0:T(8,128)(2,1)}, bf16[2,128,1792]{2,1,0:T(8,128)(2,1)S(1)}, u32[]{:S(2)}, u32[]{:S(2)}) collective-permute-start(bf16[2,128,1792]{2,1,0:T(8,128)(2,1)} %bitcast.13), channel_id=1, source_target_pairs={{0,4},{4,0},{8,12},{12,8},{1,5},{5,1},{9,13},{13,9},{2,6},{6,2},{1... | collective-permute-start | bytes 2752520 | tf_op jit(solution)/shard_map/ppermute | solution.py:691
  33.5 13.1 %collective-permute-start.6 = (bf16[64,4096]{1,0:T(8,128)(2,1)S(1)}, bf16[64,4096]{1,0:T(8,128)(2,1)}, u32[]{:S(2)}, u32[]{:S(2)}) collective-permute-start(bf16[64,4096]{1,0:T(8,128)(2,1)S(1)} %collective-permute-done.1.refs_0_.refs_4_), channel_id=1, source_target_pairs={{0,4},{4,0},{8,12},{12,8},{1,5},{5,1},{9,13},{13,9},{2,6},{6,2},{1... | collective-permute-start | bytes 1572872 | tf_op jit(solution)/shard_map/ppermute | solution.py:691
  33.6 7.4 %collective-permute-start.4 = (bf16[1,768,128]{2,1,0:T(8,128)(2,1)S(1)}, bf16[1,768,128]{2,1,0:T(8,128)(2,1)S(1)}, u32[]{:S(2)}, u32[]{:S(2)}) collective-permute-start(bf16[1,768,128]{2,1,0:T(8,128)(2,1)S(1)} %maximum_bitcast_fusion), channel_id=1, source_target_pairs={{0,1},{1,0},{2,3},{3,2},{4,5},{5,4},{6,7},{7,6},{8,9},{9,8},{10,11... | collective-permute-start | bytes 589832 | tf_op jit(solution)/shard_map/ppermute | solution.py:697
  41.0 5.7 %collective-permute-start.7 = (bf16[64,4096]{1,0:T(8,128)(2,1)S(1)}, bf16[64,4096]{1,0:T(8,128)(2,1)}, u32[]{:S(2)}, u32[]{:S(2)}) collective-permute-start(bf16[64,4096]{1,0:T(8,128)(2,1)S(1)} %collective-permute-done.2.refs_1_.refs_5_), channel_id=1, source_target_pairs={{0,4},{4,0},{8,12},{12,8},{1,5},{5,1},{9,13},{13,9},{2,6},{6,2},{1... | collective-permute-start | bytes 1572872 | tf_op jit(solution)/shard_map/ppermute | solution.py:691
  41.1 15.8 %copy-start.1 = (bf16[128,8192]{1,0:T(8,128)(2,1)S(1)}, bf16[128,8192]{1,0:T(8,128)(2,1)}, u32[]{:S(2)}) copy-start(bf16[128,8192]{1,0:T(8,128)(2,1)} %refs_1_.11) | copy-start | bytes 6291460
  41.1 35.0 %collective-permute-start.9 = (bf16[2,128,1792]{2,1,0:T(8,128)(2,1)}, bf16[2,128,1792]{2,1,0:T(8,128)(2,1)S(1)}, u32[]{:S(2)}, u32[]{:S(2)}) collective-permute-start(bf16[2,128,1792]{2,1,0:T(8,128)(2,1)} %fusion.1), channel_id=1, source_target_pairs={{0,8},{4,12},{8,0},{12,4},{1,9},{5,13},{9,1},{13,5},{2,10},{6,14},... | collective-permute-start | bytes 2752520 | tf_op jit(solution)/shard_map/ppermute | solution.py:694
  43.5 27.2 %collective-permute-start.10 = (bf16[2,768,128]{2,1,0:T(8,128)(2,1)S(1)}, bf16[2,768,128]{2,1,0:T(8,128)(2,1)S(1)}, u32[]{:S(2)}, u32[]{:S(2)}) collective-permute-start(bf16[2,768,128]{2,1,0:T(8,128)(2,1)S(1)} %pad_maximum_fusion.1), channel_id=1, source_target_pairs={{0,2},{1,3},{2,0},{3,1},{4,6},{5,7},{6,4},{7,5},{8,10},{9,11},{10,... | collective-permute-start | bytes 1179656 | tf_op jit(solution)/shard_map/ppermute | solution.py:697
  44.7 31.4 %collective-permute-start.8 = (bf16[64,4096]{1,0:T(8,128)(2,1)}, bf16[64,4096]{1,0:T(8,128)(2,1)}, u32[]{:S(2)}, u32[]{:S(2)}) collective-permute-start(bf16[64,4096]{1,0:T(8,128)(2,1)} %cut_tokens.3), channel_id=1, source_target_pairs={{0,8},{4,12},{8,0},{12,4},{1,9},{5,13},{9,1},{13,5},{2,10},{6,14},... | collective-permute-start | bytes 1572872 | tf_op jit(solution)/shard_map/ppermute | solution.py:694
  56.8 12.6 %collective-permute-start.11 = (bf16[2,128,1792]{2,1,0:T(8,128)(2,1)S(1)}, bf16[2,128,1792]{2,1,0:T(8,128)(2,1)S(1)}, u32[]{:S(2)}, u32[]{:S(2)}) collective-permute-start(bf16[2,128,1792]{2,1,0:T(8,128)(2,1)S(1)} %bitcast.62), channel_id=1, source_target_pairs={{0,4},{4,0},{8,12},{12,8},{1,5},{5,1},{9,13},{13,9},{2,6},{6,2},{1... | collective-permute-start | bytes 2752520 | tf_op jit(solution)/shard_map/ppermute | solution.py:691
  69.4 10.8 %copy-start.4 = (bf16[2,2,128,1792]{3,2,1,0:T(8,128)(2,1)}, bf16[2,2,128,1792]{3,2,1,0:T(8,128)(2,1)S(1)}, u32[]{:S(2)}) copy-start(bf16[2,2,128,1792]{3,2,1,0:T(8,128)(2,1)S(1)} %get-tuple-element.54) | copy-start | bytes 5505028
  76.1 3.8 %collective-permute-start.12 = (bf16[2,2,128,1792]{3,2,1,0:T(8,128)(2,1)S(1)}, bf16[2,2,128,1792]{3,2,1,0:T(8,128)(2,1)S(1)}, u32[]{:S(2)}, u32[]{:S(2)}) collective-permute-start(bf16[2,2,128,1792]{3,2,1,0:T(8,128)(2,1)S(1)} %get-tuple-element.59), channel_id=1, source_target_pairs={{0,4},{4,0},{8,12},{12,8},{1,5},{5,1},{9,13},{13,9},{2,6},{6,2},{1... | collective-permute-start | bytes 5505032 | tf_op jit(solution)/shard_map/ppermute | solution.py:691
  79.9 1.3 copy-start.9
  82.2 8.7 %collective-permute-start.14 = (bf16[128,1792]{1,0:T(8,128)(2,1)}, bf16[128,1792]{1,0:T(8,128)(2,1)}, u32[]{:S(2)}, u32[]{:S(2)}) collective-permute-start(bf16[128,1792]{1,0:T(8,128)(2,1)} %fusion.5.mine_ref), channel_id=1, source_target_pairs={{0,4},{4,0},{8,12},{12,8},{1,5},{5,1},{9,13},{13,9},{2,6},{6,2},{1... | collective-permute-start | bytes 1376264 | tf_op jit(solution)/shard_map/ppermute | solution.py:691
  83.0 29.0 %collective-permute-start.15 = (bf16[64,4096]{1,0:T(8,128)(2,1)}, bf16[64,4096]{1,0:T(8,128)(2,1)}, u32[]{:S(2)}, u32[]{:S(2)}) collective-permute-start(bf16[64,4096]{1,0:T(8,128)(2,1)} %collective-permute-done.8.refs_4_.refs_8_), channel_id=1, source_target_pairs={{0,4},{4,0},{8,12},{12,8},{1,5},{5,1},{9,13},{13,9},{2,6},{6,2},{1... | collective-permute-start | bytes 1572872 | tf_op jit(solution)/shard_map/ppermute | solution.py:691
  84.3 23.5 %collective-permute-start.17 = (bf16[2,128,1792]{2,1,0:T(8,128)(2,1)}, bf16[2,128,1792]{2,1,0:T(8,128)(2,1)}, u32[]{:S(2)}, u32[]{:S(2)}) collective-permute-start(bf16[2,128,1792]{2,1,0:T(8,128)(2,1)} %fusion), channel_id=1, source_target_pairs={{0,8},{4,12},{8,0},{12,4},{1,9},{5,13},{9,1},{13,5},{2,10},{6,14},... | collective-permute-start | bytes 2752520 | tf_op jit(solution)/shard_map/ppermute | solution.py:694
  86.0 31.7 %collective-permute-start.20 = (bf16[128,1792]{1,0:T(8,128)(2,1)}, bf16[128,1792]{1,0:T(8,128)(2,1)}, u32[]{:S(2)}, u32[]{:S(2)}) collective-permute-start(bf16[128,1792]{1,0:T(8,128)(2,1)} %fusion.5.mine_ref), channel_id=1, source_target_pairs={{0,8},{4,12},{8,0},{12,4},{1,9},{5,13},{9,1},{13,5},{2,10},{6,14},... | collective-permute-start | bytes 1376264 | tf_op jit(solution)/shard_map/ppermute | solution.py:694
  86.3 21.5 %collective-permute-start.13 = (bf16[64,4096]{1,0:T(8,128)(2,1)}, bf16[64,4096]{1,0:T(8,128)(2,1)}, u32[]{:S(2)}, u32[]{:S(2)}) collective-permute-start(bf16[64,4096]{1,0:T(8,128)(2,1)} %collective-permute-done.8.refs_4_.refs_8_), channel_id=1, source_target_pairs={{0,1},{1,0},{2,3},{3,2},{4,5},{5,4},{6,7},{7,6},{8,9},{9,8},{10,11... | collective-permute-start | bytes 1572872 | tf_op jit(solution)/shard_map/ppermute | solution.py:697
  90.9 7.5 %copy-start.2 = (bf16[8,256,256]{2,1,0:T(8,128)(2,1)S(1)}, bf16[8,256,256]{2,1,0:T(8,128)(2,1)}, u32[]{:S(2)}) copy-start(bf16[8,256,256]{2,1,0:T(8,128)(2,1)} %spread_left.1.refs_6_.refs_10_.refs_9_) | copy-start | bytes 3145732
  90.9 7.5 %copy-start.3 = (bf16[4,768,128]{2,1,0:T(8,128)(2,1)S(1)}, bf16[4,768,128]{2,1,0:T(8,128)(2,1)}, u32[]{:S(2)}) copy-start(bf16[4,768,128]{2,1,0:T(8,128)(2,1)} %pad_maximum_fusion.rows_ref.refs_4_.refs_5_.refs_8_.refs_9_) | copy-start | bytes 2359300
  90.9 7.5 %copy-start.8 = (s32[4]{0:T(128)S(1)}, s32[4]{0:T(128)}, u32[]{:S(2)}) copy-start(s32[4]{0:T(128)} %pad_add_fusion.idx_ref) | copy-start | bytes 52
  98.5 9.4 %copy-start.5 = (bf16[2,2,128,1792]{3,2,1,0:T(8,128)(2,1)S(1)}, bf16[2,2,128,1792]{3,2,1,0:T(8,128)(2,1)}, u32[]{:S(2)}) copy-start(bf16[2,2,128,1792]{3,2,1,0:T(8,128)(2,1)} %copy-done.4) | copy-start | bytes 5505028
  98.5 9.4 %copy-start.10 = (bf16[2,2,128,1792]{3,2,1,0:T(8,128)(2,1)S(1)}, bf16[2,2,128,1792]{3,2,1,0:T(8,128)(2,1)}, u32[]{:S(2)}) copy-start(bf16[2,2,128,1792]{3,2,1,0:T(8,128)(2,1)} %copy-done.9) | copy-start | bytes 5505028
  107.8 4.1 %collective-permute-start.16 = (bf16[64,4096]{1,0:T(8,128)(2,1)}, bf16[64,4096]{1,0:T(8,128)(2,1)S(1)}, u32[]{:S(2)}, u32[]{:S(2)}) collective-permute-start(bf16[64,4096]{1,0:T(8,128)(2,1)} %collective-permute-done.13.refs_5_.refs_9_), channel_id=1, source_target_pairs={{0,4},{4,0},{8,12},{12,8},{1,5},{5,1},{9,13},{13,9},{2,6},{6,2},{1... | collective-permute-start | bytes 1572872 | tf_op jit(solution)/shard_map/ppermute | solution.py:691
  109.6 8.2 %collective-permute-start.19 = (bf16[128,1792]{1,0:T(8,128)(2,1)S(1)}, bf16[128,1792]{1,0:T(8,128)(2,1)S(1)}, u32[]{:S(2)}, u32[]{:S(2)}) collective-permute-start(bf16[128,1792]{1,0:T(8,128)(2,1)S(1)} %fusion.3.mine_ref), channel_id=1, source_target_pairs={{0,4},{4,0},{8,12},{12,8},{1,5},{5,1},{9,13},{13,9},{2,6},{6,2},{1... | collective-permute-start | bytes 1376264 | tf_op jit(solution)/shard_map/ppermute | solution.py:691
  110.2 16.4 %collective-permute-start.18 = (bf16[128,1792]{1,0:T(8,128)(2,1)S(1)}, bf16[128,1792]{1,0:T(8,128)(2,1)S(1)}, u32[]{:S(2)}, u32[]{:S(2)}) collective-permute-start(bf16[128,1792]{1,0:T(8,128)(2,1)S(1)} %fusion.3.mine_ref), channel_id=1, source_target_pairs={{0,8},{4,12},{8,0},{12,4},{1,9},{5,13},{9,1},{13,5},{2,10},{6,14},... | collective-permute-start | bytes 1376264 | tf_op jit(solution)/shard_map/ppermute | solution.py:694
  117.8 8.8 %collective-permute-start.22 = (bf16[128,1792]{1,0:T(8,128)(2,1)}, bf16[128,1792]{1,0:T(8,128)(2,1)S(1)}, u32[]{:S(2)}, u32[]{:S(2)}) collective-permute-start(bf16[128,1792]{1,0:T(8,128)(2,1)} %collective-permute-done.20.refs_1_), channel_id=1, source_target_pairs={{0,4},{4,0},{8,12},{12,8},{1,5},{5,1},{9,13},{13,9},{2,6},{6,2},{1... | collective-permute-start | bytes 1376264 | tf_op jit(solution)/shard_map/ppermute | solution.py:691
  126.6 1.8 %collective-permute-start.21 = (bf16[128,1792]{1,0:T(8,128)(2,1)S(1)}, bf16[128,1792]{1,0:T(8,128)(2,1)S(1)}, u32[]{:S(2)}, u32[]{:S(2)}) collective-permute-start(bf16[128,1792]{1,0:T(8,128)(2,1)S(1)} %collective-permute-done.18.refs_0_), channel_id=1, source_target_pairs={{0,4},{4,0},{8,12},{12,8},{1,5},{5,1},{9,13},{13,9},{2,6},{6,2},{1... | collective-permute-start | bytes 1376264 | tf_op jit(solution)/shard_map/ppermute | solution.py:691
  139.7 6.0 %collective-permute-start.23 = (bf16[2,256,128]{2,1,0:T(8,128)(2,1)S(1)}, bf16[2,256,128]{2,1,0:T(8,128)(2,1)S(1)}, u32[]{:S(2)}, u32[]{:S(2)}) collective-permute-start(bf16[2,256,128]{2,1,0:T(8,128)(2,1)S(1)} %slice.51), channel_id=1, source_target_pairs={{0,1},{1,0},{2,3},{3,2},{4,5},{5,4},{6,7},{7,6},{8,9},{9,8},{10,11... | collective-permute-start | bytes 393224 | tf_op jit(solution)/shard_map/ppermute | solution.py:697
  145.2 9.5 %collective-permute-start.24 = (bf16[2,512,128]{2,1,0:T(8,128)(2,1)S(1)}, bf16[2,512,128]{2,1,0:T(8,128)(2,1)S(1)}, u32[]{:S(2)}, u32[]{:S(2)}) collective-permute-start(bf16[2,512,128]{2,1,0:T(8,128)(2,1)S(1)} %right_grads.2), channel_id=1, source_target_pairs={{0,1},{1,0},{2,3},{3,2},{4,5},{5,4},{6,7},{7,6},{8,9},{9,8},{10,11... | collective-permute-start | bytes 786440 | tf_op jit(solution)/shard_map/ppermute | solution.py:697
  145.8 14.6 %collective-permute-start.27 = (bf16[256,128]{1,0:T(8,128)(2,1)S(1)}, bf16[256,128]{1,0:T(8,128)(2,1)S(1)}, u32[]{:S(2)}, u32[]{:S(2)}) collective-permute-start(bf16[256,128]{1,0:T(8,128)(2,1)S(1)} %slice_bitcast_fusion.6), channel_id=1, source_target_pairs={{0,2},{1,3},{2,0},{3,1},{4,6},{5,7},{6,4},{7,5},{8,10},{9,11},{10,... | collective-permute-start | bytes 196616 | tf_op jit(solution)/shard_map/ppermute | solution.py:697
  154.9 6.5 %collective-permute-start.25 = (bf16[512,128]{1,0:T(8,128)(2,1)S(1)}, bf16[512,128]{1,0:T(8,128)(2,1)S(1)}, u32[]{:S(2)}, u32[]{:S(2)}) collective-permute-start(bf16[512,128]{1,0:T(8,128)(2,1)S(1)} %get-tuple-element.78), channel_id=1, source_target_pairs={{0,0},{1,4},{2,8},{3,12},{4,1},{5,5},{6,9},{7,13},{8,2},{9,6},{10,... | collective-permute-start | bytes 393224 | tf_op jit(solution)/shard_map/ppermute | solution.py:704
  155.5 15.1 %collective-permute-start.26 = (bf16[512,128]{1,0:T(8,128)(2,1)S(1)}, bf16[512,128]{1,0:T(8,128)(2,1)S(1)}, u32[]{:S(2)}, u32[]{:S(2)}) collective-permute-start(bf16[512,128]{1,0:T(8,128)(2,1)S(1)} %get-tuple-element.79), channel_id=1, source_target_pairs={{0,8},{1,12},{2,0},{3,4},{4,9},{5,13},{6,1},{7,5},{8,10},{9,14},{1... | collective-permute-start | bytes 393224 | tf_op jit(solution)/shard_map/ppermute | solution.py:704

commit v11 on v10

--- a/solution.py
+++ b/solution.py
@@ -302,31 +302,41 @@
     return grad_right, grad_left
 
 
-def cut_kernel(count, idx_ref, *refs):
-    for in_ref, out_ref in zip(refs[:count], refs[count:]):
-        out_ref[...] = in_ref[...]
-
-
-def cut_tokens(tokens, places, cost=SMALL):
-    block = (tokens.shape[0] // 2, tokens.shape[1] // 2)
-    shape = jax.ShapeDtypeStruct(block, BF16)
-    count = len(places)
-    flat = [index for place in places for index in place]
+def cut_kernel(idx_ref, in_ref, out_ref):
+    out_ref[...] = in_ref[...]
+
+
+def cut_tokens(tokens, rows, row, column, cost=SMALL):
+    width = tokens.shape[1] // 2
+    steps = 4
     return pl.pallas_call(
-        functools.partial(cut_kernel, count),
+        cut_kernel,
         grid_spec=pltpu.PrefetchScalarGridSpec(
             num_scalar_prefetch=1,
-            grid=(1,),
-            in_specs=[
-                pl.BlockSpec(block, lambda n, s, k=k: (s[2 * k], s[2 * k + 1]))
-                for k in range(count)
-            ],
-            out_specs=[pl.BlockSpec(block, lambda n, s: (0, 0))] * count,
-        ),
-        out_shape=[shape] * count,
+            grid=(steps,),
+            in_specs=[pl.BlockSpec((rows, width // steps), lambda n, s: (s[0], s[1] * steps + n))],
+            out_specs=pl.BlockSpec((rows, width // steps), lambda n, s: (0, n)),
+        ),
+        out_shape=jax.ShapeDtypeStruct((rows, width), BF16),
         cost_estimate=cost,
         name="cut_tokens",
-    )(jnp.stack(flat).astype(jnp.int32), *[tokens] * count)
+    )(jnp.stack([row, column]).astype(jnp.int32), tokens)
+
+
+def join_kernel(mine_ref, more_ref, out_ref):
+    count = mine_ref.shape[0]
+    out_ref[:count] = mine_ref[...]
+    out_ref[count:] = more_ref[...]
+
+
+def join(mine, more):
+    shape = (2 * mine.shape[0],) + mine.shape[1:]
+    return pl.pallas_call(
+        join_kernel,
+        out_shape=jax.ShapeDtypeStruct(shape, mine.dtype),
+        cost_estimate=LARGE,
+        name="join",
+    )(mine, more)
 
 
 def products_kernel(sets, idx_ref, *refs):
@@ -379,7 +389,7 @@
 
 
 def whole_spec(array):
-    return pl.BlockSpec(array.shape, lambda n, s: (0,) * array.ndim)
+    return pl.BlockSpec(array.shape, lambda n, s: (0,) * len(array.shape))
 
 
 def target_kernel(sign, idx_ref, mine_ref, near_ref, weight_ref, *refs):
@@ -392,14 +402,15 @@
 def target_part(sign, terms, mine, near, weight, chip):
     rows, width = mine.shape
     outs = weight.shape[1]
-    block = pl.BlockSpec((2 * rows, BLK), lambda n, s: (0, n))
+    wide = 2 * BLK if outs % (2 * BLK) == 0 else BLK
+    block = pl.BlockSpec((2 * rows, wide), lambda n, s: (0, n))
     return pl.pallas_call(
         functools.partial(target_kernel, sign),
         grid_spec=pltpu.PrefetchScalarGridSpec(
             num_scalar_prefetch=1,
-            grid=(outs // BLK,),
+            grid=(outs // wide,),
             in_specs=[whole_spec(mine), whole_spec(near)]
-            + [pl.BlockSpec((width, BLK), lambda n, s: (s[0], n))]
+            + [pl.BlockSpec((width, wide), lambda n, s: (s[0], n))]
             + [block] * len(terms),
             out_specs=block,
         ),
@@ -419,7 +430,7 @@
     return lax.rem(chip + step // per_chip, 2) * per_chip + lax.rem(step, per_chip)
 
 
-def spread_kernel(idx_ref, rows_ref, out_ref, scratch):
+def spread_left(z, rows_ref, out_ref, scratch):
     groups = out_ref.shape[0]
     parts, _, size = rows_ref.shape
     blocks = size // 2
@@ -432,7 +443,7 @@
         for pair in range(fold // 2):
             row = begin + (g * (fold // 2) + pair) * share
             picked = [
-                rows_ref[idx_ref[3] ^ owner, row : row + share, :] for owner in range(parts)
+                rows_ref[z ^ owner, row : row + share, :] for owner in range(parts)
             ]
             turned = jnp.concatenate(picked + picked, axis=0).astype(F32).T
             for a in range(2):
@@ -445,27 +456,16 @@
         out_ref[g] = scratch[...].astype(BF16)
 
 
-def spread_left(scalars, rows, groups):
-    return pl.pallas_call(
-        spread_kernel,
-        grid_spec=pltpu.PrefetchScalarGridSpec(
-            num_scalar_prefetch=1,
-            grid=(1,),
-            in_specs=[whole_spec(rows)],
-            out_specs=pl.BlockSpec((groups, BLK, BLK), lambda n, s: (0, 0, 0)),
-            scratch_shapes=[pltpu.VMEM((BLK, BLK), F32)],
-        ),
-        out_shape=jax.ShapeDtypeStruct((groups, BLK, BLK), BF16),
-        cost_estimate=SMALL,
-        name="spread_left",
-    )(scalars, rows)
-
-
 def student_kernel(steps, late, tensor_count, idx_ref, *refs):
     tokens, refs = refs[: 8 if late else 4], refs[8 if late else 4 :]
-    rights, left_ref, targets = refs[:2], refs[2], refs[3:-3]
-    mixed_ref, student_ref, spread = refs[-3:]
+    rights, left_ref, refs = refs[:2], refs[2], refs[3:]
     step = pl.program_id(0)
+    if late:
+        target_ref, mixed_ref, student_ref, spread = refs
+    else:
+        mixed_ref, student_ref, diag_ref, spread, scratch = refs
+        rows_ref, left_ref = left_ref, diag_ref
+        pl.when(step == 0)(lambda: spread_left(idx_ref[3], rows_ref, diag_ref, scratch))
     pair = natural(step, idx_ref[2], steps // 2)
     groups = left_ref.shape[0]
     size = spread.shape[2]
@@ -503,24 +503,30 @@
                 mixed_ref[g], left_ref[g], TN, preferred_element_type=F32
             )
             student = student * (1.0 / tensor_count)
-            student_ref[:, span] = sum((-ref[:, span] for ref in targets), student)
+            student_ref[:, span] = student - target_ref[:, span] if late else student
 
 
 def token_specs(half, width, chunk, late):
-    if not late:
+    def specs(place):
         return [
-            pl.BlockSpec((half, width), lambda n, s, p=p: (s[p % 2], chunk(n, s)))
+            pl.BlockSpec((half, width), lambda n, s, p=p: (s[p % 2], place(n, s)))
             for p in range(4)
         ]
-    inner = pl.BlockSpec((half, width), lambda n, s: (0, lax.rem(chunk(n, s), 2)))
-    return [inner] * 8
-
-
-def student_part(tokens, late, scalars, factors, left_diag, targets, pairs, tensor_count):
-    parts, _, size = factors.shape
-    half = tokens[0].shape[0] // (1 if late else 2)
-    groups = left_diag.shape[0]
-    blocks = groups * BLK // pairs
+
+    if not late:
+        return specs(chunk)
+
+    def inner(n, s):
+        return lax.rem(chunk(n, s), 2)
+
+    return specs(inner) + [pl.BlockSpec((half, width), lambda n, s: (0, inner(n, s)))] * 4
+
+
+def student_part(tokens, scalars, factors, pairs, tensor_count, late=()):
+    size = factors.shape[2]
+    half = tokens[0].shape[0] // 2
+    blocks = size // 2
+    groups = pairs * blocks // BLK
     steps = blocks // (2 * WIDE)
 
     def chunk(n, s):
@@ -528,32 +534,36 @@
 
     def right_spec(half):
         return pl.BlockSpec(
-            (1, WIDE * pairs, size),
-            lambda n, s: (s[3] ^ chunk(n, s), half, 0),
+            (1, WIDE * pairs, size), lambda n, s: (s[3] ^ chunk(n, s), half, 0)
         )
 
+    diag = (groups, BLK, BLK)
+    shapes = [
+        jax.ShapeDtypeStruct((groups, BLK, 4 * half), BF16),
+        jax.ShapeDtypeStruct((4 * half, groups * BLK), F32),
+    ]
+    scratch = [pltpu.VMEM((WIDE, pairs * WIDE, size), F32)]
+    extra = list(late)
+    if not late:
+        shapes.append(jax.ShapeDtypeStruct(diag, BF16))
+        scratch.append(pltpu.VMEM((BLK, BLK), F32))
+        extra = [factors]
     return pl.pallas_call(
-        functools.partial(student_kernel, steps, late, tensor_count),
+        functools.partial(student_kernel, steps, bool(late), tensor_count),
         grid_spec=pltpu.PrefetchScalarGridSpec(
             num_scalar_prefetch=1,
             grid=(steps,),
-            in_specs=token_specs(half, 2 * WIDE * size, chunk, late)
-            + [right_spec(0), right_spec(1), whole_spec(left_diag)]
-            + [whole_spec(target) for target in targets],
-            out_specs=[
-                pl.BlockSpec((groups, BLK, 4 * half), lambda n, s: (0, 0, 0)),
-                pl.BlockSpec((4 * half, groups * BLK), lambda n, s: (0, 0)),
-            ],
-            scratch_shapes=[pltpu.VMEM((WIDE, pairs * WIDE, size), F32)],
-        ),
-        out_shape=[
-            jax.ShapeDtypeStruct((groups, BLK, 4 * half), BF16),
-            jax.ShapeDtypeStruct((4 * half, groups * BLK), F32),
-        ],
+            in_specs=token_specs(half, 2 * WIDE * size, chunk, bool(late))
+            + [right_spec(0), right_spec(1)]
+            + [whole_spec(array) for array in extra],
+            out_specs=[whole_spec(shape) for shape in shapes],
+            scratch_shapes=scratch,
+        ),
+        out_shape=shapes,
         compiler_params=pltpu.CompilerParams(vmem_limit_bytes=40 * 2**20),
         cost_estimate=LARGE,
         name="student_part",
-    )(scalars, *tokens, factors, factors, left_diag, *targets)
+    )(scalars, *tokens, factors, factors, *extra)
 
 
 def place(z, owner):
@@ -654,7 +664,7 @@
 
 
 def right_grads(back, own, late, scalars, pairs, bit, size, cost):
-    half = late[0].shape[0]
+    half = late[0].shape[0] // 2
     rows, count = back.shape[1:]
 
     def owner(n, s):
@@ -710,8 +720,8 @@
         return sum(term.astype(F32) for term in terms)
 
     near_tokens = swap(tokens)
-    first = cut_tokens(tokens, [(odd, 1 - chip), (1 - odd, 1 - chip)])
-    arrived = [across(value) for value in first]
+    first = cut_tokens(tokens, rows, jnp.int32(0), 1 - chip)
+    arrived = across(first)
     base = jnp.stack([odd, 1 - odd])
     mine_block = lax.div(part, BLK) * chip
     other_block = lax.div(part, BLK) * (1 - chip)
@@ -721,30 +731,30 @@
 
     own_pieces = [(t, row, 2) for t in (tokens, near_tokens) for row in (0, 1)]
     mine, other = products(
-        own_pieces, after(scalars(other_block), *first), gate_weight, up_weight, 0, part
+        own_pieces, after(scalars(other_block), first), gate_weight, up_weight, 0, part
     )
 
     pairs, blocks = left_factor.shape[0], left_factor.shape[2]
     left_rows = left_factor.reshape(pairs // 2, 2, -1, blocks).transpose(0, 2, 1, 3)
     turned = turn(after(right_factor, mine), 0)
-    (rest,) = cut_tokens(after(tokens, mine), [(odd, chip)], LARGE)
+    rest = cut_tokens(after(tokens, mine), rows // 2, odd, chip, LARGE)
     factors = jnp.concatenate(
         [after(turned, rest).reshape(-1, LANES), left_rows.reshape(-1, LANES)], axis=0
     )[None]
     more = along(factors, 1)
     sums = add(mine[0], swap(other[0])).astype(BF16)
-    arrived = [after(arrived[0], rest), after(arrived[1], more, rest, sums)]
+    arrived = after(arrived, more, rest, sums)
     got_early = across(sums)
     late_first = across(after(rest, sums))
-    factors = jnp.concatenate([factors, more], axis=0)
-    more = along(after(factors, arrived[1]), 2)
+    factors = join(after(factors, arrived), more)
+    more = along(factors, 2)
 
     order = jnp.concatenate([base, jnp.stack([chip, z])]).astype(jnp.int32)
     own = [tokens, tokens, near_tokens, near_tokens]
-    near_arrived = [swap(value) for value in arrived]
-    late = arrived + near_arrived
-    late_pieces = [(t, None, 3) for t in late]
-    late_order = after(scalars(other_block), sums)
+    near_arrived = swap(arrived)
+    late = [arrived, arrived, near_arrived, near_arrived]
+    late_pieces = [(t, row, 3) for t in (arrived, near_arrived) for row in (0, 1)]
+    late_order = after(scalars(other_block), factors)
     mine, other = products(late_pieces, late_order, gate_weight, up_weight, 0, part)
     near = swap(other[0])
     mine_order = after(scalars(mine_block), mine)
@@ -763,33 +773,23 @@
     hidden1 = activate(1, got_early)
     got1 = across(hidden1)
     near1 = swap(hidden1)
-    left_diag = spread_left(order, after(factors, hidden1), pairs * blocks // BLK)
     late_partner = along(after(late_first, hidden1), 1)
-    target1 = target_part(1.0, [], hidden1, near1, down_weight, chip)
-    mixed0, rest0 = student_part(
-        [after(tokens, target1)] + own[1:],
-        False,
-        order,
-        factors,
-        left_diag,
-        [],
-        pairs,
-        tensor_count,
-    )
-    hidden0 = activate(0, after(got, mixed0))
+    mixed0, rest0, left_diag = student_part(
+        [after(tokens, hidden1, sums)] + own[1:], order, factors, pairs, tensor_count
+    )
+    target1 = target_part(1.0, [], hidden1, after(near1, mixed0), down_weight, chip)
+    hidden0 = activate(0, after(got, target1))
     got0 = across(hidden0)
     near0 = swap(hidden0)
     late_partner = after(late_partner, mixed0)
     late += [late_first, late_partner, swap(late_first), swap(late_partner)]
     mixed1, rest1 = student_part(
         [after(late[0], hidden0)] + late[1:],
-        True,
         order,
         factors,
-        left_diag,
-        [target1],
         pairs,
         tensor_count,
+        (left_diag, target1),
     )
     near0 = after(near0, mixed1)
     rest0 = target_part(-1.0, [rest0], hidden0, near0, down_weight, chip)

time: 173 us -> 165 us (0.954)
  waiting for transfers between devices: 39.3 us -> 48.2 us
  starting transfers between devices: 31.6 us -> 24.3 us
  Pallas kernels: 86.8 us -> 81.3 us
  other arithmetic: 9.43 us -> 4.73 us
    ppermute x7 -> x6, waiting for transfers between devices: 17.6 us -> 25.7 us  [across(): return lax.ppermute(value, 'fsdp', [(i, i ^ 2) for i in range(fsdp_count)])]
    ppermute x7 -> x6, starting transfers between devices: 10.7 us -> 5.47 us  [across(): return lax.ppermute(value, 'fsdp', [(i, i ^ 2) for i in range(fsdp_count)])]
    pallas_call x2, Pallas kernels: 14.7 us -> 10.7 us  [target_part(): pl.pallas_call(functools.partial(target_kernel, sign), grid_spec=pltpu.Pr...]
    ppermute x6, starting transfers between devices: 9.45 us -> 12.9 us  [along(): lax.ppermute(value, 'tensor', [(i, i ^ bit) for i in range(tensor_count)])]
    ppermute x12 -> x11, starting transfers between devices: 5.24 us -> 2.19 us  [swap(): return lax.ppermute(value, 'fsdp', [(i, i ^ 1) for i in range(fsdp_count)])]
    ppermute x3, starting transfers between devices: 6.2 us -> 3.78 us  [turn(): return lax.ppermute(value, both_axes, perm)]
    unnamed x26 -> x34, local copies, waits for them, and re-layouts: 1.94 us -> 3.48 us
    ppermute x12 -> x11, waiting for transfers between devices: 5.62 us -> 5.08 us  [swap(): return lax.ppermute(value, 'fsdp', [(i, i ^ 1) for i in range(fsdp_count)])]
  transfers between devices with their start and end apart: 28 -> 26, of which waited for: 9 -> 12; matrix products, arithmetic and copies ran while one was open for 5% -> 3% of each run, Pallas kernels for 44% -> 43%
where the time goes in v11:
time: 165 us; the launch traced here: 164 us
  Pallas kernels  81.3 us (49%)
  waiting for transfers between devices  48.2 us (29%)
  starting transfers between devices  24.3 us (15%)
  local copies, waits for them, and re-layouts  4.81 us (3%)
  other arithmetic  4.73 us (3%)
    pallas_call x3, Pallas kernels, products(): pl.pallas_call(functools.partial(products_kernel, sets), grid_spec=pltpu....  33.1 us
    ppermute x6, waiting for transfers between devices, across(): return lax.ppermute(value, 'fsdp', [(i, i ^ 2) for i in range(fsdp_count)])  25.7 us
    ppermute x6, starting transfers between devices, along(): lax.ppermute(value, 'tensor', [(i, i ^ bit) for i in range(tensor_count)])  12.9 us
    pallas_call x1, Pallas kernels, left_grads(): pl.pallas_call(functools.partial(left_kernel, chunks, scale), grid_spec=p...  11.1 us
    pallas_call x2, Pallas kernels, target_part(): pl.pallas_call(functools.partial(target_kernel, sign), grid_spec=pltpu.Pr...  10.7 us
    ppermute x3, waiting for transfers between devices, turn(): return lax.ppermute(value, both_axes, perm)  10.5 us
    pallas_call x2, Pallas kernels, student_part(): pl.pallas_call(functools.partial(student_kernel, steps, bool(late), tenso...  9.8 us
    pallas_call x2, Pallas kernels, cut_tokens(): pl.pallas_call(cut_kernel, grid_spec=pltpu.PrefetchScalarGridSpec(num_sca...  8.09 us
  transfers between devices with their start and end apart: 26, of which 12 were waited for; matrix products, arithmetic and copies ran while one was open for 3% of the time, Pallas kernels for 43%

profile of v11, /device:TPU:0, one launch (start us, length us, event | category | flops | bytes accessed | tf_op | source)
XLA Modules:
  0.0 164.3 jit_solution(16166105795238039669)
XLA Ops:
  0.6 0.5 collective-permute-start
  1.2 0.6 pad_add_fusion.1.idx_ref
  1.7 4.2 %cut_tokens.2 = bf16[128,4096]{1,0:T(8,128)(2,1)} custom-call(s32[2]{0:T(128)} %pad_add_fusion.1.idx_ref, bf16[128,8192]{1,0:T(8,128)(2,1)} %refs_1_.9), custom_call_target="tpu_custom_call" | custom-call | flops 1 | bytes 1 | tf_op jit(solution)/shard_map/cut_tokens/pallas_call | solution.py:312
  6.0 2.5 %collective-permute-start.1 = (bf16[128,4096]{1,0:T(8,128)(2,1)}, bf16[128,4096]{1,0:T(8,128)(2,1)S(1)}, u32[]{:S(2)}, u32[]{:S(2)}) collective-permute-start(bf16[128,4096]{1,0:T(8,128)(2,1)} %cut_tokens.2), channel_id=1, source_target_pairs={{0,8},{4,12},{8,0},{12,4},{1,9},{5,13},{9,1},{13,5},{2,10},{6,14},... | collective-permute-start | bytes 3145736 | tf_op jit(solution)/shard_map/ppermute | solution.py:704
  8.5 0.1 concatenate.21.idx_ref
  8.6 0.1 copy.11
  8.7 0.1 reshape.38
  8.8 0.6 pad_add_fusion.2.idx_ref
  9.4 10.8 %gate_up_products.3 = (bf16[1,2,128,1792]{3,2,1,0:T(8,128)(2,1)S(1)}, bf16[1,2,128,1792]{3,2,1,0:T(8,128)(2,1)}) custom-call(s32[5]{0:T(128)S(1)} %concatenate.21.idx_ref, bf16[128,8192]{1,0:T(8,128)(2,1)S(1)} %copy-done, bf16[128,8192]{1,0:T(8,128)(2,1)S(1)} %copy-done, bf16[128,8192]{1,0:T(8,128)(2,1)} %collective-permute-done.refs_2_.refs_3_, ...), custom_call_target="tpu_custom_call" | custom-call | flops 1 | bytes 1 | tf_op jit(solution)/shard_map/gate_up_products/pallas_call | solution.py:369
  20.2 1.0 copy-done.4
  21.1 0.2 collective-permute-start.4
  21.3 0.8 collective-permute-start.2
  22.1 3.9 %cut_tokens.3 = bf16[64,4096]{1,0:T(8,128)(2,1)} custom-call(s32[2]{0:T(128)} %pad_add_fusion.2.idx_ref, bf16[128,8192]{1,0:T(8,128)(2,1)} %refs_1_.9), custom_call_target="tpu_custom_call" | custom-call | flops 10000000000 | bytes 10000000 | tf_op jit(solution)/shard_map/cut_tokens/pallas_call | solution.py:312
  26.0 3.4 %collective-permute-start.3 = (bf16[1,768,128]{2,1,0:T(8,128)(2,1)S(1)}, bf16[1,768,128]{2,1,0:T(8,128)(2,1)S(1)}, u32[]{:S(2)}, u32[]{:S(2)}) collective-permute-start(bf16[1,768,128]{2,1,0:T(8,128)(2,1)S(1)} %maximum_bitcast_fusion.mine_ref), channel_id=1, source_target_pairs={{0,1},{1,0},{2,3},{3,2},{4,5},{5,4},{6,7},{7,6},{8,9},{9,8},{10,11... | collective-permute-start | bytes 589832 | tf_op jit(solution)/shard_map/ppermute | solution.py:707
  29.4 1.2 fusion.1
  30.6 4.1 %collective-permute-done.1.refs_0_.refs_1_.refs_4_.refs_5_ = bf16[128,4096]{1,0:T(8,128)(2,1)S(1)} collective-permute-done((bf16[128,4096]{1,0:T(8,128)(2,1)}, bf16[128,4096]{1,0:T(8,128)(2,1)S(1)}, u32[]{:S(2)}, u32[]{:S(2)}) %collective-permute-start.1) | collective-permute-done | bytes 1048608 | tf_op jit(solution)/shard_map/ppermute | solution.py:704
  34.7 1.4 collective-permute-done.3.more_ref
  36.0 0.1 collective-permute-start.5
  36.2 0.1 concatenate.23.idx_ref
  36.2 0.5 copy-done.15
  36.7 1.8 %join.1 = bf16[2,768,128]{2,1,0:T(8,128)(2,1)} custom-call(bf16[1,768,128]{2,1,0:T(8,128)(2,1)} %copy-done.13, bf16[1,768,128]{2,1,0:T(8,128)(2,1)} %copy-done.15), custom_call_target="tpu_custom_call" | custom-call | flops 10000000000 | bytes 10000000 | tf_op jit(solution)/shard_map/join/pallas_call | solution.py:334
  38.5 5.0 %collective-permute-start.8 = (bf16[2,768,128]{2,1,0:T(8,128)(2,1)}, bf16[2,768,128]{2,1,0:T(8,128)(2,1)S(1)}, u32[]{:S(2)}, u32[]{:S(2)}) collective-permute-start(bf16[2,768,128]{2,1,0:T(8,128)(2,1)} %join.1), channel_id=1, source_target_pairs={{0,2},{1,3},{2,0},{3,1},{4,6},{5,7},{6,4},{7,5},{8,10},{9,11},{10,... | collective-permute-start | bytes 1179656 | tf_op jit(solution)/shard_map/ppermute | solution.py:707
  43.6 2.0 %collective-permute-start.6 = (bf16[64,4096]{1,0:T(8,128)(2,1)}, bf16[64,4096]{1,0:T(8,128)(2,1)S(1)}, u32[]{:S(2)}, u32[]{:S(2)}) collective-permute-start(bf16[64,4096]{1,0:T(8,128)(2,1)} %cut_tokens.3), channel_id=1, source_target_pairs={{0,8},{4,12},{8,0},{12,4},{1,9},{5,13},{9,1},{13,5},{2,10},{6,14},... | collective-permute-start | bytes 1572872 | tf_op jit(solution)/shard_map/ppermute | solution.py:704
  45.6 10.0 %gate_up_products.4 = (bf16[1,2,128,1792]{3,2,1,0:T(8,128)(2,1)S(1)}, bf16[1,2,128,1792]{3,2,1,0:T(8,128)(2,1)S(1)}) custom-call(s32[5]{0:T(128)S(1)} %concatenate.21.idx_ref, bf16[128,4096]{1,0:T(8,128)(2,1)S(1)} %collective-permute-done.1.refs_0_.refs_1_.refs_4_.refs_5_, bf16[128,4096]{1,0:T(8,128)(2,1)S(1)} %collective-permute-done.1.refs_0_.refs_1_.refs_4_.refs_5_, ...), custom_call_target="tpu_custom_call" | custom-call | flops 1 | bytes 1 | tf_op jit(solution)/shard_map/gate_up_products/pallas_call | solution.py:369
  55.7 12.4 %gate_up_products.5 = (bf16[2,2,128,1792]{3,2,1,0:T(8,128)(2,1)S(1)}, bf16[2,2,128,1792]{3,2,1,0:T(8,128)(2,1)S(1)}) custom-call(s32[5]{0:T(128)S(1)} %concatenate.23.idx_ref, bf16[128,8192]{1,0:T(8,128)(2,1)S(1)} %copy-done.1, bf16[128,8192]{1,0:T(8,128)(2,1)S(1)} %copy-done.1, bf16[128,8192]{1,0:T(8,128)(2,1)} %collective-permute-done.refs_2_.refs_3_, ...), custom_call_target="tpu_custom_call" | custom-call | flops 10000000000 | bytes 10000000 | tf_op jit(solution)/shard_map/gate_up_products/pallas_call | solution.py:369
  68.1 0.2 fusion
  68.3 9.2 %collective-permute-done.6.refs_4_.refs_8_ = bf16[64,4096]{1,0:T(8,128)(2,1)S(1)} collective-permute-done((bf16[64,4096]{1,0:T(8,128)(2,1)}, bf16[64,4096]{1,0:T(8,128)(2,1)S(1)}, u32[]{:S(2)}, u32[]{:S(2)}) %collective-permute-start.6) | collective-permute-done | bytes 524320 | tf_op jit(solution)/shard_map/ppermute | solution.py:704
  77.6 0.5 collective-permute-start.12
  78.1 0.3 collective-permute-start.14
  78.5 2.8 %collective-permute-done.10 = bf16[2,2,128,1792]{3,2,1,0:T(8,128)(2,1)S(1)} collective-permute-done((bf16[2,2,128,1792]{3,2,1,0:T(8,128)(2,1)S(1)}, bf16[2,2,128,1792]{3,2,1,0:T(8,128)(2,1)S(1)}, u32[]{:S(2)}, u32[]{:S(2)}) %collective-permute-start.10) | collective-permute-done | bytes 1835040 | tf_op jit(solution)/shard_map/ppermute | solution.py:701
  81.3 0.3 bitcast_add_fusion.1
  81.6 0.3 fusion.5.mine_ref
  81.9 0.2 collective-permute-start.15
  82.1 0.3 collective-permute-start.18
  82.4 2.0 %collective-permute-start.11 = (bf16[64,4096]{1,0:T(8,128)(2,1)S(1)}, bf16[64,4096]{1,0:T(8,128)(2,1)S(1)}, u32[]{:S(2)}, u32[]{:S(2)}) collective-permute-start(bf16[64,4096]{1,0:T(8,128)(2,1)S(1)} %collective-permute-done.6.refs_4_.refs_8_), channel_id=1, source_target_pairs={{0,1},{1,0},{2,3},{3,2},{4,5},{5,4},{6,7},{7,6},{8,9},{9,8},{10,11... | collective-permute-start | bytes 1572872 | tf_op jit(solution)/shard_map/ppermute | solution.py:707
  84.3 5.3 %student_part.2 = (bf16[8,256,256]{2,1,0:T(8,128)(2,1)S(1)}, f32[256,2048]{1,0:T(8,128)S(1)}, bf16[8,256,256]{2,1,0:T(8,128)(2,1)S(1)}) custom-call(s32[4]{0:T(128)S(1)} %pad_add_fusion.idx_ref, bf16[128,8192]{1,0:T(8,128)(2,1)S(1)} %copy-done.1, bf16[128,8192]{1,0:T(8,128)(2,1)S(1)} %copy-done.1, bf16[128,8192]{1,0:T(8,128)(2,1)} %collective-permute-done.refs_2_.refs_3_, ...), custom_call_target="tpu_custom_call" | custom-call | flops 10000000000 | bytes 10000000 | tf_op jit(solution)/shard_map/student_part/pallas_call | solution.py:551
  89.6 5.2 %target_part.2.refs_11_ = f32[256,2048]{1,0:T(8,128)S(1)} custom-call(s32[1]{0:T(128)} %bitcast.2.idx_ref, bf16[128,1792]{1,0:T(8,128)(2,1)S(1)} %fusion.5.mine_ref, bf16[128,1792]{1,0:T(8,128)(2,1)S(1)} %collective-permute-done.15.near_ref, bf16[3584,2048]{1,0:T(8,128)(2,1)} %refs_4_.5), custom_call_target="tpu_custom_call" | custom-call | flops 1 | bytes 1 | tf_op jit(solution)/shard_map/target_part/pallas_call | solution.py:407
  94.8 6.6 %collective-permute-done.14 = bf16[2,128,1792]{2,1,0:T(8,128)(2,1)S(1)} collective-permute-done((bf16[2,128,1792]{2,1,0:T(8,128)(2,1)S(1)}, bf16[2,128,1792]{2,1,0:T(8,128)(2,1)S(1)}, u32[]{:S(2)}, u32[]{:S(2)}) %collective-permute-start.14) | collective-permute-done | bytes 917536 | tf_op jit(solution)/shard_map/ppermute | solution.py:704
  101.4 0.3 bitcast_add_fusion
  101.7 0.3 fusion.3.mine_ref
  102.0 0.6 collective-permute-start.17
  102.6 0.3 collective-permute-start.16
  102.9 0.5 collective-permute-done.13.refs_7_.refs_11_
  103.3 4.5 %student_part.3 = (bf16[8,256,256]{2,1,0:T(8,128)(2,1)S(1)}, f32[256,2048]{1,0:T(8,128)S(1)}) custom-call(s32[4]{0:T(128)S(1)} %pad_add_fusion.idx_ref, bf16[128,4096]{1,0:T(8,128)(2,1)S(1)} %collective-permute-done.1.refs_0_.refs_1_.refs_4_.refs_5_, bf16[128,4096]{1,0:T(8,128)(2,1)S(1)} %collective-permute-done.1.refs_0_.refs_1_.refs_4_.refs_5_, ...), custom_call_target="tpu_custom_call" | custom-call | flops 10000000000 | bytes 10000000 | tf_op jit(solution)/shard_map/student_part/pallas_call | solution.py:551
  107.9 1.0 copy-done.2
  108.8 2.4 %collective-permute-done.18.refs_1_ = bf16[128,1792]{1,0:T(8,128)(2,1)S(1)} collective-permute-done((bf16[128,1792]{1,0:T(8,128)(2,1)S(1)}, bf16[128,1792]{1,0:T(8,128)(2,1)S(1)}, u32[]{:S(2)}, u32[]{:S(2)}) %collective-permute-start.18) | collective-permute-done | bytes 458784 | tf_op jit(solution)/shard_map/ppermute | solution.py:704
  111.3 5.4 %target_part.3.refs_5_ = f32[256,2048]{1,0:T(8,128)S(1)} custom-call(s32[1]{0:T(128)} %bitcast.2.idx_ref, bf16[128,1792]{1,0:T(8,128)(2,1)S(1)} %fusion.3.mine_ref, bf16[128,1792]{1,0:T(8,128)(2,1)S(1)} %collective-permute-done.17.near_ref, bf16[3584,2048]{1,0:T(8,128)(2,1)} %refs_4_.5, f32[256,2048]{1,0:T(8,128)S(1)} %get-tuple-element.66.refs_0_), custom_call_target="tpu_custom_call" | custom-call | flops 1 | bytes 1 | tf_op jit(solution)/shard_map/target_part/pallas_call | solution.py:407
  116.7 3.4 %collective-permute-done.16.refs_0_ = bf16[128,1792]{1,0:T(8,128)(2,1)S(1)} collective-permute-done((bf16[128,1792]{1,0:T(8,128)(2,1)S(1)}, bf16[128,1792]{1,0:T(8,128)(2,1)S(1)}, u32[]{:S(2)}, u32[]{:S(2)}) %collective-permute-start.16) | collective-permute-done | bytes 458784 | tf_op jit(solution)/shard_map/ppermute | solution.py:704
  120.2 1.8 %collective-permute-done.19.refs_2_ = bf16[128,1792]{1,0:T(8,128)(2,1)S(1)} collective-permute-done((bf16[128,1792]{1,0:T(8,128)(2,1)S(1)}, bf16[128,1792]{1,0:T(8,128)(2,1)S(1)}, u32[]{:S(2)}, u32[]{:S(2)}) %collective-permute-start.19) | collective-permute-done | bytes 458784 | tf_op jit(solution)/shard_map/ppermute | solution.py:701
  122.0 1.0 copy-done.11
  123.0 11.1 %left_grads.1 = (bf16[4,256,128]{2,1,0:T(8,128)(2,1)S(1)}, bf16[8,256,512]{2,1,0:T(8,128)(2,1)S(1)}) custom-call(s32[4]{0:T(128)S(1)} %pad_add_fusion.idx_ref, bf16[128,1792]{1,0:T(8,128)(2,1)S(1)} %collective-permute-done.16.refs_0_, bf16[128,1792]{1,0:T(8,128)(2,1)S(1)} %copy-done.11, bf16[128,1792]{1,0:T(8,128)(2,1)S(1)} %collective-permute-done.19.refs_2_, ...), custom_call_target="tpu_custom_call" | custom-call | flops 1 | bytes 1 | tf_op jit(solution)/shard_map/left_grads/pallas_call | solution.py:619
  134.2 2.0 %collective-permute-start.21 = (bf16[2,256,128]{2,1,0:T(8,128)(2,1)S(1)}, bf16[2,256,128]{2,1,0:T(8,128)(2,1)S(1)}, u32[]{:S(2)}, u32[]{:S(2)}) collective-permute-start(bf16[2,256,128]{2,1,0:T(8,128)(2,1)S(1)} %slice.51), channel_id=1, source_target_pairs={{0,1},{1,0},{2,3},{3,2},{4,5},{5,4},{6,7},{7,6},{8,9},{9,8},{10,11... | collective-permute-start | bytes 393224 | tf_op jit(solution)/shard_map/ppermute | solution.py:707
  136.2 3.4 %right_grads.2 = bf16[2,512,128]{2,1,0:T(8,128)(2,1)S(1)} custom-call(s32[4]{0:T(128)S(1)} %pad_add_fusion.idx_ref, bf16[128,8192]{1,0:T(8,128)(2,1)S(1)} %copy-done.1, bf16[128,8192]{1,0:T(8,128)(2,1)S(1)} %copy-done.1, bf16[128,8192]{1,0:T(8,128)(2,1)} %collective-permute-done.refs_2_.refs_3_, bf16[128,8192]{1,0:T(8,128)(2,1)} %collective-permute-done.refs_2_.refs_3_, ...), custom_call_target="tpu_custom_call" | custom-call | flops 1 | bytes 1 | tf_op jit(solution)/shard_map/right_grads/pallas_call | solution.py:673
  139.6 0.1 collective-permute-start.22
  139.7 0.3 collective-permute-done.21
  140.0 0.3 collective-permute-start.25
  140.4 3.4 %right_grads.3 = bf16[2,512,128]{2,1,0:T(8,128)(2,1)S(1)} custom-call(s32[4]{0:T(128)S(1)} %pad_add_fusion.idx_ref, bf16[128,8192]{1,0:T(8,128)(2,1)S(1)} %copy-done.1, bf16[128,8192]{1,0:T(8,128)(2,1)S(1)} %copy-done.1, bf16[128,8192]{1,0:T(8,128)(2,1)} %collective-permute-done.refs_2_.refs_3_, bf16[128,8192]{1,0:T(8,128)(2,1)} %collective-permute-done.refs_2_.refs_3_, ...), custom_call_target="tpu_custom_call" | custom-call | flops 10000000000 | bytes 10000000 | tf_op jit(solution)/shard_map/right_grads/pallas_call | solution.py:673
  143.7 5.3 %collective-permute-done.22 = bf16[2,512,128]{2,1,0:T(8,128)(2,1)S(1)} collective-permute-done((bf16[2,512,128]{2,1,0:T(8,128)(2,1)S(1)}, bf16[2,512,128]{2,1,0:T(8,128)(2,1)S(1)}, u32[]{:S(2)}, u32[]{:S(2)}) %collective-permute-start.22) | collective-permute-done | bytes 262176 | tf_op jit(solution)/shard_map/ppermute | solution.py:707
  149.2 0.7 collective-permute-start.23
  149.9 2.3 %collective-permute-start.24 = (bf16[512,128]{1,0:T(8,128)(2,1)S(1)}, bf16[512,128]{1,0:T(8,128)(2,1)S(1)}, u32[]{:S(2)}, u32[]{:S(2)}) collective-permute-start(bf16[512,128]{1,0:T(8,128)(2,1)S(1)} %get-tuple-element.75), channel_id=1, source_target_pairs={{0,8},{1,12},{2,0},{3,4},{4,9},{5,13},{6,1},{7,5},{8,10},{9,14},{1... | collective-permute-start | bytes 393224 | tf_op jit(solution)/shard_map/ppermute | solution.py:714
  152.2 0.2 reshape.40
  152.4 0.7 copy.9
  153.1 10.5 %collective-permute-done.24 = bf16[512,128]{1,0:T(8,128)(2,1)S(1)} collective-permute-done((bf16[512,128]{1,0:T(8,128)(2,1)S(1)}, bf16[512,128]{1,0:T(8,128)(2,1)S(1)}, u32[]{:S(2)}, u32[]{:S(2)}) %collective-permute-start.24) | collective-permute-done | bytes 131104 | tf_op jit(solution)/shard_map/ppermute | solution.py:714
  163.6 0.7 convert_add_fusion.2
  (59 shorter events, 0.5 us)
Async XLA Ops:
  0.6 7.9 %copy-start.14 = (bf16[32,16,64]{2,1,0:T(8,128)(2,1)S(1)}, bf16[32,16,64]{2,1,0:T(8,128)(2,1)}, u32[]{:S(2)}) copy-start(bf16[32,16,64]{2,1,0:T(8,128)(2,1)} %param.11) | copy-start | bytes 196612
  0.6 8.8 %collective-permute-start = (bf16[128,8192]{1,0:T(8,128)(2,1)}, bf16[128,8192]{1,0:T(8,128)(2,1)}, u32[]{:S(2)}, u32[]{:S(2)}) collective-permute-start(bf16[128,8192]{1,0:T(8,128)(2,1)} %refs_1_.9), channel_id=1, source_target_pairs={{0,4},{4,0},{8,12},{12,8},{1,5},{5,1},{9,13},{13,9},{2,6},{6,2},{1... | collective-permute-start | bytes 6291464 | tf_op jit(solution)/shard_map/ppermute | solution.py:701
  1.2 8.2 %copy-start = (bf16[128,8192]{1,0:T(8,128)(2,1)S(1)}, bf16[128,8192]{1,0:T(8,128)(2,1)}, u32[]{:S(2)}) copy-start(bf16[128,8192]{1,0:T(8,128)(2,1)} %refs_1_.9) | copy-start | bytes 6291460
  6.0 28.7 %collective-permute-start.1 = (bf16[128,4096]{1,0:T(8,128)(2,1)}, bf16[128,4096]{1,0:T(8,128)(2,1)S(1)}, u32[]{:S(2)}, u32[]{:S(2)}) collective-permute-start(bf16[128,4096]{1,0:T(8,128)(2,1)} %cut_tokens.2), channel_id=1, source_target_pairs={{0,8},{4,12},{8,0},{12,4},{1,9},{5,13},{9,1},{13,5},{2,10},{6,14},... | collective-permute-start | bytes 3145736 | tf_op jit(solution)/shard_map/ppermute | solution.py:704
  9.4 12.0 %copy-start.16 = (bf16[16,32,128]{2,1,0:T(8,128)(2,1)S(1)}, bf16[16,32,128]{2,1,0:T(8,128)(2,1)}, u32[]{:S(2)}) copy-start(bf16[16,32,128]{2,1,0:T(8,128)(2,1)} %param.10) | copy-start | bytes 393220
  20.2 1.0 copy-start.4
  21.1 8.3 %collective-permute-start.4 = (bf16[2,128,1792]{2,1,0:T(8,128)(2,1)}, bf16[2,128,1792]{2,1,0:T(8,128)(2,1)S(1)}, u32[]{:S(2)}, u32[]{:S(2)}) collective-permute-start(bf16[2,128,1792]{2,1,0:T(8,128)(2,1)} %bitcast.13), channel_id=1, source_target_pairs={{0,4},{4,0},{8,12},{12,8},{1,5},{5,1},{9,13},{13,9},{2,6},{6,2},{1... | collective-permute-start | bytes 2752520 | tf_op jit(solution)/shard_map/ppermute | solution.py:701
  21.3 8.1 %copy-start.5 = (bf16[1,2,128,1792]{3,2,1,0:T(8,128)(2,1)S(1)}, bf16[1,2,128,1792]{3,2,1,0:T(8,128)(2,1)}, u32[]{:S(2)}) copy-start(bf16[1,2,128,1792]{3,2,1,0:T(8,128)(2,1)} %copy-done.4) | copy-start | bytes 2752516
  21.3 4.7 %collective-permute-start.2 = (bf16[16,32,128]{2,1,0:T(8,128)(2,1)S(1)}, bf16[16,32,128]{2,1,0:T(8,128)(2,1)S(1)}, u32[]{:S(2)}, u32[]{:S(2)}) collective-permute-start(bf16[16,32,128]{2,1,0:T(8,128)(2,1)S(1)} %copy-done.16), channel_id=1, source_target_pairs={{0,0},{1,4},{2,8},{3,12},{4,1},{5,5},{6,9},{7,13},{8,2},{9,6},{10,... | collective-permute-start | bytes 393224 | tf_op jit(solution)/shard_map/ppermute | solution.py:714
  26.0 10.2 %copy-start.13 = (bf16[1,768,128]{2,1,0:T(8,128)(2,1)}, bf16[1,768,128]{2,1,0:T(8,128)(2,1)S(1)}, u32[]{:S(2)}) copy-start(bf16[1,768,128]{2,1,0:T(8,128)(2,1)S(1)} %maximum_bitcast_fusion.mine_ref) | copy-start | bytes 589828
  26.0 10.0 %collective-permute-start.3 = (bf16[1,768,128]{2,1,0:T(8,128)(2,1)S(1)}, bf16[1,768,128]{2,1,0:T(8,128)(2,1)S(1)}, u32[]{:S(2)}, u32[]{:S(2)}) collective-permute-start(bf16[1,768,128]{2,1,0:T(8,128)(2,1)S(1)} %maximum_bitcast_fusion.mine_ref), channel_id=1, source_target_pairs={{0,1},{1,0},{2,3},{3,2},{4,5},{5,4},{6,7},{7,6},{8,9},{9,8},{10,11... | collective-permute-start | bytes 589832 | tf_op jit(solution)/shard_map/ppermute | solution.py:707
  36.0 0.7 copy-start.15
  36.0 9.6 %collective-permute-start.5 = (bf16[128,4096]{1,0:T(8,128)(2,1)S(1)}, bf16[128,4096]{1,0:T(8,128)(2,1)S(1)}, u32[]{:S(2)}, u32[]{:S(2)}) collective-permute-start(bf16[128,4096]{1,0:T(8,128)(2,1)S(1)} %collective-permute-done.1.refs_0_.refs_1_.refs_4_.refs_5_), channel_id=1, source_target_pairs={{0,4},{4,0},{8,12},{12,8},{1,5},{5,1},{9,13},{13,9},{2,6},{6,2},{1... | collective-permute-start | bytes 3145736 | tf_op jit(solution)/shard_map/ppermute | solution.py:701
  38.5 17.1 %copy-start.1 = (bf16[128,8192]{1,0:T(8,128)(2,1)S(1)}, bf16[128,8192]{1,0:T(8,128)(2,1)}, u32[]{:S(2)}) copy-start(bf16[128,8192]{1,0:T(8,128)(2,1)} %refs_1_.9) | copy-start | bytes 6291460
  38.5 29.8 %collective-permute-start.8 = (bf16[2,768,128]{2,1,0:T(8,128)(2,1)}, bf16[2,768,128]{2,1,0:T(8,128)(2,1)S(1)}, u32[]{:S(2)}, u32[]{:S(2)}) collective-permute-start(bf16[2,768,128]{2,1,0:T(8,128)(2,1)} %join.1), channel_id=1, source_target_pairs={{0,2},{1,3},{2,0},{3,1},{4,6},{5,7},{6,4},{7,5},{8,10},{9,11},{10,... | collective-permute-start | bytes 1179656 | tf_op jit(solution)/shard_map/ppermute | solution.py:707
  43.6 33.9 %collective-permute-start.7 = (bf16[2,128,1792]{2,1,0:T(8,128)(2,1)}, bf16[2,128,1792]{2,1,0:T(8,128)(2,1)S(1)}, u32[]{:S(2)}, u32[]{:S(2)}) collective-permute-start(bf16[2,128,1792]{2,1,0:T(8,128)(2,1)} %fusion.1), channel_id=1, source_target_pairs={{0,8},{4,12},{8,0},{12,4},{1,9},{5,13},{9,1},{13,5},{2,10},{6,14},... | collective-permute-start | bytes 2752520 | tf_op jit(solution)/shard_map/ppermute | solution.py:704
  43.6 33.9 %collective-permute-start.6 = (bf16[64,4096]{1,0:T(8,128)(2,1)}, bf16[64,4096]{1,0:T(8,128)(2,1)S(1)}, u32[]{:S(2)}, u32[]{:S(2)}) collective-permute-start(bf16[64,4096]{1,0:T(8,128)(2,1)} %cut_tokens.3), channel_id=1, source_target_pairs={{0,8},{4,12},{8,0},{12,4},{1,9},{5,13},{9,1},{13,5},{2,10},{6,14},... | collective-permute-start | bytes 1572872 | tf_op jit(solution)/shard_map/ppermute | solution.py:704
  55.6 12.5 %collective-permute-start.9 = (bf16[2,128,1792]{2,1,0:T(8,128)(2,1)S(1)}, bf16[2,128,1792]{2,1,0:T(8,128)(2,1)S(1)}, u32[]{:S(2)}, u32[]{:S(2)}) collective-permute-start(bf16[2,128,1792]{2,1,0:T(8,128)(2,1)S(1)} %bitcast.62), channel_id=1, source_target_pairs={{0,4},{4,0},{8,12},{12,8},{1,5},{5,1},{9,13},{13,9},{2,6},{6,2},{1... | collective-permute-start | bytes 2752520 | tf_op jit(solution)/shard_map/ppermute | solution.py:701
  68.0 10.0 %copy-start.12 = (bf16[2,768,128]{2,1,0:T(8,128)(2,1)S(1)}, bf16[2,768,128]{2,1,0:T(8,128)(2,1)}, u32[]{:S(2)}) copy-start(bf16[2,768,128]{2,1,0:T(8,128)(2,1)} %join.1) | copy-start | bytes 1179652
  77.5 3.8 %collective-permute-start.10 = (bf16[2,2,128,1792]{3,2,1,0:T(8,128)(2,1)S(1)}, bf16[2,2,128,1792]{3,2,1,0:T(8,128)(2,1)S(1)}, u32[]{:S(2)}, u32[]{:S(2)}) collective-permute-start(bf16[2,2,128,1792]{3,2,1,0:T(8,128)(2,1)S(1)} %get-tuple-element.54), channel_id=1, source_target_pairs={{0,4},{4,0},{8,12},{12,8},{1,5},{5,1},{9,13},{13,9},{2,6},{6,2},{1... | collective-permute-start | bytes 5505032 | tf_op jit(solution)/shard_map/ppermute | solution.py:701
  77.6 25.3 %collective-permute-start.12 = (bf16[64,4096]{1,0:T(8,128)(2,1)S(1)}, bf16[64,4096]{1,0:T(8,128)(2,1)S(1)}, u32[]{:S(2)}, u32[]{:S(2)}) collective-permute-start(bf16[64,4096]{1,0:T(8,128)(2,1)S(1)} %collective-permute-done.6.refs_4_.refs_8_), channel_id=1, source_target_pairs={{0,4},{4,0},{8,12},{12,8},{1,5},{5,1},{9,13},{13,9},{2,6},{6,2},{1... | collective-permute-start | bytes 1572872 | tf_op jit(solution)/shard_map/ppermute | solution.py:701
  78.1 23.3 %collective-permute-start.14 = (bf16[2,128,1792]{2,1,0:T(8,128)(2,1)S(1)}, bf16[2,128,1792]{2,1,0:T(8,128)(2,1)S(1)}, u32[]{:S(2)}, u32[]{:S(2)}) collective-permute-start(bf16[2,128,1792]{2,1,0:T(8,128)(2,1)S(1)} %fusion), channel_id=1, source_target_pairs={{0,8},{4,12},{8,0},{12,4},{1,9},{5,13},{9,1},{13,5},{2,10},{6,14},... | collective-permute-start | bytes 2752520 | tf_op jit(solution)/shard_map/ppermute | solution.py:704
  81.9 7.7 %collective-permute-start.15 = (bf16[128,1792]{1,0:T(8,128)(2,1)S(1)}, bf16[128,1792]{1,0:T(8,128)(2,1)S(1)}, u32[]{:S(2)}, u32[]{:S(2)}) collective-permute-start(bf16[128,1792]{1,0:T(8,128)(2,1)S(1)} %fusion.5.mine_ref), channel_id=1, source_target_pairs={{0,4},{4,0},{8,12},{12,8},{1,5},{5,1},{9,13},{13,9},{2,6},{6,2},{1... | collective-permute-start | bytes 1376264 | tf_op jit(solution)/shard_map/ppermute | solution.py:701
  82.1 29.2 %collective-permute-start.18 = (bf16[128,1792]{1,0:T(8,128)(2,1)S(1)}, bf16[128,1792]{1,0:T(8,128)(2,1)S(1)}, u32[]{:S(2)}, u32[]{:S(2)}) collective-permute-start(bf16[128,1792]{1,0:T(8,128)(2,1)S(1)} %fusion.5.mine_ref), channel_id=1, source_target_pairs={{0,8},{4,12},{8,0},{12,4},{1,9},{5,13},{9,1},{13,5},{2,10},{6,14},... | collective-permute-start | bytes 1376264 | tf_op jit(solution)/shard_map/ppermute | solution.py:704
  82.4 19.0 %collective-permute-start.11 = (bf16[64,4096]{1,0:T(8,128)(2,1)S(1)}, bf16[64,4096]{1,0:T(8,128)(2,1)S(1)}, u32[]{:S(2)}, u32[]{:S(2)}) collective-permute-start(bf16[64,4096]{1,0:T(8,128)(2,1)S(1)} %collective-permute-done.6.refs_4_.refs_8_), channel_id=1, source_target_pairs={{0,1},{1,0},{2,3},{3,2},{4,5},{5,4},{6,7},{7,6},{8,9},{9,8},{10,11... | collective-permute-start | bytes 1572872 | tf_op jit(solution)/shard_map/ppermute | solution.py:707
  101.4 1.9 %copy-start.8 = (bf16[64,4096]{1,0:T(8,128)(2,1)}, bf16[64,4096]{1,0:T(8,128)(2,1)S(1)}, u32[]{:S(2)}) copy-start(bf16[64,4096]{1,0:T(8,128)(2,1)S(1)} %collective-permute-done.11.refs_5_.refs_9_) | copy-start | bytes 1572868
  101.4 1.9 %collective-permute-start.13 = (bf16[64,4096]{1,0:T(8,128)(2,1)S(1)}, bf16[64,4096]{1,0:T(8,128)(2,1)S(1)}, u32[]{:S(2)}, u32[]{:S(2)}) collective-permute-start(bf16[64,4096]{1,0:T(8,128)(2,1)S(1)} %collective-permute-done.11.refs_5_.refs_9_), channel_id=1, source_target_pairs={{0,4},{4,0},{8,12},{12,8},{1,5},{5,1},{9,13},{13,9},{2,6},{6,2},{1... | collective-permute-start | bytes 1572872 | tf_op jit(solution)/shard_map/ppermute | solution.py:701
  102.0 9.3 %collective-permute-start.17 = (bf16[128,1792]{1,0:T(8,128)(2,1)S(1)}, bf16[128,1792]{1,0:T(8,128)(2,1)S(1)}, u32[]{:S(2)}, u32[]{:S(2)}) collective-permute-start(bf16[128,1792]{1,0:T(8,128)(2,1)S(1)} %fusion.3.mine_ref), channel_id=1, source_target_pairs={{0,4},{4,0},{8,12},{12,8},{1,5},{5,1},{9,13},{13,9},{2,6},{6,2},{1... | collective-permute-start | bytes 1376264 | tf_op jit(solution)/shard_map/ppermute | solution.py:701
  102.6 17.6 %collective-permute-start.16 = (bf16[128,1792]{1,0:T(8,128)(2,1)S(1)}, bf16[128,1792]{1,0:T(8,128)(2,1)S(1)}, u32[]{:S(2)}, u32[]{:S(2)}) collective-permute-start(bf16[128,1792]{1,0:T(8,128)(2,1)S(1)} %fusion.3.mine_ref), channel_id=1, source_target_pairs={{0,8},{4,12},{8,0},{12,4},{1,9},{5,13},{9,1},{13,5},{2,10},{6,14},... | collective-permute-start | bytes 1376264 | tf_op jit(solution)/shard_map/ppermute | solution.py:704
  102.9 5.0 %copy-start.6 = (bf16[64,4096]{1,0:T(8,128)(2,1)}, bf16[64,4096]{1,0:T(8,128)(2,1)S(1)}, u32[]{:S(2)}) copy-start(bf16[64,4096]{1,0:T(8,128)(2,1)S(1)} %collective-permute-done.12.refs_6_.refs_10_) | copy-start | bytes 1572868
  107.9 1.0 copy-start.2
  111.2 5.5 %copy-start.10 = (bf16[128,1792]{1,0:T(8,128)(2,1)}, bf16[128,1792]{1,0:T(8,128)(2,1)S(1)}, u32[]{:S(2)}) copy-start(bf16[128,1792]{1,0:T(8,128)(2,1)S(1)} %collective-permute-done.18.refs_1_) | copy-start | bytes 1376260
  111.3 8.9 %collective-permute-start.20 = (bf16[128,1792]{1,0:T(8,128)(2,1)S(1)}, bf16[128,1792]{1,0:T(8,128)(2,1)S(1)}, u32[]{:S(2)}, u32[]{:S(2)}) collective-permute-start(bf16[128,1792]{1,0:T(8,128)(2,1)S(1)} %collective-permute-done.18.refs_1_), channel_id=1, source_target_pairs={{0,4},{4,0},{8,12},{12,8},{1,5},{5,1},{9,13},{13,9},{2,6},{6,2},{1... | collective-permute-start | bytes 1376264 | tf_op jit(solution)/shard_map/ppermute | solution.py:701
  111.3 10.7 %copy-start.3 = (bf16[8,256,256]{2,1,0:T(8,128)(2,1)S(1)}, bf16[8,256,256]{2,1,0:T(8,128)(2,1)}, u32[]{:S(2)}) copy-start(bf16[8,256,256]{2,1,0:T(8,128)(2,1)} %copy-done.2) | copy-start | bytes 3145732
  120.1 1.8 %collective-permute-start.19 = (bf16[128,1792]{1,0:T(8,128)(2,1)S(1)}, bf16[128,1792]{1,0:T(8,128)(2,1)S(1)}, u32[]{:S(2)}, u32[]{:S(2)}) collective-permute-start(bf16[128,1792]{1,0:T(8,128)(2,1)S(1)} %collective-permute-done.16.refs_0_), channel_id=1, source_target_pairs={{0,4},{4,0},{8,12},{12,8},{1,5},{5,1},{9,13},{13,9},{2,6},{6,2},{1... | collective-permute-start | bytes 1376264 | tf_op jit(solution)/shard_map/ppermute | solution.py:701
  122.0 1.0 copy-start.11
  123.0 13.2 %copy-start.7 = (bf16[64,4096]{1,0:T(8,128)(2,1)S(1)}, bf16[64,4096]{1,0:T(8,128)(2,1)}, u32[]{:S(2)}) copy-start(bf16[64,4096]{1,0:T(8,128)(2,1)} %copy-done.6) | copy-start | bytes 1572868
  123.0 13.2 %copy-start.9 = (bf16[64,4096]{1,0:T(8,128)(2,1)S(1)}, bf16[64,4096]{1,0:T(8,128)(2,1)}, u32[]{:S(2)}) copy-start(bf16[64,4096]{1,0:T(8,128)(2,1)} %copy-done.8) | copy-start | bytes 1572868
  134.2 5.8 %collective-permute-start.21 = (bf16[2,256,128]{2,1,0:T(8,128)(2,1)S(1)}, bf16[2,256,128]{2,1,0:T(8,128)(2,1)S(1)}, u32[]{:S(2)}, u32[]{:S(2)}) collective-permute-start(bf16[2,256,128]{2,1,0:T(8,128)(2,1)S(1)} %slice.51), channel_id=1, source_target_pairs={{0,1},{1,0},{2,3},{3,2},{4,5},{5,4},{6,7},{7,6},{8,9},{9,8},{10,11... | collective-permute-start | bytes 393224 | tf_op jit(solution)/shard_map/ppermute | solution.py:707
  139.6 9.5 %collective-permute-start.22 = (bf16[2,512,128]{2,1,0:T(8,128)(2,1)S(1)}, bf16[2,512,128]{2,1,0:T(8,128)(2,1)S(1)}, u32[]{:S(2)}, u32[]{:S(2)}) collective-permute-start(bf16[2,512,128]{2,1,0:T(8,128)(2,1)S(1)} %right_grads.2), channel_id=1, source_target_pairs={{0,1},{1,0},{2,3},{3,2},{4,5},{5,4},{6,7},{7,6},{8,9},{9,8},{10,11... | collective-permute-start | bytes 786440 | tf_op jit(solution)/shard_map/ppermute | solution.py:707
  140.0 12.2 %collective-permute-start.25 = (bf16[256,128]{1,0:T(8,128)(2,1)S(1)}, bf16[256,128]{1,0:T(8,128)(2,1)S(1)}, u32[]{:S(2)}, u32[]{:S(2)}) collective-permute-start(bf16[256,128]{1,0:T(8,128)(2,1)S(1)} %slice_bitcast_fusion.6), channel_id=1, source_target_pairs={{0,2},{1,3},{2,0},{3,1},{4,6},{5,7},{6,4},{7,5},{8,10},{9,11},{10,... | collective-permute-start | bytes 196616 | tf_op jit(solution)/shard_map/ppermute | solution.py:707
  149.2 3.9 %collective-permute-start.23 = (bf16[512,128]{1,0:T(8,128)(2,1)S(1)}, bf16[512,128]{1,0:T(8,128)(2,1)S(1)}, u32[]{:S(2)}, u32[]{:S(2)}) collective-permute-start(bf16[512,128]{1,0:T(8,128)(2,1)S(1)} %get-tuple-element.74), channel_id=1, source_target_pairs={{0,0},{1,4},{2,8},{3,12},{4,1},{5,5},{6,9},{7,13},{8,2},{9,6},{10,... | collective-permute-start | bytes 393224 | tf_op jit(solution)/shard_map/ppermute | solution.py:714
  149.9 13.7 %collective-permute-start.24 = (bf16[512,128]{1,0:T(8,128)(2,1)S(1)}, bf16[512,128]{1,0:T(8,128)(2,1)S(1)}, u32[]{:S(2)}, u32[]{:S(2)}) collective-permute-start(bf16[512,128]{1,0:T(8,128)(2,1)S(1)} %get-tuple-element.75), channel_id=1, source_target_pairs={{0,8},{1,12},{2,0},{3,4},{4,9},{5,13},{6,1},{7,5},{8,10},{9,14},{1... | collective-permute-start | bytes 393224 | tf_op jit(solution)/shard_map/ppermute | solution.py:714

commit v12 on v11

--- a/solution.py
+++ b/solution.py
@@ -323,20 +323,22 @@
     )(jnp.stack([row, column]).astype(jnp.int32), tokens)
 
 
-def join_kernel(mine_ref, more_ref, out_ref):
-    count = mine_ref.shape[0]
-    out_ref[:count] = mine_ref[...]
-    out_ref[count:] = more_ref[...]
-
-
-def join(mine, more):
-    shape = (2 * mine.shape[0],) + mine.shape[1:]
+def pack_kernel(left_ref, out_ref):
+    share = left_ref.shape[1]
+    for pair in range(left_ref.shape[0] // 2):
+        both = [left_ref[2 * pair].astype(F32), left_ref[2 * pair + 1].astype(F32)]
+        both = jnp.concatenate(both, axis=1)
+        out_ref[pair * share : (pair + 1) * share, :] = both.astype(BF16)
+
+
+def pack_left(left):
+    pairs, share, blocks = left.shape
     return pl.pallas_call(
-        join_kernel,
-        out_shape=jax.ShapeDtypeStruct(shape, mine.dtype),
+        pack_kernel,
+        out_shape=jax.ShapeDtypeStruct((pairs // 2 * share, 2 * blocks), BF16),
         cost_estimate=LARGE,
-        name="join",
-    )(mine, more)
+        name="pack_left",
+    )(left)
 
 
 def products_kernel(sets, idx_ref, *refs):
@@ -735,26 +737,25 @@
     )
 
     pairs, blocks = left_factor.shape[0], left_factor.shape[2]
-    left_rows = left_factor.reshape(pairs // 2, 2, -1, blocks).transpose(0, 2, 1, 3)
     turned = turn(after(right_factor, mine), 0)
-    rest = cut_tokens(after(tokens, mine), rows // 2, odd, chip, LARGE)
+    left_rows = pack_left(after(left_factor, mine))
     factors = jnp.concatenate(
-        [after(turned, rest).reshape(-1, LANES), left_rows.reshape(-1, LANES)], axis=0
+        [after(turned, left_rows).reshape(-1, LANES), left_rows], axis=0
     )[None]
     more = along(factors, 1)
     sums = add(mine[0], swap(other[0])).astype(BF16)
-    arrived = after(arrived, more, rest, sums)
+    rest = cut_tokens(after(tokens, left_rows), rows // 2, odd, chip)
+    arrived = after(arrived, more, sums, rest)
     got_early = across(sums)
     late_first = across(after(rest, sums))
-    factors = join(after(factors, arrived), more)
-    more = along(factors, 2)
+    factors = jnp.concatenate([factors, more], axis=0)
 
     order = jnp.concatenate([base, jnp.stack([chip, z])]).astype(jnp.int32)
     own = [tokens, tokens, near_tokens, near_tokens]
     near_arrived = swap(arrived)
     late = [arrived, arrived, near_arrived, near_arrived]
     late_pieces = [(t, row, 3) for t in (arrived, near_arrived) for row in (0, 1)]
-    late_order = after(scalars(other_block), factors)
+    late_order = after(scalars(other_block), rest)
     mine, other = products(late_pieces, late_order, gate_weight, up_weight, 0, part)
     near = swap(other[0])
     mine_order = after(scalars(mine_block), mine)
@@ -763,9 +764,10 @@
     )
     sums = add(mine[0], after(near, kept)).astype(BF16)
     got = across(sums)
-    near_kept = swap(after(other, got_early, late_first, more, sums))
-
-    factors = jnp.concatenate([factors, after(more, kept)], axis=0)
+    near_kept = swap(after(other, got_early, late_first, sums))
+    factors = after(factors, kept)
+    more = along(factors, 2)
+
     def activate(u, term):
         total = add(kept[u], near_kept[u], term)
         return (jax.nn.silu(total[0]) * total[1]).astype(BF16)
@@ -774,6 +776,7 @@
     got1 = across(hidden1)
     near1 = swap(hidden1)
     late_partner = along(after(late_first, hidden1), 1)
+    factors = jnp.concatenate([factors, after(more, hidden1)], axis=0)
     mixed0, rest0, left_diag = student_part(
         [after(tokens, hidden1, sums)] + own[1:], order, factors, pairs, tensor_count
     )

time: 165 us -> 167 us (1.012)
  starting transfers between devices: 24.3 us -> 27.9 us
    ppermute x6, waiting for transfers between devices: 7 us -> 22.8 us  [along(): lax.ppermute(value, 'tensor', [(i, i ^ bit) for i in range(tensor_count)])]
    ppermute x6, waiting for transfers between devices: 25.7 us -> 12.4 us  [across(): return lax.ppermute(value, 'fsdp', [(i, i ^ 2) for i in range(fsdp_count)])]
    ppermute x6, starting transfers between devices: 5.47 us -> 11 us  [across(): return lax.ppermute(value, 'fsdp', [(i, i ^ 2) for i in range(fsdp_count)])]
    ppermute x6, starting transfers between devices: 12.9 us -> 8.05 us  [along(): lax.ppermute(value, 'tensor', [(i, i ^ bit) for i in range(tensor_count)])]
    ppermute x11, waiting for transfers between devices: 5.08 us -> 2.46 us  [swap(): return lax.ppermute(value, 'fsdp', [(i, i ^ 1) for i in range(fsdp_count)])]
    ppermute x3, starting transfers between devices: 3.78 us -> 5.66 us  [turn(): return lax.ppermute(value, both_axes, perm)]
    unnamed x34 -> x29, local copies, waits for them, and re-layouts: 3.48 us -> 3.02 us
  transfers between devices with their start and end apart: 26 -> 26, of which waited for: 12 -> 10; matrix products, arithmetic and copies ran while one was open for 3% -> 3% of each run, Pallas kernels for 43% -> 42%
where the time goes in v12:
time: 167 us; the launch traced here: 166 us
  Pallas kernels  81.1 us (49%)
  waiting for transfers between devices  47.7 us (29%)
  starting transfers between devices  27.9 us (17%)
  other arithmetic  4.62 us (3%)
  local copies, waits for them, and re-layouts  4.18 us (3%)
    pallas_call x3, Pallas kernels, products(): pl.pallas_call(functools.partial(products_kernel, sets), grid_spec=pltpu....  33.1 us
    ppermute x6, waiting for transfers between devices, along(): lax.ppermute(value, 'tensor', [(i, i ^ bit) for i in range(tensor_count)])  22.8 us
    ppermute x6, waiting for transfers between devices, across(): return lax.ppermute(value, 'fsdp', [(i, i ^ 2) for i in range(fsdp_count)])  12.4 us
    pallas_call x1, Pallas kernels, left_grads(): pl.pallas_call(functools.partial(left_kernel, chunks, scale), grid_spec=p...  11.1 us
    ppermute x6, starting transfers between devices, across(): return lax.ppermute(value, 'fsdp', [(i, i ^ 2) for i in range(fsdp_count)])  11 us
    pallas_call x2, Pallas kernels, target_part(): pl.pallas_call(functools.partial(target_kernel, sign), grid_spec=pltpu.Pr...  10.7 us
    ppermute x3, waiting for transfers between devices, turn(): return lax.ppermute(value, both_axes, perm)  10 us
    pallas_call x2, Pallas kernels, student_part(): pl.pallas_call(functools.partial(student_kernel, steps, bool(late), tenso...  9.81 us
  transfers between devices with their start and end apart: 26, of which 10 were waited for; matrix products, arithmetic and copies ran while one was open for 3% of the time, Pallas kernels for 42%

profile of v12, /device:TPU:0, one launch (start us, length us, event | category | flops | bytes accessed | tf_op | source)
XLA Modules:
  0.0 166.4 jit_solution(14767047446650528453)
XLA Ops:
  0.6 0.5 collective-permute-start
  1.2 0.6 pad_add_fusion.1.idx_ref
  1.7 4.1 %cut_tokens.2 = bf16[128,4096]{1,0:T(8,128)(2,1)} custom-call(s32[2]{0:T(128)} %pad_add_fusion.1.idx_ref, bf16[128,8192]{1,0:T(8,128)(2,1)} %refs_1_.9), custom_call_target="tpu_custom_call" | custom-call | flops 1 | bytes 1 | tf_op jit(solution)/shard_map/cut_tokens/pallas_call | solution.py:312
  5.8 2.5 %collective-permute-start.1 = (bf16[128,4096]{1,0:T(8,128)(2,1)}, bf16[128,4096]{1,0:T(8,128)(2,1)S(1)}, u32[]{:S(2)}, u32[]{:S(2)}) collective-permute-start(bf16[128,4096]{1,0:T(8,128)(2,1)} %cut_tokens.2), channel_id=1, source_target_pairs={{0,8},{4,12},{8,0},{12,4},{1,9},{5,13},{9,1},{13,5},{2,10},{6,14},... | collective-permute-start | bytes 3145736 | tf_op jit(solution)/shard_map/ppermute | solution.py:706
  8.3 0.1 concatenate.24.idx_ref
  8.4 0.6 pad_add_fusion.2.idx_ref
  9.0 10.8 %gate_up_products.3 = (bf16[1,2,128,1792]{3,2,1,0:T(8,128)(2,1)S(1)}, bf16[1,2,128,1792]{3,2,1,0:T(8,128)(2,1)}) custom-call(s32[5]{0:T(128)S(1)} %concatenate.24.idx_ref, bf16[128,8192]{1,0:T(8,128)(2,1)S(1)} %copy-done, bf16[128,8192]{1,0:T(8,128)(2,1)S(1)} %copy-done, bf16[128,8192]{1,0:T(8,128)(2,1)} %collective-permute-done.refs_2_.refs_3_, ...), custom_call_target="tpu_custom_call" | custom-call | flops 1 | bytes 1 | tf_op jit(solution)/shard_map/gate_up_products/pallas_call | solution.py:371
  19.8 1.0 copy-done.4
  20.8 0.2 collective-permute-start.4
  21.0 0.7 collective-permute-start.2
  21.6 1.6 pack_left.1
  23.3 4.0 %cut_tokens.3 = bf16[64,4096]{1,0:T(8,128)(2,1)} custom-call(s32[2]{0:T(128)} %pad_add_fusion.2.idx_ref, bf16[128,8192]{1,0:T(8,128)(2,1)} %refs_1_.9), custom_call_target="tpu_custom_call" | custom-call | flops 1 | bytes 1 | tf_op jit(solution)/shard_map/cut_tokens/pallas_call | solution.py:312
  27.3 3.2 %collective-permute-start.3 = (bf16[1,768,128]{2,1,0:T(8,128)(2,1)S(1)}, bf16[1,768,128]{2,1,0:T(8,128)(2,1)S(1)}, u32[]{:S(2)}, u32[]{:S(2)}) collective-permute-start(bf16[1,768,128]{2,1,0:T(8,128)(2,1)S(1)} %maximum_bitcast_fusion), channel_id=1, source_target_pairs={{0,1},{1,0},{2,3},{3,2},{4,5},{5,4},{6,7},{7,6},{8,9},{9,8},{10,11... | collective-permute-start | bytes 589832 | tf_op jit(solution)/shard_map/ppermute | solution.py:709
  30.5 1.1 fusion.1
  31.7 2.9 %collective-permute-done.1.refs_0_.refs_1_.refs_4_.refs_5_ = bf16[128,4096]{1,0:T(8,128)(2,1)S(1)} collective-permute-done((bf16[128,4096]{1,0:T(8,128)(2,1)}, bf16[128,4096]{1,0:T(8,128)(2,1)S(1)}, u32[]{:S(2)}, u32[]{:S(2)}) %collective-permute-start.1) | collective-permute-done | bytes 1048608 | tf_op jit(solution)/shard_map/ppermute | solution.py:706
  34.5 1.6 collective-permute-done.3
  36.1 0.3 collective-permute-start.5
  36.4 0.1 concatenate.26.idx_ref
  36.5 4.2 %collective-permute-start.7 = (bf16[2,128,1792]{2,1,0:T(8,128)(2,1)}, bf16[2,128,1792]{2,1,0:T(8,128)(2,1)S(1)}, u32[]{:S(2)}, u32[]{:S(2)}) collective-permute-start(bf16[2,128,1792]{2,1,0:T(8,128)(2,1)} %fusion.1), channel_id=1, source_target_pairs={{0,8},{4,12},{8,0},{12,4},{1,9},{5,13},{9,1},{13,5},{2,10},{6,14},... | collective-permute-start | bytes 2752520 | tf_op jit(solution)/shard_map/ppermute | solution.py:706
  40.7 0.1 collective-permute-start.6
  40.7 10.0 %gate_up_products.4 = (bf16[1,2,128,1792]{3,2,1,0:T(8,128)(2,1)S(1)}, bf16[1,2,128,1792]{3,2,1,0:T(8,128)(2,1)S(1)}) custom-call(s32[5]{0:T(128)S(1)} %concatenate.24.idx_ref, bf16[128,4096]{1,0:T(8,128)(2,1)S(1)} %collective-permute-done.1.refs_0_.refs_1_.refs_4_.refs_5_, bf16[128,4096]{1,0:T(8,128)(2,1)S(1)} %collective-permute-done.1.refs_0_.refs_1_.refs_4_.refs_5_, ...), custom_call_target="tpu_custom_call" | custom-call | flops 1 | bytes 1 | tf_op jit(solution)/shard_map/gate_up_products/pallas_call | solution.py:371
  50.7 0.3 collective-permute-start.8
  51.0 12.4 %gate_up_products.5 = (bf16[2,2,128,1792]{3,2,1,0:T(8,128)(2,1)S(1)}, bf16[2,2,128,1792]{3,2,1,0:T(8,128)(2,1)S(1)}) custom-call(s32[5]{0:T(128)S(1)} %concatenate.26.idx_ref, bf16[128,8192]{1,0:T(8,128)(2,1)S(1)} %copy-done.1, bf16[128,8192]{1,0:T(8,128)(2,1)S(1)} %copy-done.1, bf16[128,8192]{1,0:T(8,128)(2,1)} %collective-permute-done.refs_2_.refs_3_, ...), custom_call_target="tpu_custom_call" | custom-call | flops 10000000000 | bytes 10000000 | tf_op jit(solution)/shard_map/gate_up_products/pallas_call | solution.py:371
  63.4 0.2 fusion
  63.6 9.5 %collective-permute-done.6.refs_4_.refs_8_ = bf16[64,4096]{1,0:T(8,128)(2,1)S(1)} collective-permute-done((bf16[64,4096]{1,0:T(8,128)(2,1)}, bf16[64,4096]{1,0:T(8,128)(2,1)S(1)}, u32[]{:S(2)}, u32[]{:S(2)}) %collective-permute-start.6) | collective-permute-done | bytes 524320 | tf_op jit(solution)/shard_map/ppermute | solution.py:706
  73.1 0.1 pad_add_fusion.idx_ref
  73.3 0.6 collective-permute-start.12
  73.8 1.7 %collective-permute-start.11 = (bf16[2,768,128]{2,1,0:T(8,128)(2,1)S(1)}, bf16[2,768,128]{2,1,0:T(8,128)(2,1)S(1)}, u32[]{:S(2)}, u32[]{:S(2)}) collective-permute-start(bf16[2,768,128]{2,1,0:T(8,128)(2,1)S(1)} %pad_maximum_fusion), channel_id=1, source_target_pairs={{0,2},{1,3},{2,0},{3,1},{4,6},{5,7},{6,4},{7,5},{8,10},{9,11},{10,... | collective-permute-start | bytes 1179656 | tf_op jit(solution)/shard_map/ppermute | solution.py:709
  75.6 0.4 collective-permute-start.14
  75.9 1.0 collective-permute-done.9
  76.9 0.3 bitcast_add_fusion.1
  77.2 0.3 fusion.5.mine_ref
  77.5 0.2 collective-permute-start.15
  77.7 1.8 %collective-permute-start.18 = (bf16[128,1792]{1,0:T(8,128)(2,1)S(1)}, bf16[128,1792]{1,0:T(8,128)(2,1)S(1)}, u32[]{:S(2)}, u32[]{:S(2)}) collective-permute-start(bf16[128,1792]{1,0:T(8,128)(2,1)S(1)} %fusion.5.mine_ref), channel_id=1, source_target_pairs={{0,8},{4,12},{8,0},{12,4},{1,9},{5,13},{9,1},{13,5},{2,10},{6,14},... | collective-permute-start | bytes 1376264 | tf_op jit(solution)/shard_map/ppermute | solution.py:706
  79.5 14.8 %collective-permute-done.11 = bf16[2,768,128]{2,1,0:T(8,128)(2,1)S(1)} collective-permute-done((bf16[2,768,128]{2,1,0:T(8,128)(2,1)S(1)}, bf16[2,768,128]{2,1,0:T(8,128)(2,1)S(1)}, u32[]{:S(2)}, u32[]{:S(2)}) %collective-permute-start.11) | collective-permute-done | bytes 393248 | tf_op jit(solution)/shard_map/ppermute | solution.py:709
  94.3 0.1 constant_dynamic-update-slice_fusion.refs_4_.refs_5_.refs_6_.refs_8_.refs_9_
  94.3 5.3 %student_part.2 = (bf16[8,256,256]{2,1,0:T(8,128)(2,1)S(1)}, f32[256,2048]{1,0:T(8,128)S(1)}, bf16[8,256,256]{2,1,0:T(8,128)(2,1)S(1)}) custom-call(s32[4]{0:T(128)S(1)} %pad_add_fusion.idx_ref, bf16[128,8192]{1,0:T(8,128)(2,1)S(1)} %copy-done.1, bf16[128,8192]{1,0:T(8,128)(2,1)S(1)} %copy-done.1, bf16[128,8192]{1,0:T(8,128)(2,1)} %collective-permute-done.refs_2_.refs_3_, ...), custom_call_target="tpu_custom_call" | custom-call | flops 10000000000 | bytes 10000000 | tf_op jit(solution)/shard_map/student_part/pallas_call | solution.py:553
  99.6 5.2 %target_part.2.refs_11_ = f32[256,2048]{1,0:T(8,128)S(1)} custom-call(s32[1]{0:T(128)} %bitcast.2.idx_ref, bf16[128,1792]{1,0:T(8,128)(2,1)S(1)} %fusion.5.mine_ref, bf16[128,1792]{1,0:T(8,128)(2,1)S(1)} %collective-permute-done.15.near_ref, bf16[3584,2048]{1,0:T(8,128)(2,1)} %refs_4_.5), custom_call_target="tpu_custom_call" | custom-call | flops 1 | bytes 1 | tf_op jit(solution)/shard_map/target_part/pallas_call | solution.py:409
  104.8 2.8 %collective-permute-done.10.refs_5_.refs_9_ = bf16[64,4096]{1,0:T(8,128)(2,1)S(1)} collective-permute-done((bf16[64,4096]{1,0:T(8,128)(2,1)S(1)}, bf16[64,4096]{1,0:T(8,128)(2,1)S(1)}, u32[]{:S(2)}, u32[]{:S(2)}) %collective-permute-start.10) | collective-permute-done | bytes 524320 | tf_op jit(solution)/shard_map/ppermute | solution.py:709
  107.7 0.3 bitcast_add_fusion
  108.0 0.3 fusion.3.mine_ref
  108.2 0.6 collective-permute-start.17
  108.8 2.1 %collective-permute-start.16 = (bf16[128,1792]{1,0:T(8,128)(2,1)S(1)}, bf16[128,1792]{1,0:T(8,128)(2,1)S(1)}, u32[]{:S(2)}, u32[]{:S(2)}) collective-permute-start(bf16[128,1792]{1,0:T(8,128)(2,1)S(1)} %fusion.3.mine_ref), channel_id=1, source_target_pairs={{0,8},{4,12},{8,0},{12,4},{1,9},{5,13},{9,1},{13,5},{2,10},{6,14},... | collective-permute-start | bytes 1376264 | tf_op jit(solution)/shard_map/ppermute | solution.py:706
  111.0 4.5 %student_part.3 = (bf16[8,256,256]{2,1,0:T(8,128)(2,1)S(1)}, f32[256,2048]{1,0:T(8,128)S(1)}) custom-call(s32[4]{0:T(128)S(1)} %pad_add_fusion.idx_ref, bf16[128,4096]{1,0:T(8,128)(2,1)S(1)} %collective-permute-done.1.refs_0_.refs_1_.refs_4_.refs_5_, bf16[128,4096]{1,0:T(8,128)(2,1)S(1)} %collective-permute-done.1.refs_0_.refs_1_.refs_4_.refs_5_, ...), custom_call_target="tpu_custom_call" | custom-call | flops 10000000000 | bytes 10000000 | tf_op jit(solution)/shard_map/student_part/pallas_call | solution.py:553
  115.5 1.0 copy-done.2
  116.5 5.5 %target_part.3.refs_5_ = f32[256,2048]{1,0:T(8,128)S(1)} custom-call(s32[1]{0:T(128)} %bitcast.2.idx_ref, bf16[128,1792]{1,0:T(8,128)(2,1)S(1)} %fusion.3.mine_ref, bf16[128,1792]{1,0:T(8,128)(2,1)S(1)} %collective-permute-done.17.near_ref, bf16[3584,2048]{1,0:T(8,128)(2,1)} %refs_4_.5, f32[256,2048]{1,0:T(8,128)S(1)} %get-tuple-element.68.refs_0_), custom_call_target="tpu_custom_call" | custom-call | flops 1 | bytes 1 | tf_op jit(solution)/shard_map/target_part/pallas_call | solution.py:409
  122.0 0.4 collective-permute-start.19
  122.5 1.4 collective-permute-done.19.refs_2_
  123.9 1.0 copy-done.11
  124.9 11.1 %left_grads.1 = (bf16[4,256,128]{2,1,0:T(8,128)(2,1)S(1)}, bf16[8,256,512]{2,1,0:T(8,128)(2,1)S(1)}) custom-call(s32[4]{0:T(128)S(1)} %pad_add_fusion.idx_ref, bf16[128,1792]{1,0:T(8,128)(2,1)S(1)} %collective-permute-done.16.refs_0_, bf16[128,1792]{1,0:T(8,128)(2,1)S(1)} %copy-done.11, bf16[128,1792]{1,0:T(8,128)(2,1)S(1)} %collective-permute-done.19.refs_2_, ...), custom_call_target="tpu_custom_call" | custom-call | flops 1 | bytes 1 | tf_op jit(solution)/shard_map/left_grads/pallas_call | solution.py:621
  136.1 0.4 collective-permute-start.21
  136.5 3.4 %right_grads.2 = bf16[2,512,128]{2,1,0:T(8,128)(2,1)S(1)} custom-call(s32[4]{0:T(128)S(1)} %pad_add_fusion.idx_ref, bf16[128,8192]{1,0:T(8,128)(2,1)S(1)} %copy-done.1, bf16[128,8192]{1,0:T(8,128)(2,1)S(1)} %copy-done.1, bf16[128,8192]{1,0:T(8,128)(2,1)} %collective-permute-done.refs_2_.refs_3_, bf16[128,8192]{1,0:T(8,128)(2,1)} %collective-permute-done.refs_2_.refs_3_, ...), custom_call_target="tpu_custom_call" | custom-call | flops 1 | bytes 1 | tf_op jit(solution)/shard_map/right_grads/pallas_call | solution.py:675
  139.8 1.8 %collective-permute-start.22 = (bf16[2,512,128]{2,1,0:T(8,128)(2,1)S(1)}, bf16[2,512,128]{2,1,0:T(8,128)(2,1)S(1)}, u32[]{:S(2)}, u32[]{:S(2)}) collective-permute-start(bf16[2,512,128]{2,1,0:T(8,128)(2,1)S(1)} %right_grads.2), channel_id=1, source_target_pairs={{0,1},{1,0},{2,3},{3,2},{4,5},{5,4},{6,7},{7,6},{8,9},{9,8},{10,11... | collective-permute-start | bytes 786440 | tf_op jit(solution)/shard_map/ppermute | solution.py:709
  141.6 0.3 collective-permute-done.21
  142.0 0.9 collective-permute-start.25
  142.9 3.4 %right_grads.3 = bf16[2,512,128]{2,1,0:T(8,128)(2,1)S(1)} custom-call(s32[4]{0:T(128)S(1)} %pad_add_fusion.idx_ref, bf16[128,8192]{1,0:T(8,128)(2,1)S(1)} %copy-done.1, bf16[128,8192]{1,0:T(8,128)(2,1)S(1)} %copy-done.1, bf16[128,8192]{1,0:T(8,128)(2,1)} %collective-permute-done.refs_2_.refs_3_, bf16[128,8192]{1,0:T(8,128)(2,1)} %collective-permute-done.refs_2_.refs_3_, ...), custom_call_target="tpu_custom_call" | custom-call | flops 10000000000 | bytes 10000000 | tf_op jit(solution)/shard_map/right_grads/pallas_call | solution.py:675
  146.3 3.3 %collective-permute-done.22 = bf16[2,512,128]{2,1,0:T(8,128)(2,1)S(1)} collective-permute-done((bf16[2,512,128]{2,1,0:T(8,128)(2,1)S(1)}, bf16[2,512,128]{2,1,0:T(8,128)(2,1)S(1)}, u32[]{:S(2)}, u32[]{:S(2)}) %collective-permute-start.22) | collective-permute-done | bytes 262176 | tf_op jit(solution)/shard_map/ppermute | solution.py:709
  149.6 0.1 add_convert_fusion
  149.7 0.7 collective-permute-start.23
  150.4 4.3 %collective-permute-start.24 = (bf16[512,128]{1,0:T(8,128)(2,1)S(1)}, bf16[512,128]{1,0:T(8,128)(2,1)S(1)}, u32[]{:S(2)}, u32[]{:S(2)}) collective-permute-start(bf16[512,128]{1,0:T(8,128)(2,1)S(1)} %get-tuple-element.77), channel_id=1, source_target_pairs={{0,8},{1,12},{2,0},{3,4},{4,9},{5,13},{6,1},{7,5},{8,10},{9,14},{1... | collective-permute-start | bytes 393224 | tf_op jit(solution)/shard_map/ppermute | solution.py:716
  154.8 0.2 reshape.32
  155.0 0.7 copy.8
  155.7 10.0 %collective-permute-done.24 = bf16[512,128]{1,0:T(8,128)(2,1)S(1)} collective-permute-done((bf16[512,128]{1,0:T(8,128)(2,1)S(1)}, bf16[512,128]{1,0:T(8,128)(2,1)S(1)}, u32[]{:S(2)}, u32[]{:S(2)}) %collective-permute-start.24) | collective-permute-done | bytes 131104 | tf_op jit(solution)/shard_map/ppermute | solution.py:716
  165.7 0.7 convert_add_fusion.2
  (53 shorter events, 0.3 us)
Async XLA Ops:
  0.6 8.4 %copy-start = (bf16[128,8192]{1,0:T(8,128)(2,1)S(1)}, bf16[128,8192]{1,0:T(8,128)(2,1)}, u32[]{:S(2)}) copy-start(bf16[128,8192]{1,0:T(8,128)(2,1)} %refs_1_.9) | copy-start | bytes 6291460
  0.6 8.3 %collective-permute-start = (bf16[128,8192]{1,0:T(8,128)(2,1)}, bf16[128,8192]{1,0:T(8,128)(2,1)}, u32[]{:S(2)}, u32[]{:S(2)}) collective-permute-start(bf16[128,8192]{1,0:T(8,128)(2,1)} %refs_1_.9), channel_id=1, source_target_pairs={{0,4},{4,0},{8,12},{12,8},{1,5},{5,1},{9,13},{13,9},{2,6},{6,2},{1... | collective-permute-start | bytes 6291464 | tf_op jit(solution)/shard_map/ppermute | solution.py:703
  5.8 28.7 %collective-permute-start.1 = (bf16[128,4096]{1,0:T(8,128)(2,1)}, bf16[128,4096]{1,0:T(8,128)(2,1)S(1)}, u32[]{:S(2)}, u32[]{:S(2)}) collective-permute-start(bf16[128,4096]{1,0:T(8,128)(2,1)} %cut_tokens.2), channel_id=1, source_target_pairs={{0,8},{4,12},{8,0},{12,4},{1,9},{5,13},{9,1},{13,5},{2,10},{6,14},... | collective-permute-start | bytes 3145736 | tf_op jit(solution)/shard_map/ppermute | solution.py:706
  9.0 12.0 %copy-start.13 = (bf16[16,32,128]{2,1,0:T(8,128)(2,1)S(1)}, bf16[16,32,128]{2,1,0:T(8,128)(2,1)}, u32[]{:S(2)}) copy-start(bf16[16,32,128]{2,1,0:T(8,128)(2,1)} %param.10) | copy-start | bytes 393220
  19.8 1.0 copy-start.4
  20.8 9.7 %collective-permute-start.4 = (bf16[2,128,1792]{2,1,0:T(8,128)(2,1)}, bf16[2,128,1792]{2,1,0:T(8,128)(2,1)S(1)}, u32[]{:S(2)}, u32[]{:S(2)}) collective-permute-start(bf16[2,128,1792]{2,1,0:T(8,128)(2,1)} %bitcast.11), channel_id=1, source_target_pairs={{0,4},{4,0},{8,12},{12,8},{1,5},{5,1},{9,13},{13,9},{2,6},{6,2},{1... | collective-permute-start | bytes 2752520 | tf_op jit(solution)/shard_map/ppermute | solution.py:703
  21.0 6.3 %collective-permute-start.2 = (bf16[16,32,128]{2,1,0:T(8,128)(2,1)S(1)}, bf16[16,32,128]{2,1,0:T(8,128)(2,1)S(1)}, u32[]{:S(2)}, u32[]{:S(2)}) collective-permute-start(bf16[16,32,128]{2,1,0:T(8,128)(2,1)S(1)} %copy-done.13), channel_id=1, source_target_pairs={{0,0},{1,4},{2,8},{3,12},{4,1},{5,5},{6,9},{7,13},{8,2},{9,6},{10,... | collective-permute-start | bytes 393224 | tf_op jit(solution)/shard_map/ppermute | solution.py:716
  23.3 4.0 %copy-start.12 = (bf16[256,128]{1,0:T(8,128)(2,1)S(1)}, bf16[256,128]{1,0:T(8,128)(2,1)}, u32[]{:S(2)}) copy-start(bf16[256,128]{1,0:T(8,128)(2,1)} %pack_left.1) | copy-start | bytes 196612
  23.3 7.2 %copy-start.5 = (bf16[1,2,128,1792]{3,2,1,0:T(8,128)(2,1)S(1)}, bf16[1,2,128,1792]{3,2,1,0:T(8,128)(2,1)}, u32[]{:S(2)}) copy-start(bf16[1,2,128,1792]{3,2,1,0:T(8,128)(2,1)} %copy-done.4) | copy-start | bytes 2752516
  27.3 8.8 %collective-permute-start.3 = (bf16[1,768,128]{2,1,0:T(8,128)(2,1)S(1)}, bf16[1,768,128]{2,1,0:T(8,128)(2,1)S(1)}, u32[]{:S(2)}, u32[]{:S(2)}) collective-permute-start(bf16[1,768,128]{2,1,0:T(8,128)(2,1)S(1)} %maximum_bitcast_fusion), channel_id=1, source_target_pairs={{0,1},{1,0},{2,3},{3,2},{4,5},{5,4},{6,7},{7,6},{8,9},{9,8},{10,11... | collective-permute-start | bytes 589832 | tf_op jit(solution)/shard_map/ppermute | solution.py:709
  36.1 4.7 %collective-permute-start.5 = (bf16[128,4096]{1,0:T(8,128)(2,1)S(1)}, bf16[128,4096]{1,0:T(8,128)(2,1)S(1)}, u32[]{:S(2)}, u32[]{:S(2)}) collective-permute-start(bf16[128,4096]{1,0:T(8,128)(2,1)S(1)} %collective-permute-done.1.refs_0_.refs_1_.refs_4_.refs_5_), channel_id=1, source_target_pairs={{0,4},{4,0},{8,12},{12,8},{1,5},{5,1},{9,13},{13,9},{2,6},{6,2},{1... | collective-permute-start | bytes 3145736 | tf_op jit(solution)/shard_map/ppermute | solution.py:703
  36.5 14.5 %copy-start.1 = (bf16[128,8192]{1,0:T(8,128)(2,1)S(1)}, bf16[128,8192]{1,0:T(8,128)(2,1)}, u32[]{:S(2)}) copy-start(bf16[128,8192]{1,0:T(8,128)(2,1)} %refs_1_.9) | copy-start | bytes 6291460
  36.5 36.7 %collective-permute-start.7 = (bf16[2,128,1792]{2,1,0:T(8,128)(2,1)}, bf16[2,128,1792]{2,1,0:T(8,128)(2,1)S(1)}, u32[]{:S(2)}, u32[]{:S(2)}) collective-permute-start(bf16[2,128,1792]{2,1,0:T(8,128)(2,1)} %fusion.1), channel_id=1, source_target_pairs={{0,8},{4,12},{8,0},{12,4},{1,9},{5,13},{9,1},{13,5},{2,10},{6,14},... | collective-permute-start | bytes 2752520 | tf_op jit(solution)/shard_map/ppermute | solution.py:706
  40.7 32.5 %collective-permute-start.6 = (bf16[64,4096]{1,0:T(8,128)(2,1)}, bf16[64,4096]{1,0:T(8,128)(2,1)S(1)}, u32[]{:S(2)}, u32[]{:S(2)}) collective-permute-start(bf16[64,4096]{1,0:T(8,128)(2,1)} %cut_tokens.3), channel_id=1, source_target_pairs={{0,8},{4,12},{8,0},{12,4},{1,9},{5,13},{9,1},{13,5},{2,10},{6,14},... | collective-permute-start | bytes 1572872 | tf_op jit(solution)/shard_map/ppermute | solution.py:706
  50.7 12.7 %collective-permute-start.8 = (bf16[2,128,1792]{2,1,0:T(8,128)(2,1)S(1)}, bf16[2,128,1792]{2,1,0:T(8,128)(2,1)S(1)}, u32[]{:S(2)}, u32[]{:S(2)}) collective-permute-start(bf16[2,128,1792]{2,1,0:T(8,128)(2,1)S(1)} %bitcast.58), channel_id=1, source_target_pairs={{0,4},{4,0},{8,12},{12,8},{1,5},{5,1},{9,13},{13,9},{2,6},{6,2},{1... | collective-permute-start | bytes 2752520 | tf_op jit(solution)/shard_map/ppermute | solution.py:703
  73.1 3.8 %collective-permute-start.9 = (bf16[2,2,128,1792]{3,2,1,0:T(8,128)(2,1)S(1)}, bf16[2,2,128,1792]{3,2,1,0:T(8,128)(2,1)S(1)}, u32[]{:S(2)}, u32[]{:S(2)}) collective-permute-start(bf16[2,2,128,1792]{3,2,1,0:T(8,128)(2,1)S(1)} %get-tuple-element.55), channel_id=1, source_target_pairs={{0,4},{4,0},{8,12},{12,8},{1,5},{5,1},{9,13},{13,9},{2,6},{6,2},{1... | collective-permute-start | bytes 5505032 | tf_op jit(solution)/shard_map/ppermute | solution.py:703
  73.3 37.7 %collective-permute-start.12 = (bf16[64,4096]{1,0:T(8,128)(2,1)S(1)}, bf16[64,4096]{1,0:T(8,128)(2,1)S(1)}, u32[]{:S(2)}, u32[]{:S(2)}) collective-permute-start(bf16[64,4096]{1,0:T(8,128)(2,1)S(1)} %collective-permute-done.6.refs_4_.refs_8_), channel_id=1, source_target_pairs={{0,4},{4,0},{8,12},{12,8},{1,5},{5,1},{9,13},{13,9},{2,6},{6,2},{1... | collective-permute-start | bytes 1572872 | tf_op jit(solution)/shard_map/ppermute | solution.py:703
  73.8 20.4 %collective-permute-start.11 = (bf16[2,768,128]{2,1,0:T(8,128)(2,1)S(1)}, bf16[2,768,128]{2,1,0:T(8,128)(2,1)S(1)}, u32[]{:S(2)}, u32[]{:S(2)}) collective-permute-start(bf16[2,768,128]{2,1,0:T(8,128)(2,1)S(1)} %pad_maximum_fusion), channel_id=1, source_target_pairs={{0,2},{1,3},{2,0},{3,1},{4,6},{5,7},{6,4},{7,5},{8,10},{9,11},{10,... | collective-permute-start | bytes 1179656 | tf_op jit(solution)/shard_map/ppermute | solution.py:709
  75.6 29.3 %collective-permute-start.14 = (bf16[2,128,1792]{2,1,0:T(8,128)(2,1)S(1)}, bf16[2,128,1792]{2,1,0:T(8,128)(2,1)S(1)}, u32[]{:S(2)}, u32[]{:S(2)}) collective-permute-start(bf16[2,128,1792]{2,1,0:T(8,128)(2,1)S(1)} %fusion), channel_id=1, source_target_pairs={{0,8},{4,12},{8,0},{12,4},{1,9},{5,13},{9,1},{13,5},{2,10},{6,14},... | collective-permute-start | bytes 2752520 | tf_op jit(solution)/shard_map/ppermute | solution.py:706
  77.5 22.1 %collective-permute-start.15 = (bf16[128,1792]{1,0:T(8,128)(2,1)S(1)}, bf16[128,1792]{1,0:T(8,128)(2,1)S(1)}, u32[]{:S(2)}, u32[]{:S(2)}) collective-permute-start(bf16[128,1792]{1,0:T(8,128)(2,1)S(1)} %fusion.5.mine_ref), channel_id=1, source_target_pairs={{0,4},{4,0},{8,12},{12,8},{1,5},{5,1},{9,13},{13,9},{2,6},{6,2},{1... | collective-permute-start | bytes 1376264 | tf_op jit(solution)/shard_map/ppermute | solution.py:703
  77.7 38.8 %collective-permute-start.18 = (bf16[128,1792]{1,0:T(8,128)(2,1)S(1)}, bf16[128,1792]{1,0:T(8,128)(2,1)S(1)}, u32[]{:S(2)}, u32[]{:S(2)}) collective-permute-start(bf16[128,1792]{1,0:T(8,128)(2,1)S(1)} %fusion.5.mine_ref), channel_id=1, source_target_pairs={{0,8},{4,12},{8,0},{12,4},{1,9},{5,13},{9,1},{13,5},{2,10},{6,14},... | collective-permute-start | bytes 1376264 | tf_op jit(solution)/shard_map/ppermute | solution.py:706
  94.3 13.4 %collective-permute-start.10 = (bf16[64,4096]{1,0:T(8,128)(2,1)S(1)}, bf16[64,4096]{1,0:T(8,128)(2,1)S(1)}, u32[]{:S(2)}, u32[]{:S(2)}) collective-permute-start(bf16[64,4096]{1,0:T(8,128)(2,1)S(1)} %collective-permute-done.6.refs_4_.refs_8_), channel_id=1, source_target_pairs={{0,1},{1,0},{2,3},{3,2},{4,5},{5,4},{6,7},{7,6},{8,9},{9,8},{10,11... | collective-permute-start | bytes 1572872 | tf_op jit(solution)/shard_map/ppermute | solution.py:709
  107.7 3.3 %copy-start.8 = (bf16[64,4096]{1,0:T(8,128)(2,1)}, bf16[64,4096]{1,0:T(8,128)(2,1)S(1)}, u32[]{:S(2)}) copy-start(bf16[64,4096]{1,0:T(8,128)(2,1)S(1)} %collective-permute-done.10.refs_5_.refs_9_) | copy-start | bytes 1572868
  107.7 3.3 %collective-permute-start.13 = (bf16[64,4096]{1,0:T(8,128)(2,1)S(1)}, bf16[64,4096]{1,0:T(8,128)(2,1)S(1)}, u32[]{:S(2)}, u32[]{:S(2)}) collective-permute-start(bf16[64,4096]{1,0:T(8,128)(2,1)S(1)} %collective-permute-done.10.refs_5_.refs_9_), channel_id=1, source_target_pairs={{0,4},{4,0},{8,12},{12,8},{1,5},{5,1},{9,13},{13,9},{2,6},{6,2},{1... | collective-permute-start | bytes 1572872 | tf_op jit(solution)/shard_map/ppermute | solution.py:703
  108.2 8.3 %collective-permute-start.17 = (bf16[128,1792]{1,0:T(8,128)(2,1)S(1)}, bf16[128,1792]{1,0:T(8,128)(2,1)S(1)}, u32[]{:S(2)}, u32[]{:S(2)}) collective-permute-start(bf16[128,1792]{1,0:T(8,128)(2,1)S(1)} %fusion.3.mine_ref), channel_id=1, source_target_pairs={{0,4},{4,0},{8,12},{12,8},{1,5},{5,1},{9,13},{13,9},{2,6},{6,2},{1... | collective-permute-start | bytes 1376264 | tf_op jit(solution)/shard_map/ppermute | solution.py:703
  108.8 13.2 %collective-permute-start.16 = (bf16[128,1792]{1,0:T(8,128)(2,1)S(1)}, bf16[128,1792]{1,0:T(8,128)(2,1)S(1)}, u32[]{:S(2)}, u32[]{:S(2)}) collective-permute-start(bf16[128,1792]{1,0:T(8,128)(2,1)S(1)} %fusion.3.mine_ref), channel_id=1, source_target_pairs={{0,8},{4,12},{8,0},{12,4},{1,9},{5,13},{9,1},{13,5},{2,10},{6,14},... | collective-permute-start | bytes 1376264 | tf_op jit(solution)/shard_map/ppermute | solution.py:706
  111.0 4.6 %copy-start.6 = (bf16[64,4096]{1,0:T(8,128)(2,1)}, bf16[64,4096]{1,0:T(8,128)(2,1)S(1)}, u32[]{:S(2)}) copy-start(bf16[64,4096]{1,0:T(8,128)(2,1)S(1)} %collective-permute-done.12.refs_6_.refs_10_) | copy-start | bytes 1572868
  115.5 1.0 copy-start.2
  116.5 5.5 %copy-start.10 = (bf16[128,1792]{1,0:T(8,128)(2,1)}, bf16[128,1792]{1,0:T(8,128)(2,1)S(1)}, u32[]{:S(2)}) copy-start(bf16[128,1792]{1,0:T(8,128)(2,1)S(1)} %collective-permute-done.18.refs_1_) | copy-start | bytes 1376260
  116.5 6.0 %collective-permute-start.20 = (bf16[128,1792]{1,0:T(8,128)(2,1)S(1)}, bf16[128,1792]{1,0:T(8,128)(2,1)S(1)}, u32[]{:S(2)}, u32[]{:S(2)}) collective-permute-start(bf16[128,1792]{1,0:T(8,128)(2,1)S(1)} %collective-permute-done.18.refs_1_), channel_id=1, source_target_pairs={{0,4},{4,0},{8,12},{12,8},{1,5},{5,1},{9,13},{13,9},{2,6},{6,2},{1... | collective-permute-start | bytes 1376264 | tf_op jit(solution)/shard_map/ppermute | solution.py:703
  116.5 7.4 %copy-start.3 = (bf16[8,256,256]{2,1,0:T(8,128)(2,1)S(1)}, bf16[8,256,256]{2,1,0:T(8,128)(2,1)}, u32[]{:S(2)}) copy-start(bf16[8,256,256]{2,1,0:T(8,128)(2,1)} %copy-done.2) | copy-start | bytes 3145732
  122.0 1.9 %collective-permute-start.19 = (bf16[128,1792]{1,0:T(8,128)(2,1)S(1)}, bf16[128,1792]{1,0:T(8,128)(2,1)S(1)}, u32[]{:S(2)}, u32[]{:S(2)}) collective-permute-start(bf16[128,1792]{1,0:T(8,128)(2,1)S(1)} %collective-permute-done.16.refs_0_), channel_id=1, source_target_pairs={{0,4},{4,0},{8,12},{12,8},{1,5},{5,1},{9,13},{13,9},{2,6},{6,2},{1... | collective-permute-start | bytes 1376264 | tf_op jit(solution)/shard_map/ppermute | solution.py:703
  123.9 1.0 copy-start.11
  124.9 11.5 %copy-start.7 = (bf16[64,4096]{1,0:T(8,128)(2,1)S(1)}, bf16[64,4096]{1,0:T(8,128)(2,1)}, u32[]{:S(2)}) copy-start(bf16[64,4096]{1,0:T(8,128)(2,1)} %copy-done.6) | copy-start | bytes 1572868
  124.9 11.5 %copy-start.9 = (bf16[64,4096]{1,0:T(8,128)(2,1)S(1)}, bf16[64,4096]{1,0:T(8,128)(2,1)}, u32[]{:S(2)}) copy-start(bf16[64,4096]{1,0:T(8,128)(2,1)} %copy-done.8) | copy-start | bytes 1572868
  136.1 5.8 %collective-permute-start.21 = (bf16[2,256,128]{2,1,0:T(8,128)(2,1)S(1)}, bf16[2,256,128]{2,1,0:T(8,128)(2,1)S(1)}, u32[]{:S(2)}, u32[]{:S(2)}) collective-permute-start(bf16[2,256,128]{2,1,0:T(8,128)(2,1)S(1)} %slice.51), channel_id=1, source_target_pairs={{0,1},{1,0},{2,3},{3,2},{4,5},{5,4},{6,7},{7,6},{8,9},{9,8},{10,11... | collective-permute-start | bytes 393224 | tf_op jit(solution)/shard_map/ppermute | solution.py:709
  139.8 9.8 %collective-permute-start.22 = (bf16[2,512,128]{2,1,0:T(8,128)(2,1)S(1)}, bf16[2,512,128]{2,1,0:T(8,128)(2,1)S(1)}, u32[]{:S(2)}, u32[]{:S(2)}) collective-permute-start(bf16[2,512,128]{2,1,0:T(8,128)(2,1)S(1)} %right_grads.2), channel_id=1, source_target_pairs={{0,1},{1,0},{2,3},{3,2},{4,5},{5,4},{6,7},{7,6},{8,9},{9,8},{10,11... | collective-permute-start | bytes 786440 | tf_op jit(solution)/shard_map/ppermute | solution.py:709
  142.0 12.8 %collective-permute-start.25 = (bf16[256,128]{1,0:T(8,128)(2,1)S(1)}, bf16[256,128]{1,0:T(8,128)(2,1)S(1)}, u32[]{:S(2)}, u32[]{:S(2)}) collective-permute-start(bf16[256,128]{1,0:T(8,128)(2,1)S(1)} %slice_bitcast_fusion.6), channel_id=1, source_target_pairs={{0,2},{1,3},{2,0},{3,1},{4,6},{5,7},{6,4},{7,5},{8,10},{9,11},{10,... | collective-permute-start | bytes 196616 | tf_op jit(solution)/shard_map/ppermute | solution.py:709
  149.7 6.0 %collective-permute-start.23 = (bf16[512,128]{1,0:T(8,128)(2,1)S(1)}, bf16[512,128]{1,0:T(8,128)(2,1)S(1)}, u32[]{:S(2)}, u32[]{:S(2)}) collective-permute-start(bf16[512,128]{1,0:T(8,128)(2,1)S(1)} %get-tuple-element.76), channel_id=1, source_target_pairs={{0,0},{1,4},{2,8},{3,12},{4,1},{5,5},{6,9},{7,13},{8,2},{9,6},{10,... | collective-permute-start | bytes 393224 | tf_op jit(solution)/shard_map/ppermute | solution.py:716
  150.4 15.3 %collective-permute-start.24 = (bf16[512,128]{1,0:T(8,128)(2,1)S(1)}, bf16[512,128]{1,0:T(8,128)(2,1)S(1)}, u32[]{:S(2)}, u32[]{:S(2)}) collective-permute-start(bf16[512,128]{1,0:T(8,128)(2,1)S(1)} %get-tuple-element.77), channel_id=1, source_target_pairs={{0,8},{1,12},{2,0},{3,4},{4,9},{5,13},{6,1},{7,5},{8,10},{9,14},{1... | collective-permute-start | bytes 393224 | tf_op jit(solution)/shard_map/ppermute | solution.py:716

commit v13 on v12

--- a/solution.py
+++ b/solution.py
@@ -757,14 +757,14 @@
     late_pieces = [(t, row, 3) for t in (arrived, near_arrived) for row in (0, 1)]
     late_order = after(scalars(other_block), rest)
     mine, other = products(late_pieces, late_order, gate_weight, up_weight, 0, part)
-    near = swap(other[0])
+    near = swap(after(other[0], late_first))
     mine_order = after(scalars(mine_block), mine)
     kept, other = products(
         own_pieces + late_pieces, mine_order, gate_weight, up_weight, 0, part
     )
     sums = add(mine[0], after(near, kept)).astype(BF16)
     got = across(sums)
-    near_kept = swap(after(other, got_early, late_first, sums))
+    near_kept = swap(after(other, got_early, sums))
     factors = after(factors, kept)
     more = along(factors, 2)
 
@@ -773,13 +773,13 @@
         return (jax.nn.silu(total[0]) * total[1]).astype(BF16)
 
     hidden1 = activate(1, got_early)
-    got1 = across(hidden1)
     near1 = swap(hidden1)
-    late_partner = along(after(late_first, hidden1), 1)
+    late_partner = along(after(late_first, kept), 1)
     factors = jnp.concatenate([factors, after(more, hidden1)], axis=0)
     mixed0, rest0, left_diag = student_part(
         [after(tokens, hidden1, sums)] + own[1:], order, factors, pairs, tensor_count
     )
+    got1 = across(after(hidden1, mixed0))
     target1 = target_part(1.0, [], hidden1, after(near1, mixed0), down_weight, chip)
     hidden0 = activate(0, after(got, target1))
     got0 = across(hidden0)

time: 167 us -> 167 us (level)
    ppermute x6, waiting for transfers between devices: 22.8 us -> 20.2 us  [along(): lax.ppermute(value, 'tensor', [(i, i ^ bit) for i in range(tensor_count)])]
    ppermute x6, starting transfers between devices: 8.05 us -> 10.5 us  [along(): lax.ppermute(value, 'tensor', [(i, i ^ bit) for i in range(tensor_count)])]
    ppermute x6, waiting for transfers between devices: 12.4 us -> 14.7 us  [across(): return lax.ppermute(value, 'fsdp', [(i, i ^ 2) for i in range(fsdp_count)])]
    ppermute x6, starting transfers between devices: 11 us -> 9.14 us  [across(): return lax.ppermute(value, 'fsdp', [(i, i ^ 2) for i in range(fsdp_count)])]
  transfers between devices with their start and end apart: 26 -> 26, of which waited for: 10 -> 9; matrix products, arithmetic and copies ran while one was open for 3% -> 3% of each run, Pallas kernels for 42% -> 43%
where the time goes in v13:
time: 167 us; the launch traced here: 166 us
  Pallas kernels  82.2 us (49%)
  waiting for transfers between devices  46.7 us (28%)
  starting transfers between devices  27.9 us (17%)
  other arithmetic  4.71 us (3%)
  local copies, waits for them, and re-layouts  3.18 us (2%)
    pallas_call x3, Pallas kernels, products(): pl.pallas_call(functools.partial(products_kernel, sets), grid_spec=pltpu....  33.1 us
    ppermute x6, waiting for transfers between devices, along(): lax.ppermute(value, 'tensor', [(i, i ^ bit) for i in range(tensor_count)])  20.2 us
    ppermute x6, waiting for transfers between devices, across(): return lax.ppermute(value, 'fsdp', [(i, i ^ 2) for i in range(fsdp_count)])  14.7 us
    pallas_call x1, Pallas kernels, left_grads(): pl.pallas_call(functools.partial(left_kernel, chunks, scale), grid_spec=p...  11.1 us
    pallas_call x2, Pallas kernels, target_part(): pl.pallas_call(functools.partial(target_kernel, sign), grid_spec=pltpu.Pr...  10.7 us
    pallas_call x2, Pallas kernels, student_part(): pl.pallas_call(functools.partial(student_kernel, steps, bool(late), tenso...  10.6 us
    ppermute x6, starting transfers between devices, along(): lax.ppermute(value, 'tensor', [(i, i ^ bit) for i in range(tensor_count)])  10.5 us
    ppermute x3, waiting for transfers between devices, turn(): return lax.ppermute(value, both_axes, perm)  10 us
  transfers between devices with their start and end apart: 26, of which 9 were waited for; matrix products, arithmetic and copies ran while one was open for 3% of the time, Pallas kernels for 43%

profile of v13, /device:TPU:0, one launch (start us, length us, event | category | flops | bytes accessed | tf_op | source)
XLA Modules:
  0.0 165.7 jit_solution(9975780897404828404)
XLA Ops:
  0.6 0.0 copy-start
  0.6 0.5 collective-permute-start
  1.2 0.6 pad_add_fusion.1.idx_ref
  1.7 4.1 %cut_tokens.2 = bf16[128,4096]{1,0:T(8,128)(2,1)} custom-call(s32[2]{0:T(128)} %pad_add_fusion.1.idx_ref, bf16[128,8192]{1,0:T(8,128)(2,1)} %refs_1_.9), custom_call_target="tpu_custom_call" | custom-call | flops 1 | bytes 1 | tf_op jit(solution)/shard_map/cut_tokens/pallas_call | solution.py:312
  5.9 2.5 %collective-permute-start.1 = (bf16[128,4096]{1,0:T(8,128)(2,1)}, bf16[128,4096]{1,0:T(8,128)(2,1)S(1)}, u32[]{:S(2)}, u32[]{:S(2)}) collective-permute-start(bf16[128,4096]{1,0:T(8,128)(2,1)} %cut_tokens.2), channel_id=1, source_target_pairs={{0,8},{4,12},{8,0},{12,4},{1,9},{5,13},{9,1},{13,5},{2,10},{6,14},... | collective-permute-start | bytes 3145736 | tf_op jit(solution)/shard_map/ppermute | solution.py:706
  8.4 0.1 concatenate.24.idx_ref
  8.4 0.6 pad_add_fusion.2.idx_ref
  9.1 0.0 collective-permute-done.refs_2_.refs_3_
  9.1 10.8 %gate_up_products.3 = (bf16[1,2,128,1792]{3,2,1,0:T(8,128)(2,1)S(1)}, bf16[1,2,128,1792]{3,2,1,0:T(8,128)(2,1)}) custom-call(s32[5]{0:T(128)S(1)} %concatenate.24.idx_ref, bf16[128,8192]{1,0:T(8,128)(2,1)S(1)} %copy-done, bf16[128,8192]{1,0:T(8,128)(2,1)S(1)} %copy-done, bf16[128,8192]{1,0:T(8,128)(2,1)} %collective-permute-done.refs_2_.refs_3_, ...), custom_call_target="tpu_custom_call" | custom-call | flops 1 | bytes 1 | tf_op jit(solution)/shard_map/gate_up_products/pallas_call | solution.py:371
  19.9 1.0 copy-done.4
  20.8 0.2 collective-permute-start.4
  21.0 0.7 collective-permute-start.2
  21.7 1.6 pack_left.1
  23.3 4.0 %cut_tokens.3 = bf16[64,4096]{1,0:T(8,128)(2,1)} custom-call(s32[2]{0:T(128)} %pad_add_fusion.2.idx_ref, bf16[128,8192]{1,0:T(8,128)(2,1)} %refs_1_.9), custom_call_target="tpu_custom_call" | custom-call | flops 1 | bytes 1 | tf_op jit(solution)/shard_map/cut_tokens/pallas_call | solution.py:312
  27.3 0.0 collective-permute-done.2
  27.4 3.2 %collective-permute-start.3 = (bf16[1,768,128]{2,1,0:T(8,128)(2,1)S(1)}, bf16[1,768,128]{2,1,0:T(8,128)(2,1)S(1)}, u32[]{:S(2)}, u32[]{:S(2)}) collective-permute-start(bf16[1,768,128]{2,1,0:T(8,128)(2,1)S(1)} %maximum_bitcast_fusion), channel_id=1, source_target_pairs={{0,1},{1,0},{2,3},{3,2},{4,5},{5,4},{6,7},{7,6},{8,9},{9,8},{10,11... | collective-permute-start | bytes 589832 | tf_op jit(solution)/shard_map/ppermute | solution.py:709
  30.6 1.1 fusion.1
  31.7 2.8 %collective-permute-done.1.refs_0_.refs_1_.refs_4_.refs_5_ = bf16[128,4096]{1,0:T(8,128)(2,1)S(1)} collective-permute-done((bf16[128,4096]{1,0:T(8,128)(2,1)}, bf16[128,4096]{1,0:T(8,128)(2,1)S(1)}, u32[]{:S(2)}, u32[]{:S(2)}) %collective-permute-start.1) | collective-permute-done | bytes 1048608 | tf_op jit(solution)/shard_map/ppermute | solution.py:706
  34.6 1.6 collective-permute-done.3
  36.2 0.3 collective-permute-start.5
  36.5 4.2 %collective-permute-start.6 = (bf16[64,4096]{1,0:T(8,128)(2,1)}, bf16[64,4096]{1,0:T(8,128)(2,1)}, u32[]{:S(2)}, u32[]{:S(2)}) collective-permute-start(bf16[64,4096]{1,0:T(8,128)(2,1)} %cut_tokens.3), channel_id=1, source_target_pairs={{0,8},{4,12},{8,0},{12,4},{1,9},{5,13},{9,1},{13,5},{2,10},{6,14},... | collective-permute-start | bytes 1572872 | tf_op jit(solution)/shard_map/ppermute | solution.py:706
  40.7 0.1 concatenate.26.idx_ref
  40.7 0.0 collective-permute-start.8
  40.8 10.0 %gate_up_products.4 = (bf16[1,2,128,1792]{3,2,1,0:T(8,128)(2,1)S(1)}, bf16[1,2,128,1792]{3,2,1,0:T(8,128)(2,1)S(1)}) custom-call(s32[5]{0:T(128)S(1)} %concatenate.24.idx_ref, bf16[128,4096]{1,0:T(8,128)(2,1)S(1)} %collective-permute-done.1.refs_0_.refs_1_.refs_4_.refs_5_, bf16[128,4096]{1,0:T(8,128)(2,1)S(1)} %collective-permute-done.1.refs_0_.refs_1_.refs_4_.refs_5_, ...), custom_call_target="tpu_custom_call" | custom-call | flops 1 | bytes 1 | tf_op jit(solution)/shard_map/gate_up_products/pallas_call | solution.py:371
  50.8 3.0 %collective-permute-done.6.refs_4_.refs_8_ = bf16[64,4096]{1,0:T(8,128)(2,1)} collective-permute-done((bf16[64,4096]{1,0:T(8,128)(2,1)}, bf16[64,4096]{1,0:T(8,128)(2,1)}, u32[]{:S(2)}, u32[]{:S(2)}) %collective-permute-start.6) | collective-permute-done | bytes 524320 | tf_op jit(solution)/shard_map/ppermute | solution.py:706
  53.7 12.4 %gate_up_products.5 = (bf16[2,2,128,1792]{3,2,1,0:T(8,128)(2,1)S(1)}, bf16[2,2,128,1792]{3,2,1,0:T(8,128)(2,1)S(1)}) custom-call(s32[5]{0:T(128)S(1)} %concatenate.26.idx_ref, bf16[128,8192]{1,0:T(8,128)(2,1)S(1)} %copy-done.1, bf16[128,8192]{1,0:T(8,128)(2,1)S(1)} %copy-done.1, bf16[128,8192]{1,0:T(8,128)(2,1)} %collective-permute-done.refs_2_.refs_3_, ...), custom_call_target="tpu_custom_call" | custom-call | flops 10000000000 | bytes 10000000 | tf_op jit(solution)/shard_map/gate_up_products/pallas_call | solution.py:371
  66.1 0.2 fusion
  66.4 6.8 %collective-permute-done.8 = bf16[2,128,1792]{2,1,0:T(8,128)(2,1)S(1)} collective-permute-done((bf16[2,128,1792]{2,1,0:T(8,128)(2,1)}, bf16[2,128,1792]{2,1,0:T(8,128)(2,1)S(1)}, u32[]{:S(2)}, u32[]{:S(2)}) %collective-permute-start.8) | collective-permute-done | bytes 917536 | tf_op jit(solution)/shard_map/ppermute | solution.py:706
  73.1 0.1 pad_add_fusion.idx_ref
  73.2 0.6 collective-permute-start.12
  73.8 1.7 %collective-permute-start.11 = (bf16[2,768,128]{2,1,0:T(8,128)(2,1)S(1)}, bf16[2,768,128]{2,1,0:T(8,128)(2,1)S(1)}, u32[]{:S(2)}, u32[]{:S(2)}) collective-permute-start(bf16[2,768,128]{2,1,0:T(8,128)(2,1)S(1)} %pad_maximum_fusion), channel_id=1, source_target_pairs={{0,2},{1,3},{2,0},{3,1},{4,6},{5,7},{6,4},{7,5},{8,10},{9,11},{10,... | collective-permute-start | bytes 1179656 | tf_op jit(solution)/shard_map/ppermute | solution.py:709
  75.5 1.9 %collective-permute-start.7 = (bf16[64,4096]{1,0:T(8,128)(2,1)}, bf16[64,4096]{1,0:T(8,128)(2,1)S(1)}, u32[]{:S(2)}, u32[]{:S(2)}) collective-permute-start(bf16[64,4096]{1,0:T(8,128)(2,1)} %collective-permute-done.6.refs_4_.refs_8_), channel_id=1, source_target_pairs={{0,1},{1,0},{2,3},{3,2},{4,5},{5,4},{6,7},{7,6},{8,9},{9,8},{10,11... | collective-permute-start | bytes 1572872 | tf_op jit(solution)/shard_map/ppermute | solution.py:709
  77.5 0.3 collective-permute-start.14
  77.8 0.3 bitcast_add_fusion.1
  78.1 0.3 fusion.5.mine_ref
  78.4 0.1 collective-permute-start.15
  78.5 15.9 %collective-permute-done.11 = bf16[2,768,128]{2,1,0:T(8,128)(2,1)S(1)} collective-permute-done((bf16[2,768,128]{2,1,0:T(8,128)(2,1)S(1)}, bf16[2,768,128]{2,1,0:T(8,128)(2,1)S(1)}, u32[]{:S(2)}, u32[]{:S(2)}) %collective-permute-start.11) | collective-permute-done | bytes 393248 | tf_op jit(solution)/shard_map/ppermute | solution.py:709
  94.3 0.1 constant_dynamic-update-slice_fusion.refs_4_.refs_5_.refs_6_.refs_8_.refs_9_
  94.4 5.3 %student_part.2 = (bf16[8,256,256]{2,1,0:T(8,128)(2,1)S(1)}, f32[256,2048]{1,0:T(8,128)S(1)}, bf16[8,256,256]{2,1,0:T(8,128)(2,1)S(1)}) custom-call(s32[4]{0:T(128)S(1)} %pad_add_fusion.idx_ref, bf16[128,8192]{1,0:T(8,128)(2,1)S(1)} %copy-done.1, bf16[128,8192]{1,0:T(8,128)(2,1)S(1)} %copy-done.1, bf16[128,8192]{1,0:T(8,128)(2,1)} %collective-permute-done.refs_2_.refs_3_, ...), custom_call_target="tpu_custom_call" | custom-call | flops 10000000000 | bytes 10000000 | tf_op jit(solution)/shard_map/student_part/pallas_call | solution.py:553
  99.7 1.8 %collective-permute-start.18 = (bf16[128,1792]{1,0:T(8,128)(2,1)S(1)}, bf16[128,1792]{1,0:T(8,128)(2,1)S(1)}, u32[]{:S(2)}, u32[]{:S(2)}) collective-permute-start(bf16[128,1792]{1,0:T(8,128)(2,1)S(1)} %fusion.5.mine_ref), channel_id=1, source_target_pairs={{0,8},{4,12},{8,0},{12,4},{1,9},{5,13},{9,1},{13,5},{2,10},{6,14},... | collective-permute-start | bytes 1376264 | tf_op jit(solution)/shard_map/ppermute | solution.py:706
  101.5 5.4 %target_part.2.refs_11_ = f32[256,2048]{1,0:T(8,128)S(1)} custom-call(s32[1]{0:T(128)} %bitcast.2.idx_ref, bf16[128,1792]{1,0:T(8,128)(2,1)S(1)} %fusion.5.mine_ref, bf16[128,1792]{1,0:T(8,128)(2,1)S(1)} %collective-permute-done.15.near_ref, bf16[3584,2048]{1,0:T(8,128)(2,1)} %refs_4_.5), custom_call_target="tpu_custom_call" | custom-call | flops 1 | bytes 1 | tf_op jit(solution)/shard_map/target_part/pallas_call | solution.py:409
  106.9 0.3 bitcast_add_fusion
  107.2 0.3 fusion.3.mine_ref
  107.5 0.4 collective-permute-start.17
  107.8 0.3 collective-permute-start.16
  108.2 5.3 %student_part.3 = (bf16[8,256,256]{2,1,0:T(8,128)(2,1)S(1)}, f32[256,2048]{1,0:T(8,128)S(1)}) custom-call(s32[4]{0:T(128)S(1)} %pad_add_fusion.idx_ref, bf16[128,4096]{1,0:T(8,128)(2,1)S(1)} %collective-permute-done.1.refs_0_.refs_1_.refs_4_.refs_5_, bf16[128,4096]{1,0:T(8,128)(2,1)S(1)} %collective-permute-done.1.refs_0_.refs_1_.refs_4_.refs_5_, ...), custom_call_target="tpu_custom_call" | custom-call | flops 10000000000 | bytes 10000000 | tf_op jit(solution)/shard_map/student_part/pallas_call | solution.py:553
  113.5 1.0 copy-done.2
  114.5 5.3 %target_part.3.refs_5_ = f32[256,2048]{1,0:T(8,128)S(1)} custom-call(s32[1]{0:T(128)} %bitcast.2.idx_ref, bf16[128,1792]{1,0:T(8,128)(2,1)S(1)} %fusion.3.mine_ref, bf16[128,1792]{1,0:T(8,128)(2,1)S(1)} %collective-permute-done.17.near_ref, bf16[3584,2048]{1,0:T(8,128)(2,1)} %refs_4_.5, f32[256,2048]{1,0:T(8,128)S(1)} %get-tuple-element.71.refs_0_), custom_call_target="tpu_custom_call" | custom-call | flops 1 | bytes 1 | tf_op jit(solution)/shard_map/target_part/pallas_call | solution.py:409
  119.8 2.1 %collective-permute-done.16.refs_0_ = bf16[128,1792]{1,0:T(8,128)(2,1)S(1)} collective-permute-done((bf16[128,1792]{1,0:T(8,128)(2,1)S(1)}, bf16[128,1792]{1,0:T(8,128)(2,1)S(1)}, u32[]{:S(2)}, u32[]{:S(2)}) %collective-permute-start.16) | collective-permute-done | bytes 458784 | tf_op jit(solution)/shard_map/ppermute | solution.py:706
  122.0 1.8 %collective-permute-done.19.refs_2_ = bf16[128,1792]{1,0:T(8,128)(2,1)S(1)} collective-permute-done((bf16[128,1792]{1,0:T(8,128)(2,1)S(1)}, bf16[128,1792]{1,0:T(8,128)(2,1)S(1)}, u32[]{:S(2)}, u32[]{:S(2)}) %collective-permute-start.19) | collective-permute-done | bytes 458784 | tf_op jit(solution)/shard_map/ppermute | solution.py:703
  123.8 11.1 %left_grads.1 = (bf16[4,256,128]{2,1,0:T(8,128)(2,1)S(1)}, bf16[8,256,512]{2,1,0:T(8,128)(2,1)S(1)}) custom-call(s32[4]{0:T(128)S(1)} %pad_add_fusion.idx_ref, bf16[128,1792]{1,0:T(8,128)(2,1)S(1)} %collective-permute-done.16.refs_0_, bf16[128,1792]{1,0:T(8,128)(2,1)S(1)} %collective-permute-done.18.refs_1_, ...), custom_call_target="tpu_custom_call" | custom-call | flops 1 | bytes 1 | tf_op jit(solution)/shard_map/left_grads/pallas_call | solution.py:621
  134.9 0.1 collective-permute-start.21
  135.0 3.5 %right_grads.2 = bf16[2,512,128]{2,1,0:T(8,128)(2,1)S(1)} custom-call(s32[4]{0:T(128)S(1)} %pad_add_fusion.idx_ref, bf16[128,8192]{1,0:T(8,128)(2,1)S(1)} %copy-done.1, bf16[128,8192]{1,0:T(8,128)(2,1)S(1)} %copy-done.1, bf16[128,8192]{1,0:T(8,128)(2,1)} %collective-permute-done.refs_2_.refs_3_, bf16[128,8192]{1,0:T(8,128)(2,1)} %collective-permute-done.refs_2_.refs_3_, ...), custom_call_target="tpu_custom_call" | custom-call | flops 1 | bytes 1 | tf_op jit(solution)/shard_map/right_grads/pallas_call | solution.py:675
  138.5 2.0 %collective-permute-start.22 = (bf16[2,512,128]{2,1,0:T(8,128)(2,1)S(1)}, bf16[2,512,128]{2,1,0:T(8,128)(2,1)S(1)}, u32[]{:S(2)}, u32[]{:S(2)}) collective-permute-start(bf16[2,512,128]{2,1,0:T(8,128)(2,1)S(1)} %right_grads.2), channel_id=1, source_target_pairs={{0,1},{1,0},{2,3},{3,2},{4,5},{5,4},{6,7},{7,6},{8,9},{9,8},{10,11... | collective-permute-start | bytes 786440 | tf_op jit(solution)/shard_map/ppermute | solution.py:709
  140.6 1.5 collective-permute-start.25
  142.1 3.5 %right_grads.3 = bf16[2,512,128]{2,1,0:T(8,128)(2,1)S(1)} custom-call(s32[4]{0:T(128)S(1)} %pad_add_fusion.idx_ref, bf16[128,8192]{1,0:T(8,128)(2,1)S(1)} %copy-done.1, bf16[128,8192]{1,0:T(8,128)(2,1)S(1)} %copy-done.1, bf16[128,8192]{1,0:T(8,128)(2,1)} %collective-permute-done.refs_2_.refs_3_, bf16[128,8192]{1,0:T(8,128)(2,1)} %collective-permute-done.refs_2_.refs_3_, ...), custom_call_target="tpu_custom_call" | custom-call | flops 10000000000 | bytes 10000000 | tf_op jit(solution)/shard_map/right_grads/pallas_call | solution.py:675
  145.6 2.7 %collective-permute-done.22 = bf16[2,512,128]{2,1,0:T(8,128)(2,1)S(1)} collective-permute-done((bf16[2,512,128]{2,1,0:T(8,128)(2,1)S(1)}, bf16[2,512,128]{2,1,0:T(8,128)(2,1)S(1)}, u32[]{:S(2)}, u32[]{:S(2)}) %collective-permute-start.22) | collective-permute-done | bytes 262176 | tf_op jit(solution)/shard_map/ppermute | solution.py:709
  148.4 0.1 add_convert_fusion
  148.5 0.7 collective-permute-start.23
  149.1 4.9 %collective-permute-start.24 = (bf16[512,128]{1,0:T(8,128)(2,1)S(1)}, bf16[512,128]{1,0:T(8,128)(2,1)S(1)}, u32[]{:S(2)}, u32[]{:S(2)}) collective-permute-start(bf16[512,128]{1,0:T(8,128)(2,1)S(1)} %get-tuple-element.81), channel_id=1, source_target_pairs={{0,8},{1,12},{2,0},{3,4},{4,9},{5,13},{6,1},{7,5},{8,10},{9,14},{1... | collective-permute-start | bytes 393224 | tf_op jit(solution)/shard_map/ppermute | solution.py:716
  154.1 0.2 reshape.32
  154.3 0.7 copy.8
  155.0 10.0 %collective-permute-done.24 = bf16[512,128]{1,0:T(8,128)(2,1)S(1)} collective-permute-done((bf16[512,128]{1,0:T(8,128)(2,1)S(1)}, bf16[512,128]{1,0:T(8,128)(2,1)S(1)}, u32[]{:S(2)}, u32[]{:S(2)}) %collective-permute-start.24) | collective-permute-done | bytes 131104 | tf_op jit(solution)/shard_map/ppermute | solution.py:716
  165.0 0.7 convert_add_fusion.2
  (49 shorter events, 0.3 us)
Async XLA Ops:
  0.6 8.5 %copy-start = (bf16[128,8192]{1,0:T(8,128)(2,1)S(1)}, bf16[128,8192]{1,0:T(8,128)(2,1)}, u32[]{:S(2)}) copy-start(bf16[128,8192]{1,0:T(8,128)(2,1)} %refs_1_.9) | copy-start | bytes 6291460
  0.6 8.5 %collective-permute-start = (bf16[128,8192]{1,0:T(8,128)(2,1)}, bf16[128,8192]{1,0:T(8,128)(2,1)}, u32[]{:S(2)}, u32[]{:S(2)}) collective-permute-start(bf16[128,8192]{1,0:T(8,128)(2,1)} %refs_1_.9), channel_id=1, source_target_pairs={{0,4},{4,0},{8,12},{12,8},{1,5},{5,1},{9,13},{13,9},{2,6},{6,2},{1... | collective-permute-start | bytes 6291464 | tf_op jit(solution)/shard_map/ppermute | solution.py:703
  5.9 28.7 %collective-permute-start.1 = (bf16[128,4096]{1,0:T(8,128)(2,1)}, bf16[128,4096]{1,0:T(8,128)(2,1)S(1)}, u32[]{:S(2)}, u32[]{:S(2)}) collective-permute-start(bf16[128,4096]{1,0:T(8,128)(2,1)} %cut_tokens.2), channel_id=1, source_target_pairs={{0,8},{4,12},{8,0},{12,4},{1,9},{5,13},{9,1},{13,5},{2,10},{6,14},... | collective-permute-start | bytes 3145736 | tf_op jit(solution)/shard_map/ppermute | solution.py:706
  9.1 11.9 %copy-start.11 = (bf16[16,32,128]{2,1,0:T(8,128)(2,1)S(1)}, bf16[16,32,128]{2,1,0:T(8,128)(2,1)}, u32[]{:S(2)}) copy-start(bf16[16,32,128]{2,1,0:T(8,128)(2,1)} %param.10) | copy-start | bytes 393220
  19.9 1.0 copy-start.4
  20.8 9.8 %collective-permute-start.4 = (bf16[2,128,1792]{2,1,0:T(8,128)(2,1)}, bf16[2,128,1792]{2,1,0:T(8,128)(2,1)S(1)}, u32[]{:S(2)}, u32[]{:S(2)}) collective-permute-start(bf16[2,128,1792]{2,1,0:T(8,128)(2,1)} %bitcast.11), channel_id=1, source_target_pairs={{0,4},{4,0},{8,12},{12,8},{1,5},{5,1},{9,13},{13,9},{2,6},{6,2},{1... | collective-permute-start | bytes 2752520 | tf_op jit(solution)/shard_map/ppermute | solution.py:703
  21.0 6.3 %collective-permute-start.2 = (bf16[16,32,128]{2,1,0:T(8,128)(2,1)S(1)}, bf16[16,32,128]{2,1,0:T(8,128)(2,1)S(1)}, u32[]{:S(2)}, u32[]{:S(2)}) collective-permute-start(bf16[16,32,128]{2,1,0:T(8,128)(2,1)S(1)} %copy-done.11), channel_id=1, source_target_pairs={{0,0},{1,4},{2,8},{3,12},{4,1},{5,5},{6,9},{7,13},{8,2},{9,6},{10,... | collective-permute-start | bytes 393224 | tf_op jit(solution)/shard_map/ppermute | solution.py:716
  23.3 4.0 %copy-start.10 = (bf16[256,128]{1,0:T(8,128)(2,1)S(1)}, bf16[256,128]{1,0:T(8,128)(2,1)}, u32[]{:S(2)}) copy-start(bf16[256,128]{1,0:T(8,128)(2,1)} %pack_left.1) | copy-start | bytes 196612
  23.3 7.3 %copy-start.5 = (bf16[1,2,128,1792]{3,2,1,0:T(8,128)(2,1)S(1)}, bf16[1,2,128,1792]{3,2,1,0:T(8,128)(2,1)}, u32[]{:S(2)}) copy-start(bf16[1,2,128,1792]{3,2,1,0:T(8,128)(2,1)} %copy-done.4) | copy-start | bytes 2752516
  27.4 8.8 %collective-permute-start.3 = (bf16[1,768,128]{2,1,0:T(8,128)(2,1)S(1)}, bf16[1,768,128]{2,1,0:T(8,128)(2,1)S(1)}, u32[]{:S(2)}, u32[]{:S(2)}) collective-permute-start(bf16[1,768,128]{2,1,0:T(8,128)(2,1)S(1)} %maximum_bitcast_fusion), channel_id=1, source_target_pairs={{0,1},{1,0},{2,3},{3,2},{4,5},{5,4},{6,7},{7,6},{8,9},{9,8},{10,11... | collective-permute-start | bytes 589832 | tf_op jit(solution)/shard_map/ppermute | solution.py:709
  36.2 4.6 %collective-permute-start.5 = (bf16[128,4096]{1,0:T(8,128)(2,1)S(1)}, bf16[128,4096]{1,0:T(8,128)(2,1)S(1)}, u32[]{:S(2)}, u32[]{:S(2)}) collective-permute-start(bf16[128,4096]{1,0:T(8,128)(2,1)S(1)} %collective-permute-done.1.refs_0_.refs_1_.refs_4_.refs_5_), channel_id=1, source_target_pairs={{0,4},{4,0},{8,12},{12,8},{1,5},{5,1},{9,13},{13,9},{2,6},{6,2},{1... | collective-permute-start | bytes 3145736 | tf_op jit(solution)/shard_map/ppermute | solution.py:703
  36.5 17.3 %collective-permute-start.6 = (bf16[64,4096]{1,0:T(8,128)(2,1)}, bf16[64,4096]{1,0:T(8,128)(2,1)}, u32[]{:S(2)}, u32[]{:S(2)}) collective-permute-start(bf16[64,4096]{1,0:T(8,128)(2,1)} %cut_tokens.3), channel_id=1, source_target_pairs={{0,8},{4,12},{8,0},{12,4},{1,9},{5,13},{9,1},{13,5},{2,10},{6,14},... | collective-permute-start | bytes 1572872 | tf_op jit(solution)/shard_map/ppermute | solution.py:706
  40.7 13.0 %copy-start.1 = (bf16[128,8192]{1,0:T(8,128)(2,1)S(1)}, bf16[128,8192]{1,0:T(8,128)(2,1)}, u32[]{:S(2)}) copy-start(bf16[128,8192]{1,0:T(8,128)(2,1)} %refs_1_.9) | copy-start | bytes 6291460
  40.7 32.4 %collective-permute-start.8 = (bf16[2,128,1792]{2,1,0:T(8,128)(2,1)}, bf16[2,128,1792]{2,1,0:T(8,128)(2,1)S(1)}, u32[]{:S(2)}, u32[]{:S(2)}) collective-permute-start(bf16[2,128,1792]{2,1,0:T(8,128)(2,1)} %fusion.1), channel_id=1, source_target_pairs={{0,8},{4,12},{8,0},{12,4},{1,9},{5,13},{9,1},{13,5},{2,10},{6,14},... | collective-permute-start | bytes 2752520 | tf_op jit(solution)/shard_map/ppermute | solution.py:706
  53.7 12.4 %collective-permute-start.9 = (bf16[2,128,1792]{2,1,0:T(8,128)(2,1)S(1)}, bf16[2,128,1792]{2,1,0:T(8,128)(2,1)S(1)}, u32[]{:S(2)}, u32[]{:S(2)}) collective-permute-start(bf16[2,128,1792]{2,1,0:T(8,128)(2,1)S(1)} %bitcast.58), channel_id=1, source_target_pairs={{0,4},{4,0},{8,12},{12,8},{1,5},{5,1},{9,13},{13,9},{2,6},{6,2},{1... | collective-permute-start | bytes 2752520 | tf_op jit(solution)/shard_map/ppermute | solution.py:703
  73.1 4.7 %collective-permute-start.10 = (bf16[2,2,128,1792]{3,2,1,0:T(8,128)(2,1)S(1)}, bf16[2,2,128,1792]{3,2,1,0:T(8,128)(2,1)S(1)}, u32[]{:S(2)}, u32[]{:S(2)}) collective-permute-start(bf16[2,2,128,1792]{3,2,1,0:T(8,128)(2,1)S(1)} %get-tuple-element.59), channel_id=1, source_target_pairs={{0,4},{4,0},{8,12},{12,8},{1,5},{5,1},{9,13},{13,9},{2,6},{6,2},{1... | collective-permute-start | bytes 5505032 | tf_op jit(solution)/shard_map/ppermute | solution.py:703
  73.2 34.9 %collective-permute-start.12 = (bf16[64,4096]{1,0:T(8,128)(2,1)}, bf16[64,4096]{1,0:T(8,128)(2,1)S(1)}, u32[]{:S(2)}, u32[]{:S(2)}) collective-permute-start(bf16[64,4096]{1,0:T(8,128)(2,1)} %collective-permute-done.6.refs_4_.refs_8_), channel_id=1, source_target_pairs={{0,4},{4,0},{8,12},{12,8},{1,5},{5,1},{9,13},{13,9},{2,6},{6,2},{1... | collective-permute-start | bytes 1572872 | tf_op jit(solution)/shard_map/ppermute | solution.py:703
  73.8 20.5 %collective-permute-start.11 = (bf16[2,768,128]{2,1,0:T(8,128)(2,1)S(1)}, bf16[2,768,128]{2,1,0:T(8,128)(2,1)S(1)}, u32[]{:S(2)}, u32[]{:S(2)}) collective-permute-start(bf16[2,768,128]{2,1,0:T(8,128)(2,1)S(1)} %pad_maximum_fusion), channel_id=1, source_target_pairs={{0,2},{1,3},{2,0},{3,1},{4,6},{5,7},{6,4},{7,5},{8,10},{9,11},{10,... | collective-permute-start | bytes 1179656 | tf_op jit(solution)/shard_map/ppermute | solution.py:709
  75.5 26.0 %collective-permute-start.7 = (bf16[64,4096]{1,0:T(8,128)(2,1)}, bf16[64,4096]{1,0:T(8,128)(2,1)S(1)}, u32[]{:S(2)}, u32[]{:S(2)}) collective-permute-start(bf16[64,4096]{1,0:T(8,128)(2,1)} %collective-permute-done.6.refs_4_.refs_8_), channel_id=1, source_target_pairs={{0,1},{1,0},{2,3},{3,2},{4,5},{5,4},{6,7},{7,6},{8,9},{9,8},{10,11... | collective-permute-start | bytes 1572872 | tf_op jit(solution)/shard_map/ppermute | solution.py:709
  77.5 29.4 %collective-permute-start.14 = (bf16[2,128,1792]{2,1,0:T(8,128)(2,1)S(1)}, bf16[2,128,1792]{2,1,0:T(8,128)(2,1)S(1)}, u32[]{:S(2)}, u32[]{:S(2)}) collective-permute-start(bf16[2,128,1792]{2,1,0:T(8,128)(2,1)S(1)} %fusion), channel_id=1, source_target_pairs={{0,8},{4,12},{8,0},{12,4},{1,9},{5,13},{9,1},{13,5},{2,10},{6,14},... | collective-permute-start | bytes 2752520 | tf_op jit(solution)/shard_map/ppermute | solution.py:706
  78.4 23.1 %collective-permute-start.15 = (bf16[128,1792]{1,0:T(8,128)(2,1)S(1)}, bf16[128,1792]{1,0:T(8,128)(2,1)S(1)}, u32[]{:S(2)}, u32[]{:S(2)}) collective-permute-start(bf16[128,1792]{1,0:T(8,128)(2,1)S(1)} %fusion.5.mine_ref), channel_id=1, source_target_pairs={{0,4},{4,0},{8,12},{12,8},{1,5},{5,1},{9,13},{13,9},{2,6},{6,2},{1... | collective-permute-start | bytes 1376264 | tf_op jit(solution)/shard_map/ppermute | solution.py:703
  99.7 14.8 %collective-permute-start.18 = (bf16[128,1792]{1,0:T(8,128)(2,1)S(1)}, bf16[128,1792]{1,0:T(8,128)(2,1)S(1)}, u32[]{:S(2)}, u32[]{:S(2)}) collective-permute-start(bf16[128,1792]{1,0:T(8,128)(2,1)S(1)} %fusion.5.mine_ref), channel_id=1, source_target_pairs={{0,8},{4,12},{8,0},{12,4},{1,9},{5,13},{9,1},{13,5},{2,10},{6,14},... | collective-permute-start | bytes 1376264 | tf_op jit(solution)/shard_map/ppermute | solution.py:706
  101.5 6.7 %copy-start.6 = (bf16[64,4096]{1,0:T(8,128)(2,1)}, bf16[64,4096]{1,0:T(8,128)(2,1)S(1)}, u32[]{:S(2)}) copy-start(bf16[64,4096]{1,0:T(8,128)(2,1)S(1)} %collective-permute-done.7.refs_5_.refs_9_) | copy-start | bytes 1572868
  101.5 6.7 %collective-permute-start.13 = (bf16[64,4096]{1,0:T(8,128)(2,1)S(1)}, bf16[64,4096]{1,0:T(8,128)(2,1)S(1)}, u32[]{:S(2)}, u32[]{:S(2)}) collective-permute-start(bf16[64,4096]{1,0:T(8,128)(2,1)S(1)} %collective-permute-done.7.refs_5_.refs_9_), channel_id=1, source_target_pairs={{0,4},{4,0},{8,12},{12,8},{1,5},{5,1},{9,13},{13,9},{2,6},{6,2},{1... | collective-permute-start | bytes 1572872 | tf_op jit(solution)/shard_map/ppermute | solution.py:703
  107.5 7.0 %collective-permute-start.17 = (bf16[128,1792]{1,0:T(8,128)(2,1)S(1)}, bf16[128,1792]{1,0:T(8,128)(2,1)S(1)}, u32[]{:S(2)}, u32[]{:S(2)}) collective-permute-start(bf16[128,1792]{1,0:T(8,128)(2,1)S(1)} %fusion.3.mine_ref), channel_id=1, source_target_pairs={{0,4},{4,0},{8,12},{12,8},{1,5},{5,1},{9,13},{13,9},{2,6},{6,2},{1... | collective-permute-start | bytes 1376264 | tf_op jit(solution)/shard_map/ppermute | solution.py:703
  107.8 14.1 %collective-permute-start.16 = (bf16[128,1792]{1,0:T(8,128)(2,1)S(1)}, bf16[128,1792]{1,0:T(8,128)(2,1)S(1)}, u32[]{:S(2)}, u32[]{:S(2)}) collective-permute-start(bf16[128,1792]{1,0:T(8,128)(2,1)S(1)} %fusion.3.mine_ref), channel_id=1, source_target_pairs={{0,8},{4,12},{8,0},{12,4},{1,9},{5,13},{9,1},{13,5},{2,10},{6,14},... | collective-permute-start | bytes 1376264 | tf_op jit(solution)/shard_map/ppermute | solution.py:706
  108.2 5.3 %copy-start.8 = (bf16[64,4096]{1,0:T(8,128)(2,1)}, bf16[64,4096]{1,0:T(8,128)(2,1)S(1)}, u32[]{:S(2)}) copy-start(bf16[64,4096]{1,0:T(8,128)(2,1)S(1)} %collective-permute-done.13.refs_7_.refs_11_) | copy-start | bytes 1572868
  113.5 1.0 copy-start.2
  114.5 7.5 %collective-permute-start.20 = (bf16[128,1792]{1,0:T(8,128)(2,1)S(1)}, bf16[128,1792]{1,0:T(8,128)(2,1)S(1)}, u32[]{:S(2)}, u32[]{:S(2)}) collective-permute-start(bf16[128,1792]{1,0:T(8,128)(2,1)S(1)} %collective-permute-done.18.refs_1_), channel_id=1, source_target_pairs={{0,4},{4,0},{8,12},{12,8},{1,5},{5,1},{9,13},{13,9},{2,6},{6,2},{1... | collective-permute-start | bytes 1376264 | tf_op jit(solution)/shard_map/ppermute | solution.py:703
  114.5 9.3 %copy-start.3 = (bf16[8,256,256]{2,1,0:T(8,128)(2,1)S(1)}, bf16[8,256,256]{2,1,0:T(8,128)(2,1)}, u32[]{:S(2)}) copy-start(bf16[8,256,256]{2,1,0:T(8,128)(2,1)} %copy-done.2) | copy-start | bytes 3145732
  122.0 1.8 %collective-permute-start.19 = (bf16[128,1792]{1,0:T(8,128)(2,1)S(1)}, bf16[128,1792]{1,0:T(8,128)(2,1)S(1)}, u32[]{:S(2)}, u32[]{:S(2)}) collective-permute-start(bf16[128,1792]{1,0:T(8,128)(2,1)S(1)} %collective-permute-done.16.refs_0_), channel_id=1, source_target_pairs={{0,4},{4,0},{8,12},{12,8},{1,5},{5,1},{9,13},{13,9},{2,6},{6,2},{1... | collective-permute-start | bytes 1376264 | tf_op jit(solution)/shard_map/ppermute | solution.py:703
  123.8 11.2 %copy-start.7 = (bf16[64,4096]{1,0:T(8,128)(2,1)S(1)}, bf16[64,4096]{1,0:T(8,128)(2,1)}, u32[]{:S(2)}) copy-start(bf16[64,4096]{1,0:T(8,128)(2,1)} %copy-done.6) | copy-start | bytes 1572868
  123.8 11.3 %copy-start.9 = (bf16[64,4096]{1,0:T(8,128)(2,1)S(1)}, bf16[64,4096]{1,0:T(8,128)(2,1)}, u32[]{:S(2)}) copy-start(bf16[64,4096]{1,0:T(8,128)(2,1)} %copy-done.8) | copy-start | bytes 1572868
  134.9 5.6 %collective-permute-start.21 = (bf16[2,256,128]{2,1,0:T(8,128)(2,1)S(1)}, bf16[2,256,128]{2,1,0:T(8,128)(2,1)S(1)}, u32[]{:S(2)}, u32[]{:S(2)}) collective-permute-start(bf16[2,256,128]{2,1,0:T(8,128)(2,1)S(1)} %slice.51), channel_id=1, source_target_pairs={{0,1},{1,0},{2,3},{3,2},{4,5},{5,4},{6,7},{7,6},{8,9},{9,8},{10,11... | collective-permute-start | bytes 393224 | tf_op jit(solution)/shard_map/ppermute | solution.py:709
  138.5 9.8 %collective-permute-start.22 = (bf16[2,512,128]{2,1,0:T(8,128)(2,1)S(1)}, bf16[2,512,128]{2,1,0:T(8,128)(2,1)S(1)}, u32[]{:S(2)}, u32[]{:S(2)}) collective-permute-start(bf16[2,512,128]{2,1,0:T(8,128)(2,1)S(1)} %right_grads.2), channel_id=1, source_target_pairs={{0,1},{1,0},{2,3},{3,2},{4,5},{5,4},{6,7},{7,6},{8,9},{9,8},{10,11... | collective-permute-start | bytes 786440 | tf_op jit(solution)/shard_map/ppermute | solution.py:709
  140.6 13.4 %collective-permute-start.25 = (bf16[256,128]{1,0:T(8,128)(2,1)S(1)}, bf16[256,128]{1,0:T(8,128)(2,1)S(1)}, u32[]{:S(2)}, u32[]{:S(2)}) collective-permute-start(bf16[256,128]{1,0:T(8,128)(2,1)S(1)} %slice_bitcast_fusion.6), channel_id=1, source_target_pairs={{0,2},{1,3},{2,0},{3,1},{4,6},{5,7},{6,4},{7,5},{8,10},{9,11},{10,... | collective-permute-start | bytes 196616 | tf_op jit(solution)/shard_map/ppermute | solution.py:709
  148.5 6.5 %collective-permute-start.23 = (bf16[512,128]{1,0:T(8,128)(2,1)S(1)}, bf16[512,128]{1,0:T(8,128)(2,1)S(1)}, u32[]{:S(2)}, u32[]{:S(2)}) collective-permute-start(bf16[512,128]{1,0:T(8,128)(2,1)S(1)} %get-tuple-element.80), channel_id=1, source_target_pairs={{0,0},{1,4},{2,8},{3,12},{4,1},{5,5},{6,9},{7,13},{8,2},{9,6},{10,... | collective-permute-start | bytes 393224 | tf_op jit(solution)/shard_map/ppermute | solution.py:716
  149.1 15.9 %collective-permute-start.24 = (bf16[512,128]{1,0:T(8,128)(2,1)S(1)}, bf16[512,128]{1,0:T(8,128)(2,1)S(1)}, u32[]{:S(2)}, u32[]{:S(2)}) collective-permute-start(bf16[512,128]{1,0:T(8,128)(2,1)S(1)} %get-tuple-element.81), channel_id=1, source_target_pairs={{0,8},{1,12},{2,0},{3,4},{4,9},{5,13},{6,1},{7,5},{8,10},{9,14},{1... | collective-permute-start | bytes 393224 | tf_op jit(solution)/shard_map/ppermute | solution.py:716

commit v14 on v13

--- a/solution.py
+++ b/solution.py
@@ -445,7 +445,7 @@
         for pair in range(fold // 2):
             row = begin + (g * (fold // 2) + pair) * share
             picked = [
-                rows_ref[z ^ owner, row : row + share, :] for owner in range(parts)
+                rows_ref[place(z, owner), row : row + share, :] for owner in range(parts)
             ]
             turned = jnp.concatenate(picked + picked, axis=0).astype(F32).T
             for a in range(2):
@@ -509,24 +509,18 @@
 
 
 def token_specs(half, width, chunk, late):
-    def specs(place):
+    if not late:
         return [
-            pl.BlockSpec((half, width), lambda n, s, p=p: (s[p % 2], place(n, s)))
+            pl.BlockSpec((half, width), lambda n, s, p=p: (s[p % 2], chunk(n, s)))
             for p in range(4)
         ]
-
-    if not late:
-        return specs(chunk)
-
-    def inner(n, s):
-        return lax.rem(chunk(n, s), 2)
-
-    return specs(inner) + [pl.BlockSpec((half, width), lambda n, s: (0, inner(n, s)))] * 4
+    inner = pl.BlockSpec((half, width), lambda n, s: (0, lax.rem(chunk(n, s), 2)))
+    return [inner] * 8
 
 
 def student_part(tokens, scalars, factors, pairs, tensor_count, late=()):
     size = factors.shape[2]
-    half = tokens[0].shape[0] // 2
+    half = tokens[0].shape[0] // (1 if late else 2)
     blocks = size // 2
     groups = pairs * blocks // BLK
     steps = blocks // (2 * WIDE)
@@ -536,7 +530,7 @@
 
     def right_spec(half):
         return pl.BlockSpec(
-            (1, WIDE * pairs, size), lambda n, s: (s[3] ^ chunk(n, s), half, 0)
+            (1, WIDE * pairs, size), lambda n, s: (place(s[3], chunk(n, s)), half, 0)
         )
 
     diag = (groups, BLK, BLK)
@@ -666,7 +660,7 @@
 
 
 def right_grads(back, own, late, scalars, pairs, bit, size, cost):
-    half = late[0].shape[0] // 2
+    half = late[0].shape[0]
     rows, count = back.shape[1:]
 
     def owner(n, s):
@@ -722,7 +716,7 @@
         return sum(term.astype(F32) for term in terms)
 
     near_tokens = swap(tokens)
-    first = cut_tokens(tokens, rows, jnp.int32(0), 1 - chip)
+    first = cut_tokens(tokens, rows // 2, odd, 1 - chip)
     arrived = across(first)
     base = jnp.stack([odd, 1 - odd])
     mine_block = lax.div(part, BLK) * chip
@@ -742,31 +736,31 @@
     factors = jnp.concatenate(
         [after(turned, left_rows).reshape(-1, LANES), left_rows], axis=0
     )[None]
-    more = along(factors, 1)
     sums = add(mine[0], swap(other[0])).astype(BF16)
-    rest = cut_tokens(after(tokens, left_rows), rows // 2, odd, chip)
-    arrived = after(arrived, more, sums, rest)
+
+    arrived = after(arrived, mine)
+    partner = along(arrived, 1)
+    near_arrived = swap(arrived)
+    late_first = across(cut_tokens(after(tokens, left_rows), rows // 2, odd, chip))
+    partner = after(partner, late_first, sums, factors)
     got_early = across(sums)
-    late_first = across(after(rest, sums))
-    factors = jnp.concatenate([factors, more], axis=0)
-
+    more = along(after(factors, partner), 2)
     order = jnp.concatenate([base, jnp.stack([chip, z])]).astype(jnp.int32)
     own = [tokens, tokens, near_tokens, near_tokens]
-    near_arrived = swap(arrived)
-    late = [arrived, arrived, near_arrived, near_arrived]
-    late_pieces = [(t, row, 3) for t in (arrived, near_arrived) for row in (0, 1)]
-    late_order = after(scalars(other_block), rest)
+    late = [arrived, partner, near_arrived, swap(partner)]
+    late_pieces = [(t, None, 3) for t in late]
+    late_order = after(scalars(other_block), sums)
     mine, other = products(late_pieces, late_order, gate_weight, up_weight, 0, part)
-    near = swap(after(other[0], late_first))
+    near = swap(other[0])
     mine_order = after(scalars(mine_block), mine)
     kept, other = products(
         own_pieces + late_pieces, mine_order, gate_weight, up_weight, 0, part
     )
     sums = add(mine[0], after(near, kept)).astype(BF16)
     got = across(sums)
-    near_kept = swap(after(other, got_early, sums))
-    factors = after(factors, kept)
-    more = along(factors, 2)
+    near_kept = swap(after(other, got_early, sums, more))
+    factors = jnp.concatenate([factors, after(more, kept)], axis=0)
+    more = along(factors, 1)
 
     def activate(u, term):
         total = add(kept[u], near_kept[u], term)
@@ -774,17 +768,16 @@
 
     hidden1 = activate(1, got_early)
     near1 = swap(hidden1)
-    late_partner = along(after(late_first, kept), 1)
     factors = jnp.concatenate([factors, after(more, hidden1)], axis=0)
     mixed0, rest0, left_diag = student_part(
         [after(tokens, hidden1, sums)] + own[1:], order, factors, pairs, tensor_count
     )
     got1 = across(after(hidden1, mixed0))
+    late_partner = along(after(late_first, mixed0), 1)
     target1 = target_part(1.0, [], hidden1, after(near1, mixed0), down_weight, chip)
     hidden0 = activate(0, after(got, target1))
     got0 = across(hidden0)
     near0 = swap(hidden0)
-    late_partner = after(late_partner, mixed0)
     late += [late_first, late_partner, swap(late_first), swap(late_partner)]
     mixed1, rest1 = student_part(
         [after(late[0], hidden0)] + late[1:],

time: 167 us -> 164 us (0.982)
  waiting for transfers between devices: 46.7 us -> 40.3 us
  starting transfers between devices: 27.9 us -> 31.5 us
    ppermute x6 -> x7, waiting for transfers between devices: 20.2 us -> 15.2 us  [along(): lax.ppermute(value, 'tensor', [(i, i ^ bit) for i in range(tensor_count)])]
    ppermute x6, starting transfers between devices: 9.14 us -> 13.7 us  [across(): return lax.ppermute(value, 'fsdp', [(i, i ^ 2) for i in range(fsdp_count)])]
    ppermute x6 -> x7, starting transfers between devices: 10.5 us -> 8.37 us  [along(): lax.ppermute(value, 'tensor', [(i, i ^ bit) for i in range(tensor_count)])]
    ppermute x11 -> x12, starting transfers between devices: 2.06 us -> 3.63 us  [swap(): return lax.ppermute(value, 'fsdp', [(i, i ^ 1) for i in range(fsdp_count)])]
  transfers between devices with their start and end apart: 26 -> 28, of which waited for: 9 -> 9; matrix products, arithmetic and copies ran while one was open for 3% -> 4% of each run, Pallas kernels for 43% -> 43%
where the time goes in v14:
time: 164 us; the launch traced here: 163 us
  Pallas kernels  80.8 us (49%)
  waiting for transfers between devices  40.3 us (25%)
  starting transfers between devices  31.5 us (19%)
  other arithmetic  5.5 us (3%)
  local copies, waits for them, and re-layouts  3.93 us (2%)
    pallas_call x3, Pallas kernels, products(): pl.pallas_call(functools.partial(products_kernel, sets), grid_spec=pltpu....  33.1 us
    ppermute x7, waiting for transfers between devices, along(): lax.ppermute(value, 'tensor', [(i, i ^ bit) for i in range(tensor_count)])  15.2 us
    ppermute x6, starting transfers between devices, across(): return lax.ppermute(value, 'fsdp', [(i, i ^ 2) for i in range(fsdp_count)])  13.7 us
    ppermute x6, waiting for transfers between devices, across(): return lax.ppermute(value, 'fsdp', [(i, i ^ 2) for i in range(fsdp_count)])  13 us
    pallas_call x1, Pallas kernels, left_grads(): pl.pallas_call(functools.partial(left_kernel, chunks, scale), grid_spec=p...  11.1 us
    pallas_call x2, Pallas kernels, target_part(): pl.pallas_call(functools.partial(target_kernel, sign), grid_spec=pltpu.Pr...  10.6 us
    ppermute x3, waiting for transfers between devices, turn(): return lax.ppermute(value, both_axes, perm)  10.3 us
    pallas_call x2, Pallas kernels, student_part(): pl.pallas_call(functools.partial(student_kernel, steps, bool(late), tenso...  9.84 us
  transfers between devices with their start and end apart: 28, of which 9 were waited for; matrix products, arithmetic and copies ran while one was open for 4% of the time, Pallas kernels for 43%

profile of v14, /device:TPU:0, one launch (start us, length us, event | category | flops | bytes accessed | tf_op | source)
XLA Modules:
  0.0 163.0 jit_solution(4490103314132825338)
XLA Ops:
  0.6 0.0 copy-start
  0.6 0.5 collective-permute-start
  1.2 0.7 pad_add_fusion.1
  1.8 3.8 %cut_tokens.2 = bf16[64,4096]{1,0:T(8,128)(2,1)} custom-call(s32[2]{0:T(128)} %get-tuple-element.80.idx_ref, bf16[128,8192]{1,0:T(8,128)(2,1)} %refs_1_.9), custom_call_target="tpu_custom_call" | custom-call | flops 1 | bytes 1 | tf_op jit(solution)/shard_map/cut_tokens/pallas_call | solution.py:312
  5.7 2.5 %collective-permute-start.1 = (bf16[64,4096]{1,0:T(8,128)(2,1)}, bf16[64,4096]{1,0:T(8,128)(2,1)S(1)}, u32[]{:S(2)}, u32[]{:S(2)}) collective-permute-start(bf16[64,4096]{1,0:T(8,128)(2,1)} %cut_tokens.2), channel_id=1, source_target_pairs={{0,8},{4,12},{8,0},{12,4},{1,9},{5,13},{9,1},{13,5},{2,10},{6,14},... | collective-permute-start | bytes 1572872 | tf_op jit(solution)/shard_map/ppermute | solution.py:700
  8.2 0.1 concatenate.25.idx_ref
  8.3 10.8 %gate_up_products.3 = (bf16[1,2,128,1792]{3,2,1,0:T(8,128)(2,1)S(1)}, bf16[1,2,128,1792]{3,2,1,0:T(8,128)(2,1)}) custom-call(s32[5]{0:T(128)S(1)} %concatenate.25.idx_ref, bf16[128,8192]{1,0:T(8,128)(2,1)S(1)} %copy-done, bf16[128,8192]{1,0:T(8,128)(2,1)S(1)} %copy-done, bf16[128,8192]{1,0:T(8,128)(2,1)} %collective-permute-done.refs_2_.refs_3_, ...), custom_call_target="tpu_custom_call" | custom-call | flops 1 | bytes 1 | tf_op jit(solution)/shard_map/gate_up_products/pallas_call | solution.py:371
  19.0 1.9 %collective-permute-done.1.refs_0_.refs_4_ = bf16[64,4096]{1,0:T(8,128)(2,1)S(1)} collective-permute-done((bf16[64,4096]{1,0:T(8,128)(2,1)}, bf16[64,4096]{1,0:T(8,128)(2,1)S(1)}, u32[]{:S(2)}, u32[]{:S(2)}) %collective-permute-start.1) | collective-permute-done | bytes 524320 | tf_op jit(solution)/shard_map/ppermute | solution.py:700
  21.0 1.8 %collective-permute-start.2 = (bf16[64,4096]{1,0:T(8,128)(2,1)S(1)}, bf16[64,4096]{1,0:T(8,128)(2,1)S(1)}, u32[]{:S(2)}, u32[]{:S(2)}) collective-permute-start(bf16[64,4096]{1,0:T(8,128)(2,1)S(1)} %collective-permute-done.1.refs_0_.refs_4_), channel_id=1, source_target_pairs={{0,1},{1,0},{2,3},{3,2},{4,5},{5,4},{6,7},{7,6},{8,9},{9,8},{10,11... | collective-permute-start | bytes 1572872 | tf_op jit(solution)/shard_map/ppermute | solution.py:703
  22.8 1.6 collective-permute-start.5
  24.3 0.9 collective-permute-start.4
  25.3 1.6 pack_left.1
  26.9 4.0 %cut_tokens.3 = bf16[64,4096]{1,0:T(8,128)(2,1)} custom-call(s32[2]{0:T(128)} %get-tuple-element.81.idx_ref, bf16[128,8192]{1,0:T(8,128)(2,1)} %refs_1_.9), custom_call_target="tpu_custom_call" | custom-call | flops 1 | bytes 1 | tf_op jit(solution)/shard_map/cut_tokens/pallas_call | solution.py:312
  30.9 3.5 %collective-permute-start.3 = (bf16[64,4096]{1,0:T(8,128)(2,1)}, bf16[64,4096]{1,0:T(8,128)(2,1)S(1)}, u32[]{:S(2)}, u32[]{:S(2)}) collective-permute-start(bf16[64,4096]{1,0:T(8,128)(2,1)} %cut_tokens.3), channel_id=1, source_target_pairs={{0,8},{4,12},{8,0},{12,4},{1,9},{5,13},{9,1},{13,5},{2,10},{6,14},... | collective-permute-start | bytes 1572872 | tf_op jit(solution)/shard_map/ppermute | solution.py:700
  34.4 0.0 copy-start.12
  34.5 2.4 %fusion.1 = bf16[2,128,1792]{2,1,0:T(8,128)(2,1)} fusion(bf16[2,128,1792]{2,1,0:T(8,128)(2,1)} %collective-permute-done.4, bf16[1,2,128,1792]{3,2,1,0:T(8,128)(2,1)S(1)} %get-tuple-element.41), kind=kLoop, calls=%fused_computation.3 | loop fusion | flops 1835008 | bytes 2752512 | tf_op jit(solution)/shard_map/convert_element_type | solution.py:739
  36.9 11.1 %collective-permute-done.3.refs_4_.refs_8_ = bf16[64,4096]{1,0:T(8,128)(2,1)S(1)} collective-permute-done((bf16[64,4096]{1,0:T(8,128)(2,1)}, bf16[64,4096]{1,0:T(8,128)(2,1)S(1)}, u32[]{:S(2)}, u32[]{:S(2)}) %collective-permute-start.3) | collective-permute-done | bytes 524320 | tf_op jit(solution)/shard_map/ppermute | solution.py:700
  48.0 0.8 copy-done.4
  48.8 0.1 concatenate.27.idx_ref
  48.9 2.4 %collective-permute-start.8 = (bf16[2,128,1792]{2,1,0:T(8,128)(2,1)}, bf16[2,128,1792]{2,1,0:T(8,128)(2,1)S(1)}, u32[]{:S(2)}, u32[]{:S(2)}) collective-permute-start(bf16[2,128,1792]{2,1,0:T(8,128)(2,1)} %fusion.1), channel_id=1, source_target_pairs={{0,8},{4,12},{8,0},{12,4},{1,9},{5,13},{9,1},{13,5},{2,10},{6,14},... | collective-permute-start | bytes 2752520 | tf_op jit(solution)/shard_map/ppermute | solution.py:700
  51.2 10.0 %gate_up_products.4 = (bf16[1,2,128,1792]{3,2,1,0:T(8,128)(2,1)S(1)}, bf16[1,2,128,1792]{3,2,1,0:T(8,128)(2,1)S(1)}) custom-call(s32[5]{0:T(128)S(1)} %concatenate.25.idx_ref, bf16[64,4096]{1,0:T(8,128)(2,1)S(1)} %collective-permute-done.1.refs_0_.refs_4_, bf16[64,4096]{1,0:T(8,128)(2,1)S(1)} %collective-permute-done.2.refs_1_.refs_5_, ...), custom_call_target="tpu_custom_call" | custom-call | flops 1 | bytes 1 | tf_op jit(solution)/shard_map/gate_up_products/pallas_call | solution.py:371
  61.2 0.3 collective-permute-start.9
  61.5 12.3 %gate_up_products.5 = (bf16[2,2,128,1792]{3,2,1,0:T(8,128)(2,1)S(1)}, bf16[2,2,128,1792]{3,2,1,0:T(8,128)(2,1)S(1)}) custom-call(s32[5]{0:T(128)S(1)} %concatenate.27.idx_ref, bf16[128,8192]{1,0:T(8,128)(2,1)S(1)} %copy-done.1, bf16[128,8192]{1,0:T(8,128)(2,1)S(1)} %copy-done.1, bf16[128,8192]{1,0:T(8,128)(2,1)} %collective-permute-done.refs_2_.refs_3_, ...), custom_call_target="tpu_custom_call" | custom-call | flops 10000000000 | bytes 10000000 | tf_op jit(solution)/shard_map/gate_up_products/pallas_call | solution.py:371
  73.9 0.2 fusion
  74.1 0.3 collective-permute-start.11
  74.5 0.1 pad_add_fusion.idx_ref
  74.6 1.1 collective-permute-start.12
  75.7 2.0 %collective-permute-start.16 = (bf16[2,128,1792]{2,1,0:T(8,128)(2,1)S(1)}, bf16[2,128,1792]{2,1,0:T(8,128)(2,1)S(1)}, u32[]{:S(2)}, u32[]{:S(2)}) collective-permute-start(bf16[2,128,1792]{2,1,0:T(8,128)(2,1)S(1)} %fusion), channel_id=1, source_target_pairs={{0,8},{4,12},{8,0},{12,4},{1,9},{5,13},{9,1},{13,5},{2,10},{6,14},... | collective-permute-start | bytes 2752520 | tf_op jit(solution)/shard_map/ppermute | solution.py:700
  77.7 0.3 collective-permute-done.11
  78.0 0.3 bitcast_add_fusion.1
  78.3 0.3 fusion.5.mine_ref
  78.6 7.4 %collective-permute-done.12 = bf16[2,768,128]{2,1,0:T(8,128)(2,1)S(1)} collective-permute-done((bf16[2,768,128]{2,1,0:T(8,128)(2,1)S(1)}, bf16[2,768,128]{2,1,0:T(8,128)(2,1)S(1)}, u32[]{:S(2)}, u32[]{:S(2)}) %collective-permute-start.12) | collective-permute-done | bytes 393248 | tf_op jit(solution)/shard_map/ppermute | solution.py:703
  85.9 0.1 pad_maximum_fusion.refs_4_.refs_5_.refs_6_.refs_8_.refs_9_
  86.0 5.3 %student_part.2 = (bf16[8,256,256]{2,1,0:T(8,128)(2,1)S(1)}, f32[256,2048]{1,0:T(8,128)S(1)}, bf16[8,256,256]{2,1,0:T(8,128)(2,1)S(1)}) custom-call(s32[4]{0:T(128)S(1)} %pad_add_fusion.idx_ref, bf16[128,8192]{1,0:T(8,128)(2,1)S(1)} %copy-done.1, bf16[128,8192]{1,0:T(8,128)(2,1)S(1)} %copy-done.1, bf16[128,8192]{1,0:T(8,128)(2,1)} %collective-permute-done.refs_2_.refs_3_, ...), custom_call_target="tpu_custom_call" | custom-call | flops 10000000000 | bytes 10000000 | tf_op jit(solution)/shard_map/student_part/pallas_call | solution.py:547
  91.3 1.1 collective-permute-start.13
  92.5 0.5 collective-permute-start.14
  93.0 1.8 %collective-permute-start.20 = (bf16[128,1792]{1,0:T(8,128)(2,1)S(1)}, bf16[128,1792]{1,0:T(8,128)(2,1)S(1)}, u32[]{:S(2)}, u32[]{:S(2)}) collective-permute-start(bf16[128,1792]{1,0:T(8,128)(2,1)S(1)} %fusion.5.mine_ref), channel_id=1, source_target_pairs={{0,8},{4,12},{8,0},{12,4},{1,9},{5,13},{9,1},{13,5},{2,10},{6,14},... | collective-permute-start | bytes 1376264 | tf_op jit(solution)/shard_map/ppermute | solution.py:700
  94.7 5.2 %target_part.2.refs_11_ = f32[256,2048]{1,0:T(8,128)S(1)} custom-call(s32[1]{0:T(128)} %bitcast.2.idx_ref, bf16[128,1792]{1,0:T(8,128)(2,1)S(1)} %fusion.5.mine_ref, bf16[128,1792]{1,0:T(8,128)(2,1)S(1)} %collective-permute-done.17.near_ref, bf16[3584,2048]{1,0:T(8,128)(2,1)} %refs_4_.5), custom_call_target="tpu_custom_call" | custom-call | flops 1 | bytes 1 | tf_op jit(solution)/shard_map/target_part/pallas_call | solution.py:409
  99.9 4.7 %collective-permute-done.13.refs_5_.refs_9_ = bf16[64,4096]{1,0:T(8,128)(2,1)S(1)} collective-permute-done((bf16[64,4096]{1,0:T(8,128)(2,1)S(1)}, bf16[64,4096]{1,0:T(8,128)(2,1)S(1)}, u32[]{:S(2)}, u32[]{:S(2)}) %collective-permute-start.13) | collective-permute-done | bytes 524320 | tf_op jit(solution)/shard_map/ppermute | solution.py:703
  104.6 0.3 bitcast_add_fusion
  104.9 0.3 fusion.3.mine_ref
  105.2 0.6 collective-permute-start.19
  105.8 1.6 collective-permute-start.18
  107.4 4.5 %student_part.3 = (bf16[8,256,256]{2,1,0:T(8,128)(2,1)S(1)}, f32[256,2048]{1,0:T(8,128)S(1)}) custom-call(s32[4]{0:T(128)S(1)} %pad_add_fusion.idx_ref, bf16[64,4096]{1,0:T(8,128)(2,1)S(1)} %collective-permute-done.1.refs_0_.refs_4_, bf16[64,4096]{1,0:T(8,128)(2,1)S(1)} %collective-permute-done.2.refs_1_.refs_5_, ...), custom_call_target="tpu_custom_call" | custom-call | flops 10000000000 | bytes 10000000 | tf_op jit(solution)/shard_map/student_part/pallas_call | solution.py:547
  111.9 1.0 copy-done.2
  112.9 5.5 %target_part.3.refs_5_ = f32[256,2048]{1,0:T(8,128)S(1)} custom-call(s32[1]{0:T(128)} %bitcast.2.idx_ref, bf16[128,1792]{1,0:T(8,128)(2,1)S(1)} %fusion.3.mine_ref, bf16[128,1792]{1,0:T(8,128)(2,1)S(1)} %collective-permute-done.19.near_ref, bf16[3584,2048]{1,0:T(8,128)(2,1)} %refs_4_.5, f32[256,2048]{1,0:T(8,128)S(1)} %get-tuple-element.69.refs_0_), custom_call_target="tpu_custom_call" | custom-call | flops 1 | bytes 1 | tf_op jit(solution)/shard_map/target_part/pallas_call | solution.py:409
  118.4 0.4 collective-permute-start.21
  118.9 1.4 collective-permute-done.21.refs_2_
  120.3 1.0 copy-done.11
  121.3 11.1 %left_grads.1 = (bf16[4,256,128]{2,1,0:T(8,128)(2,1)S(1)}, bf16[8,256,512]{2,1,0:T(8,128)(2,1)S(1)}) custom-call(s32[4]{0:T(128)S(1)} %pad_add_fusion.idx_ref, bf16[128,1792]{1,0:T(8,128)(2,1)S(1)} %collective-permute-done.18.refs_0_, bf16[128,1792]{1,0:T(8,128)(2,1)S(1)} %copy-done.11, bf16[128,1792]{1,0:T(8,128)(2,1)S(1)} %collective-permute-done.21.refs_2_, ...), custom_call_target="tpu_custom_call" | custom-call | flops 1 | bytes 1 | tf_op jit(solution)/shard_map/left_grads/pallas_call | solution.py:615
  132.5 1.1 collective-permute-start.23
  133.6 3.4 %right_grads.2 = bf16[2,512,128]{2,1,0:T(8,128)(2,1)S(1)} custom-call(s32[4]{0:T(128)S(1)} %pad_add_fusion.idx_ref, bf16[128,8192]{1,0:T(8,128)(2,1)S(1)} %copy-done.1, bf16[128,8192]{1,0:T(8,128)(2,1)S(1)} %copy-done.1, bf16[128,8192]{1,0:T(8,128)(2,1)} %collective-permute-done.refs_2_.refs_3_, bf16[128,8192]{1,0:T(8,128)(2,1)} %collective-permute-done.refs_2_.refs_3_, ...), custom_call_target="tpu_custom_call" | custom-call | flops 1 | bytes 1 | tf_op jit(solution)/shard_map/right_grads/pallas_call | solution.py:669
  136.9 1.1 collective-permute-start.24
  138.0 0.3 collective-permute-done.23
  138.4 2.1 %collective-permute-start.27 = (bf16[256,128]{1,0:T(8,128)(2,1)S(1)}, bf16[256,128]{1,0:T(8,128)(2,1)S(1)}, u32[]{:S(2)}, u32[]{:S(2)}) collective-permute-start(bf16[256,128]{1,0:T(8,128)(2,1)S(1)} %slice_bitcast_fusion.6), channel_id=1, source_target_pairs={{0,2},{1,3},{2,0},{3,1},{4,6},{5,7},{6,4},{7,5},{8,10},{9,11},{10,... | collective-permute-start | bytes 196616 | tf_op jit(solution)/shard_map/ppermute | solution.py:703
  140.5 3.4 %right_grads.3 = bf16[2,512,128]{2,1,0:T(8,128)(2,1)S(1)} custom-call(s32[4]{0:T(128)S(1)} %pad_add_fusion.idx_ref, bf16[128,8192]{1,0:T(8,128)(2,1)S(1)} %copy-done.1, bf16[128,8192]{1,0:T(8,128)(2,1)S(1)} %copy-done.1, bf16[128,8192]{1,0:T(8,128)(2,1)} %collective-permute-done.refs_2_.refs_3_, bf16[128,8192]{1,0:T(8,128)(2,1)} %collective-permute-done.refs_2_.refs_3_, ...), custom_call_target="tpu_custom_call" | custom-call | flops 10000000000 | bytes 10000000 | tf_op jit(solution)/shard_map/right_grads/pallas_call | solution.py:669
  143.9 2.8 %collective-permute-done.24 = bf16[2,512,128]{2,1,0:T(8,128)(2,1)S(1)} collective-permute-done((bf16[2,512,128]{2,1,0:T(8,128)(2,1)S(1)}, bf16[2,512,128]{2,1,0:T(8,128)(2,1)S(1)}, u32[]{:S(2)}, u32[]{:S(2)}) %collective-permute-start.24) | collective-permute-done | bytes 262176 | tf_op jit(solution)/shard_map/ppermute | solution.py:703
  146.7 0.1 add_convert_fusion
  146.8 0.7 collective-permute-start.25
  147.5 3.6 %collective-permute-start.26 = (bf16[512,128]{1,0:T(8,128)(2,1)S(1)}, bf16[512,128]{1,0:T(8,128)(2,1)S(1)}, u32[]{:S(2)}, u32[]{:S(2)}) collective-permute-start(bf16[512,128]{1,0:T(8,128)(2,1)S(1)} %get-tuple-element.79), channel_id=1, source_target_pairs={{0,8},{1,12},{2,0},{3,4},{4,9},{5,13},{6,1},{7,5},{8,10},{9,14},{1... | collective-permute-start | bytes 393224 | tf_op jit(solution)/shard_map/ppermute | solution.py:710
  151.1 0.2 reshape.32
  151.3 0.7 copy.8
  152.0 10.3 %collective-permute-done.26 = bf16[512,128]{1,0:T(8,128)(2,1)S(1)} collective-permute-done((bf16[512,128]{1,0:T(8,128)(2,1)S(1)}, bf16[512,128]{1,0:T(8,128)(2,1)S(1)}, u32[]{:S(2)}, u32[]{:S(2)}) %collective-permute-start.26) | collective-permute-done | bytes 131104 | tf_op jit(solution)/shard_map/ppermute | solution.py:710
  162.3 0.7 convert_add_fusion.2
  (57 shorter events, 0.3 us)
Async XLA Ops:
  0.6 7.6 %copy-start = (bf16[128,8192]{1,0:T(8,128)(2,1)S(1)}, bf16[128,8192]{1,0:T(8,128)(2,1)}, u32[]{:S(2)}) copy-start(bf16[128,8192]{1,0:T(8,128)(2,1)} %refs_1_.9) | copy-start | bytes 6291460
  0.6 7.6 %collective-permute-start = (bf16[128,8192]{1,0:T(8,128)(2,1)}, bf16[128,8192]{1,0:T(8,128)(2,1)}, u32[]{:S(2)}, u32[]{:S(2)}) collective-permute-start(bf16[128,8192]{1,0:T(8,128)(2,1)} %refs_1_.9), channel_id=1, source_target_pairs={{0,4},{4,0},{8,12},{12,8},{1,5},{5,1},{9,13},{13,9},{2,6},{6,2},{1... | collective-permute-start | bytes 6291464 | tf_op jit(solution)/shard_map/ppermute | solution.py:697
  5.7 15.3 %collective-permute-start.1 = (bf16[64,4096]{1,0:T(8,128)(2,1)}, bf16[64,4096]{1,0:T(8,128)(2,1)S(1)}, u32[]{:S(2)}, u32[]{:S(2)}) collective-permute-start(bf16[64,4096]{1,0:T(8,128)(2,1)} %cut_tokens.2), channel_id=1, source_target_pairs={{0,8},{4,12},{8,0},{12,4},{1,9},{5,13},{9,1},{13,5},{2,10},{6,14},... | collective-permute-start | bytes 1572872 | tf_op jit(solution)/shard_map/ppermute | solution.py:700
  21.0 27.8 %collective-permute-start.2 = (bf16[64,4096]{1,0:T(8,128)(2,1)S(1)}, bf16[64,4096]{1,0:T(8,128)(2,1)S(1)}, u32[]{:S(2)}, u32[]{:S(2)}) collective-permute-start(bf16[64,4096]{1,0:T(8,128)(2,1)S(1)} %collective-permute-done.1.refs_0_.refs_4_), channel_id=1, source_target_pairs={{0,1},{1,0},{2,3},{3,2},{4,5},{5,4},{6,7},{7,6},{8,9},{9,8},{10,11... | collective-permute-start | bytes 1572872 | tf_op jit(solution)/shard_map/ppermute | solution.py:703
  22.8 28.5 %collective-permute-start.6 = (bf16[64,4096]{1,0:T(8,128)(2,1)S(1)}, bf16[64,4096]{1,0:T(8,128)(2,1)S(1)}, u32[]{:S(2)}, u32[]{:S(2)}) collective-permute-start(bf16[64,4096]{1,0:T(8,128)(2,1)S(1)} %collective-permute-done.1.refs_0_.refs_4_), channel_id=1, source_target_pairs={{0,4},{4,0},{8,12},{12,8},{1,5},{5,1},{9,13},{13,9},{2,6},{6,2},{1... | collective-permute-start | bytes 1572872 | tf_op jit(solution)/shard_map/ppermute | solution.py:697
  22.8 11.6 %collective-permute-start.5 = (bf16[16,32,128]{2,1,0:T(8,128)(2,1)}, bf16[16,32,128]{2,1,0:T(8,128)(2,1)S(1)}, u32[]{:S(2)}, u32[]{:S(2)}) collective-permute-start(bf16[16,32,128]{2,1,0:T(8,128)(2,1)} %param.10), channel_id=1, source_target_pairs={{0,0},{1,4},{2,8},{3,12},{4,1},{5,5},{6,9},{7,13},{8,2},{9,6},{10,... | collective-permute-start | bytes 393224 | tf_op jit(solution)/shard_map/ppermute | solution.py:710
  24.3 10.1 %collective-permute-start.4 = (bf16[2,128,1792]{2,1,0:T(8,128)(2,1)}, bf16[2,128,1792]{2,1,0:T(8,128)(2,1)}, u32[]{:S(2)}, u32[]{:S(2)}) collective-permute-start(bf16[2,128,1792]{2,1,0:T(8,128)(2,1)} %bitcast.9), channel_id=1, source_target_pairs={{0,4},{4,0},{8,12},{12,8},{1,5},{5,1},{9,13},{13,9},{2,6},{6,2},{1... | collective-permute-start | bytes 2752520 | tf_op jit(solution)/shard_map/ppermute | solution.py:697
  26.9 7.5 %copy-start.14 = (bf16[256,128]{1,0:T(8,128)(2,1)S(1)}, bf16[256,128]{1,0:T(8,128)(2,1)}, u32[]{:S(2)}) copy-start(bf16[256,128]{1,0:T(8,128)(2,1)} %pack_left.1) | copy-start | bytes 196612
  30.9 17.1 %collective-permute-start.3 = (bf16[64,4096]{1,0:T(8,128)(2,1)}, bf16[64,4096]{1,0:T(8,128)(2,1)S(1)}, u32[]{:S(2)}, u32[]{:S(2)}) collective-permute-start(bf16[64,4096]{1,0:T(8,128)(2,1)} %cut_tokens.3), channel_id=1, source_target_pairs={{0,8},{4,12},{8,0},{12,4},{1,9},{5,13},{9,1},{13,5},{2,10},{6,14},... | collective-permute-start | bytes 1572872 | tf_op jit(solution)/shard_map/ppermute | solution.py:700
  34.4 40.1 %copy-start.12 = (bf16[1,768,128]{2,1,0:T(8,128)(2,1)}, bf16[1,768,128]{2,1,0:T(8,128)(2,1)S(1)}, u32[]{:S(2)}) copy-start(bf16[1,768,128]{2,1,0:T(8,128)(2,1)S(1)} %maximum_bitcast_fusion) | copy-start | bytes 589828
  48.0 0.8 copy-start.4
  48.8 2.5 %collective-permute-start.7 = (bf16[64,4096]{1,0:T(8,128)(2,1)S(1)}, bf16[64,4096]{1,0:T(8,128)(2,1)S(1)}, u32[]{:S(2)}, u32[]{:S(2)}) collective-permute-start(bf16[64,4096]{1,0:T(8,128)(2,1)S(1)} %collective-permute-done.2.refs_1_.refs_5_), channel_id=1, source_target_pairs={{0,4},{4,0},{8,12},{12,8},{1,5},{5,1},{9,13},{13,9},{2,6},{6,2},{1... | collective-permute-start | bytes 1572872 | tf_op jit(solution)/shard_map/ppermute | solution.py:697
  48.9 12.7 %copy-start.1 = (bf16[128,8192]{1,0:T(8,128)(2,1)S(1)}, bf16[128,8192]{1,0:T(8,128)(2,1)}, u32[]{:S(2)}) copy-start(bf16[128,8192]{1,0:T(8,128)(2,1)} %refs_1_.9) | copy-start | bytes 6291460
  48.9 25.3 %collective-permute-start.8 = (bf16[2,128,1792]{2,1,0:T(8,128)(2,1)}, bf16[2,128,1792]{2,1,0:T(8,128)(2,1)S(1)}, u32[]{:S(2)}, u32[]{:S(2)}) collective-permute-start(bf16[2,128,1792]{2,1,0:T(8,128)(2,1)} %fusion.1), channel_id=1, source_target_pairs={{0,8},{4,12},{8,0},{12,4},{1,9},{5,13},{9,1},{13,5},{2,10},{6,14},... | collective-permute-start | bytes 2752520 | tf_op jit(solution)/shard_map/ppermute | solution.py:700
  51.2 22.9 %collective-permute-start.10 = (bf16[1,768,128]{2,1,0:T(8,128)(2,1)S(1)}, bf16[1,768,128]{2,1,0:T(8,128)(2,1)S(1)}, u32[]{:S(2)}, u32[]{:S(2)}) collective-permute-start(bf16[1,768,128]{2,1,0:T(8,128)(2,1)S(1)} %maximum_bitcast_fusion), channel_id=1, source_target_pairs={{0,2},{1,3},{2,0},{3,1},{4,6},{5,7},{6,4},{7,5},{8,10},{9,11},{10,... | collective-permute-start | bytes 589832 | tf_op jit(solution)/shard_map/ppermute | solution.py:703
  61.2 12.7 %collective-permute-start.9 = (bf16[2,128,1792]{2,1,0:T(8,128)(2,1)S(1)}, bf16[2,128,1792]{2,1,0:T(8,128)(2,1)S(1)}, u32[]{:S(2)}, u32[]{:S(2)}) collective-permute-start(bf16[2,128,1792]{2,1,0:T(8,128)(2,1)S(1)} %bitcast.58), channel_id=1, source_target_pairs={{0,4},{4,0},{8,12},{12,8},{1,5},{5,1},{9,13},{13,9},{2,6},{6,2},{1... | collective-permute-start | bytes 2752520 | tf_op jit(solution)/shard_map/ppermute | solution.py:697
  74.1 3.9 %collective-permute-start.11 = (bf16[2,2,128,1792]{3,2,1,0:T(8,128)(2,1)S(1)}, bf16[2,2,128,1792]{3,2,1,0:T(8,128)(2,1)S(1)}, u32[]{:S(2)}, u32[]{:S(2)}) collective-permute-start(bf16[2,2,128,1792]{3,2,1,0:T(8,128)(2,1)S(1)} %get-tuple-element.57), channel_id=1, source_target_pairs={{0,4},{4,0},{8,12},{12,8},{1,5},{5,1},{9,13},{13,9},{2,6},{6,2},{1... | collective-permute-start | bytes 5505032 | tf_op jit(solution)/shard_map/ppermute | solution.py:697
  74.6 11.3 %collective-permute-start.12 = (bf16[2,768,128]{2,1,0:T(8,128)(2,1)S(1)}, bf16[2,768,128]{2,1,0:T(8,128)(2,1)S(1)}, u32[]{:S(2)}, u32[]{:S(2)}) collective-permute-start(bf16[2,768,128]{2,1,0:T(8,128)(2,1)S(1)} %pad_maximum_fusion.1), channel_id=1, source_target_pairs={{0,1},{1,0},{2,3},{3,2},{4,5},{5,4},{6,7},{7,6},{8,9},{9,8},{10,11... | collective-permute-start | bytes 1179656 | tf_op jit(solution)/shard_map/ppermute | solution.py:703
  75.7 24.2 %collective-permute-start.16 = (bf16[2,128,1792]{2,1,0:T(8,128)(2,1)S(1)}, bf16[2,128,1792]{2,1,0:T(8,128)(2,1)S(1)}, u32[]{:S(2)}, u32[]{:S(2)}) collective-permute-start(bf16[2,128,1792]{2,1,0:T(8,128)(2,1)S(1)} %fusion), channel_id=1, source_target_pairs={{0,8},{4,12},{8,0},{12,4},{1,9},{5,13},{9,1},{13,5},{2,10},{6,14},... | collective-permute-start | bytes 2752520 | tf_op jit(solution)/shard_map/ppermute | solution.py:700
  78.3 7.6 %copy-start.13 = (bf16[1,768,128]{2,1,0:T(8,128)(2,1)S(1)}, bf16[1,768,128]{2,1,0:T(8,128)(2,1)}, u32[]{:S(2)}) copy-start(bf16[1,768,128]{2,1,0:T(8,128)(2,1)} %copy-done.12) | copy-start | bytes 589828
  86.0 5.3 %copy-start.5 = (bf16[64,4096]{1,0:T(8,128)(2,1)S(1)}, bf16[64,4096]{1,0:T(8,128)(2,1)}, u32[]{:S(2)}) copy-start(bf16[64,4096]{1,0:T(8,128)(2,1)} %copy-done.4) | copy-start | bytes 1572868
  91.3 13.3 %collective-permute-start.13 = (bf16[64,4096]{1,0:T(8,128)(2,1)S(1)}, bf16[64,4096]{1,0:T(8,128)(2,1)S(1)}, u32[]{:S(2)}, u32[]{:S(2)}) collective-permute-start(bf16[64,4096]{1,0:T(8,128)(2,1)S(1)} %copy-done.5), channel_id=1, source_target_pairs={{0,1},{1,0},{2,3},{3,2},{4,5},{5,4},{6,7},{7,6},{8,9},{9,8},{10,11... | collective-permute-start | bytes 1572872 | tf_op jit(solution)/shard_map/ppermute | solution.py:703
  92.5 2.3 %collective-permute-start.17 = (bf16[128,1792]{1,0:T(8,128)(2,1)S(1)}, bf16[128,1792]{1,0:T(8,128)(2,1)S(1)}, u32[]{:S(2)}, u32[]{:S(2)}) collective-permute-start(bf16[128,1792]{1,0:T(8,128)(2,1)S(1)} %fusion.5.mine_ref), channel_id=1, source_target_pairs={{0,4},{4,0},{8,12},{12,8},{1,5},{5,1},{9,13},{13,9},{2,6},{6,2},{1... | collective-permute-start | bytes 1376264 | tf_op jit(solution)/shard_map/ppermute | solution.py:697
  92.5 14.9 %collective-permute-start.14 = (bf16[64,4096]{1,0:T(8,128)(2,1)S(1)}, bf16[64,4096]{1,0:T(8,128)(2,1)S(1)}, u32[]{:S(2)}, u32[]{:S(2)}) collective-permute-start(bf16[64,4096]{1,0:T(8,128)(2,1)S(1)} %copy-done.5), channel_id=1, source_target_pairs={{0,4},{4,0},{8,12},{12,8},{1,5},{5,1},{9,13},{13,9},{2,6},{6,2},{1... | collective-permute-start | bytes 1572872 | tf_op jit(solution)/shard_map/ppermute | solution.py:697
  93.0 19.9 %collective-permute-start.20 = (bf16[128,1792]{1,0:T(8,128)(2,1)S(1)}, bf16[128,1792]{1,0:T(8,128)(2,1)S(1)}, u32[]{:S(2)}, u32[]{:S(2)}) collective-permute-start(bf16[128,1792]{1,0:T(8,128)(2,1)S(1)} %fusion.5.mine_ref), channel_id=1, source_target_pairs={{0,8},{4,12},{8,0},{12,4},{1,9},{5,13},{9,1},{13,5},{2,10},{6,14},... | collective-permute-start | bytes 1376264 | tf_op jit(solution)/shard_map/ppermute | solution.py:700
  104.6 2.7 %collective-permute-start.15 = (bf16[64,4096]{1,0:T(8,128)(2,1)S(1)}, bf16[64,4096]{1,0:T(8,128)(2,1)S(1)}, u32[]{:S(2)}, u32[]{:S(2)}) collective-permute-start(bf16[64,4096]{1,0:T(8,128)(2,1)S(1)} %collective-permute-done.13.refs_5_.refs_9_), channel_id=1, source_target_pairs={{0,4},{4,0},{8,12},{12,8},{1,5},{5,1},{9,13},{13,9},{2,6},{6,2},{1... | collective-permute-start | bytes 1572872 | tf_op jit(solution)/shard_map/ppermute | solution.py:697
  105.2 7.7 %collective-permute-start.19 = (bf16[128,1792]{1,0:T(8,128)(2,1)S(1)}, bf16[128,1792]{1,0:T(8,128)(2,1)S(1)}, u32[]{:S(2)}, u32[]{:S(2)}) collective-permute-start(bf16[128,1792]{1,0:T(8,128)(2,1)S(1)} %fusion.3.mine_ref), channel_id=1, source_target_pairs={{0,4},{4,0},{8,12},{12,8},{1,5},{5,1},{9,13},{13,9},{2,6},{6,2},{1... | collective-permute-start | bytes 1376264 | tf_op jit(solution)/shard_map/ppermute | solution.py:697
  105.8 12.6 %collective-permute-start.18 = (bf16[128,1792]{1,0:T(8,128)(2,1)S(1)}, bf16[128,1792]{1,0:T(8,128)(2,1)S(1)}, u32[]{:S(2)}, u32[]{:S(2)}) collective-permute-start(bf16[128,1792]{1,0:T(8,128)(2,1)S(1)} %fusion.3.mine_ref), channel_id=1, source_target_pairs={{0,8},{4,12},{8,0},{12,4},{1,9},{5,13},{9,1},{13,5},{2,10},{6,14},... | collective-permute-start | bytes 1376264 | tf_op jit(solution)/shard_map/ppermute | solution.py:700
  107.3 4.6 %copy-start.6 = (bf16[64,4096]{1,0:T(8,128)(2,1)}, bf16[64,4096]{1,0:T(8,128)(2,1)S(1)}, u32[]{:S(2)}) copy-start(bf16[64,4096]{1,0:T(8,128)(2,1)S(1)} %collective-permute-done.14.refs_6_.refs_10_) | copy-start | bytes 1572868
  107.4 4.6 %copy-start.8 = (bf16[64,4096]{1,0:T(8,128)(2,1)}, bf16[64,4096]{1,0:T(8,128)(2,1)S(1)}, u32[]{:S(2)}) copy-start(bf16[64,4096]{1,0:T(8,128)(2,1)S(1)} %collective-permute-done.15.refs_7_.refs_11_) | copy-start | bytes 1572868
  111.9 1.0 copy-start.2
  112.9 5.5 %copy-start.10 = (bf16[128,1792]{1,0:T(8,128)(2,1)}, bf16[128,1792]{1,0:T(8,128)(2,1)S(1)}, u32[]{:S(2)}) copy-start(bf16[128,1792]{1,0:T(8,128)(2,1)S(1)} %collective-permute-done.20.refs_1_) | copy-start | bytes 1376260
  112.9 5.9 %collective-permute-start.22 = (bf16[128,1792]{1,0:T(8,128)(2,1)S(1)}, bf16[128,1792]{1,0:T(8,128)(2,1)S(1)}, u32[]{:S(2)}, u32[]{:S(2)}) collective-permute-start(bf16[128,1792]{1,0:T(8,128)(2,1)S(1)} %collective-permute-done.20.refs_1_), channel_id=1, source_target_pairs={{0,4},{4,0},{8,12},{12,8},{1,5},{5,1},{9,13},{13,9},{2,6},{6,2},{1... | collective-permute-start | bytes 1376264 | tf_op jit(solution)/shard_map/ppermute | solution.py:697
  112.9 7.4 %copy-start.3 = (bf16[8,256,256]{2,1,0:T(8,128)(2,1)S(1)}, bf16[8,256,256]{2,1,0:T(8,128)(2,1)}, u32[]{:S(2)}) copy-start(bf16[8,256,256]{2,1,0:T(8,128)(2,1)} %copy-done.2) | copy-start | bytes 3145732
  118.4 1.9 %collective-permute-start.21 = (bf16[128,1792]{1,0:T(8,128)(2,1)S(1)}, bf16[128,1792]{1,0:T(8,128)(2,1)S(1)}, u32[]{:S(2)}, u32[]{:S(2)}) collective-permute-start(bf16[128,1792]{1,0:T(8,128)(2,1)S(1)} %collective-permute-done.18.refs_0_), channel_id=1, source_target_pairs={{0,4},{4,0},{8,12},{12,8},{1,5},{5,1},{9,13},{13,9},{2,6},{6,2},{1... | collective-permute-start | bytes 1376264 | tf_op jit(solution)/shard_map/ppermute | solution.py:697
  120.3 1.0 copy-start.11
  121.3 12.3 %copy-start.7 = (bf16[64,4096]{1,0:T(8,128)(2,1)S(1)}, bf16[64,4096]{1,0:T(8,128)(2,1)}, u32[]{:S(2)}) copy-start(bf16[64,4096]{1,0:T(8,128)(2,1)} %copy-done.6) | copy-start | bytes 1572868
  121.3 12.3 %copy-start.9 = (bf16[64,4096]{1,0:T(8,128)(2,1)S(1)}, bf16[64,4096]{1,0:T(8,128)(2,1)}, u32[]{:S(2)}) copy-start(bf16[64,4096]{1,0:T(8,128)(2,1)} %copy-done.8) | copy-start | bytes 1572868
  132.5 5.8 %collective-permute-start.23 = (bf16[2,256,128]{2,1,0:T(8,128)(2,1)S(1)}, bf16[2,256,128]{2,1,0:T(8,128)(2,1)S(1)}, u32[]{:S(2)}, u32[]{:S(2)}) collective-permute-start(bf16[2,256,128]{2,1,0:T(8,128)(2,1)S(1)} %slice.51), channel_id=1, source_target_pairs={{0,1},{1,0},{2,3},{3,2},{4,5},{5,4},{6,7},{7,6},{8,9},{9,8},{10,11... | collective-permute-start | bytes 393224 | tf_op jit(solution)/shard_map/ppermute | solution.py:703
  136.9 9.8 %collective-permute-start.24 = (bf16[2,512,128]{2,1,0:T(8,128)(2,1)S(1)}, bf16[2,512,128]{2,1,0:T(8,128)(2,1)S(1)}, u32[]{:S(2)}, u32[]{:S(2)}) collective-permute-start(bf16[2,512,128]{2,1,0:T(8,128)(2,1)S(1)} %right_grads.2), channel_id=1, source_target_pairs={{0,1},{1,0},{2,3},{3,2},{4,5},{5,4},{6,7},{7,6},{8,9},{9,8},{10,11... | collective-permute-start | bytes 786440 | tf_op jit(solution)/shard_map/ppermute | solution.py:703
  138.4 12.7 %collective-permute-start.27 = (bf16[256,128]{1,0:T(8,128)(2,1)S(1)}, bf16[256,128]{1,0:T(8,128)(2,1)S(1)}, u32[]{:S(2)}, u32[]{:S(2)}) collective-permute-start(bf16[256,128]{1,0:T(8,128)(2,1)S(1)} %slice_bitcast_fusion.6), channel_id=1, source_target_pairs={{0,2},{1,3},{2,0},{3,1},{4,6},{5,7},{6,4},{7,5},{8,10},{9,11},{10,... | collective-permute-start | bytes 196616 | tf_op jit(solution)/shard_map/ppermute | solution.py:703
  146.8 5.2 %collective-permute-start.25 = (bf16[512,128]{1,0:T(8,128)(2,1)S(1)}, bf16[512,128]{1,0:T(8,128)(2,1)S(1)}, u32[]{:S(2)}, u32[]{:S(2)}) collective-permute-start(bf16[512,128]{1,0:T(8,128)(2,1)S(1)} %get-tuple-element.78), channel_id=1, source_target_pairs={{0,0},{1,4},{2,8},{3,12},{4,1},{5,5},{6,9},{7,13},{8,2},{9,6},{10,... | collective-permute-start | bytes 393224 | tf_op jit(solution)/shard_map/ppermute | solution.py:710
  147.5 14.8 %collective-permute-start.26 = (bf16[512,128]{1,0:T(8,128)(2,1)S(1)}, bf16[512,128]{1,0:T(8,128)(2,1)S(1)}, u32[]{:S(2)}, u32[]{:S(2)}) collective-permute-start(bf16[512,128]{1,0:T(8,128)(2,1)S(1)} %get-tuple-element.79), channel_id=1, source_target_pairs={{0,8},{1,12},{2,0},{3,4},{4,9},{5,13},{6,1},{7,5},{8,10},{9,14},{1... | collective-permute-start | bytes 393224 | tf_op jit(solution)/shard_map/ppermute | solution.py:710

commit v15 on v14

--- a/solution.py
+++ b/solution.py
@@ -302,25 +302,28 @@
     return grad_right, grad_left
 
 
-def cut_kernel(idx_ref, in_ref, out_ref):
-    out_ref[...] = in_ref[...]
-
-
-def cut_tokens(tokens, rows, row, column, cost=SMALL):
-    width = tokens.shape[1] // 2
-    steps = 4
+def cut_kernel(count, idx_ref, *refs):
+    for in_ref, out_ref in zip(refs[:count], refs[count:]):
+        out_ref[...] = in_ref[...]
+
+
+def cut_tokens(tokens, row, columns):
+    block = (tokens.shape[0] // 2, tokens.shape[1] // 2)
+    count = len(columns)
     return pl.pallas_call(
-        cut_kernel,
+        functools.partial(cut_kernel, count),
         grid_spec=pltpu.PrefetchScalarGridSpec(
             num_scalar_prefetch=1,
-            grid=(steps,),
-            in_specs=[pl.BlockSpec((rows, width // steps), lambda n, s: (s[0], s[1] * steps + n))],
-            out_specs=pl.BlockSpec((rows, width // steps), lambda n, s: (0, n)),
-        ),
-        out_shape=jax.ShapeDtypeStruct((rows, width), BF16),
-        cost_estimate=cost,
+            grid=(1,),
+            in_specs=[
+                pl.BlockSpec(block, lambda n, s, k=k: (s[0], s[1 + k])) for k in range(count)
+            ],
+            out_specs=[pl.BlockSpec(block, lambda n, s: (0, 0))] * count,
+        ),
+        out_shape=[jax.ShapeDtypeStruct(block, BF16)] * count,
+        cost_estimate=SMALL,
         name="cut_tokens",
-    )(jnp.stack([row, column]).astype(jnp.int32), tokens)
+    )(jnp.stack([row, *columns]).astype(jnp.int32), *[tokens] * count)
 
 
 def pack_kernel(left_ref, out_ref):
@@ -716,7 +719,7 @@
         return sum(term.astype(F32) for term in terms)
 
     near_tokens = swap(tokens)
-    first = cut_tokens(tokens, rows // 2, odd, 1 - chip)
+    first, rest = cut_tokens(tokens, odd, [1 - chip, chip])
     arrived = across(first)
     base = jnp.stack([odd, 1 - odd])
     mine_block = lax.div(part, BLK) * chip
@@ -741,7 +744,7 @@
     arrived = after(arrived, mine)
     partner = along(arrived, 1)
     near_arrived = swap(arrived)
-    late_first = across(cut_tokens(after(tokens, left_rows), rows // 2, odd, chip))
+    late_first = across(after(rest, mine))
     partner = after(partner, late_first, sums, factors)
     got_early = across(sums)
     more = along(after(factors, partner), 2)
@@ -752,13 +755,14 @@
     late_order = after(scalars(other_block), sums)
     mine, other = products(late_pieces, late_order, gate_weight, up_weight, 0, part)
     near = swap(other[0])
+    late_partner = along(after(late_first, mine), 1)
     mine_order = after(scalars(mine_block), mine)
     kept, other = products(
         own_pieces + late_pieces, mine_order, gate_weight, up_weight, 0, part
     )
     sums = add(mine[0], after(near, kept)).astype(BF16)
     got = across(sums)
-    near_kept = swap(after(other, got_early, sums, more))
+    near_kept = swap(after(other, got_early, sums, more, late_partner))
     factors = jnp.concatenate([factors, after(more, kept)], axis=0)
     more = along(factors, 1)
 
@@ -773,12 +777,12 @@
         [after(tokens, hidden1, sums)] + own[1:], order, factors, pairs, tensor_count
     )
     got1 = across(after(hidden1, mixed0))
-    late_partner = along(after(late_first, mixed0), 1)
     target1 = target_part(1.0, [], hidden1, after(near1, mixed0), down_weight, chip)
     hidden0 = activate(0, after(got, target1))
     got0 = across(hidden0)
     near0 = swap(hidden0)
-    late += [late_first, late_partner, swap(late_first), swap(late_partner)]
+    late_partner = after(late_partner, mixed0)
+    late += [late_first, late_partner, swap(after(late_first, mixed0)), swap(late_partner)]
     mixed1, rest1 = student_part(
         [after(late[0], hidden0)] + late[1:],
         order,

time: 164 us -> 160 us (0.976)
  Pallas kernels: 80.8 us -> 77.3 us
    ppermute x7, waiting for transfers between devices: 15.2 us -> 10 us  [along(): lax.ppermute(value, 'tensor', [(i, i ^ bit) for i in range(tensor_count)])]
    pallas_call x2 -> x1, Pallas kernels: 7.79 us -> 3.02 us  [cut_tokens(): pl.pallas_call(functools.partial(cut_kernel, count), grid_spec=pltpu.Pref...]
    ppermute x6, waiting for transfers between devices: 13 us -> 17 us  [across(): return lax.ppermute(value, 'fsdp', [(i, i ^ 2) for i in range(fsdp_count)])]
  transfers between devices with their start and end apart: 28 -> 28, of which waited for: 9 -> 10; matrix products, arithmetic and copies ran while one was open for 4% -> 4% of each run, Pallas kernels for 43% -> 42%
where the time goes in v15:
time: 160 us; the launch traced here: 159 us
  Pallas kernels  77.3 us (48%)
  waiting for transfers between devices  39.4 us (25%)
  starting transfers between devices  32 us (20%)
  other arithmetic  6.49 us (4%)
  local copies, waits for them, and re-layouts  2.83 us (2%)
    pallas_call x3, Pallas kernels, products(): pl.pallas_call(functools.partial(products_kernel, sets), grid_spec=pltpu....  33.4 us
    ppermute x6, waiting for transfers between devices, across(): return lax.ppermute(value, 'fsdp', [(i, i ^ 2) for i in range(fsdp_count)])  17 us
    ppermute x6, starting transfers between devices, across(): return lax.ppermute(value, 'fsdp', [(i, i ^ 2) for i in range(fsdp_count)])  13.8 us
    pallas_call x1, Pallas kernels, left_grads(): pl.pallas_call(functools.partial(left_kernel, chunks, scale), grid_spec=p...  11.1 us
    pallas_call x2, Pallas kernels, student_part(): pl.pallas_call(functools.partial(student_kernel, steps, bool(late), tenso...  10.6 us
    pallas_call x2, Pallas kernels, target_part(): pl.pallas_call(functools.partial(target_kernel, sign), grid_spec=pltpu.Pr...  10.5 us
    ppermute x7, waiting for transfers between devices, along(): lax.ppermute(value, 'tensor', [(i, i ^ bit) for i in range(tensor_count)])  10 us
    ppermute x3, waiting for transfers between devices, turn(): return lax.ppermute(value, both_axes, perm)  9.95 us
  transfers between devices with their start and end apart: 28, of which 10 were waited for; matrix products, arithmetic and copies ran while one was open for 4% of the time, Pallas kernels for 42%

profile of v15, /device:TPU:0, one launch (start us, length us, event | category | flops | bytes accessed | tf_op | source)
XLA Modules:
  0.0 158.8 jit_solution(15596586782263894967)
XLA Ops:
  0.6 0.5 collective-permute-start
  1.1 0.7 pad_add_fusion.1.idx_ref
  1.8 3.0 %cut_tokens.1 = (bf16[64,4096]{1,0:T(8,128)(2,1)}, bf16[64,4096]{1,0:T(8,128)(2,1)}) custom-call(s32[3]{0:T(128)} %pad_add_fusion.1.idx_ref, bf16[128,8192]{1,0:T(8,128)(2,1)} %refs_1_.11, bf16[128,8192]{1,0:T(8,128)(2,1)} %refs_1_.11), custom_call_target="tpu_custom_call" | custom-call | flops 1 | bytes 1 | tf_op jit(solution)/shard_map/cut_tokens/pallas_call | solution.py:313
  4.8 2.5 %collective-permute-start.1 = (bf16[64,4096]{1,0:T(8,128)(2,1)}, bf16[64,4096]{1,0:T(8,128)(2,1)S(1)}, u32[]{:S(2)}, u32[]{:S(2)}) collective-permute-start(bf16[64,4096]{1,0:T(8,128)(2,1)} %get-tuple-element.44), channel_id=1, source_target_pairs={{0,8},{4,12},{8,0},{12,4},{1,9},{5,13},{9,1},{13,5},{2,10},{6,14},... | collective-permute-start | bytes 1572872 | tf_op jit(solution)/shard_map/ppermute | solution.py:703
  7.3 0.1 concatenate.25.idx_ref
  7.4 0.0 collective-permute-done.refs_2_.refs_3_
  7.4 10.8 %gate_up_products.3 = (bf16[1,2,128,1792]{3,2,1,0:T(8,128)(2,1)S(1)}, bf16[1,2,128,1792]{3,2,1,0:T(8,128)(2,1)}) custom-call(s32[5]{0:T(128)S(1)} %concatenate.25.idx_ref, bf16[128,8192]{1,0:T(8,128)(2,1)S(1)} %copy-done, bf16[128,8192]{1,0:T(8,128)(2,1)S(1)} %copy-done, bf16[128,8192]{1,0:T(8,128)(2,1)} %collective-permute-done.refs_2_.refs_3_, ...), custom_call_target="tpu_custom_call" | custom-call | flops 1 | bytes 1 | tf_op jit(solution)/shard_map/gate_up_products/pallas_call | solution.py:374
  18.2 0.9 copy-done.1
  19.1 1.0 collective-permute-done.1.refs_0_.refs_4_
  20.1 1.8 %collective-permute-start.2 = (bf16[64,4096]{1,0:T(8,128)(2,1)S(1)}, bf16[64,4096]{1,0:T(8,128)(2,1)S(1)}, u32[]{:S(2)}, u32[]{:S(2)}) collective-permute-start(bf16[64,4096]{1,0:T(8,128)(2,1)S(1)} %collective-permute-done.1.refs_0_.refs_4_), channel_id=1, source_target_pairs={{0,1},{1,0},{2,3},{3,2},{4,5},{5,4},{6,7},{7,6},{8,9},{9,8},{10,11... | collective-permute-start | bytes 1572872 | tf_op jit(solution)/shard_map/ppermute | solution.py:706
  21.9 0.7 collective-permute-start.5
  22.6 1.8 %collective-permute-start.4 = (bf16[2,128,1792]{2,1,0:T(8,128)(2,1)}, bf16[2,128,1792]{2,1,0:T(8,128)(2,1)}, u32[]{:S(2)}, u32[]{:S(2)}) collective-permute-start(bf16[2,128,1792]{2,1,0:T(8,128)(2,1)} %bitcast.9), channel_id=1, source_target_pairs={{0,4},{4,0},{8,12},{12,8},{1,5},{5,1},{9,13},{13,9},{2,6},{6,2},{1... | collective-permute-start | bytes 2752520 | tf_op jit(solution)/shard_map/ppermute | solution.py:700
  24.4 1.6 %pack_left.1 = bf16[256,128]{1,0:T(8,128)(2,1)} custom-call(bf16[32,16,64]{2,1,0:T(8,128)(2,1)} %left_ref), custom_call_target="tpu_custom_call" | custom-call | flops 10000000000 | bytes 10000000 | tf_op jit(solution)/shard_map/pack_left/pallas_call | solution.py:339
  26.1 3.5 %collective-permute-start.3 = (bf16[64,4096]{1,0:T(8,128)(2,1)}, bf16[64,4096]{1,0:T(8,128)(2,1)S(1)}, u32[]{:S(2)}, u32[]{:S(2)}) collective-permute-start(bf16[64,4096]{1,0:T(8,128)(2,1)} %get-tuple-element.49), channel_id=1, source_target_pairs={{0,8},{4,12},{8,0},{12,4},{1,9},{5,13},{9,1},{13,5},{2,10},{6,14},... | collective-permute-start | bytes 1572872 | tf_op jit(solution)/shard_map/ppermute | solution.py:703
  29.6 0.9 maximum_bitcast_fusion
  30.5 2.6 %fusion.1 = bf16[2,128,1792]{2,1,0:T(8,128)(2,1)} fusion(bf16[2,128,1792]{2,1,0:T(8,128)(2,1)} %collective-permute-done.4, bf16[1,2,128,1792]{3,2,1,0:T(8,128)(2,1)} %copy-done.1), kind=kLoop, calls=%fused_computation.3 | loop fusion | flops 1835008 | bytes 2752512 | tf_op jit(solution)/shard_map/convert_element_type | solution.py:742
  33.1 10.1 %collective-permute-done.3.refs_4_.refs_8_ = bf16[64,4096]{1,0:T(8,128)(2,1)S(1)} collective-permute-done((bf16[64,4096]{1,0:T(8,128)(2,1)}, bf16[64,4096]{1,0:T(8,128)(2,1)S(1)}, u32[]{:S(2)}, u32[]{:S(2)}) %collective-permute-start.3) | collective-permute-done | bytes 524320 | tf_op jit(solution)/shard_map/ppermute | solution.py:703
  43.2 0.8 copy-done.2
  44.0 0.1 concatenate.27.idx_ref
  44.0 2.4 %collective-permute-start.9 = (bf16[2,128,1792]{2,1,0:T(8,128)(2,1)}, bf16[2,128,1792]{2,1,0:T(8,128)(2,1)S(1)}, u32[]{:S(2)}, u32[]{:S(2)}) collective-permute-start(bf16[2,128,1792]{2,1,0:T(8,128)(2,1)} %fusion.1), channel_id=1, source_target_pairs={{0,8},{4,12},{8,0},{12,4},{1,9},{5,13},{9,1},{13,5},{2,10},{6,14},... | collective-permute-start | bytes 2752520 | tf_op jit(solution)/shard_map/ppermute | solution.py:703
  46.4 0.3 collective-permute-start.11
  46.8 10.1 %gate_up_products.4 = (bf16[1,2,128,1792]{3,2,1,0:T(8,128)(2,1)S(1)}, bf16[1,2,128,1792]{3,2,1,0:T(8,128)(2,1)S(1)}) custom-call(s32[5]{0:T(128)S(1)} %concatenate.25.idx_ref, bf16[64,4096]{1,0:T(8,128)(2,1)S(1)} %collective-permute-done.1.refs_0_.refs_4_, bf16[64,4096]{1,0:T(8,128)(2,1)S(1)} %collective-permute-done.2.refs_1_.refs_5_, ...), custom_call_target="tpu_custom_call" | custom-call | flops 1 | bytes 1 | tf_op jit(solution)/shard_map/gate_up_products/pallas_call | solution.py:374
  56.9 0.3 collective-permute-start.10
  57.1 1.3 collective-permute-start.8
  58.4 12.5 %gate_up_products.5 = (bf16[2,2,128,1792]{3,2,1,0:T(8,128)(2,1)S(1)}, bf16[2,2,128,1792]{3,2,1,0:T(8,128)(2,1)S(1)}) custom-call(s32[5]{0:T(128)S(1)} %concatenate.27.idx_ref, bf16[128,8192]{1,0:T(8,128)(2,1)S(1)} %copy-done, bf16[128,8192]{1,0:T(8,128)(2,1)S(1)} %copy-done, bf16[128,8192]{1,0:T(8,128)(2,1)} %collective-permute-done.refs_2_.refs_3_, ...), custom_call_target="tpu_custom_call" | custom-call | flops 10000000000 | bytes 10000000 | tf_op jit(solution)/shard_map/gate_up_products/pallas_call | solution.py:374
  70.9 0.2 fusion
  71.2 0.1 collective-permute-done.8.refs_5_.refs_9_
  71.3 0.1 collective-permute-start.12
  71.4 0.1 pad_add_fusion.idx_ref
  71.5 1.3 collective-permute-start.13
  72.9 1.7 %collective-permute-start.16 = (bf16[2,128,1792]{2,1,0:T(8,128)(2,1)S(1)}, bf16[2,128,1792]{2,1,0:T(8,128)(2,1)S(1)}, u32[]{:S(2)}, u32[]{:S(2)}) collective-permute-start(bf16[2,128,1792]{2,1,0:T(8,128)(2,1)S(1)} %fusion), channel_id=1, source_target_pairs={{0,8},{4,12},{8,0},{12,4},{1,9},{5,13},{9,1},{13,5},{2,10},{6,14},... | collective-permute-start | bytes 2752520 | tf_op jit(solution)/shard_map/ppermute | solution.py:703
  74.6 0.5 collective-permute-done.12
  75.1 0.3 bitcast_add_fusion.1
  75.4 0.3 fusion.5.mine_ref
  75.6 0.2 collective-permute-start.17
  75.9 7.2 %collective-permute-done.13 = bf16[2,768,128]{2,1,0:T(8,128)(2,1)S(1)} collective-permute-done((bf16[2,768,128]{2,1,0:T(8,128)(2,1)S(1)}, bf16[2,768,128]{2,1,0:T(8,128)(2,1)S(1)}, u32[]{:S(2)}, u32[]{:S(2)}) %collective-permute-start.13) | collective-permute-done | bytes 393248 | tf_op jit(solution)/shard_map/ppermute | solution.py:706
  83.0 0.1 pad_maximum_fusion.refs_4_.refs_5_.refs_6_.refs_8_.refs_9_
  83.1 5.3 %student_part.2 = (bf16[8,256,256]{2,1,0:T(8,128)(2,1)S(1)}, f32[256,2048]{1,0:T(8,128)S(1)}, bf16[8,256,256]{2,1,0:T(8,128)(2,1)S(1)}) custom-call(s32[4]{0:T(128)S(1)} %pad_add_fusion.idx_ref, bf16[128,8192]{1,0:T(8,128)(2,1)S(1)} %copy-done, bf16[128,8192]{1,0:T(8,128)(2,1)S(1)} %copy-done, bf16[128,8192]{1,0:T(8,128)(2,1)} %collective-permute-done.refs_2_.refs_3_, ...), custom_call_target="tpu_custom_call" | custom-call | flops 10000000000 | bytes 10000000 | tf_op jit(solution)/shard_map/student_part/pallas_call | solution.py:550
  88.4 2.0 %collective-permute-start.20 = (bf16[128,1792]{1,0:T(8,128)(2,1)S(1)}, bf16[128,1792]{1,0:T(8,128)(2,1)S(1)}, u32[]{:S(2)}, u32[]{:S(2)}) collective-permute-start(bf16[128,1792]{1,0:T(8,128)(2,1)S(1)} %fusion.5.mine_ref), channel_id=1, source_target_pairs={{0,8},{4,12},{8,0},{12,4},{1,9},{5,13},{9,1},{13,5},{2,10},{6,14},... | collective-permute-start | bytes 1376264 | tf_op jit(solution)/shard_map/ppermute | solution.py:703
  90.4 0.5 collective-permute-start.15
  90.9 5.2 %target_part.2.refs_11_ = f32[256,2048]{1,0:T(8,128)S(1)} custom-call(s32[1]{0:T(128)} %bitcast.2.idx_ref, bf16[128,1792]{1,0:T(8,128)(2,1)S(1)} %fusion.5.mine_ref, bf16[128,1792]{1,0:T(8,128)(2,1)S(1)} %collective-permute-done.17.near_ref, bf16[3584,2048]{1,0:T(8,128)(2,1)} %refs_4_.5), custom_call_target="tpu_custom_call" | custom-call | flops 1 | bytes 1 | tf_op jit(solution)/shard_map/target_part/pallas_call | solution.py:412
  96.1 0.3 bitcast_add_fusion
  96.5 0.3 fusion.3.mine_ref
  96.7 0.1 collective-permute-start.19
  96.8 1.7 %collective-permute-start.18 = (bf16[128,1792]{1,0:T(8,128)(2,1)S(1)}, bf16[128,1792]{1,0:T(8,128)(2,1)S(1)}, u32[]{:S(2)}, u32[]{:S(2)}) collective-permute-start(bf16[128,1792]{1,0:T(8,128)(2,1)S(1)} %fusion.3.mine_ref), channel_id=1, source_target_pairs={{0,8},{4,12},{8,0},{12,4},{1,9},{5,13},{9,1},{13,5},{2,10},{6,14},... | collective-permute-start | bytes 1376264 | tf_op jit(solution)/shard_map/ppermute | solution.py:703
  98.5 5.3 %student_part.3 = (bf16[8,256,256]{2,1,0:T(8,128)(2,1)S(1)}, f32[256,2048]{1,0:T(8,128)S(1)}) custom-call(s32[4]{0:T(128)S(1)} %pad_add_fusion.idx_ref, bf16[64,4096]{1,0:T(8,128)(2,1)S(1)} %collective-permute-done.1.refs_0_.refs_4_, bf16[64,4096]{1,0:T(8,128)(2,1)S(1)} %collective-permute-done.2.refs_1_.refs_5_, ...), custom_call_target="tpu_custom_call" | custom-call | flops 10000000000 | bytes 10000000 | tf_op jit(solution)/shard_map/student_part/pallas_call | solution.py:550
  103.8 2.1 %collective-permute-done.20.refs_1_ = bf16[128,1792]{1,0:T(8,128)(2,1)S(1)} collective-permute-done((bf16[128,1792]{1,0:T(8,128)(2,1)S(1)}, bf16[128,1792]{1,0:T(8,128)(2,1)S(1)}, u32[]{:S(2)}, u32[]{:S(2)}) %collective-permute-start.20) | collective-permute-done | bytes 458784 | tf_op jit(solution)/shard_map/ppermute | solution.py:703
  105.9 5.3 %target_part.3.refs_5_ = f32[256,2048]{1,0:T(8,128)S(1)} custom-call(s32[1]{0:T(128)} %bitcast.2.idx_ref, bf16[128,1792]{1,0:T(8,128)(2,1)S(1)} %fusion.3.mine_ref, bf16[128,1792]{1,0:T(8,128)(2,1)S(1)} %collective-permute-done.19.near_ref, bf16[3584,2048]{1,0:T(8,128)(2,1)} %refs_4_.5, f32[256,2048]{1,0:T(8,128)S(1)} %get-tuple-element.77.refs_0_), custom_call_target="tpu_custom_call" | custom-call | flops 1 | bytes 1 | tf_op jit(solution)/shard_map/target_part/pallas_call | solution.py:412
  111.1 3.9 %collective-permute-done.18.refs_0_ = bf16[128,1792]{1,0:T(8,128)(2,1)S(1)} collective-permute-done((bf16[128,1792]{1,0:T(8,128)(2,1)S(1)}, bf16[128,1792]{1,0:T(8,128)(2,1)S(1)}, u32[]{:S(2)}, u32[]{:S(2)}) %collective-permute-start.18) | collective-permute-done | bytes 458784 | tf_op jit(solution)/shard_map/ppermute | solution.py:703
  115.0 1.8 %collective-permute-done.21.refs_2_ = bf16[128,1792]{1,0:T(8,128)(2,1)S(1)} collective-permute-done((bf16[128,1792]{1,0:T(8,128)(2,1)S(1)}, bf16[128,1792]{1,0:T(8,128)(2,1)S(1)}, u32[]{:S(2)}, u32[]{:S(2)}) %collective-permute-start.21) | collective-permute-done | bytes 458784 | tf_op jit(solution)/shard_map/ppermute | solution.py:700
  116.8 11.1 %left_grads.1 = (bf16[4,256,128]{2,1,0:T(8,128)(2,1)S(1)}, bf16[8,256,512]{2,1,0:T(8,128)(2,1)S(1)}) custom-call(s32[4]{0:T(128)S(1)} %pad_add_fusion.idx_ref, bf16[128,1792]{1,0:T(8,128)(2,1)S(1)} %collective-permute-done.18.refs_0_, bf16[128,1792]{1,0:T(8,128)(2,1)S(1)} %collective-permute-done.20.refs_1_, ...), custom_call_target="tpu_custom_call" | custom-call | flops 1 | bytes 1 | tf_op jit(solution)/shard_map/left_grads/pallas_call | solution.py:618
  128.0 0.9 collective-permute-start.23
  128.9 3.5 %right_grads.2 = bf16[2,512,128]{2,1,0:T(8,128)(2,1)S(1)} custom-call(s32[4]{0:T(128)S(1)} %pad_add_fusion.idx_ref, bf16[128,8192]{1,0:T(8,128)(2,1)S(1)} %copy-done, bf16[128,8192]{1,0:T(8,128)(2,1)S(1)} %copy-done, bf16[128,8192]{1,0:T(8,128)(2,1)} %collective-permute-done.refs_2_.refs_3_, bf16[128,8192]{1,0:T(8,128)(2,1)} %collective-permute-done.refs_2_.refs_3_, ...), custom_call_target="tpu_custom_call" | custom-call | flops 1 | bytes 1 | tf_op jit(solution)/shard_map/right_grads/pallas_call | solution.py:672
  132.5 1.2 collective-permute-start.24
  133.8 2.0 %collective-permute-start.27 = (bf16[256,128]{1,0:T(8,128)(2,1)S(1)}, bf16[256,128]{1,0:T(8,128)(2,1)S(1)}, u32[]{:S(2)}, u32[]{:S(2)}) collective-permute-start(bf16[256,128]{1,0:T(8,128)(2,1)S(1)} %slice_bitcast_fusion.6), channel_id=1, source_target_pairs={{0,2},{1,3},{2,0},{3,1},{4,6},{5,7},{6,4},{7,5},{8,10},{9,11},{10,... | collective-permute-start | bytes 196616 | tf_op jit(solution)/shard_map/ppermute | solution.py:706
  135.7 3.5 %right_grads.3 = bf16[2,512,128]{2,1,0:T(8,128)(2,1)S(1)} custom-call(s32[4]{0:T(128)S(1)} %pad_add_fusion.idx_ref, bf16[128,8192]{1,0:T(8,128)(2,1)S(1)} %copy-done, bf16[128,8192]{1,0:T(8,128)(2,1)S(1)} %copy-done, bf16[128,8192]{1,0:T(8,128)(2,1)} %collective-permute-done.refs_2_.refs_3_, bf16[128,8192]{1,0:T(8,128)(2,1)} %collective-permute-done.refs_2_.refs_3_, ...), custom_call_target="tpu_custom_call" | custom-call | flops 10000000000 | bytes 10000000 | tf_op jit(solution)/shard_map/right_grads/pallas_call | solution.py:672
  139.3 2.7 %collective-permute-done.24 = bf16[2,512,128]{2,1,0:T(8,128)(2,1)S(1)} collective-permute-done((bf16[2,512,128]{2,1,0:T(8,128)(2,1)S(1)}, bf16[2,512,128]{2,1,0:T(8,128)(2,1)S(1)}, u32[]{:S(2)}, u32[]{:S(2)}) %collective-permute-start.24) | collective-permute-done | bytes 262176 | tf_op jit(solution)/shard_map/ppermute | solution.py:706
  142.0 0.1 add_convert_fusion
  142.1 0.7 collective-permute-start.25
  142.8 4.4 %collective-permute-start.26 = (bf16[512,128]{1,0:T(8,128)(2,1)S(1)}, bf16[512,128]{1,0:T(8,128)(2,1)S(1)}, u32[]{:S(2)}, u32[]{:S(2)}) collective-permute-start(bf16[512,128]{1,0:T(8,128)(2,1)S(1)} %get-tuple-element.87), channel_id=1, source_target_pairs={{0,8},{1,12},{2,0},{3,4},{4,9},{5,13},{6,1},{7,5},{8,10},{9,14},{1... | collective-permute-start | bytes 393224 | tf_op jit(solution)/shard_map/ppermute | solution.py:713
  147.2 0.2 reshape.32
  147.4 0.7 copy.8
  148.2 9.9 %collective-permute-done.26 = bf16[512,128]{1,0:T(8,128)(2,1)S(1)} collective-permute-done((bf16[512,128]{1,0:T(8,128)(2,1)S(1)}, bf16[512,128]{1,0:T(8,128)(2,1)S(1)}, u32[]{:S(2)}, u32[]{:S(2)}) %collective-permute-start.26) | collective-permute-done | bytes 131104 | tf_op jit(solution)/shard_map/ppermute | solution.py:713
  158.1 0.7 convert_add_fusion.2
  (36 shorter events, 0.2 us)
Async XLA Ops:
  0.6 6.8 %collective-permute-start = (bf16[128,8192]{1,0:T(8,128)(2,1)}, bf16[128,8192]{1,0:T(8,128)(2,1)}, u32[]{:S(2)}, u32[]{:S(2)}) collective-permute-start(bf16[128,8192]{1,0:T(8,128)(2,1)} %refs_1_.11), channel_id=1, source_target_pairs={{0,4},{4,0},{8,12},{12,8},{1,5},{5,1},{9,13},{13,9},{2,6},{6,2},{1... | collective-permute-start | bytes 6291464 | tf_op jit(solution)/shard_map/ppermute | solution.py:700
  1.8 5.6 %copy-start = (bf16[128,8192]{1,0:T(8,128)(2,1)S(1)}, bf16[128,8192]{1,0:T(8,128)(2,1)}, u32[]{:S(2)}) copy-start(bf16[128,8192]{1,0:T(8,128)(2,1)} %refs_1_.11) | copy-start | bytes 6291460
  4.8 15.3 %collective-permute-start.1 = (bf16[64,4096]{1,0:T(8,128)(2,1)}, bf16[64,4096]{1,0:T(8,128)(2,1)S(1)}, u32[]{:S(2)}, u32[]{:S(2)}) collective-permute-start(bf16[64,4096]{1,0:T(8,128)(2,1)} %get-tuple-element.44), channel_id=1, source_target_pairs={{0,8},{4,12},{8,0},{12,4},{1,9},{5,13},{9,1},{13,5},{2,10},{6,14},... | collective-permute-start | bytes 1572872 | tf_op jit(solution)/shard_map/ppermute | solution.py:703
  7.4 14.5 %copy-start.4 = (bf16[16,32,128]{2,1,0:T(8,128)(2,1)S(1)}, bf16[16,32,128]{2,1,0:T(8,128)(2,1)}, u32[]{:S(2)}) copy-start(bf16[16,32,128]{2,1,0:T(8,128)(2,1)} %param.10) | copy-start | bytes 393220
  18.2 0.9 copy-start.1
  20.1 23.1 %collective-permute-start.2 = (bf16[64,4096]{1,0:T(8,128)(2,1)S(1)}, bf16[64,4096]{1,0:T(8,128)(2,1)S(1)}, u32[]{:S(2)}, u32[]{:S(2)}) collective-permute-start(bf16[64,4096]{1,0:T(8,128)(2,1)S(1)} %collective-permute-done.1.refs_0_.refs_4_), channel_id=1, source_target_pairs={{0,1},{1,0},{2,3},{3,2},{4,5},{5,4},{6,7},{7,6},{8,9},{9,8},{10,11... | collective-permute-start | bytes 1572872 | tf_op jit(solution)/shard_map/ppermute | solution.py:706
  21.9 24.8 %collective-permute-start.6 = (bf16[64,4096]{1,0:T(8,128)(2,1)S(1)}, bf16[64,4096]{1,0:T(8,128)(2,1)}, u32[]{:S(2)}, u32[]{:S(2)}) collective-permute-start(bf16[64,4096]{1,0:T(8,128)(2,1)S(1)} %collective-permute-done.1.refs_0_.refs_4_), channel_id=1, source_target_pairs={{0,4},{4,0},{8,12},{12,8},{1,5},{5,1},{9,13},{13,9},{2,6},{6,2},{1... | collective-permute-start | bytes 1572872 | tf_op jit(solution)/shard_map/ppermute | solution.py:700
  21.9 7.7 %collective-permute-start.5 = (bf16[16,32,128]{2,1,0:T(8,128)(2,1)S(1)}, bf16[16,32,128]{2,1,0:T(8,128)(2,1)S(1)}, u32[]{:S(2)}, u32[]{:S(2)}) collective-permute-start(bf16[16,32,128]{2,1,0:T(8,128)(2,1)S(1)} %copy-done.4), channel_id=1, source_target_pairs={{0,0},{1,4},{2,8},{3,12},{4,1},{5,5},{6,9},{7,13},{8,2},{9,6},{10,... | collective-permute-start | bytes 393224 | tf_op jit(solution)/shard_map/ppermute | solution.py:713
  22.6 7.9 %collective-permute-start.4 = (bf16[2,128,1792]{2,1,0:T(8,128)(2,1)}, bf16[2,128,1792]{2,1,0:T(8,128)(2,1)}, u32[]{:S(2)}, u32[]{:S(2)}) collective-permute-start(bf16[2,128,1792]{2,1,0:T(8,128)(2,1)} %bitcast.9), channel_id=1, source_target_pairs={{0,4},{4,0},{8,12},{12,8},{1,5},{5,1},{9,13},{13,9},{2,6},{6,2},{1... | collective-permute-start | bytes 2752520 | tf_op jit(solution)/shard_map/ppermute | solution.py:700
  26.1 17.1 %collective-permute-start.3 = (bf16[64,4096]{1,0:T(8,128)(2,1)}, bf16[64,4096]{1,0:T(8,128)(2,1)S(1)}, u32[]{:S(2)}, u32[]{:S(2)}) collective-permute-start(bf16[64,4096]{1,0:T(8,128)(2,1)} %get-tuple-element.49), channel_id=1, source_target_pairs={{0,8},{4,12},{8,0},{12,4},{1,9},{5,13},{9,1},{13,5},{2,10},{6,14},... | collective-permute-start | bytes 1572872 | tf_op jit(solution)/shard_map/ppermute | solution.py:703
  43.2 0.8 copy-start.2
  44.0 2.8 %collective-permute-start.7 = (bf16[64,4096]{1,0:T(8,128)(2,1)S(1)}, bf16[64,4096]{1,0:T(8,128)(2,1)}, u32[]{:S(2)}, u32[]{:S(2)}) collective-permute-start(bf16[64,4096]{1,0:T(8,128)(2,1)S(1)} %collective-permute-done.2.refs_1_.refs_5_), channel_id=1, source_target_pairs={{0,4},{4,0},{8,12},{12,8},{1,5},{5,1},{9,13},{13,9},{2,6},{6,2},{1... | collective-permute-start | bytes 1572872 | tf_op jit(solution)/shard_map/ppermute | solution.py:700
  44.0 13.1 %copy-start.3 = (bf16[64,4096]{1,0:T(8,128)(2,1)S(1)}, bf16[64,4096]{1,0:T(8,128)(2,1)}, u32[]{:S(2)}) copy-start(bf16[64,4096]{1,0:T(8,128)(2,1)} %copy-done.2) | copy-start | bytes 1572868
  44.0 27.1 %collective-permute-start.9 = (bf16[2,128,1792]{2,1,0:T(8,128)(2,1)}, bf16[2,128,1792]{2,1,0:T(8,128)(2,1)S(1)}, u32[]{:S(2)}, u32[]{:S(2)}) collective-permute-start(bf16[2,128,1792]{2,1,0:T(8,128)(2,1)} %fusion.1), channel_id=1, source_target_pairs={{0,8},{4,12},{8,0},{12,4},{1,9},{5,13},{9,1},{13,5},{2,10},{6,14},... | collective-permute-start | bytes 2752520 | tf_op jit(solution)/shard_map/ppermute | solution.py:703
  46.4 24.7 %collective-permute-start.11 = (bf16[1,768,128]{2,1,0:T(8,128)(2,1)S(1)}, bf16[1,768,128]{2,1,0:T(8,128)(2,1)S(1)}, u32[]{:S(2)}, u32[]{:S(2)}) collective-permute-start(bf16[1,768,128]{2,1,0:T(8,128)(2,1)S(1)} %maximum_bitcast_fusion), channel_id=1, source_target_pairs={{0,2},{1,3},{2,0},{3,1},{4,6},{5,7},{6,4},{7,5},{8,10},{9,11},{10,... | collective-permute-start | bytes 589832 | tf_op jit(solution)/shard_map/ppermute | solution.py:706
  56.9 14.0 %collective-permute-start.10 = (bf16[2,128,1792]{2,1,0:T(8,128)(2,1)S(1)}, bf16[2,128,1792]{2,1,0:T(8,128)(2,1)S(1)}, u32[]{:S(2)}, u32[]{:S(2)}) collective-permute-start(bf16[2,128,1792]{2,1,0:T(8,128)(2,1)S(1)} %bitcast.58), channel_id=1, source_target_pairs={{0,4},{4,0},{8,12},{12,8},{1,5},{5,1},{9,13},{13,9},{2,6},{6,2},{1... | collective-permute-start | bytes 2752520 | tf_op jit(solution)/shard_map/ppermute | solution.py:700
  57.1 14.2 %collective-permute-start.8 = (bf16[64,4096]{1,0:T(8,128)(2,1)S(1)}, bf16[64,4096]{1,0:T(8,128)(2,1)S(1)}, u32[]{:S(2)}, u32[]{:S(2)}) collective-permute-start(bf16[64,4096]{1,0:T(8,128)(2,1)S(1)} %copy-done.3), channel_id=1, source_target_pairs={{0,1},{1,0},{2,3},{3,2},{4,5},{5,4},{6,7},{7,6},{8,9},{9,8},{10,11... | collective-permute-start | bytes 1572872 | tf_op jit(solution)/shard_map/ppermute | solution.py:706
  71.3 3.8 %collective-permute-start.12 = (bf16[2,2,128,1792]{3,2,1,0:T(8,128)(2,1)S(1)}, bf16[2,2,128,1792]{3,2,1,0:T(8,128)(2,1)S(1)}, u32[]{:S(2)}, u32[]{:S(2)}) collective-permute-start(bf16[2,2,128,1792]{3,2,1,0:T(8,128)(2,1)S(1)} %get-tuple-element.64), channel_id=1, source_target_pairs={{0,4},{4,0},{8,12},{12,8},{1,5},{5,1},{9,13},{13,9},{2,6},{6,2},{1... | collective-permute-start | bytes 5505032 | tf_op jit(solution)/shard_map/ppermute | solution.py:700
  71.5 11.5 %collective-permute-start.13 = (bf16[2,768,128]{2,1,0:T(8,128)(2,1)S(1)}, bf16[2,768,128]{2,1,0:T(8,128)(2,1)S(1)}, u32[]{:S(2)}, u32[]{:S(2)}) collective-permute-start(bf16[2,768,128]{2,1,0:T(8,128)(2,1)S(1)} %pad_maximum_fusion.1), channel_id=1, source_target_pairs={{0,1},{1,0},{2,3},{3,2},{4,5},{5,4},{6,7},{7,6},{8,9},{9,8},{10,11... | collective-permute-start | bytes 1179656 | tf_op jit(solution)/shard_map/ppermute | solution.py:706
  72.9 23.3 %collective-permute-start.16 = (bf16[2,128,1792]{2,1,0:T(8,128)(2,1)S(1)}, bf16[2,128,1792]{2,1,0:T(8,128)(2,1)S(1)}, u32[]{:S(2)}, u32[]{:S(2)}) collective-permute-start(bf16[2,128,1792]{2,1,0:T(8,128)(2,1)S(1)} %fusion), channel_id=1, source_target_pairs={{0,8},{4,12},{8,0},{12,4},{1,9},{5,13},{9,1},{13,5},{2,10},{6,14},... | collective-permute-start | bytes 2752520 | tf_op jit(solution)/shard_map/ppermute | solution.py:703
  75.6 15.3 %collective-permute-start.17 = (bf16[128,1792]{1,0:T(8,128)(2,1)S(1)}, bf16[128,1792]{1,0:T(8,128)(2,1)S(1)}, u32[]{:S(2)}, u32[]{:S(2)}) collective-permute-start(bf16[128,1792]{1,0:T(8,128)(2,1)S(1)} %fusion.5.mine_ref), channel_id=1, source_target_pairs={{0,4},{4,0},{8,12},{12,8},{1,5},{5,1},{9,13},{13,9},{2,6},{6,2},{1... | collective-permute-start | bytes 1376264 | tf_op jit(solution)/shard_map/ppermute | solution.py:700
  88.4 17.4 %collective-permute-start.20 = (bf16[128,1792]{1,0:T(8,128)(2,1)S(1)}, bf16[128,1792]{1,0:T(8,128)(2,1)S(1)}, u32[]{:S(2)}, u32[]{:S(2)}) collective-permute-start(bf16[128,1792]{1,0:T(8,128)(2,1)S(1)} %fusion.5.mine_ref), channel_id=1, source_target_pairs={{0,8},{4,12},{8,0},{12,4},{1,9},{5,13},{9,1},{13,5},{2,10},{6,14},... | collective-permute-start | bytes 1376264 | tf_op jit(solution)/shard_map/ppermute | solution.py:703
  90.4 8.1 %collective-permute-start.14 = (bf16[64,4096]{1,0:T(8,128)(2,1)S(1)}, bf16[64,4096]{1,0:T(8,128)(2,1)S(1)}, u32[]{:S(2)}, u32[]{:S(2)}) collective-permute-start(bf16[64,4096]{1,0:T(8,128)(2,1)S(1)} %copy-done.3), channel_id=1, source_target_pairs={{0,4},{4,0},{8,12},{12,8},{1,5},{5,1},{9,13},{13,9},{2,6},{6,2},{1... | collective-permute-start | bytes 1572872 | tf_op jit(solution)/shard_map/ppermute | solution.py:700
  90.4 8.1 %collective-permute-start.15 = (bf16[64,4096]{1,0:T(8,128)(2,1)S(1)}, bf16[64,4096]{1,0:T(8,128)(2,1)S(1)}, u32[]{:S(2)}, u32[]{:S(2)}) collective-permute-start(bf16[64,4096]{1,0:T(8,128)(2,1)S(1)} %collective-permute-done.8.refs_5_.refs_9_), channel_id=1, source_target_pairs={{0,4},{4,0},{8,12},{12,8},{1,5},{5,1},{9,13},{13,9},{2,6},{6,2},{1... | collective-permute-start | bytes 1572872 | tf_op jit(solution)/shard_map/ppermute | solution.py:700
  96.7 9.2 %collective-permute-start.19 = (bf16[128,1792]{1,0:T(8,128)(2,1)S(1)}, bf16[128,1792]{1,0:T(8,128)(2,1)S(1)}, u32[]{:S(2)}, u32[]{:S(2)}) collective-permute-start(bf16[128,1792]{1,0:T(8,128)(2,1)S(1)} %fusion.3.mine_ref), channel_id=1, source_target_pairs={{0,4},{4,0},{8,12},{12,8},{1,5},{5,1},{9,13},{13,9},{2,6},{6,2},{1... | collective-permute-start | bytes 1376264 | tf_op jit(solution)/shard_map/ppermute | solution.py:700
  96.8 18.2 %collective-permute-start.18 = (bf16[128,1792]{1,0:T(8,128)(2,1)S(1)}, bf16[128,1792]{1,0:T(8,128)(2,1)S(1)}, u32[]{:S(2)}, u32[]{:S(2)}) collective-permute-start(bf16[128,1792]{1,0:T(8,128)(2,1)S(1)} %fusion.3.mine_ref), channel_id=1, source_target_pairs={{0,8},{4,12},{8,0},{12,4},{1,9},{5,13},{9,1},{13,5},{2,10},{6,14},... | collective-permute-start | bytes 1376264 | tf_op jit(solution)/shard_map/ppermute | solution.py:703
  105.9 9.1 %collective-permute-start.22 = (bf16[128,1792]{1,0:T(8,128)(2,1)S(1)}, bf16[128,1792]{1,0:T(8,128)(2,1)S(1)}, u32[]{:S(2)}, u32[]{:S(2)}) collective-permute-start(bf16[128,1792]{1,0:T(8,128)(2,1)S(1)} %collective-permute-done.20.refs_1_), channel_id=1, source_target_pairs={{0,4},{4,0},{8,12},{12,8},{1,5},{5,1},{9,13},{13,9},{2,6},{6,2},{1... | collective-permute-start | bytes 1376264 | tf_op jit(solution)/shard_map/ppermute | solution.py:700
  115.0 1.8 %collective-permute-start.21 = (bf16[128,1792]{1,0:T(8,128)(2,1)S(1)}, bf16[128,1792]{1,0:T(8,128)(2,1)S(1)}, u32[]{:S(2)}, u32[]{:S(2)}) collective-permute-start(bf16[128,1792]{1,0:T(8,128)(2,1)S(1)} %collective-permute-done.18.refs_0_), channel_id=1, source_target_pairs={{0,4},{4,0},{8,12},{12,8},{1,5},{5,1},{9,13},{13,9},{2,6},{6,2},{1... | collective-permute-start | bytes 1376264 | tf_op jit(solution)/shard_map/ppermute | solution.py:700
  128.0 5.7 %collective-permute-start.23 = (bf16[2,256,128]{2,1,0:T(8,128)(2,1)S(1)}, bf16[2,256,128]{2,1,0:T(8,128)(2,1)S(1)}, u32[]{:S(2)}, u32[]{:S(2)}) collective-permute-start(bf16[2,256,128]{2,1,0:T(8,128)(2,1)S(1)} %slice.51), channel_id=1, source_target_pairs={{0,1},{1,0},{2,3},{3,2},{4,5},{5,4},{6,7},{7,6},{8,9},{9,8},{10,11... | collective-permute-start | bytes 393224 | tf_op jit(solution)/shard_map/ppermute | solution.py:706
  132.5 9.5 %collective-permute-start.24 = (bf16[2,512,128]{2,1,0:T(8,128)(2,1)S(1)}, bf16[2,512,128]{2,1,0:T(8,128)(2,1)S(1)}, u32[]{:S(2)}, u32[]{:S(2)}) collective-permute-start(bf16[2,512,128]{2,1,0:T(8,128)(2,1)S(1)} %right_grads.2), channel_id=1, source_target_pairs={{0,1},{1,0},{2,3},{3,2},{4,5},{5,4},{6,7},{7,6},{8,9},{9,8},{10,11... | collective-permute-start | bytes 786440 | tf_op jit(solution)/shard_map/ppermute | solution.py:706
  133.8 13.5 %collective-permute-start.27 = (bf16[256,128]{1,0:T(8,128)(2,1)S(1)}, bf16[256,128]{1,0:T(8,128)(2,1)S(1)}, u32[]{:S(2)}, u32[]{:S(2)}) collective-permute-start(bf16[256,128]{1,0:T(8,128)(2,1)S(1)} %slice_bitcast_fusion.6), channel_id=1, source_target_pairs={{0,2},{1,3},{2,0},{3,1},{4,6},{5,7},{6,4},{7,5},{8,10},{9,11},{10,... | collective-permute-start | bytes 196616 | tf_op jit(solution)/shard_map/ppermute | solution.py:706
  142.1 6.1 %collective-permute-start.25 = (bf16[512,128]{1,0:T(8,128)(2,1)S(1)}, bf16[512,128]{1,0:T(8,128)(2,1)S(1)}, u32[]{:S(2)}, u32[]{:S(2)}) collective-permute-start(bf16[512,128]{1,0:T(8,128)(2,1)S(1)} %get-tuple-element.86), channel_id=1, source_target_pairs={{0,0},{1,4},{2,8},{3,12},{4,1},{5,5},{6,9},{7,13},{8,2},{9,6},{10,... | collective-permute-start | bytes 393224 | tf_op jit(solution)/shard_map/ppermute | solution.py:713
  142.8 15.3 %collective-permute-start.26 = (bf16[512,128]{1,0:T(8,128)(2,1)S(1)}, bf16[512,128]{1,0:T(8,128)(2,1)S(1)}, u32[]{:S(2)}, u32[]{:S(2)}) collective-permute-start(bf16[512,128]{1,0:T(8,128)(2,1)S(1)} %get-tuple-element.87), channel_id=1, source_target_pairs={{0,8},{1,12},{2,0},{3,4},{4,9},{5,13},{6,1},{7,5},{8,10},{9,14},{1... | collective-permute-start | bytes 393224 | tf_op jit(solution)/shard_map/ppermute | solution.py:713

commit v16 on v15

--- a/solution.py
+++ b/solution.py
@@ -745,7 +745,7 @@
     partner = along(arrived, 1)
     near_arrived = swap(arrived)
     late_first = across(after(rest, mine))
-    partner = after(partner, late_first, sums, factors)
+    partner = after(partner, sums, factors)
     got_early = across(sums)
     more = along(after(factors, partner), 2)
     order = jnp.concatenate([base, jnp.stack([chip, z])]).astype(jnp.int32)
@@ -754,17 +754,17 @@
     late_pieces = [(t, None, 3) for t in late]
     late_order = after(scalars(other_block), sums)
     mine, other = products(late_pieces, late_order, gate_weight, up_weight, 0, part)
-    near = swap(other[0])
-    late_partner = along(after(late_first, mine), 1)
+    near = swap(after(other[0], late_first))
+    factors = jnp.concatenate([factors, after(more, mine)], axis=0)
+    more = along(factors, 1)
     mine_order = after(scalars(mine_block), mine)
     kept, other = products(
         own_pieces + late_pieces, mine_order, gate_weight, up_weight, 0, part
     )
     sums = add(mine[0], after(near, kept)).astype(BF16)
     got = across(sums)
-    near_kept = swap(after(other, got_early, sums, more, late_partner))
-    factors = jnp.concatenate([factors, after(more, kept)], axis=0)
-    more = along(factors, 1)
+    near_kept = swap(after(other, got_early, sums, more))
+    late_partner = along(after(late_first, kept), 1)
 
     def activate(u, term):
         total = add(kept[u], near_kept[u], term)

time: 160 us -> 164 us (1.025)
  starting transfers between devices: 32 us -> 36.7 us
    ppermute x12, starting transfers between devices: 3.49 us -> 7.4 us  [swap(): return lax.ppermute(value, 'fsdp', [(i, i ^ 1) for i in range(fsdp_count)])]
    ppermute x7, starting transfers between devices: 8.89 us -> 11.2 us  [along(): lax.ppermute(value, 'tensor', [(i, i ^ bit) for i in range(tensor_count)])]
    ppermute x6, starting transfers between devices: 13.8 us -> 12.1 us  [across(): return lax.ppermute(value, 'fsdp', [(i, i ^ 2) for i in range(fsdp_count)])]
  transfers between devices with their start and end apart: 28 -> 28, of which waited for: 10 -> 11; matrix products, arithmetic and copies ran while one was open for 4% -> 4% of each run, Pallas kernels for 42% -> 41%
where the time goes in v16:
time: 164 us; the launch traced here: 163 us
  Pallas kernels  77.7 us (47%)
  waiting for transfers between devices  39.3 us (24%)
  starting transfers between devices  36.7 us (22%)
  other arithmetic  6.46 us (4%)
  local copies, waits for them, and re-layouts  2.05 us (1%)
    pallas_call x3, Pallas kernels, products(): pl.pallas_call(functools.partial(products_kernel, sets), grid_spec=pltpu....  33.4 us
    ppermute x6, waiting for transfers between devices, across(): return lax.ppermute(value, 'fsdp', [(i, i ^ 2) for i in range(fsdp_count)])  15.5 us
    ppermute x6, starting transfers between devices, across(): return lax.ppermute(value, 'fsdp', [(i, i ^ 2) for i in range(fsdp_count)])  12.1 us
    ppermute x7, starting transfers between devices, along(): lax.ppermute(value, 'tensor', [(i, i ^ bit) for i in range(tensor_count)])  11.2 us
    pallas_call x1, Pallas kernels, left_grads(): pl.pallas_call(functools.partial(left_kernel, chunks, scale), grid_spec=p...  11.1 us
    pallas_call x2, Pallas kernels, student_part(): pl.pallas_call(functools.partial(student_kernel, steps, bool(late), tenso...  10.8 us
    pallas_call x2, Pallas kernels, target_part(): pl.pallas_call(functools.partial(target_kernel, sign), grid_spec=pltpu.Pr...  10.5 us
    ppermute x3, waiting for transfers between devices, turn(): return lax.ppermute(value, both_axes, perm)  10.1 us
  transfers between devices with their start and end apart: 28, of which 11 were waited for; matrix products, arithmetic and copies ran while one was open for 4% of the time, Pallas kernels for 41%

profile of v16, /device:TPU:0, one launch (start us, length us, event | category | flops | bytes accessed | tf_op | source)
XLA Modules:
  0.0 163.1 jit_solution(8492175898455856735)
XLA Ops:
  0.6 0.5 collective-permute-start
  1.1 0.6 pad_add_fusion.1.idx_ref
  1.8 3.1 %cut_tokens.1 = (bf16[64,4096]{1,0:T(8,128)(2,1)}, bf16[64,4096]{1,0:T(8,128)(2,1)}) custom-call(s32[3]{0:T(128)} %pad_add_fusion.1.idx_ref, bf16[128,8192]{1,0:T(8,128)(2,1)} %refs_1_.11, bf16[128,8192]{1,0:T(8,128)(2,1)} %refs_1_.11), custom_call_target="tpu_custom_call" | custom-call | flops 1 | bytes 1 | tf_op jit(solution)/shard_map/cut_tokens/pallas_call | solution.py:313
  4.8 2.5 %collective-permute-start.1 = (bf16[64,4096]{1,0:T(8,128)(2,1)}, bf16[64,4096]{1,0:T(8,128)(2,1)S(1)}, u32[]{:S(2)}, u32[]{:S(2)}) collective-permute-start(bf16[64,4096]{1,0:T(8,128)(2,1)} %get-tuple-element.45), channel_id=1, source_target_pairs={{0,8},{4,12},{8,0},{12,4},{1,9},{5,13},{9,1},{13,5},{2,10},{6,14},... | collective-permute-start | bytes 1572872 | tf_op jit(solution)/shard_map/ppermute | solution.py:703
  7.3 0.1 concatenate.25.idx_ref
  7.4 0.0 collective-permute-done.refs_2_.refs_3_
  7.4 10.8 %gate_up_products.3 = (bf16[1,2,128,1792]{3,2,1,0:T(8,128)(2,1)S(1)}, bf16[1,2,128,1792]{3,2,1,0:T(8,128)(2,1)}) custom-call(s32[5]{0:T(128)S(1)} %concatenate.25.idx_ref, bf16[128,8192]{1,0:T(8,128)(2,1)S(1)} %copy-done, bf16[128,8192]{1,0:T(8,128)(2,1)S(1)} %copy-done, bf16[128,8192]{1,0:T(8,128)(2,1)} %collective-permute-done.refs_2_.refs_3_, ...), custom_call_target="tpu_custom_call" | custom-call | flops 1 | bytes 1 | tf_op jit(solution)/shard_map/gate_up_products/pallas_call | solution.py:374
  18.2 0.9 copy-done.1
  19.1 1.0 collective-permute-done.1.refs_0_.refs_4_
  20.1 1.8 %collective-permute-start.2 = (bf16[64,4096]{1,0:T(8,128)(2,1)S(1)}, bf16[64,4096]{1,0:T(8,128)(2,1)S(1)}, u32[]{:S(2)}, u32[]{:S(2)}) collective-permute-start(bf16[64,4096]{1,0:T(8,128)(2,1)S(1)} %collective-permute-done.1.refs_0_.refs_4_), channel_id=1, source_target_pairs={{0,1},{1,0},{2,3},{3,2},{4,5},{5,4},{6,7},{7,6},{8,9},{9,8},{10,11... | collective-permute-start | bytes 1572872 | tf_op jit(solution)/shard_map/ppermute | solution.py:706
  21.9 0.7 collective-permute-start.4
  22.6 1.8 %collective-permute-start.3 = (bf16[2,128,1792]{2,1,0:T(8,128)(2,1)}, bf16[2,128,1792]{2,1,0:T(8,128)(2,1)}, u32[]{:S(2)}, u32[]{:S(2)}) collective-permute-start(bf16[2,128,1792]{2,1,0:T(8,128)(2,1)} %bitcast.9), channel_id=1, source_target_pairs={{0,4},{4,0},{8,12},{12,8},{1,5},{5,1},{9,13},{13,9},{2,6},{6,2},{1... | collective-permute-start | bytes 2752520 | tf_op jit(solution)/shard_map/ppermute | solution.py:700
  24.4 1.6 pack_left.1
  26.1 0.0 collective-permute-done.4
  26.1 0.9 maximum_bitcast_fusion
  26.9 2.6 %fusion.1 = bf16[2,128,1792]{2,1,0:T(8,128)(2,1)} fusion(bf16[2,128,1792]{2,1,0:T(8,128)(2,1)} %collective-permute-done.3, bf16[1,2,128,1792]{3,2,1,0:T(8,128)(2,1)} %copy-done.1), kind=kLoop, calls=%fused_computation.3 | loop fusion | flops 1835008 | bytes 2752512 | tf_op jit(solution)/shard_map/convert_element_type | solution.py:742
  29.5 5.7 %collective-permute-done.2.refs_1_.refs_5_ = bf16[64,4096]{1,0:T(8,128)(2,1)S(1)} collective-permute-done((bf16[64,4096]{1,0:T(8,128)(2,1)S(1)}, bf16[64,4096]{1,0:T(8,128)(2,1)S(1)}, u32[]{:S(2)}, u32[]{:S(2)}) %collective-permute-start.2) | collective-permute-done | bytes 524320 | tf_op jit(solution)/shard_map/ppermute | solution.py:706
  35.2 4.7 %collective-permute-start.6 = (bf16[64,4096]{1,0:T(8,128)(2,1)S(1)}, bf16[64,4096]{1,0:T(8,128)(2,1)}, u32[]{:S(2)}, u32[]{:S(2)}) collective-permute-start(bf16[64,4096]{1,0:T(8,128)(2,1)S(1)} %collective-permute-done.2.refs_1_.refs_5_), channel_id=1, source_target_pairs={{0,4},{4,0},{8,12},{12,8},{1,5},{5,1},{9,13},{13,9},{2,6},{6,2},{1... | collective-permute-start | bytes 1572872 | tf_op jit(solution)/shard_map/ppermute | solution.py:700
  39.9 3.5 %collective-permute-start.7 = (bf16[64,4096]{1,0:T(8,128)(2,1)}, bf16[64,4096]{1,0:T(8,128)(2,1)}, u32[]{:S(2)}, u32[]{:S(2)}) collective-permute-start(bf16[64,4096]{1,0:T(8,128)(2,1)} %get-tuple-element.55), channel_id=1, source_target_pairs={{0,8},{4,12},{8,0},{12,4},{1,9},{5,13},{9,1},{13,5},{2,10},{6,14},... | collective-permute-start | bytes 1572872 | tf_op jit(solution)/shard_map/ppermute | solution.py:703
  43.5 1.5 collective-permute-start.11
  44.9 0.1 concatenate.27.idx_ref
  45.0 0.6 collective-permute-start.9
  45.7 10.1 %gate_up_products.4 = (bf16[1,2,128,1792]{3,2,1,0:T(8,128)(2,1)S(1)}, bf16[1,2,128,1792]{3,2,1,0:T(8,128)(2,1)S(1)}) custom-call(s32[5]{0:T(128)S(1)} %concatenate.25.idx_ref, bf16[64,4096]{1,0:T(8,128)(2,1)S(1)} %collective-permute-done.1.refs_0_.refs_4_, bf16[64,4096]{1,0:T(8,128)(2,1)S(1)} %collective-permute-done.2.refs_1_.refs_5_, ...), custom_call_target="tpu_custom_call" | custom-call | flops 1 | bytes 1 | tf_op jit(solution)/shard_map/gate_up_products/pallas_call | solution.py:374
  55.9 1.8 %collective-permute-start.12 = (bf16[2,768,128]{2,1,0:T(8,128)(2,1)S(1)}, bf16[2,768,128]{2,1,0:T(8,128)(2,1)S(1)}, u32[]{:S(2)}, u32[]{:S(2)}) collective-permute-start(bf16[2,768,128]{2,1,0:T(8,128)(2,1)S(1)} %pad_maximum_fusion.1), channel_id=1, source_target_pairs={{0,1},{1,0},{2,3},{3,2},{4,5},{5,4},{6,7},{7,6},{8,9},{9,8},{10,11... | collective-permute-start | bytes 1179656 | tf_op jit(solution)/shard_map/ppermute | solution.py:706
  57.6 12.5 %gate_up_products.5 = (bf16[2,2,128,1792]{3,2,1,0:T(8,128)(2,1)S(1)}, bf16[2,2,128,1792]{3,2,1,0:T(8,128)(2,1)S(1)}) custom-call(s32[5]{0:T(128)S(1)} %concatenate.27.idx_ref, bf16[128,8192]{1,0:T(8,128)(2,1)S(1)} %copy-done, bf16[128,8192]{1,0:T(8,128)(2,1)S(1)} %copy-done, bf16[128,8192]{1,0:T(8,128)(2,1)} %collective-permute-done.refs_2_.refs_3_, ...), custom_call_target="tpu_custom_call" | custom-call | flops 10000000000 | bytes 10000000 | tf_op jit(solution)/shard_map/gate_up_products/pallas_call | solution.py:374
  70.2 0.2 fusion
  70.4 5.0 %collective-permute-done.9 = bf16[2,128,1792]{2,1,0:T(8,128)(2,1)S(1)} collective-permute-done((bf16[2,128,1792]{2,1,0:T(8,128)(2,1)}, bf16[2,128,1792]{2,1,0:T(8,128)(2,1)S(1)}, u32[]{:S(2)}, u32[]{:S(2)}) %collective-permute-start.9) | collective-permute-done | bytes 917536 | tf_op jit(solution)/shard_map/ppermute | solution.py:703
  75.4 0.1 pad_add_fusion.idx_ref
  75.5 0.0 collective-permute-start.8
  75.5 1.8 %collective-permute-start.16 = (bf16[2,128,1792]{2,1,0:T(8,128)(2,1)S(1)}, bf16[2,128,1792]{2,1,0:T(8,128)(2,1)S(1)}, u32[]{:S(2)}, u32[]{:S(2)}) collective-permute-start(bf16[2,128,1792]{2,1,0:T(8,128)(2,1)S(1)} %fusion), channel_id=1, source_target_pairs={{0,8},{4,12},{8,0},{12,4},{1,9},{5,13},{9,1},{13,5},{2,10},{6,14},... | collective-permute-start | bytes 2752520 | tf_op jit(solution)/shard_map/ppermute | solution.py:703
  77.3 1.9 %collective-permute-done.13 = bf16[2,2,128,1792]{3,2,1,0:T(8,128)(2,1)S(1)} collective-permute-done((bf16[2,2,128,1792]{3,2,1,0:T(8,128)(2,1)S(1)}, bf16[2,2,128,1792]{3,2,1,0:T(8,128)(2,1)S(1)}, u32[]{:S(2)}, u32[]{:S(2)}) %collective-permute-start.13) | collective-permute-done | bytes 1835040 | tf_op jit(solution)/shard_map/ppermute | solution.py:700
  79.2 0.3 bitcast_add_fusion.1
  79.5 0.3 fusion.5.mine_ref
  79.8 0.2 collective-permute-start.17
  80.0 0.1 pad_maximum_fusion.refs_4_.refs_5_.refs_6_.refs_8_.refs_9_
  80.1 5.3 %student_part.2 = (bf16[8,256,256]{2,1,0:T(8,128)(2,1)S(1)}, f32[256,2048]{1,0:T(8,128)S(1)}, bf16[8,256,256]{2,1,0:T(8,128)(2,1)S(1)}) custom-call(s32[4]{0:T(128)S(1)} %pad_add_fusion.idx_ref, bf16[128,8192]{1,0:T(8,128)(2,1)S(1)} %copy-done, bf16[128,8192]{1,0:T(8,128)(2,1)S(1)} %copy-done, bf16[128,8192]{1,0:T(8,128)(2,1)} %collective-permute-done.refs_2_.refs_3_, ...), custom_call_target="tpu_custom_call" | custom-call | flops 10000000000 | bytes 10000000 | tf_op jit(solution)/shard_map/student_part/pallas_call | solution.py:550
  85.4 1.8 %collective-permute-start.20 = (bf16[128,1792]{1,0:T(8,128)(2,1)S(1)}, bf16[128,1792]{1,0:T(8,128)(2,1)S(1)}, u32[]{:S(2)}, u32[]{:S(2)}) collective-permute-start(bf16[128,1792]{1,0:T(8,128)(2,1)S(1)} %fusion.5.mine_ref), channel_id=1, source_target_pairs={{0,8},{4,12},{8,0},{12,4},{1,9},{5,13},{9,1},{13,5},{2,10},{6,14},... | collective-permute-start | bytes 1376264 | tf_op jit(solution)/shard_map/ppermute | solution.py:703
  87.2 0.1 collective-permute-start.14
  87.3 2.8 %collective-permute-done.8.refs_5_.refs_9_ = bf16[64,4096]{1,0:T(8,128)(2,1)S(1)} collective-permute-done((bf16[64,4096]{1,0:T(8,128)(2,1)}, bf16[64,4096]{1,0:T(8,128)(2,1)S(1)}, u32[]{:S(2)}, u32[]{:S(2)}) %collective-permute-start.8) | collective-permute-done | bytes 524320 | tf_op jit(solution)/shard_map/ppermute | solution.py:706
  90.1 5.2 %target_part.2.refs_11_ = f32[256,2048]{1,0:T(8,128)S(1)} custom-call(s32[1]{0:T(128)} %bitcast.2.idx_ref, bf16[128,1792]{1,0:T(8,128)(2,1)S(1)} %fusion.5.mine_ref, bf16[128,1792]{1,0:T(8,128)(2,1)S(1)} %collective-permute-done.17.near_ref, bf16[3584,2048]{1,0:T(8,128)(2,1)} %refs_4_.5), custom_call_target="tpu_custom_call" | custom-call | flops 1 | bytes 1 | tf_op jit(solution)/shard_map/target_part/pallas_call | solution.py:412
  95.3 3.5 %collective-permute-done.16 = bf16[2,128,1792]{2,1,0:T(8,128)(2,1)S(1)} collective-permute-done((bf16[2,128,1792]{2,1,0:T(8,128)(2,1)S(1)}, bf16[2,128,1792]{2,1,0:T(8,128)(2,1)S(1)}, u32[]{:S(2)}, u32[]{:S(2)}) %collective-permute-start.16) | collective-permute-done | bytes 917536 | tf_op jit(solution)/shard_map/ppermute | solution.py:703
  98.7 0.3 bitcast_add_fusion
  99.0 0.3 fusion.3.mine_ref
  99.3 0.1 collective-permute-start.19
  99.4 1.8 %collective-permute-start.18 = (bf16[128,1792]{1,0:T(8,128)(2,1)S(1)}, bf16[128,1792]{1,0:T(8,128)(2,1)S(1)}, u32[]{:S(2)}, u32[]{:S(2)}) collective-permute-start(bf16[128,1792]{1,0:T(8,128)(2,1)S(1)} %fusion.3.mine_ref), channel_id=1, source_target_pairs={{0,8},{4,12},{8,0},{12,4},{1,9},{5,13},{9,1},{13,5},{2,10},{6,14},... | collective-permute-start | bytes 1376264 | tf_op jit(solution)/shard_map/ppermute | solution.py:703
  101.2 5.5 %student_part.3 = (bf16[8,256,256]{2,1,0:T(8,128)(2,1)S(1)}, f32[256,2048]{1,0:T(8,128)S(1)}) custom-call(s32[4]{0:T(128)S(1)} %pad_add_fusion.idx_ref, bf16[64,4096]{1,0:T(8,128)(2,1)S(1)} %collective-permute-done.1.refs_0_.refs_4_, bf16[64,4096]{1,0:T(8,128)(2,1)S(1)} %collective-permute-done.2.refs_1_.refs_5_, ...), custom_call_target="tpu_custom_call" | custom-call | flops 10000000000 | bytes 10000000 | tf_op jit(solution)/shard_map/student_part/pallas_call | solution.py:550
  106.7 1.9 %collective-permute-done.20.refs_1_ = bf16[128,1792]{1,0:T(8,128)(2,1)S(1)} collective-permute-done((bf16[128,1792]{1,0:T(8,128)(2,1)S(1)}, bf16[128,1792]{1,0:T(8,128)(2,1)S(1)}, u32[]{:S(2)}, u32[]{:S(2)}) %collective-permute-start.20) | collective-permute-done | bytes 458784 | tf_op jit(solution)/shard_map/ppermute | solution.py:703
  108.6 5.3 %target_part.3.refs_5_ = f32[256,2048]{1,0:T(8,128)S(1)} custom-call(s32[1]{0:T(128)} %bitcast.2.idx_ref, bf16[128,1792]{1,0:T(8,128)(2,1)S(1)} %fusion.3.mine_ref, bf16[128,1792]{1,0:T(8,128)(2,1)S(1)} %collective-permute-done.19.near_ref, bf16[3584,2048]{1,0:T(8,128)(2,1)} %refs_4_.5, f32[256,2048]{1,0:T(8,128)S(1)} %get-tuple-element.79.refs_0_), custom_call_target="tpu_custom_call" | custom-call | flops 1 | bytes 1 | tf_op jit(solution)/shard_map/target_part/pallas_call | solution.py:412
  113.8 4.2 %collective-permute-done.18.refs_0_ = bf16[128,1792]{1,0:T(8,128)(2,1)S(1)} collective-permute-done((bf16[128,1792]{1,0:T(8,128)(2,1)S(1)}, bf16[128,1792]{1,0:T(8,128)(2,1)S(1)}, u32[]{:S(2)}, u32[]{:S(2)}) %collective-permute-start.18) | collective-permute-done | bytes 458784 | tf_op jit(solution)/shard_map/ppermute | solution.py:703
  118.0 1.8 %collective-permute-done.21.refs_2_ = bf16[128,1792]{1,0:T(8,128)(2,1)S(1)} collective-permute-done((bf16[128,1792]{1,0:T(8,128)(2,1)S(1)}, bf16[128,1792]{1,0:T(8,128)(2,1)S(1)}, u32[]{:S(2)}, u32[]{:S(2)}) %collective-permute-start.21) | collective-permute-done | bytes 458784 | tf_op jit(solution)/shard_map/ppermute | solution.py:700
  119.8 11.1 %left_grads.1 = (bf16[4,256,128]{2,1,0:T(8,128)(2,1)S(1)}, bf16[8,256,512]{2,1,0:T(8,128)(2,1)S(1)}) custom-call(s32[4]{0:T(128)S(1)} %pad_add_fusion.idx_ref, bf16[128,1792]{1,0:T(8,128)(2,1)S(1)} %collective-permute-done.18.refs_0_, bf16[128,1792]{1,0:T(8,128)(2,1)S(1)} %collective-permute-done.20.refs_1_, ...), custom_call_target="tpu_custom_call" | custom-call | flops 1 | bytes 1 | tf_op jit(solution)/shard_map/left_grads/pallas_call | solution.py:618
  131.0 1.7 %collective-permute-start.23 = (bf16[2,256,128]{2,1,0:T(8,128)(2,1)S(1)}, bf16[2,256,128]{2,1,0:T(8,128)(2,1)S(1)}, u32[]{:S(2)}, u32[]{:S(2)}) collective-permute-start(bf16[2,256,128]{2,1,0:T(8,128)(2,1)S(1)} %slice.51), channel_id=1, source_target_pairs={{0,1},{1,0},{2,3},{3,2},{4,5},{5,4},{6,7},{7,6},{8,9},{9,8},{10,11... | collective-permute-start | bytes 393224 | tf_op jit(solution)/shard_map/ppermute | solution.py:706
  132.7 3.6 %right_grads.2 = bf16[2,512,128]{2,1,0:T(8,128)(2,1)S(1)} custom-call(s32[4]{0:T(128)S(1)} %pad_add_fusion.idx_ref, bf16[128,8192]{1,0:T(8,128)(2,1)S(1)} %copy-done, bf16[128,8192]{1,0:T(8,128)(2,1)S(1)} %copy-done, bf16[128,8192]{1,0:T(8,128)(2,1)} %collective-permute-done.refs_2_.refs_3_, bf16[128,8192]{1,0:T(8,128)(2,1)} %collective-permute-done.refs_2_.refs_3_, ...), custom_call_target="tpu_custom_call" | custom-call | flops 1 | bytes 1 | tf_op jit(solution)/shard_map/right_grads/pallas_call | solution.py:672
  136.4 0.4 collective-permute-start.24
  136.9 4.0 %collective-permute-start.27 = (bf16[256,128]{1,0:T(8,128)(2,1)S(1)}, bf16[256,128]{1,0:T(8,128)(2,1)S(1)}, u32[]{:S(2)}, u32[]{:S(2)}) collective-permute-start(bf16[256,128]{1,0:T(8,128)(2,1)S(1)} %slice_bitcast_fusion.6), channel_id=1, source_target_pairs={{0,2},{1,3},{2,0},{3,1},{4,6},{5,7},{6,4},{7,5},{8,10},{9,11},{10,... | collective-permute-start | bytes 196616 | tf_op jit(solution)/shard_map/ppermute | solution.py:706
  140.8 3.6 %right_grads.3 = bf16[2,512,128]{2,1,0:T(8,128)(2,1)S(1)} custom-call(s32[4]{0:T(128)S(1)} %pad_add_fusion.idx_ref, bf16[128,8192]{1,0:T(8,128)(2,1)S(1)} %copy-done, bf16[128,8192]{1,0:T(8,128)(2,1)S(1)} %copy-done, bf16[128,8192]{1,0:T(8,128)(2,1)} %collective-permute-done.refs_2_.refs_3_, bf16[128,8192]{1,0:T(8,128)(2,1)} %collective-permute-done.refs_2_.refs_3_, ...), custom_call_target="tpu_custom_call" | custom-call | flops 10000000000 | bytes 10000000 | tf_op jit(solution)/shard_map/right_grads/pallas_call | solution.py:672
  144.5 1.5 collective-permute-done.24
  145.9 0.1 add_convert_fusion
  146.0 0.7 collective-permute-start.25
  146.7 4.6 %collective-permute-start.26 = (bf16[512,128]{1,0:T(8,128)(2,1)S(1)}, bf16[512,128]{1,0:T(8,128)(2,1)S(1)}, u32[]{:S(2)}, u32[]{:S(2)}) collective-permute-start(bf16[512,128]{1,0:T(8,128)(2,1)S(1)} %get-tuple-element.89), channel_id=1, source_target_pairs={{0,8},{1,12},{2,0},{3,4},{4,9},{5,13},{6,1},{7,5},{8,10},{9,14},{1... | collective-permute-start | bytes 393224 | tf_op jit(solution)/shard_map/ppermute | solution.py:713
  151.4 0.2 reshape.32
  151.5 0.7 copy.8
  152.3 10.1 %collective-permute-done.26 = bf16[512,128]{1,0:T(8,128)(2,1)S(1)} collective-permute-done((bf16[512,128]{1,0:T(8,128)(2,1)S(1)}, bf16[512,128]{1,0:T(8,128)(2,1)S(1)}, u32[]{:S(2)}, u32[]{:S(2)}) %collective-permute-start.26) | collective-permute-done | bytes 131104 | tf_op jit(solution)/shard_map/ppermute | solution.py:713
  162.4 0.7 convert_add_fusion.2
  (32 shorter events, 0.2 us)
Async XLA Ops:
  0.6 6.8 %collective-permute-start = (bf16[128,8192]{1,0:T(8,128)(2,1)}, bf16[128,8192]{1,0:T(8,128)(2,1)}, u32[]{:S(2)}, u32[]{:S(2)}) collective-permute-start(bf16[128,8192]{1,0:T(8,128)(2,1)} %refs_1_.11), channel_id=1, source_target_pairs={{0,4},{4,0},{8,12},{12,8},{1,5},{5,1},{9,13},{13,9},{2,6},{6,2},{1... | collective-permute-start | bytes 6291464 | tf_op jit(solution)/shard_map/ppermute | solution.py:700
  1.8 5.7 %copy-start = (bf16[128,8192]{1,0:T(8,128)(2,1)S(1)}, bf16[128,8192]{1,0:T(8,128)(2,1)}, u32[]{:S(2)}) copy-start(bf16[128,8192]{1,0:T(8,128)(2,1)} %refs_1_.11) | copy-start | bytes 6291460
  4.8 15.3 %collective-permute-start.1 = (bf16[64,4096]{1,0:T(8,128)(2,1)}, bf16[64,4096]{1,0:T(8,128)(2,1)S(1)}, u32[]{:S(2)}, u32[]{:S(2)}) collective-permute-start(bf16[64,4096]{1,0:T(8,128)(2,1)} %get-tuple-element.45), channel_id=1, source_target_pairs={{0,8},{4,12},{8,0},{12,4},{1,9},{5,13},{9,1},{13,5},{2,10},{6,14},... | collective-permute-start | bytes 1572872 | tf_op jit(solution)/shard_map/ppermute | solution.py:703
  7.4 14.5 %copy-start.2 = (bf16[16,32,128]{2,1,0:T(8,128)(2,1)S(1)}, bf16[16,32,128]{2,1,0:T(8,128)(2,1)}, u32[]{:S(2)}) copy-start(bf16[16,32,128]{2,1,0:T(8,128)(2,1)} %param.10) | copy-start | bytes 393220
  18.2 0.9 copy-start.1
  20.1 15.1 %collective-permute-start.2 = (bf16[64,4096]{1,0:T(8,128)(2,1)S(1)}, bf16[64,4096]{1,0:T(8,128)(2,1)S(1)}, u32[]{:S(2)}, u32[]{:S(2)}) collective-permute-start(bf16[64,4096]{1,0:T(8,128)(2,1)S(1)} %collective-permute-done.1.refs_0_.refs_4_), channel_id=1, source_target_pairs={{0,1},{1,0},{2,3},{3,2},{4,5},{5,4},{6,7},{7,6},{8,9},{9,8},{10,11... | collective-permute-start | bytes 1572872 | tf_op jit(solution)/shard_map/ppermute | solution.py:706
  21.9 23.7 %collective-permute-start.5 = (bf16[64,4096]{1,0:T(8,128)(2,1)S(1)}, bf16[64,4096]{1,0:T(8,128)(2,1)}, u32[]{:S(2)}, u32[]{:S(2)}) collective-permute-start(bf16[64,4096]{1,0:T(8,128)(2,1)S(1)} %collective-permute-done.1.refs_0_.refs_4_), channel_id=1, source_target_pairs={{0,4},{4,0},{8,12},{12,8},{1,5},{5,1},{9,13},{13,9},{2,6},{6,2},{1... | collective-permute-start | bytes 1572872 | tf_op jit(solution)/shard_map/ppermute | solution.py:700
  21.9 4.1 %collective-permute-start.4 = (bf16[16,32,128]{2,1,0:T(8,128)(2,1)S(1)}, bf16[16,32,128]{2,1,0:T(8,128)(2,1)S(1)}, u32[]{:S(2)}, u32[]{:S(2)}) collective-permute-start(bf16[16,32,128]{2,1,0:T(8,128)(2,1)S(1)} %copy-done.2), channel_id=1, source_target_pairs={{0,0},{1,4},{2,8},{3,12},{4,1},{5,5},{6,9},{7,13},{8,2},{9,6},{10,... | collective-permute-start | bytes 393224 | tf_op jit(solution)/shard_map/ppermute | solution.py:713
  22.6 4.3 %collective-permute-start.3 = (bf16[2,128,1792]{2,1,0:T(8,128)(2,1)}, bf16[2,128,1792]{2,1,0:T(8,128)(2,1)}, u32[]{:S(2)}, u32[]{:S(2)}) collective-permute-start(bf16[2,128,1792]{2,1,0:T(8,128)(2,1)} %bitcast.9), channel_id=1, source_target_pairs={{0,4},{4,0},{8,12},{12,8},{1,5},{5,1},{9,13},{13,9},{2,6},{6,2},{1... | collective-permute-start | bytes 2752520 | tf_op jit(solution)/shard_map/ppermute | solution.py:700
  35.2 10.4 %collective-permute-start.6 = (bf16[64,4096]{1,0:T(8,128)(2,1)S(1)}, bf16[64,4096]{1,0:T(8,128)(2,1)}, u32[]{:S(2)}, u32[]{:S(2)}) collective-permute-start(bf16[64,4096]{1,0:T(8,128)(2,1)S(1)} %collective-permute-done.2.refs_1_.refs_5_), channel_id=1, source_target_pairs={{0,4},{4,0},{8,12},{12,8},{1,5},{5,1},{9,13},{13,9},{2,6},{6,2},{1... | collective-permute-start | bytes 1572872 | tf_op jit(solution)/shard_map/ppermute | solution.py:700
  39.9 17.7 %collective-permute-start.7 = (bf16[64,4096]{1,0:T(8,128)(2,1)}, bf16[64,4096]{1,0:T(8,128)(2,1)}, u32[]{:S(2)}, u32[]{:S(2)}) collective-permute-start(bf16[64,4096]{1,0:T(8,128)(2,1)} %get-tuple-element.55), channel_id=1, source_target_pairs={{0,8},{4,12},{8,0},{12,4},{1,9},{5,13},{9,1},{13,5},{2,10},{6,14},... | collective-permute-start | bytes 1572872 | tf_op jit(solution)/shard_map/ppermute | solution.py:703
  43.5 12.3 %collective-permute-start.11 = (bf16[1,768,128]{2,1,0:T(8,128)(2,1)S(1)}, bf16[1,768,128]{2,1,0:T(8,128)(2,1)S(1)}, u32[]{:S(2)}, u32[]{:S(2)}) collective-permute-start(bf16[1,768,128]{2,1,0:T(8,128)(2,1)S(1)} %maximum_bitcast_fusion), channel_id=1, source_target_pairs={{0,2},{1,3},{2,0},{3,1},{4,6},{5,7},{6,4},{7,5},{8,10},{9,11},{10,... | collective-permute-start | bytes 589832 | tf_op jit(solution)/shard_map/ppermute | solution.py:706
  45.0 30.4 %collective-permute-start.9 = (bf16[2,128,1792]{2,1,0:T(8,128)(2,1)}, bf16[2,128,1792]{2,1,0:T(8,128)(2,1)S(1)}, u32[]{:S(2)}, u32[]{:S(2)}) collective-permute-start(bf16[2,128,1792]{2,1,0:T(8,128)(2,1)} %fusion.1), channel_id=1, source_target_pairs={{0,8},{4,12},{8,0},{12,4},{1,9},{5,13},{9,1},{13,5},{2,10},{6,14},... | collective-permute-start | bytes 2752520 | tf_op jit(solution)/shard_map/ppermute | solution.py:703
  55.9 14.6 %collective-permute-start.12 = (bf16[2,768,128]{2,1,0:T(8,128)(2,1)S(1)}, bf16[2,768,128]{2,1,0:T(8,128)(2,1)S(1)}, u32[]{:S(2)}, u32[]{:S(2)}) collective-permute-start(bf16[2,768,128]{2,1,0:T(8,128)(2,1)S(1)} %pad_maximum_fusion.1), channel_id=1, source_target_pairs={{0,1},{1,0},{2,3},{3,2},{4,5},{5,4},{6,7},{7,6},{8,9},{9,8},{10,11... | collective-permute-start | bytes 1179656 | tf_op jit(solution)/shard_map/ppermute | solution.py:706
  57.6 12.5 %collective-permute-start.10 = (bf16[2,128,1792]{2,1,0:T(8,128)(2,1)S(1)}, bf16[2,128,1792]{2,1,0:T(8,128)(2,1)S(1)}, u32[]{:S(2)}, u32[]{:S(2)}) collective-permute-start(bf16[2,128,1792]{2,1,0:T(8,128)(2,1)S(1)} %bitcast.58), channel_id=1, source_target_pairs={{0,4},{4,0},{8,12},{12,8},{1,5},{5,1},{9,13},{13,9},{2,6},{6,2},{1... | collective-permute-start | bytes 2752520 | tf_op jit(solution)/shard_map/ppermute | solution.py:700
  75.4 3.8 %collective-permute-start.13 = (bf16[2,2,128,1792]{3,2,1,0:T(8,128)(2,1)S(1)}, bf16[2,2,128,1792]{3,2,1,0:T(8,128)(2,1)S(1)}, u32[]{:S(2)}, u32[]{:S(2)}) collective-permute-start(bf16[2,2,128,1792]{3,2,1,0:T(8,128)(2,1)S(1)} %get-tuple-element.67), channel_id=1, source_target_pairs={{0,4},{4,0},{8,12},{12,8},{1,5},{5,1},{9,13},{13,9},{2,6},{6,2},{1... | collective-permute-start | bytes 5505032 | tf_op jit(solution)/shard_map/ppermute | solution.py:700
  75.5 14.5 %collective-permute-start.8 = (bf16[64,4096]{1,0:T(8,128)(2,1)}, bf16[64,4096]{1,0:T(8,128)(2,1)S(1)}, u32[]{:S(2)}, u32[]{:S(2)}) collective-permute-start(bf16[64,4096]{1,0:T(8,128)(2,1)} %collective-permute-done.7.refs_4_.refs_8_), channel_id=1, source_target_pairs={{0,1},{1,0},{2,3},{3,2},{4,5},{5,4},{6,7},{7,6},{8,9},{9,8},{10,11... | collective-permute-start | bytes 1572872 | tf_op jit(solution)/shard_map/ppermute | solution.py:706
  75.5 23.2 %collective-permute-start.16 = (bf16[2,128,1792]{2,1,0:T(8,128)(2,1)S(1)}, bf16[2,128,1792]{2,1,0:T(8,128)(2,1)S(1)}, u32[]{:S(2)}, u32[]{:S(2)}) collective-permute-start(bf16[2,128,1792]{2,1,0:T(8,128)(2,1)S(1)} %fusion), channel_id=1, source_target_pairs={{0,8},{4,12},{8,0},{12,4},{1,9},{5,13},{9,1},{13,5},{2,10},{6,14},... | collective-permute-start | bytes 2752520 | tf_op jit(solution)/shard_map/ppermute | solution.py:703
  79.8 10.3 %collective-permute-start.17 = (bf16[128,1792]{1,0:T(8,128)(2,1)S(1)}, bf16[128,1792]{1,0:T(8,128)(2,1)S(1)}, u32[]{:S(2)}, u32[]{:S(2)}) collective-permute-start(bf16[128,1792]{1,0:T(8,128)(2,1)S(1)} %fusion.5.mine_ref), channel_id=1, source_target_pairs={{0,4},{4,0},{8,12},{12,8},{1,5},{5,1},{9,13},{13,9},{2,6},{6,2},{1... | collective-permute-start | bytes 1376264 | tf_op jit(solution)/shard_map/ppermute | solution.py:700
  85.4 23.2 %collective-permute-start.20 = (bf16[128,1792]{1,0:T(8,128)(2,1)S(1)}, bf16[128,1792]{1,0:T(8,128)(2,1)S(1)}, u32[]{:S(2)}, u32[]{:S(2)}) collective-permute-start(bf16[128,1792]{1,0:T(8,128)(2,1)S(1)} %fusion.5.mine_ref), channel_id=1, source_target_pairs={{0,8},{4,12},{8,0},{12,4},{1,9},{5,13},{9,1},{13,5},{2,10},{6,14},... | collective-permute-start | bytes 1376264 | tf_op jit(solution)/shard_map/ppermute | solution.py:703
  87.2 14.0 %collective-permute-start.14 = (bf16[64,4096]{1,0:T(8,128)(2,1)}, bf16[64,4096]{1,0:T(8,128)(2,1)S(1)}, u32[]{:S(2)}, u32[]{:S(2)}) collective-permute-start(bf16[64,4096]{1,0:T(8,128)(2,1)} %collective-permute-done.7.refs_4_.refs_8_), channel_id=1, source_target_pairs={{0,4},{4,0},{8,12},{12,8},{1,5},{5,1},{9,13},{13,9},{2,6},{6,2},{1... | collective-permute-start | bytes 1572872 | tf_op jit(solution)/shard_map/ppermute | solution.py:700
  90.1 11.1 %collective-permute-start.15 = (bf16[64,4096]{1,0:T(8,128)(2,1)S(1)}, bf16[64,4096]{1,0:T(8,128)(2,1)S(1)}, u32[]{:S(2)}, u32[]{:S(2)}) collective-permute-start(bf16[64,4096]{1,0:T(8,128)(2,1)S(1)} %collective-permute-done.8.refs_5_.refs_9_), channel_id=1, source_target_pairs={{0,4},{4,0},{8,12},{12,8},{1,5},{5,1},{9,13},{13,9},{2,6},{6,2},{1... | collective-permute-start | bytes 1572872 | tf_op jit(solution)/shard_map/ppermute | solution.py:700
  99.3 9.3 %collective-permute-start.19 = (bf16[128,1792]{1,0:T(8,128)(2,1)S(1)}, bf16[128,1792]{1,0:T(8,128)(2,1)S(1)}, u32[]{:S(2)}, u32[]{:S(2)}) collective-permute-start(bf16[128,1792]{1,0:T(8,128)(2,1)S(1)} %fusion.3.mine_ref), channel_id=1, source_target_pairs={{0,4},{4,0},{8,12},{12,8},{1,5},{5,1},{9,13},{13,9},{2,6},{6,2},{1... | collective-permute-start | bytes 1376264 | tf_op jit(solution)/shard_map/ppermute | solution.py:700
  99.4 18.6 %collective-permute-start.18 = (bf16[128,1792]{1,0:T(8,128)(2,1)S(1)}, bf16[128,1792]{1,0:T(8,128)(2,1)S(1)}, u32[]{:S(2)}, u32[]{:S(2)}) collective-permute-start(bf16[128,1792]{1,0:T(8,128)(2,1)S(1)} %fusion.3.mine_ref), channel_id=1, source_target_pairs={{0,8},{4,12},{8,0},{12,4},{1,9},{5,13},{9,1},{13,5},{2,10},{6,14},... | collective-permute-start | bytes 1376264 | tf_op jit(solution)/shard_map/ppermute | solution.py:703
  108.6 9.5 %collective-permute-start.22 = (bf16[128,1792]{1,0:T(8,128)(2,1)S(1)}, bf16[128,1792]{1,0:T(8,128)(2,1)S(1)}, u32[]{:S(2)}, u32[]{:S(2)}) collective-permute-start(bf16[128,1792]{1,0:T(8,128)(2,1)S(1)} %collective-permute-done.20.refs_1_), channel_id=1, source_target_pairs={{0,4},{4,0},{8,12},{12,8},{1,5},{5,1},{9,13},{13,9},{2,6},{6,2},{1... | collective-permute-start | bytes 1376264 | tf_op jit(solution)/shard_map/ppermute | solution.py:700
  118.0 1.8 %collective-permute-start.21 = (bf16[128,1792]{1,0:T(8,128)(2,1)S(1)}, bf16[128,1792]{1,0:T(8,128)(2,1)S(1)}, u32[]{:S(2)}, u32[]{:S(2)}) collective-permute-start(bf16[128,1792]{1,0:T(8,128)(2,1)S(1)} %collective-permute-done.18.refs_0_), channel_id=1, source_target_pairs={{0,4},{4,0},{8,12},{12,8},{1,5},{5,1},{9,13},{13,9},{2,6},{6,2},{1... | collective-permute-start | bytes 1376264 | tf_op jit(solution)/shard_map/ppermute | solution.py:700
  131.0 5.8 %collective-permute-start.23 = (bf16[2,256,128]{2,1,0:T(8,128)(2,1)S(1)}, bf16[2,256,128]{2,1,0:T(8,128)(2,1)S(1)}, u32[]{:S(2)}, u32[]{:S(2)}) collective-permute-start(bf16[2,256,128]{2,1,0:T(8,128)(2,1)S(1)} %slice.51), channel_id=1, source_target_pairs={{0,1},{1,0},{2,3},{3,2},{4,5},{5,4},{6,7},{7,6},{8,9},{9,8},{10,11... | collective-permute-start | bytes 393224 | tf_op jit(solution)/shard_map/ppermute | solution.py:706
  136.4 9.5 %collective-permute-start.24 = (bf16[2,512,128]{2,1,0:T(8,128)(2,1)S(1)}, bf16[2,512,128]{2,1,0:T(8,128)(2,1)S(1)}, u32[]{:S(2)}, u32[]{:S(2)}) collective-permute-start(bf16[2,512,128]{2,1,0:T(8,128)(2,1)S(1)} %right_grads.2), channel_id=1, source_target_pairs={{0,1},{1,0},{2,3},{3,2},{4,5},{5,4},{6,7},{7,6},{8,9},{9,8},{10,11... | collective-permute-start | bytes 786440 | tf_op jit(solution)/shard_map/ppermute | solution.py:706
  136.9 14.5 %collective-permute-start.27 = (bf16[256,128]{1,0:T(8,128)(2,1)S(1)}, bf16[256,128]{1,0:T(8,128)(2,1)S(1)}, u32[]{:S(2)}, u32[]{:S(2)}) collective-permute-start(bf16[256,128]{1,0:T(8,128)(2,1)S(1)} %slice_bitcast_fusion.6), channel_id=1, source_target_pairs={{0,2},{1,3},{2,0},{3,1},{4,6},{5,7},{6,4},{7,5},{8,10},{9,11},{10,... | collective-permute-start | bytes 196616 | tf_op jit(solution)/shard_map/ppermute | solution.py:706
  146.0 6.3 %collective-permute-start.25 = (bf16[512,128]{1,0:T(8,128)(2,1)S(1)}, bf16[512,128]{1,0:T(8,128)(2,1)S(1)}, u32[]{:S(2)}, u32[]{:S(2)}) collective-permute-start(bf16[512,128]{1,0:T(8,128)(2,1)S(1)} %get-tuple-element.88), channel_id=1, source_target_pairs={{0,0},{1,4},{2,8},{3,12},{4,1},{5,5},{6,9},{7,13},{8,2},{9,6},{10,... | collective-permute-start | bytes 393224 | tf_op jit(solution)/shard_map/ppermute | solution.py:713
  146.7 15.7 %collective-permute-start.26 = (bf16[512,128]{1,0:T(8,128)(2,1)S(1)}, bf16[512,128]{1,0:T(8,128)(2,1)S(1)}, u32[]{:S(2)}, u32[]{:S(2)}) collective-permute-start(bf16[512,128]{1,0:T(8,128)(2,1)S(1)} %get-tuple-element.89), channel_id=1, source_target_pairs={{0,8},{1,12},{2,0},{3,4},{4,9},{5,13},{6,1},{7,5},{8,10},{9,14},{1... | collective-permute-start | bytes 393224 | tf_op jit(solution)/shard_map/ppermute | solution.py:713

commit v17 on v15

--- a/solution.py
+++ b/solution.py
@@ -736,16 +736,15 @@
     pairs, blocks = left_factor.shape[0], left_factor.shape[2]
     turned = turn(after(right_factor, mine), 0)
     left_rows = pack_left(after(left_factor, mine))
-    factors = jnp.concatenate(
-        [after(turned, left_rows).reshape(-1, LANES), left_rows], axis=0
-    )[None]
+    late_first = across(after(rest, mine))
+    turned = after(turned, left_rows, late_first)
+    factors = jnp.concatenate([turned.reshape(-1, LANES), left_rows], axis=0)[None]
     sums = add(mine[0], swap(other[0])).astype(BF16)
 
     arrived = after(arrived, mine)
     partner = along(arrived, 1)
     near_arrived = swap(arrived)
-    late_first = across(after(rest, mine))
-    partner = after(partner, late_first, sums, factors)
+    partner = after(partner, factors)
     got_early = across(sums)
     more = along(after(factors, partner), 2)
     order = jnp.concatenate([base, jnp.stack([chip, z])]).astype(jnp.int32)

time: 160 us -> 158 us (0.988)
  starting transfers between devices: 32 us -> 26.4 us
  waiting for transfers between devices: 39.4 us -> 44.8 us
    ppermute x6, starting transfers between devices: 13.8 us -> 7.69 us  [across(): return lax.ppermute(value, 'fsdp', [(i, i ^ 2) for i in range(fsdp_count)])]
    ppermute x6, waiting for transfers between devices: 17 us -> 20.2 us  [across(): return lax.ppermute(value, 'fsdp', [(i, i ^ 2) for i in range(fsdp_count)])]
    ppermute x7, starting transfers between devices: 8.89 us -> 11.4 us  [along(): lax.ppermute(value, 'tensor', [(i, i ^ bit) for i in range(tensor_count)])]
where the time goes in v17:
time: 158 us; the launch traced here: 157 us
  Pallas kernels  77.2 us (49%)
  waiting for transfers between devices  44.8 us (28%)
  starting transfers between devices  26.4 us (17%)
  other arithmetic  5.59 us (4%)
  local copies, waits for them, and re-layouts  2.05 us (1%)
    pallas_call x3, Pallas kernels, products(): pl.pallas_call(functools.partial(products_kernel, sets), grid_spec=pltpu....  33.2 us
    ppermute x6, waiting for transfers between devices, across(): return lax.ppermute(value, 'fsdp', [(i, i ^ 2) for i in range(fsdp_count)])  20.2 us
    ppermute x7, starting transfers between devices, along(): lax.ppermute(value, 'tensor', [(i, i ^ bit) for i in range(tensor_count)])  11.4 us
    pallas_call x1, Pallas kernels, left_grads(): pl.pallas_call(functools.partial(left_kernel, chunks, scale), grid_spec=p...  11.1 us
    ppermute x7, waiting for transfers between devices, along(): lax.ppermute(value, 'tensor', [(i, i ^ bit) for i in range(tensor_count)])  10.9 us
    ppermute x3, waiting for transfers between devices, turn(): return lax.ppermute(value, both_axes, perm)  10.6 us
    pallas_call x2, Pallas kernels, student_part(): pl.pallas_call(functools.partial(student_kernel, steps, bool(late), tenso...  10.6 us
    pallas_call x2, Pallas kernels, target_part(): pl.pallas_call(functools.partial(target_kernel, sign), grid_spec=pltpu.Pr...  10.5 us
  transfers between devices with their start and end apart: 28, of which 10 were waited for; matrix products, arithmetic and copies ran while one was open for 4% of the time, Pallas kernels for 42%

profile of v17, /device:TPU:0, one launch (start us, length us, event | category | flops | bytes accessed | tf_op | source)
XLA Modules:
  0.0 156.9 jit_solution(18147125156098760874)
XLA Ops:
  0.6 0.5 collective-permute-start
  1.1 0.6 pad_add_fusion.1.idx_ref
  1.8 3.1 %cut_tokens.1 = (bf16[64,4096]{1,0:T(8,128)(2,1)}, bf16[64,4096]{1,0:T(8,128)(2,1)}) custom-call(s32[3]{0:T(128)} %pad_add_fusion.1.idx_ref, bf16[128,8192]{1,0:T(8,128)(2,1)} %refs_1_.11, bf16[128,8192]{1,0:T(8,128)(2,1)} %refs_1_.11), custom_call_target="tpu_custom_call" | custom-call | flops 1 | bytes 1 | tf_op jit(solution)/shard_map/cut_tokens/pallas_call | solution.py:313
  4.8 2.5 %collective-permute-start.1 = (bf16[64,4096]{1,0:T(8,128)(2,1)}, bf16[64,4096]{1,0:T(8,128)(2,1)S(1)}, u32[]{:S(2)}, u32[]{:S(2)}) collective-permute-start(bf16[64,4096]{1,0:T(8,128)(2,1)} %get-tuple-element.44), channel_id=1, source_target_pairs={{0,8},{4,12},{8,0},{12,4},{1,9},{5,13},{9,1},{13,5},{2,10},{6,14},... | collective-permute-start | bytes 1572872 | tf_op jit(solution)/shard_map/ppermute | solution.py:703
  7.3 0.1 concatenate.25.idx_ref
  7.4 0.1 concatenate.27.idx_ref
  7.5 10.8 %gate_up_products.3 = (bf16[1,2,128,1792]{3,2,1,0:T(8,128)(2,1)S(1)}, bf16[1,2,128,1792]{3,2,1,0:T(8,128)(2,1)}) custom-call(s32[5]{0:T(128)S(1)} %concatenate.25.idx_ref, bf16[128,8192]{1,0:T(8,128)(2,1)S(1)} %copy-done, bf16[128,8192]{1,0:T(8,128)(2,1)S(1)} %copy-done, bf16[128,8192]{1,0:T(8,128)(2,1)} %collective-permute-done.refs_2_.refs_3_, ...), custom_call_target="tpu_custom_call" | custom-call | flops 1 | bytes 1 | tf_op jit(solution)/shard_map/gate_up_products/pallas_call | solution.py:374
  18.3 0.9 copy-done.1
  19.2 0.9 collective-permute-done.1.refs_0_.refs_4_
  20.1 1.8 %collective-permute-start.2 = (bf16[64,4096]{1,0:T(8,128)(2,1)S(1)}, bf16[64,4096]{1,0:T(8,128)(2,1)S(1)}, u32[]{:S(2)}, u32[]{:S(2)}) collective-permute-start(bf16[64,4096]{1,0:T(8,128)(2,1)S(1)} %collective-permute-done.1.refs_0_.refs_4_), channel_id=1, source_target_pairs={{0,1},{1,0},{2,3},{3,2},{4,5},{5,4},{6,7},{7,6},{8,9},{9,8},{10,11... | collective-permute-start | bytes 1572872 | tf_op jit(solution)/shard_map/ppermute | solution.py:706
  21.9 0.5 collective-permute-start.7
  22.4 1.5 collective-permute-start.4
  23.9 0.7 collective-permute-start.3
  24.6 1.6 %pack_left.1 = bf16[256,128]{1,0:T(8,128)(2,1)} custom-call(bf16[32,16,64]{2,1,0:T(8,128)(2,1)} %left_ref), custom_call_target="tpu_custom_call" | custom-call | flops 10000000000 | bytes 10000000 | tf_op jit(solution)/shard_map/pack_left/pallas_call | solution.py:339
  26.2 12.2 %collective-permute-done.4.refs_4_.refs_8_ = bf16[64,4096]{1,0:T(8,128)(2,1)} collective-permute-done((bf16[64,4096]{1,0:T(8,128)(2,1)}, bf16[64,4096]{1,0:T(8,128)(2,1)}, u32[]{:S(2)}, u32[]{:S(2)}) %collective-permute-start.4) | collective-permute-done | bytes 524320 | tf_op jit(solution)/shard_map/ppermute | solution.py:703
  38.4 0.9 maximum_bitcast_fusion
  39.3 0.1 collective-permute-start.6
  39.4 3.6 %collective-permute-start.11 = (bf16[1,768,128]{2,1,0:T(8,128)(2,1)S(1)}, bf16[1,768,128]{2,1,0:T(8,128)(2,1)S(1)}, u32[]{:S(2)}, u32[]{:S(2)}) collective-permute-start(bf16[1,768,128]{2,1,0:T(8,128)(2,1)S(1)} %maximum_bitcast_fusion), channel_id=1, source_target_pairs={{0,2},{1,3},{2,0},{3,1},{4,6},{5,7},{6,4},{7,5},{8,10},{9,11},{10,... | collective-permute-start | bytes 589832 | tf_op jit(solution)/shard_map/ppermute | solution.py:706
  43.0 1.7 %fusion.1 = bf16[2,128,1792]{2,1,0:T(8,128)(2,1)S(1)} fusion(bf16[2,128,1792]{2,1,0:T(8,128)(2,1)} %collective-permute-done.7, bf16[1,2,128,1792]{3,2,1,0:T(8,128)(2,1)} %copy-done.1), kind=kLoop, calls=%fused_computation.3 | loop fusion | flops 1835008 | bytes 2752512 | tf_op jit(solution)/shard_map/convert_element_type | solution.py:742
  44.7 0.1 collective-permute-start.9
  44.8 10.0 %gate_up_products.4 = (bf16[1,2,128,1792]{3,2,1,0:T(8,128)(2,1)S(1)}, bf16[1,2,128,1792]{3,2,1,0:T(8,128)(2,1)S(1)}) custom-call(s32[5]{0:T(128)S(1)} %concatenate.25.idx_ref, bf16[64,4096]{1,0:T(8,128)(2,1)S(1)} %collective-permute-done.1.refs_0_.refs_4_, bf16[64,4096]{1,0:T(8,128)(2,1)S(1)} %collective-permute-done.2.refs_1_.refs_5_, ...), custom_call_target="tpu_custom_call" | custom-call | flops 1 | bytes 1 | tf_op jit(solution)/shard_map/gate_up_products/pallas_call | solution.py:374
  54.8 0.3 collective-permute-start.10
  55.1 1.6 %collective-permute-start.8 = (bf16[64,4096]{1,0:T(8,128)(2,1)}, bf16[64,4096]{1,0:T(8,128)(2,1)S(1)}, u32[]{:S(2)}, u32[]{:S(2)}) collective-permute-start(bf16[64,4096]{1,0:T(8,128)(2,1)} %collective-permute-done.4.refs_4_.refs_8_), channel_id=1, source_target_pairs={{0,1},{1,0},{2,3},{3,2},{4,5},{5,4},{6,7},{7,6},{8,9},{9,8},{10,11... | collective-permute-start | bytes 1572872 | tf_op jit(solution)/shard_map/ppermute | solution.py:706
  56.7 12.4 %gate_up_products.5 = (bf16[2,2,128,1792]{3,2,1,0:T(8,128)(2,1)S(1)}, bf16[2,2,128,1792]{3,2,1,0:T(8,128)(2,1)S(1)}) custom-call(s32[5]{0:T(128)S(1)} %concatenate.27.idx_ref, bf16[128,8192]{1,0:T(8,128)(2,1)S(1)} %copy-done, bf16[128,8192]{1,0:T(8,128)(2,1)S(1)} %copy-done, bf16[128,8192]{1,0:T(8,128)(2,1)} %collective-permute-done.refs_2_.refs_3_, ...), custom_call_target="tpu_custom_call" | custom-call | flops 10000000000 | bytes 10000000 | tf_op jit(solution)/shard_map/gate_up_products/pallas_call | solution.py:374
  69.2 0.2 fusion
  69.4 0.0 collective-permute-done.8.refs_5_.refs_9_
  69.4 0.2 collective-permute-start.12
  69.7 0.1 pad_add_fusion.idx_ref
  69.8 1.6 %collective-permute-start.13 = (bf16[2,768,128]{2,1,0:T(8,128)(2,1)S(1)}, bf16[2,768,128]{2,1,0:T(8,128)(2,1)S(1)}, u32[]{:S(2)}, u32[]{:S(2)}) collective-permute-start(bf16[2,768,128]{2,1,0:T(8,128)(2,1)S(1)} %pad_maximum_fusion.1), channel_id=1, source_target_pairs={{0,1},{1,0},{2,3},{3,2},{4,5},{5,4},{6,7},{7,6},{8,9},{9,8},{10,11... | collective-permute-start | bytes 1179656 | tf_op jit(solution)/shard_map/ppermute | solution.py:706
  71.4 0.8 collective-permute-start.16
  72.1 1.1 collective-permute-done.12
  73.3 0.3 bitcast_add_fusion.1
  73.6 0.3 fusion.5.mine_ref
  73.9 0.2 collective-permute-start.17
  74.1 7.1 %collective-permute-done.13 = bf16[2,768,128]{2,1,0:T(8,128)(2,1)S(1)} collective-permute-done((bf16[2,768,128]{2,1,0:T(8,128)(2,1)S(1)}, bf16[2,768,128]{2,1,0:T(8,128)(2,1)S(1)}, u32[]{:S(2)}, u32[]{:S(2)}) %collective-permute-start.13) | collective-permute-done | bytes 393248 | tf_op jit(solution)/shard_map/ppermute | solution.py:706
  81.2 0.1 pad_maximum_fusion.refs_4_.refs_5_.refs_6_.refs_8_.refs_9_
  81.3 5.3 %student_part.2 = (bf16[8,256,256]{2,1,0:T(8,128)(2,1)S(1)}, f32[256,2048]{1,0:T(8,128)S(1)}, bf16[8,256,256]{2,1,0:T(8,128)(2,1)S(1)}) custom-call(s32[4]{0:T(128)S(1)} %pad_add_fusion.idx_ref, bf16[128,8192]{1,0:T(8,128)(2,1)S(1)} %copy-done, bf16[128,8192]{1,0:T(8,128)(2,1)S(1)} %copy-done, bf16[128,8192]{1,0:T(8,128)(2,1)} %collective-permute-done.refs_2_.refs_3_, ...), custom_call_target="tpu_custom_call" | custom-call | flops 10000000000 | bytes 10000000 | tf_op jit(solution)/shard_map/student_part/pallas_call | solution.py:550
  86.6 2.0 %collective-permute-start.20 = (bf16[128,1792]{1,0:T(8,128)(2,1)S(1)}, bf16[128,1792]{1,0:T(8,128)(2,1)S(1)}, u32[]{:S(2)}, u32[]{:S(2)}) collective-permute-start(bf16[128,1792]{1,0:T(8,128)(2,1)S(1)} %fusion.5.mine_ref), channel_id=1, source_target_pairs={{0,8},{4,12},{8,0},{12,4},{1,9},{5,13},{9,1},{13,5},{2,10},{6,14},... | collective-permute-start | bytes 1376264 | tf_op jit(solution)/shard_map/ppermute | solution.py:703
  88.6 0.5 collective-permute-start.15
  89.1 5.2 %target_part.2.refs_11_ = f32[256,2048]{1,0:T(8,128)S(1)} custom-call(s32[1]{0:T(128)} %bitcast.2.idx_ref, bf16[128,1792]{1,0:T(8,128)(2,1)S(1)} %fusion.5.mine_ref, bf16[128,1792]{1,0:T(8,128)(2,1)S(1)} %collective-permute-done.17.near_ref, bf16[3584,2048]{1,0:T(8,128)(2,1)} %refs_4_.5), custom_call_target="tpu_custom_call" | custom-call | flops 1 | bytes 1 | tf_op jit(solution)/shard_map/target_part/pallas_call | solution.py:412
  94.3 0.2 collective-permute-done.16
  94.6 0.3 bitcast_add_fusion
  94.9 0.3 fusion.3.mine_ref
  95.1 0.1 collective-permute-start.19
  95.2 0.8 collective-permute-start.18
  96.1 5.3 %student_part.3 = (bf16[8,256,256]{2,1,0:T(8,128)(2,1)S(1)}, f32[256,2048]{1,0:T(8,128)S(1)}) custom-call(s32[4]{0:T(128)S(1)} %pad_add_fusion.idx_ref, bf16[64,4096]{1,0:T(8,128)(2,1)S(1)} %collective-permute-done.1.refs_0_.refs_4_, bf16[64,4096]{1,0:T(8,128)(2,1)S(1)} %collective-permute-done.2.refs_1_.refs_5_, ...), custom_call_target="tpu_custom_call" | custom-call | flops 10000000000 | bytes 10000000 | tf_op jit(solution)/shard_map/student_part/pallas_call | solution.py:550
  101.4 3.0 %collective-permute-done.20.refs_1_ = bf16[128,1792]{1,0:T(8,128)(2,1)S(1)} collective-permute-done((bf16[128,1792]{1,0:T(8,128)(2,1)S(1)}, bf16[128,1792]{1,0:T(8,128)(2,1)S(1)}, u32[]{:S(2)}, u32[]{:S(2)}) %collective-permute-start.20) | collective-permute-done | bytes 458784 | tf_op jit(solution)/shard_map/ppermute | solution.py:703
  104.4 5.3 %target_part.3.refs_5_ = f32[256,2048]{1,0:T(8,128)S(1)} custom-call(s32[1]{0:T(128)} %bitcast.2.idx_ref, bf16[128,1792]{1,0:T(8,128)(2,1)S(1)} %fusion.3.mine_ref, bf16[128,1792]{1,0:T(8,128)(2,1)S(1)} %collective-permute-done.19.near_ref, bf16[3584,2048]{1,0:T(8,128)(2,1)} %refs_4_.5, f32[256,2048]{1,0:T(8,128)S(1)} %get-tuple-element.77.refs_0_), custom_call_target="tpu_custom_call" | custom-call | flops 1 | bytes 1 | tf_op jit(solution)/shard_map/target_part/pallas_call | solution.py:412
  109.7 3.9 %collective-permute-done.18.refs_0_ = bf16[128,1792]{1,0:T(8,128)(2,1)S(1)} collective-permute-done((bf16[128,1792]{1,0:T(8,128)(2,1)S(1)}, bf16[128,1792]{1,0:T(8,128)(2,1)S(1)}, u32[]{:S(2)}, u32[]{:S(2)}) %collective-permute-start.18) | collective-permute-done | bytes 458784 | tf_op jit(solution)/shard_map/ppermute | solution.py:703
  113.5 1.8 %collective-permute-done.21.refs_2_ = bf16[128,1792]{1,0:T(8,128)(2,1)S(1)} collective-permute-done((bf16[128,1792]{1,0:T(8,128)(2,1)S(1)}, bf16[128,1792]{1,0:T(8,128)(2,1)S(1)}, u32[]{:S(2)}, u32[]{:S(2)}) %collective-permute-start.21) | collective-permute-done | bytes 458784 | tf_op jit(solution)/shard_map/ppermute | solution.py:700
  115.3 11.1 %left_grads.1 = (bf16[4,256,128]{2,1,0:T(8,128)(2,1)S(1)}, bf16[8,256,512]{2,1,0:T(8,128)(2,1)S(1)}) custom-call(s32[4]{0:T(128)S(1)} %pad_add_fusion.idx_ref, bf16[128,1792]{1,0:T(8,128)(2,1)S(1)} %collective-permute-done.18.refs_0_, bf16[128,1792]{1,0:T(8,128)(2,1)S(1)} %collective-permute-done.20.refs_1_, ...), custom_call_target="tpu_custom_call" | custom-call | flops 1 | bytes 1 | tf_op jit(solution)/shard_map/left_grads/pallas_call | solution.py:618
  126.5 0.6 collective-permute-start.23
  127.1 3.5 %right_grads.2 = bf16[2,512,128]{2,1,0:T(8,128)(2,1)S(1)} custom-call(s32[4]{0:T(128)S(1)} %pad_add_fusion.idx_ref, bf16[128,8192]{1,0:T(8,128)(2,1)S(1)} %copy-done, bf16[128,8192]{1,0:T(8,128)(2,1)S(1)} %copy-done, bf16[128,8192]{1,0:T(8,128)(2,1)} %collective-permute-done.refs_2_.refs_3_, bf16[128,8192]{1,0:T(8,128)(2,1)} %collective-permute-done.refs_2_.refs_3_, ...), custom_call_target="tpu_custom_call" | custom-call | flops 1 | bytes 1 | tf_op jit(solution)/shard_map/right_grads/pallas_call | solution.py:672
  130.6 1.5 collective-permute-start.24
  132.2 0.6 collective-permute-start.27
  132.8 3.5 %right_grads.3 = bf16[2,512,128]{2,1,0:T(8,128)(2,1)S(1)} custom-call(s32[4]{0:T(128)S(1)} %pad_add_fusion.idx_ref, bf16[128,8192]{1,0:T(8,128)(2,1)S(1)} %copy-done, bf16[128,8192]{1,0:T(8,128)(2,1)S(1)} %copy-done, bf16[128,8192]{1,0:T(8,128)(2,1)} %collective-permute-done.refs_2_.refs_3_, bf16[128,8192]{1,0:T(8,128)(2,1)} %collective-permute-done.refs_2_.refs_3_, ...), custom_call_target="tpu_custom_call" | custom-call | flops 10000000000 | bytes 10000000 | tf_op jit(solution)/shard_map/right_grads/pallas_call | solution.py:672
  136.4 3.8 %collective-permute-done.24 = bf16[2,512,128]{2,1,0:T(8,128)(2,1)S(1)} collective-permute-done((bf16[2,512,128]{2,1,0:T(8,128)(2,1)S(1)}, bf16[2,512,128]{2,1,0:T(8,128)(2,1)S(1)}, u32[]{:S(2)}, u32[]{:S(2)}) %collective-permute-start.24) | collective-permute-done | bytes 262176 | tf_op jit(solution)/shard_map/ppermute | solution.py:706
  140.2 0.1 add_convert_fusion
  140.3 0.7 collective-permute-start.25
  141.0 3.6 %collective-permute-start.26 = (bf16[512,128]{1,0:T(8,128)(2,1)S(1)}, bf16[512,128]{1,0:T(8,128)(2,1)S(1)}, u32[]{:S(2)}, u32[]{:S(2)}) collective-permute-start(bf16[512,128]{1,0:T(8,128)(2,1)S(1)} %get-tuple-element.87), channel_id=1, source_target_pairs={{0,8},{1,12},{2,0},{3,4},{4,9},{5,13},{6,1},{7,5},{8,10},{9,14},{1... | collective-permute-start | bytes 393224 | tf_op jit(solution)/shard_map/ppermute | solution.py:713
  144.6 0.2 reshape.32
  144.8 0.7 copy.8
  145.5 10.6 %collective-permute-done.26 = bf16[512,128]{1,0:T(8,128)(2,1)S(1)} collective-permute-done((bf16[512,128]{1,0:T(8,128)(2,1)S(1)}, bf16[512,128]{1,0:T(8,128)(2,1)S(1)}, u32[]{:S(2)}, u32[]{:S(2)}) %collective-permute-start.26) | collective-permute-done | bytes 131104 | tf_op jit(solution)/shard_map/ppermute | solution.py:713
  156.1 0.7 convert_add_fusion.2
  (32 shorter events, 0.2 us)
Async XLA Ops:
  0.6 6.9 %collective-permute-start = (bf16[128,8192]{1,0:T(8,128)(2,1)}, bf16[128,8192]{1,0:T(8,128)(2,1)}, u32[]{:S(2)}, u32[]{:S(2)}) collective-permute-start(bf16[128,8192]{1,0:T(8,128)(2,1)} %refs_1_.11), channel_id=1, source_target_pairs={{0,4},{4,0},{8,12},{12,8},{1,5},{5,1},{9,13},{13,9},{2,6},{6,2},{1... | collective-permute-start | bytes 6291464 | tf_op jit(solution)/shard_map/ppermute | solution.py:700
  1.8 5.8 %copy-start = (bf16[128,8192]{1,0:T(8,128)(2,1)S(1)}, bf16[128,8192]{1,0:T(8,128)(2,1)}, u32[]{:S(2)}) copy-start(bf16[128,8192]{1,0:T(8,128)(2,1)} %refs_1_.11) | copy-start | bytes 6291460
  4.8 15.3 %collective-permute-start.1 = (bf16[64,4096]{1,0:T(8,128)(2,1)}, bf16[64,4096]{1,0:T(8,128)(2,1)S(1)}, u32[]{:S(2)}, u32[]{:S(2)}) collective-permute-start(bf16[64,4096]{1,0:T(8,128)(2,1)} %get-tuple-element.44), channel_id=1, source_target_pairs={{0,8},{4,12},{8,0},{12,4},{1,9},{5,13},{9,1},{13,5},{2,10},{6,14},... | collective-permute-start | bytes 1572872 | tf_op jit(solution)/shard_map/ppermute | solution.py:703
  7.5 16.4 %copy-start.2 = (bf16[16,32,128]{2,1,0:T(8,128)(2,1)S(1)}, bf16[16,32,128]{2,1,0:T(8,128)(2,1)}, u32[]{:S(2)}) copy-start(bf16[16,32,128]{2,1,0:T(8,128)(2,1)} %param.10) | copy-start | bytes 393220
  18.3 0.9 copy-start.1
  20.1 19.2 %collective-permute-start.2 = (bf16[64,4096]{1,0:T(8,128)(2,1)S(1)}, bf16[64,4096]{1,0:T(8,128)(2,1)S(1)}, u32[]{:S(2)}, u32[]{:S(2)}) collective-permute-start(bf16[64,4096]{1,0:T(8,128)(2,1)S(1)} %collective-permute-done.1.refs_0_.refs_4_), channel_id=1, source_target_pairs={{0,1},{1,0},{2,3},{3,2},{4,5},{5,4},{6,7},{7,6},{8,9},{9,8},{10,11... | collective-permute-start | bytes 1572872 | tf_op jit(solution)/shard_map/ppermute | solution.py:706
  21.9 22.8 %collective-permute-start.5 = (bf16[64,4096]{1,0:T(8,128)(2,1)S(1)}, bf16[64,4096]{1,0:T(8,128)(2,1)}, u32[]{:S(2)}, u32[]{:S(2)}) collective-permute-start(bf16[64,4096]{1,0:T(8,128)(2,1)S(1)} %collective-permute-done.1.refs_0_.refs_4_), channel_id=1, source_target_pairs={{0,4},{4,0},{8,12},{12,8},{1,5},{5,1},{9,13},{13,9},{2,6},{6,2},{1... | collective-permute-start | bytes 1572872 | tf_op jit(solution)/shard_map/ppermute | solution.py:700
  21.9 21.1 %collective-permute-start.7 = (bf16[2,128,1792]{2,1,0:T(8,128)(2,1)}, bf16[2,128,1792]{2,1,0:T(8,128)(2,1)}, u32[]{:S(2)}, u32[]{:S(2)}) collective-permute-start(bf16[2,128,1792]{2,1,0:T(8,128)(2,1)} %bitcast.11), channel_id=1, source_target_pairs={{0,4},{4,0},{8,12},{12,8},{1,5},{5,1},{9,13},{13,9},{2,6},{6,2},{1... | collective-permute-start | bytes 2752520 | tf_op jit(solution)/shard_map/ppermute | solution.py:700
  22.4 16.0 %collective-permute-start.4 = (bf16[64,4096]{1,0:T(8,128)(2,1)}, bf16[64,4096]{1,0:T(8,128)(2,1)}, u32[]{:S(2)}, u32[]{:S(2)}) collective-permute-start(bf16[64,4096]{1,0:T(8,128)(2,1)} %get-tuple-element.51), channel_id=1, source_target_pairs={{0,8},{4,12},{8,0},{12,4},{1,9},{5,13},{9,1},{13,5},{2,10},{6,14},... | collective-permute-start | bytes 1572872 | tf_op jit(solution)/shard_map/ppermute | solution.py:703
  23.9 2.3 %collective-permute-start.3 = (bf16[16,32,128]{2,1,0:T(8,128)(2,1)S(1)}, bf16[16,32,128]{2,1,0:T(8,128)(2,1)S(1)}, u32[]{:S(2)}, u32[]{:S(2)}) collective-permute-start(bf16[16,32,128]{2,1,0:T(8,128)(2,1)S(1)} %copy-done.2), channel_id=1, source_target_pairs={{0,0},{1,4},{2,8},{3,12},{4,1},{5,5},{6,9},{7,13},{8,2},{9,6},{10,... | collective-permute-start | bytes 393224 | tf_op jit(solution)/shard_map/ppermute | solution.py:713
  39.3 5.5 %collective-permute-start.6 = (bf16[64,4096]{1,0:T(8,128)(2,1)S(1)}, bf16[64,4096]{1,0:T(8,128)(2,1)S(1)}, u32[]{:S(2)}, u32[]{:S(2)}) collective-permute-start(bf16[64,4096]{1,0:T(8,128)(2,1)S(1)} %collective-permute-done.2.refs_1_.refs_5_), channel_id=1, source_target_pairs={{0,4},{4,0},{8,12},{12,8},{1,5},{5,1},{9,13},{13,9},{2,6},{6,2},{1... | collective-permute-start | bytes 1572872 | tf_op jit(solution)/shard_map/ppermute | solution.py:700
  39.4 30.0 %collective-permute-start.11 = (bf16[1,768,128]{2,1,0:T(8,128)(2,1)S(1)}, bf16[1,768,128]{2,1,0:T(8,128)(2,1)S(1)}, u32[]{:S(2)}, u32[]{:S(2)}) collective-permute-start(bf16[1,768,128]{2,1,0:T(8,128)(2,1)S(1)} %maximum_bitcast_fusion), channel_id=1, source_target_pairs={{0,2},{1,3},{2,0},{3,1},{4,6},{5,7},{6,4},{7,5},{8,10},{9,11},{10,... | collective-permute-start | bytes 589832 | tf_op jit(solution)/shard_map/ppermute | solution.py:706
  44.7 24.8 %collective-permute-start.9 = (bf16[2,128,1792]{2,1,0:T(8,128)(2,1)S(1)}, bf16[2,128,1792]{2,1,0:T(8,128)(2,1)S(1)}, u32[]{:S(2)}, u32[]{:S(2)}) collective-permute-start(bf16[2,128,1792]{2,1,0:T(8,128)(2,1)S(1)} %fusion.1), channel_id=1, source_target_pairs={{0,8},{4,12},{8,0},{12,4},{1,9},{5,13},{9,1},{13,5},{2,10},{6,14},... | collective-permute-start | bytes 2752520 | tf_op jit(solution)/shard_map/ppermute | solution.py:703
  54.8 14.3 %collective-permute-start.10 = (bf16[2,128,1792]{2,1,0:T(8,128)(2,1)S(1)}, bf16[2,128,1792]{2,1,0:T(8,128)(2,1)S(1)}, u32[]{:S(2)}, u32[]{:S(2)}) collective-permute-start(bf16[2,128,1792]{2,1,0:T(8,128)(2,1)S(1)} %bitcast.58), channel_id=1, source_target_pairs={{0,4},{4,0},{8,12},{12,8},{1,5},{5,1},{9,13},{13,9},{2,6},{6,2},{1... | collective-permute-start | bytes 2752520 | tf_op jit(solution)/shard_map/ppermute | solution.py:700
  55.1 14.3 %collective-permute-start.8 = (bf16[64,4096]{1,0:T(8,128)(2,1)}, bf16[64,4096]{1,0:T(8,128)(2,1)S(1)}, u32[]{:S(2)}, u32[]{:S(2)}) collective-permute-start(bf16[64,4096]{1,0:T(8,128)(2,1)} %collective-permute-done.4.refs_4_.refs_8_), channel_id=1, source_target_pairs={{0,1},{1,0},{2,3},{3,2},{4,5},{5,4},{6,7},{7,6},{8,9},{9,8},{10,11... | collective-permute-start | bytes 1572872 | tf_op jit(solution)/shard_map/ppermute | solution.py:706
  69.4 3.8 %collective-permute-start.12 = (bf16[2,2,128,1792]{3,2,1,0:T(8,128)(2,1)S(1)}, bf16[2,2,128,1792]{3,2,1,0:T(8,128)(2,1)S(1)}, u32[]{:S(2)}, u32[]{:S(2)}) collective-permute-start(bf16[2,2,128,1792]{3,2,1,0:T(8,128)(2,1)S(1)} %get-tuple-element.64), channel_id=1, source_target_pairs={{0,4},{4,0},{8,12},{12,8},{1,5},{5,1},{9,13},{13,9},{2,6},{6,2},{1... | collective-permute-start | bytes 5505032 | tf_op jit(solution)/shard_map/ppermute | solution.py:700
  69.8 11.4 %collective-permute-start.13 = (bf16[2,768,128]{2,1,0:T(8,128)(2,1)S(1)}, bf16[2,768,128]{2,1,0:T(8,128)(2,1)S(1)}, u32[]{:S(2)}, u32[]{:S(2)}) collective-permute-start(bf16[2,768,128]{2,1,0:T(8,128)(2,1)S(1)} %pad_maximum_fusion.1), channel_id=1, source_target_pairs={{0,1},{1,0},{2,3},{3,2},{4,5},{5,4},{6,7},{7,6},{8,9},{9,8},{10,11... | collective-permute-start | bytes 1179656 | tf_op jit(solution)/shard_map/ppermute | solution.py:706
  71.4 23.2 %collective-permute-start.16 = (bf16[2,128,1792]{2,1,0:T(8,128)(2,1)S(1)}, bf16[2,128,1792]{2,1,0:T(8,128)(2,1)S(1)}, u32[]{:S(2)}, u32[]{:S(2)}) collective-permute-start(bf16[2,128,1792]{2,1,0:T(8,128)(2,1)S(1)} %fusion), channel_id=1, source_target_pairs={{0,8},{4,12},{8,0},{12,4},{1,9},{5,13},{9,1},{13,5},{2,10},{6,14},... | collective-permute-start | bytes 2752520 | tf_op jit(solution)/shard_map/ppermute | solution.py:703
  73.9 15.2 %collective-permute-start.17 = (bf16[128,1792]{1,0:T(8,128)(2,1)S(1)}, bf16[128,1792]{1,0:T(8,128)(2,1)S(1)}, u32[]{:S(2)}, u32[]{:S(2)}) collective-permute-start(bf16[128,1792]{1,0:T(8,128)(2,1)S(1)} %fusion.5.mine_ref), channel_id=1, source_target_pairs={{0,4},{4,0},{8,12},{12,8},{1,5},{5,1},{9,13},{13,9},{2,6},{6,2},{1... | collective-permute-start | bytes 1376264 | tf_op jit(solution)/shard_map/ppermute | solution.py:700
  86.6 17.8 %collective-permute-start.20 = (bf16[128,1792]{1,0:T(8,128)(2,1)S(1)}, bf16[128,1792]{1,0:T(8,128)(2,1)S(1)}, u32[]{:S(2)}, u32[]{:S(2)}) collective-permute-start(bf16[128,1792]{1,0:T(8,128)(2,1)S(1)} %fusion.5.mine_ref), channel_id=1, source_target_pairs={{0,8},{4,12},{8,0},{12,4},{1,9},{5,13},{9,1},{13,5},{2,10},{6,14},... | collective-permute-start | bytes 1376264 | tf_op jit(solution)/shard_map/ppermute | solution.py:703
  88.6 7.4 %collective-permute-start.14 = (bf16[64,4096]{1,0:T(8,128)(2,1)}, bf16[64,4096]{1,0:T(8,128)(2,1)S(1)}, u32[]{:S(2)}, u32[]{:S(2)}) collective-permute-start(bf16[64,4096]{1,0:T(8,128)(2,1)} %collective-permute-done.4.refs_4_.refs_8_), channel_id=1, source_target_pairs={{0,4},{4,0},{8,12},{12,8},{1,5},{5,1},{9,13},{13,9},{2,6},{6,2},{1... | collective-permute-start | bytes 1572872 | tf_op jit(solution)/shard_map/ppermute | solution.py:700
  88.6 7.4 %collective-permute-start.15 = (bf16[64,4096]{1,0:T(8,128)(2,1)S(1)}, bf16[64,4096]{1,0:T(8,128)(2,1)S(1)}, u32[]{:S(2)}, u32[]{:S(2)}) collective-permute-start(bf16[64,4096]{1,0:T(8,128)(2,1)S(1)} %collective-permute-done.8.refs_5_.refs_9_), channel_id=1, source_target_pairs={{0,4},{4,0},{8,12},{12,8},{1,5},{5,1},{9,13},{13,9},{2,6},{6,2},{1... | collective-permute-start | bytes 1572872 | tf_op jit(solution)/shard_map/ppermute | solution.py:700
  95.1 9.3 %collective-permute-start.19 = (bf16[128,1792]{1,0:T(8,128)(2,1)S(1)}, bf16[128,1792]{1,0:T(8,128)(2,1)S(1)}, u32[]{:S(2)}, u32[]{:S(2)}) collective-permute-start(bf16[128,1792]{1,0:T(8,128)(2,1)S(1)} %fusion.3.mine_ref), channel_id=1, source_target_pairs={{0,4},{4,0},{8,12},{12,8},{1,5},{5,1},{9,13},{13,9},{2,6},{6,2},{1... | collective-permute-start | bytes 1376264 | tf_op jit(solution)/shard_map/ppermute | solution.py:700
  95.2 18.3 %collective-permute-start.18 = (bf16[128,1792]{1,0:T(8,128)(2,1)S(1)}, bf16[128,1792]{1,0:T(8,128)(2,1)S(1)}, u32[]{:S(2)}, u32[]{:S(2)}) collective-permute-start(bf16[128,1792]{1,0:T(8,128)(2,1)S(1)} %fusion.3.mine_ref), channel_id=1, source_target_pairs={{0,8},{4,12},{8,0},{12,4},{1,9},{5,13},{9,1},{13,5},{2,10},{6,14},... | collective-permute-start | bytes 1376264 | tf_op jit(solution)/shard_map/ppermute | solution.py:703
  104.4 9.1 %collective-permute-start.22 = (bf16[128,1792]{1,0:T(8,128)(2,1)S(1)}, bf16[128,1792]{1,0:T(8,128)(2,1)S(1)}, u32[]{:S(2)}, u32[]{:S(2)}) collective-permute-start(bf16[128,1792]{1,0:T(8,128)(2,1)S(1)} %collective-permute-done.20.refs_1_), channel_id=1, source_target_pairs={{0,4},{4,0},{8,12},{12,8},{1,5},{5,1},{9,13},{13,9},{2,6},{6,2},{1... | collective-permute-start | bytes 1376264 | tf_op jit(solution)/shard_map/ppermute | solution.py:700
  113.5 1.8 %collective-permute-start.21 = (bf16[128,1792]{1,0:T(8,128)(2,1)S(1)}, bf16[128,1792]{1,0:T(8,128)(2,1)S(1)}, u32[]{:S(2)}, u32[]{:S(2)}) collective-permute-start(bf16[128,1792]{1,0:T(8,128)(2,1)S(1)} %collective-permute-done.18.refs_0_), channel_id=1, source_target_pairs={{0,4},{4,0},{8,12},{12,8},{1,5},{5,1},{9,13},{13,9},{2,6},{6,2},{1... | collective-permute-start | bytes 1376264 | tf_op jit(solution)/shard_map/ppermute | solution.py:700
  126.5 5.7 %collective-permute-start.23 = (bf16[2,256,128]{2,1,0:T(8,128)(2,1)S(1)}, bf16[2,256,128]{2,1,0:T(8,128)(2,1)S(1)}, u32[]{:S(2)}, u32[]{:S(2)}) collective-permute-start(bf16[2,256,128]{2,1,0:T(8,128)(2,1)S(1)} %slice.51), channel_id=1, source_target_pairs={{0,1},{1,0},{2,3},{3,2},{4,5},{5,4},{6,7},{7,6},{8,9},{9,8},{10,11... | collective-permute-start | bytes 393224 | tf_op jit(solution)/shard_map/ppermute | solution.py:706
  130.6 9.5 %collective-permute-start.24 = (bf16[2,512,128]{2,1,0:T(8,128)(2,1)S(1)}, bf16[2,512,128]{2,1,0:T(8,128)(2,1)S(1)}, u32[]{:S(2)}, u32[]{:S(2)}) collective-permute-start(bf16[2,512,128]{2,1,0:T(8,128)(2,1)S(1)} %right_grads.2), channel_id=1, source_target_pairs={{0,1},{1,0},{2,3},{3,2},{4,5},{5,4},{6,7},{7,6},{8,9},{9,8},{10,11... | collective-permute-start | bytes 786440 | tf_op jit(solution)/shard_map/ppermute | solution.py:706
  132.2 12.3 %collective-permute-start.27 = (bf16[256,128]{1,0:T(8,128)(2,1)S(1)}, bf16[256,128]{1,0:T(8,128)(2,1)S(1)}, u32[]{:S(2)}, u32[]{:S(2)}) collective-permute-start(bf16[256,128]{1,0:T(8,128)(2,1)S(1)} %slice_bitcast_fusion.6), channel_id=1, source_target_pairs={{0,2},{1,3},{2,0},{3,1},{4,6},{5,7},{6,4},{7,5},{8,10},{9,11},{10,... | collective-permute-start | bytes 196616 | tf_op jit(solution)/shard_map/ppermute | solution.py:706
  140.3 5.2 %collective-permute-start.25 = (bf16[512,128]{1,0:T(8,128)(2,1)S(1)}, bf16[512,128]{1,0:T(8,128)(2,1)S(1)}, u32[]{:S(2)}, u32[]{:S(2)}) collective-permute-start(bf16[512,128]{1,0:T(8,128)(2,1)S(1)} %get-tuple-element.86), channel_id=1, source_target_pairs={{0,0},{1,4},{2,8},{3,12},{4,1},{5,5},{6,9},{7,13},{8,2},{9,6},{10,... | collective-permute-start | bytes 393224 | tf_op jit(solution)/shard_map/ppermute | solution.py:713
  141.0 15.2 %collective-permute-start.26 = (bf16[512,128]{1,0:T(8,128)(2,1)S(1)}, bf16[512,128]{1,0:T(8,128)(2,1)S(1)}, u32[]{:S(2)}, u32[]{:S(2)}) collective-permute-start(bf16[512,128]{1,0:T(8,128)(2,1)S(1)} %get-tuple-element.87), channel_id=1, source_target_pairs={{0,8},{1,12},{2,0},{3,4},{4,9},{5,13},{6,1},{7,5},{8,10},{9,14},{1... | collective-permute-start | bytes 393224 | tf_op jit(solution)/shard_map/ppermute | solution.py:713

commit v18 on v17

--- a/solution.py
+++ b/solution.py
@@ -739,29 +739,29 @@
     late_first = across(after(rest, mine))
     turned = after(turned, left_rows, late_first)
     factors = jnp.concatenate([turned.reshape(-1, LANES), left_rows], axis=0)[None]
-    sums = add(mine[0], swap(other[0])).astype(BF16)
+    sums = add(mine[0], after(swap(other[0]), left_rows)).astype(BF16)
 
     arrived = after(arrived, mine)
     partner = along(arrived, 1)
     near_arrived = swap(arrived)
     partner = after(partner, factors)
     got_early = across(sums)
-    more = along(after(factors, partner), 2)
     order = jnp.concatenate([base, jnp.stack([chip, z])]).astype(jnp.int32)
     own = [tokens, tokens, near_tokens, near_tokens]
     late = [arrived, partner, near_arrived, swap(partner)]
     late_pieces = [(t, None, 3) for t in late]
     late_order = after(scalars(other_block), sums)
     mine, other = products(late_pieces, late_order, gate_weight, up_weight, 0, part)
-    near = swap(other[0])
+    near = swap(after(other[0], got_early))
+    more = along(after(factors, mine), 2)
     late_partner = along(after(late_first, mine), 1)
-    mine_order = after(scalars(mine_block), mine)
+    sums = add(mine[0], near).astype(BF16)
+    got = across(sums)
+    mine_order = after(scalars(mine_block), sums)
     kept, other = products(
         own_pieces + late_pieces, mine_order, gate_weight, up_weight, 0, part
     )
-    sums = add(mine[0], after(near, kept)).astype(BF16)
-    got = across(sums)
-    near_kept = swap(after(other, got_early, sums, more, late_partner))
+    near_kept = swap(after(other, got, more, late_partner))
     factors = jnp.concatenate([factors, after(more, kept)], axis=0)
     more = along(factors, 1)
 
@@ -770,20 +770,20 @@
         return (jax.nn.silu(total[0]) * total[1]).astype(BF16)
 
     hidden1 = activate(1, got_early)
+    got1 = across(hidden1)
     near1 = swap(hidden1)
-    factors = jnp.concatenate([factors, after(more, hidden1)], axis=0)
-    mixed0, rest0, left_diag = student_part(
-        [after(tokens, hidden1, sums)] + own[1:], order, factors, pairs, tensor_count
-    )
-    got1 = across(after(hidden1, mixed0))
-    target1 = target_part(1.0, [], hidden1, after(near1, mixed0), down_weight, chip)
-    hidden0 = activate(0, after(got, target1))
+    hidden0 = activate(0, after(got, hidden1))
     got0 = across(hidden0)
     near0 = swap(hidden0)
-    late_partner = after(late_partner, mixed0)
-    late += [late_first, late_partner, swap(after(late_first, mixed0)), swap(late_partner)]
+    target1 = target_part(1.0, [], hidden1, after(near1, hidden0), down_weight, chip)
+    factors = jnp.concatenate([factors, after(more, target1)], axis=0)
+    mixed0, rest0, left_diag = student_part(
+        [after(tokens, target1)] + own[1:], order, factors, pairs, tensor_count
+    )
+    late_partner = after(late_partner, target1)
+    late += [late_first, late_partner, swap(after(late_first, target1)), swap(late_partner)]
     mixed1, rest1 = student_part(
-        [after(late[0], hidden0)] + late[1:],
+        [after(late[0], mixed0)] + late[1:],
         order,
         factors,
         pairs,

time: 158 us -> 159 us (level)
  waiting for transfers between devices: 44.8 us -> 39 us
  starting transfers between devices: 26.4 us -> 30.2 us
  local copies, waits for them, and re-layouts: 2.05 us -> 3.97 us
    ppermute x7, waiting for transfers between devices: 10.9 us -> 5.79 us  [along(): lax.ppermute(value, 'tensor', [(i, i ^ bit) for i in range(tensor_count)])]
    ppermute x12, starting transfers between devices: 2.41 us -> 5.78 us  [swap(): return lax.ppermute(value, 'fsdp', [(i, i ^ 1) for i in range(fsdp_count)])]
    ppermute x12, waiting for transfers between devices: 2.98 us -> 6.17 us  [swap(): return lax.ppermute(value, 'fsdp', [(i, i ^ 1) for i in range(fsdp_count)])]
    ppermute x6, waiting for transfers between devices: 20.2 us -> 17.6 us  [across(): return lax.ppermute(value, 'fsdp', [(i, i ^ 2) for i in range(fsdp_count)])]
    unnamed x6 -> x22, local copies, waits for them, and re-layouts: 0.94 us -> 2.85 us
  transfers between devices with their start and end apart: 28 -> 28, of which waited for: 10 -> 12; matrix products, arithmetic and copies ran while one was open for 4% -> 4% of each run, Pallas kernels for 42% -> 42%
where the time goes in v18:
time: 159 us; the launch traced here: 158 us
  Pallas kernels  77.4 us (49%)
  waiting for transfers between devices  39 us (25%)
  starting transfers between devices  30.2 us (19%)
  other arithmetic  6.18 us (4%)
  local copies, waits for them, and re-layouts  3.97 us (2%)
    pallas_call x3, Pallas kernels, products(): pl.pallas_call(functools.partial(products_kernel, sets), grid_spec=pltpu....  33.7 us
    ppermute x6, waiting for transfers between devices, across(): return lax.ppermute(value, 'fsdp', [(i, i ^ 2) for i in range(fsdp_count)])  17.6 us
    ppermute x7, starting transfers between devices, along(): lax.ppermute(value, 'tensor', [(i, i ^ bit) for i in range(tensor_count)])  11.8 us
    pallas_call x1, Pallas kernels, left_grads(): pl.pallas_call(functools.partial(left_kernel, chunks, scale), grid_spec=p...  11.1 us
    pallas_call x2, Pallas kernels, student_part(): pl.pallas_call(functools.partial(student_kernel, steps, bool(late), tenso...  10.6 us
    pallas_call x2, Pallas kernels, target_part(): pl.pallas_call(functools.partial(target_kernel, sign), grid_spec=pltpu.Pr...  10.4 us
    ppermute x3, waiting for transfers between devices, turn(): return lax.ppermute(value, both_axes, perm)  9.44 us
    pallas_call x2, Pallas kernels, right_grads(): pl.pallas_call(functools.partial(right_kernel, pairs, bit), grid_spec=plt...  6.88 us
  transfers between devices with their start and end apart: 28, of which 12 were waited for; matrix products, arithmetic and copies ran while one was open for 4% of the time, Pallas kernels for 42%

profile of v18, /device:TPU:0, one launch (start us, length us, event | category | flops | bytes accessed | tf_op | source)
XLA Modules:
  0.0 157.7 jit_solution(1999241346609835267)
XLA Ops:
  0.6 0.5 collective-permute-start
  1.1 0.6 pad_add_fusion.1.idx_ref
  1.7 3.0 %cut_tokens.1 = (bf16[64,4096]{1,0:T(8,128)(2,1)}, bf16[64,4096]{1,0:T(8,128)(2,1)}) custom-call(s32[3]{0:T(128)} %pad_add_fusion.1.idx_ref, bf16[128,8192]{1,0:T(8,128)(2,1)} %refs_1_.11, bf16[128,8192]{1,0:T(8,128)(2,1)} %refs_1_.11), custom_call_target="tpu_custom_call" | custom-call | flops 1 | bytes 1 | tf_op jit(solution)/shard_map/cut_tokens/pallas_call | solution.py:313
  4.8 2.5 %collective-permute-start.1 = (bf16[64,4096]{1,0:T(8,128)(2,1)}, bf16[64,4096]{1,0:T(8,128)(2,1)S(1)}, u32[]{:S(2)}, u32[]{:S(2)}) collective-permute-start(bf16[64,4096]{1,0:T(8,128)(2,1)} %get-tuple-element.44), channel_id=1, source_target_pairs={{0,8},{4,12},{8,0},{12,4},{1,9},{5,13},{9,1},{13,5},{2,10},{6,14},... | collective-permute-start | bytes 1572872 | tf_op jit(solution)/shard_map/ppermute | solution.py:703
  7.3 0.1 concatenate.25.idx_ref
  7.4 10.8 %gate_up_products.3 = (bf16[1,2,128,1792]{3,2,1,0:T(8,128)(2,1)S(1)}, bf16[1,2,128,1792]{3,2,1,0:T(8,128)(2,1)}) custom-call(s32[5]{0:T(128)S(1)} %concatenate.25.idx_ref, bf16[128,8192]{1,0:T(8,128)(2,1)S(1)} %copy-done, bf16[128,8192]{1,0:T(8,128)(2,1)S(1)} %copy-done, bf16[128,8192]{1,0:T(8,128)(2,1)} %collective-permute-done.refs_2_.refs_3_, ...), custom_call_target="tpu_custom_call" | custom-call | flops 1 | bytes 1 | tf_op jit(solution)/shard_map/gate_up_products/pallas_call | solution.py:374
  18.1 0.9 copy-done.6
  19.1 0.2 collective-permute-start.7
  19.3 0.7 collective-permute-start.4
  20.1 1.8 %collective-permute-start.2 = (bf16[64,4096]{1,0:T(8,128)(2,1)S(1)}, bf16[64,4096]{1,0:T(8,128)(2,1)S(1)}, u32[]{:S(2)}, u32[]{:S(2)}) collective-permute-start(bf16[64,4096]{1,0:T(8,128)(2,1)S(1)} %collective-permute-done.1.refs_0_.refs_4_), channel_id=1, source_target_pairs={{0,1},{1,0},{2,3},{3,2},{4,5},{5,4},{6,7},{7,6},{8,9},{9,8},{10,11... | collective-permute-start | bytes 1572872 | tf_op jit(solution)/shard_map/ppermute | solution.py:706
  21.9 1.6 %pack_left.1 = bf16[256,128]{1,0:T(8,128)(2,1)} custom-call(bf16[32,16,64]{2,1,0:T(8,128)(2,1)} %left_ref), custom_call_target="tpu_custom_call" | custom-call | flops 10000000000 | bytes 10000000 | tf_op jit(solution)/shard_map/pack_left/pallas_call | solution.py:339
  23.5 1.7 %fusion.1 = bf16[2,128,1792]{2,1,0:T(8,128)(2,1)S(1)} fusion(bf16[2,128,1792]{2,1,0:T(8,128)(2,1)} %collective-permute-done.7, bf16[1,2,128,1792]{3,2,1,0:T(8,128)(2,1)} %copy-done.6), kind=kLoop, calls=%fused_computation.3 | loop fusion | flops 1835008 | bytes 2752512 | tf_op jit(solution)/shard_map/convert_element_type | solution.py:742
  25.2 1.6 collective-permute-start.9
  26.8 0.7 collective-permute-start.3
  27.5 1.9 %collective-permute-start.5 = (bf16[64,4096]{1,0:T(8,128)(2,1)S(1)}, bf16[64,4096]{1,0:T(8,128)(2,1)S(1)}, u32[]{:S(2)}, u32[]{:S(2)}) collective-permute-start(bf16[64,4096]{1,0:T(8,128)(2,1)S(1)} %collective-permute-done.1.refs_0_.refs_4_), channel_id=1, source_target_pairs={{0,4},{4,0},{8,12},{12,8},{1,5},{5,1},{9,13},{13,9},{2,6},{6,2},{1... | collective-permute-start | bytes 1572872 | tf_op jit(solution)/shard_map/ppermute | solution.py:700
  29.3 5.0 %collective-permute-done.4.refs_4_.refs_8_ = bf16[64,4096]{1,0:T(8,128)(2,1)} collective-permute-done((bf16[64,4096]{1,0:T(8,128)(2,1)}, bf16[64,4096]{1,0:T(8,128)(2,1)}, u32[]{:S(2)}, u32[]{:S(2)}) %collective-permute-start.4) | collective-permute-done | bytes 524320 | tf_op jit(solution)/shard_map/ppermute | solution.py:703
  34.4 0.9 collective-permute-done.2.refs_1_.refs_5_
  35.3 1.6 %collective-permute-start.6 = (bf16[64,4096]{1,0:T(8,128)(2,1)S(1)}, bf16[64,4096]{1,0:T(8,128)(2,1)S(1)}, u32[]{:S(2)}, u32[]{:S(2)}) collective-permute-start(bf16[64,4096]{1,0:T(8,128)(2,1)S(1)} %collective-permute-done.2.refs_1_.refs_5_), channel_id=1, source_target_pairs={{0,4},{4,0},{8,12},{12,8},{1,5},{5,1},{9,13},{13,9},{2,6},{6,2},{1... | collective-permute-start | bytes 1572872 | tf_op jit(solution)/shard_map/ppermute | solution.py:700
  36.9 1.5 collective-permute-done.6.refs_3_.refs_7_
  38.5 10.6 %gate_up_products.4 = (bf16[1,2,128,1792]{3,2,1,0:T(8,128)(2,1)S(1)}, bf16[1,2,128,1792]{3,2,1,0:T(8,128)(2,1)}) custom-call(s32[5]{0:T(128)S(1)} %concatenate.25.idx_ref, bf16[64,4096]{1,0:T(8,128)(2,1)S(1)} %collective-permute-done.1.refs_0_.refs_4_, bf16[64,4096]{1,0:T(8,128)(2,1)S(1)} %collective-permute-done.2.refs_1_.refs_5_, ...), custom_call_target="tpu_custom_call" | custom-call | flops 1 | bytes 1 | tf_op jit(solution)/shard_map/gate_up_products/pallas_call | solution.py:374
  49.1 0.9 copy-done.5
  50.0 4.4 %collective-permute-done.9 = bf16[2,128,1792]{2,1,0:T(8,128)(2,1)S(1)} collective-permute-done((bf16[2,128,1792]{2,1,0:T(8,128)(2,1)S(1)}, bf16[2,128,1792]{2,1,0:T(8,128)(2,1)S(1)}, u32[]{:S(2)}, u32[]{:S(2)}) %collective-permute-start.9) | collective-permute-done | bytes 917536 | tf_op jit(solution)/shard_map/ppermute | solution.py:703
  54.4 0.9 copy-done.7
  55.3 0.1 concatenate.27.idx_ref
  55.4 4.4 %collective-permute-start.12 = (bf16[1,768,128]{2,1,0:T(8,128)(2,1)S(1)}, bf16[1,768,128]{2,1,0:T(8,128)(2,1)S(1)}, u32[]{:S(2)}, u32[]{:S(2)}) collective-permute-start(bf16[1,768,128]{2,1,0:T(8,128)(2,1)S(1)} %maximum_bitcast_fusion), channel_id=1, source_target_pairs={{0,2},{1,3},{2,0},{3,1},{4,6},{5,7},{6,4},{7,5},{8,10},{9,11},{10,... | collective-permute-start | bytes 589832 | tf_op jit(solution)/shard_map/ppermute | solution.py:706
  59.8 1.6 collective-permute-start.8
  61.3 1.7 %fusion = bf16[2,128,1792]{2,1,0:T(8,128)(2,1)S(1)} fusion(bf16[2,128,1792]{2,1,0:T(8,128)(2,1)} %collective-permute-done.10, bf16[1,2,128,1792]{3,2,1,0:T(8,128)(2,1)} %copy-done.5), kind=kLoop, calls=%fused_computation.1 | loop fusion | flops 1835008 | bytes 2752512 | tf_op jit(solution)/shard_map/convert_element_type | solution.py:758
  63.1 12.4 %gate_up_products.5 = (bf16[2,2,128,1792]{3,2,1,0:T(8,128)(2,1)S(1)}, bf16[2,2,128,1792]{3,2,1,0:T(8,128)(2,1)S(1)}) custom-call(s32[5]{0:T(128)S(1)} %concatenate.27.idx_ref, bf16[128,8192]{1,0:T(8,128)(2,1)S(1)} %copy-done, bf16[128,8192]{1,0:T(8,128)(2,1)S(1)} %copy-done, bf16[128,8192]{1,0:T(8,128)(2,1)} %collective-permute-done.refs_2_.refs_3_, ...), custom_call_target="tpu_custom_call" | custom-call | flops 10000000000 | bytes 10000000 | tf_op jit(solution)/shard_map/gate_up_products/pallas_call | solution.py:374
  75.5 1.6 %collective-permute-done.8.refs_5_.refs_9_ = bf16[64,4096]{1,0:T(8,128)(2,1)S(1)} collective-permute-done((bf16[64,4096]{1,0:T(8,128)(2,1)}, bf16[64,4096]{1,0:T(8,128)(2,1)S(1)}, u32[]{:S(2)}, u32[]{:S(2)}) %collective-permute-start.8) | collective-permute-done | bytes 524320 | tf_op jit(solution)/shard_map/ppermute | solution.py:706
  77.1 8.2 %collective-permute-done.11 = bf16[2,128,1792]{2,1,0:T(8,128)(2,1)S(1)} collective-permute-done((bf16[2,128,1792]{2,1,0:T(8,128)(2,1)S(1)}, bf16[2,128,1792]{2,1,0:T(8,128)(2,1)S(1)}, u32[]{:S(2)}, u32[]{:S(2)}) %collective-permute-start.11) | collective-permute-done | bytes 917536 | tf_op jit(solution)/shard_map/ppermute | solution.py:703
  85.4 0.5 collective-permute-start.19
  85.9 3.1 %collective-permute-done.13 = bf16[2,2,128,1792]{3,2,1,0:T(8,128)(2,1)S(1)} collective-permute-done((bf16[2,2,128,1792]{3,2,1,0:T(8,128)(2,1)S(1)}, bf16[2,2,128,1792]{3,2,1,0:T(8,128)(2,1)S(1)}, u32[]{:S(2)}, u32[]{:S(2)}) %collective-permute-start.13) | collective-permute-done | bytes 1835040 | tf_op jit(solution)/shard_map/ppermute | solution.py:700
  89.1 0.3 bitcast_add_fusion.1
  89.4 0.3 fusion.5.mine_ref
  89.6 0.2 collective-permute-start.14
  89.8 0.3 collective-permute-start.20
  90.1 0.3 bitcast_add_fusion
  90.5 0.3 fusion.3.mine_ref
  90.8 0.1 collective-permute-start.18
  90.9 1.7 %collective-permute-start.17 = (bf16[128,1792]{1,0:T(8,128)(2,1)S(1)}, bf16[128,1792]{1,0:T(8,128)(2,1)S(1)}, u32[]{:S(2)}, u32[]{:S(2)}) collective-permute-start(bf16[128,1792]{1,0:T(8,128)(2,1)S(1)} %fusion.3.mine_ref), channel_id=1, source_target_pairs={{0,8},{4,12},{8,0},{12,4},{1,9},{5,13},{9,1},{13,5},{2,10},{6,14},... | collective-permute-start | bytes 1376264 | tf_op jit(solution)/shard_map/ppermute | solution.py:703
  92.7 5.2 %target_part.2.refs_11_ = f32[256,2048]{1,0:T(8,128)S(1)} custom-call(s32[1]{0:T(128)} %bitcast.2.idx_ref, bf16[128,1792]{1,0:T(8,128)(2,1)S(1)} %fusion.5.mine_ref, bf16[128,1792]{1,0:T(8,128)(2,1)S(1)} %collective-permute-done.14.near_ref, bf16[3584,2048]{1,0:T(8,128)(2,1)} %refs_4_.5), custom_call_target="tpu_custom_call" | custom-call | flops 1 | bytes 1 | tf_op jit(solution)/shard_map/target_part/pallas_call | solution.py:412
  97.9 0.1 pad_maximum_fusion.refs_4_.refs_5_.refs_6_.refs_8_.refs_9_
  98.0 0.2 collective-permute-start.15
  98.2 0.3 collective-permute-start.16
  98.5 5.3 %student_part.2 = (bf16[8,256,256]{2,1,0:T(8,128)(2,1)S(1)}, f32[256,2048]{1,0:T(8,128)S(1)}, bf16[8,256,256]{2,1,0:T(8,128)(2,1)S(1)}) custom-call(s32[4]{0:T(128)S(1)} %pad_add_fusion.idx_ref, bf16[128,8192]{1,0:T(8,128)(2,1)S(1)} %copy-done, bf16[128,8192]{1,0:T(8,128)(2,1)S(1)} %copy-done, bf16[128,8192]{1,0:T(8,128)(2,1)} %collective-permute-done.refs_2_.refs_3_, ...), custom_call_target="tpu_custom_call" | custom-call | flops 10000000000 | bytes 10000000 | tf_op jit(solution)/shard_map/student_part/pallas_call | solution.py:550
  103.8 5.3 %student_part.3 = (bf16[8,256,256]{2,1,0:T(8,128)(2,1)S(1)}, f32[256,2048]{1,0:T(8,128)S(1)}) custom-call(s32[4]{0:T(128)S(1)} %pad_add_fusion.idx_ref, bf16[64,4096]{1,0:T(8,128)(2,1)S(1)} %collective-permute-done.1.refs_0_.refs_4_, bf16[64,4096]{1,0:T(8,128)(2,1)S(1)} %collective-permute-done.2.refs_1_.refs_5_, bf16[64,4096]{1,0:T(8,128)(2,1)S(1)} %copy-done.2, ...), custom_call_target="tpu_custom_call" | custom-call | flops 10000000000 | bytes 10000000 | tf_op jit(solution)/shard_map/student_part/pallas_call | solution.py:550
  109.1 0.2 collective-permute-start.22
  109.4 5.2 %target_part.3.refs_5_ = f32[256,2048]{1,0:T(8,128)S(1)} custom-call(s32[1]{0:T(128)} %bitcast.2.idx_ref, bf16[128,1792]{1,0:T(8,128)(2,1)S(1)} %fusion.3.mine_ref, bf16[128,1792]{1,0:T(8,128)(2,1)S(1)} %collective-permute-done.18.near_ref, bf16[3584,2048]{1,0:T(8,128)(2,1)} %refs_4_.5, f32[256,2048]{1,0:T(8,128)S(1)} %get-tuple-element.78.refs_0_), custom_call_target="tpu_custom_call" | custom-call | flops 1 | bytes 1 | tf_op jit(solution)/shard_map/target_part/pallas_call | solution.py:412
  114.6 0.4 collective-permute-start.21
  115.1 1.5 collective-permute-done.21.refs_2_
  116.5 11.1 %left_grads.1 = (bf16[4,256,128]{2,1,0:T(8,128)(2,1)S(1)}, bf16[8,256,512]{2,1,0:T(8,128)(2,1)S(1)}) custom-call(s32[4]{0:T(128)S(1)} %pad_add_fusion.idx_ref, bf16[128,1792]{1,0:T(8,128)(2,1)S(1)} %collective-permute-done.17.refs_0_, bf16[128,1792]{1,0:T(8,128)(2,1)S(1)} %collective-permute-done.20.refs_1_, ...), custom_call_target="tpu_custom_call" | custom-call | flops 1 | bytes 1 | tf_op jit(solution)/shard_map/left_grads/pallas_call | solution.py:618
  127.7 0.5 collective-permute-start.23
  128.2 3.4 %right_grads.2 = bf16[2,512,128]{2,1,0:T(8,128)(2,1)S(1)} custom-call(s32[4]{0:T(128)S(1)} %pad_add_fusion.idx_ref, bf16[128,8192]{1,0:T(8,128)(2,1)S(1)} %copy-done, bf16[128,8192]{1,0:T(8,128)(2,1)S(1)} %copy-done, bf16[128,8192]{1,0:T(8,128)(2,1)} %collective-permute-done.refs_2_.refs_3_, bf16[128,8192]{1,0:T(8,128)(2,1)} %collective-permute-done.refs_2_.refs_3_, ...), custom_call_target="tpu_custom_call" | custom-call | flops 1 | bytes 1 | tf_op jit(solution)/shard_map/right_grads/pallas_call | solution.py:672
  131.6 1.6 %collective-permute-start.24 = (bf16[2,512,128]{2,1,0:T(8,128)(2,1)S(1)}, bf16[2,512,128]{2,1,0:T(8,128)(2,1)S(1)}, u32[]{:S(2)}, u32[]{:S(2)}) collective-permute-start(bf16[2,512,128]{2,1,0:T(8,128)(2,1)S(1)} %right_grads.2), channel_id=1, source_target_pairs={{0,1},{1,0},{2,3},{3,2},{4,5},{5,4},{6,7},{7,6},{8,9},{9,8},{10,11... | collective-permute-start | bytes 786440 | tf_op jit(solution)/shard_map/ppermute | solution.py:706
  133.3 0.2 collective-permute-done.23
  133.5 1.4 collective-permute-start.27
  134.9 3.4 %right_grads.3 = bf16[2,512,128]{2,1,0:T(8,128)(2,1)S(1)} custom-call(s32[4]{0:T(128)S(1)} %pad_add_fusion.idx_ref, bf16[128,8192]{1,0:T(8,128)(2,1)S(1)} %copy-done, bf16[128,8192]{1,0:T(8,128)(2,1)S(1)} %copy-done, bf16[128,8192]{1,0:T(8,128)(2,1)} %collective-permute-done.refs_2_.refs_3_, bf16[128,8192]{1,0:T(8,128)(2,1)} %collective-permute-done.refs_2_.refs_3_, ...), custom_call_target="tpu_custom_call" | custom-call | flops 10000000000 | bytes 10000000 | tf_op jit(solution)/shard_map/right_grads/pallas_call | solution.py:672
  138.4 3.0 %collective-permute-done.24 = bf16[2,512,128]{2,1,0:T(8,128)(2,1)S(1)} collective-permute-done((bf16[2,512,128]{2,1,0:T(8,128)(2,1)S(1)}, bf16[2,512,128]{2,1,0:T(8,128)(2,1)S(1)}, u32[]{:S(2)}, u32[]{:S(2)}) %collective-permute-start.24) | collective-permute-done | bytes 262176 | tf_op jit(solution)/shard_map/ppermute | solution.py:706
  141.5 0.7 collective-permute-start.25
  142.2 4.5 %collective-permute-start.26 = (bf16[512,128]{1,0:T(8,128)(2,1)S(1)}, bf16[512,128]{1,0:T(8,128)(2,1)S(1)}, u32[]{:S(2)}, u32[]{:S(2)}) collective-permute-start(bf16[512,128]{1,0:T(8,128)(2,1)S(1)} %get-tuple-element.87), channel_id=1, source_target_pairs={{0,8},{1,12},{2,0},{3,4},{4,9},{5,13},{6,1},{7,5},{8,10},{9,14},{1... | collective-permute-start | bytes 393224 | tf_op jit(solution)/shard_map/ppermute | solution.py:713
  146.7 0.2 reshape.32
  146.9 0.7 copy.8
  147.6 9.4 %collective-permute-done.26 = bf16[512,128]{1,0:T(8,128)(2,1)S(1)} collective-permute-done((bf16[512,128]{1,0:T(8,128)(2,1)S(1)}, bf16[512,128]{1,0:T(8,128)(2,1)S(1)}, u32[]{:S(2)}, u32[]{:S(2)}) %collective-permute-start.26) | collective-permute-done | bytes 131104 | tf_op jit(solution)/shard_map/ppermute | solution.py:713
  157.0 0.7 convert_add_fusion.2
  (48 shorter events, 0.5 us)
Async XLA Ops:
  0.6 6.8 %collective-permute-start = (bf16[128,8192]{1,0:T(8,128)(2,1)}, bf16[128,8192]{1,0:T(8,128)(2,1)}, u32[]{:S(2)}, u32[]{:S(2)}) collective-permute-start(bf16[128,8192]{1,0:T(8,128)(2,1)} %refs_1_.11), channel_id=1, source_target_pairs={{0,4},{4,0},{8,12},{12,8},{1,5},{5,1},{9,13},{13,9},{2,6},{6,2},{1... | collective-permute-start | bytes 6291464 | tf_op jit(solution)/shard_map/ppermute | solution.py:700
  1.7 5.7 %copy-start = (bf16[128,8192]{1,0:T(8,128)(2,1)S(1)}, bf16[128,8192]{1,0:T(8,128)(2,1)}, u32[]{:S(2)}) copy-start(bf16[128,8192]{1,0:T(8,128)(2,1)} %refs_1_.11) | copy-start | bytes 6291460
  4.8 15.3 %collective-permute-start.1 = (bf16[64,4096]{1,0:T(8,128)(2,1)}, bf16[64,4096]{1,0:T(8,128)(2,1)S(1)}, u32[]{:S(2)}, u32[]{:S(2)}) collective-permute-start(bf16[64,4096]{1,0:T(8,128)(2,1)} %get-tuple-element.44), channel_id=1, source_target_pairs={{0,8},{4,12},{8,0},{12,4},{1,9},{5,13},{9,1},{13,5},{2,10},{6,14},... | collective-permute-start | bytes 1572872 | tf_op jit(solution)/shard_map/ppermute | solution.py:703
  18.1 0.9 copy-start.6
  19.1 4.4 %collective-permute-start.7 = (bf16[2,128,1792]{2,1,0:T(8,128)(2,1)}, bf16[2,128,1792]{2,1,0:T(8,128)(2,1)}, u32[]{:S(2)}, u32[]{:S(2)}) collective-permute-start(bf16[2,128,1792]{2,1,0:T(8,128)(2,1)} %bitcast.11), channel_id=1, source_target_pairs={{0,4},{4,0},{8,12},{12,8},{1,5},{5,1},{9,13},{13,9},{2,6},{6,2},{1... | collective-permute-start | bytes 2752520 | tf_op jit(solution)/shard_map/ppermute | solution.py:700
  19.3 15.1 %collective-permute-start.4 = (bf16[64,4096]{1,0:T(8,128)(2,1)}, bf16[64,4096]{1,0:T(8,128)(2,1)}, u32[]{:S(2)}, u32[]{:S(2)}) collective-permute-start(bf16[64,4096]{1,0:T(8,128)(2,1)} %get-tuple-element.51), channel_id=1, source_target_pairs={{0,8},{4,12},{8,0},{12,4},{1,9},{5,13},{9,1},{13,5},{2,10},{6,14},... | collective-permute-start | bytes 1572872 | tf_op jit(solution)/shard_map/ppermute | solution.py:703
  20.1 15.2 %collective-permute-start.2 = (bf16[64,4096]{1,0:T(8,128)(2,1)S(1)}, bf16[64,4096]{1,0:T(8,128)(2,1)S(1)}, u32[]{:S(2)}, u32[]{:S(2)}) collective-permute-start(bf16[64,4096]{1,0:T(8,128)(2,1)S(1)} %collective-permute-done.1.refs_0_.refs_4_), channel_id=1, source_target_pairs={{0,1},{1,0},{2,3},{3,2},{4,5},{5,4},{6,7},{7,6},{8,9},{9,8},{10,11... | collective-permute-start | bytes 1572872 | tf_op jit(solution)/shard_map/ppermute | solution.py:706
  23.5 3.3 %copy-start.10 = (bf16[16,32,128]{2,1,0:T(8,128)(2,1)S(1)}, bf16[16,32,128]{2,1,0:T(8,128)(2,1)}, u32[]{:S(2)}) copy-start(bf16[16,32,128]{2,1,0:T(8,128)(2,1)} %param.10) | copy-start | bytes 393220
  23.5 10.8 %copy-start.9 = (bf16[256,128]{1,0:T(8,128)(2,1)S(1)}, bf16[256,128]{1,0:T(8,128)(2,1)}, u32[]{:S(2)}) copy-start(bf16[256,128]{1,0:T(8,128)(2,1)} %pack_left.1) | copy-start | bytes 196612
  25.2 29.1 %collective-permute-start.9 = (bf16[2,128,1792]{2,1,0:T(8,128)(2,1)S(1)}, bf16[2,128,1792]{2,1,0:T(8,128)(2,1)S(1)}, u32[]{:S(2)}, u32[]{:S(2)}) collective-permute-start(bf16[2,128,1792]{2,1,0:T(8,128)(2,1)S(1)} %fusion.1), channel_id=1, source_target_pairs={{0,8},{4,12},{8,0},{12,4},{1,9},{5,13},{9,1},{13,5},{2,10},{6,14},... | collective-permute-start | bytes 2752520 | tf_op jit(solution)/shard_map/ppermute | solution.py:703
  26.8 2.5 %collective-permute-start.3 = (bf16[16,32,128]{2,1,0:T(8,128)(2,1)S(1)}, bf16[16,32,128]{2,1,0:T(8,128)(2,1)S(1)}, u32[]{:S(2)}, u32[]{:S(2)}) collective-permute-start(bf16[16,32,128]{2,1,0:T(8,128)(2,1)S(1)} %copy-done.10), channel_id=1, source_target_pairs={{0,0},{1,4},{2,8},{3,12},{4,1},{5,5},{6,9},{7,13},{8,2},{9,6},{10,... | collective-permute-start | bytes 393224 | tf_op jit(solution)/shard_map/ppermute | solution.py:713
  27.5 9.5 %collective-permute-start.5 = (bf16[64,4096]{1,0:T(8,128)(2,1)S(1)}, bf16[64,4096]{1,0:T(8,128)(2,1)S(1)}, u32[]{:S(2)}, u32[]{:S(2)}) collective-permute-start(bf16[64,4096]{1,0:T(8,128)(2,1)S(1)} %collective-permute-done.1.refs_0_.refs_4_), channel_id=1, source_target_pairs={{0,4},{4,0},{8,12},{12,8},{1,5},{5,1},{9,13},{13,9},{2,6},{6,2},{1... | collective-permute-start | bytes 1572872 | tf_op jit(solution)/shard_map/ppermute | solution.py:700
  35.3 3.2 %collective-permute-start.6 = (bf16[64,4096]{1,0:T(8,128)(2,1)S(1)}, bf16[64,4096]{1,0:T(8,128)(2,1)S(1)}, u32[]{:S(2)}, u32[]{:S(2)}) collective-permute-start(bf16[64,4096]{1,0:T(8,128)(2,1)S(1)} %collective-permute-done.2.refs_1_.refs_5_), channel_id=1, source_target_pairs={{0,4},{4,0},{8,12},{12,8},{1,5},{5,1},{9,13},{13,9},{2,6},{6,2},{1... | collective-permute-start | bytes 1572872 | tf_op jit(solution)/shard_map/ppermute | solution.py:700
  36.9 12.1 %copy-start.1 = (bf16[64,4096]{1,0:T(8,128)(2,1)}, bf16[64,4096]{1,0:T(8,128)(2,1)S(1)}, u32[]{:S(2)}) copy-start(bf16[64,4096]{1,0:T(8,128)(2,1)S(1)} %collective-permute-done.5.refs_2_.refs_6_) | copy-start | bytes 1572868
  38.5 10.6 %copy-start.3 = (bf16[64,4096]{1,0:T(8,128)(2,1)}, bf16[64,4096]{1,0:T(8,128)(2,1)S(1)}, u32[]{:S(2)}) copy-start(bf16[64,4096]{1,0:T(8,128)(2,1)S(1)} %collective-permute-done.6.refs_3_.refs_7_) | copy-start | bytes 1572868
  49.1 1.0 copy-start.5
  54.4 0.9 copy-start.7
  55.3 6.0 %collective-permute-start.10 = (bf16[2,128,1792]{2,1,0:T(8,128)(2,1)}, bf16[2,128,1792]{2,1,0:T(8,128)(2,1)}, u32[]{:S(2)}, u32[]{:S(2)}) collective-permute-start(bf16[2,128,1792]{2,1,0:T(8,128)(2,1)} %bitcast.14), channel_id=1, source_target_pairs={{0,4},{4,0},{8,12},{12,8},{1,5},{5,1},{9,13},{13,9},{2,6},{6,2},{1... | collective-permute-start | bytes 2752520 | tf_op jit(solution)/shard_map/ppermute | solution.py:700
  55.4 7.7 %copy-start.2 = (bf16[64,4096]{1,0:T(8,128)(2,1)S(1)}, bf16[64,4096]{1,0:T(8,128)(2,1)}, u32[]{:S(2)}) copy-start(bf16[64,4096]{1,0:T(8,128)(2,1)} %copy-done.1) | copy-start | bytes 1572868
  55.4 7.7 %copy-start.4 = (bf16[64,4096]{1,0:T(8,128)(2,1)S(1)}, bf16[64,4096]{1,0:T(8,128)(2,1)}, u32[]{:S(2)}) copy-start(bf16[64,4096]{1,0:T(8,128)(2,1)} %copy-done.3) | copy-start | bytes 1572868
  55.4 20.1 %collective-permute-start.12 = (bf16[1,768,128]{2,1,0:T(8,128)(2,1)S(1)}, bf16[1,768,128]{2,1,0:T(8,128)(2,1)S(1)}, u32[]{:S(2)}, u32[]{:S(2)}) collective-permute-start(bf16[1,768,128]{2,1,0:T(8,128)(2,1)S(1)} %maximum_bitcast_fusion), channel_id=1, source_target_pairs={{0,2},{1,3},{2,0},{3,1},{4,6},{5,7},{6,4},{7,5},{8,10},{9,11},{10,... | collective-permute-start | bytes 589832 | tf_op jit(solution)/shard_map/ppermute | solution.py:706
  59.8 17.4 %collective-permute-start.8 = (bf16[64,4096]{1,0:T(8,128)(2,1)}, bf16[64,4096]{1,0:T(8,128)(2,1)S(1)}, u32[]{:S(2)}, u32[]{:S(2)}) collective-permute-start(bf16[64,4096]{1,0:T(8,128)(2,1)} %collective-permute-done.4.refs_4_.refs_8_), channel_id=1, source_target_pairs={{0,1},{1,0},{2,3},{3,2},{4,5},{5,4},{6,7},{7,6},{8,9},{9,8},{10,11... | collective-permute-start | bytes 1572872 | tf_op jit(solution)/shard_map/ppermute | solution.py:706
  63.0 26.1 %copy-start.8 = (bf16[2,128,1792]{2,1,0:T(8,128)(2,1)S(1)}, bf16[2,128,1792]{2,1,0:T(8,128)(2,1)}, u32[]{:S(2)}) copy-start(bf16[2,128,1792]{2,1,0:T(8,128)(2,1)} %copy-done.7) | copy-start | bytes 2752516
  63.0 22.3 %collective-permute-start.11 = (bf16[2,128,1792]{2,1,0:T(8,128)(2,1)S(1)}, bf16[2,128,1792]{2,1,0:T(8,128)(2,1)S(1)}, u32[]{:S(2)}, u32[]{:S(2)}) collective-permute-start(bf16[2,128,1792]{2,1,0:T(8,128)(2,1)S(1)} %fusion), channel_id=1, source_target_pairs={{0,8},{4,12},{8,0},{12,4},{1,9},{5,13},{9,1},{13,5},{2,10},{6,14},... | collective-permute-start | bytes 2752520 | tf_op jit(solution)/shard_map/ppermute | solution.py:703
  85.3 3.8 %collective-permute-start.13 = (bf16[2,2,128,1792]{3,2,1,0:T(8,128)(2,1)S(1)}, bf16[2,2,128,1792]{3,2,1,0:T(8,128)(2,1)S(1)}, u32[]{:S(2)}, u32[]{:S(2)}) collective-permute-start(bf16[2,2,128,1792]{3,2,1,0:T(8,128)(2,1)S(1)} %get-tuple-element.65), channel_id=1, source_target_pairs={{0,4},{4,0},{8,12},{12,8},{1,5},{5,1},{9,13},{13,9},{2,6},{6,2},{1... | collective-permute-start | bytes 5505032 | tf_op jit(solution)/shard_map/ppermute | solution.py:700
  85.4 12.5 %collective-permute-start.19 = (bf16[2,768,128]{2,1,0:T(8,128)(2,1)S(1)}, bf16[2,768,128]{2,1,0:T(8,128)(2,1)S(1)}, u32[]{:S(2)}, u32[]{:S(2)}) collective-permute-start(bf16[2,768,128]{2,1,0:T(8,128)(2,1)S(1)} %pad_maximum_fusion.1), channel_id=1, source_target_pairs={{0,1},{1,0},{2,3},{3,2},{4,5},{5,4},{6,7},{7,6},{8,9},{9,8},{10,11... | collective-permute-start | bytes 1179656 | tf_op jit(solution)/shard_map/ppermute | solution.py:706
  89.6 3.0 %collective-permute-start.14 = (bf16[128,1792]{1,0:T(8,128)(2,1)S(1)}, bf16[128,1792]{1,0:T(8,128)(2,1)S(1)}, u32[]{:S(2)}, u32[]{:S(2)}) collective-permute-start(bf16[128,1792]{1,0:T(8,128)(2,1)S(1)} %fusion.5.mine_ref), channel_id=1, source_target_pairs={{0,4},{4,0},{8,12},{12,8},{1,5},{5,1},{9,13},{13,9},{2,6},{6,2},{1... | collective-permute-start | bytes 1376264 | tf_op jit(solution)/shard_map/ppermute | solution.py:700
  89.8 19.3 %collective-permute-start.20 = (bf16[128,1792]{1,0:T(8,128)(2,1)S(1)}, bf16[128,1792]{1,0:T(8,128)(2,1)S(1)}, u32[]{:S(2)}, u32[]{:S(2)}) collective-permute-start(bf16[128,1792]{1,0:T(8,128)(2,1)S(1)} %fusion.5.mine_ref), channel_id=1, source_target_pairs={{0,8},{4,12},{8,0},{12,4},{1,9},{5,13},{9,1},{13,5},{2,10},{6,14},... | collective-permute-start | bytes 1376264 | tf_op jit(solution)/shard_map/ppermute | solution.py:703
  90.8 18.6 %collective-permute-start.18 = (bf16[128,1792]{1,0:T(8,128)(2,1)S(1)}, bf16[128,1792]{1,0:T(8,128)(2,1)S(1)}, u32[]{:S(2)}, u32[]{:S(2)}) collective-permute-start(bf16[128,1792]{1,0:T(8,128)(2,1)S(1)} %fusion.3.mine_ref), channel_id=1, source_target_pairs={{0,4},{4,0},{8,12},{12,8},{1,5},{5,1},{9,13},{13,9},{2,6},{6,2},{1... | collective-permute-start | bytes 1376264 | tf_op jit(solution)/shard_map/ppermute | solution.py:700
  90.9 23.7 %collective-permute-start.17 = (bf16[128,1792]{1,0:T(8,128)(2,1)S(1)}, bf16[128,1792]{1,0:T(8,128)(2,1)S(1)}, u32[]{:S(2)}, u32[]{:S(2)}) collective-permute-start(bf16[128,1792]{1,0:T(8,128)(2,1)S(1)} %fusion.3.mine_ref), channel_id=1, source_target_pairs={{0,8},{4,12},{8,0},{12,4},{1,9},{5,13},{9,1},{13,5},{2,10},{6,14},... | collective-permute-start | bytes 1376264 | tf_op jit(solution)/shard_map/ppermute | solution.py:703
  98.0 5.9 %collective-permute-start.15 = (bf16[64,4096]{1,0:T(8,128)(2,1)}, bf16[64,4096]{1,0:T(8,128)(2,1)S(1)}, u32[]{:S(2)}, u32[]{:S(2)}) collective-permute-start(bf16[64,4096]{1,0:T(8,128)(2,1)} %collective-permute-done.4.refs_4_.refs_8_), channel_id=1, source_target_pairs={{0,4},{4,0},{8,12},{12,8},{1,5},{5,1},{9,13},{13,9},{2,6},{6,2},{1... | collective-permute-start | bytes 1572872 | tf_op jit(solution)/shard_map/ppermute | solution.py:700
  98.2 5.7 %collective-permute-start.16 = (bf16[64,4096]{1,0:T(8,128)(2,1)S(1)}, bf16[64,4096]{1,0:T(8,128)(2,1)S(1)}, u32[]{:S(2)}, u32[]{:S(2)}) collective-permute-start(bf16[64,4096]{1,0:T(8,128)(2,1)S(1)} %collective-permute-done.8.refs_5_.refs_9_), channel_id=1, source_target_pairs={{0,4},{4,0},{8,12},{12,8},{1,5},{5,1},{9,13},{13,9},{2,6},{6,2},{1... | collective-permute-start | bytes 1572872 | tf_op jit(solution)/shard_map/ppermute | solution.py:700
  109.1 5.9 %collective-permute-start.22 = (bf16[128,1792]{1,0:T(8,128)(2,1)S(1)}, bf16[128,1792]{1,0:T(8,128)(2,1)S(1)}, u32[]{:S(2)}, u32[]{:S(2)}) collective-permute-start(bf16[128,1792]{1,0:T(8,128)(2,1)S(1)} %collective-permute-done.20.refs_1_), channel_id=1, source_target_pairs={{0,4},{4,0},{8,12},{12,8},{1,5},{5,1},{9,13},{13,9},{2,6},{6,2},{1... | collective-permute-start | bytes 1376264 | tf_op jit(solution)/shard_map/ppermute | solution.py:700
  114.6 1.9 %collective-permute-start.21 = (bf16[128,1792]{1,0:T(8,128)(2,1)S(1)}, bf16[128,1792]{1,0:T(8,128)(2,1)S(1)}, u32[]{:S(2)}, u32[]{:S(2)}) collective-permute-start(bf16[128,1792]{1,0:T(8,128)(2,1)S(1)} %collective-permute-done.17.refs_0_), channel_id=1, source_target_pairs={{0,4},{4,0},{8,12},{12,8},{1,5},{5,1},{9,13},{13,9},{2,6},{6,2},{1... | collective-permute-start | bytes 1376264 | tf_op jit(solution)/shard_map/ppermute | solution.py:700
  127.7 5.8 %collective-permute-start.23 = (bf16[2,256,128]{2,1,0:T(8,128)(2,1)S(1)}, bf16[2,256,128]{2,1,0:T(8,128)(2,1)S(1)}, u32[]{:S(2)}, u32[]{:S(2)}) collective-permute-start(bf16[2,256,128]{2,1,0:T(8,128)(2,1)S(1)} %slice.51), channel_id=1, source_target_pairs={{0,1},{1,0},{2,3},{3,2},{4,5},{5,4},{6,7},{7,6},{8,9},{9,8},{10,11... | collective-permute-start | bytes 393224 | tf_op jit(solution)/shard_map/ppermute | solution.py:706
  131.6 9.7 %collective-permute-start.24 = (bf16[2,512,128]{2,1,0:T(8,128)(2,1)S(1)}, bf16[2,512,128]{2,1,0:T(8,128)(2,1)S(1)}, u32[]{:S(2)}, u32[]{:S(2)}) collective-permute-start(bf16[2,512,128]{2,1,0:T(8,128)(2,1)S(1)} %right_grads.2), channel_id=1, source_target_pairs={{0,1},{1,0},{2,3},{3,2},{4,5},{5,4},{6,7},{7,6},{8,9},{9,8},{10,11... | collective-permute-start | bytes 786440 | tf_op jit(solution)/shard_map/ppermute | solution.py:706
  133.5 13.1 %collective-permute-start.27 = (bf16[256,128]{1,0:T(8,128)(2,1)S(1)}, bf16[256,128]{1,0:T(8,128)(2,1)S(1)}, u32[]{:S(2)}, u32[]{:S(2)}) collective-permute-start(bf16[256,128]{1,0:T(8,128)(2,1)S(1)} %slice_bitcast_fusion.6), channel_id=1, source_target_pairs={{0,2},{1,3},{2,0},{3,1},{4,6},{5,7},{6,4},{7,5},{8,10},{9,11},{10,... | collective-permute-start | bytes 196616 | tf_op jit(solution)/shard_map/ppermute | solution.py:706
  141.5 6.1 %collective-permute-start.25 = (bf16[512,128]{1,0:T(8,128)(2,1)S(1)}, bf16[512,128]{1,0:T(8,128)(2,1)S(1)}, u32[]{:S(2)}, u32[]{:S(2)}) collective-permute-start(bf16[512,128]{1,0:T(8,128)(2,1)S(1)} %get-tuple-element.86), channel_id=1, source_target_pairs={{0,0},{1,4},{2,8},{3,12},{4,1},{5,5},{6,9},{7,13},{8,2},{9,6},{10,... | collective-permute-start | bytes 393224 | tf_op jit(solution)/shard_map/ppermute | solution.py:713
  142.2 14.8 %collective-permute-start.26 = (bf16[512,128]{1,0:T(8,128)(2,1)S(1)}, bf16[512,128]{1,0:T(8,128)(2,1)S(1)}, u32[]{:S(2)}, u32[]{:S(2)}) collective-permute-start(bf16[512,128]{1,0:T(8,128)(2,1)S(1)} %get-tuple-element.87), channel_id=1, source_target_pairs={{0,8},{1,12},{2,0},{3,4},{4,9},{5,13},{6,1},{7,5},{8,10},{9,14},{1... | collective-permute-start | bytes 393224 | tf_op jit(solution)/shard_map/ppermute | solution.py:713

commit v19 on v18

--- a/solution.py
+++ b/solution.py
@@ -753,17 +753,14 @@
     late_order = after(scalars(other_block), sums)
     mine, other = products(late_pieces, late_order, gate_weight, up_weight, 0, part)
     near = swap(after(other[0], got_early))
-    more = along(after(factors, mine), 2)
-    late_partner = along(after(late_first, mine), 1)
     sums = add(mine[0], near).astype(BF16)
     got = across(sums)
     mine_order = after(scalars(mine_block), sums)
     kept, other = products(
         own_pieces + late_pieces, mine_order, gate_weight, up_weight, 0, part
     )
-    near_kept = swap(after(other, got, more, late_partner))
-    factors = jnp.concatenate([factors, after(more, kept)], axis=0)
-    more = along(factors, 1)
+    near_kept = swap(after(other, got))
+    more = along(after(factors, kept), 2)
 
     def activate(u, term):
         total = add(kept[u], near_kept[u], term)
@@ -775,6 +772,9 @@
     hidden0 = activate(0, after(got, hidden1))
     got0 = across(hidden0)
     near0 = swap(hidden0)
+    factors = jnp.concatenate([factors, after(more, hidden0)], axis=0)
+    more = along(factors, 1)
+    late_partner = along(after(late_first, hidden0), 1)
     target1 = target_part(1.0, [], hidden1, after(near1, hidden0), down_weight, chip)
     factors = jnp.concatenate([factors, after(more, target1)], axis=0)
     mixed0, rest0, left_diag = student_part(

time: 159 us -> 180 us (1.13)
  waiting for transfers between devices: 39 us -> 57.1 us
  starting transfers between devices: 30.2 us -> 33.4 us
    ppermute x7, waiting for transfers between devices: 5.79 us -> 24.1 us  [along(): lax.ppermute(value, 'tensor', [(i, i ^ bit) for i in range(tensor_count)])]
    ppermute x6, starting transfers between devices: 6.87 us -> 9.34 us  [across(): return lax.ppermute(value, 'fsdp', [(i, i ^ 2) for i in range(fsdp_count)])]
  transfers between devices with their start and end apart: 28 -> 28, of which waited for: 12 -> 14; matrix products, arithmetic and copies ran while one was open for 4% -> 3% of each run, Pallas kernels for 42% -> 37%
where the time goes in v19:
time: 180 us; the launch traced here: 179 us
  Pallas kernels  77.4 us (43%)
  waiting for transfers between devices  57.1 us (32%)
  starting transfers between devices  33.4 us (19%)
  other arithmetic  6.18 us (3%)
  local copies, waits for them, and re-layouts  3.97 us (2%)
    pallas_call x3, Pallas kernels, products(): pl.pallas_call(functools.partial(products_kernel, sets), grid_spec=pltpu....  33.7 us
    ppermute x7, waiting for transfers between devices, along(): lax.ppermute(value, 'tensor', [(i, i ^ bit) for i in range(tensor_count)])  24.1 us
    ppermute x6, waiting for transfers between devices, across(): return lax.ppermute(value, 'fsdp', [(i, i ^ 2) for i in range(fsdp_count)])  17.8 us
    ppermute x7, starting transfers between devices, along(): lax.ppermute(value, 'tensor', [(i, i ^ bit) for i in range(tensor_count)])  12.2 us
    pallas_call x1, Pallas kernels, left_grads(): pl.pallas_call(functools.partial(left_kernel, chunks, scale), grid_spec=p...  11.1 us
    pallas_call x2, Pallas kernels, student_part(): pl.pallas_call(functools.partial(student_kernel, steps, bool(late), tenso...  10.6 us
    pallas_call x2, Pallas kernels, target_part(): pl.pallas_call(functools.partial(target_kernel, sign), grid_spec=pltpu.Pr...  10.4 us
    ppermute x6, starting transfers between devices, across(): return lax.ppermute(value, 'fsdp', [(i, i ^ 2) for i in range(fsdp_count)])  9.34 us
  transfers between devices with their start and end apart: 28, of which 14 were waited for; matrix products, arithmetic and copies ran while one was open for 3% of the time, Pallas kernels for 37%

profile of v19, /device:TPU:0, one launch (start us, length us, event | category | flops | bytes accessed | tf_op | source)
XLA Modules:
  0.0 178.9 jit_solution(12168128638492028603)
XLA Ops:
  0.6 0.5 collective-permute-start
  1.1 0.6 pad_add_fusion.1.idx_ref
  1.7 3.0 %cut_tokens.1 = (bf16[64,4096]{1,0:T(8,128)(2,1)}, bf16[64,4096]{1,0:T(8,128)(2,1)}) custom-call(s32[3]{0:T(128)} %pad_add_fusion.1.idx_ref, bf16[128,8192]{1,0:T(8,128)(2,1)} %refs_1_.11, bf16[128,8192]{1,0:T(8,128)(2,1)} %refs_1_.11), custom_call_target="tpu_custom_call" | custom-call | flops 1 | bytes 1 | tf_op jit(solution)/shard_map/cut_tokens/pallas_call | solution.py:313
  4.8 2.5 %collective-permute-start.1 = (bf16[64,4096]{1,0:T(8,128)(2,1)}, bf16[64,4096]{1,0:T(8,128)(2,1)S(1)}, u32[]{:S(2)}, u32[]{:S(2)}) collective-permute-start(bf16[64,4096]{1,0:T(8,128)(2,1)} %get-tuple-element.44), channel_id=1, source_target_pairs={{0,8},{4,12},{8,0},{12,4},{1,9},{5,13},{9,1},{13,5},{2,10},{6,14},... | collective-permute-start | bytes 1572872 | tf_op jit(solution)/shard_map/ppermute | solution.py:703
  7.3 0.1 concatenate.25.idx_ref
  7.4 10.8 %gate_up_products.3 = (bf16[1,2,128,1792]{3,2,1,0:T(8,128)(2,1)S(1)}, bf16[1,2,128,1792]{3,2,1,0:T(8,128)(2,1)}) custom-call(s32[5]{0:T(128)S(1)} %concatenate.25.idx_ref, bf16[128,8192]{1,0:T(8,128)(2,1)S(1)} %copy-done, bf16[128,8192]{1,0:T(8,128)(2,1)S(1)} %copy-done, bf16[128,8192]{1,0:T(8,128)(2,1)} %collective-permute-done.refs_2_.refs_3_, ...), custom_call_target="tpu_custom_call" | custom-call | flops 1 | bytes 1 | tf_op jit(solution)/shard_map/gate_up_products/pallas_call | solution.py:374
  18.1 0.9 copy-done.5
  19.1 0.2 collective-permute-start.7
  19.3 0.7 collective-permute-start.4
  20.0 0.1 collective-permute-done.1.refs_0_.refs_4_
  20.1 1.8 %collective-permute-start.2 = (bf16[64,4096]{1,0:T(8,128)(2,1)S(1)}, bf16[64,4096]{1,0:T(8,128)(2,1)S(1)}, u32[]{:S(2)}, u32[]{:S(2)}) collective-permute-start(bf16[64,4096]{1,0:T(8,128)(2,1)S(1)} %collective-permute-done.1.refs_0_.refs_4_), channel_id=1, source_target_pairs={{0,1},{1,0},{2,3},{3,2},{4,5},{5,4},{6,7},{7,6},{8,9},{9,8},{10,11... | collective-permute-start | bytes 1572872 | tf_op jit(solution)/shard_map/ppermute | solution.py:706
  21.9 1.6 pack_left.1
  23.5 1.7 fusion.1
  25.2 1.6 collective-permute-start.8
  26.8 0.7 collective-permute-start.3
  27.5 1.9 %collective-permute-start.5 = (bf16[64,4096]{1,0:T(8,128)(2,1)S(1)}, bf16[64,4096]{1,0:T(8,128)(2,1)S(1)}, u32[]{:S(2)}, u32[]{:S(2)}) collective-permute-start(bf16[64,4096]{1,0:T(8,128)(2,1)S(1)} %collective-permute-done.1.refs_0_.refs_4_), channel_id=1, source_target_pairs={{0,4},{4,0},{8,12},{12,8},{1,5},{5,1},{9,13},{13,9},{2,6},{6,2},{1... | collective-permute-start | bytes 1572872 | tf_op jit(solution)/shard_map/ppermute | solution.py:700
  29.3 5.0 %collective-permute-done.4.refs_4_.refs_8_ = bf16[64,4096]{1,0:T(8,128)(2,1)} collective-permute-done((bf16[64,4096]{1,0:T(8,128)(2,1)}, bf16[64,4096]{1,0:T(8,128)(2,1)}, u32[]{:S(2)}, u32[]{:S(2)}) %collective-permute-start.4) | collective-permute-done | bytes 524320 | tf_op jit(solution)/shard_map/ppermute | solution.py:703
  34.4 0.9 collective-permute-done.2.refs_1_.refs_5_
  35.3 1.6 collective-permute-start.6
  36.9 1.5 collective-permute-done.6.refs_3_.refs_7_
  38.5 10.6 %gate_up_products.4 = (bf16[1,2,128,1792]{3,2,1,0:T(8,128)(2,1)S(1)}, bf16[1,2,128,1792]{3,2,1,0:T(8,128)(2,1)}) custom-call(s32[5]{0:T(128)S(1)} %concatenate.25.idx_ref, bf16[64,4096]{1,0:T(8,128)(2,1)S(1)} %collective-permute-done.1.refs_0_.refs_4_, bf16[64,4096]{1,0:T(8,128)(2,1)S(1)} %collective-permute-done.2.refs_1_.refs_5_, ...), custom_call_target="tpu_custom_call" | custom-call | flops 1 | bytes 1 | tf_op jit(solution)/shard_map/gate_up_products/pallas_call | solution.py:374
  49.1 0.9 copy-done.6
  50.0 4.4 %collective-permute-done.8 = bf16[2,128,1792]{2,1,0:T(8,128)(2,1)S(1)} collective-permute-done((bf16[2,128,1792]{2,1,0:T(8,128)(2,1)S(1)}, bf16[2,128,1792]{2,1,0:T(8,128)(2,1)S(1)}, u32[]{:S(2)}, u32[]{:S(2)}) %collective-permute-start.8) | collective-permute-done | bytes 917536 | tf_op jit(solution)/shard_map/ppermute | solution.py:703
  54.4 0.9 copy-done.7
  55.3 0.1 concatenate.27.idx_ref
  55.4 2.7 %collective-permute-done.9 = bf16[2,128,1792]{2,1,0:T(8,128)(2,1)} collective-permute-done((bf16[2,128,1792]{2,1,0:T(8,128)(2,1)}, bf16[2,128,1792]{2,1,0:T(8,128)(2,1)}, u32[]{:S(2)}, u32[]{:S(2)}) %collective-permute-start.9) | collective-permute-done | bytes 917536 | tf_op jit(solution)/shard_map/ppermute | solution.py:700
  58.1 1.7 fusion
  59.8 2.5 %collective-permute-start.10 = (bf16[2,128,1792]{2,1,0:T(8,128)(2,1)S(1)}, bf16[2,128,1792]{2,1,0:T(8,128)(2,1)S(1)}, u32[]{:S(2)}, u32[]{:S(2)}) collective-permute-start(bf16[2,128,1792]{2,1,0:T(8,128)(2,1)S(1)} %fusion), channel_id=1, source_target_pairs={{0,8},{4,12},{8,0},{12,4},{1,9},{5,13},{9,1},{13,5},{2,10},{6,14},... | collective-permute-start | bytes 2752520 | tf_op jit(solution)/shard_map/ppermute | solution.py:703
  62.4 12.3 %gate_up_products.5 = (bf16[2,2,128,1792]{3,2,1,0:T(8,128)(2,1)S(1)}, bf16[2,2,128,1792]{3,2,1,0:T(8,128)(2,1)S(1)}) custom-call(s32[5]{0:T(128)S(1)} %concatenate.27.idx_ref, bf16[128,8192]{1,0:T(8,128)(2,1)S(1)} %copy-done, bf16[128,8192]{1,0:T(8,128)(2,1)S(1)} %copy-done, bf16[128,8192]{1,0:T(8,128)(2,1)} %collective-permute-done.refs_2_.refs_3_, ...), custom_call_target="tpu_custom_call" | custom-call | flops 10000000000 | bytes 10000000 | tf_op jit(solution)/shard_map/gate_up_products/pallas_call | solution.py:374
  74.7 8.3 %collective-permute-done.10 = bf16[2,128,1792]{2,1,0:T(8,128)(2,1)S(1)} collective-permute-done((bf16[2,128,1792]{2,1,0:T(8,128)(2,1)S(1)}, bf16[2,128,1792]{2,1,0:T(8,128)(2,1)S(1)}, u32[]{:S(2)}, u32[]{:S(2)}) %collective-permute-start.10) | collective-permute-done | bytes 917536 | tf_op jit(solution)/shard_map/ppermute | solution.py:703
  83.0 3.6 %collective-permute-start.18 = (bf16[1,768,128]{2,1,0:T(8,128)(2,1)S(1)}, bf16[1,768,128]{2,1,0:T(8,128)(2,1)S(1)}, u32[]{:S(2)}, u32[]{:S(2)}) collective-permute-start(bf16[1,768,128]{2,1,0:T(8,128)(2,1)S(1)} %maximum_bitcast_fusion), channel_id=1, source_target_pairs={{0,2},{1,3},{2,0},{3,1},{4,6},{5,7},{6,4},{7,5},{8,10},{9,11},{10,... | collective-permute-start | bytes 589832 | tf_op jit(solution)/shard_map/ppermute | solution.py:706
  86.6 0.2 collective-permute-done.11
  86.8 0.3 bitcast_add_fusion
  87.1 0.3 fusion.5.mine_ref
  87.4 0.2 collective-permute-start.13
  87.6 0.3 bitcast_add_fusion.1
  87.9 0.3 fusion.3.mine_ref
  88.2 8.2 %collective-permute-done.18 = bf16[1,768,128]{2,1,0:T(8,128)(2,1)S(1)} collective-permute-done((bf16[1,768,128]{2,1,0:T(8,128)(2,1)S(1)}, bf16[1,768,128]{2,1,0:T(8,128)(2,1)S(1)}, u32[]{:S(2)}, u32[]{:S(2)}) %collective-permute-start.18) | collective-permute-done | bytes 196640 | tf_op jit(solution)/shard_map/ppermute | solution.py:706
  96.4 0.8 collective-permute-start.19
  97.2 1.3 collective-permute-start.12
  98.6 0.8 collective-permute-start.20
  99.4 1.2 collective-permute-start.16
  100.6 5.2 %target_part.2.refs_11_ = f32[256,2048]{1,0:T(8,128)S(1)} custom-call(s32[1]{0:T(128)} %bitcast.2.idx_ref, bf16[128,1792]{1,0:T(8,128)(2,1)S(1)} %fusion.5.mine_ref, bf16[128,1792]{1,0:T(8,128)(2,1)S(1)} %collective-permute-done.13.near_ref, bf16[3584,2048]{1,0:T(8,128)(2,1)} %refs_4_.5), custom_call_target="tpu_custom_call" | custom-call | flops 1 | bytes 1 | tf_op jit(solution)/shard_map/target_part/pallas_call | solution.py:412
  105.8 2.6 %collective-permute-done.19 = bf16[2,768,128]{2,1,0:T(8,128)(2,1)S(1)} collective-permute-done((bf16[2,768,128]{2,1,0:T(8,128)(2,1)S(1)}, bf16[2,768,128]{2,1,0:T(8,128)(2,1)S(1)}, u32[]{:S(2)}, u32[]{:S(2)}) %collective-permute-start.19) | collective-permute-done | bytes 393248 | tf_op jit(solution)/shard_map/ppermute | solution.py:706
  108.6 10.1 %collective-permute-done.12.refs_5_.refs_9_ = bf16[64,4096]{1,0:T(8,128)(2,1)S(1)} collective-permute-done((bf16[64,4096]{1,0:T(8,128)(2,1)}, bf16[64,4096]{1,0:T(8,128)(2,1)S(1)}, u32[]{:S(2)}, u32[]{:S(2)}) %collective-permute-start.12) | collective-permute-done | bytes 524320 | tf_op jit(solution)/shard_map/ppermute | solution.py:706
  118.7 5.3 %student_part.2 = (bf16[8,256,256]{2,1,0:T(8,128)(2,1)S(1)}, f32[256,2048]{1,0:T(8,128)S(1)}, bf16[8,256,256]{2,1,0:T(8,128)(2,1)S(1)}) custom-call(s32[4]{0:T(128)S(1)} %pad_add_fusion.idx_ref, bf16[128,8192]{1,0:T(8,128)(2,1)S(1)} %copy-done, bf16[128,8192]{1,0:T(8,128)(2,1)S(1)} %copy-done, bf16[128,8192]{1,0:T(8,128)(2,1)} %collective-permute-done.refs_2_.refs_3_, ...), custom_call_target="tpu_custom_call" | custom-call | flops 10000000000 | bytes 10000000 | tf_op jit(solution)/shard_map/student_part/pallas_call | solution.py:550
  124.0 5.3 %student_part.3 = (bf16[8,256,256]{2,1,0:T(8,128)(2,1)S(1)}, f32[256,2048]{1,0:T(8,128)S(1)}) custom-call(s32[4]{0:T(128)S(1)} %pad_add_fusion.idx_ref, bf16[64,4096]{1,0:T(8,128)(2,1)S(1)} %collective-permute-done.1.refs_0_.refs_4_, bf16[64,4096]{1,0:T(8,128)(2,1)S(1)} %collective-permute-done.2.refs_1_.refs_5_, bf16[64,4096]{1,0:T(8,128)(2,1)S(1)} %copy-done.2, ...), custom_call_target="tpu_custom_call" | custom-call | flops 10000000000 | bytes 10000000 | tf_op jit(solution)/shard_map/student_part/pallas_call | solution.py:550
  129.3 0.6 collective-permute-start.22
  129.9 5.2 %target_part.3.refs_5_ = f32[256,2048]{1,0:T(8,128)S(1)} custom-call(s32[1]{0:T(128)} %bitcast.2.idx_ref, bf16[128,1792]{1,0:T(8,128)(2,1)S(1)} %fusion.3.mine_ref, bf16[128,1792]{1,0:T(8,128)(2,1)S(1)} %collective-permute-done.17.near_ref, bf16[3584,2048]{1,0:T(8,128)(2,1)} %refs_4_.5, f32[256,2048]{1,0:T(8,128)S(1)} %get-tuple-element.78.refs_0_), custom_call_target="tpu_custom_call" | custom-call | flops 1 | bytes 1 | tf_op jit(solution)/shard_map/target_part/pallas_call | solution.py:412
  135.1 0.1 collective-permute-start.21
  135.2 1.8 collective-permute-done.21.refs_2_
  137.0 11.1 %left_grads.1 = (bf16[4,256,128]{2,1,0:T(8,128)(2,1)S(1)}, bf16[8,256,512]{2,1,0:T(8,128)(2,1)S(1)}) custom-call(s32[4]{0:T(128)S(1)} %pad_add_fusion.idx_ref, bf16[128,1792]{1,0:T(8,128)(2,1)S(1)} %collective-permute-done.16.refs_0_, bf16[128,1792]{1,0:T(8,128)(2,1)S(1)} %collective-permute-done.20.refs_1_, ...), custom_call_target="tpu_custom_call" | custom-call | flops 1 | bytes 1 | tf_op jit(solution)/shard_map/left_grads/pallas_call | solution.py:618
  148.2 0.9 collective-permute-start.23
  149.1 3.4 %right_grads.2 = bf16[2,512,128]{2,1,0:T(8,128)(2,1)S(1)} custom-call(s32[4]{0:T(128)S(1)} %pad_add_fusion.idx_ref, bf16[128,8192]{1,0:T(8,128)(2,1)S(1)} %copy-done, bf16[128,8192]{1,0:T(8,128)(2,1)S(1)} %copy-done, bf16[128,8192]{1,0:T(8,128)(2,1)} %collective-permute-done.refs_2_.refs_3_, bf16[128,8192]{1,0:T(8,128)(2,1)} %collective-permute-done.refs_2_.refs_3_, ...), custom_call_target="tpu_custom_call" | custom-call | flops 1 | bytes 1 | tf_op jit(solution)/shard_map/right_grads/pallas_call | solution.py:672
  152.5 1.2 collective-permute-start.24
  153.8 2.6 %collective-permute-start.27 = (bf16[256,128]{1,0:T(8,128)(2,1)S(1)}, bf16[256,128]{1,0:T(8,128)(2,1)S(1)}, u32[]{:S(2)}, u32[]{:S(2)}) collective-permute-start(bf16[256,128]{1,0:T(8,128)(2,1)S(1)} %slice_bitcast_fusion.6), channel_id=1, source_target_pairs={{0,2},{1,3},{2,0},{3,1},{4,6},{5,7},{6,4},{7,5},{8,10},{9,11},{10,... | collective-permute-start | bytes 196616 | tf_op jit(solution)/shard_map/ppermute | solution.py:706
  156.4 3.4 %right_grads.3 = bf16[2,512,128]{2,1,0:T(8,128)(2,1)S(1)} custom-call(s32[4]{0:T(128)S(1)} %pad_add_fusion.idx_ref, bf16[128,8192]{1,0:T(8,128)(2,1)S(1)} %copy-done, bf16[128,8192]{1,0:T(8,128)(2,1)S(1)} %copy-done, bf16[128,8192]{1,0:T(8,128)(2,1)} %collective-permute-done.refs_2_.refs_3_, bf16[128,8192]{1,0:T(8,128)(2,1)} %collective-permute-done.refs_2_.refs_3_, ...), custom_call_target="tpu_custom_call" | custom-call | flops 10000000000 | bytes 10000000 | tf_op jit(solution)/shard_map/right_grads/pallas_call | solution.py:672
  159.8 2.2 %collective-permute-done.24 = bf16[2,512,128]{2,1,0:T(8,128)(2,1)S(1)} collective-permute-done((bf16[2,512,128]{2,1,0:T(8,128)(2,1)S(1)}, bf16[2,512,128]{2,1,0:T(8,128)(2,1)S(1)}, u32[]{:S(2)}, u32[]{:S(2)}) %collective-permute-start.24) | collective-permute-done | bytes 262176 | tf_op jit(solution)/shard_map/ppermute | solution.py:706
  162.2 0.7 collective-permute-start.25
  162.8 5.4 %collective-permute-start.26 = (bf16[512,128]{1,0:T(8,128)(2,1)S(1)}, bf16[512,128]{1,0:T(8,128)(2,1)S(1)}, u32[]{:S(2)}, u32[]{:S(2)}) collective-permute-start(bf16[512,128]{1,0:T(8,128)(2,1)S(1)} %get-tuple-element.87), channel_id=1, source_target_pairs={{0,8},{1,12},{2,0},{3,4},{4,9},{5,13},{6,1},{7,5},{8,10},{9,14},{1... | collective-permute-start | bytes 393224 | tf_op jit(solution)/shard_map/ppermute | solution.py:713
  168.3 0.2 reshape.32
  168.5 0.7 copy.8
  169.2 9.0 %collective-permute-done.26 = bf16[512,128]{1,0:T(8,128)(2,1)S(1)} collective-permute-done((bf16[512,128]{1,0:T(8,128)(2,1)S(1)}, bf16[512,128]{1,0:T(8,128)(2,1)S(1)}, u32[]{:S(2)}, u32[]{:S(2)}) %collective-permute-start.26) | collective-permute-done | bytes 131104 | tf_op jit(solution)/shard_map/ppermute | solution.py:713
  178.2 0.7 convert_add_fusion.2
  (48 shorter events, 0.5 us)
Async XLA Ops:
  0.6 6.8 %collective-permute-start = (bf16[128,8192]{1,0:T(8,128)(2,1)}, bf16[128,8192]{1,0:T(8,128)(2,1)}, u32[]{:S(2)}, u32[]{:S(2)}) collective-permute-start(bf16[128,8192]{1,0:T(8,128)(2,1)} %refs_1_.11), channel_id=1, source_target_pairs={{0,4},{4,0},{8,12},{12,8},{1,5},{5,1},{9,13},{13,9},{2,6},{6,2},{1... | collective-permute-start | bytes 6291464 | tf_op jit(solution)/shard_map/ppermute | solution.py:700
  1.7 5.7 %copy-start = (bf16[128,8192]{1,0:T(8,128)(2,1)S(1)}, bf16[128,8192]{1,0:T(8,128)(2,1)}, u32[]{:S(2)}) copy-start(bf16[128,8192]{1,0:T(8,128)(2,1)} %refs_1_.11) | copy-start | bytes 6291460
  4.8 15.3 %collective-permute-start.1 = (bf16[64,4096]{1,0:T(8,128)(2,1)}, bf16[64,4096]{1,0:T(8,128)(2,1)S(1)}, u32[]{:S(2)}, u32[]{:S(2)}) collective-permute-start(bf16[64,4096]{1,0:T(8,128)(2,1)} %get-tuple-element.44), channel_id=1, source_target_pairs={{0,8},{4,12},{8,0},{12,4},{1,9},{5,13},{9,1},{13,5},{2,10},{6,14},... | collective-permute-start | bytes 1572872 | tf_op jit(solution)/shard_map/ppermute | solution.py:703
  18.1 0.9 copy-start.5
  19.1 4.4 %collective-permute-start.7 = (bf16[2,128,1792]{2,1,0:T(8,128)(2,1)}, bf16[2,128,1792]{2,1,0:T(8,128)(2,1)}, u32[]{:S(2)}, u32[]{:S(2)}) collective-permute-start(bf16[2,128,1792]{2,1,0:T(8,128)(2,1)} %bitcast.12), channel_id=1, source_target_pairs={{0,4},{4,0},{8,12},{12,8},{1,5},{5,1},{9,13},{13,9},{2,6},{6,2},{1... | collective-permute-start | bytes 2752520 | tf_op jit(solution)/shard_map/ppermute | solution.py:700
  19.3 15.1 %collective-permute-start.4 = (bf16[64,4096]{1,0:T(8,128)(2,1)}, bf16[64,4096]{1,0:T(8,128)(2,1)}, u32[]{:S(2)}, u32[]{:S(2)}) collective-permute-start(bf16[64,4096]{1,0:T(8,128)(2,1)} %get-tuple-element.51), channel_id=1, source_target_pairs={{0,8},{4,12},{8,0},{12,4},{1,9},{5,13},{9,1},{13,5},{2,10},{6,14},... | collective-permute-start | bytes 1572872 | tf_op jit(solution)/shard_map/ppermute | solution.py:703
  20.1 15.2 %collective-permute-start.2 = (bf16[64,4096]{1,0:T(8,128)(2,1)S(1)}, bf16[64,4096]{1,0:T(8,128)(2,1)S(1)}, u32[]{:S(2)}, u32[]{:S(2)}) collective-permute-start(bf16[64,4096]{1,0:T(8,128)(2,1)S(1)} %collective-permute-done.1.refs_0_.refs_4_), channel_id=1, source_target_pairs={{0,1},{1,0},{2,3},{3,2},{4,5},{5,4},{6,7},{7,6},{8,9},{9,8},{10,11... | collective-permute-start | bytes 1572872 | tf_op jit(solution)/shard_map/ppermute | solution.py:706
  23.5 3.3 %copy-start.10 = (bf16[16,32,128]{2,1,0:T(8,128)(2,1)S(1)}, bf16[16,32,128]{2,1,0:T(8,128)(2,1)}, u32[]{:S(2)}) copy-start(bf16[16,32,128]{2,1,0:T(8,128)(2,1)} %param.10) | copy-start | bytes 393220
  23.5 10.8 %copy-start.9 = (bf16[256,128]{1,0:T(8,128)(2,1)S(1)}, bf16[256,128]{1,0:T(8,128)(2,1)}, u32[]{:S(2)}) copy-start(bf16[256,128]{1,0:T(8,128)(2,1)} %pack_left.1) | copy-start | bytes 196612
  25.2 29.1 %collective-permute-start.8 = (bf16[2,128,1792]{2,1,0:T(8,128)(2,1)S(1)}, bf16[2,128,1792]{2,1,0:T(8,128)(2,1)S(1)}, u32[]{:S(2)}, u32[]{:S(2)}) collective-permute-start(bf16[2,128,1792]{2,1,0:T(8,128)(2,1)S(1)} %fusion.1), channel_id=1, source_target_pairs={{0,8},{4,12},{8,0},{12,4},{1,9},{5,13},{9,1},{13,5},{2,10},{6,14},... | collective-permute-start | bytes 2752520 | tf_op jit(solution)/shard_map/ppermute | solution.py:703
  26.8 2.5 %collective-permute-start.3 = (bf16[16,32,128]{2,1,0:T(8,128)(2,1)S(1)}, bf16[16,32,128]{2,1,0:T(8,128)(2,1)S(1)}, u32[]{:S(2)}, u32[]{:S(2)}) collective-permute-start(bf16[16,32,128]{2,1,0:T(8,128)(2,1)S(1)} %copy-done.10), channel_id=1, source_target_pairs={{0,0},{1,4},{2,8},{3,12},{4,1},{5,5},{6,9},{7,13},{8,2},{9,6},{10,... | collective-permute-start | bytes 393224 | tf_op jit(solution)/shard_map/ppermute | solution.py:713
  27.5 9.5 %collective-permute-start.5 = (bf16[64,4096]{1,0:T(8,128)(2,1)S(1)}, bf16[64,4096]{1,0:T(8,128)(2,1)S(1)}, u32[]{:S(2)}, u32[]{:S(2)}) collective-permute-start(bf16[64,4096]{1,0:T(8,128)(2,1)S(1)} %collective-permute-done.1.refs_0_.refs_4_), channel_id=1, source_target_pairs={{0,4},{4,0},{8,12},{12,8},{1,5},{5,1},{9,13},{13,9},{2,6},{6,2},{1... | collective-permute-start | bytes 1572872 | tf_op jit(solution)/shard_map/ppermute | solution.py:700
  35.3 3.2 %collective-permute-start.6 = (bf16[64,4096]{1,0:T(8,128)(2,1)S(1)}, bf16[64,4096]{1,0:T(8,128)(2,1)S(1)}, u32[]{:S(2)}, u32[]{:S(2)}) collective-permute-start(bf16[64,4096]{1,0:T(8,128)(2,1)S(1)} %collective-permute-done.2.refs_1_.refs_5_), channel_id=1, source_target_pairs={{0,4},{4,0},{8,12},{12,8},{1,5},{5,1},{9,13},{13,9},{2,6},{6,2},{1... | collective-permute-start | bytes 1572872 | tf_op jit(solution)/shard_map/ppermute | solution.py:700
  36.9 12.1 %copy-start.1 = (bf16[64,4096]{1,0:T(8,128)(2,1)}, bf16[64,4096]{1,0:T(8,128)(2,1)S(1)}, u32[]{:S(2)}) copy-start(bf16[64,4096]{1,0:T(8,128)(2,1)S(1)} %collective-permute-done.5.refs_2_.refs_6_) | copy-start | bytes 1572868
  38.5 10.6 %copy-start.3 = (bf16[64,4096]{1,0:T(8,128)(2,1)}, bf16[64,4096]{1,0:T(8,128)(2,1)S(1)}, u32[]{:S(2)}) copy-start(bf16[64,4096]{1,0:T(8,128)(2,1)S(1)} %collective-permute-done.6.refs_3_.refs_7_) | copy-start | bytes 1572868
  49.1 1.0 copy-start.6
  54.4 0.9 copy-start.7
  55.3 2.8 %collective-permute-start.9 = (bf16[2,128,1792]{2,1,0:T(8,128)(2,1)}, bf16[2,128,1792]{2,1,0:T(8,128)(2,1)}, u32[]{:S(2)}, u32[]{:S(2)}) collective-permute-start(bf16[2,128,1792]{2,1,0:T(8,128)(2,1)} %bitcast.14), channel_id=1, source_target_pairs={{0,4},{4,0},{8,12},{12,8},{1,5},{5,1},{9,13},{13,9},{2,6},{6,2},{1... | collective-permute-start | bytes 2752520 | tf_op jit(solution)/shard_map/ppermute | solution.py:700
  55.4 7.0 %copy-start.2 = (bf16[64,4096]{1,0:T(8,128)(2,1)S(1)}, bf16[64,4096]{1,0:T(8,128)(2,1)}, u32[]{:S(2)}) copy-start(bf16[64,4096]{1,0:T(8,128)(2,1)} %copy-done.1) | copy-start | bytes 1572868
  55.4 7.0 %copy-start.4 = (bf16[64,4096]{1,0:T(8,128)(2,1)S(1)}, bf16[64,4096]{1,0:T(8,128)(2,1)}, u32[]{:S(2)}) copy-start(bf16[64,4096]{1,0:T(8,128)(2,1)} %copy-done.3) | copy-start | bytes 1572868
  59.8 27.0 %copy-start.8 = (bf16[2,128,1792]{2,1,0:T(8,128)(2,1)S(1)}, bf16[2,128,1792]{2,1,0:T(8,128)(2,1)}, u32[]{:S(2)}) copy-start(bf16[2,128,1792]{2,1,0:T(8,128)(2,1)} %copy-done.7) | copy-start | bytes 2752516
  59.8 23.2 %collective-permute-start.10 = (bf16[2,128,1792]{2,1,0:T(8,128)(2,1)S(1)}, bf16[2,128,1792]{2,1,0:T(8,128)(2,1)S(1)}, u32[]{:S(2)}, u32[]{:S(2)}) collective-permute-start(bf16[2,128,1792]{2,1,0:T(8,128)(2,1)S(1)} %fusion), channel_id=1, source_target_pairs={{0,8},{4,12},{8,0},{12,4},{1,9},{5,13},{9,1},{13,5},{2,10},{6,14},... | collective-permute-start | bytes 2752520 | tf_op jit(solution)/shard_map/ppermute | solution.py:703
  83.0 3.8 %collective-permute-start.11 = (bf16[2,2,128,1792]{3,2,1,0:T(8,128)(2,1)S(1)}, bf16[2,2,128,1792]{3,2,1,0:T(8,128)(2,1)S(1)}, u32[]{:S(2)}, u32[]{:S(2)}) collective-permute-start(bf16[2,2,128,1792]{3,2,1,0:T(8,128)(2,1)S(1)} %get-tuple-element.63), channel_id=1, source_target_pairs={{0,4},{4,0},{8,12},{12,8},{1,5},{5,1},{9,13},{13,9},{2,6},{6,2},{1... | collective-permute-start | bytes 5505032 | tf_op jit(solution)/shard_map/ppermute | solution.py:700
  83.0 13.4 %collective-permute-start.18 = (bf16[1,768,128]{2,1,0:T(8,128)(2,1)S(1)}, bf16[1,768,128]{2,1,0:T(8,128)(2,1)S(1)}, u32[]{:S(2)}, u32[]{:S(2)}) collective-permute-start(bf16[1,768,128]{2,1,0:T(8,128)(2,1)S(1)} %maximum_bitcast_fusion), channel_id=1, source_target_pairs={{0,2},{1,3},{2,0},{3,1},{4,6},{5,7},{6,4},{7,5},{8,10},{9,11},{10,... | collective-permute-start | bytes 589832 | tf_op jit(solution)/shard_map/ppermute | solution.py:706
  87.4 12.0 %collective-permute-start.13 = (bf16[128,1792]{1,0:T(8,128)(2,1)S(1)}, bf16[128,1792]{1,0:T(8,128)(2,1)S(1)}, u32[]{:S(2)}, u32[]{:S(2)}) collective-permute-start(bf16[128,1792]{1,0:T(8,128)(2,1)S(1)} %fusion.5.mine_ref), channel_id=1, source_target_pairs={{0,4},{4,0},{8,12},{12,8},{1,5},{5,1},{9,13},{13,9},{2,6},{6,2},{1... | collective-permute-start | bytes 1376264 | tf_op jit(solution)/shard_map/ppermute | solution.py:700
  96.4 12.1 %collective-permute-start.19 = (bf16[2,768,128]{2,1,0:T(8,128)(2,1)S(1)}, bf16[2,768,128]{2,1,0:T(8,128)(2,1)S(1)}, u32[]{:S(2)}, u32[]{:S(2)}) collective-permute-start(bf16[2,768,128]{2,1,0:T(8,128)(2,1)S(1)} %pad_maximum_fusion.1), channel_id=1, source_target_pairs={{0,1},{1,0},{2,3},{3,2},{4,5},{5,4},{6,7},{7,6},{8,9},{9,8},{10,11... | collective-permute-start | bytes 1179656 | tf_op jit(solution)/shard_map/ppermute | solution.py:706
  97.2 21.4 %collective-permute-start.12 = (bf16[64,4096]{1,0:T(8,128)(2,1)}, bf16[64,4096]{1,0:T(8,128)(2,1)S(1)}, u32[]{:S(2)}, u32[]{:S(2)}) collective-permute-start(bf16[64,4096]{1,0:T(8,128)(2,1)} %collective-permute-done.4.refs_4_.refs_8_), channel_id=1, source_target_pairs={{0,1},{1,0},{2,3},{3,2},{4,5},{5,4},{6,7},{7,6},{8,9},{9,8},{10,11... | collective-permute-start | bytes 1572872 | tf_op jit(solution)/shard_map/ppermute | solution.py:706
  98.6 30.7 %collective-permute-start.20 = (bf16[128,1792]{1,0:T(8,128)(2,1)S(1)}, bf16[128,1792]{1,0:T(8,128)(2,1)S(1)}, u32[]{:S(2)}, u32[]{:S(2)}) collective-permute-start(bf16[128,1792]{1,0:T(8,128)(2,1)S(1)} %fusion.5.mine_ref), channel_id=1, source_target_pairs={{0,8},{4,12},{8,0},{12,4},{1,9},{5,13},{9,1},{13,5},{2,10},{6,14},... | collective-permute-start | bytes 1376264 | tf_op jit(solution)/shard_map/ppermute | solution.py:703
  99.4 30.5 %collective-permute-start.17 = (bf16[128,1792]{1,0:T(8,128)(2,1)S(1)}, bf16[128,1792]{1,0:T(8,128)(2,1)S(1)}, u32[]{:S(2)}, u32[]{:S(2)}) collective-permute-start(bf16[128,1792]{1,0:T(8,128)(2,1)S(1)} %fusion.3.mine_ref), channel_id=1, source_target_pairs={{0,4},{4,0},{8,12},{12,8},{1,5},{5,1},{9,13},{13,9},{2,6},{6,2},{1... | collective-permute-start | bytes 1376264 | tf_op jit(solution)/shard_map/ppermute | solution.py:700
  99.4 35.7 %collective-permute-start.16 = (bf16[128,1792]{1,0:T(8,128)(2,1)S(1)}, bf16[128,1792]{1,0:T(8,128)(2,1)S(1)}, u32[]{:S(2)}, u32[]{:S(2)}) collective-permute-start(bf16[128,1792]{1,0:T(8,128)(2,1)S(1)} %fusion.3.mine_ref), channel_id=1, source_target_pairs={{0,8},{4,12},{8,0},{12,4},{1,9},{5,13},{9,1},{13,5},{2,10},{6,14},... | collective-permute-start | bytes 1376264 | tf_op jit(solution)/shard_map/ppermute | solution.py:703
  108.5 15.5 %collective-permute-start.14 = (bf16[64,4096]{1,0:T(8,128)(2,1)}, bf16[64,4096]{1,0:T(8,128)(2,1)S(1)}, u32[]{:S(2)}, u32[]{:S(2)}) collective-permute-start(bf16[64,4096]{1,0:T(8,128)(2,1)} %collective-permute-done.4.refs_4_.refs_8_), channel_id=1, source_target_pairs={{0,4},{4,0},{8,12},{12,8},{1,5},{5,1},{9,13},{13,9},{2,6},{6,2},{1... | collective-permute-start | bytes 1572872 | tf_op jit(solution)/shard_map/ppermute | solution.py:700
  118.7 5.3 %collective-permute-start.15 = (bf16[64,4096]{1,0:T(8,128)(2,1)S(1)}, bf16[64,4096]{1,0:T(8,128)(2,1)S(1)}, u32[]{:S(2)}, u32[]{:S(2)}) collective-permute-start(bf16[64,4096]{1,0:T(8,128)(2,1)S(1)} %collective-permute-done.12.refs_5_.refs_9_), channel_id=1, source_target_pairs={{0,4},{4,0},{8,12},{12,8},{1,5},{5,1},{9,13},{13,9},{2,6},{6,2},{1... | collective-permute-start | bytes 1572872 | tf_op jit(solution)/shard_map/ppermute | solution.py:700
  129.3 6.0 %collective-permute-start.22 = (bf16[128,1792]{1,0:T(8,128)(2,1)S(1)}, bf16[128,1792]{1,0:T(8,128)(2,1)S(1)}, u32[]{:S(2)}, u32[]{:S(2)}) collective-permute-start(bf16[128,1792]{1,0:T(8,128)(2,1)S(1)} %collective-permute-done.20.refs_1_), channel_id=1, source_target_pairs={{0,4},{4,0},{8,12},{12,8},{1,5},{5,1},{9,13},{13,9},{2,6},{6,2},{1... | collective-permute-start | bytes 1376264 | tf_op jit(solution)/shard_map/ppermute | solution.py:700
  135.1 1.9 %collective-permute-start.21 = (bf16[128,1792]{1,0:T(8,128)(2,1)S(1)}, bf16[128,1792]{1,0:T(8,128)(2,1)S(1)}, u32[]{:S(2)}, u32[]{:S(2)}) collective-permute-start(bf16[128,1792]{1,0:T(8,128)(2,1)S(1)} %collective-permute-done.16.refs_0_), channel_id=1, source_target_pairs={{0,4},{4,0},{8,12},{12,8},{1,5},{5,1},{9,13},{13,9},{2,6},{6,2},{1... | collective-permute-start | bytes 1376264 | tf_op jit(solution)/shard_map/ppermute | solution.py:700
  148.2 5.6 %collective-permute-start.23 = (bf16[2,256,128]{2,1,0:T(8,128)(2,1)S(1)}, bf16[2,256,128]{2,1,0:T(8,128)(2,1)S(1)}, u32[]{:S(2)}, u32[]{:S(2)}) collective-permute-start(bf16[2,256,128]{2,1,0:T(8,128)(2,1)S(1)} %slice.51), channel_id=1, source_target_pairs={{0,1},{1,0},{2,3},{3,2},{4,5},{5,4},{6,7},{7,6},{8,9},{9,8},{10,11... | collective-permute-start | bytes 393224 | tf_op jit(solution)/shard_map/ppermute | solution.py:706
  152.5 9.5 %collective-permute-start.24 = (bf16[2,512,128]{2,1,0:T(8,128)(2,1)S(1)}, bf16[2,512,128]{2,1,0:T(8,128)(2,1)S(1)}, u32[]{:S(2)}, u32[]{:S(2)}) collective-permute-start(bf16[2,512,128]{2,1,0:T(8,128)(2,1)S(1)} %right_grads.2), channel_id=1, source_target_pairs={{0,1},{1,0},{2,3},{3,2},{4,5},{5,4},{6,7},{7,6},{8,9},{9,8},{10,11... | collective-permute-start | bytes 786440 | tf_op jit(solution)/shard_map/ppermute | solution.py:706
  153.8 14.5 %collective-permute-start.27 = (bf16[256,128]{1,0:T(8,128)(2,1)S(1)}, bf16[256,128]{1,0:T(8,128)(2,1)S(1)}, u32[]{:S(2)}, u32[]{:S(2)}) collective-permute-start(bf16[256,128]{1,0:T(8,128)(2,1)S(1)} %slice_bitcast_fusion.6), channel_id=1, source_target_pairs={{0,2},{1,3},{2,0},{3,1},{4,6},{5,7},{6,4},{7,5},{8,10},{9,11},{10,... | collective-permute-start | bytes 196616 | tf_op jit(solution)/shard_map/ppermute | solution.py:706
  162.2 7.0 %collective-permute-start.25 = (bf16[512,128]{1,0:T(8,128)(2,1)S(1)}, bf16[512,128]{1,0:T(8,128)(2,1)S(1)}, u32[]{:S(2)}, u32[]{:S(2)}) collective-permute-start(bf16[512,128]{1,0:T(8,128)(2,1)S(1)} %get-tuple-element.86), channel_id=1, source_target_pairs={{0,0},{1,4},{2,8},{3,12},{4,1},{5,5},{6,9},{7,13},{8,2},{9,6},{10,... | collective-permute-start | bytes 393224 | tf_op jit(solution)/shard_map/ppermute | solution.py:713
  162.8 15.4 %collective-permute-start.26 = (bf16[512,128]{1,0:T(8,128)(2,1)S(1)}, bf16[512,128]{1,0:T(8,128)(2,1)S(1)}, u32[]{:S(2)}, u32[]{:S(2)}) collective-permute-start(bf16[512,128]{1,0:T(8,128)(2,1)S(1)} %get-tuple-element.87), channel_id=1, source_target_pairs={{0,8},{1,12},{2,0},{3,4},{4,9},{5,13},{6,1},{7,5},{8,10},{9,14},{1... | collective-permute-start | bytes 393224 | tf_op jit(solution)/shard_map/ppermute | solution.py:713

commit v20 on v17

--- a/solution.py
+++ b/solution.py
@@ -746,7 +746,6 @@
     near_arrived = swap(arrived)
     partner = after(partner, factors)
     got_early = across(sums)
-    more = along(after(factors, partner), 2)
     order = jnp.concatenate([base, jnp.stack([chip, z])]).astype(jnp.int32)
     own = [tokens, tokens, near_tokens, near_tokens]
     late = [arrived, partner, near_arrived, swap(partner)]
@@ -754,6 +753,7 @@
     late_order = after(scalars(other_block), sums)
     mine, other = products(late_pieces, late_order, gate_weight, up_weight, 0, part)
     near = swap(other[0])
+    more = along(after(factors, mine), 2)
     late_partner = along(after(late_first, mine), 1)
     mine_order = after(scalars(mine_block), mine)
     kept, other = products(

time: 158 us -> 162 us (1.025)
  waiting for transfers between devices: 44.8 us -> 49.3 us
    ppermute x7, waiting for transfers between devices: 10.9 us -> 15.3 us  [along(): lax.ppermute(value, 'tensor', [(i, i ^ bit) for i in range(tensor_count)])]
    ppermute x6, starting transfers between devices: 7.69 us -> 11 us  [across(): return lax.ppermute(value, 'fsdp', [(i, i ^ 2) for i in range(fsdp_count)])]
    ppermute x7, starting transfers between devices: 11.4 us -> 8.54 us  [along(): lax.ppermute(value, 'tensor', [(i, i ^ bit) for i in range(tensor_count)])]
  transfers between devices with their start and end apart: 28 -> 28, of which waited for: 10 -> 10; matrix products, arithmetic and copies ran while one was open for 4% -> 4% of each run, Pallas kernels for 42% -> 41%
where the time goes in v20:
time: 162 us; the launch traced here: 161 us
  Pallas kernels  77.2 us (48%)
  waiting for transfers between devices  49.3 us (30%)
  starting transfers between devices  25.9 us (16%)
  other arithmetic  5.59 us (3%)
  local copies, waits for them, and re-layouts  2.05 us (1%)
    pallas_call x3, Pallas kernels, products(): pl.pallas_call(functools.partial(products_kernel, sets), grid_spec=pltpu....  33.2 us
    ppermute x6, waiting for transfers between devices, across(): return lax.ppermute(value, 'fsdp', [(i, i ^ 2) for i in range(fsdp_count)])  19.3 us
    ppermute x7, waiting for transfers between devices, along(): lax.ppermute(value, 'tensor', [(i, i ^ bit) for i in range(tensor_count)])  15.3 us
    ppermute x3, waiting for transfers between devices, turn(): return lax.ppermute(value, both_axes, perm)  11.2 us
    pallas_call x1, Pallas kernels, left_grads(): pl.pallas_call(functools.partial(left_kernel, chunks, scale), grid_spec=p...  11.1 us
    ppermute x6, starting transfers between devices, across(): return lax.ppermute(value, 'fsdp', [(i, i ^ 2) for i in range(fsdp_count)])  11 us
    pallas_call x2, Pallas kernels, student_part(): pl.pallas_call(functools.partial(student_kernel, steps, bool(late), tenso...  10.6 us
    pallas_call x2, Pallas kernels, target_part(): pl.pallas_call(functools.partial(target_kernel, sign), grid_spec=pltpu.Pr...  10.5 us
  transfers between devices with their start and end apart: 28, of which 10 were waited for; matrix products, arithmetic and copies ran while one was open for 4% of the time, Pallas kernels for 41%

profile of v20, /device:TPU:0, one launch (start us, length us, event | category | flops | bytes accessed | tf_op | source)
XLA Modules:
  0.0 160.9 jit_solution(5989938569186107057)
XLA Ops:
  0.6 0.5 collective-permute-start
  1.1 0.6 pad_add_fusion.1.idx_ref
  1.8 3.1 %cut_tokens.1 = (bf16[64,4096]{1,0:T(8,128)(2,1)}, bf16[64,4096]{1,0:T(8,128)(2,1)}) custom-call(s32[3]{0:T(128)} %pad_add_fusion.1.idx_ref, bf16[128,8192]{1,0:T(8,128)(2,1)} %refs_1_.11, bf16[128,8192]{1,0:T(8,128)(2,1)} %refs_1_.11), custom_call_target="tpu_custom_call" | custom-call | flops 1 | bytes 1 | tf_op jit(solution)/shard_map/cut_tokens/pallas_call | solution.py:313
  4.8 2.5 %collective-permute-start.1 = (bf16[64,4096]{1,0:T(8,128)(2,1)}, bf16[64,4096]{1,0:T(8,128)(2,1)S(1)}, u32[]{:S(2)}, u32[]{:S(2)}) collective-permute-start(bf16[64,4096]{1,0:T(8,128)(2,1)} %get-tuple-element.44), channel_id=1, source_target_pairs={{0,8},{4,12},{8,0},{12,4},{1,9},{5,13},{9,1},{13,5},{2,10},{6,14},... | collective-permute-start | bytes 1572872 | tf_op jit(solution)/shard_map/ppermute | solution.py:703
  7.3 0.1 concatenate.25.idx_ref
  7.4 0.1 concatenate.27.idx_ref
  7.5 0.0 collective-permute-done.refs_2_.refs_3_
  7.5 10.8 %gate_up_products.3 = (bf16[1,2,128,1792]{3,2,1,0:T(8,128)(2,1)S(1)}, bf16[1,2,128,1792]{3,2,1,0:T(8,128)(2,1)}) custom-call(s32[5]{0:T(128)S(1)} %concatenate.25.idx_ref, bf16[128,8192]{1,0:T(8,128)(2,1)S(1)} %copy-done, bf16[128,8192]{1,0:T(8,128)(2,1)S(1)} %copy-done, bf16[128,8192]{1,0:T(8,128)(2,1)} %collective-permute-done.refs_2_.refs_3_, ...), custom_call_target="tpu_custom_call" | custom-call | flops 1 | bytes 1 | tf_op jit(solution)/shard_map/gate_up_products/pallas_call | solution.py:374
  18.3 0.9 copy-done.1
  19.2 0.9 collective-permute-done.1.refs_0_.refs_4_
  20.1 1.8 %collective-permute-start.2 = (bf16[64,4096]{1,0:T(8,128)(2,1)S(1)}, bf16[64,4096]{1,0:T(8,128)(2,1)S(1)}, u32[]{:S(2)}, u32[]{:S(2)}) collective-permute-start(bf16[64,4096]{1,0:T(8,128)(2,1)S(1)} %collective-permute-done.1.refs_0_.refs_4_), channel_id=1, source_target_pairs={{0,1},{1,0},{2,3},{3,2},{4,5},{5,4},{6,7},{7,6},{8,9},{9,8},{10,11... | collective-permute-start | bytes 1572872 | tf_op jit(solution)/shard_map/ppermute | solution.py:706
  21.9 0.0 collective-permute-start.5
  21.9 0.5 collective-permute-start.7
  22.4 1.5 collective-permute-start.4
  23.9 0.7 collective-permute-start.3
  24.6 1.6 %pack_left.1 = bf16[256,128]{1,0:T(8,128)(2,1)} custom-call(bf16[32,16,64]{2,1,0:T(8,128)(2,1)} %left_ref), custom_call_target="tpu_custom_call" | custom-call | flops 10000000000 | bytes 10000000 | tf_op jit(solution)/shard_map/pack_left/pallas_call | solution.py:339
  26.2 12.2 %collective-permute-done.4.refs_4_.refs_8_ = bf16[64,4096]{1,0:T(8,128)(2,1)} collective-permute-done((bf16[64,4096]{1,0:T(8,128)(2,1)}, bf16[64,4096]{1,0:T(8,128)(2,1)}, u32[]{:S(2)}, u32[]{:S(2)}) %collective-permute-start.4) | collective-permute-done | bytes 524320 | tf_op jit(solution)/shard_map/ppermute | solution.py:703
  38.4 0.9 maximum_bitcast_fusion
  39.3 0.1 collective-permute-start.6
  39.4 1.7 %fusion.1 = bf16[2,128,1792]{2,1,0:T(8,128)(2,1)S(1)} fusion(bf16[2,128,1792]{2,1,0:T(8,128)(2,1)} %collective-permute-done.7, bf16[1,2,128,1792]{3,2,1,0:T(8,128)(2,1)} %copy-done.1), kind=kLoop, calls=%fused_computation.3 | loop fusion | flops 1835008 | bytes 2752512 | tf_op jit(solution)/shard_map/convert_element_type | solution.py:742
  41.1 2.5 %collective-permute-start.9 = (bf16[2,128,1792]{2,1,0:T(8,128)(2,1)S(1)}, bf16[2,128,1792]{2,1,0:T(8,128)(2,1)S(1)}, u32[]{:S(2)}, u32[]{:S(2)}) collective-permute-start(bf16[2,128,1792]{2,1,0:T(8,128)(2,1)S(1)} %fusion.1), channel_id=1, source_target_pairs={{0,8},{4,12},{8,0},{12,4},{1,9},{5,13},{9,1},{13,5},{2,10},{6,14},... | collective-permute-start | bytes 2752520 | tf_op jit(solution)/shard_map/ppermute | solution.py:703
  43.6 10.0 %gate_up_products.4 = (bf16[1,2,128,1792]{3,2,1,0:T(8,128)(2,1)S(1)}, bf16[1,2,128,1792]{3,2,1,0:T(8,128)(2,1)S(1)}) custom-call(s32[5]{0:T(128)S(1)} %concatenate.25.idx_ref, bf16[64,4096]{1,0:T(8,128)(2,1)S(1)} %collective-permute-done.1.refs_0_.refs_4_, bf16[64,4096]{1,0:T(8,128)(2,1)S(1)} %collective-permute-done.2.refs_1_.refs_5_, ...), custom_call_target="tpu_custom_call" | custom-call | flops 1 | bytes 1 | tf_op jit(solution)/shard_map/gate_up_products/pallas_call | solution.py:374
  53.6 1.3 collective-permute-start.11
  54.9 0.2 collective-permute-start.10
  55.1 1.5 collective-permute-start.8
  56.6 12.4 %gate_up_products.5 = (bf16[2,2,128,1792]{3,2,1,0:T(8,128)(2,1)S(1)}, bf16[2,2,128,1792]{3,2,1,0:T(8,128)(2,1)S(1)}) custom-call(s32[5]{0:T(128)S(1)} %concatenate.27.idx_ref, bf16[128,8192]{1,0:T(8,128)(2,1)S(1)} %copy-done, bf16[128,8192]{1,0:T(8,128)(2,1)S(1)} %copy-done, bf16[128,8192]{1,0:T(8,128)(2,1)} %collective-permute-done.refs_2_.refs_3_, ...), custom_call_target="tpu_custom_call" | custom-call | flops 10000000000 | bytes 10000000 | tf_op jit(solution)/shard_map/gate_up_products/pallas_call | solution.py:374
  69.0 0.2 fusion
  69.3 4.4 %collective-permute-done.8.refs_5_.refs_9_ = bf16[64,4096]{1,0:T(8,128)(2,1)S(1)} collective-permute-done((bf16[64,4096]{1,0:T(8,128)(2,1)}, bf16[64,4096]{1,0:T(8,128)(2,1)S(1)}, u32[]{:S(2)}, u32[]{:S(2)}) %collective-permute-start.8) | collective-permute-done | bytes 524320 | tf_op jit(solution)/shard_map/ppermute | solution.py:706
  73.6 0.1 pad_add_fusion.idx_ref
  73.8 0.1 collective-permute-start.13
  73.8 1.9 %collective-permute-start.16 = (bf16[2,128,1792]{2,1,0:T(8,128)(2,1)S(1)}, bf16[2,128,1792]{2,1,0:T(8,128)(2,1)S(1)}, u32[]{:S(2)}, u32[]{:S(2)}) collective-permute-start(bf16[2,128,1792]{2,1,0:T(8,128)(2,1)S(1)} %fusion), channel_id=1, source_target_pairs={{0,8},{4,12},{8,0},{12,4},{1,9},{5,13},{9,1},{13,5},{2,10},{6,14},... | collective-permute-start | bytes 2752520 | tf_op jit(solution)/shard_map/ppermute | solution.py:703
  75.8 1.7 %collective-permute-done.12 = bf16[2,2,128,1792]{3,2,1,0:T(8,128)(2,1)S(1)} collective-permute-done((bf16[2,2,128,1792]{3,2,1,0:T(8,128)(2,1)S(1)}, bf16[2,2,128,1792]{3,2,1,0:T(8,128)(2,1)S(1)}, u32[]{:S(2)}, u32[]{:S(2)}) %collective-permute-start.12) | collective-permute-done | bytes 1835040 | tf_op jit(solution)/shard_map/ppermute | solution.py:700
  77.4 0.3 bitcast_add_fusion.1
  77.8 0.3 fusion.5.mine_ref
  78.0 0.2 collective-permute-start.17
  78.2 7.1 %collective-permute-done.13 = bf16[2,768,128]{2,1,0:T(8,128)(2,1)S(1)} collective-permute-done((bf16[2,768,128]{2,1,0:T(8,128)(2,1)S(1)}, bf16[2,768,128]{2,1,0:T(8,128)(2,1)S(1)}, u32[]{:S(2)}, u32[]{:S(2)}) %collective-permute-start.13) | collective-permute-done | bytes 393248 | tf_op jit(solution)/shard_map/ppermute | solution.py:706
  85.4 0.1 pad_maximum_fusion.refs_4_.refs_5_.refs_6_.refs_8_.refs_9_
  85.4 5.3 %student_part.2 = (bf16[8,256,256]{2,1,0:T(8,128)(2,1)S(1)}, f32[256,2048]{1,0:T(8,128)S(1)}, bf16[8,256,256]{2,1,0:T(8,128)(2,1)S(1)}) custom-call(s32[4]{0:T(128)S(1)} %pad_add_fusion.idx_ref, bf16[128,8192]{1,0:T(8,128)(2,1)S(1)} %copy-done, bf16[128,8192]{1,0:T(8,128)(2,1)S(1)} %copy-done, bf16[128,8192]{1,0:T(8,128)(2,1)} %collective-permute-done.refs_2_.refs_3_, ...), custom_call_target="tpu_custom_call" | custom-call | flops 10000000000 | bytes 10000000 | tf_op jit(solution)/shard_map/student_part/pallas_call | solution.py:550
  90.7 1.9 %collective-permute-start.20 = (bf16[128,1792]{1,0:T(8,128)(2,1)S(1)}, bf16[128,1792]{1,0:T(8,128)(2,1)S(1)}, u32[]{:S(2)}, u32[]{:S(2)}) collective-permute-start(bf16[128,1792]{1,0:T(8,128)(2,1)S(1)} %fusion.5.mine_ref), channel_id=1, source_target_pairs={{0,8},{4,12},{8,0},{12,4},{1,9},{5,13},{9,1},{13,5},{2,10},{6,14},... | collective-permute-start | bytes 1376264 | tf_op jit(solution)/shard_map/ppermute | solution.py:703
  92.7 0.5 collective-permute-start.15
  93.2 5.2 %target_part.2.refs_11_ = f32[256,2048]{1,0:T(8,128)S(1)} custom-call(s32[1]{0:T(128)} %bitcast.2.idx_ref, bf16[128,1792]{1,0:T(8,128)(2,1)S(1)} %fusion.5.mine_ref, bf16[128,1792]{1,0:T(8,128)(2,1)S(1)} %collective-permute-done.17.near_ref, bf16[3584,2048]{1,0:T(8,128)(2,1)} %refs_4_.5), custom_call_target="tpu_custom_call" | custom-call | flops 1 | bytes 1 | tf_op jit(solution)/shard_map/target_part/pallas_call | solution.py:412
  98.4 0.3 bitcast_add_fusion
  98.7 0.3 fusion.3.mine_ref
  99.0 0.1 collective-permute-start.19
  99.1 0.6 collective-permute-start.18
  99.6 5.3 %student_part.3 = (bf16[8,256,256]{2,1,0:T(8,128)(2,1)S(1)}, f32[256,2048]{1,0:T(8,128)S(1)}) custom-call(s32[4]{0:T(128)S(1)} %pad_add_fusion.idx_ref, bf16[64,4096]{1,0:T(8,128)(2,1)S(1)} %collective-permute-done.1.refs_0_.refs_4_, bf16[64,4096]{1,0:T(8,128)(2,1)S(1)} %collective-permute-done.2.refs_1_.refs_5_, ...), custom_call_target="tpu_custom_call" | custom-call | flops 10000000000 | bytes 10000000 | tf_op jit(solution)/shard_map/student_part/pallas_call | solution.py:550
  105.0 2.0 %collective-permute-done.20.refs_1_ = bf16[128,1792]{1,0:T(8,128)(2,1)S(1)} collective-permute-done((bf16[128,1792]{1,0:T(8,128)(2,1)S(1)}, bf16[128,1792]{1,0:T(8,128)(2,1)S(1)}, u32[]{:S(2)}, u32[]{:S(2)}) %collective-permute-start.20) | collective-permute-done | bytes 458784 | tf_op jit(solution)/shard_map/ppermute | solution.py:703
  107.0 5.3 %target_part.3.refs_5_ = f32[256,2048]{1,0:T(8,128)S(1)} custom-call(s32[1]{0:T(128)} %bitcast.2.idx_ref, bf16[128,1792]{1,0:T(8,128)(2,1)S(1)} %fusion.3.mine_ref, bf16[128,1792]{1,0:T(8,128)(2,1)S(1)} %collective-permute-done.19.near_ref, bf16[3584,2048]{1,0:T(8,128)(2,1)} %refs_4_.5, f32[256,2048]{1,0:T(8,128)S(1)} %get-tuple-element.77.refs_0_), custom_call_target="tpu_custom_call" | custom-call | flops 1 | bytes 1 | tf_op jit(solution)/shard_map/target_part/pallas_call | solution.py:412
  112.2 4.2 %collective-permute-done.18.refs_0_ = bf16[128,1792]{1,0:T(8,128)(2,1)S(1)} collective-permute-done((bf16[128,1792]{1,0:T(8,128)(2,1)S(1)}, bf16[128,1792]{1,0:T(8,128)(2,1)S(1)}, u32[]{:S(2)}, u32[]{:S(2)}) %collective-permute-start.18) | collective-permute-done | bytes 458784 | tf_op jit(solution)/shard_map/ppermute | solution.py:703
  116.5 1.8 %collective-permute-done.21.refs_2_ = bf16[128,1792]{1,0:T(8,128)(2,1)S(1)} collective-permute-done((bf16[128,1792]{1,0:T(8,128)(2,1)S(1)}, bf16[128,1792]{1,0:T(8,128)(2,1)S(1)}, u32[]{:S(2)}, u32[]{:S(2)}) %collective-permute-start.21) | collective-permute-done | bytes 458784 | tf_op jit(solution)/shard_map/ppermute | solution.py:700
  118.3 11.1 %left_grads.1 = (bf16[4,256,128]{2,1,0:T(8,128)(2,1)S(1)}, bf16[8,256,512]{2,1,0:T(8,128)(2,1)S(1)}) custom-call(s32[4]{0:T(128)S(1)} %pad_add_fusion.idx_ref, bf16[128,1792]{1,0:T(8,128)(2,1)S(1)} %collective-permute-done.18.refs_0_, bf16[128,1792]{1,0:T(8,128)(2,1)S(1)} %collective-permute-done.20.refs_1_, ...), custom_call_target="tpu_custom_call" | custom-call | flops 1 | bytes 1 | tf_op jit(solution)/shard_map/left_grads/pallas_call | solution.py:618
  129.4 1.7 %collective-permute-start.23 = (bf16[2,256,128]{2,1,0:T(8,128)(2,1)S(1)}, bf16[2,256,128]{2,1,0:T(8,128)(2,1)S(1)}, u32[]{:S(2)}, u32[]{:S(2)}) collective-permute-start(bf16[2,256,128]{2,1,0:T(8,128)(2,1)S(1)} %slice.51), channel_id=1, source_target_pairs={{0,1},{1,0},{2,3},{3,2},{4,5},{5,4},{6,7},{7,6},{8,9},{9,8},{10,11... | collective-permute-start | bytes 393224 | tf_op jit(solution)/shard_map/ppermute | solution.py:706
  131.2 3.5 %right_grads.2 = bf16[2,512,128]{2,1,0:T(8,128)(2,1)S(1)} custom-call(s32[4]{0:T(128)S(1)} %pad_add_fusion.idx_ref, bf16[128,8192]{1,0:T(8,128)(2,1)S(1)} %copy-done, bf16[128,8192]{1,0:T(8,128)(2,1)S(1)} %copy-done, bf16[128,8192]{1,0:T(8,128)(2,1)} %collective-permute-done.refs_2_.refs_3_, bf16[128,8192]{1,0:T(8,128)(2,1)} %collective-permute-done.refs_2_.refs_3_, ...), custom_call_target="tpu_custom_call" | custom-call | flops 1 | bytes 1 | tf_op jit(solution)/shard_map/right_grads/pallas_call | solution.py:672
  134.7 0.4 collective-permute-start.24
  135.2 1.7 %collective-permute-start.27 = (bf16[256,128]{1,0:T(8,128)(2,1)S(1)}, bf16[256,128]{1,0:T(8,128)(2,1)S(1)}, u32[]{:S(2)}, u32[]{:S(2)}) collective-permute-start(bf16[256,128]{1,0:T(8,128)(2,1)S(1)} %slice_bitcast_fusion.6), channel_id=1, source_target_pairs={{0,2},{1,3},{2,0},{3,1},{4,6},{5,7},{6,4},{7,5},{8,10},{9,11},{10,... | collective-permute-start | bytes 196616 | tf_op jit(solution)/shard_map/ppermute | solution.py:706
  136.9 3.5 %right_grads.3 = bf16[2,512,128]{2,1,0:T(8,128)(2,1)S(1)} custom-call(s32[4]{0:T(128)S(1)} %pad_add_fusion.idx_ref, bf16[128,8192]{1,0:T(8,128)(2,1)S(1)} %copy-done, bf16[128,8192]{1,0:T(8,128)(2,1)S(1)} %copy-done, bf16[128,8192]{1,0:T(8,128)(2,1)} %collective-permute-done.refs_2_.refs_3_, bf16[128,8192]{1,0:T(8,128)(2,1)} %collective-permute-done.refs_2_.refs_3_, ...), custom_call_target="tpu_custom_call" | custom-call | flops 10000000000 | bytes 10000000 | tf_op jit(solution)/shard_map/right_grads/pallas_call | solution.py:672
  140.4 3.8 %collective-permute-done.24 = bf16[2,512,128]{2,1,0:T(8,128)(2,1)S(1)} collective-permute-done((bf16[2,512,128]{2,1,0:T(8,128)(2,1)S(1)}, bf16[2,512,128]{2,1,0:T(8,128)(2,1)S(1)}, u32[]{:S(2)}, u32[]{:S(2)}) %collective-permute-start.24) | collective-permute-done | bytes 262176 | tf_op jit(solution)/shard_map/ppermute | solution.py:706
  144.2 0.1 add_convert_fusion
  144.3 0.7 collective-permute-start.25
  145.0 3.0 %collective-permute-start.26 = (bf16[512,128]{1,0:T(8,128)(2,1)S(1)}, bf16[512,128]{1,0:T(8,128)(2,1)S(1)}, u32[]{:S(2)}, u32[]{:S(2)}) collective-permute-start(bf16[512,128]{1,0:T(8,128)(2,1)S(1)} %get-tuple-element.87), channel_id=1, source_target_pairs={{0,8},{1,12},{2,0},{3,4},{4,9},{5,13},{6,1},{7,5},{8,10},{9,14},{1... | collective-permute-start | bytes 393224 | tf_op jit(solution)/shard_map/ppermute | solution.py:713
  148.1 0.2 reshape.32
  148.3 0.7 copy.8
  149.0 11.2 %collective-permute-done.26 = bf16[512,128]{1,0:T(8,128)(2,1)S(1)} collective-permute-done((bf16[512,128]{1,0:T(8,128)(2,1)S(1)}, bf16[512,128]{1,0:T(8,128)(2,1)S(1)}, u32[]{:S(2)}, u32[]{:S(2)}) %collective-permute-start.26) | collective-permute-done | bytes 131104 | tf_op jit(solution)/shard_map/ppermute | solution.py:713
  160.2 0.7 convert_add_fusion.2
  (32 shorter events, 0.2 us)
Async XLA Ops:
  0.6 6.9 %collective-permute-start = (bf16[128,8192]{1,0:T(8,128)(2,1)}, bf16[128,8192]{1,0:T(8,128)(2,1)}, u32[]{:S(2)}, u32[]{:S(2)}) collective-permute-start(bf16[128,8192]{1,0:T(8,128)(2,1)} %refs_1_.11), channel_id=1, source_target_pairs={{0,4},{4,0},{8,12},{12,8},{1,5},{5,1},{9,13},{13,9},{2,6},{6,2},{1... | collective-permute-start | bytes 6291464 | tf_op jit(solution)/shard_map/ppermute | solution.py:700
  1.8 5.8 %copy-start = (bf16[128,8192]{1,0:T(8,128)(2,1)S(1)}, bf16[128,8192]{1,0:T(8,128)(2,1)}, u32[]{:S(2)}) copy-start(bf16[128,8192]{1,0:T(8,128)(2,1)} %refs_1_.11) | copy-start | bytes 6291460
  4.8 15.3 %collective-permute-start.1 = (bf16[64,4096]{1,0:T(8,128)(2,1)}, bf16[64,4096]{1,0:T(8,128)(2,1)S(1)}, u32[]{:S(2)}, u32[]{:S(2)}) collective-permute-start(bf16[64,4096]{1,0:T(8,128)(2,1)} %get-tuple-element.44), channel_id=1, source_target_pairs={{0,8},{4,12},{8,0},{12,4},{1,9},{5,13},{9,1},{13,5},{2,10},{6,14},... | collective-permute-start | bytes 1572872 | tf_op jit(solution)/shard_map/ppermute | solution.py:703
  7.5 16.4 %copy-start.2 = (bf16[16,32,128]{2,1,0:T(8,128)(2,1)S(1)}, bf16[16,32,128]{2,1,0:T(8,128)(2,1)}, u32[]{:S(2)}) copy-start(bf16[16,32,128]{2,1,0:T(8,128)(2,1)} %param.10) | copy-start | bytes 393220
  18.3 0.9 copy-start.1
  20.1 19.2 %collective-permute-start.2 = (bf16[64,4096]{1,0:T(8,128)(2,1)S(1)}, bf16[64,4096]{1,0:T(8,128)(2,1)S(1)}, u32[]{:S(2)}, u32[]{:S(2)}) collective-permute-start(bf16[64,4096]{1,0:T(8,128)(2,1)S(1)} %collective-permute-done.1.refs_0_.refs_4_), channel_id=1, source_target_pairs={{0,1},{1,0},{2,3},{3,2},{4,5},{5,4},{6,7},{7,6},{8,9},{9,8},{10,11... | collective-permute-start | bytes 1572872 | tf_op jit(solution)/shard_map/ppermute | solution.py:706
  21.9 21.7 %collective-permute-start.5 = (bf16[64,4096]{1,0:T(8,128)(2,1)S(1)}, bf16[64,4096]{1,0:T(8,128)(2,1)}, u32[]{:S(2)}, u32[]{:S(2)}) collective-permute-start(bf16[64,4096]{1,0:T(8,128)(2,1)S(1)} %collective-permute-done.1.refs_0_.refs_4_), channel_id=1, source_target_pairs={{0,4},{4,0},{8,12},{12,8},{1,5},{5,1},{9,13},{13,9},{2,6},{6,2},{1... | collective-permute-start | bytes 1572872 | tf_op jit(solution)/shard_map/ppermute | solution.py:700
  21.9 17.5 %collective-permute-start.7 = (bf16[2,128,1792]{2,1,0:T(8,128)(2,1)}, bf16[2,128,1792]{2,1,0:T(8,128)(2,1)}, u32[]{:S(2)}, u32[]{:S(2)}) collective-permute-start(bf16[2,128,1792]{2,1,0:T(8,128)(2,1)} %bitcast.11), channel_id=1, source_target_pairs={{0,4},{4,0},{8,12},{12,8},{1,5},{5,1},{9,13},{13,9},{2,6},{6,2},{1... | collective-permute-start | bytes 2752520 | tf_op jit(solution)/shard_map/ppermute | solution.py:700
  22.4 16.0 %collective-permute-start.4 = (bf16[64,4096]{1,0:T(8,128)(2,1)}, bf16[64,4096]{1,0:T(8,128)(2,1)}, u32[]{:S(2)}, u32[]{:S(2)}) collective-permute-start(bf16[64,4096]{1,0:T(8,128)(2,1)} %get-tuple-element.51), channel_id=1, source_target_pairs={{0,8},{4,12},{8,0},{12,4},{1,9},{5,13},{9,1},{13,5},{2,10},{6,14},... | collective-permute-start | bytes 1572872 | tf_op jit(solution)/shard_map/ppermute | solution.py:703
  23.9 2.3 %collective-permute-start.3 = (bf16[16,32,128]{2,1,0:T(8,128)(2,1)S(1)}, bf16[16,32,128]{2,1,0:T(8,128)(2,1)S(1)}, u32[]{:S(2)}, u32[]{:S(2)}) collective-permute-start(bf16[16,32,128]{2,1,0:T(8,128)(2,1)S(1)} %copy-done.2), channel_id=1, source_target_pairs={{0,0},{1,4},{2,8},{3,12},{4,1},{5,5},{6,9},{7,13},{8,2},{9,6},{10,... | collective-permute-start | bytes 393224 | tf_op jit(solution)/shard_map/ppermute | solution.py:713
  39.3 4.3 %collective-permute-start.6 = (bf16[64,4096]{1,0:T(8,128)(2,1)S(1)}, bf16[64,4096]{1,0:T(8,128)(2,1)S(1)}, u32[]{:S(2)}, u32[]{:S(2)}) collective-permute-start(bf16[64,4096]{1,0:T(8,128)(2,1)S(1)} %collective-permute-done.2.refs_1_.refs_5_), channel_id=1, source_target_pairs={{0,4},{4,0},{8,12},{12,8},{1,5},{5,1},{9,13},{13,9},{2,6},{6,2},{1... | collective-permute-start | bytes 1572872 | tf_op jit(solution)/shard_map/ppermute | solution.py:700
  41.1 32.6 %collective-permute-start.9 = (bf16[2,128,1792]{2,1,0:T(8,128)(2,1)S(1)}, bf16[2,128,1792]{2,1,0:T(8,128)(2,1)S(1)}, u32[]{:S(2)}, u32[]{:S(2)}) collective-permute-start(bf16[2,128,1792]{2,1,0:T(8,128)(2,1)S(1)} %fusion.1), channel_id=1, source_target_pairs={{0,8},{4,12},{8,0},{12,4},{1,9},{5,13},{9,1},{13,5},{2,10},{6,14},... | collective-permute-start | bytes 2752520 | tf_op jit(solution)/shard_map/ppermute | solution.py:703
  53.6 15.6 %collective-permute-start.11 = (bf16[1,768,128]{2,1,0:T(8,128)(2,1)S(1)}, bf16[1,768,128]{2,1,0:T(8,128)(2,1)S(1)}, u32[]{:S(2)}, u32[]{:S(2)}) collective-permute-start(bf16[1,768,128]{2,1,0:T(8,128)(2,1)S(1)} %maximum_bitcast_fusion), channel_id=1, source_target_pairs={{0,2},{1,3},{2,0},{3,1},{4,6},{5,7},{6,4},{7,5},{8,10},{9,11},{10,... | collective-permute-start | bytes 589832 | tf_op jit(solution)/shard_map/ppermute | solution.py:706
  54.9 14.1 %collective-permute-start.10 = (bf16[2,128,1792]{2,1,0:T(8,128)(2,1)S(1)}, bf16[2,128,1792]{2,1,0:T(8,128)(2,1)S(1)}, u32[]{:S(2)}, u32[]{:S(2)}) collective-permute-start(bf16[2,128,1792]{2,1,0:T(8,128)(2,1)S(1)} %bitcast.58), channel_id=1, source_target_pairs={{0,4},{4,0},{8,12},{12,8},{1,5},{5,1},{9,13},{13,9},{2,6},{6,2},{1... | collective-permute-start | bytes 2752520 | tf_op jit(solution)/shard_map/ppermute | solution.py:700
  55.1 18.5 %collective-permute-start.8 = (bf16[64,4096]{1,0:T(8,128)(2,1)}, bf16[64,4096]{1,0:T(8,128)(2,1)S(1)}, u32[]{:S(2)}, u32[]{:S(2)}) collective-permute-start(bf16[64,4096]{1,0:T(8,128)(2,1)} %collective-permute-done.4.refs_4_.refs_8_), channel_id=1, source_target_pairs={{0,1},{1,0},{2,3},{3,2},{4,5},{5,4},{6,7},{7,6},{8,9},{9,8},{10,11... | collective-permute-start | bytes 1572872 | tf_op jit(solution)/shard_map/ppermute | solution.py:706
  73.6 3.8 %collective-permute-start.12 = (bf16[2,2,128,1792]{3,2,1,0:T(8,128)(2,1)S(1)}, bf16[2,2,128,1792]{3,2,1,0:T(8,128)(2,1)S(1)}, u32[]{:S(2)}, u32[]{:S(2)}) collective-permute-start(bf16[2,2,128,1792]{3,2,1,0:T(8,128)(2,1)S(1)} %get-tuple-element.64), channel_id=1, source_target_pairs={{0,4},{4,0},{8,12},{12,8},{1,5},{5,1},{9,13},{13,9},{2,6},{6,2},{1... | collective-permute-start | bytes 5505032 | tf_op jit(solution)/shard_map/ppermute | solution.py:700
  73.8 11.6 %collective-permute-start.13 = (bf16[2,768,128]{2,1,0:T(8,128)(2,1)S(1)}, bf16[2,768,128]{2,1,0:T(8,128)(2,1)S(1)}, u32[]{:S(2)}, u32[]{:S(2)}) collective-permute-start(bf16[2,768,128]{2,1,0:T(8,128)(2,1)S(1)} %pad_maximum_fusion.1), channel_id=1, source_target_pairs={{0,1},{1,0},{2,3},{3,2},{4,5},{5,4},{6,7},{7,6},{8,9},{9,8},{10,11... | collective-permute-start | bytes 1179656 | tf_op jit(solution)/shard_map/ppermute | solution.py:706
  73.8 24.5 %collective-permute-start.16 = (bf16[2,128,1792]{2,1,0:T(8,128)(2,1)S(1)}, bf16[2,128,1792]{2,1,0:T(8,128)(2,1)S(1)}, u32[]{:S(2)}, u32[]{:S(2)}) collective-permute-start(bf16[2,128,1792]{2,1,0:T(8,128)(2,1)S(1)} %fusion), channel_id=1, source_target_pairs={{0,8},{4,12},{8,0},{12,4},{1,9},{5,13},{9,1},{13,5},{2,10},{6,14},... | collective-permute-start | bytes 2752520 | tf_op jit(solution)/shard_map/ppermute | solution.py:703
  78.0 15.1 %collective-permute-start.17 = (bf16[128,1792]{1,0:T(8,128)(2,1)S(1)}, bf16[128,1792]{1,0:T(8,128)(2,1)S(1)}, u32[]{:S(2)}, u32[]{:S(2)}) collective-permute-start(bf16[128,1792]{1,0:T(8,128)(2,1)S(1)} %fusion.5.mine_ref), channel_id=1, source_target_pairs={{0,4},{4,0},{8,12},{12,8},{1,5},{5,1},{9,13},{13,9},{2,6},{6,2},{1... | collective-permute-start | bytes 1376264 | tf_op jit(solution)/shard_map/ppermute | solution.py:700
  90.7 16.2 %collective-permute-start.20 = (bf16[128,1792]{1,0:T(8,128)(2,1)S(1)}, bf16[128,1792]{1,0:T(8,128)(2,1)S(1)}, u32[]{:S(2)}, u32[]{:S(2)}) collective-permute-start(bf16[128,1792]{1,0:T(8,128)(2,1)S(1)} %fusion.5.mine_ref), channel_id=1, source_target_pairs={{0,8},{4,12},{8,0},{12,4},{1,9},{5,13},{9,1},{13,5},{2,10},{6,14},... | collective-permute-start | bytes 1376264 | tf_op jit(solution)/shard_map/ppermute | solution.py:703
  92.7 7.0 %collective-permute-start.14 = (bf16[64,4096]{1,0:T(8,128)(2,1)}, bf16[64,4096]{1,0:T(8,128)(2,1)S(1)}, u32[]{:S(2)}, u32[]{:S(2)}) collective-permute-start(bf16[64,4096]{1,0:T(8,128)(2,1)} %collective-permute-done.4.refs_4_.refs_8_), channel_id=1, source_target_pairs={{0,4},{4,0},{8,12},{12,8},{1,5},{5,1},{9,13},{13,9},{2,6},{6,2},{1... | collective-permute-start | bytes 1572872 | tf_op jit(solution)/shard_map/ppermute | solution.py:700
  92.7 7.0 %collective-permute-start.15 = (bf16[64,4096]{1,0:T(8,128)(2,1)S(1)}, bf16[64,4096]{1,0:T(8,128)(2,1)S(1)}, u32[]{:S(2)}, u32[]{:S(2)}) collective-permute-start(bf16[64,4096]{1,0:T(8,128)(2,1)S(1)} %collective-permute-done.8.refs_5_.refs_9_), channel_id=1, source_target_pairs={{0,4},{4,0},{8,12},{12,8},{1,5},{5,1},{9,13},{13,9},{2,6},{6,2},{1... | collective-permute-start | bytes 1572872 | tf_op jit(solution)/shard_map/ppermute | solution.py:700
  99.0 8.0 %collective-permute-start.19 = (bf16[128,1792]{1,0:T(8,128)(2,1)S(1)}, bf16[128,1792]{1,0:T(8,128)(2,1)S(1)}, u32[]{:S(2)}, u32[]{:S(2)}) collective-permute-start(bf16[128,1792]{1,0:T(8,128)(2,1)S(1)} %fusion.3.mine_ref), channel_id=1, source_target_pairs={{0,4},{4,0},{8,12},{12,8},{1,5},{5,1},{9,13},{13,9},{2,6},{6,2},{1... | collective-permute-start | bytes 1376264 | tf_op jit(solution)/shard_map/ppermute | solution.py:700
  99.1 17.4 %collective-permute-start.18 = (bf16[128,1792]{1,0:T(8,128)(2,1)S(1)}, bf16[128,1792]{1,0:T(8,128)(2,1)S(1)}, u32[]{:S(2)}, u32[]{:S(2)}) collective-permute-start(bf16[128,1792]{1,0:T(8,128)(2,1)S(1)} %fusion.3.mine_ref), channel_id=1, source_target_pairs={{0,8},{4,12},{8,0},{12,4},{1,9},{5,13},{9,1},{13,5},{2,10},{6,14},... | collective-permute-start | bytes 1376264 | tf_op jit(solution)/shard_map/ppermute | solution.py:703
  107.0 9.5 %collective-permute-start.22 = (bf16[128,1792]{1,0:T(8,128)(2,1)S(1)}, bf16[128,1792]{1,0:T(8,128)(2,1)S(1)}, u32[]{:S(2)}, u32[]{:S(2)}) collective-permute-start(bf16[128,1792]{1,0:T(8,128)(2,1)S(1)} %collective-permute-done.20.refs_1_), channel_id=1, source_target_pairs={{0,4},{4,0},{8,12},{12,8},{1,5},{5,1},{9,13},{13,9},{2,6},{6,2},{1... | collective-permute-start | bytes 1376264 | tf_op jit(solution)/shard_map/ppermute | solution.py:700
  116.5 1.8 %collective-permute-start.21 = (bf16[128,1792]{1,0:T(8,128)(2,1)S(1)}, bf16[128,1792]{1,0:T(8,128)(2,1)S(1)}, u32[]{:S(2)}, u32[]{:S(2)}) collective-permute-start(bf16[128,1792]{1,0:T(8,128)(2,1)S(1)} %collective-permute-done.18.refs_0_), channel_id=1, source_target_pairs={{0,4},{4,0},{8,12},{12,8},{1,5},{5,1},{9,13},{13,9},{2,6},{6,2},{1... | collective-permute-start | bytes 1376264 | tf_op jit(solution)/shard_map/ppermute | solution.py:700
  129.4 5.7 %collective-permute-start.23 = (bf16[2,256,128]{2,1,0:T(8,128)(2,1)S(1)}, bf16[2,256,128]{2,1,0:T(8,128)(2,1)S(1)}, u32[]{:S(2)}, u32[]{:S(2)}) collective-permute-start(bf16[2,256,128]{2,1,0:T(8,128)(2,1)S(1)} %slice.51), channel_id=1, source_target_pairs={{0,1},{1,0},{2,3},{3,2},{4,5},{5,4},{6,7},{7,6},{8,9},{9,8},{10,11... | collective-permute-start | bytes 393224 | tf_op jit(solution)/shard_map/ppermute | solution.py:706
  134.7 9.5 %collective-permute-start.24 = (bf16[2,512,128]{2,1,0:T(8,128)(2,1)S(1)}, bf16[2,512,128]{2,1,0:T(8,128)(2,1)S(1)}, u32[]{:S(2)}, u32[]{:S(2)}) collective-permute-start(bf16[2,512,128]{2,1,0:T(8,128)(2,1)S(1)} %right_grads.2), channel_id=1, source_target_pairs={{0,1},{1,0},{2,3},{3,2},{4,5},{5,4},{6,7},{7,6},{8,9},{9,8},{10,11... | collective-permute-start | bytes 786440 | tf_op jit(solution)/shard_map/ppermute | solution.py:706
  135.2 12.9 %collective-permute-start.27 = (bf16[256,128]{1,0:T(8,128)(2,1)S(1)}, bf16[256,128]{1,0:T(8,128)(2,1)S(1)}, u32[]{:S(2)}, u32[]{:S(2)}) collective-permute-start(bf16[256,128]{1,0:T(8,128)(2,1)S(1)} %slice_bitcast_fusion.6), channel_id=1, source_target_pairs={{0,2},{1,3},{2,0},{3,1},{4,6},{5,7},{6,4},{7,5},{8,10},{9,11},{10,... | collective-permute-start | bytes 196616 | tf_op jit(solution)/shard_map/ppermute | solution.py:706
  144.3 4.7 %collective-permute-start.25 = (bf16[512,128]{1,0:T(8,128)(2,1)S(1)}, bf16[512,128]{1,0:T(8,128)(2,1)S(1)}, u32[]{:S(2)}, u32[]{:S(2)}) collective-permute-start(bf16[512,128]{1,0:T(8,128)(2,1)S(1)} %get-tuple-element.86), channel_id=1, source_target_pairs={{0,0},{1,4},{2,8},{3,12},{4,1},{5,5},{6,9},{7,13},{8,2},{9,6},{10,... | collective-permute-start | bytes 393224 | tf_op jit(solution)/shard_map/ppermute | solution.py:713
  145.0 15.1 %collective-permute-start.26 = (bf16[512,128]{1,0:T(8,128)(2,1)S(1)}, bf16[512,128]{1,0:T(8,128)(2,1)S(1)}, u32[]{:S(2)}, u32[]{:S(2)}) collective-permute-start(bf16[512,128]{1,0:T(8,128)(2,1)S(1)} %get-tuple-element.87), channel_id=1, source_target_pairs={{0,8},{1,12},{2,0},{3,4},{4,9},{5,13},{6,1},{7,5},{8,10},{9,14},{1... | collective-permute-start | bytes 393224 | tf_op jit(solution)/shard_map/ppermute | solution.py:713
